TPU v7x, 32 devices: a whole 2x2x4 slice. The times are simulated.
32 devices in a mesh: groups: 2 (over y), dom: 16 (over z, x, core).
Axes of the slice: x: 2, y: 2, z: 4, core: 2. Of those that a mesh axis runs over, the one named last changes fastest.
Arguments:
- nodes: bfloat16 [4096, 512], P(('groups', 'dom')), parts along dimension 0, may hold values from -6 to 6
- edges: bfloat16 [24576, 512], P(('groups', 'dom')), parts along dimension 0, may hold values from -6 to 6
- inner_pairs: int32 [8192, 2], P(('groups', 'dom')), parts along dimension 0, may hold values from 0 to 127
- cut_local: int32 [4096], P(('groups', 'dom')), parts along dimension 0, may hold values from 0 to 127
- cut_dest: int32 [4096, 1], P(('groups', 'dom')), parts along dimension 0, may hold values from 0 to 15; in each aligned block of 128 rows (0 to 127, 128 to 255, ...) at most 16 rows name the same one
- cut_remote: int32 [4096], P(('groups', 'dom')), parts along dimension 0, may hold values from 0 to 127
- w_edge_in: bfloat16 [1536, 512], replicated, may hold values from -0.15625 to 0.15625
- w_edge_out: bfloat16 [512, 512], replicated, may hold values from -0.25 to 0.25
- w_node_in: bfloat16 [1024, 512], replicated, may hold values from -0.1875 to 0.1875
- w_node_out: bfloat16 [512, 512], replicated, may hold values from -0.25 to 0.25
- ct_nodes: bfloat16 [4096, 512], P(('groups', 'dom')), parts along dimension 0, may hold values from -6 to 6
- ct_edges: bfloat16 [24576, 512], P(('groups', 'dom')), parts along dimension 0, may hold values from -6 to 6
Outputs:
- new_nodes: bfloat16 [4096, 512], P(('groups', 'dom')), parts along dimension 0
- new_edges: bfloat16 [24576, 512], P(('groups', 'dom')), parts along dimension 0
- grad_nodes: float32 [4096, 512], P(('groups', 'dom')), parts along dimension 0
- grad_edges: float32 [24576, 512], P(('groups', 'dom')), parts along dimension 0
- grad_edge_in: bfloat16 [3072, 512], P('groups'), parts along dimension 0
- grad_edge_out: bfloat16 [1024, 512], P('groups'), parts along dimension 0
- grad_node_in: bfloat16 [2048, 512], P('groups'), parts along dimension 0
- grad_node_out: bfloat16 [1024, 512], P('groups'), parts along dimension 0
There are 2 independent parts, one for each index of `groups`. A program takes and returns all parts, laid end to end along the dimension named above; an argument that names none is the same for every part. Nothing has to cross between parts.
Inputs may be any that keep to these rules, and one draw needn't show every extreme that they name: `cut_dest`: among the cut pairs of one device, at most 16 name any one device, and in every draw some device's pairs name some device exactly 16 times.
All inputs are finite; a program needn't handle non-finite values.
Results may differ from a plain program's by a relative error of at most 0.0085.
Values may be sent and summed in bfloat16 or wider, within the bound.
No kernel may reach another device: no remote copies, remote signals or barrier semaphores. Data moves between devices by JAX's collectives and lax.ppermute only.
A program may use at most 128 MiB of HBM per device.

v0:
```python
import functools

import jax
import jax.numpy as jnp
from jax import lax
from jax.experimental import pallas as pl
from jax.experimental.pallas import tpu as pltpu
from jax.sharding import PartitionSpec as P

BF16 = jnp.bfloat16
F32 = jnp.float32
VMEM_LIMIT = 40 * 1024 * 1024


def dot(left, right):
    return jnp.dot(left, right, preferred_element_type=F32)


def dot_rows(left, right):
    return lax.dot_general(left, right, (((0,), (0,)), ((), ())), preferred_element_type=F32)


def dot_cols(left, right):
    return lax.dot_general(left, right, (((1,), (1,)), ((), ())), preferred_element_type=F32)


def iota(shape, axis):
    return lax.broadcasted_iota(jnp.int32, shape, axis)


def marks(mask):
    return jnp.where(mask, 1.0, 0.0).astype(BF16)


def onehot(column, width):
    return marks(column == iota((column.shape[0], width), 1))


def to_column(row):
    count = row.shape[1]
    square = (count, count)
    kept = jnp.where(iota(square, 0) == iota(square, 1), row.astype(F32), 0.0)
    return jnp.sum(kept, axis=1, keepdims=True)


def slot_ranks(dest, domains):
    count = dest.shape[0]
    square = (count, count)
    dest_marks = onehot(dest, domains)
    before = dot(marks(iota(square, 0) > iota(square, 1)), dest_marks)
    return dest_marks, jnp.sum(before * dest_marks.astype(F32), axis=1, keepdims=True)


def pair_marks(first, second, width):
    pairs = first.shape[0]
    shape = (2 * pairs, pairs)
    edge, pair = iota(shape, 0), iota(shape, 1)
    mine = (edge >> 1) == pair
    even = marks(mine & ((edge & 1) == 0))
    odd = marks(mine & ((edge & 1) == 1))
    first_marks, second_marks = onehot(first, width), onehot(second, width)
    senders = dot(even, first_marks) + dot(odd, second_marks)
    receivers = dot(even, second_marks) + dot(odd, first_marks)
    return senders.astype(BF16), receivers.astype(BF16)


def normalise(values):
    centered = values - jnp.mean(values, axis=1, keepdims=True)
    inv_scale = lax.rsqrt(jnp.mean(centered * centered, axis=1, keepdims=True) + 1e-05)
    return centered * inv_scale, inv_scale


def activate(pre_hidden):
    gate = jax.nn.sigmoid(pre_hidden)
    return (pre_hidden * gate).astype(BF16), gate * (1.0 + pre_hidden * (1.0 - gate))


def norm_backward(upstream, normed, inv_scale):
    centered = (
        upstream
        - jnp.mean(upstream, axis=1, keepdims=True)
        - normed * jnp.mean(upstream * normed, axis=1, keepdims=True)
    )
    return (inv_scale * centered).astype(BF16)


def ask_kernel(dest_ref, remote_ref, ask_ref):
    domains, slots = ask_ref.shape
    dest_marks, rank = slot_ranks(dest_ref[...], domains)
    rank_marks = jnp.where(rank == iota((rank.shape[0], slots), 1).astype(F32), 1.0, 0.0)
    wanted = (rank_marks * to_column(remote_ref[...])).astype(BF16)
    ask_ref[...] = dot_rows(dest_marks, wanted).astype(jnp.int32)


def reply_kernel(asked_ref, nodes_ref, reply_ref, asked_marks_ref):
    domains, slots = asked_ref.shape
    total = domains * slots
    shift = slots.bit_length() - 1
    spread = marks((iota((total, domains), 0) >> shift) == iota((total, domains), 1))
    listed = dot(spread, asked_ref[...].astype(F32).astype(BF16))
    at_slot = (iota((total, slots), 0) & (slots - 1)) == iota((total, slots), 1)
    column = jnp.sum(jnp.where(at_slot, listed, 0.0), axis=1, keepdims=True)
    node_rows = nodes_ref.shape[0]
    asked_marks = marks(column == iota((total, node_rows), 1).astype(F32))
    asked_marks_ref[...] = asked_marks
    reply_ref[...] = dot(asked_marks, nodes_ref[...]).astype(BF16)


def cut_marks_kernel(dest_ref, local_ref, dep_ref, senders_ref, receivers_ref, *, domains, slots):
    width = senders_ref.shape[1]
    base = width - domains * slots
    dest = dest_ref[...]
    _, rank = slot_ranks(dest, domains)
    second = dest * slots + rank.astype(jnp.int32) + base
    first = to_column(local_ref[...]).astype(jnp.int32)
    senders, receivers = pair_marks(first, second, width)
    senders_ref[...] = senders
    receivers_ref[...] = receivers


def edge_forward(edge, sender, receiver, w_in_ref, w_out_ref):
    latent = edge.shape[1]
    pre_hidden = (
        dot(edge, w_in_ref[:latent])
        + dot(sender, w_in_ref[latent : 2 * latent])
        + dot(receiver, w_in_ref[2 * latent :])
    )
    hidden, slope = activate(pre_hidden)
    normed, inv_scale = normalise(dot(hidden, w_out_ref[...]))
    return hidden, slope, normed, inv_scale


def inner_forward_kernel(
    pairs_ref,
    edges_ref,
    nodes_ref,
    w_in_ref,
    w_out_ref,
    dep_ref,
    senders_ref,
    receivers_ref,
    sender_ref,
    receiver_ref,
    hidden_ref,
    slope_ref,
    normed_ref,
    scale_ref,
    total_ref,
):
    pairs = pairs_ref[...]
    senders, receivers = pair_marks(pairs[:, 0:1], pairs[:, 1:2], nodes_ref.shape[0])
    senders_ref[...] = senders
    receivers_ref[...] = receivers
    nodes = nodes_ref[...]
    sender = dot(senders, nodes).astype(BF16)
    receiver = dot(receivers, nodes).astype(BF16)
    sender_ref[...] = sender
    receiver_ref[...] = receiver
    hidden, slope, normed, inv_scale = edge_forward(
        edges_ref[...], sender, receiver, w_in_ref, w_out_ref
    )
    hidden_ref[...] = hidden
    slope_ref[...] = slope
    normed_ref[...] = normed
    scale_ref[...] = inv_scale
    part = dot_rows(receivers, normed.astype(BF16))

    @pl.when(pl.program_id(0) == 0)
    def _():
        total_ref[...] = part

    @pl.when(pl.program_id(0) > 0)
    def _():
        total_ref[...] += part


def cut_forward_kernel(
    senders_ref,
    receivers_ref,
    edges_ref,
    nodes_ref,
    far_ref,
    w_in_ref,
    w_out_ref,
    inner_total_ref,
    sender_ref,
    receiver_ref,
    hidden_ref,
    slope_ref,
    normed_ref,
    scale_ref,
    total_ref,
    outgoing_ref,
):
    base = nodes_ref.shape[0]
    nodes, far = nodes_ref[...], far_ref[...]

    def rows_of(marks_ref):
        return (dot(marks_ref[:, :base], nodes) + dot(marks_ref[:, base:], far)).astype(BF16)

    sender, receiver = rows_of(senders_ref), rows_of(receivers_ref)
    sender_ref[...] = sender
    receiver_ref[...] = receiver
    hidden, slope, normed, inv_scale = edge_forward(
        edges_ref[...], sender, receiver, w_in_ref, w_out_ref
    )
    hidden_ref[...] = hidden
    slope_ref[...] = slope
    normed_ref[...] = normed
    scale_ref[...] = inv_scale
    message = normed.astype(BF16)
    total_ref[...] = inner_total_ref[...] + dot_rows(receivers_ref[:, :base], message)
    outgoing_ref[...] = dot_rows(receivers_ref[:, base:], message).astype(BF16)


def new_edges_kernel(edges_ref, inner_ref, cut_ref, dep_ref, out_ref):
    inner_rows = inner_ref.shape[0]

    def added(edge, normed):
        return (edge.astype(F32) + normed.astype(BF16).astype(F32)).astype(BF16)

    out_ref[:inner_rows] = added(edges_ref[:inner_rows], inner_ref[...])
    out_ref[inner_rows:] = added(edges_ref[inner_rows:], cut_ref[...])


def node_kernel(
    incoming_ref,
    asked_marks_ref,
    total_ref,
    nodes_ref,
    ct_ref,
    w_in_ref,
    w_out_ref,
    new_nodes_ref,
    self_grad_ref,
    agg_grad_ref,
    reply_ref,
    aggregate_ref,
    hidden_ref,
    grad_out_ref,
    grad_pre_ref,
):
    latent = nodes_ref.shape[1]
    nodes, asked_marks = nodes_ref[...], asked_marks_ref[...]
    aggregate = (total_ref[...] + dot_rows(asked_marks, incoming_ref[...])).astype(BF16)
    aggregate_ref[...] = aggregate
    pre_hidden = dot(nodes, w_in_ref[:latent]) + dot(aggregate, w_in_ref[latent:])
    hidden, slope = activate(pre_hidden)
    hidden_ref[...] = hidden
    normed, inv_scale = normalise(dot(hidden, w_out_ref[...]))
    upstream = ct_ref[...].astype(F32)
    grad_out = norm_backward(upstream, normed, inv_scale)
    grad_out_ref[...] = grad_out
    grad_pre = (dot_cols(grad_out, w_out_ref[...]) * slope).astype(BF16)
    grad_pre_ref[...] = grad_pre
    agg_grad = dot_cols(grad_pre, w_in_ref[latent:]).astype(BF16)
    agg_grad_ref[...] = agg_grad
    reply_ref[...] = dot(asked_marks, agg_grad).astype(BF16)
    self_grad_ref[...] = upstream + dot_cols(grad_pre, w_in_ref[:latent])
    new_nodes_ref[...] = (nodes.astype(F32) + normed).astype(BF16)


def node_weights_kernel(
    place_ref, nodes_ref, aggregate_ref, hidden_ref, grad_out_ref, grad_pre_ref, keep_ref, send_ref
):
    latent = nodes_ref.shape[1]
    half = latent // 2

    def fill(low_ref, high_ref):
        grad_pre, grad_out = grad_pre_ref[...], grad_out_ref[...]
        low_ref[:latent] = dot_rows(nodes_ref[...], grad_pre).astype(BF16)
        low_ref[latent:] = dot_rows(aggregate_ref[:, :half], grad_pre).astype(BF16)
        high_ref[:half] = dot_rows(aggregate_ref[:, half:], grad_pre).astype(BF16)
        high_ref[half:] = dot_rows(hidden_ref[...], grad_out).astype(BF16)

    @pl.when(place_ref[0] == 0)
    def _():
        fill(keep_ref, send_ref)

    @pl.when(place_ref[0] != 0)
    def _():
        fill(send_ref, keep_ref)


def edge_backward(ct, target_grads, normed, inv_scale, slope, w_out):
    grad_out = norm_backward(ct.astype(F32) + target_grads, normed, inv_scale)
    return grad_out, (dot_cols(grad_out, w_out) * slope).astype(BF16)


def inner_backward_kernel(
    receivers_ref,
    agg_grad_ref,
    ct_ref,
    normed_ref,
    scale_ref,
    slope_ref,
    w_out_ref,
    dep_ref,
    grad_out_ref,
    grad_pre_ref,
):
    grad_out, grad_pre = edge_backward(
        ct_ref[...],
        dot(receivers_ref[...], agg_grad_ref[...]),
        normed_ref[...],
        scale_ref[...],
        slope_ref[...],
        w_out_ref[...],
    )
    grad_out_ref[...] = grad_out
    grad_pre_ref[...] = grad_pre


def cut_backward_kernel(
    receivers_ref,
    agg_grad_ref,
    far_grad_ref,
    ct_ref,
    normed_ref,
    scale_ref,
    slope_ref,
    w_out_ref,
    grad_out_ref,
    grad_pre_ref,
):
    base = agg_grad_ref.shape[0]
    target = dot(receivers_ref[:, :base], agg_grad_ref[...]) + dot(
        receivers_ref[:, base:], far_grad_ref[...]
    )
    grad_out, grad_pre = edge_backward(
        ct_ref[...], target, normed_ref[...], scale_ref[...], slope_ref[...], w_out_ref[...]
    )
    grad_out_ref[...] = grad_out
    grad_pre_ref[...] = grad_pre


def edge_weights_kernel(
    place_ref,
    edges_ref,
    inner_sender_ref,
    cut_sender_ref,
    inner_receiver_ref,
    cut_receiver_ref,
    inner_hidden_ref,
    cut_hidden_ref,
    inner_out_ref,
    cut_out_ref,
    inner_pre_ref,
    cut_pre_ref,
    dep_ref,
    out_ref,
):
    latent = edges_ref.shape[1]
    inner_rows = inner_pre_ref.shape[0]

    @pl.when(place_ref[0] == 0)
    def _():
        inner_pre, cut_pre = inner_pre_ref[...], cut_pre_ref[...]
        out_ref[:latent] = (
            dot_rows(edges_ref[:inner_rows], inner_pre) + dot_rows(edges_ref[inner_rows:], cut_pre)
        ).astype(BF16)
        out_ref[latent:] = (
            dot_rows(inner_sender_ref[...], inner_pre) + dot_rows(cut_sender_ref[...], cut_pre)
        ).astype(BF16)

    @pl.when(place_ref[0] != 0)
    def _():
        out_ref[:latent] = (
            dot_rows(inner_receiver_ref[...], inner_pre_ref[...])
            + dot_rows(cut_receiver_ref[...], cut_pre_ref[...])
        ).astype(BF16)
        out_ref[latent:] = (
            dot_rows(inner_hidden_ref[...], inner_out_ref[...])
            + dot_rows(cut_hidden_ref[...], cut_out_ref[...])
        ).astype(BF16)


def input_grads_kernel(
    inner_senders_ref,
    inner_receivers_ref,
    cut_senders_ref,
    cut_receivers_ref,
    inner_pre_ref,
    cut_pre_ref,
    w_in_ref,
    dep_ref,
    local_ref,
    outgoing_ref,
):
    latent = inner_pre_ref.shape[1]
    base = inner_senders_ref.shape[1]
    inner_pre, cut_pre = inner_pre_ref[...], cut_pre_ref[...]
    w_sender, w_receiver = w_in_ref[latent : 2 * latent], w_in_ref[2 * latent :]

    def summed(inner_marks_ref, cut_marks_ref):
        return (
            dot_rows(inner_marks_ref[...], inner_pre) + dot_rows(cut_marks_ref[:, :base], cut_pre)
        ).astype(BF16)

    outgoing_ref[...] = (
        dot_cols(dot_rows(cut_senders_ref[:, base:], cut_pre).astype(BF16), w_sender)
        + dot_cols(dot_rows(cut_receivers_ref[:, base:], cut_pre).astype(BF16), w_receiver)
    ).astype(BF16)
    local_ref[...] = dot_cols(summed(inner_senders_ref, cut_senders_ref), w_sender) + dot_cols(
        summed(inner_receivers_ref, cut_receivers_ref), w_receiver
    )


def edge_grads_kernel(ct_ref, inner_pre_ref, cut_pre_ref, w_edge_ref, dep_ref, out_ref, *, blocks):
    inside = pl.program_id(0) < blocks

    @pl.when(inside)
    def _():
        out_ref[...] = ct_ref[...].astype(F32) + dot_cols(inner_pre_ref[...], w_edge_ref[...])

    @pl.when(jnp.logical_not(inside))
    def _():
        out_ref[...] = ct_ref[...].astype(F32) + dot_cols(cut_pre_ref[...], w_edge_ref[...])


def node_grads_kernel(self_ref, local_ref, asked_marks_ref, returned_ref, out_ref):
    out_ref[...] = (
        self_ref[...] + local_ref[...] + dot_rows(asked_marks_ref[...], returned_ref[...])
    )


VMEM = pl.BlockSpec(memory_space=pltpu.VMEM)
SMEM = pl.BlockSpec(memory_space=pltpu.SMEM)
ANY = pl.BlockSpec(memory_space=pl.ANY)


def shaped(dtype, *shape):
    return jax.ShapeDtypeStruct(shape, dtype)


def run(body, outs, ins, flops, specs=None, out_specs=None, grid=None):
    single = not isinstance(outs, (list, tuple))
    out_shape = [outs] if single else list(outs)
    moved = sum(item.size * item.dtype.itemsize for item in list(ins) + out_shape)
    extra = {} if grid is None else {"grid": grid}
    result = pl.pallas_call(
        body,
        out_shape=out_shape,
        in_specs=[VMEM] * len(ins) if specs is None else specs,
        out_specs=[VMEM] * len(out_shape) if out_specs is None else out_specs,
        compiler_params=pltpu.CompilerParams(vmem_limit_bytes=VMEM_LIMIT),
        cost_estimate=pl.CostEstimate(flops=flops, bytes_accessed=moved, transcendentals=0),
        **extra,
    )(*ins)
    return result[0] if single else result


def bit_groups(devices):
    bits = devices.bit_length() - 1
    groups = [(low, 1) for low in range(min(2, bits))]
    low = 2
    while low < bits:
        groups.append((low, min(2, bits - low)))
        low += 2
    return groups


def partner_pairs(devices, mask):
    return [(device, device ^ mask) for device in range(devices)]


def reduce_rows(keep, send, devices):
    me = lax.axis_index("dom")
    groups = bit_groups(devices)
    received = lax.ppermute(send, "dom", partner_pairs(devices, 1))
    rows = (keep.astype(F32) + received.astype(F32)).astype(BF16)
    for low, width in groups[1:]:
        size = 1 << width
        place = (me >> low) & (size - 1)
        chunk = rows.shape[0] // size
        pieces = rows.reshape(size, chunk, rows.shape[1])
        total = lax.dynamic_index_in_dim(pieces, place, 0, False).astype(F32)
        for turn in range(1, size):
            sent = lax.dynamic_index_in_dim(pieces, place ^ turn, 0, False)
            total += lax.ppermute(sent, "dom", partner_pairs(devices, turn << low)).astype(F32)
        rows = total.astype(BF16)
    return rows


def gather_rows(rows, devices):
    me = lax.axis_index("dom")
    for low, width in bit_groups(devices)[::-1]:
        size = 1 << width
        place = (me >> low) & (size - 1)
        whole = jnp.zeros((size,) + rows.shape, rows.dtype)
        for turn in range(size):
            piece = rows
            if turn:
                piece = lax.ppermute(rows, "dom", partner_pairs(devices, turn << low))
            whole = lax.dynamic_update_index_in_dim(whole, piece, place ^ turn, 0)
        rows = whole.reshape(size * rows.shape[0], rows.shape[1])
    return rows


def exchange(rows, domains):
    shape = rows.shape
    split = rows.reshape((domains, shape[0] // domains) + shape[1:])
    return lax.all_to_all(split, "dom", split_axis=0, concat_axis=0, tiled=True).reshape(shape)


def shards(
    nodes,
    edges,
    inner_pairs,
    cut_local,
    cut_dest,
    cut_remote,
    w_edge_in,
    w_edge_out,
    w_node_in,
    w_node_out,
    ct_nodes,
    ct_edges,
):
    domains = lax.axis_size("dom")
    node_rows, latent = nodes.shape
    inner_count, cut_count = inner_pairs.shape[0], cut_local.shape[0]
    inner_rows, cut_rows = 2 * inner_count, 2 * cut_count
    slots = max(2, 2 * cut_count // domains)
    total_slots = domains * slots
    table = node_rows + total_slots
    square = 2 * latent * latent
    place = lax.axis_index("dom") & 1
    mine, other = place.reshape(1), (1 - place).reshape(1)

    ask = run(
        ask_kernel, shaped(jnp.int32, domains, slots), [cut_dest, cut_remote.reshape(1, -1)], 10**7
    )
    asked = lax.all_to_all(ask, "dom", split_axis=0, concat_axis=0, tiled=True)
    cut_senders, cut_receivers = run(
        functools.partial(cut_marks_kernel, domains=domains, slots=slots),
        [shaped(BF16, cut_rows, table)] * 2,
        [cut_dest, cut_local.reshape(1, -1), ask],
        10**8,
        [VMEM, VMEM, ANY],
    )
    reply, asked_marks = run(
        reply_kernel,
        [shaped(BF16, total_slots, latent), shaped(BF16, total_slots, node_rows)],
        [asked, nodes],
        10**8,
    )
    far = exchange(reply, domains)

    block = cut_rows
    blocks = inner_rows // block

    def rows_spec(width, rows=block):
        return pl.BlockSpec((rows, width), lambda step: (step, 0))

    def all_spec(array):
        return pl.BlockSpec(array.shape, lambda step: (0, 0))

    saved_widths = [node_rows, node_rows, latent, latent, latent, latent, latent, 1]
    saved_types = [BF16, BF16, BF16, BF16, BF16, F32, F32, F32]
    (
        inner_senders,
        inner_receivers,
        inner_sender,
        inner_receiver,
        inner_hidden,
        inner_slope,
        inner_normed,
        inner_scale,
        inner_total,
    ) = run(
        inner_forward_kernel,
        [shaped(kind, inner_rows, width) for kind, width in zip(saved_types, saved_widths)]
        + [shaped(F32, node_rows, latent)],
        [inner_pairs, edges, nodes, w_edge_in, w_edge_out, reply],
        inner_rows * 4 * square,
        [
            rows_spec(2, block // 2),
            rows_spec(latent),
            all_spec(nodes),
            all_spec(w_edge_in),
            all_spec(w_edge_out),
            ANY,
        ],
        [rows_spec(width) for width in saved_widths] + [all_spec(nodes)],
        (blocks,),
    )

    def last_rows(array):
        return pl.BlockSpec((block, array.shape[1]), lambda step: (blocks, 0))

    (
        cut_sender,
        cut_receiver,
        cut_hidden,
        cut_slope,
        cut_normed,
        cut_scale,
        total,
        outgoing,
    ) = run(
        cut_forward_kernel,
        [shaped(kind, cut_rows, width) for kind, width in zip(saved_types, saved_widths)][2:]
        + [shaped(F32, node_rows, latent), shaped(BF16, total_slots, latent)],
        [
            cut_senders,
            cut_receivers,
            edges,
            nodes,
            far,
            w_edge_in,
            w_edge_out,
            inner_total,
        ],
        cut_rows * 4 * square,
        [
            all_spec(cut_senders),
            all_spec(cut_receivers),
            last_rows(edges),
            all_spec(nodes),
            all_spec(far),
            all_spec(w_edge_in),
            all_spec(w_edge_out),
            all_spec(inner_total),
        ],
        [rows_spec(width) for width in saved_widths[2:]]
        + [all_spec(nodes), rows_spec(latent, total_slots)],
        (1,),
    )
    incoming = exchange(outgoing, domains)
    new_edges = run(
        new_edges_kernel,
        shaped(BF16, *edges.shape),
        [edges, inner_normed, cut_normed, outgoing],
        10**7,
        [VMEM, VMEM, VMEM, ANY],
    )
    (
        new_nodes,
        self_grad,
        agg_grad,
        grad_reply,
        aggregate,
        node_hidden,
        node_out,
        node_pre,
    ) = run(
        node_kernel,
        [
            shaped(BF16, node_rows, latent),
            shaped(F32, node_rows, latent),
            shaped(BF16, node_rows, latent),
            shaped(BF16, total_slots, latent),
        ]
        + [shaped(BF16, node_rows, latent)] * 4,
        [incoming, asked_marks, total, nodes, ct_nodes, w_node_in, w_node_out],
        node_rows * 6 * square,
    )
    far_grad = exchange(grad_reply, domains)
    node_keep, node_send = run(
        node_weights_kernel,
        [shaped(BF16, 3 * latent // 2, latent)] * 2,
        [mine, nodes, aggregate, node_hidden, node_out, node_pre],
        node_rows * 3 * square,
        [SMEM] + [VMEM] * 5,
    )
    node_total = gather_rows(reduce_rows(node_keep, node_send, domains), domains)

    inner_out, inner_pre = run(
        inner_backward_kernel,
        [shaped(BF16, inner_rows, latent)] * 2,
        [
            inner_receivers,
            agg_grad,
            ct_edges,
            inner_normed,
            inner_scale,
            inner_slope,
            w_edge_out,
            grad_reply,
        ],
        inner_rows * square,
        [
            rows_spec(node_rows),
            all_spec(agg_grad),
            rows_spec(latent),
            rows_spec(latent),
            rows_spec(1),
            rows_spec(latent),
            all_spec(w_edge_out),
            ANY,
        ],
        [rows_spec(latent)] * 2,
        (blocks,),
    )
    cut_out, cut_pre = run(
        cut_backward_kernel,
        [shaped(BF16, cut_rows, latent)] * 2,
        [
            cut_receivers,
            agg_grad,
            far_grad,
            ct_edges,
            cut_normed,
            cut_scale,
            cut_slope,
            w_edge_out,
        ],
        cut_rows * square,
        [
            all_spec(cut_receivers),
            all_spec(agg_grad),
            all_spec(far_grad),
            last_rows(ct_edges),
            all_spec(cut_normed),
            all_spec(cut_scale),
            all_spec(cut_slope),
            all_spec(w_edge_out),
        ],
        [rows_spec(latent)] * 2,
        (1,),
    )
    factors = [
        edges,
        inner_sender,
        cut_sender,
        inner_receiver,
        cut_receiver,
        inner_hidden,
        cut_hidden,
        inner_out,
        cut_out,
        inner_pre,
        cut_pre,
    ]

    def edge_weights(half, dep):
        return run(
            edge_weights_kernel,
            shaped(BF16, 2 * latent, latent),
            [half] + factors + [dep],
            (inner_rows + cut_rows) * 2 * square,
            [SMEM] + [VMEM] * len(factors) + [ANY],
        )

    edge_send = edge_weights(other, cut_pre)
    edge_keep = edge_weights(mine, edge_send)
    edge_total = gather_rows(reduce_rows(edge_keep, edge_send, domains), domains)
    local_grad, outgoing_grad = run(
        input_grads_kernel,
        [shaped(F32, node_rows, latent), shaped(BF16, total_slots, latent)],
        [
            inner_senders,
            inner_receivers,
            cut_senders,
            cut_receivers,
            inner_pre,
            cut_pre,
            w_edge_in,
            edge_keep,
        ],
        (node_rows + total_slots) * 2 * square,
        [VMEM] * 7 + [ANY],
    )
    grad_edges = run(
        functools.partial(edge_grads_kernel, blocks=blocks),
        shaped(F32, *edges.shape),
        [ct_edges, inner_pre, cut_pre, w_edge_in, edge_keep],
        (inner_rows + cut_rows) * square,
        [
            rows_spec(latent),
            pl.BlockSpec((block, latent), lambda step: (jnp.minimum(step, blocks - 1), 0)),
            all_spec(cut_pre),
            pl.BlockSpec((latent, latent), lambda step: (0, 0)),
            ANY,
        ],
        [rows_spec(latent)],
        (blocks + 1,),
    )
    returned = exchange(outgoing_grad, domains)
    grad_nodes = run(
        node_grads_kernel,
        shaped(F32, node_rows, latent),
        [self_grad, local_grad, asked_marks, returned],
        10**8,
    )
    return (
        new_nodes,
        new_edges,
        grad_nodes,
        grad_edges,
        edge_total[: 3 * latent],
        edge_total[3 * latent :],
        node_total[: 2 * latent],
        node_total[2 * latent :],
    )


def solution(mesh):
    placed = (
        P(("groups", "dom"), None),
        P(("groups", "dom"), None),
        P(("groups", "dom"), None),
        P(("groups", "dom")),
        P(("groups", "dom"), None),
        P(("groups", "dom")),
        P(),
        P(),
        P(),
        P(),
        P(("groups", "dom"), None),
        P(("groups", "dom"), None),
    )
    return jax.shard_map(
        shards,
        mesh=mesh,
        in_specs=placed,
        out_specs=(
            P(("groups", "dom"), None),
            P(("groups", "dom"), None),
            P(("groups", "dom"), None),
            P(("groups", "dom"), None),
            P("groups", None),
            P("groups", None),
            P("groups", None),
            P("groups", None),
        ),
        check_vma=False,
    )
```

profile of v0, /device:TPU:1, one launch (start us, length us, event | category | flops | bytes accessed | tf_op | source)
XLA Modules:
  0.0 204.6 jit_solution(11854225290825113019)
XLA Ops:
  2.5 12.9 %all_to_all.31 = s32[16,1,16]{2,1,0:T(1,128)S(1)} all-to-all(s32[16,1,16]{2,1,0:T(1,128)S(1)} %bitcast.95), channel_id=1, replica_groups=mesh['groups'=2,'dom'=16] {'dom'}, dimensions={0} | all-to-all | bytes 2048 | tf_op jit(solution)/shard_map/all_to_all | solution.py:534
  17.4 4.0 %all-to-all-start.1 = ((bf16[16,16,512]{2,1,0:T(8,128)(2,1)}), bf16[16,16,512]{2,1,0:T(8,128)(2,1)S(1)}, u32[]{:S(2)}, u32[]{:S(2)}) async-start(bf16[16,16,512]{2,1,0:T(8,128)(2,1)} %bitcast.5), calls=%async_computation.1 | async-start | bytes 524288 | tf_op jit(solution)/shard_map/all_to_all | solution.py:503
  21.4 1.5 copy.26.pairs_ref
  24.9 1.4 copy-done
  30.4 3.1 %shard_map.182 = (bf16[512,128]{1,0:T(8,128)(2,1)S(1)}, bf16[512,128]{1,0:T(8,128)(2,1)S(1)}, bf16[512,512]{1,0:T(8,128)(2,1)S(1)}, bf16[512,512]{1,0:T(8,128)(2...) custom-call(s32[256,2]{1,0:T(8,128)S(1)} %copy-done.87, ...), custom_call_target="tpu_custom_call" | custom-call | flops 1073741824 | bytes 7475200 | tf_op jit(solution)/shard_map/pallas_call | solution.py:441
  42.5 2.2 %shard_map.183 = (bf16[256,512]{1,0:T(8,128)(2,1)S(1)}, bf16[256,512]{1,0:T(8,128)(2,1)S(1)}, bf16[256,512]{1,0:T(8,128)(2,1)S(1)}, f32[256,512]{1,0:T(8,128)S(1...) custom-call(bf16[256,384]{1,0:T(8,128)(2,1)S(1)} %copy-done.53, ...), custom_call_target="tpu_custom_call" | custom-call | flops 536870912 | bytes 6292480 | tf_op jit(solution)/shard_map/pallas_call | solution.py:441
  49.8 6.1 %all-to-all-start.2 = ((bf16[16,16,512]{2,1,0:T(8,128)(2,1)}), bf16[16,16,512]{2,1,0:T(8,128)(2,1)S(1)}, u32[]{:S(2)}, u32[]{:S(2)}) async-start(bf16[16,16,512]{2,1,0:T(8,128)(2,1)} %bitcast.7), calls=%async_computation.2 | async-start | bytes 524288 | tf_op jit(solution)/shard_map/all_to_all | solution.py:503
  55.9 9.5 %all-to-all-done.2 = bf16[16,16,512]{2,1,0:T(8,128)(2,1)S(1)} async-done(((bf16[16,16,512]{2,1,0:T(8,128)(2,1)}), bf16[16,16,512]{2,1,0:T(8,128)(2,1)S(1)}, u32[]{:S(2)}, u32[]{:S(2)}) %all-to-all-start.2) | async-done | bytes 262176 | tf_op jit(solution)/shard_map/all_to_all | solution.py:503
  65.4 1.2 copy-done.49
  69.5 2.4 %shard_map.184 = (bf16[128,512]{1,0:T(8,128)(2,1)}, f32[128,512]{1,0:T(8,128)S(1)}, bf16[128,512]{1,0:T(8,128)(2,1)S(1)}, bf16[256,512]{1,0:T(8,128)(2,1)}, bf16...) custom-call(bf16[256,512]{1,0:T(8,128)(2,1)S(1)} %bitcast.92, ...), custom_call_target="tpu_custom_call" | custom-call | flops 402653184 | bytes 3735552 | tf_op jit(solution)/shard_map/pallas_call | solution.py:441
  72.6 1.5 shard_map.193
  75.6 4.1 %all-to-all-start.3 = ((bf16[16,16,512]{2,1,0:T(8,128)(2,1)}), bf16[16,16,512]{2,1,0:T(8,128)(2,1)}, u32[]{:S(2)}, u32[]{:S(2)}) async-start(bf16[16,16,512]{2,1,0:T(8,128)(2,1)} %bitcast.9), calls=%async_computation.3 | async-start | bytes 524288 | tf_op jit(solution)/shard_map/all_to_all | solution.py:503
  80.8 1.2 copy-done.18
  82.1 1.2 copy-done.51
  86.1 1.2 shard_map.186
  94.3 1.8 shard_map.187
  96.2 2.0 shard_map.188.dep_ref
  98.9 1.3 add_convert_fusion.1
  111.9 1.2 shard_map.189.dep_ref
  114.2 3.1 %collective-permute-start.14 = (bf16[96,512]{1,0:T(8,128)(2,1)S(1)}, bf16[96,512]{1,0:T(8,128)(2,1)S(1)}, u32[]{:S(2)}, u32[]{:S(2)}) collective-permute-start(bf16[96,512]{1,0:T(8,128)(2,1)S(1)} %get-tuple-element.90), channel_id=1, source_target_pairs={{0,12},{1,13},{2,14},{3,15},{4,8},{5,9},{6,10},{7,11},{8,4},{9,5},... | collective-permute-start | bytes 294920 | tf_op jit(solution)/shard_map/ppermute | solution.py:480
  117.8 1.5 add_convert_fusion
  119.4 1.5 collective-permute-start.1
  120.9 4.5 %collective-permute-done.13 = bf16[96,512]{1,0:T(8,128)(2,1)S(1)} collective-permute-done((bf16[96,512]{1,0:T(8,128)(2,1)S(1)}, bf16[96,512]{1,0:T(8,128)(2,1)S(1)}, u32[]{:S(2)}, u32[]{:S(2)}) %collective-permute-start.13) | collective-permute-done | bytes 98336 | tf_op jit(solution)/shard_map/ppermute | solution.py:480
  125.6 2.3 %collective-permute-start.16 = (bf16[96,512]{1,0:T(8,128)(2,1)S(1)}, bf16[96,512]{1,0:T(8,128)(2,1)S(1)}, u32[]{:S(2)}, u32[]{:S(2)}) collective-permute-start(bf16[96,512]{1,0:T(8,128)(2,1)S(1)} %get-tuple-element.83), channel_id=1, source_target_pairs={{0,8},{1,9},{2,10},{3,11},{4,12},{5,13},{6,14},{7,15},{8,0},{9,1},... | collective-permute-start | bytes 294920 | tf_op jit(solution)/shard_map/ppermute | solution.py:494
  128.0 1.2 collective-permute-start.17
  129.3 2.0 collective-permute-done.1
  131.6 3.3 %collective-permute-start.4 = (bf16[128,512]{1,0:T(8,128)(2,1)S(1)}, bf16[128,512]{1,0:T(8,128)(2,1)S(1)}, u32[]{:S(2)}, u32[]{:S(2)}) collective-permute-start(bf16[128,512]{1,0:T(8,128)(2,1)S(1)} %get-tuple-element.87), channel_id=1, source_target_pairs={{0,12},{1,13},{2,14},{3,15},{4,8},{5,9},{6,10},{7,11},{8,4},{9,5},... | collective-permute-start | bytes 393224 | tf_op jit(solution)/shard_map/ppermute | solution.py:480
  135.2 2.0 collective-permute-done.4
  137.3 10.0 %collective-permute-done.3 = bf16[128,512]{1,0:T(8,128)(2,1)S(1)} collective-permute-done((bf16[128,512]{1,0:T(8,128)(2,1)S(1)}, bf16[128,512]{1,0:T(8,128)(2,1)S(1)}, u32[]{:S(2)}, u32[]{:S(2)}) %collective-permute-start.3) | collective-permute-done | bytes 131104 | tf_op jit(solution)/shard_map/ppermute | solution.py:480
  147.5 2.0 collective-permute-start.18
  149.5 2.2 %collective-permute-start.6 = (bf16[128,512]{1,0:T(8,128)(2,1)S(1)}, bf16[128,512]{1,0:T(8,128)(2,1)S(1)}, u32[]{:S(2)}, u32[]{:S(2)}) collective-permute-start(bf16[128,512]{1,0:T(8,128)(2,1)S(1)} %get-tuple-element.85), channel_id=1, source_target_pairs={{0,8},{1,9},{2,10},{3,11},{4,12},{5,13},{6,14},{7,15},{8,0},{9,1},... | collective-permute-start | bytes 393224 | tf_op jit(solution)/shard_map/ppermute | solution.py:494
  151.7 1.3 collective-permute-start.7
  153.1 2.6 %collective-permute-done.6 = bf16[128,512]{1,0:T(8,128)(2,1)S(1)} collective-permute-done((bf16[128,512]{1,0:T(8,128)(2,1)S(1)}, bf16[128,512]{1,0:T(8,128)(2,1)S(1)}, u32[]{:S(2)}, u32[]{:S(2)}) %collective-permute-start.6) | collective-permute-done | bytes 131104 | tf_op jit(solution)/shard_map/ppermute | solution.py:494
  155.7 2.6 %collective-permute-done.7 = bf16[128,512]{1,0:T(8,128)(2,1)S(1)} collective-permute-done((bf16[128,512]{1,0:T(8,128)(2,1)S(1)}, bf16[128,512]{1,0:T(8,128)(2,1)S(1)}, u32[]{:S(2)}, u32[]{:S(2)}) %collective-permute-start.7) | collective-permute-done | bytes 131104 | tf_op jit(solution)/shard_map/ppermute | solution.py:494
  158.4 1.2 collective-permute-start.8
  162.1 4.3 %collective-permute-start.19 = (bf16[768,512]{1,0:T(8,128)(2,1)}, bf16[768,512]{1,0:T(8,128)(2,1)}, u32[]{:S(2)}, u32[]{:S(2)}) collective-permute-start(bf16[768,512]{1,0:T(8,128)(2,1)} %bitcast.50), channel_id=1, source_target_pairs={{0,1},{1,0},{2,3},{3,2},{4,5},{5,4},{6,7},{7,6},{8,9},{9,8},{10,11... | collective-permute-start | bytes 2359304 | tf_op jit(solution)/shard_map/ppermute | solution.py:494
  169.1 4.5 %collective-permute-start.9 = (bf16[1024,512]{1,0:T(8,128)(2,1)}, bf16[1024,512]{1,0:T(8,128)(2,1)}, u32[]{:S(2)}, u32[]{:S(2)}) collective-permute-start(bf16[1024,512]{1,0:T(8,128)(2,1)} %bitcast.31), channel_id=1, source_target_pairs={{0,1},{1,0},{2,3},{3,2},{4,5},{5,4},{6,7},{7,6},{8,9},{9,8},{10,11... | collective-permute-start | bytes 3145736 | tf_op jit(solution)/shard_map/ppermute | solution.py:494
  173.6 1.2 shard_map.190
  176.3 7.5 %all-to-all-start.4 = ((bf16[16,16,512]{2,1,0:T(8,128)(2,1)}), bf16[16,16,512]{2,1,0:T(8,128)(2,1)}, u32[]{:S(2)}, u32[]{:S(2)}) async-start(bf16[16,16,512]{2,1,0:T(8,128)(2,1)} %bitcast.94), calls=%async_computation.4 | async-start | bytes 524288 | tf_op jit(solution)/shard_map/all_to_all | solution.py:503
  183.8 1.2 copy-done.19
  187.7 2.3 %shard_map.192 = f32[768,512]{1,0:T(8,128)} custom-call(bf16[768,512]{1,0:T(8,128)(2,1)S(1)} %copy-done.10, bf16[512,512]{1,0:T(8,128)(2,1)S(1)} %copy-done.7, bf16[256,512]{1,0:T(8,128)(2,1)S(1)} %copy-done.14, bf16[1536,512]{1,0:T(8,128)(2,1)S(1)} %copy-done.1, bf16[1024,512]{1,0:T(8,128)(2,1)S(1)} %shard_map.189.dep_ref), custom_call_target="tpu_custom_call" | custom-call | flops 402653184 | bytes 5767168 | tf_op jit(solution)/shard_map/pallas_call | solution.py:441
  190.0 3.4 %all-to-all-done.4 = bf16[16,16,512]{2,1,0:T(8,128)(2,1)} async-done(((bf16[16,16,512]{2,1,0:T(8,128)(2,1)}), bf16[16,16,512]{2,1,0:T(8,128)(2,1)}, u32[]{:S(2)}, u32[]{:S(2)}) %all-to-all-start.4) | async-done | bytes 262176 | tf_op jit(solution)/shard_map/all_to_all | solution.py:503
  193.4 1.9 shard_map.191
  195.4 1.2 bitcast_dynamic-update-slice_fusion.3
  196.6 1.2 bitcast_dynamic-update-slice_fusion.2
  199.8 1.3 bitcast_dynamic-update-slice_fusion.1
  201.2 1.3 bitcast_dynamic-update-slice_fusion
  202.5 1.2 slice.16
  (236 shorter events, 67.5 us)
Async XLA Ops:
  17.4 48.0 %copy-start.77 = (bf16[256,128]{1,0:T(8,128)(2,1)}, bf16[256,128]{1,0:T(8,128)(2,1)S(1)}, u32[]{:S(2)}) copy-start(bf16[256,128]{1,0:T(8,128)(2,1)S(1)} %get-tuple-element.50.asked_marks_ref) | copy-start | bytes 196612
  17.4 23.2 %all-to-all-start.1 = ((bf16[16,16,512]{2,1,0:T(8,128)(2,1)}), bf16[16,16,512]{2,1,0:T(8,128)(2,1)S(1)}, u32[]{:S(2)}, u32[]{:S(2)}) async-start(bf16[16,16,512]{2,1,0:T(8,128)(2,1)} %bitcast.5), calls=%async_computation.1 | async-start | bytes 524288 | tf_op jit(solution)/shard_map/all_to_all | solution.py:503
  30.3 10.2 %copy-start.35 = (bf16[256,384]{1,0:T(8,128)(2,1)}, bf16[256,384]{1,0:T(8,128)(2,1)S(1)}, u32[]{:S(2)}) copy-start(bf16[256,384]{1,0:T(8,128)(2,1)S(1)} %get-tuple-element.46.receivers_ref.cut_receivers_ref) | copy-start | bytes 589828
  30.3 10.2 %copy-start.1 = (bf16[1536,512]{1,0:T(8,128)(2,1)S(1)}, bf16[1536,512]{1,0:T(8,128)(2,1)}, u32[]{:S(2)}) copy-start(bf16[1536,512]{1,0:T(8,128)(2,1)} %w_edge_ref.1) | copy-start | bytes 4718596
  30.3 10.2 %copy-start.3 = (bf16[768,512]{1,0:T(8,128)(2,1)S(1)}, bf16[768,512]{1,0:T(8,128)(2,1)}, u32[]{:S(2)}) copy-start(bf16[768,512]{1,0:T(8,128)(2,1)} %edges_ref.9) | copy-start | bytes 2359300
  30.3 10.3 %copy-start.16 = (bf16[512,512]{1,0:T(8,128)(2,1)S(1)}, bf16[512,512]{1,0:T(8,128)(2,1)}, u32[]{:S(2)}) copy-start(bf16[512,512]{1,0:T(8,128)(2,1)} %w_out_ref.9) | copy-start | bytes 1572868
  30.3 10.3 %copy-start.60 = (bf16[128,512]{1,0:T(8,128)(2,1)S(1)}, bf16[128,512]{1,0:T(8,128)(2,1)}, u32[]{:S(2)}) copy-start(bf16[128,512]{1,0:T(8,128)(2,1)} %nodes_ref.9) | copy-start | bytes 393220
  49.8 15.6 %all-to-all-start.2 = ((bf16[16,16,512]{2,1,0:T(8,128)(2,1)}), bf16[16,16,512]{2,1,0:T(8,128)(2,1)S(1)}, u32[]{:S(2)}, u32[]{:S(2)}) async-start(bf16[16,16,512]{2,1,0:T(8,128)(2,1)} %bitcast.7), calls=%async_computation.2 | async-start | bytes 524288 | tf_op jit(solution)/shard_map/all_to_all | solution.py:503
  74.9 24.0 %collective-permute-start.10 = (bf16[768,512]{1,0:T(8,128)(2,1)}, bf16[768,512]{1,0:T(8,128)(2,1)}, u32[]{:S(2)}, u32[]{:S(2)}) collective-permute-start(bf16[768,512]{1,0:T(8,128)(2,1)} %get-tuple-element.81), channel_id=1, source_target_pairs={{0,1},{1,0},{2,3},{3,2},{4,5},{5,4},{6,7},{7,6},{8,9},{9,8},{10,11... | collective-permute-start | bytes 2359304 | tf_op jit(solution)/shard_map/ppermute | solution.py:470
  75.6 13.6 %all-to-all-start.3 = ((bf16[16,16,512]{2,1,0:T(8,128)(2,1)}), bf16[16,16,512]{2,1,0:T(8,128)(2,1)}, u32[]{:S(2)}, u32[]{:S(2)}) async-start(bf16[16,16,512]{2,1,0:T(8,128)(2,1)} %bitcast.9), calls=%async_computation.3 | async-start | bytes 524288 | tf_op jit(solution)/shard_map/all_to_all | solution.py:503
  86.1 3.1 %copy-start.66 = (bf16[128,512]{1,0:T(8,128)(2,1)S(1)}, bf16[128,512]{1,0:T(8,128)(2,1)}, u32[]{:S(2)}) copy-start(bf16[128,512]{1,0:T(8,128)(2,1)} %copy-done.64) | copy-start | bytes 393220
  88.0 10.1 %copy-start.4 = (bf16[512,512]{1,0:T(8,128)(2,1)}, bf16[512,512]{1,0:T(8,128)(2,1)S(1)}, u32[]{:S(2)}) copy-start(bf16[512,512]{1,0:T(8,128)(2,1)S(1)} %get-tuple-element.62.inner_pre_ref) | copy-start | bytes 1572868
  94.2 1.9 copy-start.33
  94.2 1.9 copy-start.39
  94.2 1.9 copy-start.42
  94.3 1.9 copy-start.45
  96.1 2.1 %copy-start.11 = (bf16[256,512]{1,0:T(8,128)(2,1)}, bf16[256,512]{1,0:T(8,128)(2,1)S(1)}, u32[]{:S(2)}) copy-start(bf16[256,512]{1,0:T(8,128)(2,1)S(1)} %get-tuple-element.65.cut_pre_ref.dep_ref) | copy-start | bytes 786436
  96.1 2.1 %copy-start.47 = (bf16[256,512]{1,0:T(8,128)(2,1)}, bf16[256,512]{1,0:T(8,128)(2,1)S(1)}, u32[]{:S(2)}) copy-start(bf16[256,512]{1,0:T(8,128)(2,1)S(1)} %get-tuple-element.73.cut_out_ref) | copy-start | bytes 786436
  96.1 2.8 %copy-start.56 = (bf16[768,512]{1,0:T(8,128)(2,1)S(1)}, bf16[768,512]{1,0:T(8,128)(2,1)}, u32[]{:S(2)}) copy-start(bf16[768,512]{1,0:T(8,128)(2,1)} %copy-done.55) | copy-start | bytes 2359300
  98.2 19.7 %collective-permute-start = (bf16[1024,512]{1,0:T(8,128)(2,1)}, bf16[1024,512]{1,0:T(8,128)(2,1)}, u32[]{:S(2)}, u32[]{:S(2)}) collective-permute-start(bf16[1024,512]{1,0:T(8,128)(2,1)} %shard_map.188.dep_ref), channel_id=1, source_target_pairs={{0,1},{1,0},{2,3},{3,2},{4,5},{5,4},{6,7},{7,6},{8,9},{9,8},{10,11... | collective-permute-start | bytes 3145736 | tf_op jit(solution)/shard_map/ppermute | solution.py:470
  101.9 11.2 %collective-permute-start.11 = (bf16[384,512]{1,0:T(8,128)(2,1)}, bf16[384,512]{1,0:T(8,128)(2,1)}, u32[]{:S(2)}, u32[]{:S(2)}) collective-permute-start(bf16[384,512]{1,0:T(8,128)(2,1)} %dynamic-slice_bitcast_fusion.1), channel_id=1, source_target_pairs={{0,2},{1,3},{2,0},{3,1},{4,6},{5,7},{6,4},{7,5},{8,10},{9,11},{10,... | collective-permute-start | bytes 1179656 | tf_op jit(solution)/shard_map/ppermute | solution.py:480
  114.2 6.7 %collective-permute-start.14 = (bf16[96,512]{1,0:T(8,128)(2,1)S(1)}, bf16[96,512]{1,0:T(8,128)(2,1)S(1)}, u32[]{:S(2)}, u32[]{:S(2)}) collective-permute-start(bf16[96,512]{1,0:T(8,128)(2,1)S(1)} %get-tuple-element.90), channel_id=1, source_target_pairs={{0,12},{1,13},{2,14},{3,15},{4,8},{5,9},{6,10},{7,11},{8,4},{9,5},... | collective-permute-start | bytes 294920 | tf_op jit(solution)/shard_map/ppermute | solution.py:480
  117.3 8.1 %collective-permute-start.13 = (bf16[96,512]{1,0:T(8,128)(2,1)S(1)}, bf16[96,512]{1,0:T(8,128)(2,1)S(1)}, u32[]{:S(2)}, u32[]{:S(2)}) collective-permute-start(bf16[96,512]{1,0:T(8,128)(2,1)S(1)} %get-tuple-element.91), channel_id=1, source_target_pairs={{0,8},{1,9},{2,10},{3,11},{4,12},{5,13},{6,14},{7,15},{8,0},{9,1},... | collective-permute-start | bytes 294920 | tf_op jit(solution)/shard_map/ppermute | solution.py:480
  117.3 8.1 %collective-permute-start.12 = (bf16[96,512]{1,0:T(8,128)(2,1)S(1)}, bf16[96,512]{1,0:T(8,128)(2,1)S(1)}, u32[]{:S(2)}, u32[]{:S(2)}) collective-permute-start(bf16[96,512]{1,0:T(8,128)(2,1)S(1)} %get-tuple-element.89), channel_id=1, source_target_pairs={{0,4},{1,5},{2,6},{3,7},{4,0},{5,1},{6,2},{7,3},{8,12},{9,13},{10,... | collective-permute-start | bytes 294920 | tf_op jit(solution)/shard_map/ppermute | solution.py:480
  119.4 12.0 %collective-permute-start.1 = (bf16[512,512]{1,0:T(8,128)(2,1)S(1)}, bf16[512,512]{1,0:T(8,128)(2,1)S(1)}, u32[]{:S(2)}, u32[]{:S(2)}) collective-permute-start(bf16[512,512]{1,0:T(8,128)(2,1)S(1)} %dynamic-slice_bitcast_fusion), channel_id=1, source_target_pairs={{0,2},{1,3},{2,0},{3,1},{4,6},{5,7},{6,4},{7,5},{8,10},{9,11},{10,... | collective-permute-start | bytes 1572872 | tf_op jit(solution)/shard_map/ppermute | solution.py:480
  125.5 3.8 %collective-permute-start.15 = (bf16[96,512]{1,0:T(8,128)(2,1)S(1)}, bf16[96,512]{1,0:T(8,128)(2,1)S(1)}, u32[]{:S(2)}, u32[]{:S(2)}) collective-permute-start(bf16[96,512]{1,0:T(8,128)(2,1)S(1)} %get-tuple-element.83), channel_id=1, source_target_pairs={{0,4},{1,5},{2,6},{3,7},{4,0},{5,1},{6,2},{7,3},{8,12},{9,13},{10,... | collective-permute-start | bytes 294920 | tf_op jit(solution)/shard_map/ppermute | solution.py:494
  125.6 9.6 %collective-permute-start.16 = (bf16[96,512]{1,0:T(8,128)(2,1)S(1)}, bf16[96,512]{1,0:T(8,128)(2,1)S(1)}, u32[]{:S(2)}, u32[]{:S(2)}) collective-permute-start(bf16[96,512]{1,0:T(8,128)(2,1)S(1)} %get-tuple-element.83), channel_id=1, source_target_pairs={{0,8},{1,9},{2,10},{3,11},{4,12},{5,13},{6,14},{7,15},{8,0},{9,1},... | collective-permute-start | bytes 294920 | tf_op jit(solution)/shard_map/ppermute | solution.py:494
  128.0 19.5 %collective-permute-start.17 = (bf16[96,512]{1,0:T(8,128)(2,1)S(1)}, bf16[96,512]{1,0:T(8,128)(2,1)S(1)}, u32[]{:S(2)}, u32[]{:S(2)}) collective-permute-start(bf16[96,512]{1,0:T(8,128)(2,1)S(1)} %get-tuple-element.83), channel_id=1, source_target_pairs={{0,12},{1,13},{2,14},{3,15},{4,8},{5,9},{6,10},{7,11},{8,4},{9,5},... | collective-permute-start | bytes 294920 | tf_op jit(solution)/shard_map/ppermute | solution.py:494
  131.6 5.7 %collective-permute-start.4 = (bf16[128,512]{1,0:T(8,128)(2,1)S(1)}, bf16[128,512]{1,0:T(8,128)(2,1)S(1)}, u32[]{:S(2)}, u32[]{:S(2)}) collective-permute-start(bf16[128,512]{1,0:T(8,128)(2,1)S(1)} %get-tuple-element.87), channel_id=1, source_target_pairs={{0,12},{1,13},{2,14},{3,15},{4,8},{5,9},{6,10},{7,11},{8,4},{9,5},... | collective-permute-start | bytes 393224 | tf_op jit(solution)/shard_map/ppermute | solution.py:480
  134.8 12.4 %collective-permute-start.3 = (bf16[128,512]{1,0:T(8,128)(2,1)S(1)}, bf16[128,512]{1,0:T(8,128)(2,1)S(1)}, u32[]{:S(2)}, u32[]{:S(2)}) collective-permute-start(bf16[128,512]{1,0:T(8,128)(2,1)S(1)} %get-tuple-element.88), channel_id=1, source_target_pairs={{0,8},{1,9},{2,10},{3,11},{4,12},{5,13},{6,14},{7,15},{8,0},{9,1},... | collective-permute-start | bytes 393224 | tf_op jit(solution)/shard_map/ppermute | solution.py:480
  134.8 12.4 %collective-permute-start.2 = (bf16[128,512]{1,0:T(8,128)(2,1)S(1)}, bf16[128,512]{1,0:T(8,128)(2,1)S(1)}, u32[]{:S(2)}, u32[]{:S(2)}) collective-permute-start(bf16[128,512]{1,0:T(8,128)(2,1)S(1)} %get-tuple-element.86), channel_id=1, source_target_pairs={{0,4},{1,5},{2,6},{3,7},{4,0},{5,1},{6,2},{7,3},{8,12},{9,13},{10,... | collective-permute-start | bytes 393224 | tf_op jit(solution)/shard_map/ppermute | solution.py:480
  147.4 5.7 %collective-permute-start.5 = (bf16[128,512]{1,0:T(8,128)(2,1)S(1)}, bf16[128,512]{1,0:T(8,128)(2,1)S(1)}, u32[]{:S(2)}, u32[]{:S(2)}) collective-permute-start(bf16[128,512]{1,0:T(8,128)(2,1)S(1)} %get-tuple-element.85), channel_id=1, source_target_pairs={{0,4},{1,5},{2,6},{3,7},{4,0},{5,1},{6,2},{7,3},{8,12},{9,13},{10,... | collective-permute-start | bytes 393224 | tf_op jit(solution)/shard_map/ppermute | solution.py:494
  147.5 13.8 %collective-permute-start.18 = (bf16[384,512]{1,0:T(8,128)(2,1)S(1)}, bf16[384,512]{1,0:T(8,128)(2,1)S(1)}, u32[]{:S(2)}, u32[]{:S(2)}) collective-permute-start(bf16[384,512]{1,0:T(8,128)(2,1)S(1)} %bitcast.111), channel_id=1, source_target_pairs={{0,2},{1,3},{2,0},{3,1},{4,6},{5,7},{6,4},{7,5},{8,10},{9,11},{10,... | collective-permute-start | bytes 1179656 | tf_op jit(solution)/shard_map/ppermute | solution.py:494
  149.5 6.2 %collective-permute-start.6 = (bf16[128,512]{1,0:T(8,128)(2,1)S(1)}, bf16[128,512]{1,0:T(8,128)(2,1)S(1)}, u32[]{:S(2)}, u32[]{:S(2)}) collective-permute-start(bf16[128,512]{1,0:T(8,128)(2,1)S(1)} %get-tuple-element.85), channel_id=1, source_target_pairs={{0,8},{1,9},{2,10},{3,11},{4,12},{5,13},{6,14},{7,15},{8,0},{9,1},... | collective-permute-start | bytes 393224 | tf_op jit(solution)/shard_map/ppermute | solution.py:494
  151.7 6.6 %collective-permute-start.7 = (bf16[128,512]{1,0:T(8,128)(2,1)S(1)}, bf16[128,512]{1,0:T(8,128)(2,1)S(1)}, u32[]{:S(2)}, u32[]{:S(2)}) collective-permute-start(bf16[128,512]{1,0:T(8,128)(2,1)S(1)} %get-tuple-element.85), channel_id=1, source_target_pairs={{0,12},{1,13},{2,14},{3,15},{4,8},{5,9},{6,10},{7,11},{8,4},{9,5},... | collective-permute-start | bytes 393224 | tf_op jit(solution)/shard_map/ppermute | solution.py:494
  158.4 9.9 %collective-permute-start.8 = (bf16[512,512]{1,0:T(8,128)(2,1)S(1)}, bf16[512,512]{1,0:T(8,128)(2,1)S(1)}, u32[]{:S(2)}, u32[]{:S(2)}) collective-permute-start(bf16[512,512]{1,0:T(8,128)(2,1)S(1)} %bitcast.109), channel_id=1, source_target_pairs={{0,2},{1,3},{2,0},{3,1},{4,6},{5,7},{6,4},{7,5},{8,10},{9,11},{10,... | collective-permute-start | bytes 1572872 | tf_op jit(solution)/shard_map/ppermute | solution.py:494
  162.1 34.5 %collective-permute-start.19 = (bf16[768,512]{1,0:T(8,128)(2,1)}, bf16[768,512]{1,0:T(8,128)(2,1)}, u32[]{:S(2)}, u32[]{:S(2)}) collective-permute-start(bf16[768,512]{1,0:T(8,128)(2,1)} %bitcast.50), channel_id=1, source_target_pairs={{0,1},{1,0},{2,3},{3,2},{4,5},{5,4},{6,7},{7,6},{8,9},{9,8},{10,11... | collective-permute-start | bytes 2359304 | tf_op jit(solution)/shard_map/ppermute | solution.py:494
  166.4 7.2 %copy-start.6 = (bf16[512,512]{1,0:T(8,128)(2,1)S(1)}, bf16[512,512]{1,0:T(8,128)(2,1)}, u32[]{:S(2)}) copy-start(bf16[512,512]{1,0:T(8,128)(2,1)} %copy-done.4) | copy-start | bytes 1572868
  166.4 7.2 %copy-start.13 = (bf16[256,512]{1,0:T(8,128)(2,1)S(1)}, bf16[256,512]{1,0:T(8,128)(2,1)}, u32[]{:S(2)}) copy-start(bf16[256,512]{1,0:T(8,128)(2,1)} %copy-done.11) | copy-start | bytes 786436
  166.4 7.2 %copy-start.37 = (bf16[256,384]{1,0:T(8,128)(2,1)S(1)}, bf16[256,384]{1,0:T(8,128)(2,1)}, u32[]{:S(2)}) copy-start(bf16[256,384]{1,0:T(8,128)(2,1)} %copy-done.35) | copy-start | bytes 589828
  166.4 7.2 %copy-start.54 = (bf16[256,384]{1,0:T(8,128)(2,1)S(1)}, bf16[256,384]{1,0:T(8,128)(2,1)}, u32[]{:S(2)}) copy-start(bf16[256,384]{1,0:T(8,128)(2,1)} %copy-done.52) | copy-start | bytes 589828
  166.4 7.2 %copy-start.63 = (bf16[512,128]{1,0:T(8,128)(2,1)S(1)}, bf16[512,128]{1,0:T(8,128)(2,1)}, u32[]{:S(2)}) copy-start(bf16[512,128]{1,0:T(8,128)(2,1)} %copy-done.61) | copy-start | bytes 393220
  166.4 7.2 %copy-start.84 = (bf16[512,128]{1,0:T(8,128)(2,1)S(1)}, bf16[512,128]{1,0:T(8,128)(2,1)}, u32[]{:S(2)}) copy-start(bf16[512,128]{1,0:T(8,128)(2,1)} %copy-done.83) | copy-start | bytes 393220
  169.1 32.0 %collective-permute-start.9 = (bf16[1024,512]{1,0:T(8,128)(2,1)}, bf16[1024,512]{1,0:T(8,128)(2,1)}, u32[]{:S(2)}, u32[]{:S(2)}) collective-permute-start(bf16[1024,512]{1,0:T(8,128)(2,1)} %bitcast.31), channel_id=1, source_target_pairs={{0,1},{1,0},{2,3},{3,2},{4,5},{5,4},{6,7},{7,6},{8,9},{9,8},{10,11... | collective-permute-start | bytes 3145736 | tf_op jit(solution)/shard_map/ppermute | solution.py:494
  176.3 17.1 %all-to-all-start.4 = ((bf16[16,16,512]{2,1,0:T(8,128)(2,1)}), bf16[16,16,512]{2,1,0:T(8,128)(2,1)}, u32[]{:S(2)}, u32[]{:S(2)}) async-start(bf16[16,16,512]{2,1,0:T(8,128)(2,1)} %bitcast.94), calls=%async_computation.4 | async-start | bytes 524288 | tf_op jit(solution)/shard_map/all_to_all | solution.py:503
  187.7 5.7 %copy-start.70 = (f32[128,512]{1,0:T(8,128)S(1)}, f32[128,512]{1,0:T(8,128)}, u32[]{:S(2)}) copy-start(f32[128,512]{1,0:T(8,128)} %copy-done.69) | copy-start | bytes 786436
  187.7 5.7 %copy-start.74 = (f32[128,512]{1,0:T(8,128)S(1)}, f32[128,512]{1,0:T(8,128)}, u32[]{:S(2)}) copy-start(f32[128,512]{1,0:T(8,128)} %copy-done.73) | copy-start | bytes 786436
  187.7 5.7 %copy-start.78 = (bf16[256,128]{1,0:T(8,128)(2,1)S(1)}, bf16[256,128]{1,0:T(8,128)(2,1)}, u32[]{:S(2)}) copy-start(bf16[256,128]{1,0:T(8,128)(2,1)} %copy-done.77) | copy-start | bytes 196612
  (68 other events, 67.3 us)
where the time goes:
time: 207 us; the launch traced here: 205 us
  local copies, waits for them, and re-layouts  73 us (35%)
  starting transfers between devices  51.1 us (25%)
  waiting for transfers between devices  38.1 us (18%)
  Pallas kernels  24 us (12%)
  blocking collectives  12.9 us (6%)
  other arithmetic  4.22 us (2%)
    unnamed x186, local copies, waits for them, and re-layouts  57.5 us
    pallas_call x15, Pallas kernels, run(): pl.pallas_call(body, out_shape=out_shape, in_specs=[VMEM] * len(ins) if s...  24 us
    all_to_all x4, starting transfers between devices, exchange(): lax.all_to_all(split, 'dom', split_axis=0, concat_axis=0, tiled=True)  21.8 us
    ppermute x10, starting transfers between devices, gather_rows(): piece = lax.ppermute(rows, 'dom', partner_pairs(devices, turn << low))  19.2 us
    ppermute x8, waiting for transfers between devices, reduce_rows(): lax.ppermute(sent, 'dom', partner_pairs(devices, turn << low)).astype(F32)  18.6 us
    all_to_all x4, waiting for transfers between devices, exchange(): lax.all_to_all(split, 'dom', split_axis=0, concat_axis=0, tiled=True)  14.1 us
    all_to_all x1, blocking collectives, shards(): asked = lax.all_to_all(ask, 'dom', split_axis=0, concat_axis=0, tiled=True)  12.9 us
    ppermute x8, starting transfers between devices, reduce_rows(): lax.ppermute(sent, 'dom', partner_pairs(devices, turn << low)).astype(F32)  8.76 us
  transfers between devices with their start and end apart: 24, of which 10 were waited for; matrix products, arithmetic and copies ran while one was open for 9% of the time, Pallas kernels for 8%

commit v1 on v0

--- a/solution.py
+++ b/solution.py
@@ -9,7 +9,7 @@
 
 BF16 = jnp.bfloat16
 F32 = jnp.float32
-VMEM_LIMIT = 40 * 1024 * 1024
+VMEM_LIMIT = 60 * 1024 * 1024
 
 
 def dot(left, right):
@@ -86,7 +86,7 @@
 
 def ask_kernel(dest_ref, remote_ref, ask_ref):
     domains, slots = ask_ref.shape
-    dest_marks, rank = slot_ranks(dest_ref[...], domains)
+    dest_marks, rank = slot_ranks(to_column(dest_ref[...]).astype(jnp.int32), domains)
     rank_marks = jnp.where(rank == iota((rank.shape[0], slots), 1).astype(F32), 1.0, 0.0)
     wanted = (rank_marks * to_column(remote_ref[...])).astype(BF16)
     ask_ref[...] = dot_rows(dest_marks, wanted).astype(jnp.int32)
@@ -109,7 +109,7 @@
 def cut_marks_kernel(dest_ref, local_ref, dep_ref, senders_ref, receivers_ref, *, domains, slots):
     width = senders_ref.shape[1]
     base = width - domains * slots
-    dest = dest_ref[...]
+    dest = to_column(dest_ref[...]).astype(jnp.int32)
     _, rank = slot_ranks(dest, domains)
     second = dest * slots + rank.astype(jnp.int32) + base
     first = to_column(local_ref[...]).astype(jnp.int32)
@@ -147,8 +147,8 @@
     scale_ref,
     total_ref,
 ):
-    pairs = pairs_ref[...]
-    senders, receivers = pair_marks(pairs[:, 0:1], pairs[:, 1:2], nodes_ref.shape[0])
+    first, second = (to_column(pairs_ref[side : side + 1]).astype(jnp.int32) for side in range(2))
+    senders, receivers = pair_marks(first, second, nodes_ref.shape[0])
     senders_ref[...] = senders
     receivers_ref[...] = receivers
     nodes = nodes_ref[...]
@@ -529,13 +529,13 @@
     mine, other = place.reshape(1), (1 - place).reshape(1)
 
     ask = run(
-        ask_kernel, shaped(jnp.int32, domains, slots), [cut_dest, cut_remote.reshape(1, -1)], 10**7
+        ask_kernel, shaped(jnp.int32, domains, slots), [cut_dest.reshape(1, -1), cut_remote.reshape(1, -1)], 10**7
     )
     asked = lax.all_to_all(ask, "dom", split_axis=0, concat_axis=0, tiled=True)
     cut_senders, cut_receivers = run(
         functools.partial(cut_marks_kernel, domains=domains, slots=slots),
         [shaped(BF16, cut_rows, table)] * 2,
-        [cut_dest, cut_local.reshape(1, -1), ask],
+        [cut_dest.reshape(1, -1), cut_local.reshape(1, -1), ask],
         10**8,
         [VMEM, VMEM, ANY],
     )
@@ -572,10 +572,10 @@
         inner_forward_kernel,
         [shaped(kind, inner_rows, width) for kind, width in zip(saved_types, saved_widths)]
         + [shaped(F32, node_rows, latent)],
-        [inner_pairs, edges, nodes, w_edge_in, w_edge_out, reply],
+        [inner_pairs.T, edges, nodes, w_edge_in, w_edge_out, reply],
         inner_rows * 4 * square,
         [
-            rows_spec(2, block // 2),
+            pl.BlockSpec((2, block // 2), lambda step: (0, step)),
             rows_spec(latent),
             all_spec(nodes),
             all_spec(w_edge_in),

time: 207 us -> 180 us (0.87)
  local copies, waits for them, and re-layouts: 73 us -> 9.01 us
  Pallas kernels: 24 us -> 51.4 us
  waiting for transfers between devices: 38.1 us -> 55.9 us
  starting transfers between devices: 51.1 us -> 46.9 us
  other arithmetic: 4.22 us -> 0.89 us
    unnamed x186 -> x12, local copies, waits for them, and re-layouts: 57.5 us -> 2.82 us
    pallas_call x15, Pallas kernels: 24 us -> 51.4 us  [run(): pl.pallas_call(body, out_shape=out_shape, in_specs=[VMEM] * len(ins) if s...]
    ppermute x8, waiting for transfers between devices: 18.6 us -> 26.9 us  [reduce_rows(): lax.ppermute(sent, 'dom', partner_pairs(devices, turn << low)).astype(F32)]
    dynamic_update_slice x14, local copies, waits for them, and re-layouts: 8.33 us -> 1.68 us  [gather_rows(): whole = lax.dynamic_update_index_in_dim(whole, piece, place ^ turn, 0)]
    all_to_all x4, waiting for transfers between devices: 14.1 us -> 19.5 us  [exchange(): lax.all_to_all(split, 'dom', split_axis=0, concat_axis=0, tiled=True)]
    ppermute x10, waiting for transfers between devices: 5.5 us -> 9.52 us  [gather_rows(): piece = lax.ppermute(rows, 'dom', partner_pairs(devices, turn << low))]
    convert_element_type x2, other arithmetic: 2.85 us -> 0.51 us  [reduce_rows(): rows = (keep.astype(F32) + received.astype(F32)).astype(BF16)]
  transfers between devices with their start and end apart: 24 -> 24, of which waited for: 10 -> 14; matrix products, arithmetic and copies ran while one was open for 9% -> 3% of each run, Pallas kernels for 8% -> 20%
where the time goes in v1:
time: 180 us; the launch traced here: 178 us
  waiting for transfers between devices  55.9 us (31%)
  Pallas kernels  51.4 us (29%)
  starting transfers between devices  46.9 us (26%)
  blocking collectives  13.1 us (7%)
  local copies, waits for them, and re-layouts  9.01 us (5%)
    pallas_call x15, Pallas kernels, run(): pl.pallas_call(body, out_shape=out_shape, in_specs=[VMEM] * len(ins) if s...  51.4 us
    ppermute x8, waiting for transfers between devices, reduce_rows(): lax.ppermute(sent, 'dom', partner_pairs(devices, turn << low)).astype(F32)  26.9 us
    all_to_all x4, starting transfers between devices, exchange(): lax.all_to_all(split, 'dom', split_axis=0, concat_axis=0, tiled=True)  19.8 us
    all_to_all x4, waiting for transfers between devices, exchange(): lax.all_to_all(split, 'dom', split_axis=0, concat_axis=0, tiled=True)  19.5 us
    ppermute x10, starting transfers between devices, gather_rows(): piece = lax.ppermute(rows, 'dom', partner_pairs(devices, turn << low))  18.4 us
    all_to_all x1, blocking collectives, shards(): asked = lax.all_to_all(ask, 'dom', split_axis=0, concat_axis=0, tiled=True)  13.1 us
    ppermute x10, waiting for transfers between devices, gather_rows(): piece = lax.ppermute(rows, 'dom', partner_pairs(devices, turn << low))  9.52 us
    ppermute x8, starting transfers between devices, reduce_rows(): lax.ppermute(sent, 'dom', partner_pairs(devices, turn << low)).astype(F32)  7.37 us
  transfers between devices with their start and end apart: 24, of which 14 were waited for; matrix products, arithmetic and copies ran while one was open for 3% of the time, Pallas kernels for 20%

profile of v1, /device:TPU:1, one launch (start us, length us, event | category | flops | bytes accessed | tf_op | source)
XLA Modules:
  0.0 178.1 jit_solution(6840297789925814546)
XLA Ops:
  0.6 1.7 shard_map.179.dep_ref
  2.3 13.1 %all_to_all.31 = s32[16,1,16]{2,1,0:T(1,128)} all-to-all(s32[16,1,16]{2,1,0:T(1,128)} %bitcast.122), channel_id=1, replica_groups=mesh['groups'=2,'dom'=16] {'dom'}, dimensions={0} | all-to-all | bytes 2048 | tf_op jit(solution)/shard_map/all_to_all | solution.py:534
  15.5 2.0 %shard_map.181 = (bf16[256,512]{1,0:T(8,128)(2,1)}, bf16[256,128]{1,0:T(8,128)(2,1)}) custom-call(s32[16,16]{1,0:T(8,128)} %bitcast.123, bf16[128,512]{1,0:T(8,128)(2,1)} %nodes_ref.9), custom_call_target="tpu_custom_call" | custom-call | flops 100000000 | bytes 459776 | tf_op jit(solution)/shard_map/pallas_call | solution.py:441
  17.5 3.9 %all-to-all-start.1 = ((bf16[16,16,512]{2,1,0:T(8,128)(2,1)}), bf16[16,16,512]{2,1,0:T(8,128)(2,1)S(1)}, u32[]{:S(2)}, u32[]{:S(2)}) async-start(bf16[16,16,512]{2,1,0:T(8,128)(2,1)} %bitcast.121), calls=%async_computation.1 | async-start | bytes 524288 | tf_op jit(solution)/shard_map/all_to_all | solution.py:503
  21.4 2.0 %shard_map.180 = (bf16[256,384]{1,0:T(8,128)(2,1)}, bf16[256,384]{1,0:T(8,128)(2,1)}) custom-call(s32[1,128]{1,0:T(1,128)} %bitcast.127, s32[1,128]{1,0:T(1,128)} %bitcast.128, s32[16,16]{1,0:T(8,128)} %shard_map.179.dep_ref), custom_call_target="tpu_custom_call" | custom-call | flops 100000000 | bytes 395264 | tf_op jit(solution)/shard_map/pallas_call | solution.py:441
  23.4 6.3 %shard_map.182 = (bf16[512,128]{1,0:T(8,128)(2,1)}, bf16[512,128]{1,0:T(8,128)(2,1)}, bf16[512,512]{1,0:T(8,128)(2,1)}, bf16[512,512]{1,0:T(8,128)(2,1)}, bf16[5...) custom-call(s32[2,256]{1,0:T(2,128)} %bitcast.124, ...), custom_call_target="tpu_custom_call" | custom-call | flops 1073741824 | bytes 7475200 | tf_op jit(solution)/shard_map/pallas_call | solution.py:441
  29.7 1.3 all-to-all-done.1
  31.6 4.3 %shard_map.183 = (bf16[256,512]{1,0:T(8,128)(2,1)}, bf16[256,512]{1,0:T(8,128)(2,1)}, bf16[256,512]{1,0:T(8,128)(2,1)}, f32[256,512]{1,0:T(8,128)}, f32[256,512]...) custom-call(bf16[256,384]{1,0:T(8,128)(2,1)} %get-tuple-element.45.senders_ref.cut_senders_ref, ...), custom_call_target="tpu_custom_call" | custom-call | flops 536870912 | bytes 6292480 | tf_op jit(solution)/shard_map/pallas_call | solution.py:441
  35.9 4.9 %all-to-all-start.2 = ((bf16[16,16,512]{2,1,0:T(8,128)(2,1)}), bf16[16,16,512]{2,1,0:T(8,128)(2,1)S(1)}, u32[]{:S(2)}, u32[]{:S(2)}) async-start(bf16[16,16,512]{2,1,0:T(8,128)(2,1)} %bitcast.118), calls=%async_computation.2 | async-start | bytes 524288 | tf_op jit(solution)/shard_map/all_to_all | solution.py:503
  40.8 9.5 %all-to-all-done.2 = bf16[16,16,512]{2,1,0:T(8,128)(2,1)S(1)} async-done(((bf16[16,16,512]{2,1,0:T(8,128)(2,1)}), bf16[16,16,512]{2,1,0:T(8,128)(2,1)S(1)}, u32[]{:S(2)}, u32[]{:S(2)}) %all-to-all-start.2) | async-done | bytes 262176 | tf_op jit(solution)/shard_map/all_to_all | solution.py:503
  50.3 0.7 copy-done.3
  51.0 4.1 %shard_map.184 = (bf16[128,512]{1,0:T(8,128)(2,1)}, f32[128,512]{1,0:T(8,128)}, bf16[128,512]{1,0:T(8,128)(2,1)}, bf16[256,512]{1,0:T(8,128)(2,1)}, bf16[128,512...) custom-call(bf16[256,512]{1,0:T(8,128)(2,1)} %bitcast.117, ...), custom_call_target="tpu_custom_call" | custom-call | flops 402653184 | bytes 3735552 | tf_op jit(solution)/shard_map/pallas_call | solution.py:441
  55.1 2.9 %shard_map.193 = (bf16[768,512]{1,0:T(8,128)(2,1)}, bf16[768,512]{1,0:T(8,128)(2,1)}) custom-call(s32[1]{0:T(128)} %bitcast.13.place_ref, bf16[128,512]{1,0:T(8,128)(2,1)} %nodes_ref.9, bf16[128,512]{1,0:T(8,128)(2,1)} %get-tuple-element.76.aggregate_ref, bf16[128,512]{1,0:T(8,128)(2,1)} %get-tuple-element.77.hidden_ref, ...), custom_call_target="tpu_custom_call" | custom-call | flops 201326592 | bytes 2228228 | tf_op jit(solution)/shard_map/pallas_call | solution.py:441
  58.6 3.4 %all-to-all-start.3 = ((bf16[16,16,512]{2,1,0:T(8,128)(2,1)}), bf16[16,16,512]{2,1,0:T(8,128)(2,1)S(1)}, u32[]{:S(2)}, u32[]{:S(2)}) async-start(bf16[16,16,512]{2,1,0:T(8,128)(2,1)} %bitcast.115), calls=%async_computation.3 | async-start | bytes 524288 | tf_op jit(solution)/shard_map/all_to_all | solution.py:503
  62.1 3.6 %shard_map.186 = (bf16[512,512]{1,0:T(8,128)(2,1)}, bf16[512,512]{1,0:T(8,128)(2,1)}) custom-call(bf16[512,128]{1,0:T(8,128)(2,1)} %get-tuple-element.57.receivers_ref.inner_receivers_ref, bf16[128,512]{1,0:T(8,128)(2,1)} %get-tuple-element.58.agg_grad_ref, bf16[768,512]{1,0:T(8,128)(2,1)} %ct_ref.7, f32[512,512]{1,0:T(8,128)} %get-tuple-element.53.inner_ref.normed_ref, ...), custom_call_target="tpu_custom_call" | custom-call | flops 268435456 | bytes 4982784 | tf_op jit(solution)/shard_map/pallas_call | solution.py:441
  65.7 5.8 %all-to-all-done.3 = bf16[16,16,512]{2,1,0:T(8,128)(2,1)S(1)} async-done(((bf16[16,16,512]{2,1,0:T(8,128)(2,1)}), bf16[16,16,512]{2,1,0:T(8,128)(2,1)S(1)}, u32[]{:S(2)}, u32[]{:S(2)}) %all-to-all-start.3) | async-done | bytes 262176 | tf_op jit(solution)/shard_map/all_to_all | solution.py:503
  72.2 3.1 %shard_map.187 = (bf16[256,512]{1,0:T(8,128)(2,1)}, bf16[256,512]{1,0:T(8,128)(2,1)}) custom-call(bf16[256,384]{1,0:T(8,128)(2,1)} %get-tuple-element.46.receivers_ref.cut_receivers_ref, bf16[128,512]{1,0:T(8,128)(2,1)} %get-tuple-element.58.agg_grad_ref, bf16[256,512]{1,0:T(8,128)(2,1)} %bitcast.116, bf16[768,512]{1,0:T(8,128)(2,1)} %ct_ref.7, ...), custom_call_target="tpu_custom_call" | custom-call | flops 134217728 | bytes 3474432 | tf_op jit(solution)/shard_map/pallas_call | solution.py:441
  75.3 4.3 %shard_map.188.dep_ref = bf16[1024,512]{1,0:T(8,128)(2,1)} custom-call(s32[1]{0:T(128)} %bitcast.14.place_ref, bf16[768,512]{1,0:T(8,128)(2,1)} %edges_ref.9, bf16[512,512]{1,0:T(8,128)(2,1)} %get-tuple-element.66.inner_sender_ref, bf16[256,512]{1,0:T(8,128)(2,1)} %get-tuple-element.67.cut_sender_ref, bf16[512,512]{1,0:T(8,128)(2,1)} %get-tuple-element.68.inner_receiver_ref, ...), custom_call_target="tpu_custom_call" | custom-call | flops 805306368 | bytes 6029316 | tf_op jit(solution)/shard_map/pallas_call | solution.py:441
  80.7 4.5 %shard_map.189.dep_ref = bf16[1024,512]{1,0:T(8,128)(2,1)} custom-call(s32[1]{0:T(128)} %bitcast.13.place_ref, bf16[768,512]{1,0:T(8,128)(2,1)} %edges_ref.9, bf16[512,512]{1,0:T(8,128)(2,1)} %get-tuple-element.66.inner_sender_ref, bf16[256,512]{1,0:T(8,128)(2,1)} %get-tuple-element.67.cut_sender_ref, bf16[512,512]{1,0:T(8,128)(2,1)} %get-tuple-element.68.inner_receiver_ref, ...), custom_call_target="tpu_custom_call" | custom-call | flops 805306368 | bytes 6815748 | tf_op jit(solution)/shard_map/pallas_call | solution.py:441
  85.2 6.2 %collective-permute-done.11 = bf16[384,512]{1,0:T(8,128)(2,1)S(1)} collective-permute-done((bf16[384,512]{1,0:T(8,128)(2,1)S(1)}, bf16[384,512]{1,0:T(8,128)(2,1)S(1)}, u32[]{:S(2)}, u32[]{:S(2)}) %collective-permute-start.11) | collective-permute-done | bytes 393248 | tf_op jit(solution)/shard_map/ppermute | solution.py:480
  92.4 2.7 %collective-permute-start.12 = (bf16[96,512]{1,0:T(8,128)(2,1)S(1)}, bf16[96,512]{1,0:T(8,128)(2,1)S(1)}, u32[]{:S(2)}, u32[]{:S(2)}) collective-permute-start(bf16[96,512]{1,0:T(8,128)(2,1)S(1)} %get-tuple-element.89), channel_id=1, source_target_pairs={{0,4},{1,5},{2,6},{3,7},{4,0},{5,1},{6,2},{7,3},{8,12},{9,13},{10,... | collective-permute-start | bytes 294920 | tf_op jit(solution)/shard_map/ppermute | solution.py:480
  95.6 1.5 collective-permute-done.14
  97.1 4.8 %collective-permute-done.13 = bf16[96,512]{1,0:T(8,128)(2,1)S(1)} collective-permute-done((bf16[96,512]{1,0:T(8,128)(2,1)S(1)}, bf16[96,512]{1,0:T(8,128)(2,1)S(1)}, u32[]{:S(2)}, u32[]{:S(2)}) %collective-permute-start.13) | collective-permute-done | bytes 98336 | tf_op jit(solution)/shard_map/ppermute | solution.py:480
  102.1 2.1 %collective-permute-start.16 = (bf16[96,512]{1,0:T(8,128)(2,1)S(1)}, bf16[96,512]{1,0:T(8,128)(2,1)S(1)}, u32[]{:S(2)}, u32[]{:S(2)}) collective-permute-start(bf16[96,512]{1,0:T(8,128)(2,1)S(1)} %get-tuple-element.83), channel_id=1, source_target_pairs={{0,8},{1,9},{2,10},{3,11},{4,12},{5,13},{6,14},{7,15},{8,0},{9,1},... | collective-permute-start | bytes 294920 | tf_op jit(solution)/shard_map/ppermute | solution.py:494
  104.2 1.4 collective-permute-start.17
  105.8 1.5 collective-permute-done.1
  108.0 1.1 collective-permute-start.3
  109.1 2.1 %collective-permute-start.2 = (bf16[128,512]{1,0:T(8,128)(2,1)S(1)}, bf16[128,512]{1,0:T(8,128)(2,1)S(1)}, u32[]{:S(2)}, u32[]{:S(2)}) collective-permute-start(bf16[128,512]{1,0:T(8,128)(2,1)S(1)} %get-tuple-element.86), channel_id=1, source_target_pairs={{0,4},{1,5},{2,6},{3,7},{4,0},{5,1},{6,2},{7,3},{8,12},{9,13},{10,... | collective-permute-start | bytes 393224 | tf_op jit(solution)/shard_map/ppermute | solution.py:480
  111.2 2.2 %collective-permute-done.4 = bf16[128,512]{1,0:T(8,128)(2,1)S(1)} collective-permute-done((bf16[128,512]{1,0:T(8,128)(2,1)S(1)}, bf16[128,512]{1,0:T(8,128)(2,1)S(1)}, u32[]{:S(2)}, u32[]{:S(2)}) %collective-permute-start.4) | collective-permute-done | bytes 131104 | tf_op jit(solution)/shard_map/ppermute | solution.py:480
  113.3 10.7 %collective-permute-done.3 = bf16[128,512]{1,0:T(8,128)(2,1)S(1)} collective-permute-done((bf16[128,512]{1,0:T(8,128)(2,1)S(1)}, bf16[128,512]{1,0:T(8,128)(2,1)S(1)}, u32[]{:S(2)}, u32[]{:S(2)}) %collective-permute-start.3) | collective-permute-done | bytes 131104 | tf_op jit(solution)/shard_map/ppermute | solution.py:480
  124.4 2.4 %collective-permute-start.6 = (bf16[128,512]{1,0:T(8,128)(2,1)S(1)}, bf16[128,512]{1,0:T(8,128)(2,1)S(1)}, u32[]{:S(2)}, u32[]{:S(2)}) collective-permute-start(bf16[128,512]{1,0:T(8,128)(2,1)S(1)} %get-tuple-element.85), channel_id=1, source_target_pairs={{0,8},{1,9},{2,10},{3,11},{4,12},{5,13},{6,14},{7,15},{8,0},{9,1},... | collective-permute-start | bytes 393224 | tf_op jit(solution)/shard_map/ppermute | solution.py:494
  126.8 1.2 collective-permute-start.7
  128.0 2.0 %collective-permute-done.5 = bf16[128,512]{1,0:T(8,128)(2,1)S(1)} collective-permute-done((bf16[128,512]{1,0:T(8,128)(2,1)S(1)}, bf16[128,512]{1,0:T(8,128)(2,1)S(1)}, u32[]{:S(2)}, u32[]{:S(2)}) %collective-permute-start.5) | collective-permute-done | bytes 131104 | tf_op jit(solution)/shard_map/ppermute | solution.py:494
  130.0 4.2 %collective-permute-done.7 = bf16[128,512]{1,0:T(8,128)(2,1)S(1)} collective-permute-done((bf16[128,512]{1,0:T(8,128)(2,1)S(1)}, bf16[128,512]{1,0:T(8,128)(2,1)S(1)}, u32[]{:S(2)}, u32[]{:S(2)}) %collective-permute-start.7) | collective-permute-done | bytes 131104 | tf_op jit(solution)/shard_map/ppermute | solution.py:494
  134.4 5.8 %collective-permute-start.19 = (bf16[768,512]{1,0:T(8,128)(2,1)S(1)}, bf16[768,512]{1,0:T(8,128)(2,1)}, u32[]{:S(2)}, u32[]{:S(2)}) collective-permute-start(bf16[768,512]{1,0:T(8,128)(2,1)S(1)} %bitcast.102), channel_id=1, source_target_pairs={{0,1},{1,0},{2,3},{3,2},{4,5},{5,4},{6,7},{7,6},{8,9},{9,8},{10,11... | collective-permute-start | bytes 2359304 | tf_op jit(solution)/shard_map/ppermute | solution.py:494
  140.4 3.1 %collective-permute-done.8 = bf16[512,512]{1,0:T(8,128)(2,1)S(1)} collective-permute-done((bf16[512,512]{1,0:T(8,128)(2,1)S(1)}, bf16[512,512]{1,0:T(8,128)(2,1)S(1)}, u32[]{:S(2)}, u32[]{:S(2)}) %collective-permute-start.8) | collective-permute-done | bytes 524320 | tf_op jit(solution)/shard_map/ppermute | solution.py:494
  143.6 5.2 %collective-permute-start.9 = (bf16[1024,512]{1,0:T(8,128)(2,1)S(1)}, bf16[1024,512]{1,0:T(8,128)(2,1)S(1)}, u32[]{:S(2)}, u32[]{:S(2)}) collective-permute-start(bf16[1024,512]{1,0:T(8,128)(2,1)S(1)} %bitcast.100), channel_id=1, source_target_pairs={{0,1},{1,0},{2,3},{3,2},{4,5},{5,4},{6,7},{7,6},{8,9},{9,8},{10,11... | collective-permute-start | bytes 3145736 | tf_op jit(solution)/shard_map/ppermute | solution.py:494
  148.7 3.9 %shard_map.190 = (f32[128,512]{1,0:T(8,128)}, bf16[256,512]{1,0:T(8,128)(2,1)}) custom-call(bf16[512,128]{1,0:T(8,128)(2,1)} %get-tuple-element.56.inner_senders_ref, bf16[512,128]{1,0:T(8,128)(2,1)} %get-tuple-element.57.receivers_ref.inner_receivers_ref, bf16[256,384]{1,0:T(8,128)(2,1)} %get-tuple-element.45.senders_ref.cut_senders_ref, ...), custom_call_target="tpu_custom_call" | custom-call | flops 402653184 | bytes 4587520 | tf_op jit(solution)/shard_map/pallas_call | solution.py:441
  152.6 7.6 %all-to-all-start.4 = ((bf16[16,16,512]{2,1,0:T(8,128)(2,1)}), bf16[16,16,512]{2,1,0:T(8,128)(2,1)S(1)}, u32[]{:S(2)}, u32[]{:S(2)}) async-start(bf16[16,16,512]{2,1,0:T(8,128)(2,1)} %bitcast.120), calls=%async_computation.4 | async-start | bytes 524288 | tf_op jit(solution)/shard_map/all_to_all | solution.py:503
  160.2 2.7 %shard_map.185 = bf16[768,512]{1,0:T(8,128)(2,1)} custom-call(bf16[768,512]{1,0:T(8,128)(2,1)} %edges_ref.9, f32[512,512]{1,0:T(8,128)} %get-tuple-element.53.inner_ref.normed_ref, f32[256,512]{1,0:T(8,128)} %get-tuple-element.54.cut_ref.normed_ref, bf16[256,512]{1,0:T(8,128)(2,1)} %get-tuple-element.49.dep_ref), custom_call_target="tpu_custom_call" | custom-call | flops 10000000 | bytes 3407872 | tf_op jit(solution)/shard_map/pallas_call | solution.py:441
  162.9 3.9 %shard_map.192 = f32[768,512]{1,0:T(8,128)} custom-call(bf16[768,512]{1,0:T(8,128)(2,1)} %ct_ref.7, bf16[512,512]{1,0:T(8,128)(2,1)} %get-tuple-element.62.inner_pre_ref, bf16[256,512]{1,0:T(8,128)(2,1)} %get-tuple-element.65.cut_pre_ref.dep_ref, bf16[1536,512]{1,0:T(8,128)(2,1)} %w_edge_ref.1, bf16[1024,512]{1,0:T(8,128)(2,1)} %shard_map.189.dep_ref), custom_call_target="tpu_custom_call" | custom-call | flops 402653184 | bytes 5767168 | tf_op jit(solution)/shard_map/pallas_call | solution.py:441
  166.8 2.9 %all-to-all-done.4 = bf16[16,16,512]{2,1,0:T(8,128)(2,1)S(1)} async-done(((bf16[16,16,512]{2,1,0:T(8,128)(2,1)}), bf16[16,16,512]{2,1,0:T(8,128)(2,1)S(1)}, u32[]{:S(2)}, u32[]{:S(2)}) %all-to-all-start.4) | async-done | bytes 262176 | tf_op jit(solution)/shard_map/all_to_all | solution.py:503
  170.4 2.0 %shard_map.191 = f32[128,512]{1,0:T(8,128)} custom-call(f32[128,512]{1,0:T(8,128)} %get-tuple-element.55.self_ref, f32[128,512]{1,0:T(8,128)} %get-tuple-element.74.local_ref, bf16[256,128]{1,0:T(8,128)(2,1)} %get-tuple-element.50.asked_marks_ref, bf16[256,512]{1,0:T(8,128)(2,1)} %bitcast.114), custom_call_target="tpu_custom_call" | custom-call | flops 100000000 | bytes 1114112 | tf_op jit(solution)/shard_map/pallas_call | solution.py:441
  172.6 1.2 bitcast_dynamic-update-slice_fusion.2
  173.8 1.0 slice.18
  174.9 0.8 slice.19
  176.1 1.2 slice.16
  177.3 0.8 slice.17
  (62 shorter events, 7.4 us)
Async XLA Ops:
  17.5 13.4 %all-to-all-start.1 = ((bf16[16,16,512]{2,1,0:T(8,128)(2,1)}), bf16[16,16,512]{2,1,0:T(8,128)(2,1)S(1)}, u32[]{:S(2)}, u32[]{:S(2)}) async-start(bf16[16,16,512]{2,1,0:T(8,128)(2,1)} %bitcast.121), calls=%async_computation.1 | async-start | bytes 524288 | tf_op jit(solution)/shard_map/all_to_all | solution.py:503
  30.9 0.7 copy-start.4
  35.9 14.4 %all-to-all-start.2 = ((bf16[16,16,512]{2,1,0:T(8,128)(2,1)}), bf16[16,16,512]{2,1,0:T(8,128)(2,1)S(1)}, u32[]{:S(2)}, u32[]{:S(2)}) async-start(bf16[16,16,512]{2,1,0:T(8,128)(2,1)} %bitcast.118), calls=%async_computation.2 | async-start | bytes 524288 | tf_op jit(solution)/shard_map/all_to_all | solution.py:503
  50.2 0.7 copy-start.3
  58.0 22.3 %collective-permute-start.10 = (bf16[768,512]{1,0:T(8,128)(2,1)}, bf16[768,512]{1,0:T(8,128)(2,1)S(1)}, u32[]{:S(2)}, u32[]{:S(2)}) collective-permute-start(bf16[768,512]{1,0:T(8,128)(2,1)} %get-tuple-element.81), channel_id=1, source_target_pairs={{0,1},{1,0},{2,3},{3,2},{4,5},{5,4},{6,7},{7,6},{8,9},{9,8},{10,11... | collective-permute-start | bytes 2359304 | tf_op jit(solution)/shard_map/ppermute | solution.py:470
  58.6 12.9 %all-to-all-start.3 = ((bf16[16,16,512]{2,1,0:T(8,128)(2,1)}), bf16[16,16,512]{2,1,0:T(8,128)(2,1)S(1)}, u32[]{:S(2)}, u32[]{:S(2)}) async-start(bf16[16,16,512]{2,1,0:T(8,128)(2,1)} %bitcast.115), calls=%async_computation.3 | async-start | bytes 524288 | tf_op jit(solution)/shard_map/all_to_all | solution.py:503
  71.5 0.7 copy-start.2
  75.3 5.0 %copy-start.5 = (bf16[768,512]{1,0:T(8,128)(2,1)S(1)}, bf16[768,512]{1,0:T(8,128)(2,1)}, u32[]{:S(2)}) copy-start(bf16[768,512]{1,0:T(8,128)(2,1)} %get-tuple-element.80) | copy-start | bytes 2359300
  79.7 15.5 %collective-permute-start = (bf16[1024,512]{1,0:T(8,128)(2,1)}, bf16[1024,512]{1,0:T(8,128)(2,1)S(1)}, u32[]{:S(2)}, u32[]{:S(2)}) collective-permute-start(bf16[1024,512]{1,0:T(8,128)(2,1)} %shard_map.188.dep_ref), channel_id=1, source_target_pairs={{0,1},{1,0},{2,3},{3,2},{4,5},{5,4},{6,7},{7,6},{8,9},{9,8},{10,11... | collective-permute-start | bytes 3145736 | tf_op jit(solution)/shard_map/ppermute | solution.py:470
  80.6 10.8 %collective-permute-start.11 = (bf16[384,512]{1,0:T(8,128)(2,1)S(1)}, bf16[384,512]{1,0:T(8,128)(2,1)S(1)}, u32[]{:S(2)}, u32[]{:S(2)}) collective-permute-start(bf16[384,512]{1,0:T(8,128)(2,1)S(1)} %dynamic-slice_bitcast_fusion.1), channel_id=1, source_target_pairs={{0,2},{1,3},{2,0},{3,1},{4,6},{5,7},{6,4},{7,5},{8,10},{9,11},{10,... | collective-permute-start | bytes 1179656 | tf_op jit(solution)/shard_map/ppermute | solution.py:480
  85.2 10.0 %copy-start = (bf16[1024,512]{1,0:T(8,128)(2,1)S(1)}, bf16[1024,512]{1,0:T(8,128)(2,1)}, u32[]{:S(2)}) copy-start(bf16[1024,512]{1,0:T(8,128)(2,1)} %shard_map.189.dep_ref) | copy-start | bytes 3145732
  91.5 5.5 %collective-permute-start.14 = (bf16[96,512]{1,0:T(8,128)(2,1)S(1)}, bf16[96,512]{1,0:T(8,128)(2,1)S(1)}, u32[]{:S(2)}, u32[]{:S(2)}) collective-permute-start(bf16[96,512]{1,0:T(8,128)(2,1)S(1)} %get-tuple-element.90), channel_id=1, source_target_pairs={{0,12},{1,13},{2,14},{3,15},{4,8},{5,9},{6,10},{7,11},{8,4},{9,5},... | collective-permute-start | bytes 294920 | tf_op jit(solution)/shard_map/ppermute | solution.py:480
  92.0 9.9 %collective-permute-start.13 = (bf16[96,512]{1,0:T(8,128)(2,1)S(1)}, bf16[96,512]{1,0:T(8,128)(2,1)S(1)}, u32[]{:S(2)}, u32[]{:S(2)}) collective-permute-start(bf16[96,512]{1,0:T(8,128)(2,1)S(1)} %get-tuple-element.91), channel_id=1, source_target_pairs={{0,8},{1,9},{2,10},{3,11},{4,12},{5,13},{6,14},{7,15},{8,0},{9,1},... | collective-permute-start | bytes 294920 | tf_op jit(solution)/shard_map/ppermute | solution.py:480
  92.4 9.5 %collective-permute-start.12 = (bf16[96,512]{1,0:T(8,128)(2,1)S(1)}, bf16[96,512]{1,0:T(8,128)(2,1)S(1)}, u32[]{:S(2)}, u32[]{:S(2)}) collective-permute-start(bf16[96,512]{1,0:T(8,128)(2,1)S(1)} %get-tuple-element.89), channel_id=1, source_target_pairs={{0,4},{1,5},{2,6},{3,7},{4,0},{5,1},{6,2},{7,3},{8,12},{9,13},{10,... | collective-permute-start | bytes 294920 | tf_op jit(solution)/shard_map/ppermute | solution.py:480
  95.5 11.8 %collective-permute-start.1 = (bf16[512,512]{1,0:T(8,128)(2,1)S(1)}, bf16[512,512]{1,0:T(8,128)(2,1)S(1)}, u32[]{:S(2)}, u32[]{:S(2)}) collective-permute-start(bf16[512,512]{1,0:T(8,128)(2,1)S(1)} %dynamic-slice_bitcast_fusion), channel_id=1, source_target_pairs={{0,2},{1,3},{2,0},{3,1},{4,6},{5,7},{6,4},{7,5},{8,10},{9,11},{10,... | collective-permute-start | bytes 1572872 | tf_op jit(solution)/shard_map/ppermute | solution.py:480
  102.0 3.8 %collective-permute-start.15 = (bf16[96,512]{1,0:T(8,128)(2,1)S(1)}, bf16[96,512]{1,0:T(8,128)(2,1)S(1)}, u32[]{:S(2)}, u32[]{:S(2)}) collective-permute-start(bf16[96,512]{1,0:T(8,128)(2,1)S(1)} %get-tuple-element.83), channel_id=1, source_target_pairs={{0,4},{1,5},{2,6},{3,7},{4,0},{5,1},{6,2},{7,3},{8,12},{9,13},{10,... | collective-permute-start | bytes 294920 | tf_op jit(solution)/shard_map/ppermute | solution.py:494
  102.1 9.1 %collective-permute-start.16 = (bf16[96,512]{1,0:T(8,128)(2,1)S(1)}, bf16[96,512]{1,0:T(8,128)(2,1)S(1)}, u32[]{:S(2)}, u32[]{:S(2)}) collective-permute-start(bf16[96,512]{1,0:T(8,128)(2,1)S(1)} %get-tuple-element.83), channel_id=1, source_target_pairs={{0,8},{1,9},{2,10},{3,11},{4,12},{5,13},{6,14},{7,15},{8,0},{9,1},... | collective-permute-start | bytes 294920 | tf_op jit(solution)/shard_map/ppermute | solution.py:494
  104.2 20.1 %collective-permute-start.17 = (bf16[96,512]{1,0:T(8,128)(2,1)S(1)}, bf16[96,512]{1,0:T(8,128)(2,1)S(1)}, u32[]{:S(2)}, u32[]{:S(2)}) collective-permute-start(bf16[96,512]{1,0:T(8,128)(2,1)S(1)} %get-tuple-element.83), channel_id=1, source_target_pairs={{0,12},{1,13},{2,14},{3,15},{4,8},{5,9},{6,10},{7,11},{8,4},{9,5},... | collective-permute-start | bytes 294920 | tf_op jit(solution)/shard_map/ppermute | solution.py:494
  107.5 5.8 %collective-permute-start.4 = (bf16[128,512]{1,0:T(8,128)(2,1)S(1)}, bf16[128,512]{1,0:T(8,128)(2,1)S(1)}, u32[]{:S(2)}, u32[]{:S(2)}) collective-permute-start(bf16[128,512]{1,0:T(8,128)(2,1)S(1)} %get-tuple-element.87), channel_id=1, source_target_pairs={{0,12},{1,13},{2,14},{3,15},{4,8},{5,9},{6,10},{7,11},{8,4},{9,5},... | collective-permute-start | bytes 393224 | tf_op jit(solution)/shard_map/ppermute | solution.py:480
  108.0 16.1 %collective-permute-start.3 = (bf16[128,512]{1,0:T(8,128)(2,1)S(1)}, bf16[128,512]{1,0:T(8,128)(2,1)S(1)}, u32[]{:S(2)}, u32[]{:S(2)}) collective-permute-start(bf16[128,512]{1,0:T(8,128)(2,1)S(1)} %get-tuple-element.88), channel_id=1, source_target_pairs={{0,8},{1,9},{2,10},{3,11},{4,12},{5,13},{6,14},{7,15},{8,0},{9,1},... | collective-permute-start | bytes 393224 | tf_op jit(solution)/shard_map/ppermute | solution.py:480
  109.1 15.0 %collective-permute-start.2 = (bf16[128,512]{1,0:T(8,128)(2,1)S(1)}, bf16[128,512]{1,0:T(8,128)(2,1)S(1)}, u32[]{:S(2)}, u32[]{:S(2)}) collective-permute-start(bf16[128,512]{1,0:T(8,128)(2,1)S(1)} %get-tuple-element.86), channel_id=1, source_target_pairs={{0,4},{1,5},{2,6},{3,7},{4,0},{5,1},{6,2},{7,3},{8,12},{9,13},{10,... | collective-permute-start | bytes 393224 | tf_op jit(solution)/shard_map/ppermute | solution.py:480
  124.2 5.7 %collective-permute-start.5 = (bf16[128,512]{1,0:T(8,128)(2,1)S(1)}, bf16[128,512]{1,0:T(8,128)(2,1)S(1)}, u32[]{:S(2)}, u32[]{:S(2)}) collective-permute-start(bf16[128,512]{1,0:T(8,128)(2,1)S(1)} %get-tuple-element.85), channel_id=1, source_target_pairs={{0,4},{1,5},{2,6},{3,7},{4,0},{5,1},{6,2},{7,3},{8,12},{9,13},{10,... | collective-permute-start | bytes 393224 | tf_op jit(solution)/shard_map/ppermute | solution.py:494
  124.3 10.1 %collective-permute-start.18 = (bf16[384,512]{1,0:T(8,128)(2,1)S(1)}, bf16[384,512]{1,0:T(8,128)(2,1)S(1)}, u32[]{:S(2)}, u32[]{:S(2)}) collective-permute-start(bf16[384,512]{1,0:T(8,128)(2,1)S(1)} %bitcast.110), channel_id=1, source_target_pairs={{0,2},{1,3},{2,0},{3,1},{4,6},{5,7},{6,4},{7,5},{8,10},{9,11},{10,... | collective-permute-start | bytes 1179656 | tf_op jit(solution)/shard_map/ppermute | solution.py:494
  124.4 5.6 %collective-permute-start.6 = (bf16[128,512]{1,0:T(8,128)(2,1)S(1)}, bf16[128,512]{1,0:T(8,128)(2,1)S(1)}, u32[]{:S(2)}, u32[]{:S(2)}) collective-permute-start(bf16[128,512]{1,0:T(8,128)(2,1)S(1)} %get-tuple-element.85), channel_id=1, source_target_pairs={{0,8},{1,9},{2,10},{3,11},{4,12},{5,13},{6,14},{7,15},{8,0},{9,1},... | collective-permute-start | bytes 393224 | tf_op jit(solution)/shard_map/ppermute | solution.py:494
  126.8 7.4 %collective-permute-start.7 = (bf16[128,512]{1,0:T(8,128)(2,1)S(1)}, bf16[128,512]{1,0:T(8,128)(2,1)S(1)}, u32[]{:S(2)}, u32[]{:S(2)}) collective-permute-start(bf16[128,512]{1,0:T(8,128)(2,1)S(1)} %get-tuple-element.85), channel_id=1, source_target_pairs={{0,12},{1,13},{2,14},{3,15},{4,8},{5,9},{6,10},{7,11},{8,4},{9,5},... | collective-permute-start | bytes 393224 | tf_op jit(solution)/shard_map/ppermute | solution.py:494
  134.2 9.3 %collective-permute-start.8 = (bf16[512,512]{1,0:T(8,128)(2,1)S(1)}, bf16[512,512]{1,0:T(8,128)(2,1)S(1)}, u32[]{:S(2)}, u32[]{:S(2)}) collective-permute-start(bf16[512,512]{1,0:T(8,128)(2,1)S(1)} %bitcast.108), channel_id=1, source_target_pairs={{0,2},{1,3},{2,0},{3,1},{4,6},{5,7},{6,4},{7,5},{8,10},{9,11},{10,... | collective-permute-start | bytes 1572872 | tf_op jit(solution)/shard_map/ppermute | solution.py:494
  134.4 38.2 %collective-permute-start.19 = (bf16[768,512]{1,0:T(8,128)(2,1)S(1)}, bf16[768,512]{1,0:T(8,128)(2,1)}, u32[]{:S(2)}, u32[]{:S(2)}) collective-permute-start(bf16[768,512]{1,0:T(8,128)(2,1)S(1)} %bitcast.102), channel_id=1, source_target_pairs={{0,1},{1,0},{2,3},{3,2},{4,5},{5,4},{6,7},{7,6},{8,9},{9,8},{10,11... | collective-permute-start | bytes 2359304 | tf_op jit(solution)/shard_map/ppermute | solution.py:494
  143.6 32.4 %collective-permute-start.9 = (bf16[1024,512]{1,0:T(8,128)(2,1)S(1)}, bf16[1024,512]{1,0:T(8,128)(2,1)S(1)}, u32[]{:S(2)}, u32[]{:S(2)}) collective-permute-start(bf16[1024,512]{1,0:T(8,128)(2,1)S(1)} %bitcast.100), channel_id=1, source_target_pairs={{0,1},{1,0},{2,3},{3,2},{4,5},{5,4},{6,7},{7,6},{8,9},{9,8},{10,11... | collective-permute-start | bytes 3145736 | tf_op jit(solution)/shard_map/ppermute | solution.py:494
  152.6 17.1 %all-to-all-start.4 = ((bf16[16,16,512]{2,1,0:T(8,128)(2,1)}), bf16[16,16,512]{2,1,0:T(8,128)(2,1)S(1)}, u32[]{:S(2)}, u32[]{:S(2)}) async-start(bf16[16,16,512]{2,1,0:T(8,128)(2,1)} %bitcast.120), calls=%async_computation.4 | async-start | bytes 524288 | tf_op jit(solution)/shard_map/all_to_all | solution.py:503
  169.7 0.7 copy-start.1

commit v2 on v1

--- a/solution.py
+++ b/solution.py
@@ -106,7 +106,7 @@
     reply_ref[...] = dot(asked_marks, nodes_ref[...]).astype(BF16)
 
 
-def cut_marks_kernel(dest_ref, local_ref, dep_ref, senders_ref, receivers_ref, *, domains, slots):
+def cut_marks_kernel(dest_ref, local_ref, senders_ref, receivers_ref, *, domains, slots):
     width = senders_ref.shape[1]
     base = width - domains * slots
     dest = to_column(dest_ref[...]).astype(jnp.int32)
@@ -136,7 +136,6 @@
     nodes_ref,
     w_in_ref,
     w_out_ref,
-    dep_ref,
     senders_ref,
     receivers_ref,
     sender_ref,
@@ -213,7 +212,7 @@
     outgoing_ref[...] = dot_rows(receivers_ref[:, base:], message).astype(BF16)
 
 
-def new_edges_kernel(edges_ref, inner_ref, cut_ref, dep_ref, out_ref):
+def new_edges_kernel(edges_ref, inner_ref, cut_ref, out_ref):
     inner_rows = inner_ref.shape[0]
 
     def added(edge, normed):
@@ -261,7 +260,7 @@
 
 
 def node_weights_kernel(
-    place_ref, nodes_ref, aggregate_ref, hidden_ref, grad_out_ref, grad_pre_ref, keep_ref, send_ref
+    me_ref, nodes_ref, aggregate_ref, hidden_ref, grad_out_ref, grad_pre_ref, keep_ref, send_ref
 ):
     latent = nodes_ref.shape[1]
     half = latent // 2
@@ -273,13 +272,85 @@
         high_ref[:half] = dot_rows(aggregate_ref[:, half:], grad_pre).astype(BF16)
         high_ref[half:] = dot_rows(hidden_ref[...], grad_out).astype(BF16)
 
-    @pl.when(place_ref[0] == 0)
+    halves(me_ref, keep_ref, send_ref, fill)
+
+
+def halves(me_ref, keep_ref, send_ref, fill):
+    @pl.when((me_ref[0] & 1) == 0)
     def _():
         fill(keep_ref, send_ref)
 
-    @pl.when(place_ref[0] != 0)
+    @pl.when((me_ref[0] & 1) != 0)
     def _():
         fill(send_ref, keep_ref)
+
+
+def edge_weights_kernel(me_ref, *refs):
+    keep_ref, send_ref = refs[-2:]
+    low_inner, low_cut, high_inner, high_cut = refs[:4]
+    rights = refs[4:-2]
+
+    def fill(low_ref, high_ref):
+        low_ref[...] = (
+            dot_rows(low_inner[...], rights[0][...]) + dot_rows(low_cut[...], rights[1][...])
+        ).astype(BF16)
+        high_ref[...] = (
+            dot_rows(high_inner[...], rights[-2][...]) + dot_rows(high_cut[...], rights[-1][...])
+        ).astype(BF16)
+
+    halves(me_ref, keep_ref, send_ref, fill)
+
+
+def fold_kernel(me_ref, *refs, low, width, parts):
+    size = 1 << width
+    sources, pieces = refs[:parts], refs[parts:]
+    chunk = pieces[0].shape[0]
+    place = (me_ref[0] >> low) & (size - 1)
+    for turn in range(size):
+        start = pl.multiple_of((place ^ turn) * chunk, 16) if width else 0
+        rows = pl.ds(start, chunk)
+        total = sources[0][rows].astype(F32)
+        for source in sources[1:]:
+            total += source[rows].astype(F32)
+        pieces[turn][...] = total.astype(BF16)
+
+
+def place_kernel(me_ref, *refs):
+    out_ref = refs[-1]
+    chunk = refs[0].shape[0]
+    place = (me_ref[0] >> 2) & 3
+    for turn in range(4):
+        start = pl.multiple_of((place ^ turn) * chunk, 16)
+        out_ref[pl.ds(start, chunk)] = refs[turn][...]
+
+
+def spread_kernel(me_ref, *refs, quarters):
+    sources, outs = refs[: 4 * quarters], refs[4 * quarters :]
+    place = (me_ref[0] & 1) * 2 + ((me_ref[0] >> 1) & 1)
+    spans, top = [], 0
+    for out in outs:
+        spans.append((top, top + out.shape[0], out))
+        top += out.shape[0]
+
+    def put(row, source):
+        height = source.shape[0]
+        for start, end, out in spans:
+            first, last = max(row, start), min(row + height, end)
+            if first < last:
+                out[first - start : last - start] = source[first - row : last - row]
+
+    for stream in range(quarters):
+        group = sources[4 * stream : 4 * stream + 4]
+        near, across = group[1], group[2]
+        by_distance = [group[0], across, near, group[3]]
+        height = group[0].shape[0]
+        base = sum(4 * sources[4 * before].shape[0] for before in range(stream))
+        for mine in range(4):
+
+            @pl.when(place == mine)
+            def _():
+                for quarter in range(4):
+                    put(base + quarter * height, by_distance[quarter ^ mine])
 
 
 def edge_backward(ct, target_grads, normed, inv_scale, slope, w_out):
@@ -295,7 +366,6 @@
     scale_ref,
     slope_ref,
     w_out_ref,
-    dep_ref,
     grad_out_ref,
     grad_pre_ref,
 ):
@@ -334,47 +404,6 @@
     grad_pre_ref[...] = grad_pre
 
 
-def edge_weights_kernel(
-    place_ref,
-    edges_ref,
-    inner_sender_ref,
-    cut_sender_ref,
-    inner_receiver_ref,
-    cut_receiver_ref,
-    inner_hidden_ref,
-    cut_hidden_ref,
-    inner_out_ref,
-    cut_out_ref,
-    inner_pre_ref,
-    cut_pre_ref,
-    dep_ref,
-    out_ref,
-):
-    latent = edges_ref.shape[1]
-    inner_rows = inner_pre_ref.shape[0]
-
-    @pl.when(place_ref[0] == 0)
-    def _():
-        inner_pre, cut_pre = inner_pre_ref[...], cut_pre_ref[...]
-        out_ref[:latent] = (
-            dot_rows(edges_ref[:inner_rows], inner_pre) + dot_rows(edges_ref[inner_rows:], cut_pre)
-        ).astype(BF16)
-        out_ref[latent:] = (
-            dot_rows(inner_sender_ref[...], inner_pre) + dot_rows(cut_sender_ref[...], cut_pre)
-        ).astype(BF16)
-
-    @pl.when(place_ref[0] != 0)
-    def _():
-        out_ref[:latent] = (
-            dot_rows(inner_receiver_ref[...], inner_pre_ref[...])
-            + dot_rows(cut_receiver_ref[...], cut_pre_ref[...])
-        ).astype(BF16)
-        out_ref[latent:] = (
-            dot_rows(inner_hidden_ref[...], inner_out_ref[...])
-            + dot_rows(cut_hidden_ref[...], cut_out_ref[...])
-        ).astype(BF16)
-
-
 def input_grads_kernel(
     inner_senders_ref,
     inner_receivers_ref,
@@ -383,7 +412,6 @@
     inner_pre_ref,
     cut_pre_ref,
     w_in_ref,
-    dep_ref,
     local_ref,
     outgoing_ref,
 ):
@@ -406,7 +434,7 @@
     )
 
 
-def edge_grads_kernel(ct_ref, inner_pre_ref, cut_pre_ref, w_edge_ref, dep_ref, out_ref, *, blocks):
+def edge_grads_kernel(ct_ref, inner_pre_ref, cut_pre_ref, w_edge_ref, out_ref, *, blocks):
     inside = pl.program_id(0) < blocks
 
     @pl.when(inside)
@@ -433,68 +461,94 @@
     return jax.ShapeDtypeStruct(shape, dtype)
 
 
-def run(body, outs, ins, flops, specs=None, out_specs=None, grid=None):
-    single = not isinstance(outs, (list, tuple))
-    out_shape = [outs] if single else list(outs)
-    moved = sum(item.size * item.dtype.itemsize for item in list(ins) + out_shape)
-    extra = {} if grid is None else {"grid": grid}
-    result = pl.pallas_call(
-        body,
-        out_shape=out_shape,
-        in_specs=[VMEM] * len(ins) if specs is None else specs,
-        out_specs=[VMEM] * len(out_shape) if out_specs is None else out_specs,
-        compiler_params=pltpu.CompilerParams(vmem_limit_bytes=VMEM_LIMIT),
-        cost_estimate=pl.CostEstimate(flops=flops, bytes_accessed=moved, transcendentals=0),
-        **extra,
-    )(*ins)
-    return result[0] if single else result
-
-
-def bit_groups(devices):
-    bits = devices.bit_length() - 1
-    groups = [(low, 1) for low in range(min(2, bits))]
-    low = 2
-    while low < bits:
-        groups.append((low, min(2, bits - low)))
-        low += 2
-    return groups
-
-
-def partner_pairs(devices, mask):
-    return [(device, device ^ mask) for device in range(devices)]
-
-
-def reduce_rows(keep, send, devices):
-    me = lax.axis_index("dom")
-    groups = bit_groups(devices)
-    received = lax.ppermute(send, "dom", partner_pairs(devices, 1))
-    rows = (keep.astype(F32) + received.astype(F32)).astype(BF16)
-    for low, width in groups[1:]:
+class Line:
+    def __init__(self):
+        self.last = None
+
+    def run(self, body, outs, ins, flops, specs=None, out_specs=None, grid=None):
+        single = not isinstance(outs, (list, tuple))
+        out_shape = [outs] if single else list(outs)
+        specs = [VMEM] * len(ins) if specs is None else list(specs)
+        moved = sum(item.size * item.dtype.itemsize for item in list(ins) + out_shape)
+        count, extra = len(ins), {} if grid is None else {"grid": grid}
+        ins = list(ins)
+        if self.last is not None:
+            ins.append(self.last)
+            specs.append(ANY)
+
+        def ordered(*refs):
+            return body(*refs[:count], *refs[len(ins) :])
+
+        result = pl.pallas_call(
+            ordered,
+            out_shape=out_shape,
+            in_specs=specs,
+            out_specs=[VMEM] * len(out_shape) if out_specs is None else out_specs,
+            compiler_params=pltpu.CompilerParams(vmem_limit_bytes=VMEM_LIMIT),
+            cost_estimate=pl.CostEstimate(flops=flops, bytes_accessed=moved, transcendentals=0),
+            **extra,
+        )(*ins)
+        self.last = result[-1]
+        return result[0] if single else result
+
+
+class Stream:
+    def __init__(self, line, me, devices, keep, send):
+        self.line, self.me, self.devices = line, me, devices
+        self.keep, self.sent = keep, [send]
+        self.masks = [1]
+
+    def swap(self):
+        self.got = [
+            lax.ppermute(part, "dom", [(device, device ^ mask) for device in range(self.devices)])
+            for part, mask in zip(self.sent, self.masks)
+        ]
+
+    def fold(self, low, width):
         size = 1 << width
-        place = (me >> low) & (size - 1)
-        chunk = rows.shape[0] // size
-        pieces = rows.reshape(size, chunk, rows.shape[1])
-        total = lax.dynamic_index_in_dim(pieces, place, 0, False).astype(F32)
-        for turn in range(1, size):
-            sent = lax.dynamic_index_in_dim(pieces, place ^ turn, 0, False)
-            total += lax.ppermute(sent, "dom", partner_pairs(devices, turn << low)).astype(F32)
-        rows = total.astype(BF16)
-    return rows
-
-
-def gather_rows(rows, devices):
-    me = lax.axis_index("dom")
-    for low, width in bit_groups(devices)[::-1]:
-        size = 1 << width
-        place = (me >> low) & (size - 1)
-        whole = jnp.zeros((size,) + rows.shape, rows.dtype)
-        for turn in range(size):
-            piece = rows
-            if turn:
-                piece = lax.ppermute(rows, "dom", partner_pairs(devices, turn << low))
-            whole = lax.dynamic_update_index_in_dim(whole, piece, place ^ turn, 0)
-        rows = whole.reshape(size * rows.shape[0], rows.shape[1])
-    return rows
+        rows, latent = self.keep.shape
+        chunk = rows // size
+        piece = shaped(BF16, chunk, latent)
+        pieces = self.line.run(
+            functools.partial(fold_kernel, low=low, width=width, parts=1 + len(self.got)),
+            [piece] * size,
+            [self.me, self.keep] + self.got,
+            rows * latent * 4,
+            [SMEM] + [VMEM] * (1 + len(self.got)),
+        )
+        self.keep, self.sent = pieces[0], list(pieces[1:])
+        self.masks = [turn << low for turn in range(1, size)]
+        self.swap()
+
+    def settle(self):
+        chunk = self.line.run(
+            functools.partial(fold_kernel, low=0, width=0, parts=4),
+            [shaped(BF16, *self.keep.shape)],
+            [self.me, self.keep] + self.got,
+            self.keep.size * 4,
+            [SMEM] + [VMEM] * 4,
+        )[0]
+        if self.devices > 16:
+            alike = [list(range(low, self.devices, 16)) for low in range(16)]
+            chunk = lax.psum(chunk, "dom", axis_index_groups=alike)
+        self.keep, self.sent, self.masks = chunk, [chunk] * 3, [4, 8, 12]
+        self.swap()
+
+    def place(self):
+        rows, latent = self.keep.shape
+        column = self.line.run(
+            place_kernel,
+            shaped(BF16, 4 * rows, latent),
+            [self.me, self.keep] + self.got,
+            10**6,
+            [SMEM] + [VMEM] * 4,
+        )
+        self.keep, self.sent, self.masks = column, [column, column], [1, 2]
+        self.swap()
+        near, across = self.got
+        self.sent, self.masks = [across], [1]
+        self.swap()
+        self.quarters = [column, near, across, self.got[0]]
 
 
 def exchange(rows, domains):
@@ -525,21 +579,20 @@
     total_slots = domains * slots
     table = node_rows + total_slots
     square = 2 * latent * latent
-    place = lax.axis_index("dom") & 1
-    mine, other = place.reshape(1), (1 - place).reshape(1)
-
-    ask = run(
+    me = lax.axis_index("dom").reshape(1)
+    line = Line()
+
+    ask = line.run(
         ask_kernel, shaped(jnp.int32, domains, slots), [cut_dest.reshape(1, -1), cut_remote.reshape(1, -1)], 10**7
     )
     asked = lax.all_to_all(ask, "dom", split_axis=0, concat_axis=0, tiled=True)
-    cut_senders, cut_receivers = run(
+    cut_senders, cut_receivers = line.run(
         functools.partial(cut_marks_kernel, domains=domains, slots=slots),
         [shaped(BF16, cut_rows, table)] * 2,
-        [cut_dest.reshape(1, -1), cut_local.reshape(1, -1), ask],
+        [cut_dest.reshape(1, -1), cut_local.reshape(1, -1)],
         10**8,
-        [VMEM, VMEM, ANY],
-    )
-    reply, asked_marks = run(
+    )
+    reply, asked_marks = line.run(
         reply_kernel,
         [shaped(BF16, total_slots, latent), shaped(BF16, total_slots, node_rows)],
         [asked, nodes],
@@ -568,11 +621,11 @@
         inner_normed,
         inner_scale,
         inner_total,
-    ) = run(
+    ) = line.run(
         inner_forward_kernel,
         [shaped(kind, inner_rows, width) for kind, width in zip(saved_types, saved_widths)]
         + [shaped(F32, node_rows, latent)],
-        [inner_pairs.T, edges, nodes, w_edge_in, w_edge_out, reply],
+        [inner_pairs.T, edges, nodes, w_edge_in, w_edge_out],
         inner_rows * 4 * square,
         [
             pl.BlockSpec((2, block // 2), lambda step: (0, step)),
@@ -580,14 +633,14 @@
             all_spec(nodes),
             all_spec(w_edge_in),
             all_spec(w_edge_out),
-            ANY,
         ],
         [rows_spec(width) for width in saved_widths] + [all_spec(nodes)],
         (blocks,),
     )
 
     def last_rows(array):
-        return pl.BlockSpec((block, array.shape[1]), lambda step: (blocks, 0))
+        last = array.shape[0] // block - 1
+        return pl.BlockSpec((block, array.shape[1]), lambda step: (last, 0))
 
     (
         cut_sender,
@@ -598,7 +651,7 @@
         cut_scale,
         total,
         outgoing,
-    ) = run(
+    ) = line.run(
         cut_forward_kernel,
         [shaped(kind, cut_rows, width) for kind, width in zip(saved_types, saved_widths)][2:]
         + [shaped(F32, node_rows, latent), shaped(BF16, total_slots, latent)],
@@ -628,12 +681,11 @@
         (1,),
     )
     incoming = exchange(outgoing, domains)
-    new_edges = run(
+    new_edges = line.run(
         new_edges_kernel,
         shaped(BF16, *edges.shape),
-        [edges, inner_normed, cut_normed, outgoing],
+        [edges, inner_normed, cut_normed],
         10**7,
-        [VMEM, VMEM, VMEM, ANY],
     )
     (
         new_nodes,
@@ -644,7 +696,7 @@
         node_hidden,
         node_out,
         node_pre,
-    ) = run(
+    ) = line.run(
         node_kernel,
         [
             shaped(BF16, node_rows, latent),
@@ -657,16 +709,16 @@
         node_rows * 6 * square,
     )
     far_grad = exchange(grad_reply, domains)
-    node_keep, node_send = run(
+    node_keep, node_send = line.run(
         node_weights_kernel,
         [shaped(BF16, 3 * latent // 2, latent)] * 2,
-        [mine, nodes, aggregate, node_hidden, node_out, node_pre],
+        [me, nodes, aggregate, node_hidden, node_out, node_pre],
         node_rows * 3 * square,
         [SMEM] + [VMEM] * 5,
     )
-    node_total = gather_rows(reduce_rows(node_keep, node_send, domains), domains)
-
-    inner_out, inner_pre = run(
+    node_stream = Stream(line, me, domains, node_keep, node_send)
+    node_stream.swap()
+    inner_out, inner_pre = line.run(
         inner_backward_kernel,
         [shaped(BF16, inner_rows, latent)] * 2,
         [
@@ -677,7 +729,6 @@
             inner_scale,
             inner_slope,
             w_edge_out,
-            grad_reply,
         ],
         inner_rows * square,
         [
@@ -688,12 +739,12 @@
             rows_spec(1),
             rows_spec(latent),
             all_spec(w_edge_out),
-            ANY,
         ],
         [rows_spec(latent)] * 2,
         (blocks,),
     )
-    cut_out, cut_pre = run(
+    node_stream.fold(1, 1)
+    cut_out, cut_pre = line.run(
         cut_backward_kernel,
         [shaped(BF16, cut_rows, latent)] * 2,
         [
@@ -720,33 +771,34 @@
         [rows_spec(latent)] * 2,
         (1,),
     )
-    factors = [
-        edges,
-        inner_sender,
-        cut_sender,
+    def edge_stream(low_inner, low_cut, high_inner, high_cut, rights):
+        factors = [low_inner, low_cut, high_inner, high_cut] + rights
+        keep, send = line.run(
+            edge_weights_kernel,
+            [shaped(BF16, latent, latent)] * 2,
+            [me] + factors,
+            (inner_rows + cut_rows) * 2 * square,
+            [SMEM, rows_spec(latent, inner_rows), last_rows(low_cut)]
+            + [all_spec(array) for array in factors[2:]],
+            [rows_spec(latent, latent)] * 2,
+            (1,),
+        )
+        stream = Stream(line, me, domains, keep, send)
+        stream.swap()
+        return stream
+
+    first = edge_stream(edges, edges, inner_sender, cut_sender, [inner_pre, cut_pre])
+    second = edge_stream(
         inner_receiver,
         cut_receiver,
         inner_hidden,
         cut_hidden,
-        inner_out,
-        cut_out,
-        inner_pre,
-        cut_pre,
-    ]
-
-    def edge_weights(half, dep):
-        return run(
-            edge_weights_kernel,
-            shaped(BF16, 2 * latent, latent),
-            [half] + factors + [dep],
-            (inner_rows + cut_rows) * 2 * square,
-            [SMEM] + [VMEM] * len(factors) + [ANY],
-        )
-
-    edge_send = edge_weights(other, cut_pre)
-    edge_keep = edge_weights(mine, edge_send)
-    edge_total = gather_rows(reduce_rows(edge_keep, edge_send, domains), domains)
-    local_grad, outgoing_grad = run(
+        [inner_pre, cut_pre, inner_out, cut_out],
+    )
+    first.fold(1, 1)
+    node_stream.fold(2, 2)
+    second.fold(1, 1)
+    local_grad, outgoing_grad = line.run(
         input_grads_kernel,
         [shaped(F32, node_rows, latent), shaped(BF16, total_slots, latent)],
         [
@@ -757,42 +809,61 @@
             inner_pre,
             cut_pre,
             w_edge_in,
-            edge_keep,
         ],
         (node_rows + total_slots) * 2 * square,
-        [VMEM] * 7 + [ANY],
-    )
-    grad_edges = run(
+    )
+    returned = exchange(outgoing_grad, domains)
+    first.fold(2, 2)
+    node_stream.settle()
+    second.fold(2, 2)
+    first.settle()
+    grad_edges = line.run(
         functools.partial(edge_grads_kernel, blocks=blocks),
         shaped(F32, *edges.shape),
-        [ct_edges, inner_pre, cut_pre, w_edge_in, edge_keep],
+        [ct_edges, inner_pre, cut_pre, w_edge_in],
         (inner_rows + cut_rows) * square,
         [
             rows_spec(latent),
             pl.BlockSpec((block, latent), lambda step: (jnp.minimum(step, blocks - 1), 0)),
             all_spec(cut_pre),
             pl.BlockSpec((latent, latent), lambda step: (0, 0)),
-            ANY,
         ],
         [rows_spec(latent)],
         (blocks + 1,),
     )
-    returned = exchange(outgoing_grad, domains)
-    grad_nodes = run(
+    node_stream.place()
+    second.settle()
+    first.place()
+    grad_nodes = line.run(
         node_grads_kernel,
         shaped(F32, node_rows, latent),
         [self_grad, local_grad, asked_marks, returned],
         10**8,
+    )
+    second.place()
+    grad_node_in, grad_node_out = line.run(
+        functools.partial(spread_kernel, quarters=1),
+        [shaped(BF16, 2 * latent, latent), shaped(BF16, latent, latent)],
+        [me] + node_stream.quarters,
+        10**6,
+        [SMEM] + [VMEM] * 4,
+    )
+    grad_edge_in, grad_edge_out = line.run(
+        functools.partial(spread_kernel, quarters=2),
+        [shaped(BF16, 3 * latent, latent), shaped(BF16, latent, latent)],
+        [me] + first.quarters + second.quarters,
+        10**6,
+        [SMEM] + [VMEM] * 8,
     )
     return (
         new_nodes,
         new_edges,
         grad_nodes,
         grad_edges,
-        edge_total[: 3 * latent],
-        edge_total[3 * latent :],
-        node_total[: 2 * latent],
-        node_total[2 * latent :],
+        grad_edge_in,
+        grad_edge_out,
+        grad_node_in,
+        grad_node_out,
     )
 
 

time: 180 us -> 192 us (1.067)
  Pallas kernels: 51.4 us -> 77.5 us
  waiting for transfers between devices: 55.9 us -> 30.7 us
  starting transfers between devices: 46.9 us -> 68.4 us
  blocking collectives: 13.1 us -> 0 us
  local copies, waits for them, and re-layouts: 9.01 us -> 13.5 us
    pallas_call x15 -> x29, Pallas kernels: 51.4 us -> 77.5 us  [run(): pl.pallas_call(ordered, out_shape=out_shape, in_specs=specs, out_specs=[V...]
    ppermute x20 -> x33, waiting for transfers between devices: 36.4 us -> 14.3 us  [swap(): lax.ppermute(part, 'dom', [(device, device ^ mask) for device in range(se...]
    ppermute x20 -> x33, starting transfers between devices: 27.1 us -> 44.3 us  [swap(): lax.ppermute(part, 'dom', [(device, device ^ mask) for device in range(se...]
    all_to_all x1 -> x0, blocking collectives: 13.1 us -> none  [shards(): asked = lax.all_to_all(ask, 'dom', split_axis=0, concat_axis=0, tiled=True)]
    unnamed x12 -> x94, local copies, waits for them, and re-layouts: 2.82 us -> 13.5 us
    all_to_all x0 -> x1, starting transfers between devices: none -> 7.32 us  [shards(): asked = lax.all_to_all(ask, 'dom', split_axis=0, concat_axis=0, tiled=True)]
    all_to_all x4, waiting for transfers between devices: 19.5 us -> 12.7 us  [exchange(): lax.all_to_all(split, 'dom', split_axis=0, concat_axis=0, tiled=True)]
    slice x4 -> x0, local copies, waits for them, and re-layouts: 3.94 us -> none  [the longest x1 1.24 us: shards(): edge_total[:3 * latent]]
  transfers between devices with their start and end apart: 24 -> 38, of which waited for: 14 -> 11; matrix products, arithmetic and copies ran while one was open for 3% -> 0% of each run, Pallas kernels for 20% -> 28%
where the time goes in v2:
time: 192 us; the launch traced here: 191 us
  Pallas kernels  77.5 us (40%)
  starting transfers between devices  68.4 us (36%)
  waiting for transfers between devices  30.7 us (16%)
  local copies, waits for them, and re-layouts  13.5 us (7%)
    pallas_call x29, Pallas kernels, run(): pl.pallas_call(ordered, out_shape=out_shape, in_specs=specs, out_specs=[V...  77.5 us
    ppermute x33, starting transfers between devices, swap(): lax.ppermute(part, 'dom', [(device, device ^ mask) for device in range(se...  44.3 us
    all_to_all x4, starting transfers between devices, exchange(): lax.all_to_all(split, 'dom', split_axis=0, concat_axis=0, tiled=True)  16.8 us
    ppermute x33, waiting for transfers between devices, swap(): lax.ppermute(part, 'dom', [(device, device ^ mask) for device in range(se...  14.3 us
    unnamed x94, local copies, waits for them, and re-layouts  13.5 us
    all_to_all x4, waiting for transfers between devices, exchange(): lax.all_to_all(split, 'dom', split_axis=0, concat_axis=0, tiled=True)  12.7 us
    all_to_all x1, starting transfers between devices, shards(): asked = lax.all_to_all(ask, 'dom', split_axis=0, concat_axis=0, tiled=True)  7.32 us
  transfers between devices with their start and end apart: 38, of which 11 were waited for; matrix products, arithmetic and copies ran while one was open for 0% of the time, Pallas kernels for 28%

profile of v2, /device:TPU:1, one launch (start us, length us, event | category | flops | bytes accessed | tf_op | source)
XLA Modules:
  0.0 191.1 jit_solution(13287112003521855965)
XLA Ops:
  0.6 1.7 shard_map.179.refs_2_
  2.3 7.3 %all-to-all-start = ((s32[16,1,16]{2,1,0:T(1,128)}), s32[16,1,16]{2,1,0:T(1,128)S(1)}, u32[]{:S(2)}, u32[]{:S(2)}) async-start(s32[16,1,16]{2,1,0:T(1,128)} %bitcast.26), calls=%async_computation | async-start | bytes 16384 | tf_op jit(solution)/shard_map/all_to_all | solution.py:588
  9.7 2.0 %shard_map.180 = (bf16[256,384]{1,0:T(8,128)(2,1)}, bf16[256,384]{1,0:T(8,128)(2,1)}) custom-call(s32[1,128]{1,0:T(1,128)} %bitcast.30, s32[1,128]{1,0:T(1,128)} %bitcast.31, s32[16,16]{1,0:T(8,128)} %shard_map.179.refs_2_), custom_call_target="tpu_custom_call" | custom-call | flops 100000000 | bytes 394240 | tf_op jit(solution)/shard_map/pallas_call | solution.py:482
  11.7 3.7 %all-to-all-done = s32[16,1,16]{2,1,0:T(1,128)S(1)} async-done(((s32[16,1,16]{2,1,0:T(1,128)}), s32[16,1,16]{2,1,0:T(1,128)S(1)}, u32[]{:S(2)}, u32[]{:S(2)}) %all-to-all-start) | async-done | bytes 1056 | tf_op jit(solution)/shard_map/all_to_all | solution.py:588
  16.0 2.0 %shard_map.181 = (bf16[256,512]{1,0:T(8,128)(2,1)}, bf16[256,128]{1,0:T(8,128)(2,1)}) custom-call(s32[16,16]{1,0:T(8,128)} %bitcast.25, bf16[128,512]{1,0:T(8,128)(2,1)} %refs_1_.6, bf16[256,384]{1,0:T(8,128)(2,1)} %get-tuple-element.72.refs_2_.refs_1_.refs_0_.refs_3_), custom_call_target="tpu_custom_call" | custom-call | flops 100000000 | bytes 459776 | tf_op jit(solution)/shard_map/pallas_call | solution.py:482
  18.0 4.0 %all-to-all-start.1 = ((bf16[16,16,512]{2,1,0:T(8,128)(2,1)}), bf16[16,16,512]{2,1,0:T(8,128)(2,1)S(1)}, u32[]{:S(2)}, u32[]{:S(2)}) async-start(bf16[16,16,512]{2,1,0:T(8,128)(2,1)} %bitcast.24), calls=%async_computation.1 | async-start | bytes 524288 | tf_op jit(solution)/shard_map/all_to_all | solution.py:557
  22.0 6.3 %shard_map.182 = (bf16[512,128]{1,0:T(8,128)(2,1)}, bf16[512,128]{1,0:T(8,128)(2,1)}, bf16[512,512]{1,0:T(8,128)(2,1)}, bf16[512,512]{1,0:T(8,128)(2,1)}, bf16[5...) custom-call(s32[2,256]{1,0:T(2,128)} %bitcast.27, ...), custom_call_target="tpu_custom_call" | custom-call | flops 1073741824 | bytes 7213056 | tf_op jit(solution)/shard_map/pallas_call | solution.py:482
  28.3 3.3 %all-to-all-done.1 = bf16[16,16,512]{2,1,0:T(8,128)(2,1)S(1)} async-done(((bf16[16,16,512]{2,1,0:T(8,128)(2,1)}), bf16[16,16,512]{2,1,0:T(8,128)(2,1)S(1)}, u32[]{:S(2)}, u32[]{:S(2)}) %all-to-all-start.1) | async-done | bytes 262176 | tf_op jit(solution)/shard_map/all_to_all | solution.py:557
  32.3 4.3 %shard_map.183 = (bf16[256,512]{1,0:T(8,128)(2,1)}, bf16[256,512]{1,0:T(8,128)(2,1)}, bf16[256,512]{1,0:T(8,128)(2,1)}, f32[256,512]{1,0:T(8,128)}, f32[256,512]...) custom-call(bf16[256,384]{1,0:T(8,128)(2,1)} %get-tuple-element.71.refs_0_.refs_2_, ...), custom_call_target="tpu_custom_call" | custom-call | flops 536870912 | bytes 6292480 | tf_op jit(solution)/shard_map/pallas_call | solution.py:482
  36.6 4.0 %all-to-all-start.2 = ((bf16[16,16,512]{2,1,0:T(8,128)(2,1)}), bf16[16,16,512]{2,1,0:T(8,128)(2,1)S(1)}, u32[]{:S(2)}, u32[]{:S(2)}) async-start(bf16[16,16,512]{2,1,0:T(8,128)(2,1)} %bitcast.22), calls=%async_computation.2 | async-start | bytes 524288 | tf_op jit(solution)/shard_map/all_to_all | solution.py:557
  40.6 2.7 %shard_map.184.refs_7_ = bf16[768,512]{1,0:T(8,128)(2,1)} custom-call(bf16[768,512]{1,0:T(8,128)(2,1)} %refs_2_.7, f32[512,512]{1,0:T(8,128)} %get-tuple-element.78.refs_1_.refs_3_, f32[256,512]{1,0:T(8,128)} %get-tuple-element.79.refs_2_.refs_4_, bf16[256,512]{1,0:T(8,128)(2,1)} %get-tuple-element.76.refs_3_), custom_call_target="tpu_custom_call" | custom-call | flops 10000000 | bytes 3145728 | tf_op jit(solution)/shard_map/pallas_call | solution.py:482
  43.2 6.9 %all-to-all-done.2 = bf16[16,16,512]{2,1,0:T(8,128)(2,1)S(1)} async-done(((bf16[16,16,512]{2,1,0:T(8,128)(2,1)}), bf16[16,16,512]{2,1,0:T(8,128)(2,1)S(1)}, u32[]{:S(2)}, u32[]{:S(2)}) %all-to-all-start.2) | async-done | bytes 262176 | tf_op jit(solution)/shard_map/all_to_all | solution.py:557
  50.8 4.1 %shard_map.185 = (bf16[128,512]{1,0:T(8,128)(2,1)}, f32[128,512]{1,0:T(8,128)}, bf16[128,512]{1,0:T(8,128)(2,1)}, bf16[256,512]{1,0:T(8,128)(2,1)}, bf16[128,512...) custom-call(bf16[256,512]{1,0:T(8,128)(2,1)} %bitcast.18, ...), custom_call_target="tpu_custom_call" | custom-call | flops 402653184 | bytes 3735552 | tf_op jit(solution)/shard_map/pallas_call | solution.py:482
  55.0 2.9 %shard_map.186 = (bf16[768,512]{1,0:T(8,128)(2,1)}, bf16[768,512]{1,0:T(8,128)(2,1)}) custom-call(s32[1]{0:T(128)} %bitcast.11.refs_0_, bf16[128,512]{1,0:T(8,128)(2,1)} %refs_1_.6, bf16[128,512]{1,0:T(8,128)(2,1)} %get-tuple-element.87.refs_2_, bf16[128,512]{1,0:T(8,128)(2,1)} %get-tuple-element.88.refs_3_, bf16[128,512]{1,0:T(8,128)(2,1)} %get-tuple-element.89.refs_4_, ...), custom_call_target="tpu_custom_call" | custom-call | flops 201326592 | bytes 2228228 | tf_op jit(solution)/shard_map/pallas_call | solution.py:482
  58.5 3.4 %all-to-all-start.3 = ((bf16[16,16,512]{2,1,0:T(8,128)(2,1)}), bf16[16,16,512]{2,1,0:T(8,128)(2,1)S(1)}, u32[]{:S(2)}, u32[]{:S(2)}) async-start(bf16[16,16,512]{2,1,0:T(8,128)(2,1)} %bitcast.23), calls=%async_computation.3 | async-start | bytes 524288 | tf_op jit(solution)/shard_map/all_to_all | solution.py:557
  62.0 3.6 %shard_map.187 = (bf16[512,512]{1,0:T(8,128)(2,1)}, bf16[512,512]{1,0:T(8,128)(2,1)}) custom-call(bf16[512,128]{1,0:T(8,128)(2,1)} %get-tuple-element.83.refs_0_.refs_1_, bf16[128,512]{1,0:T(8,128)(2,1)} %get-tuple-element.84.refs_1_, bf16[768,512]{1,0:T(8,128)(2,1)} %refs_0_.3, f32[512,512]{1,0:T(8,128)} %get-tuple-element.78.refs_1_.refs_3_, ...), custom_call_target="tpu_custom_call" | custom-call | flops 268435456 | bytes 4720640 | tf_op jit(solution)/shard_map/pallas_call | solution.py:482
  66.5 2.4 %shard_map.188 = (bf16[384,512]{1,0:T(8,128)(2,1)}, bf16[384,512]{1,0:T(8,128)(2,1)}) custom-call(s32[1]{0:T(128)} %bitcast.11.refs_0_, bf16[768,512]{1,0:T(8,128)(2,1)} %get-tuple-element.96.refs_1_, bf16[768,512]{1,0:T(8,128)(2,1)} %copy-done.5, bf16[512,512]{1,0:T(8,128)(2,1)} %get-tuple-element.92.refs_3_.refs_5_.refs_4_.refs_1_), custom_call_target="tpu_custom_call" | custom-call | flops 1572864 | bytes 2359300 | tf_op jit(solution)/shard_map/pallas_call | solution.py:482
  68.9 2.5 %all-to-all-done.3 = bf16[16,16,512]{2,1,0:T(8,128)(2,1)S(1)} async-done(((bf16[16,16,512]{2,1,0:T(8,128)(2,1)}), bf16[16,16,512]{2,1,0:T(8,128)(2,1)S(1)}, u32[]{:S(2)}, u32[]{:S(2)}) %all-to-all-start.3) | async-done | bytes 262176 | tf_op jit(solution)/shard_map/all_to_all | solution.py:557
  72.1 3.1 %shard_map.189 = (bf16[256,512]{1,0:T(8,128)(2,1)}, bf16[256,512]{1,0:T(8,128)(2,1)}) custom-call(bf16[256,384]{1,0:T(8,128)(2,1)} %get-tuple-element.72.refs_2_.refs_1_.refs_0_.refs_3_, bf16[128,512]{1,0:T(8,128)(2,1)} %get-tuple-element.84.refs_1_, bf16[256,512]{1,0:T(8,128)(2,1)} %bitcast.21, bf16[768,512]{1,0:T(8,128)(2,1)} %refs_0_.3, ...), custom_call_target="tpu_custom_call" | custom-call | flops 134217728 | bytes 3474432 | tf_op jit(solution)/shard_map/pallas_call | solution.py:482
  75.2 3.6 %shard_map.190 = (bf16[512,512]{1,0:T(8,128)(2,1)}, bf16[512,512]{1,0:T(8,128)(2,1)}) custom-call(s32[1]{0:T(128)} %bitcast.11.refs_0_, bf16[768,512]{1,0:T(8,128)(2,1)} %refs_2_.7, bf16[768,512]{1,0:T(8,128)(2,1)} %refs_2_.7, bf16[512,512]{1,0:T(8,128)(2,1)} %get-tuple-element.105.refs_3_, bf16[256,512]{1,0:T(8,128)(2,1)} %get-tuple-element.106.refs_4_, ...), custom_call_target="tpu_custom_call" | custom-call | flops 805306368 | bytes 4194308 | tf_op jit(solution)/shard_map/pallas_call | solution.py:482
  79.5 3.8 %shard_map.191 = (bf16[512,512]{1,0:T(8,128)(2,1)}, bf16[512,512]{1,0:T(8,128)(2,1)}) custom-call(s32[1]{0:T(128)} %bitcast.11.refs_0_, bf16[512,512]{1,0:T(8,128)(2,1)} %get-tuple-element.99.refs_1_, bf16[256,512]{1,0:T(8,128)(2,1)} %get-tuple-element.100.refs_2_, bf16[512,512]{1,0:T(8,128)(2,1)} %get-tuple-element.101.refs_3_, ...), custom_call_target="tpu_custom_call" | custom-call | flops 805306368 | bytes 4194308 | tf_op jit(solution)/shard_map/pallas_call | solution.py:482
  84.3 2.1 %shard_map.192 = (bf16[256,512]{1,0:T(8,128)(2,1)}, bf16[256,512]{1,0:T(8,128)(2,1)}) custom-call(s32[1]{0:T(128)} %bitcast.11.refs_0_, bf16[512,512]{1,0:T(8,128)(2,1)} %get-tuple-element.111.refs_1_, bf16[512,512]{1,0:T(8,128)(2,1)} %copy-done.8, bf16[512,512]{1,0:T(8,128)(2,1)} %get-tuple-element.109.refs_3_), custom_call_target="tpu_custom_call" | custom-call | flops 1048576 | bytes 1572868 | tf_op jit(solution)/shard_map/pallas_call | solution.py:482
  87.7 5.9 %collective-permute-done.2.refs_2_ = bf16[384,512]{1,0:T(8,128)(2,1)S(1)} collective-permute-done((bf16[384,512]{1,0:T(8,128)(2,1)S(1)}, bf16[384,512]{1,0:T(8,128)(2,1)S(1)}, u32[]{:S(2)}, u32[]{:S(2)}) %collective-permute-start.2) | collective-permute-done | bytes 393248 | tf_op jit(solution)/shard_map/ppermute | solution.py:503
  94.4 1.9 shard_map.193
  97.1 2.1 %shard_map.194 = (bf16[256,512]{1,0:T(8,128)(2,1)}, bf16[256,512]{1,0:T(8,128)(2,1)}) custom-call(s32[1]{0:T(128)} %bitcast.11.refs_0_, bf16[512,512]{1,0:T(8,128)(2,1)} %get-tuple-element.108.refs_1_, bf16[512,512]{1,0:T(8,128)(2,1)} %copy-done.7, bf16[96,512]{1,0:T(8,128)(2,1)} %get-tuple-element.113.refs_3_), custom_call_target="tpu_custom_call" | custom-call | flops 1048576 | bytes 1572868 | tf_op jit(solution)/shard_map/pallas_call | solution.py:482
  99.7 3.9 %shard_map.195 = (f32[128,512]{1,0:T(8,128)}, bf16[256,512]{1,0:T(8,128)(2,1)}) custom-call(bf16[512,128]{1,0:T(8,128)(2,1)} %get-tuple-element.82.refs_0_, bf16[512,128]{1,0:T(8,128)(2,1)} %get-tuple-element.83.refs_0_.refs_1_, bf16[256,384]{1,0:T(8,128)(2,1)} %get-tuple-element.71.refs_0_.refs_2_, ...), custom_call_target="tpu_custom_call" | custom-call | flops 402653184 | bytes 3538944 | tf_op jit(solution)/shard_map/pallas_call | solution.py:482
  103.6 5.3 %all-to-all-start.4 = ((bf16[16,16,512]{2,1,0:T(8,128)(2,1)}), bf16[16,16,512]{2,1,0:T(8,128)(2,1)S(1)}, u32[]{:S(2)}, u32[]{:S(2)}) async-start(bf16[16,16,512]{2,1,0:T(8,128)(2,1)} %bitcast.20), calls=%async_computation.4 | async-start | bytes 524288 | tf_op jit(solution)/shard_map/all_to_all | solution.py:557
  110.4 2.1 %collective-permute-start.10 = (bf16[96,512]{1,0:T(8,128)(2,1)S(1)}, bf16[96,512]{1,0:T(8,128)(2,1)S(1)}, u32[]{:S(2)}, u32[]{:S(2)}) collective-permute-start(bf16[96,512]{1,0:T(8,128)(2,1)S(1)} %copy-done.43), channel_id=1, source_target_pairs={{0,8},{1,9},{2,10},{3,11},{4,12},{5,13},{6,14},{7,15},{8,0},{9,1},... | collective-permute-start | bytes 294920 | tf_op jit(solution)/shard_map/ppermute | solution.py:503
  113.3 1.8 shard_map.196
  115.5 1.8 collective-permute-done.9.refs_2_
  117.3 2.4 %collective-permute-start.6 = (bf16[64,512]{1,0:T(8,128)(2,1)}, bf16[64,512]{1,0:T(8,128)(2,1)S(1)}, u32[]{:S(2)}, u32[]{:S(2)}) collective-permute-start(bf16[64,512]{1,0:T(8,128)(2,1)} %get-tuple-element.120), channel_id=1, source_target_pairs={{0,8},{1,9},{2,10},{3,11},{4,12},{5,13},{6,14},{7,15},{8,0},{9,1},... | collective-permute-start | bytes 196616 | tf_op jit(solution)/shard_map/ppermute | solution.py:503
  120.4 5.1 %collective-permute-start.7 = (bf16[64,512]{1,0:T(8,128)(2,1)}, bf16[64,512]{1,0:T(8,128)(2,1)S(1)}, u32[]{:S(2)}, u32[]{:S(2)}) collective-permute-start(bf16[64,512]{1,0:T(8,128)(2,1)} %get-tuple-element.121.refs_5_), channel_id=1, source_target_pairs={{0,12},{1,13},{2,14},{3,15},{4,8},{5,9},{6,10},{7,11},{8,4},{9,5},... | collective-permute-start | bytes 196616 | tf_op jit(solution)/shard_map/ppermute | solution.py:503
  126.1 1.7 shard_map.197.refs_3_.refs_1_
  127.9 4.3 %collective-permute-start.19 = (bf16[96,512]{1,0:T(8,128)(2,1)}, bf16[96,512]{1,0:T(8,128)(2,1)S(1)}, u32[]{:S(2)}, u32[]{:S(2)}) collective-permute-start(bf16[96,512]{1,0:T(8,128)(2,1)} %shard_map.197.refs_3_.refs_1_), channel_id=1, source_target_pairs={{0,8},{1,9},{2,10},{3,11},{4,12},{5,13},{6,14},{7,15},{8,0},{9,1},... | collective-permute-start | bytes 294920 | tf_op jit(solution)/shard_map/ppermute | solution.py:503
  132.2 1.8 shard_map.198
  136.3 3.9 %shard_map.200.refs_5_ = f32[768,512]{1,0:T(8,128)} custom-call(bf16[768,512]{1,0:T(8,128)(2,1)} %refs_0_.3, bf16[512,512]{1,0:T(8,128)(2,1)} %get-tuple-element.92.refs_3_.refs_5_.refs_4_.refs_1_, bf16[256,512]{1,0:T(8,128)(2,1)} %get-tuple-element.98.refs_6_.refs_7_.refs_5_.refs_2_, bf16[1536,512]{1,0:T(8,128)(2,1)} %refs_3_.9, ...), custom_call_target="tpu_custom_call" | custom-call | flops 402653184 | bytes 4718592 | tf_op jit(solution)/shard_map/pallas_call | solution.py:482
  141.5 1.8 shard_map.201.refs_5_.refs_1_
  146.0 2.2 %collective-permute-start.17 = (bf16[64,512]{1,0:T(8,128)(2,1)S(1)}, bf16[64,512]{1,0:T(8,128)(2,1)S(1)}, u32[]{:S(2)}, u32[]{:S(2)}) collective-permute-start(bf16[64,512]{1,0:T(8,128)(2,1)S(1)} %copy-done.32), channel_id=1, source_target_pairs={{0,12},{1,13},{2,14},{3,15},{4,8},{5,9},{6,10},{7,11},{8,4},{9,5},... | collective-permute-start | bytes 196616 | tf_op jit(solution)/shard_map/ppermute | solution.py:503
  151.8 7.1 %collective-permute-start.30 = (bf16[384,512]{1,0:T(8,128)(2,1)}, bf16[384,512]{1,0:T(8,128)(2,1)S(1)}, u32[]{:S(2)}, u32[]{:S(2)}) collective-permute-start(bf16[384,512]{1,0:T(8,128)(2,1)} %shard_map.201.refs_5_.refs_1_), channel_id=1, source_target_pairs={{0,1},{1,0},{2,3},{3,2},{4,5},{5,4},{6,7},{7,6},{8,9},{9,8},{10,11... | collective-permute-start | bytes 1179656 | tf_op jit(solution)/shard_map/ppermute | solution.py:503
  161.3 2.0 %collective-permute-start.25 = (bf16[64,512]{1,0:T(8,128)(2,1)}, bf16[64,512]{1,0:T(8,128)(2,1)S(1)}, u32[]{:S(2)}, u32[]{:S(2)}) collective-permute-start(bf16[64,512]{1,0:T(8,128)(2,1)} %shard_map.202.refs_5_.refs_1_), channel_id=1, source_target_pairs={{0,8},{1,9},{2,10},{3,11},{4,12},{5,13},{6,14},{7,15},{8,0},{9,1},... | collective-permute-start | bytes 196616 | tf_op jit(solution)/shard_map/ppermute | solution.py:503
  164.1 1.7 shard_map.203.refs_4_.refs_1_
  166.5 2.0 %shard_map.204.refs_5_ = f32[128,512]{1,0:T(8,128)} custom-call(f32[128,512]{1,0:T(8,128)} %get-tuple-element.81.refs_0_, f32[128,512]{1,0:T(8,128)} %get-tuple-element.115.refs_1_, bf16[256,128]{1,0:T(8,128)(2,1)} %get-tuple-element.74.refs_5_.refs_1_.refs_2_, bf16[256,512]{1,0:T(8,128)(2,1)} %bitcast.19, bf16[256,512]{1,0:T(8,128)(2,1)} %shard_map.203.refs_4_.refs_1_), custom_call_target="tpu_custom_call" | custom-call | flops 100000000 | bytes 1114112 | tf_op jit(solution)/shard_map/pallas_call | solution.py:482
  171.2 1.7 shard_map.205.refs_5_
  172.9 2.0 %collective-permute-start.32 = (bf16[384,512]{1,0:T(8,128)(2,1)S(1)}, bf16[384,512]{1,0:T(8,128)(2,1)S(1)}, u32[]{:S(2)}, u32[]{:S(2)}) collective-permute-start(bf16[384,512]{1,0:T(8,128)(2,1)S(1)} %collective-permute-done.31.refs_3_), channel_id=1, source_target_pairs={{0,1},{1,0},{2,3},{3,2},{4,5},{5,4},{6,7},{7,6},{8,9},{9,8},{10,11... | collective-permute-start | bytes 1179656 | tf_op jit(solution)/shard_map/ppermute | solution.py:503
  175.1 3.5 %collective-permute-start.27 = (bf16[256,512]{1,0:T(8,128)(2,1)}, bf16[256,512]{1,0:T(8,128)(2,1)S(1)}, u32[]{:S(2)}, u32[]{:S(2)}) collective-permute-start(bf16[256,512]{1,0:T(8,128)(2,1)} %shard_map.205.refs_5_), channel_id=1, source_target_pairs={{0,1},{1,0},{2,3},{3,2},{4,5},{5,4},{6,7},{7,6},{8,9},{9,8},{10,11... | collective-permute-start | bytes 786440 | tf_op jit(solution)/shard_map/ppermute | solution.py:503
  178.7 2.8 %collective-permute-done.28.refs_7_ = bf16[256,512]{1,0:T(8,128)(2,1)S(1)} collective-permute-done((bf16[256,512]{1,0:T(8,128)(2,1)}, bf16[256,512]{1,0:T(8,128)(2,1)S(1)}, u32[]{:S(2)}, u32[]{:S(2)}) %collective-permute-start.28) | collective-permute-done | bytes 262176 | tf_op jit(solution)/shard_map/ppermute | solution.py:503
  184.5 2.6 %shard_map.206 = (bf16[1024,512]{1,0:T(8,128)(2,1)}, bf16[512,512]{1,0:T(8,128)(2,1)}) custom-call(s32[1]{0:T(128)} %bitcast.11.refs_0_, bf16[384,512]{1,0:T(8,128)(2,1)} %shard_map.201.refs_5_.refs_1_, bf16[384,512]{1,0:T(8,128)(2,1)} %copy-done.10, bf16[384,512]{1,0:T(8,128)(2,1)} %copy-done.9, bf16[384,512]{1,0:T(8,128)(2,1)} %copy-done.11, ...), custom_call_target="tpu_custom_call" | custom-call | flops 1000000 | bytes 3145732 | tf_op jit(solution)/shard_map/pallas_call | solution.py:482
  188.1 3.0 %shard_map.207 = (bf16[1536,512]{1,0:T(8,128)(2,1)}, bf16[512,512]{1,0:T(8,128)(2,1)}) custom-call(s32[1]{0:T(128)} %bitcast.11.refs_0_, bf16[256,512]{1,0:T(8,128)(2,1)} %shard_map.203.refs_4_.refs_1_, bf16[256,512]{1,0:T(8,128)(2,1)} %copy-done.18, bf16[256,512]{1,0:T(8,128)(2,1)} %copy-done.16, bf16[256,512]{1,0:T(8,128)(2,1)} %copy-done.20, ...), custom_call_target="tpu_custom_call" | custom-call | flops 1000000 | bytes 4194308 | tf_op jit(solution)/shard_map/pallas_call | solution.py:482
  (151 shorter events, 34.1 us)
Async XLA Ops:
  2.3 13.0 %all-to-all-start = ((s32[16,1,16]{2,1,0:T(1,128)}), s32[16,1,16]{2,1,0:T(1,128)S(1)}, u32[]{:S(2)}, u32[]{:S(2)}) async-start(s32[16,1,16]{2,1,0:T(1,128)} %bitcast.26), calls=%async_computation | async-start | bytes 16384 | tf_op jit(solution)/shard_map/all_to_all | solution.py:588
  18.0 13.6 %all-to-all-start.1 = ((bf16[16,16,512]{2,1,0:T(8,128)(2,1)}), bf16[16,16,512]{2,1,0:T(8,128)(2,1)S(1)}, u32[]{:S(2)}, u32[]{:S(2)}) async-start(bf16[16,16,512]{2,1,0:T(8,128)(2,1)} %bitcast.24), calls=%async_computation.1 | async-start | bytes 524288 | tf_op jit(solution)/shard_map/all_to_all | solution.py:557
  36.6 13.5 %all-to-all-start.2 = ((bf16[16,16,512]{2,1,0:T(8,128)(2,1)}), bf16[16,16,512]{2,1,0:T(8,128)(2,1)S(1)}, u32[]{:S(2)}, u32[]{:S(2)}) async-start(bf16[16,16,512]{2,1,0:T(8,128)(2,1)} %bitcast.22), calls=%async_computation.2 | async-start | bytes 524288 | tf_op jit(solution)/shard_map/all_to_all | solution.py:557
  57.9 7.8 %collective-permute-start = (bf16[768,512]{1,0:T(8,128)(2,1)}, bf16[768,512]{1,0:T(8,128)(2,1)S(1)}, u32[]{:S(2)}, u32[]{:S(2)}) collective-permute-start(bf16[768,512]{1,0:T(8,128)(2,1)} %get-tuple-element.91.refs_7_), channel_id=1, source_target_pairs={{0,1},{1,0},{2,3},{3,2},{4,5},{5,4},{6,7},{7,6},{8,9},{9,8},{10,11... | collective-permute-start | bytes 2359304 | tf_op jit(solution)/shard_map/ppermute | solution.py:503
  58.5 12.9 %all-to-all-start.3 = ((bf16[16,16,512]{2,1,0:T(8,128)(2,1)}), bf16[16,16,512]{2,1,0:T(8,128)(2,1)S(1)}, u32[]{:S(2)}, u32[]{:S(2)}) async-start(bf16[16,16,512]{2,1,0:T(8,128)(2,1)} %bitcast.23), calls=%async_computation.3 | async-start | bytes 524288 | tf_op jit(solution)/shard_map/all_to_all | solution.py:557
  78.8 4.8 %collective-permute-start.3 = (bf16[512,512]{1,0:T(8,128)(2,1)}, bf16[512,512]{1,0:T(8,128)(2,1)S(1)}, u32[]{:S(2)}, u32[]{:S(2)}) collective-permute-start(bf16[512,512]{1,0:T(8,128)(2,1)} %get-tuple-element.107.refs_9_), channel_id=1, source_target_pairs={{0,1},{1,0},{2,3},{3,2},{4,5},{5,4},{6,7},{7,6},{8,9},{9,8},{10,11... | collective-permute-start | bytes 1572872 | tf_op jit(solution)/shard_map/ppermute | solution.py:503
  83.3 13.0 %collective-permute-start.1 = (bf16[512,512]{1,0:T(8,128)(2,1)}, bf16[512,512]{1,0:T(8,128)(2,1)S(1)}, u32[]{:S(2)}, u32[]{:S(2)}) collective-permute-start(bf16[512,512]{1,0:T(8,128)(2,1)} %get-tuple-element.109.refs_3_), channel_id=1, source_target_pairs={{0,1},{1,0},{2,3},{3,2},{4,5},{5,4},{6,7},{7,6},{8,9},{9,8},{10,11... | collective-permute-start | bytes 1572872 | tf_op jit(solution)/shard_map/ppermute | solution.py:503
  83.3 10.3 %collective-permute-start.2 = (bf16[384,512]{1,0:T(8,128)(2,1)S(1)}, bf16[384,512]{1,0:T(8,128)(2,1)S(1)}, u32[]{:S(2)}, u32[]{:S(2)}) collective-permute-start(bf16[384,512]{1,0:T(8,128)(2,1)S(1)} %copy-done.13), channel_id=1, source_target_pairs={{0,2},{1,3},{2,0},{3,1},{4,6},{5,7},{6,4},{7,5},{8,10},{9,11},{10,... | collective-permute-start | bytes 1179656 | tf_op jit(solution)/shard_map/ppermute | solution.py:503
  86.4 26.2 %collective-permute-start.4 = (bf16[256,512]{1,0:T(8,128)(2,1)}, bf16[256,512]{1,0:T(8,128)(2,1)S(1)}, u32[]{:S(2)}, u32[]{:S(2)}) collective-permute-start(bf16[256,512]{1,0:T(8,128)(2,1)} %get-tuple-element.112.refs_3_), channel_id=1, source_target_pairs={{0,2},{1,3},{2,0},{3,1},{4,6},{5,7},{6,4},{7,5},{8,10},{9,11},{10,... | collective-permute-start | bytes 786440 | tf_op jit(solution)/shard_map/ppermute | solution.py:503
  99.1 28.8 %collective-permute-start.8 = (bf16[256,512]{1,0:T(8,128)(2,1)}, bf16[256,512]{1,0:T(8,128)(2,1)S(1)}, u32[]{:S(2)}, u32[]{:S(2)}) collective-permute-start(bf16[256,512]{1,0:T(8,128)(2,1)} %get-tuple-element.114.refs_7_), channel_id=1, source_target_pairs={{0,2},{1,3},{2,0},{3,1},{4,6},{5,7},{6,4},{7,5},{8,10},{9,11},{10,... | collective-permute-start | bytes 786440 | tf_op jit(solution)/shard_map/ppermute | solution.py:503
  99.7 9.3 %copy-start.44 = (bf16[96,512]{1,0:T(8,128)(2,1)S(1)}, bf16[96,512]{1,0:T(8,128)(2,1)}, u32[]{:S(2)}) copy-start(bf16[96,512]{1,0:T(8,128)(2,1)} %get-tuple-element.124) | copy-start | bytes 294916
  99.7 10.7 %copy-start.43 = (bf16[96,512]{1,0:T(8,128)(2,1)S(1)}, bf16[96,512]{1,0:T(8,128)(2,1)}, u32[]{:S(2)}) copy-start(bf16[96,512]{1,0:T(8,128)(2,1)} %get-tuple-element.125) | copy-start | bytes 294916
  99.7 12.8 %copy-start.25 = (bf16[96,512]{1,0:T(8,128)(2,1)S(1)}, bf16[96,512]{1,0:T(8,128)(2,1)}, u32[]{:S(2)}) copy-start(bf16[96,512]{1,0:T(8,128)(2,1)} %get-tuple-element.113.refs_3_) | copy-start | bytes 294916
  103.6 62.1 %all-to-all-start.4 = ((bf16[16,16,512]{2,1,0:T(8,128)(2,1)}), bf16[16,16,512]{2,1,0:T(8,128)(2,1)S(1)}, u32[]{:S(2)}, u32[]{:S(2)}) async-start(bf16[16,16,512]{2,1,0:T(8,128)(2,1)} %bitcast.20), calls=%async_computation.4 | async-start | bytes 524288 | tf_op jit(solution)/shard_map/all_to_all | solution.py:557
  109.0 8.4 %collective-permute-start.9 = (bf16[96,512]{1,0:T(8,128)(2,1)S(1)}, bf16[96,512]{1,0:T(8,128)(2,1)S(1)}, u32[]{:S(2)}, u32[]{:S(2)}) collective-permute-start(bf16[96,512]{1,0:T(8,128)(2,1)S(1)} %copy-done.44), channel_id=1, source_target_pairs={{0,4},{1,5},{2,6},{3,7},{4,0},{5,1},{6,2},{7,3},{8,12},{9,13},{10,... | collective-permute-start | bytes 294920 | tf_op jit(solution)/shard_map/ppermute | solution.py:503
  110.4 10.0 %collective-permute-start.10 = (bf16[96,512]{1,0:T(8,128)(2,1)S(1)}, bf16[96,512]{1,0:T(8,128)(2,1)S(1)}, u32[]{:S(2)}, u32[]{:S(2)}) collective-permute-start(bf16[96,512]{1,0:T(8,128)(2,1)S(1)} %copy-done.43), channel_id=1, source_target_pairs={{0,8},{1,9},{2,10},{3,11},{4,12},{5,13},{6,14},{7,15},{8,0},{9,1},... | collective-permute-start | bytes 294920 | tf_op jit(solution)/shard_map/ppermute | solution.py:503
  112.5 13.0 %collective-permute-start.11 = (bf16[96,512]{1,0:T(8,128)(2,1)S(1)}, bf16[96,512]{1,0:T(8,128)(2,1)S(1)}, u32[]{:S(2)}, u32[]{:S(2)}) collective-permute-start(bf16[96,512]{1,0:T(8,128)(2,1)S(1)} %copy-done.25), channel_id=1, source_target_pairs={{0,12},{1,13},{2,14},{3,15},{4,8},{5,9},{6,10},{7,11},{8,4},{9,5},... | collective-permute-start | bytes 294920 | tf_op jit(solution)/shard_map/ppermute | solution.py:503
  115.1 17.1 %collective-permute-start.5 = (bf16[64,512]{1,0:T(8,128)(2,1)}, bf16[64,512]{1,0:T(8,128)(2,1)S(1)}, u32[]{:S(2)}, u32[]{:S(2)}) collective-permute-start(bf16[64,512]{1,0:T(8,128)(2,1)} %get-tuple-element.119), channel_id=1, source_target_pairs={{0,4},{1,5},{2,6},{3,7},{4,0},{5,1},{6,2},{7,3},{8,12},{9,13},{10,... | collective-permute-start | bytes 196616 | tf_op jit(solution)/shard_map/ppermute | solution.py:503
  117.3 8.2 %copy-start.26 = (bf16[96,512]{1,0:T(8,128)(2,1)}, bf16[96,512]{1,0:T(8,128)(2,1)S(1)}, u32[]{:S(2)}) copy-start(bf16[96,512]{1,0:T(8,128)(2,1)S(1)} %collective-permute-done.9.refs_2_) | copy-start | bytes 294916
  117.3 16.7 %collective-permute-start.6 = (bf16[64,512]{1,0:T(8,128)(2,1)}, bf16[64,512]{1,0:T(8,128)(2,1)S(1)}, u32[]{:S(2)}, u32[]{:S(2)}) collective-permute-start(bf16[64,512]{1,0:T(8,128)(2,1)} %get-tuple-element.120), channel_id=1, source_target_pairs={{0,8},{1,9},{2,10},{3,11},{4,12},{5,13},{6,14},{7,15},{8,0},{9,1},... | collective-permute-start | bytes 196616 | tf_op jit(solution)/shard_map/ppermute | solution.py:503
  120.4 13.6 %collective-permute-start.7 = (bf16[64,512]{1,0:T(8,128)(2,1)}, bf16[64,512]{1,0:T(8,128)(2,1)S(1)}, u32[]{:S(2)}, u32[]{:S(2)}) collective-permute-start(bf16[64,512]{1,0:T(8,128)(2,1)} %get-tuple-element.121.refs_5_), channel_id=1, source_target_pairs={{0,12},{1,13},{2,14},{3,15},{4,8},{5,9},{6,10},{7,11},{8,4},{9,5},... | collective-permute-start | bytes 196616 | tf_op jit(solution)/shard_map/ppermute | solution.py:503
  127.9 12.3 %collective-permute-start.20 = (bf16[96,512]{1,0:T(8,128)(2,1)}, bf16[96,512]{1,0:T(8,128)(2,1)S(1)}, u32[]{:S(2)}, u32[]{:S(2)}) collective-permute-start(bf16[96,512]{1,0:T(8,128)(2,1)} %shard_map.197.refs_3_.refs_1_), channel_id=1, source_target_pairs={{0,12},{1,13},{2,14},{3,15},{4,8},{5,9},{6,10},{7,11},{8,4},{9,5},... | collective-permute-start | bytes 294920 | tf_op jit(solution)/shard_map/ppermute | solution.py:503
  127.9 12.3 %collective-permute-start.19 = (bf16[96,512]{1,0:T(8,128)(2,1)}, bf16[96,512]{1,0:T(8,128)(2,1)S(1)}, u32[]{:S(2)}, u32[]{:S(2)}) collective-permute-start(bf16[96,512]{1,0:T(8,128)(2,1)} %shard_map.197.refs_3_.refs_1_), channel_id=1, source_target_pairs={{0,8},{1,9},{2,10},{3,11},{4,12},{5,13},{6,14},{7,15},{8,0},{9,1},... | collective-permute-start | bytes 294920 | tf_op jit(solution)/shard_map/ppermute | solution.py:503
  132.2 8.0 %collective-permute-start.18 = (bf16[96,512]{1,0:T(8,128)(2,1)}, bf16[96,512]{1,0:T(8,128)(2,1)S(1)}, u32[]{:S(2)}, u32[]{:S(2)}) collective-permute-start(bf16[96,512]{1,0:T(8,128)(2,1)} %shard_map.197.refs_3_.refs_1_), channel_id=1, source_target_pairs={{0,4},{1,5},{2,6},{3,7},{4,0},{5,1},{6,2},{7,3},{8,12},{9,13},{10,... | collective-permute-start | bytes 294920 | tf_op jit(solution)/shard_map/ppermute | solution.py:503
  140.2 8.1 %copy-start.6 = (bf16[64,512]{1,0:T(8,128)(2,1)S(1)}, bf16[64,512]{1,0:T(8,128)(2,1)}, u32[]{:S(2)}) copy-start(bf16[64,512]{1,0:T(8,128)(2,1)} %shard_map.199.refs_4_.refs_1_) | copy-start | bytes 196612
  143.3 29.6 %collective-permute-start.31 = (bf16[384,512]{1,0:T(8,128)(2,1)}, bf16[384,512]{1,0:T(8,128)(2,1)S(1)}, u32[]{:S(2)}, u32[]{:S(2)}) collective-permute-start(bf16[384,512]{1,0:T(8,128)(2,1)} %shard_map.201.refs_5_.refs_1_), channel_id=1, source_target_pairs={{0,2},{1,3},{2,0},{3,1},{4,6},{5,7},{6,4},{7,5},{8,10},{9,11},{10,... | collective-permute-start | bytes 1179656 | tf_op jit(solution)/shard_map/ppermute | solution.py:503
  144.7 4.6 %collective-permute-start.15 = (bf16[64,512]{1,0:T(8,128)(2,1)S(1)}, bf16[64,512]{1,0:T(8,128)(2,1)S(1)}, u32[]{:S(2)}, u32[]{:S(2)}) collective-permute-start(bf16[64,512]{1,0:T(8,128)(2,1)S(1)} %copy-done.46), channel_id=1, source_target_pairs={{0,4},{1,5},{2,6},{3,7},{4,0},{5,1},{6,2},{7,3},{8,12},{9,13},{10,... | collective-permute-start | bytes 196616 | tf_op jit(solution)/shard_map/ppermute | solution.py:503
  145.9 5.3 %collective-permute-start.16 = (bf16[64,512]{1,0:T(8,128)(2,1)S(1)}, bf16[64,512]{1,0:T(8,128)(2,1)S(1)}, u32[]{:S(2)}, u32[]{:S(2)}) collective-permute-start(bf16[64,512]{1,0:T(8,128)(2,1)S(1)} %copy-done.45), channel_id=1, source_target_pairs={{0,8},{1,9},{2,10},{3,11},{4,12},{5,13},{6,14},{7,15},{8,0},{9,1},... | collective-permute-start | bytes 196616 | tf_op jit(solution)/shard_map/ppermute | solution.py:503
  146.0 5.8 %collective-permute-start.17 = (bf16[64,512]{1,0:T(8,128)(2,1)S(1)}, bf16[64,512]{1,0:T(8,128)(2,1)S(1)}, u32[]{:S(2)}, u32[]{:S(2)}) collective-permute-start(bf16[64,512]{1,0:T(8,128)(2,1)S(1)} %copy-done.32), channel_id=1, source_target_pairs={{0,12},{1,13},{2,14},{3,15},{4,8},{5,9},{6,10},{7,11},{8,4},{9,5},... | collective-permute-start | bytes 196616 | tf_op jit(solution)/shard_map/ppermute | solution.py:503
  148.3 12.3 %collective-permute-start.14 = (bf16[64,512]{1,0:T(8,128)(2,1)S(1)}, bf16[64,512]{1,0:T(8,128)(2,1)S(1)}, u32[]{:S(2)}, u32[]{:S(2)}) collective-permute-start(bf16[64,512]{1,0:T(8,128)(2,1)S(1)} %copy-done.6), channel_id=1, source_target_pairs={{0,12},{1,13},{2,14},{3,15},{4,8},{5,9},{6,10},{7,11},{8,4},{9,5},... | collective-permute-start | bytes 196616 | tf_op jit(solution)/shard_map/ppermute | solution.py:503
  149.3 9.6 %copy-start.29 = (bf16[64,512]{1,0:T(8,128)(2,1)}, bf16[64,512]{1,0:T(8,128)(2,1)S(1)}, u32[]{:S(2)}) copy-start(bf16[64,512]{1,0:T(8,128)(2,1)S(1)} %collective-permute-done.15.refs_2_) | copy-start | bytes 196612
  149.3 12.0 %collective-permute-start.13 = (bf16[64,512]{1,0:T(8,128)(2,1)S(1)}, bf16[64,512]{1,0:T(8,128)(2,1)S(1)}, u32[]{:S(2)}, u32[]{:S(2)}) collective-permute-start(bf16[64,512]{1,0:T(8,128)(2,1)S(1)} %copy-done.6), channel_id=1, source_target_pairs={{0,8},{1,9},{2,10},{3,11},{4,12},{5,13},{6,14},{7,15},{8,0},{9,1},... | collective-permute-start | bytes 196616 | tf_op jit(solution)/shard_map/ppermute | solution.py:503
  151.3 7.6 %copy-start.30 = (bf16[64,512]{1,0:T(8,128)(2,1)}, bf16[64,512]{1,0:T(8,128)(2,1)S(1)}, u32[]{:S(2)}) copy-start(bf16[64,512]{1,0:T(8,128)(2,1)S(1)} %collective-permute-done.16.refs_3_) | copy-start | bytes 196612
  151.3 12.1 %collective-permute-start.12 = (bf16[64,512]{1,0:T(8,128)(2,1)S(1)}, bf16[64,512]{1,0:T(8,128)(2,1)S(1)}, u32[]{:S(2)}, u32[]{:S(2)}) collective-permute-start(bf16[64,512]{1,0:T(8,128)(2,1)S(1)} %copy-done.6), channel_id=1, source_target_pairs={{0,4},{1,5},{2,6},{3,7},{4,0},{5,1},{6,2},{7,3},{8,12},{9,13},{10,... | collective-permute-start | bytes 196616 | tf_op jit(solution)/shard_map/ppermute | solution.py:503
  151.8 31.2 %collective-permute-start.30 = (bf16[384,512]{1,0:T(8,128)(2,1)}, bf16[384,512]{1,0:T(8,128)(2,1)S(1)}, u32[]{:S(2)}, u32[]{:S(2)}) collective-permute-start(bf16[384,512]{1,0:T(8,128)(2,1)} %shard_map.201.refs_5_.refs_1_), channel_id=1, source_target_pairs={{0,1},{1,0},{2,3},{3,2},{4,5},{5,4},{6,7},{7,6},{8,9},{9,8},{10,11... | collective-permute-start | bytes 1179656 | tf_op jit(solution)/shard_map/ppermute | solution.py:503
  160.5 8.0 %collective-permute-start.26 = (bf16[64,512]{1,0:T(8,128)(2,1)}, bf16[64,512]{1,0:T(8,128)(2,1)S(1)}, u32[]{:S(2)}, u32[]{:S(2)}) collective-permute-start(bf16[64,512]{1,0:T(8,128)(2,1)} %shard_map.202.refs_5_.refs_1_), channel_id=1, source_target_pairs={{0,12},{1,13},{2,14},{3,15},{4,8},{5,9},{6,10},{7,11},{8,4},{9,5},... | collective-permute-start | bytes 196616 | tf_op jit(solution)/shard_map/ppermute | solution.py:503
  161.3 8.6 %collective-permute-start.25 = (bf16[64,512]{1,0:T(8,128)(2,1)}, bf16[64,512]{1,0:T(8,128)(2,1)S(1)}, u32[]{:S(2)}, u32[]{:S(2)}) collective-permute-start(bf16[64,512]{1,0:T(8,128)(2,1)} %shard_map.202.refs_5_.refs_1_), channel_id=1, source_target_pairs={{0,8},{1,9},{2,10},{3,11},{4,12},{5,13},{6,14},{7,15},{8,0},{9,1},... | collective-permute-start | bytes 196616 | tf_op jit(solution)/shard_map/ppermute | solution.py:503
  163.4 6.5 %collective-permute-start.24 = (bf16[64,512]{1,0:T(8,128)(2,1)}, bf16[64,512]{1,0:T(8,128)(2,1)S(1)}, u32[]{:S(2)}, u32[]{:S(2)}) collective-permute-start(bf16[64,512]{1,0:T(8,128)(2,1)} %shard_map.202.refs_5_.refs_1_), channel_id=1, source_target_pairs={{0,4},{1,5},{2,6},{3,7},{4,0},{5,1},{6,2},{7,3},{8,12},{9,13},{10,... | collective-permute-start | bytes 196616 | tf_op jit(solution)/shard_map/ppermute | solution.py:503
  165.8 9.1 %copy-start = (bf16[256,512]{1,0:T(8,128)(2,1)S(1)}, bf16[256,512]{1,0:T(8,128)(2,1)}, u32[]{:S(2)}) copy-start(bf16[256,512]{1,0:T(8,128)(2,1)} %shard_map.203.refs_4_.refs_1_) | copy-start | bytes 786436
  168.5 6.6 %collective-permute-start.22 = (bf16[256,512]{1,0:T(8,128)(2,1)}, bf16[256,512]{1,0:T(8,128)(2,1)S(1)}, u32[]{:S(2)}, u32[]{:S(2)}) collective-permute-start(bf16[256,512]{1,0:T(8,128)(2,1)} %shard_map.203.refs_4_.refs_1_), channel_id=1, source_target_pairs={{0,2},{1,3},{2,0},{3,1},{4,6},{5,7},{6,4},{7,5},{8,10},{9,11},{10,... | collective-permute-start | bytes 786440 | tf_op jit(solution)/shard_map/ppermute | solution.py:503
  172.8 8.6 %collective-permute-start.28 = (bf16[256,512]{1,0:T(8,128)(2,1)}, bf16[256,512]{1,0:T(8,128)(2,1)S(1)}, u32[]{:S(2)}, u32[]{:S(2)}) collective-permute-start(bf16[256,512]{1,0:T(8,128)(2,1)} %shard_map.205.refs_5_), channel_id=1, source_target_pairs={{0,2},{1,3},{2,0},{3,1},{4,6},{5,7},{6,4},{7,5},{8,10},{9,11},{10,... | collective-permute-start | bytes 786440 | tf_op jit(solution)/shard_map/ppermute | solution.py:503
  172.9 10.2 %copy-start.9 = (bf16[384,512]{1,0:T(8,128)(2,1)}, bf16[384,512]{1,0:T(8,128)(2,1)S(1)}, u32[]{:S(2)}) copy-start(bf16[384,512]{1,0:T(8,128)(2,1)S(1)} %collective-permute-done.31.refs_3_) | copy-start | bytes 1179652
  172.9 10.2 %collective-permute-start.32 = (bf16[384,512]{1,0:T(8,128)(2,1)S(1)}, bf16[384,512]{1,0:T(8,128)(2,1)S(1)}, u32[]{:S(2)}, u32[]{:S(2)}) collective-permute-start(bf16[384,512]{1,0:T(8,128)(2,1)S(1)} %collective-permute-done.31.refs_3_), channel_id=1, source_target_pairs={{0,1},{1,0},{2,3},{3,2},{4,5},{5,4},{6,7},{7,6},{8,9},{9,8},{10,11... | collective-permute-start | bytes 1179656 | tf_op jit(solution)/shard_map/ppermute | solution.py:503
  174.9 12.3 %collective-permute-start.21 = (bf16[256,512]{1,0:T(8,128)(2,1)S(1)}, bf16[256,512]{1,0:T(8,128)(2,1)S(1)}, u32[]{:S(2)}, u32[]{:S(2)}) collective-permute-start(bf16[256,512]{1,0:T(8,128)(2,1)S(1)} %copy-done), channel_id=1, source_target_pairs={{0,1},{1,0},{2,3},{3,2},{4,5},{5,4},{6,7},{7,6},{8,9},{9,8},{10,11... | collective-permute-start | bytes 786440 | tf_op jit(solution)/shard_map/ppermute | solution.py:503
  175.1 12.1 %copy-start.16 = (bf16[256,512]{1,0:T(8,128)(2,1)}, bf16[256,512]{1,0:T(8,128)(2,1)S(1)}, u32[]{:S(2)}) copy-start(bf16[256,512]{1,0:T(8,128)(2,1)S(1)} %collective-permute-done.22.refs_3_) | copy-start | bytes 786436
  175.1 12.0 %collective-permute-start.27 = (bf16[256,512]{1,0:T(8,128)(2,1)}, bf16[256,512]{1,0:T(8,128)(2,1)S(1)}, u32[]{:S(2)}, u32[]{:S(2)}) collective-permute-start(bf16[256,512]{1,0:T(8,128)(2,1)} %shard_map.205.refs_5_), channel_id=1, source_target_pairs={{0,1},{1,0},{2,3},{3,2},{4,5},{5,4},{6,7},{7,6},{8,9},{9,8},{10,11... | collective-permute-start | bytes 786440 | tf_op jit(solution)/shard_map/ppermute | solution.py:503
  181.4 5.7 %collective-permute-start.23 = (bf16[256,512]{1,0:T(8,128)(2,1)S(1)}, bf16[256,512]{1,0:T(8,128)(2,1)S(1)}, u32[]{:S(2)}, u32[]{:S(2)}) collective-permute-start(bf16[256,512]{1,0:T(8,128)(2,1)S(1)} %collective-permute-done.22.refs_3_), channel_id=1, source_target_pairs={{0,1},{1,0},{2,3},{3,2},{4,5},{5,4},{6,7},{7,6},{8,9},{9,8},{10,11... | collective-permute-start | bytes 786440 | tf_op jit(solution)/shard_map/ppermute | solution.py:503
  183.1 4.1 %collective-permute-start.29 = (bf16[256,512]{1,0:T(8,128)(2,1)S(1)}, bf16[256,512]{1,0:T(8,128)(2,1)S(1)}, u32[]{:S(2)}, u32[]{:S(2)}) collective-permute-start(bf16[256,512]{1,0:T(8,128)(2,1)S(1)} %collective-permute-done.28.refs_7_), channel_id=1, source_target_pairs={{0,1},{1,0},{2,3},{3,2},{4,5},{5,4},{6,7},{7,6},{8,9},{9,8},{10,11... | collective-permute-start | bytes 786440 | tf_op jit(solution)/shard_map/ppermute | solution.py:503
  (37 other events, 69.8 us)

commit v3 on v1

--- a/solution.py
+++ b/solution.py
@@ -106,7 +106,7 @@
     reply_ref[...] = dot(asked_marks, nodes_ref[...]).astype(BF16)
 
 
-def cut_marks_kernel(dest_ref, local_ref, dep_ref, senders_ref, receivers_ref, *, domains, slots):
+def cut_marks_kernel(dest_ref, local_ref, senders_ref, receivers_ref, *, domains, slots):
     width = senders_ref.shape[1]
     base = width - domains * slots
     dest = to_column(dest_ref[...]).astype(jnp.int32)
@@ -136,7 +136,6 @@
     nodes_ref,
     w_in_ref,
     w_out_ref,
-    dep_ref,
     senders_ref,
     receivers_ref,
     sender_ref,
@@ -213,7 +212,7 @@
     outgoing_ref[...] = dot_rows(receivers_ref[:, base:], message).astype(BF16)
 
 
-def new_edges_kernel(edges_ref, inner_ref, cut_ref, dep_ref, out_ref):
+def new_edges_kernel(edges_ref, inner_ref, cut_ref, out_ref):
     inner_rows = inner_ref.shape[0]
 
     def added(edge, normed):
@@ -261,7 +260,7 @@
 
 
 def node_weights_kernel(
-    place_ref, nodes_ref, aggregate_ref, hidden_ref, grad_out_ref, grad_pre_ref, keep_ref, send_ref
+    me_ref, nodes_ref, aggregate_ref, hidden_ref, grad_out_ref, grad_pre_ref, keep_ref, send_ref
 ):
     latent = nodes_ref.shape[1]
     half = latent // 2
@@ -273,11 +272,15 @@
         high_ref[:half] = dot_rows(aggregate_ref[:, half:], grad_pre).astype(BF16)
         high_ref[half:] = dot_rows(hidden_ref[...], grad_out).astype(BF16)
 
-    @pl.when(place_ref[0] == 0)
+    halves(me_ref, keep_ref, send_ref, fill)
+
+
+def halves(me_ref, keep_ref, send_ref, fill):
+    @pl.when((me_ref[0] & 1) == 0)
     def _():
         fill(keep_ref, send_ref)
 
-    @pl.when(place_ref[0] != 0)
+    @pl.when((me_ref[0] & 1) != 0)
     def _():
         fill(send_ref, keep_ref)
 
@@ -295,7 +298,6 @@
     scale_ref,
     slope_ref,
     w_out_ref,
-    dep_ref,
     grad_out_ref,
     grad_pre_ref,
 ):
@@ -335,7 +337,7 @@
 
 
 def edge_weights_kernel(
-    place_ref,
+    me_ref,
     edges_ref,
     inner_sender_ref,
     cut_sender_ref,
@@ -347,13 +349,14 @@
     cut_out_ref,
     inner_pre_ref,
     cut_pre_ref,
-    dep_ref,
     out_ref,
+    *,
+    turned,
 ):
     latent = edges_ref.shape[1]
     inner_rows = inner_pre_ref.shape[0]
 
-    @pl.when(place_ref[0] == 0)
+    @pl.when((me_ref[0] & 1) == turned)
     def _():
         inner_pre, cut_pre = inner_pre_ref[...], cut_pre_ref[...]
         out_ref[:latent] = (
@@ -363,7 +366,7 @@
             dot_rows(inner_sender_ref[...], inner_pre) + dot_rows(cut_sender_ref[...], cut_pre)
         ).astype(BF16)
 
-    @pl.when(place_ref[0] != 0)
+    @pl.when((me_ref[0] & 1) != turned)
     def _():
         out_ref[:latent] = (
             dot_rows(inner_receiver_ref[...], inner_pre_ref[...])
@@ -383,7 +386,6 @@
     inner_pre_ref,
     cut_pre_ref,
     w_in_ref,
-    dep_ref,
     local_ref,
     outgoing_ref,
 ):
@@ -406,7 +408,7 @@
     )
 
 
-def edge_grads_kernel(ct_ref, inner_pre_ref, cut_pre_ref, w_edge_ref, dep_ref, out_ref, *, blocks):
+def edge_grads_kernel(ct_ref, inner_pre_ref, cut_pre_ref, w_edge_ref, out_ref, *, blocks):
     inside = pl.program_id(0) < blocks
 
     @pl.when(inside)
@@ -433,21 +435,35 @@
     return jax.ShapeDtypeStruct(shape, dtype)
 
 
-def run(body, outs, ins, flops, specs=None, out_specs=None, grid=None):
-    single = not isinstance(outs, (list, tuple))
-    out_shape = [outs] if single else list(outs)
-    moved = sum(item.size * item.dtype.itemsize for item in list(ins) + out_shape)
-    extra = {} if grid is None else {"grid": grid}
-    result = pl.pallas_call(
-        body,
-        out_shape=out_shape,
-        in_specs=[VMEM] * len(ins) if specs is None else specs,
-        out_specs=[VMEM] * len(out_shape) if out_specs is None else out_specs,
-        compiler_params=pltpu.CompilerParams(vmem_limit_bytes=VMEM_LIMIT),
-        cost_estimate=pl.CostEstimate(flops=flops, bytes_accessed=moved, transcendentals=0),
-        **extra,
-    )(*ins)
-    return result[0] if single else result
+class Line:
+    def __init__(self):
+        self.last = None
+
+    def run(self, body, outs, ins, flops, specs=None, out_specs=None, grid=None):
+        single = not isinstance(outs, (list, tuple))
+        out_shape = [outs] if single else list(outs)
+        specs = [VMEM] * len(ins) if specs is None else list(specs)
+        moved = sum(item.size * item.dtype.itemsize for item in list(ins) + out_shape)
+        count, extra = len(ins), {} if grid is None else {"grid": grid}
+        ins = list(ins)
+        if self.last is not None:
+            ins.append(self.last)
+            specs.append(ANY)
+
+        def ordered(*refs):
+            return body(*refs[:count], *refs[len(ins) :])
+
+        result = pl.pallas_call(
+            ordered,
+            out_shape=out_shape,
+            in_specs=specs,
+            out_specs=[VMEM] * len(out_shape) if out_specs is None else out_specs,
+            compiler_params=pltpu.CompilerParams(vmem_limit_bytes=VMEM_LIMIT),
+            cost_estimate=pl.CostEstimate(flops=flops, bytes_accessed=moved, transcendentals=0),
+            **extra,
+        )(*ins)
+        self.last = result[-1]
+        return result[0] if single else result
 
 
 def bit_groups(devices):
@@ -460,41 +476,55 @@
     return groups
 
 
-def partner_pairs(devices, mask):
-    return [(device, device ^ mask) for device in range(devices)]
-
-
-def reduce_rows(keep, send, devices):
-    me = lax.axis_index("dom")
-    groups = bit_groups(devices)
-    received = lax.ppermute(send, "dom", partner_pairs(devices, 1))
-    rows = (keep.astype(F32) + received.astype(F32)).astype(BF16)
-    for low, width in groups[1:]:
-        size = 1 << width
-        place = (me >> low) & (size - 1)
-        chunk = rows.shape[0] // size
-        pieces = rows.reshape(size, chunk, rows.shape[1])
-        total = lax.dynamic_index_in_dim(pieces, place, 0, False).astype(F32)
-        for turn in range(1, size):
-            sent = lax.dynamic_index_in_dim(pieces, place ^ turn, 0, False)
-            total += lax.ppermute(sent, "dom", partner_pairs(devices, turn << low)).astype(F32)
-        rows = total.astype(BF16)
-    return rows
-
-
-def gather_rows(rows, devices):
-    me = lax.axis_index("dom")
-    for low, width in bit_groups(devices)[::-1]:
-        size = 1 << width
-        place = (me >> low) & (size - 1)
-        whole = jnp.zeros((size,) + rows.shape, rows.dtype)
-        for turn in range(size):
-            piece = rows
-            if turn:
-                piece = lax.ppermute(rows, "dom", partner_pairs(devices, turn << low))
-            whole = lax.dynamic_update_index_in_dim(whole, piece, place ^ turn, 0)
-        rows = whole.reshape(size * rows.shape[0], rows.shape[1])
-    return rows
+def across(rows, devices, mask):
+    return lax.ppermute(rows, "dom", [(device, device ^ mask) for device in range(devices)])
+
+
+def fence(*values):
+    return lax.optimization_barrier(values)
+
+
+def place_of(low, size):
+    return (lax.axis_index("dom") >> low) & (size - 1)
+
+
+def pieces_of(rows, low, width):
+    size = 1 << width
+    place = place_of(low, size)
+    pieces = rows.reshape(size, rows.shape[0] // size, rows.shape[1])
+    return [lax.dynamic_index_in_dim(pieces, place ^ turn, 0, False) for turn in range(size)]
+
+
+def traded(pieces, devices, low):
+    return pieces[:1] + [
+        across(piece, devices, turn << low) for turn, piece in enumerate(pieces) if turn
+    ]
+
+
+def handed(rows, devices, low, width):
+    return traded([rows] * (1 << width), devices, low)
+
+
+def added(*parts):
+    return sum(part.astype(F32) for part in parts).astype(BF16)
+
+
+def joined(parts, low):
+    size = len(parts)
+    place = place_of(low, size)
+    if size == 2:
+        orders = [jnp.concatenate(parts), jnp.concatenate(parts[::-1])]
+        return jnp.where(place == 0, *orders)
+    whole = jnp.zeros((size,) + parts[0].shape, parts[0].dtype)
+    for turn, part in enumerate(parts):
+        whole = lax.dynamic_update_index_in_dim(whole, part, place ^ turn, 0)
+    return whole.reshape(size * parts[0].shape[0], parts[0].shape[1])
+
+
+def last_step(rows, others, lower, split):
+    half = rows.shape[0]
+    low, high = jnp.where(lower, rows, others), jnp.where(lower, others, rows)
+    return jnp.concatenate([low, high[: split - half]], axis=0), high[split - half :]
 
 
 def exchange(rows, domains):
@@ -525,21 +555,20 @@
     total_slots = domains * slots
     table = node_rows + total_slots
     square = 2 * latent * latent
-    place = lax.axis_index("dom") & 1
-    mine, other = place.reshape(1), (1 - place).reshape(1)
-
-    ask = run(
+    me = lax.axis_index("dom").reshape(1)
+    line = Line()
+
+    ask = line.run(
         ask_kernel, shaped(jnp.int32, domains, slots), [cut_dest.reshape(1, -1), cut_remote.reshape(1, -1)], 10**7
     )
     asked = lax.all_to_all(ask, "dom", split_axis=0, concat_axis=0, tiled=True)
-    cut_senders, cut_receivers = run(
+    cut_senders, cut_receivers = line.run(
         functools.partial(cut_marks_kernel, domains=domains, slots=slots),
         [shaped(BF16, cut_rows, table)] * 2,
-        [cut_dest.reshape(1, -1), cut_local.reshape(1, -1), ask],
+        [cut_dest.reshape(1, -1), cut_local.reshape(1, -1)],
         10**8,
-        [VMEM, VMEM, ANY],
-    )
-    reply, asked_marks = run(
+    )
+    reply, asked_marks = line.run(
         reply_kernel,
         [shaped(BF16, total_slots, latent), shaped(BF16, total_slots, node_rows)],
         [asked, nodes],
@@ -568,11 +597,11 @@
         inner_normed,
         inner_scale,
         inner_total,
-    ) = run(
+    ) = line.run(
         inner_forward_kernel,
         [shaped(kind, inner_rows, width) for kind, width in zip(saved_types, saved_widths)]
         + [shaped(F32, node_rows, latent)],
-        [inner_pairs.T, edges, nodes, w_edge_in, w_edge_out, reply],
+        [inner_pairs.T, edges, nodes, w_edge_in, w_edge_out],
         inner_rows * 4 * square,
         [
             pl.BlockSpec((2, block // 2), lambda step: (0, step)),
@@ -580,14 +609,14 @@
             all_spec(nodes),
             all_spec(w_edge_in),
             all_spec(w_edge_out),
-            ANY,
         ],
         [rows_spec(width) for width in saved_widths] + [all_spec(nodes)],
         (blocks,),
     )
 
     def last_rows(array):
-        return pl.BlockSpec((block, array.shape[1]), lambda step: (blocks, 0))
+        last = array.shape[0] // block - 1
+        return pl.BlockSpec((block, array.shape[1]), lambda step: (last, 0))
 
     (
         cut_sender,
@@ -598,7 +627,7 @@
         cut_scale,
         total,
         outgoing,
-    ) = run(
+    ) = line.run(
         cut_forward_kernel,
         [shaped(kind, cut_rows, width) for kind, width in zip(saved_types, saved_widths)][2:]
         + [shaped(F32, node_rows, latent), shaped(BF16, total_slots, latent)],
@@ -628,12 +657,11 @@
         (1,),
     )
     incoming = exchange(outgoing, domains)
-    new_edges = run(
+    new_edges = line.run(
         new_edges_kernel,
         shaped(BF16, *edges.shape),
-        [edges, inner_normed, cut_normed, outgoing],
+        [edges, inner_normed, cut_normed],
         10**7,
-        [VMEM, VMEM, VMEM, ANY],
     )
     (
         new_nodes,
@@ -644,7 +672,7 @@
         node_hidden,
         node_out,
         node_pre,
-    ) = run(
+    ) = line.run(
         node_kernel,
         [
             shaped(BF16, node_rows, latent),
@@ -657,16 +685,15 @@
         node_rows * 6 * square,
     )
     far_grad = exchange(grad_reply, domains)
-    node_keep, node_send = run(
+    node_keep, node_send = line.run(
         node_weights_kernel,
         [shaped(BF16, 3 * latent // 2, latent)] * 2,
-        [mine, nodes, aggregate, node_hidden, node_out, node_pre],
+        [me, nodes, aggregate, node_hidden, node_out, node_pre],
         node_rows * 3 * square,
         [SMEM] + [VMEM] * 5,
     )
-    node_total = gather_rows(reduce_rows(node_keep, node_send, domains), domains)
-
-    inner_out, inner_pre = run(
+    node_sum = added(node_keep, across(node_send, domains, 1))
+    inner_out, inner_pre = line.run(
         inner_backward_kernel,
         [shaped(BF16, inner_rows, latent)] * 2,
         [
@@ -677,7 +704,6 @@
             inner_scale,
             inner_slope,
             w_edge_out,
-            grad_reply,
         ],
         inner_rows * square,
         [
@@ -688,12 +714,15 @@
             rows_spec(1),
             rows_spec(latent),
             all_spec(w_edge_out),
-            ANY,
         ],
         [rows_spec(latent)] * 2,
         (blocks,),
     )
-    cut_out, cut_pre = run(
+    groups = bit_groups(domains)
+    bit_one, bits_two = groups[1], groups[2]
+    far_grad, node_sum, inner_pre = fence(far_grad, node_sum, inner_pre)
+    node_parts = traded(pieces_of(node_sum, *bit_one), domains, bit_one[0])
+    cut_out, cut_pre = line.run(
         cut_backward_kernel,
         [shaped(BF16, cut_rows, latent)] * 2,
         [
@@ -734,19 +763,28 @@
         cut_pre,
     ]
 
-    def edge_weights(half, dep):
-        return run(
-            edge_weights_kernel,
+    def edge_weights(turned, place):
+        return line.run(
+            functools.partial(edge_weights_kernel, turned=turned),
             shaped(BF16, 2 * latent, latent),
-            [half] + factors + [dep],
+            [place] + factors,
             (inner_rows + cut_rows) * 2 * square,
-            [SMEM] + [VMEM] * len(factors) + [ANY],
+            [SMEM] + [VMEM] * len(factors),
         )
 
-    edge_send = edge_weights(other, cut_pre)
-    edge_keep = edge_weights(mine, edge_send)
-    edge_total = gather_rows(reduce_rows(edge_keep, edge_send, domains), domains)
-    local_grad, outgoing_grad = run(
+    edge_send, place, *node_parts = fence(edge_weights(1, me), me, *node_parts)
+    edge_parts = [edge_weights(0, place), across(edge_send, domains, 1)]
+    node_parts = traded(pieces_of(added(*node_parts), *bits_two), domains, bits_two[0])
+    fenced = fence(*edge_parts, *node_parts, inner_pre, cut_pre)
+    edge_sum, node_sum = added(*fenced[:2]), added(*fenced[2:6])
+    inner_pre, cut_pre = fenced[6:]
+    for low, width in groups[3:]:
+        node_sum = added(*traded(pieces_of(node_sum, low, width), domains, low))
+    for low, width in groups[:2:-1]:
+        node_sum = joined(handed(node_sum, domains, low, width), low)
+    edge_parts = traded(pieces_of(edge_sum, *bit_one), domains, bit_one[0])
+    node_parts = handed(node_sum, domains, *bits_two)
+    local_grad, outgoing_grad = line.run(
         input_grads_kernel,
         [shaped(F32, node_rows, latent), shaped(BF16, total_slots, latent)],
         [
@@ -757,42 +795,62 @@
             inner_pre,
             cut_pre,
             w_edge_in,
-            edge_keep,
         ],
         (node_rows + total_slots) * 2 * square,
-        [VMEM] * 7 + [ANY],
-    )
-    grad_edges = run(
+    )
+    returned = exchange(outgoing_grad, domains)
+    fenced = fence(*edge_parts, *node_parts, inner_pre, cut_pre, local_grad)
+    edge_sum, node_sum = added(*fenced[:2]), joined(fenced[2:6], bits_two[0])
+    inner_pre, cut_pre, local_grad = fenced[6:]
+    edge_parts = traded(pieces_of(edge_sum, *bits_two), domains, bits_two[0])
+    node_parts = handed(node_sum, domains, *bit_one)
+    grad_edges = line.run(
         functools.partial(edge_grads_kernel, blocks=blocks),
         shaped(F32, *edges.shape),
-        [ct_edges, inner_pre, cut_pre, w_edge_in, edge_keep],
+        [ct_edges, inner_pre, cut_pre, w_edge_in],
         (inner_rows + cut_rows) * square,
         [
             rows_spec(latent),
             pl.BlockSpec((block, latent), lambda step: (jnp.minimum(step, blocks - 1), 0)),
             all_spec(cut_pre),
             pl.BlockSpec((latent, latent), lambda step: (0, 0)),
-            ANY,
         ],
         [rows_spec(latent)],
         (blocks + 1,),
     )
-    returned = exchange(outgoing_grad, domains)
-    grad_nodes = run(
+    fenced = fence(*edge_parts, *node_parts, returned, grad_edges)
+    edge_sum, node_sum = added(*fenced[:4]), joined(fenced[4:6], bit_one[0])
+    returned, grad_edges = fenced[6:]
+    for low, width in groups[3:]:
+        edge_sum = added(*traded(pieces_of(edge_sum, low, width), domains, low))
+    for low, width in groups[:2:-1]:
+        edge_sum = joined(handed(edge_sum, domains, low, width), low)
+    edge_parts = handed(edge_sum, domains, *bits_two)
+    others = across(node_sum, domains, 1)
+    grad_nodes = line.run(
         node_grads_kernel,
         shaped(F32, node_rows, latent),
         [self_grad, local_grad, asked_marks, returned],
         10**8,
+    )
+    *edge_parts, node_sum, others, grad_nodes = fence(*edge_parts, node_sum, others, grad_nodes)
+    edge_parts = handed(joined(edge_parts, bits_two[0]), domains, *bit_one)
+    lower = place_of(0, 2) == 0
+    grad_node_in, grad_node_out = last_step(node_sum, others, lower, 2 * latent)
+    *edge_parts, grad_node_in, grad_node_out = fence(*edge_parts, grad_node_in, grad_node_out)
+    edge_sum = joined(edge_parts, bit_one[0])
+    grad_edge_in, grad_edge_out = last_step(
+        edge_sum, across(edge_sum, domains, 1), lower, 3 * latent
     )
     return (
         new_nodes,
         new_edges,
         grad_nodes,
         grad_edges,
-        edge_total[: 3 * latent],
-        edge_total[3 * latent :],
-        node_total[: 2 * latent],
-        node_total[2 * latent :],
+        grad_edge_in,
+        grad_edge_out,
+        grad_node_in,
+        grad_node_out,
     )
 
 

time: 180 us -> 164 us (0.911)
  blocking collectives: 13.1 us -> 0 us
  waiting for transfers between devices: 55.9 us -> 48.5 us
  local copies, waits for them, and re-layouts: 9.01 us -> 4.31 us
  starting transfers between devices: 46.9 us -> 51.4 us
  other arithmetic: 0.89 us -> 5.36 us
    all_to_all x1 -> x0, blocking collectives: 13.1 us -> none  [shards(): asked = lax.all_to_all(ask, 'dom', split_axis=0, concat_axis=0, tiled=True)]
    all_to_all x0 -> x1, starting transfers between devices: none -> 7.32 us  [shards(): asked = lax.all_to_all(ask, 'dom', split_axis=0, concat_axis=0, tiled=True)]
    ppermute x20, waiting for transfers between devices: 36.4 us -> 29.2 us  [across(): lax.ppermute(rows, 'dom', [(device, device ^ mask) for device in range(de...]
    all_to_all x4, waiting for transfers between devices: 19.5 us -> 15.7 us  [exchange(): lax.all_to_all(split, 'dom', split_axis=0, concat_axis=0, tiled=True)]
    all_to_all x0 -> x1, waiting for transfers between devices: none -> 3.67 us  [shards(): asked = lax.all_to_all(ask, 'dom', split_axis=0, concat_axis=0, tiled=True)]
    all_to_all x4, starting transfers between devices: 19.8 us -> 16.8 us  [exchange(): lax.all_to_all(split, 'dom', split_axis=0, concat_axis=0, tiled=True)]
    concatenate x0 -> x2, other arithmetic: none -> 2.28 us  [last_step(): jnp.concatenate([low, high[:split - half]], axis=0)]
    slice x4 -> x3, local copies, waits for them, and re-layouts: 3.94 us -> 1.71 us  [the longest x2 1.69 us: last_step(): high[split - half:]]
  transfers between devices with their start and end apart: 24 -> 25, of which waited for: 14 -> 13; matrix products, arithmetic and copies ran while one was open for 3% -> 2% of each run, Pallas kernels for 20% -> 22%
where the time goes in v3:
time: 164 us; the launch traced here: 162 us
  Pallas kernels  51.4 us (31%)
  starting transfers between devices  51.4 us (31%)
  waiting for transfers between devices  48.5 us (30%)
  other arithmetic  5.36 us (3%)
  local copies, waits for them, and re-layouts  4.31 us (3%)
    pallas_call x15, Pallas kernels, run(): pl.pallas_call(ordered, out_shape=out_shape, in_specs=specs, out_specs=[V...  51.4 us
    ppermute x20, waiting for transfers between devices, across(): lax.ppermute(rows, 'dom', [(device, device ^ mask) for device in range(de...  29.2 us
    ppermute x20, starting transfers between devices, across(): lax.ppermute(rows, 'dom', [(device, device ^ mask) for device in range(de...  27.3 us
    all_to_all x4, starting transfers between devices, exchange(): lax.all_to_all(split, 'dom', split_axis=0, concat_axis=0, tiled=True)  16.8 us
    all_to_all x4, waiting for transfers between devices, exchange(): lax.all_to_all(split, 'dom', split_axis=0, concat_axis=0, tiled=True)  15.7 us
    all_to_all x1, starting transfers between devices, shards(): asked = lax.all_to_all(ask, 'dom', split_axis=0, concat_axis=0, tiled=True)  7.32 us
    all_to_all x1, waiting for transfers between devices, shards(): asked = lax.all_to_all(ask, 'dom', split_axis=0, concat_axis=0, tiled=True)  3.67 us
  transfers between devices with their start and end apart: 25, of which 13 were waited for; matrix products, arithmetic and copies ran while one was open for 2% of the time, Pallas kernels for 22%

profile of v3, /device:TPU:1, one launch (start us, length us, event | category | flops | bytes accessed | tf_op | source)
XLA Modules:
  0.0 161.9 jit_solution(4602594315052287262)
XLA Ops:
  0.6 1.7 %shard_map.179.refs_2_ = s32[16,16]{1,0:T(8,128)} custom-call(s32[1,128]{1,0:T(1,128)} %bitcast.83, s32[1,128]{1,0:T(1,128)} %bitcast.82), custom_call_target="tpu_custom_call" | custom-call | flops 10000000 | bytes 2048 | tf_op jit(solution)/shard_map/pallas_call | solution.py:456
  2.3 7.3 %all-to-all-start = ((s32[16,1,16]{2,1,0:T(1,128)}), s32[16,1,16]{2,1,0:T(1,128)S(1)}, u32[]{:S(2)}, u32[]{:S(2)}) async-start(s32[16,1,16]{2,1,0:T(1,128)} %bitcast.80), calls=%async_computation | async-start | bytes 16384 | tf_op jit(solution)/shard_map/all_to_all | solution.py:564
  9.7 2.0 %shard_map.180 = (bf16[256,384]{1,0:T(8,128)(2,1)}, bf16[256,384]{1,0:T(8,128)(2,1)}) custom-call(s32[1,128]{1,0:T(1,128)} %bitcast.84, s32[1,128]{1,0:T(1,128)} %bitcast.85, s32[16,16]{1,0:T(8,128)} %shard_map.179.refs_2_), custom_call_target="tpu_custom_call" | custom-call | flops 100000000 | bytes 394240 | tf_op jit(solution)/shard_map/pallas_call | solution.py:456
  11.7 3.7 %all-to-all-done = s32[16,1,16]{2,1,0:T(1,128)S(1)} async-done(((s32[16,1,16]{2,1,0:T(1,128)}), s32[16,1,16]{2,1,0:T(1,128)S(1)}, u32[]{:S(2)}, u32[]{:S(2)}) %all-to-all-start) | async-done | bytes 1056 | tf_op jit(solution)/shard_map/all_to_all | solution.py:564
  16.0 2.0 %shard_map.181 = (bf16[256,512]{1,0:T(8,128)(2,1)}, bf16[256,128]{1,0:T(8,128)(2,1)}) custom-call(s32[16,16]{1,0:T(8,128)} %bitcast.79, bf16[128,512]{1,0:T(8,128)(2,1)} %refs_1_.7, bf16[256,384]{1,0:T(8,128)(2,1)} %get-tuple-element.89.refs_2_.refs_1_.refs_0_.refs_3_), custom_call_target="tpu_custom_call" | custom-call | flops 100000000 | bytes 459776 | tf_op jit(solution)/shard_map/pallas_call | solution.py:456
  18.0 4.0 %all-to-all-start.1 = ((bf16[16,16,512]{2,1,0:T(8,128)(2,1)}), bf16[16,16,512]{2,1,0:T(8,128)(2,1)S(1)}, u32[]{:S(2)}, u32[]{:S(2)}) async-start(bf16[16,16,512]{2,1,0:T(8,128)(2,1)} %bitcast.78), calls=%async_computation.1 | async-start | bytes 524288 | tf_op jit(solution)/shard_map/all_to_all | solution.py:533
  22.0 6.3 %shard_map.182 = (bf16[512,128]{1,0:T(8,128)(2,1)}, bf16[512,128]{1,0:T(8,128)(2,1)}, bf16[512,512]{1,0:T(8,128)(2,1)}, bf16[512,512]{1,0:T(8,128)(2,1)}, bf16[5...) custom-call(s32[2,256]{1,0:T(2,128)} %bitcast.81, ...), custom_call_target="tpu_custom_call" | custom-call | flops 1073741824 | bytes 7213056 | tf_op jit(solution)/shard_map/pallas_call | solution.py:456
  28.3 3.3 %all-to-all-done.1 = bf16[16,16,512]{2,1,0:T(8,128)(2,1)S(1)} async-done(((bf16[16,16,512]{2,1,0:T(8,128)(2,1)}), bf16[16,16,512]{2,1,0:T(8,128)(2,1)S(1)}, u32[]{:S(2)}, u32[]{:S(2)}) %all-to-all-start.1) | async-done | bytes 262176 | tf_op jit(solution)/shard_map/all_to_all | solution.py:533
  32.3 4.3 %shard_map.183 = (bf16[256,512]{1,0:T(8,128)(2,1)}, bf16[256,512]{1,0:T(8,128)(2,1)}, bf16[256,512]{1,0:T(8,128)(2,1)}, f32[256,512]{1,0:T(8,128)}, f32[256,512]...) custom-call(bf16[256,384]{1,0:T(8,128)(2,1)} %get-tuple-element.88.refs_0_.refs_2_, ...), custom_call_target="tpu_custom_call" | custom-call | flops 536870912 | bytes 6292480 | tf_op jit(solution)/shard_map/pallas_call | solution.py:456
  36.6 4.0 %all-to-all-start.2 = ((bf16[16,16,512]{2,1,0:T(8,128)(2,1)}), bf16[16,16,512]{2,1,0:T(8,128)(2,1)S(1)}, u32[]{:S(2)}, u32[]{:S(2)}) async-start(bf16[16,16,512]{2,1,0:T(8,128)(2,1)} %bitcast.76), calls=%async_computation.2 | async-start | bytes 524288 | tf_op jit(solution)/shard_map/all_to_all | solution.py:533
  40.6 2.7 %shard_map.184.refs_7_ = bf16[768,512]{1,0:T(8,128)(2,1)} custom-call(bf16[768,512]{1,0:T(8,128)(2,1)} %refs_1_.9, f32[512,512]{1,0:T(8,128)} %get-tuple-element.95.refs_1_.refs_3_, f32[256,512]{1,0:T(8,128)} %get-tuple-element.96.refs_2_.refs_4_, bf16[256,512]{1,0:T(8,128)(2,1)} %get-tuple-element.93.refs_3_), custom_call_target="tpu_custom_call" | custom-call | flops 10000000 | bytes 3145728 | tf_op jit(solution)/shard_map/pallas_call | solution.py:456
  43.2 6.9 %all-to-all-done.2 = bf16[16,16,512]{2,1,0:T(8,128)(2,1)S(1)} async-done(((bf16[16,16,512]{2,1,0:T(8,128)(2,1)}), bf16[16,16,512]{2,1,0:T(8,128)(2,1)S(1)}, u32[]{:S(2)}, u32[]{:S(2)}) %all-to-all-start.2) | async-done | bytes 262176 | tf_op jit(solution)/shard_map/all_to_all | solution.py:533
  50.8 4.1 %shard_map.185 = (bf16[128,512]{1,0:T(8,128)(2,1)}, f32[128,512]{1,0:T(8,128)}, bf16[128,512]{1,0:T(8,128)(2,1)}, bf16[256,512]{1,0:T(8,128)(2,1)}, bf16[128,512...) custom-call(bf16[256,512]{1,0:T(8,128)(2,1)} %bitcast.74, ...), custom_call_target="tpu_custom_call" | custom-call | flops 402653184 | bytes 3735552 | tf_op jit(solution)/shard_map/pallas_call | solution.py:456
  55.0 2.9 %shard_map.186 = (bf16[768,512]{1,0:T(8,128)(2,1)}, bf16[768,512]{1,0:T(8,128)(2,1)}) custom-call(s32[1]{0:T(128)} %bitcast.11.refs_0_, bf16[128,512]{1,0:T(8,128)(2,1)} %refs_1_.7, bf16[128,512]{1,0:T(8,128)(2,1)} %get-tuple-element.108.refs_2_, bf16[128,512]{1,0:T(8,128)(2,1)} %get-tuple-element.109.refs_3_, bf16[128,512]{1,0:T(8,128)(2,1)} %get-tuple-element.110.refs_4_, ...), custom_call_target="tpu_custom_call" | custom-call | flops 201326592 | bytes 2228228 | tf_op jit(solution)/shard_map/pallas_call | solution.py:456
  58.5 3.4 %all-to-all-start.3 = ((bf16[16,16,512]{2,1,0:T(8,128)(2,1)}), bf16[16,16,512]{2,1,0:T(8,128)(2,1)S(1)}, u32[]{:S(2)}, u32[]{:S(2)}) async-start(bf16[16,16,512]{2,1,0:T(8,128)(2,1)} %bitcast.77), calls=%async_computation.3 | async-start | bytes 524288 | tf_op jit(solution)/shard_map/all_to_all | solution.py:533
  62.0 3.7 %shard_map.187 = (bf16[512,512]{1,0:T(8,128)(2,1)}, bf16[512,512]{1,0:T(8,128)(2,1)}) custom-call(bf16[512,128]{1,0:T(8,128)(2,1)} %get-tuple-element.104.refs_0_.refs_1_, bf16[128,512]{1,0:T(8,128)(2,1)} %get-tuple-element.105.refs_1_, bf16[768,512]{1,0:T(8,128)(2,1)} %refs_0_.3, f32[512,512]{1,0:T(8,128)} %get-tuple-element.95.refs_1_.refs_3_, ...), custom_call_target="tpu_custom_call" | custom-call | flops 268435456 | bytes 4720640 | tf_op jit(solution)/shard_map/pallas_call | solution.py:456
  65.9 5.5 %all-to-all-done.3 = bf16[16,16,512]{2,1,0:T(8,128)(2,1)S(1)} async-done(((bf16[16,16,512]{2,1,0:T(8,128)(2,1)}), bf16[16,16,512]{2,1,0:T(8,128)(2,1)S(1)}, u32[]{:S(2)}, u32[]{:S(2)}) %all-to-all-start.3) | async-done | bytes 262176 | tf_op jit(solution)/shard_map/all_to_all | solution.py:533
  72.1 3.1 %shard_map.188 = (bf16[256,512]{1,0:T(8,128)(2,1)}, bf16[256,512]{1,0:T(8,128)(2,1)}) custom-call(bf16[256,384]{1,0:T(8,128)(2,1)} %get-tuple-element.89.refs_2_.refs_1_.refs_0_.refs_3_, bf16[128,512]{1,0:T(8,128)(2,1)} %get-tuple-element.105.refs_1_, bf16[256,512]{1,0:T(8,128)(2,1)} %bitcast.72, bf16[768,512]{1,0:T(8,128)(2,1)} %refs_0_.3, ...), custom_call_target="tpu_custom_call" | custom-call | flops 134217728 | bytes 3474432 | tf_op jit(solution)/shard_map/pallas_call | solution.py:456
  75.2 4.3 %shard_map.189.refs_12_ = bf16[1024,512]{1,0:T(8,128)(2,1)} custom-call(s32[1]{0:T(128)} %bitcast.11.refs_0_, bf16[768,512]{1,0:T(8,128)(2,1)} %refs_1_.9, bf16[512,512]{1,0:T(8,128)(2,1)} %get-tuple-element.98.refs_2_, bf16[256,512]{1,0:T(8,128)(2,1)} %get-tuple-element.99.refs_3_, bf16[512,512]{1,0:T(8,128)(2,1)} %get-tuple-element.100.refs_4_, ...), custom_call_target="tpu_custom_call" | custom-call | flops 805306368 | bytes 5767172 | tf_op jit(solution)/shard_map/pallas_call | solution.py:456
  79.5 2.0 %collective-permute-done.1 = bf16[384,512]{1,0:T(8,128)(2,1)S(1)} collective-permute-done((bf16[384,512]{1,0:T(8,128)(2,1)S(1)}, bf16[384,512]{1,0:T(8,128)(2,1)S(1)}, u32[]{:S(2)}, u32[]{:S(2)}) %collective-permute-start.1) | collective-permute-done | bytes 393248 | tf_op jit(solution)/shard_map/ppermute | solution.py:480
  81.5 1.5 collective-permute-start.2
  84.7 2.1 %collective-permute-start.5 = (bf16[96,512]{1,0:T(8,128)(2,1)S(1)}, bf16[96,512]{1,0:T(8,128)(2,1)S(1)}, u32[]{:S(2)}, u32[]{:S(2)}) collective-permute-start(bf16[96,512]{1,0:T(8,128)(2,1)S(1)} %get-tuple-element.182), channel_id=1, source_target_pairs={{0,12},{1,13},{2,14},{3,15},{4,8},{5,9},{6,10},{7,11},{8,4},{9,5},... | collective-permute-start | bytes 294920 | tf_op jit(solution)/shard_map/ppermute | solution.py:480
  86.8 4.4 %shard_map.190.refs_7_ = bf16[1024,512]{1,0:T(8,128)(2,1)} custom-call(s32[1]{0:T(128)} %bitcast.11.refs_0_, bf16[768,512]{1,0:T(8,128)(2,1)} %refs_1_.9, bf16[512,512]{1,0:T(8,128)(2,1)} %get-tuple-element.98.refs_2_, bf16[256,512]{1,0:T(8,128)(2,1)} %get-tuple-element.99.refs_3_, bf16[512,512]{1,0:T(8,128)(2,1)} %get-tuple-element.100.refs_4_, ...), custom_call_target="tpu_custom_call" | custom-call | flops 805306368 | bytes 5767172 | tf_op jit(solution)/shard_map/pallas_call | solution.py:456
  91.3 1.8 %collective-permute-done.4 = bf16[96,512]{1,0:T(8,128)(2,1)S(1)} collective-permute-done((bf16[96,512]{1,0:T(8,128)(2,1)S(1)}, bf16[96,512]{1,0:T(8,128)(2,1)S(1)}, u32[]{:S(2)}, u32[]{:S(2)}) %collective-permute-start.4) | collective-permute-done | bytes 98336 | tf_op jit(solution)/shard_map/ppermute | solution.py:480
  93.1 1.5 add_convert_fusion
  95.3 2.5 %collective-permute-start.7 = (bf16[96,512]{1,0:T(8,128)(2,1)S(1)}, bf16[96,512]{1,0:T(8,128)(2,1)S(1)}, u32[]{:S(2)}, u32[]{:S(2)}) collective-permute-start(bf16[96,512]{1,0:T(8,128)(2,1)S(1)} %add_convert_fusion.5), channel_id=1, source_target_pairs={{0,4},{1,5},{2,6},{3,7},{4,0},{5,1},{6,2},{7,3},{8,12},{9,13},{10,... | collective-permute-start | bytes 294920 | tf_op jit(solution)/shard_map/ppermute | solution.py:480
  97.8 2.2 %collective-permute-start.9 = (bf16[96,512]{1,0:T(8,128)(2,1)S(1)}, bf16[96,512]{1,0:T(8,128)(2,1)S(1)}, u32[]{:S(2)}, u32[]{:S(2)}) collective-permute-start(bf16[96,512]{1,0:T(8,128)(2,1)S(1)} %add_convert_fusion.5), channel_id=1, source_target_pairs={{0,12},{1,13},{2,14},{3,15},{4,8},{5,9},{6,10},{7,11},{8,4},{9,5},... | collective-permute-start | bytes 294920 | tf_op jit(solution)/shard_map/ppermute | solution.py:480
  99.9 3.9 %shard_map.191 = (f32[128,512]{1,0:T(8,128)}, bf16[256,512]{1,0:T(8,128)(2,1)}) custom-call(bf16[512,128]{1,0:T(8,128)(2,1)} %get-tuple-element.136.refs_0_, bf16[512,128]{1,0:T(8,128)(2,1)} %get-tuple-element.104.refs_0_.refs_1_, bf16[256,384]{1,0:T(8,128)(2,1)} %get-tuple-element.88.refs_0_.refs_2_, ...), custom_call_target="tpu_custom_call" | custom-call | flops 402653184 | bytes 3538944 | tf_op jit(solution)/shard_map/pallas_call | solution.py:456
  103.8 5.3 %all-to-all-start.4 = ((bf16[16,16,512]{2,1,0:T(8,128)(2,1)}), bf16[16,16,512]{2,1,0:T(8,128)(2,1)S(1)}, u32[]{:S(2)}, u32[]{:S(2)}) async-start(bf16[16,16,512]{2,1,0:T(8,128)(2,1)} %bitcast.71), calls=%async_computation.4 | async-start | bytes 524288 | tf_op jit(solution)/shard_map/all_to_all | solution.py:533
  109.3 1.5 collective-permute-start.13
  110.9 1.2 collective-permute-start.10
  112.2 2.1 %collective-permute-start.11 = (bf16[128,512]{1,0:T(8,128)(2,1)S(1)}, bf16[128,512]{1,0:T(8,128)(2,1)S(1)}, u32[]{:S(2)}, u32[]{:S(2)}) collective-permute-start(bf16[128,512]{1,0:T(8,128)(2,1)S(1)} %get-tuple-element.179), channel_id=1, source_target_pairs={{0,8},{1,9},{2,10},{3,11},{4,12},{5,13},{6,14},{7,15},{8,0},{9,1},... | collective-permute-start | bytes 393224 | tf_op jit(solution)/shard_map/ppermute | solution.py:480
  114.5 3.9 %shard_map.192.refs_4_ = f32[768,512]{1,0:T(8,128)} custom-call(bf16[768,512]{1,0:T(8,128)(2,1)} %refs_0_.3, bf16[512,512]{1,0:T(8,128)(2,1)} %get-tuple-element.145.refs_8_.refs_10_.refs_4_.refs_1_, bf16[256,512]{1,0:T(8,128)(2,1)} %get-tuple-element.146.refs_11_.refs_12_.refs_5_.refs_2_, bf16[1536,512]{1,0:T(8,128)(2,1)} %refs_3_.9, ...), custom_call_target="tpu_custom_call" | custom-call | flops 402653184 | bytes 4718592 | tf_op jit(solution)/shard_map/pallas_call | solution.py:456
  118.4 2.5 %collective-permute-done.10 = bf16[128,512]{1,0:T(8,128)(2,1)S(1)} collective-permute-done((bf16[128,512]{1,0:T(8,128)(2,1)S(1)}, bf16[128,512]{1,0:T(8,128)(2,1)S(1)}, u32[]{:S(2)}, u32[]{:S(2)}) %collective-permute-start.10) | collective-permute-done | bytes 131104 | tf_op jit(solution)/shard_map/ppermute | solution.py:480
  121.3 4.7 %collective-permute-done.12 = bf16[128,512]{1,0:T(8,128)(2,1)S(1)} collective-permute-done((bf16[128,512]{1,0:T(8,128)(2,1)S(1)}, bf16[128,512]{1,0:T(8,128)(2,1)S(1)}, u32[]{:S(2)}, u32[]{:S(2)}) %collective-permute-start.12) | collective-permute-done | bytes 131104 | tf_op jit(solution)/shard_map/ppermute | solution.py:480
  126.3 1.9 %collective-permute-start.17 = (bf16[768,512]{1,0:T(8,128)(2,1)S(1)}, bf16[768,512]{1,0:T(8,128)(2,1)S(1)}, u32[]{:S(2)}, u32[]{:S(2)}) collective-permute-start(bf16[768,512]{1,0:T(8,128)(2,1)S(1)} %maximum_select_fusion.1), channel_id=1, source_target_pairs={{0,1},{1,0},{2,3},{3,2},{4,5},{5,4},{6,7},{7,6},{8,9},{9,8},{10,11... | collective-permute-start | bytes 2359304 | tf_op jit(solution)/shard_map/ppermute | solution.py:480
  128.2 2.7 %collective-permute-start.14 = (bf16[128,512]{1,0:T(8,128)(2,1)S(1)}, bf16[128,512]{1,0:T(8,128)(2,1)S(1)}, u32[]{:S(2)}, u32[]{:S(2)}) collective-permute-start(bf16[128,512]{1,0:T(8,128)(2,1)S(1)} %add_convert_fusion.4), channel_id=1, source_target_pairs={{0,4},{1,5},{2,6},{3,7},{4,0},{5,1},{6,2},{7,3},{8,12},{9,13},{10,... | collective-permute-start | bytes 393224 | tf_op jit(solution)/shard_map/ppermute | solution.py:480
  131.0 2.1 %collective-permute-start.16 = (bf16[128,512]{1,0:T(8,128)(2,1)S(1)}, bf16[128,512]{1,0:T(8,128)(2,1)S(1)}, u32[]{:S(2)}, u32[]{:S(2)}) collective-permute-start(bf16[128,512]{1,0:T(8,128)(2,1)S(1)} %add_convert_fusion.4), channel_id=1, source_target_pairs={{0,12},{1,13},{2,14},{3,15},{4,8},{5,9},{6,10},{7,11},{8,4},{9,5},... | collective-permute-start | bytes 393224 | tf_op jit(solution)/shard_map/ppermute | solution.py:480
  133.1 2.0 %shard_map.193 = f32[128,512]{1,0:T(8,128)} custom-call(f32[128,512]{1,0:T(8,128)} %get-tuple-element.153.refs_0_, f32[128,512]{1,0:T(8,128)} %get-tuple-element.154.refs_1_, bf16[256,128]{1,0:T(8,128)(2,1)} %get-tuple-element.91.refs_5_.refs_1_.refs_2_, bf16[256,512]{1,0:T(8,128)(2,1)} %bitcast.75, f32[768,512]{1,0:T(8,128)} %shard_map.192.refs_4_), custom_call_target="tpu_custom_call" | custom-call | flops 100000000 | bytes 1114112 | tf_op jit(solution)/shard_map/pallas_call | solution.py:456
  135.1 1.0 collective-permute-done.14
  136.1 6.1 %collective-permute-done.15 = bf16[128,512]{1,0:T(8,128)(2,1)S(1)} collective-permute-done((bf16[128,512]{1,0:T(8,128)(2,1)S(1)}, bf16[128,512]{1,0:T(8,128)(2,1)S(1)}, u32[]{:S(2)}, u32[]{:S(2)}) %collective-permute-start.15) | collective-permute-done | bytes 131104 | tf_op jit(solution)/shard_map/ppermute | solution.py:480
  142.4 1.2 collective-permute-start.18
  144.6 1.0 pad_maximum_fusion.1
  145.6 8.4 %collective-permute-done.18 = bf16[512,512]{1,0:T(8,128)(2,1)S(1)} collective-permute-done((bf16[512,512]{1,0:T(8,128)(2,1)S(1)}, bf16[512,512]{1,0:T(8,128)(2,1)S(1)}, u32[]{:S(2)}, u32[]{:S(2)}) %collective-permute-start.18) | collective-permute-done | bytes 524320 | tf_op jit(solution)/shard_map/ppermute | solution.py:480
  154.5 2.8 %collective-permute-start.19 = (bf16[1024,512]{1,0:T(8,128)(2,1)S(1)}, bf16[1024,512]{1,0:T(8,128)(2,1)S(1)}, u32[]{:S(2)}, u32[]{:S(2)}) collective-permute-start(bf16[1024,512]{1,0:T(8,128)(2,1)S(1)} %maximum_select_fusion), channel_id=1, source_target_pairs={{0,1},{1,0},{2,3},{3,2},{4,5},{5,4},{6,7},{7,6},{8,9},{9,8},{10,11... | collective-permute-start | bytes 3145736 | tf_op jit(solution)/shard_map/ppermute | solution.py:480
  157.3 2.3 %collective-permute-done.19 = bf16[1024,512]{1,0:T(8,128)(2,1)S(1)} collective-permute-done((bf16[1024,512]{1,0:T(8,128)(2,1)S(1)}, bf16[1024,512]{1,0:T(8,128)(2,1)S(1)}, u32[]{:S(2)}, u32[]{:S(2)}) %collective-permute-start.19) | collective-permute-done | bytes 1048608 | tf_op jit(solution)/shard_map/ppermute | solution.py:480
  159.8 0.9 fusion
  160.6 1.2 pad_maximum_fusion
  (58 shorter events, 9.0 us)
Async XLA Ops:
  2.3 13.0 %all-to-all-start = ((s32[16,1,16]{2,1,0:T(1,128)}), s32[16,1,16]{2,1,0:T(1,128)S(1)}, u32[]{:S(2)}, u32[]{:S(2)}) async-start(s32[16,1,16]{2,1,0:T(1,128)} %bitcast.80), calls=%async_computation | async-start | bytes 16384 | tf_op jit(solution)/shard_map/all_to_all | solution.py:564
  15.4 0.6 copy-start.5
  18.0 13.6 %all-to-all-start.1 = ((bf16[16,16,512]{2,1,0:T(8,128)(2,1)}), bf16[16,16,512]{2,1,0:T(8,128)(2,1)S(1)}, u32[]{:S(2)}, u32[]{:S(2)}) async-start(bf16[16,16,512]{2,1,0:T(8,128)(2,1)} %bitcast.78), calls=%async_computation.1 | async-start | bytes 524288 | tf_op jit(solution)/shard_map/all_to_all | solution.py:533
  31.6 0.7 copy-start.1
  36.6 13.5 %all-to-all-start.2 = ((bf16[16,16,512]{2,1,0:T(8,128)(2,1)}), bf16[16,16,512]{2,1,0:T(8,128)(2,1)S(1)}, u32[]{:S(2)}, u32[]{:S(2)}) async-start(bf16[16,16,512]{2,1,0:T(8,128)(2,1)} %bitcast.76), calls=%async_computation.2 | async-start | bytes 524288 | tf_op jit(solution)/shard_map/all_to_all | solution.py:533
  50.1 0.7 copy-start.2
  57.9 7.8 %collective-permute-start = (bf16[768,512]{1,0:T(8,128)(2,1)}, bf16[768,512]{1,0:T(8,128)(2,1)S(1)}, u32[]{:S(2)}, u32[]{:S(2)}) collective-permute-start(bf16[768,512]{1,0:T(8,128)(2,1)} %get-tuple-element.112.refs_7_), channel_id=1, source_target_pairs={{0,1},{1,0},{2,3},{3,2},{4,5},{5,4},{6,7},{7,6},{8,9},{9,8},{10,11... | collective-permute-start | bytes 2359304 | tf_op jit(solution)/shard_map/ppermute | solution.py:480
  58.5 12.9 %all-to-all-start.3 = ((bf16[16,16,512]{2,1,0:T(8,128)(2,1)}), bf16[16,16,512]{2,1,0:T(8,128)(2,1)S(1)}, u32[]{:S(2)}, u32[]{:S(2)}) async-start(bf16[16,16,512]{2,1,0:T(8,128)(2,1)} %bitcast.77), calls=%async_computation.3 | async-start | bytes 524288 | tf_op jit(solution)/shard_map/all_to_all | solution.py:533
  62.0 3.7 %copy-start.4 = (bf16[768,512]{1,0:T(8,128)(2,1)S(1)}, bf16[768,512]{1,0:T(8,128)(2,1)}, u32[]{:S(2)}) copy-start(bf16[768,512]{1,0:T(8,128)(2,1)} %get-tuple-element.115) | copy-start | bytes 2359300
  71.4 0.7 copy-start
  71.5 10.0 %collective-permute-start.1 = (bf16[384,512]{1,0:T(8,128)(2,1)S(1)}, bf16[384,512]{1,0:T(8,128)(2,1)S(1)}, u32[]{:S(2)}, u32[]{:S(2)}) collective-permute-start(bf16[384,512]{1,0:T(8,128)(2,1)S(1)} %get-tuple-element.176), channel_id=1, source_target_pairs={{0,2},{1,3},{2,0},{3,1},{4,6},{5,7},{6,4},{7,5},{8,10},{9,11},{10,... | collective-permute-start | bytes 1179656 | tf_op jit(solution)/shard_map/ppermute | solution.py:480
  81.5 11.6 %collective-permute-start.2 = (bf16[1024,512]{1,0:T(8,128)(2,1)}, bf16[1024,512]{1,0:T(8,128)(2,1)S(1)}, u32[]{:S(2)}, u32[]{:S(2)}) collective-permute-start(bf16[1024,512]{1,0:T(8,128)(2,1)} %shard_map.189.refs_12_), channel_id=1, source_target_pairs={{0,1},{1,0},{2,3},{3,2},{4,5},{5,4},{6,7},{7,6},{8,9},{9,8},{10,11... | collective-permute-start | bytes 3145736 | tf_op jit(solution)/shard_map/ppermute | solution.py:480
  83.2 8.1 %collective-permute-start.3 = (bf16[96,512]{1,0:T(8,128)(2,1)S(1)}, bf16[96,512]{1,0:T(8,128)(2,1)S(1)}, u32[]{:S(2)}, u32[]{:S(2)}) collective-permute-start(bf16[96,512]{1,0:T(8,128)(2,1)S(1)} %get-tuple-element.184), channel_id=1, source_target_pairs={{0,4},{1,5},{2,6},{3,7},{4,0},{5,1},{6,2},{7,3},{8,12},{9,13},{10,... | collective-permute-start | bytes 294920 | tf_op jit(solution)/shard_map/ppermute | solution.py:480
  83.9 9.2 %collective-permute-start.4 = (bf16[96,512]{1,0:T(8,128)(2,1)S(1)}, bf16[96,512]{1,0:T(8,128)(2,1)S(1)}, u32[]{:S(2)}, u32[]{:S(2)}) collective-permute-start(bf16[96,512]{1,0:T(8,128)(2,1)S(1)} %get-tuple-element.183), channel_id=1, source_target_pairs={{0,8},{1,9},{2,10},{3,11},{4,12},{5,13},{6,14},{7,15},{8,0},{9,1},... | collective-permute-start | bytes 294920 | tf_op jit(solution)/shard_map/ppermute | solution.py:480
  84.7 8.4 %collective-permute-start.5 = (bf16[96,512]{1,0:T(8,128)(2,1)S(1)}, bf16[96,512]{1,0:T(8,128)(2,1)S(1)}, u32[]{:S(2)}, u32[]{:S(2)}) collective-permute-start(bf16[96,512]{1,0:T(8,128)(2,1)S(1)} %get-tuple-element.182), channel_id=1, source_target_pairs={{0,12},{1,13},{2,14},{3,15},{4,8},{5,9},{6,10},{7,11},{8,4},{9,5},... | collective-permute-start | bytes 294920 | tf_op jit(solution)/shard_map/ppermute | solution.py:480
  94.7 14.4 %collective-permute-start.6 = (bf16[512,512]{1,0:T(8,128)(2,1)S(1)}, bf16[512,512]{1,0:T(8,128)(2,1)S(1)}, u32[]{:S(2)}, u32[]{:S(2)}) collective-permute-start(bf16[512,512]{1,0:T(8,128)(2,1)S(1)} %get-tuple-element.174), channel_id=1, source_target_pairs={{0,2},{1,3},{2,0},{3,1},{4,6},{5,7},{6,4},{7,5},{8,10},{9,11},{10,... | collective-permute-start | bytes 1572872 | tf_op jit(solution)/shard_map/ppermute | solution.py:480
  95.3 13.8 %collective-permute-start.7 = (bf16[96,512]{1,0:T(8,128)(2,1)S(1)}, bf16[96,512]{1,0:T(8,128)(2,1)S(1)}, u32[]{:S(2)}, u32[]{:S(2)}) collective-permute-start(bf16[96,512]{1,0:T(8,128)(2,1)S(1)} %add_convert_fusion.5), channel_id=1, source_target_pairs={{0,4},{1,5},{2,6},{3,7},{4,0},{5,1},{6,2},{7,3},{8,12},{9,13},{10,... | collective-permute-start | bytes 294920 | tf_op jit(solution)/shard_map/ppermute | solution.py:480
  97.8 11.4 %collective-permute-start.8 = (bf16[96,512]{1,0:T(8,128)(2,1)S(1)}, bf16[96,512]{1,0:T(8,128)(2,1)S(1)}, u32[]{:S(2)}, u32[]{:S(2)}) collective-permute-start(bf16[96,512]{1,0:T(8,128)(2,1)S(1)} %add_convert_fusion.5), channel_id=1, source_target_pairs={{0,8},{1,9},{2,10},{3,11},{4,12},{5,13},{6,14},{7,15},{8,0},{9,1},... | collective-permute-start | bytes 294920 | tf_op jit(solution)/shard_map/ppermute | solution.py:480
  97.8 11.4 %collective-permute-start.9 = (bf16[96,512]{1,0:T(8,128)(2,1)S(1)}, bf16[96,512]{1,0:T(8,128)(2,1)S(1)}, u32[]{:S(2)}, u32[]{:S(2)}) collective-permute-start(bf16[96,512]{1,0:T(8,128)(2,1)S(1)} %add_convert_fusion.5), channel_id=1, source_target_pairs={{0,12},{1,13},{2,14},{3,15},{4,8},{5,9},{6,10},{7,11},{8,4},{9,5},... | collective-permute-start | bytes 294920 | tf_op jit(solution)/shard_map/ppermute | solution.py:480
  103.8 14.6 %all-to-all-start.4 = ((bf16[16,16,512]{2,1,0:T(8,128)(2,1)}), bf16[16,16,512]{2,1,0:T(8,128)(2,1)S(1)}, u32[]{:S(2)}, u32[]{:S(2)}) async-start(bf16[16,16,512]{2,1,0:T(8,128)(2,1)} %bitcast.71), calls=%async_computation.4 | async-start | bytes 524288 | tf_op jit(solution)/shard_map/all_to_all | solution.py:533
  109.3 16.7 %collective-permute-start.13 = (bf16[384,512]{1,0:T(8,128)(2,1)S(1)}, bf16[384,512]{1,0:T(8,128)(2,1)S(1)}, u32[]{:S(2)}, u32[]{:S(2)}) collective-permute-start(bf16[384,512]{1,0:T(8,128)(2,1)S(1)} %bitcast.69), channel_id=1, source_target_pairs={{0,2},{1,3},{2,0},{3,1},{4,6},{5,7},{6,4},{7,5},{8,10},{9,11},{10,... | collective-permute-start | bytes 1179656 | tf_op jit(solution)/shard_map/ppermute | solution.py:480
  110.9 10.0 %collective-permute-start.10 = (bf16[128,512]{1,0:T(8,128)(2,1)S(1)}, bf16[128,512]{1,0:T(8,128)(2,1)S(1)}, u32[]{:S(2)}, u32[]{:S(2)}) collective-permute-start(bf16[128,512]{1,0:T(8,128)(2,1)S(1)} %get-tuple-element.180), channel_id=1, source_target_pairs={{0,4},{1,5},{2,6},{3,7},{4,0},{5,1},{6,2},{7,3},{8,12},{9,13},{10,... | collective-permute-start | bytes 393224 | tf_op jit(solution)/shard_map/ppermute | solution.py:480
  112.2 9.1 %collective-permute-start.11 = (bf16[128,512]{1,0:T(8,128)(2,1)S(1)}, bf16[128,512]{1,0:T(8,128)(2,1)S(1)}, u32[]{:S(2)}, u32[]{:S(2)}) collective-permute-start(bf16[128,512]{1,0:T(8,128)(2,1)S(1)} %get-tuple-element.179), channel_id=1, source_target_pairs={{0,8},{1,9},{2,10},{3,11},{4,12},{5,13},{6,14},{7,15},{8,0},{9,1},... | collective-permute-start | bytes 393224 | tf_op jit(solution)/shard_map/ppermute | solution.py:480
  114.2 11.7 %collective-permute-start.12 = (bf16[128,512]{1,0:T(8,128)(2,1)S(1)}, bf16[128,512]{1,0:T(8,128)(2,1)S(1)}, u32[]{:S(2)}, u32[]{:S(2)}) collective-permute-start(bf16[128,512]{1,0:T(8,128)(2,1)S(1)} %get-tuple-element.178), channel_id=1, source_target_pairs={{0,12},{1,13},{2,14},{3,15},{4,8},{5,9},{6,10},{7,11},{8,4},{9,5},... | collective-permute-start | bytes 393224 | tf_op jit(solution)/shard_map/ppermute | solution.py:480
  118.4 14.6 %copy-start.3 = (bf16[16,16,512]{2,1,0:T(8,128)(2,1)}, bf16[16,16,512]{2,1,0:T(8,128)(2,1)S(1)}, u32[]{:S(2)}) copy-start(bf16[16,16,512]{2,1,0:T(8,128)(2,1)S(1)} %all-to-all-done.4) | copy-start | bytes 786436
  126.3 16.0 %collective-permute-start.17 = (bf16[768,512]{1,0:T(8,128)(2,1)S(1)}, bf16[768,512]{1,0:T(8,128)(2,1)S(1)}, u32[]{:S(2)}, u32[]{:S(2)}) collective-permute-start(bf16[768,512]{1,0:T(8,128)(2,1)S(1)} %maximum_select_fusion.1), channel_id=1, source_target_pairs={{0,1},{1,0},{2,3},{3,2},{4,5},{5,4},{6,7},{7,6},{8,9},{9,8},{10,11... | collective-permute-start | bytes 2359304 | tf_op jit(solution)/shard_map/ppermute | solution.py:480
  128.2 7.9 %collective-permute-start.14 = (bf16[128,512]{1,0:T(8,128)(2,1)S(1)}, bf16[128,512]{1,0:T(8,128)(2,1)S(1)}, u32[]{:S(2)}, u32[]{:S(2)}) collective-permute-start(bf16[128,512]{1,0:T(8,128)(2,1)S(1)} %add_convert_fusion.4), channel_id=1, source_target_pairs={{0,4},{1,5},{2,6},{3,7},{4,0},{5,1},{6,2},{7,3},{8,12},{9,13},{10,... | collective-permute-start | bytes 393224 | tf_op jit(solution)/shard_map/ppermute | solution.py:480
  130.9 11.4 %collective-permute-start.15 = (bf16[128,512]{1,0:T(8,128)(2,1)S(1)}, bf16[128,512]{1,0:T(8,128)(2,1)S(1)}, u32[]{:S(2)}, u32[]{:S(2)}) collective-permute-start(bf16[128,512]{1,0:T(8,128)(2,1)S(1)} %add_convert_fusion.4), channel_id=1, source_target_pairs={{0,8},{1,9},{2,10},{3,11},{4,12},{5,13},{6,14},{7,15},{8,0},{9,1},... | collective-permute-start | bytes 393224 | tf_op jit(solution)/shard_map/ppermute | solution.py:480
  131.0 11.3 %collective-permute-start.16 = (bf16[128,512]{1,0:T(8,128)(2,1)S(1)}, bf16[128,512]{1,0:T(8,128)(2,1)S(1)}, u32[]{:S(2)}, u32[]{:S(2)}) collective-permute-start(bf16[128,512]{1,0:T(8,128)(2,1)S(1)} %add_convert_fusion.4), channel_id=1, source_target_pairs={{0,12},{1,13},{2,14},{3,15},{4,8},{5,9},{6,10},{7,11},{8,4},{9,5},... | collective-permute-start | bytes 393224 | tf_op jit(solution)/shard_map/ppermute | solution.py:480
  142.4 11.6 %collective-permute-start.18 = (bf16[512,512]{1,0:T(8,128)(2,1)S(1)}, bf16[512,512]{1,0:T(8,128)(2,1)S(1)}, u32[]{:S(2)}, u32[]{:S(2)}) collective-permute-start(bf16[512,512]{1,0:T(8,128)(2,1)S(1)} %bitcast.66), channel_id=1, source_target_pairs={{0,2},{1,3},{2,0},{3,1},{4,6},{5,7},{6,4},{7,5},{8,10},{9,11},{10,... | collective-permute-start | bytes 1572872 | tf_op jit(solution)/shard_map/ppermute | solution.py:480
  154.5 5.1 %collective-permute-start.19 = (bf16[1024,512]{1,0:T(8,128)(2,1)S(1)}, bf16[1024,512]{1,0:T(8,128)(2,1)S(1)}, u32[]{:S(2)}, u32[]{:S(2)}) collective-permute-start(bf16[1024,512]{1,0:T(8,128)(2,1)S(1)} %maximum_select_fusion), channel_id=1, source_target_pairs={{0,1},{1,0},{2,3},{3,2},{4,5},{5,4},{6,7},{7,6},{8,9},{9,8},{10,11... | collective-permute-start | bytes 3145736 | tf_op jit(solution)/shard_map/ppermute | solution.py:480

commit v4 on v3

--- a/solution.py
+++ b/solution.py
@@ -521,10 +521,11 @@
     return whole.reshape(size * parts[0].shape[0], parts[0].shape[1])
 
 
-def last_step(rows, others, lower, split):
-    half = rows.shape[0]
-    low, high = jnp.where(lower, rows, others), jnp.where(lower, others, rows)
-    return jnp.concatenate([low, high[: split - half]], axis=0), high[split - half :]
+def by_owner(rows, groups):
+    sizes = [1 << width for _, width in groups]
+    split = rows.reshape(sizes[::-1] + [-1, rows.shape[1]])
+    turned = list(range(len(sizes)))[::-1] + [len(sizes), len(sizes) + 1]
+    return split.transpose(turned).reshape(rows.shape)
 
 
 def exchange(rows, domains):
@@ -685,14 +686,6 @@
         node_rows * 6 * square,
     )
     far_grad = exchange(grad_reply, domains)
-    node_keep, node_send = line.run(
-        node_weights_kernel,
-        [shaped(BF16, 3 * latent // 2, latent)] * 2,
-        [me, nodes, aggregate, node_hidden, node_out, node_pre],
-        node_rows * 3 * square,
-        [SMEM] + [VMEM] * 5,
-    )
-    node_sum = added(node_keep, across(node_send, domains, 1))
     inner_out, inner_pre = line.run(
         inner_backward_kernel,
         [shaped(BF16, inner_rows, latent)] * 2,
@@ -718,10 +711,18 @@
         [rows_spec(latent)] * 2,
         (blocks,),
     )
+    node_keep, node_send = line.run(
+        node_weights_kernel,
+        [shaped(BF16, 3 * latent // 2, latent)] * 2,
+        [me, nodes, aggregate, node_hidden, node_out, node_pre],
+        node_rows * 3 * square,
+        [SMEM] + [VMEM] * 5,
+    )
+    node_sum = added(node_keep, across(node_send, domains, 1))
     groups = bit_groups(domains)
     bit_one, bits_two = groups[1], groups[2]
+    node_parts = traded(pieces_of(node_sum, *bit_one), domains, bit_one[0])
     far_grad, node_sum, inner_pre = fence(far_grad, node_sum, inner_pre)
-    node_parts = traded(pieces_of(node_sum, *bit_one), domains, bit_one[0])
     cut_out, cut_pre = line.run(
         cut_backward_kernel,
         [shaped(BF16, cut_rows, latent)] * 2,
@@ -774,16 +775,10 @@
 
     edge_send, place, *node_parts = fence(edge_weights(1, me), me, *node_parts)
     edge_parts = [edge_weights(0, place), across(edge_send, domains, 1)]
+    fenced = fence(*edge_parts, *node_parts, inner_pre, cut_pre)
+    edge_parts, node_parts, (inner_pre, cut_pre) = fenced[:2], fenced[2:4], fenced[4:]
+    edge_parts = traded(pieces_of(added(*edge_parts), *bit_one), domains, bit_one[0])
     node_parts = traded(pieces_of(added(*node_parts), *bits_two), domains, bits_two[0])
-    fenced = fence(*edge_parts, *node_parts, inner_pre, cut_pre)
-    edge_sum, node_sum = added(*fenced[:2]), added(*fenced[2:6])
-    inner_pre, cut_pre = fenced[6:]
-    for low, width in groups[3:]:
-        node_sum = added(*traded(pieces_of(node_sum, low, width), domains, low))
-    for low, width in groups[:2:-1]:
-        node_sum = joined(handed(node_sum, domains, low, width), low)
-    edge_parts = traded(pieces_of(edge_sum, *bit_one), domains, bit_one[0])
-    node_parts = handed(node_sum, domains, *bits_two)
     local_grad, outgoing_grad = line.run(
         input_grads_kernel,
         [shaped(F32, node_rows, latent), shaped(BF16, total_slots, latent)],
@@ -800,10 +795,12 @@
     )
     returned = exchange(outgoing_grad, domains)
     fenced = fence(*edge_parts, *node_parts, inner_pre, cut_pre, local_grad)
-    edge_sum, node_sum = added(*fenced[:2]), joined(fenced[2:6], bits_two[0])
+    edge_parts, node_sum = fenced[:2], added(*fenced[2:6])
     inner_pre, cut_pre, local_grad = fenced[6:]
-    edge_parts = traded(pieces_of(edge_sum, *bits_two), domains, bits_two[0])
-    node_parts = handed(node_sum, domains, *bit_one)
+    for low, width in groups[3:]:
+        node_sum = added(*traded(pieces_of(node_sum, low, width), domains, low))
+    node_total = lax.all_gather(node_sum, "dom", axis=0, tiled=True)
+    edge_parts = traded(pieces_of(added(*edge_parts), *bits_two), domains, bits_two[0])
     grad_edges = line.run(
         functools.partial(edge_grads_kernel, blocks=blocks),
         shaped(F32, *edges.shape),
@@ -818,30 +815,38 @@
         [rows_spec(latent)],
         (blocks + 1,),
     )
-    fenced = fence(*edge_parts, *node_parts, returned, grad_edges)
-    edge_sum, node_sum = added(*fenced[:4]), joined(fenced[4:6], bit_one[0])
-    returned, grad_edges = fenced[6:]
+    *edge_parts, returned, grad_edges = fence(*edge_parts, returned, grad_edges)
+    edge_sum = added(*edge_parts)
     for low, width in groups[3:]:
         edge_sum = added(*traded(pieces_of(edge_sum, low, width), domains, low))
     for low, width in groups[:2:-1]:
         edge_sum = joined(handed(edge_sum, domains, low, width), low)
     edge_parts = handed(edge_sum, domains, *bits_two)
-    others = across(node_sum, domains, 1)
     grad_nodes = line.run(
         node_grads_kernel,
         shaped(F32, node_rows, latent),
         [self_grad, local_grad, asked_marks, returned],
         10**8,
     )
-    *edge_parts, node_sum, others, grad_nodes = fence(*edge_parts, node_sum, others, grad_nodes)
-    edge_parts = handed(joined(edge_parts, bits_two[0]), domains, *bit_one)
-    lower = place_of(0, 2) == 0
-    grad_node_in, grad_node_out = last_step(node_sum, others, lower, 2 * latent)
-    *edge_parts, grad_node_in, grad_node_out = fence(*edge_parts, grad_node_in, grad_node_out)
-    edge_sum = joined(edge_parts, bit_one[0])
-    grad_edge_in, grad_edge_out = last_step(
-        edge_sum, across(edge_sum, domains, 1), lower, 3 * latent
-    )
+    *edge_parts, grad_nodes, node_total = fence(*edge_parts, grad_nodes, node_total)
+    edge_sum = joined(edge_parts, bits_two[0])
+    edge_parts = handed(edge_sum, domains, *bit_one) + [across(edge_sum, domains, 1)]
+    node_total = by_owner(node_total, groups)
+    grad_node_in, grad_node_out = node_total[: 2 * latent], node_total[2 * latent :]
+    mine, far, near, grad_node_in, grad_node_out = fence(*edge_parts, grad_node_in, grad_node_out)
+    corner = across(far, domains, 1)
+    lower, left = place_of(0, 2) == 0, place_of(bit_one[0], 2) == 0
+    own, other = [mine, far], [near, corner]
+    low_half = [jnp.where(lower, one, two) for one, two in zip(own, other)]
+    high_half = [jnp.where(lower, two, one) for one, two in zip(own, other)]
+    grad_edge_in = jnp.concatenate(
+        [
+            jnp.where(left, low_half[0], low_half[1]),
+            jnp.where(left, low_half[1], low_half[0]),
+            jnp.where(left, high_half[0], high_half[1]),
+        ]
+    )
+    grad_edge_out = jnp.where(left, high_half[1], high_half[0])
     return (
         new_nodes,
         new_edges,

time: 164 us -> 186 us (1.13)
  waiting for transfers between devices: 48.5 us -> 66.2 us
  between operations: 0.89 us -> 14.2 us
  starting transfers between devices: 51.4 us -> 41.6 us
    ppermute x20 -> x16, starting transfers between devices: 27.3 us -> 18.6 us  [across(): lax.ppermute(rows, 'dom', [(device, device ^ mask) for device in range(de...]
    ppermute x20 -> x16, waiting for transfers between devices: 29.2 us -> 36.9 us  [across(): lax.ppermute(rows, 'dom', [(device, device ^ mask) for device in range(de...]
    all_gather x0 -> x1, waiting for transfers between devices: none -> 6.29 us  [shards(): node_total = lax.all_gather(node_sum, 'dom', axis=0, tiled=True)]
    all_to_all x4, waiting for transfers between devices: 15.7 us -> 19.4 us  [exchange(): lax.all_to_all(split, 'dom', split_axis=0, concat_axis=0, tiled=True)]
  transfers between devices with their start and end apart: 25 -> 22, of which waited for: 13 -> 15; matrix products, arithmetic and copies ran while one was open for 2% -> 2% of each run, Pallas kernels for 22% -> 18%
where the time goes in v4:
time: 186 us; the launch traced here: 184 us
  waiting for transfers between devices  66.2 us (36%)
  Pallas kernels  51.3 us (28%)
  starting transfers between devices  41.6 us (22%)
  between operations  14.2 us (8%)
  other arithmetic  6.05 us (3%)
  local copies, waits for them, and re-layouts  5.03 us (3%)
    pallas_call x15, Pallas kernels, run(): pl.pallas_call(ordered, out_shape=out_shape, in_specs=specs, out_specs=[V...  51.3 us
    ppermute x16, waiting for transfers between devices, across(): lax.ppermute(rows, 'dom', [(device, device ^ mask) for device in range(de...  36.9 us
    all_to_all x4, waiting for transfers between devices, exchange(): lax.all_to_all(split, 'dom', split_axis=0, concat_axis=0, tiled=True)  19.4 us
    ppermute x16, starting transfers between devices, across(): lax.ppermute(rows, 'dom', [(device, device ^ mask) for device in range(de...  18.6 us
    all_to_all x4, starting transfers between devices, exchange(): lax.all_to_all(split, 'dom', split_axis=0, concat_axis=0, tiled=True)  15.6 us
    all_to_all x1, starting transfers between devices, shards(): asked = lax.all_to_all(ask, 'dom', split_axis=0, concat_axis=0, tiled=True)  7.32 us
    all_gather x1, waiting for transfers between devices, shards(): node_total = lax.all_gather(node_sum, 'dom', axis=0, tiled=True)  6.29 us
    convert_element_type x6, other arithmetic, added(): return sum((part.astype(F32) for part in parts)).astype(BF16)  3.84 us
  transfers between devices with their start and end apart: 22, of which 15 were waited for; matrix products, arithmetic and copies ran while one was open for 2% of the time, Pallas kernels for 18%

profile of v4, /device:TPU:1, one launch (start us, length us, event | category | flops | bytes accessed | tf_op | source)
XLA Modules:
  0.0 184.5 jit_solution(7602783121255460431)
XLA Ops:
  7.2 1.7 shard_map.179.refs_2_
  8.9 7.3 %all-to-all-start = ((s32[16,1,16]{2,1,0:T(1,128)}), s32[16,1,16]{2,1,0:T(1,128)S(1)}, u32[]{:S(2)}, u32[]{:S(2)}) async-start(s32[16,1,16]{2,1,0:T(1,128)} %bitcast.76), calls=%async_computation | async-start | bytes 16384 | tf_op jit(solution)/shard_map/all_to_all | solution.py:565
  16.2 2.1 %shard_map.180 = (bf16[256,384]{1,0:T(8,128)(2,1)}, bf16[256,384]{1,0:T(8,128)(2,1)}) custom-call(s32[1,128]{1,0:T(1,128)} %bitcast.80, s32[1,128]{1,0:T(1,128)} %bitcast.81, s32[16,16]{1,0:T(8,128)} %shard_map.179.refs_2_), custom_call_target="tpu_custom_call" | custom-call | flops 100000000 | bytes 394240 | tf_op jit(solution)/shard_map/pallas_call | solution.py:456
  18.2 3.7 %all-to-all-done = s32[16,1,16]{2,1,0:T(1,128)S(1)} async-done(((s32[16,1,16]{2,1,0:T(1,128)}), s32[16,1,16]{2,1,0:T(1,128)S(1)}, u32[]{:S(2)}, u32[]{:S(2)}) %all-to-all-start) | async-done | bytes 1056 | tf_op jit(solution)/shard_map/all_to_all | solution.py:565
  22.5 2.0 %shard_map.181 = (bf16[256,512]{1,0:T(8,128)(2,1)}, bf16[256,128]{1,0:T(8,128)(2,1)}) custom-call(s32[16,16]{1,0:T(8,128)} %bitcast.75, bf16[128,512]{1,0:T(8,128)(2,1)} %refs_1_.7, bf16[256,384]{1,0:T(8,128)(2,1)} %get-tuple-element.84.refs_2_.refs_1_.refs_0_.refs_3_), custom_call_target="tpu_custom_call" | custom-call | flops 100000000 | bytes 459776 | tf_op jit(solution)/shard_map/pallas_call | solution.py:456
  24.5 4.0 %all-to-all-start.1 = ((bf16[16,16,512]{2,1,0:T(8,128)(2,1)}), bf16[16,16,512]{2,1,0:T(8,128)(2,1)S(1)}, u32[]{:S(2)}, u32[]{:S(2)}) async-start(bf16[16,16,512]{2,1,0:T(8,128)(2,1)} %bitcast.74), calls=%async_computation.1 | async-start | bytes 524288 | tf_op jit(solution)/shard_map/all_to_all | solution.py:534
  28.6 6.3 %shard_map.182 = (bf16[512,128]{1,0:T(8,128)(2,1)}, bf16[512,128]{1,0:T(8,128)(2,1)}, bf16[512,512]{1,0:T(8,128)(2,1)}, bf16[512,512]{1,0:T(8,128)(2,1)}, bf16[5...) custom-call(s32[2,256]{1,0:T(2,128)} %bitcast.77, ...), custom_call_target="tpu_custom_call" | custom-call | flops 1073741824 | bytes 7213056 | tf_op jit(solution)/shard_map/pallas_call | solution.py:456
  34.8 3.3 %all-to-all-done.1 = bf16[16,16,512]{2,1,0:T(8,128)(2,1)S(1)} async-done(((bf16[16,16,512]{2,1,0:T(8,128)(2,1)}), bf16[16,16,512]{2,1,0:T(8,128)(2,1)S(1)}, u32[]{:S(2)}, u32[]{:S(2)}) %all-to-all-start.1) | async-done | bytes 262176 | tf_op jit(solution)/shard_map/all_to_all | solution.py:534
  38.8 4.3 %shard_map.183 = (bf16[256,512]{1,0:T(8,128)(2,1)}, bf16[256,512]{1,0:T(8,128)(2,1)}, bf16[256,512]{1,0:T(8,128)(2,1)}, f32[256,512]{1,0:T(8,128)}, f32[256,512]...) custom-call(bf16[256,384]{1,0:T(8,128)(2,1)} %get-tuple-element.83.refs_0_.refs_2_, ...), custom_call_target="tpu_custom_call" | custom-call | flops 536870912 | bytes 6292480 | tf_op jit(solution)/shard_map/pallas_call | solution.py:456
  43.1 4.0 %all-to-all-start.2 = ((bf16[16,16,512]{2,1,0:T(8,128)(2,1)}), bf16[16,16,512]{2,1,0:T(8,128)(2,1)S(1)}, u32[]{:S(2)}, u32[]{:S(2)}) async-start(bf16[16,16,512]{2,1,0:T(8,128)(2,1)} %bitcast.72), calls=%async_computation.2 | async-start | bytes 524288 | tf_op jit(solution)/shard_map/all_to_all | solution.py:534
  47.1 2.7 %shard_map.184.refs_7_ = bf16[768,512]{1,0:T(8,128)(2,1)} custom-call(bf16[768,512]{1,0:T(8,128)(2,1)} %refs_1_.9, f32[512,512]{1,0:T(8,128)} %get-tuple-element.90.refs_1_.refs_3_, f32[256,512]{1,0:T(8,128)} %get-tuple-element.91.refs_2_.refs_4_, bf16[256,512]{1,0:T(8,128)(2,1)} %get-tuple-element.88.refs_3_), custom_call_target="tpu_custom_call" | custom-call | flops 10000000 | bytes 3145728 | tf_op jit(solution)/shard_map/pallas_call | solution.py:456
  49.8 6.9 %all-to-all-done.2 = bf16[16,16,512]{2,1,0:T(8,128)(2,1)S(1)} async-done(((bf16[16,16,512]{2,1,0:T(8,128)(2,1)}), bf16[16,16,512]{2,1,0:T(8,128)(2,1)S(1)}, u32[]{:S(2)}, u32[]{:S(2)}) %all-to-all-start.2) | async-done | bytes 262176 | tf_op jit(solution)/shard_map/all_to_all | solution.py:534
  57.4 4.1 %shard_map.185 = (bf16[128,512]{1,0:T(8,128)(2,1)}, f32[128,512]{1,0:T(8,128)}, bf16[128,512]{1,0:T(8,128)(2,1)}, bf16[256,512]{1,0:T(8,128)(2,1)}, bf16[128,512...) custom-call(bf16[256,512]{1,0:T(8,128)(2,1)} %bitcast.70, ...), custom_call_target="tpu_custom_call" | custom-call | flops 402653184 | bytes 3735552 | tf_op jit(solution)/shard_map/pallas_call | solution.py:456
  61.5 3.6 %shard_map.186 = (bf16[512,512]{1,0:T(8,128)(2,1)}, bf16[512,512]{1,0:T(8,128)(2,1)}) custom-call(bf16[512,128]{1,0:T(8,128)(2,1)} %get-tuple-element.99.refs_0_.refs_1_, bf16[128,512]{1,0:T(8,128)(2,1)} %get-tuple-element.100.refs_1_, bf16[768,512]{1,0:T(8,128)(2,1)} %refs_0_.3, f32[512,512]{1,0:T(8,128)} %get-tuple-element.90.refs_1_.refs_3_, ...), custom_call_target="tpu_custom_call" | custom-call | flops 268435456 | bytes 4720640 | tf_op jit(solution)/shard_map/pallas_call | solution.py:456
  65.2 2.9 %shard_map.187 = (bf16[768,512]{1,0:T(8,128)(2,1)}, bf16[768,512]{1,0:T(8,128)(2,1)}) custom-call(s32[1]{0:T(128)} %bitcast.11.refs_0_, bf16[128,512]{1,0:T(8,128)(2,1)} %refs_1_.7, bf16[128,512]{1,0:T(8,128)(2,1)} %get-tuple-element.106.refs_2_, bf16[128,512]{1,0:T(8,128)(2,1)} %get-tuple-element.107.refs_3_, bf16[128,512]{1,0:T(8,128)(2,1)} %get-tuple-element.108.refs_4_, ...), custom_call_target="tpu_custom_call" | custom-call | flops 201326592 | bytes 2228228 | tf_op jit(solution)/shard_map/pallas_call | solution.py:456
  68.7 3.4 %all-to-all-start.3 = ((bf16[16,16,512]{2,1,0:T(8,128)(2,1)}), bf16[16,16,512]{2,1,0:T(8,128)(2,1)S(1)}, u32[]{:S(2)}, u32[]{:S(2)}) async-start(bf16[16,16,512]{2,1,0:T(8,128)(2,1)} %bitcast.12), calls=%async_computation.3 | async-start | bytes 524288 | tf_op jit(solution)/shard_map/all_to_all | solution.py:534
  72.2 1.3 add_convert_fusion.1
  73.6 1.3 collective-permute-start.1
  75.0 6.6 %all-to-all-done.3 = bf16[16,16,512]{2,1,0:T(8,128)(2,1)S(1)} async-done(((bf16[16,16,512]{2,1,0:T(8,128)(2,1)}), bf16[16,16,512]{2,1,0:T(8,128)(2,1)S(1)}, u32[]{:S(2)}, u32[]{:S(2)}) %all-to-all-start.3) | async-done | bytes 262176 | tf_op jit(solution)/shard_map/all_to_all | solution.py:534
  82.3 3.1 %shard_map.188 = (bf16[256,512]{1,0:T(8,128)(2,1)}, bf16[256,512]{1,0:T(8,128)(2,1)}) custom-call(bf16[256,384]{1,0:T(8,128)(2,1)} %get-tuple-element.84.refs_2_.refs_1_.refs_0_.refs_3_, bf16[128,512]{1,0:T(8,128)(2,1)} %get-tuple-element.100.refs_1_, bf16[256,512]{1,0:T(8,128)(2,1)} %bitcast.73, bf16[768,512]{1,0:T(8,128)(2,1)} %refs_0_.3, ...), custom_call_target="tpu_custom_call" | custom-call | flops 134217728 | bytes 3474432 | tf_op jit(solution)/shard_map/pallas_call | solution.py:456
  85.4 4.3 %shard_map.189.refs_12_ = bf16[1024,512]{1,0:T(8,128)(2,1)} custom-call(s32[1]{0:T(128)} %bitcast.11.refs_0_, bf16[768,512]{1,0:T(8,128)(2,1)} %refs_1_.9, bf16[512,512]{1,0:T(8,128)(2,1)} %get-tuple-element.93.refs_2_, bf16[256,512]{1,0:T(8,128)(2,1)} %get-tuple-element.94.refs_3_, bf16[512,512]{1,0:T(8,128)(2,1)} %get-tuple-element.95.refs_4_, ...), custom_call_target="tpu_custom_call" | custom-call | flops 805306368 | bytes 5767172 | tf_op jit(solution)/shard_map/pallas_call | solution.py:456
  90.4 4.4 %shard_map.190.refs_7_ = bf16[1024,512]{1,0:T(8,128)(2,1)} custom-call(s32[1]{0:T(128)} %bitcast.11.refs_0_, bf16[768,512]{1,0:T(8,128)(2,1)} %refs_1_.9, bf16[512,512]{1,0:T(8,128)(2,1)} %get-tuple-element.93.refs_2_, bf16[256,512]{1,0:T(8,128)(2,1)} %get-tuple-element.94.refs_3_, bf16[512,512]{1,0:T(8,128)(2,1)} %get-tuple-element.95.refs_4_, ...), custom_call_target="tpu_custom_call" | custom-call | flops 805306368 | bytes 5767172 | tf_op jit(solution)/shard_map/pallas_call | solution.py:456
  94.8 1.5 add_convert_fusion
  97.3 1.2 collective-permute-start.5
  98.5 1.7 collective-permute-start.6
  100.3 3.9 %shard_map.191 = (f32[128,512]{1,0:T(8,128)}, bf16[256,512]{1,0:T(8,128)(2,1)}) custom-call(bf16[512,128]{1,0:T(8,128)(2,1)} %get-tuple-element.128.refs_0_, bf16[512,128]{1,0:T(8,128)(2,1)} %get-tuple-element.99.refs_0_.refs_1_, bf16[256,384]{1,0:T(8,128)(2,1)} %get-tuple-element.83.refs_0_.refs_2_, ...), custom_call_target="tpu_custom_call" | custom-call | flops 402653184 | bytes 3538944 | tf_op jit(solution)/shard_map/pallas_call | solution.py:456
  104.2 1.2 collective-permute-done.6
  105.3 4.7 %collective-permute-done.3 = bf16[512,512]{1,0:T(8,128)(2,1)S(1)} collective-permute-done((bf16[512,512]{1,0:T(8,128)(2,1)S(1)}, bf16[512,512]{1,0:T(8,128)(2,1)S(1)}, u32[]{:S(2)}, u32[]{:S(2)}) %collective-permute-start.3) | collective-permute-done | bytes 524320 | tf_op jit(solution)/shard_map/ppermute | solution.py:480
  110.7 4.2 %all-to-all-start.4 = ((bf16[16,16,512]{2,1,0:T(8,128)(2,1)}), bf16[16,16,512]{2,1,0:T(8,128)(2,1)S(1)}, u32[]{:S(2)}, u32[]{:S(2)}) async-start(bf16[16,16,512]{2,1,0:T(8,128)(2,1)} %bitcast.68), calls=%async_computation.4 | async-start | bytes 524288 | tf_op jit(solution)/shard_map/all_to_all | solution.py:534
  115.1 1.5 collective-permute-start.7
  116.5 2.1 %collective-permute-start.8 = (bf16[128,512]{1,0:T(8,128)(2,1)S(1)}, bf16[128,512]{1,0:T(8,128)(2,1)S(1)}, u32[]{:S(2)}, u32[]{:S(2)}) collective-permute-start(bf16[128,512]{1,0:T(8,128)(2,1)S(1)} %get-tuple-element.167), channel_id=1, source_target_pairs={{0,8},{1,9},{2,10},{3,11},{4,12},{5,13},{6,14},{7,15},{8,0},{9,1},... | collective-permute-start | bytes 393224 | tf_op jit(solution)/shard_map/ppermute | solution.py:480
  118.7 3.9 %shard_map.192.refs_4_ = f32[768,512]{1,0:T(8,128)} custom-call(bf16[768,512]{1,0:T(8,128)(2,1)} %refs_0_.3, bf16[512,512]{1,0:T(8,128)(2,1)} %get-tuple-element.133.refs_6_.refs_10_.refs_4_.refs_1_, bf16[256,512]{1,0:T(8,128)(2,1)} %get-tuple-element.134.refs_11_.refs_12_.refs_5_.refs_2_, bf16[1536,512]{1,0:T(8,128)(2,1)} %refs_3_.9, ...), custom_call_target="tpu_custom_call" | custom-call | flops 402653184 | bytes 4718592 | tf_op jit(solution)/shard_map/pallas_call | solution.py:456
  122.6 2.6 %all-to-all-done.4 = bf16[16,16,512]{2,1,0:T(8,128)(2,1)S(1)} async-done(((bf16[16,16,512]{2,1,0:T(8,128)(2,1)}), bf16[16,16,512]{2,1,0:T(8,128)(2,1)S(1)}, u32[]{:S(2)}, u32[]{:S(2)}) %all-to-all-start.4) | async-done | bytes 262176 | tf_op jit(solution)/shard_map/all_to_all | solution.py:534
  125.2 1.6 collective-permute-done.7
  126.8 4.0 %collective-permute-done.8 = bf16[128,512]{1,0:T(8,128)(2,1)S(1)} collective-permute-done((bf16[128,512]{1,0:T(8,128)(2,1)S(1)}, bf16[128,512]{1,0:T(8,128)(2,1)S(1)}, u32[]{:S(2)}, u32[]{:S(2)}) %collective-permute-start.8) | collective-permute-done | bytes 131104 | tf_op jit(solution)/shard_map/ppermute | solution.py:480
  130.8 4.1 %collective-permute-done.9 = bf16[128,512]{1,0:T(8,128)(2,1)S(1)} collective-permute-done((bf16[128,512]{1,0:T(8,128)(2,1)S(1)}, bf16[128,512]{1,0:T(8,128)(2,1)S(1)}, u32[]{:S(2)}, u32[]{:S(2)}) %collective-permute-start.9) | collective-permute-done | bytes 131104 | tf_op jit(solution)/shard_map/ppermute | solution.py:480
  135.0 3.6 %collective-permute-start.10 = (bf16[128,512]{1,0:T(8,128)(2,1)S(1)}, bf16[128,512]{1,0:T(8,128)(2,1)S(1)}, u32[]{:S(2)}, u32[]{:S(2)}) collective-permute-start(bf16[128,512]{1,0:T(8,128)(2,1)S(1)} %add_convert_fusion.4), channel_id=1, source_target_pairs={{0,4},{1,5},{2,6},{3,7},{4,0},{5,1},{6,2},{7,3},{8,12},{9,13},{10,... | collective-permute-start | bytes 393224 | tf_op jit(solution)/shard_map/ppermute | solution.py:480
  138.8 1.9 %collective-permute-start.12 = (bf16[128,512]{1,0:T(8,128)(2,1)S(1)}, bf16[128,512]{1,0:T(8,128)(2,1)S(1)}, u32[]{:S(2)}, u32[]{:S(2)}) collective-permute-start(bf16[128,512]{1,0:T(8,128)(2,1)S(1)} %add_convert_fusion.4), channel_id=1, source_target_pairs={{0,12},{1,13},{2,14},{3,15},{4,8},{5,9},{6,10},{7,11},{8,4},{9,5},... | collective-permute-start | bytes 393224 | tf_op jit(solution)/shard_map/ppermute | solution.py:480
  140.8 2.0 %shard_map.193 = f32[128,512]{1,0:T(8,128)} custom-call(f32[128,512]{1,0:T(8,128)} %get-tuple-element.139.refs_0_, f32[128,512]{1,0:T(8,128)} %get-tuple-element.140.refs_1_, bf16[256,128]{1,0:T(8,128)(2,1)} %get-tuple-element.86.refs_5_.refs_1_.refs_2_, bf16[256,512]{1,0:T(8,128)(2,1)} %bitcast.71, f32[768,512]{1,0:T(8,128)} %shard_map.192.refs_4_), custom_call_target="tpu_custom_call" | custom-call | flops 100000000 | bytes 1114112 | tf_op jit(solution)/shard_map/pallas_call | solution.py:456
  143.0 10.0 %collective-permute-done.11 = bf16[128,512]{1,0:T(8,128)(2,1)S(1)} collective-permute-done((bf16[128,512]{1,0:T(8,128)(2,1)S(1)}, bf16[128,512]{1,0:T(8,128)(2,1)S(1)}, u32[]{:S(2)}, u32[]{:S(2)}) %collective-permute-start.11) | collective-permute-done | bytes 131104 | tf_op jit(solution)/shard_map/ppermute | solution.py:480
  153.0 6.3 %all-gather.2.cloned.1.call-done = bf16[1536,512]{1,0:T(8,128)(2,1)} async-done(((bf16[96,512]{1,0:T(8,128)(2,1)}), bf16[1536,512]{1,0:T(8,128)(2,1)}) %all-gather.2.cloned.1.call-update) | async-done | bytes 1572880 | tf_op jit(solution)/shard_map/all_gather | solution.py:802
  159.5 1.2 collective-permute-start.13
  161.4 1.0 slice.8
  163.2 9.6 %collective-permute-done.13 = bf16[512,512]{1,0:T(8,128)(2,1)S(1)} collective-permute-done((bf16[512,512]{1,0:T(8,128)(2,1)S(1)}, bf16[512,512]{1,0:T(8,128)(2,1)S(1)}, u32[]{:S(2)}, u32[]{:S(2)}) %collective-permute-start.13) | collective-permute-done | bytes 524320 | tf_op jit(solution)/shard_map/ppermute | solution.py:480
  172.8 1.1 collective-permute-start.15
  173.9 1.5 collective-permute-done.15
  175.4 1.0 broadcast_select_fusion.4
  176.4 1.2 pad_maximum_fusion
  (44 shorter events, 8.2 us)
Async XLA Ops:
  8.9 13.0 %all-to-all-start = ((s32[16,1,16]{2,1,0:T(1,128)}), s32[16,1,16]{2,1,0:T(1,128)S(1)}, u32[]{:S(2)}, u32[]{:S(2)}) async-start(s32[16,1,16]{2,1,0:T(1,128)} %bitcast.76), calls=%async_computation | async-start | bytes 16384 | tf_op jit(solution)/shard_map/all_to_all | solution.py:565
  21.9 0.6 copy-start.5
  24.5 13.6 %all-to-all-start.1 = ((bf16[16,16,512]{2,1,0:T(8,128)(2,1)}), bf16[16,16,512]{2,1,0:T(8,128)(2,1)S(1)}, u32[]{:S(2)}, u32[]{:S(2)}) async-start(bf16[16,16,512]{2,1,0:T(8,128)(2,1)} %bitcast.74), calls=%async_computation.1 | async-start | bytes 524288 | tf_op jit(solution)/shard_map/all_to_all | solution.py:534
  38.1 0.7 copy-start.1
  43.1 13.5 %all-to-all-start.2 = ((bf16[16,16,512]{2,1,0:T(8,128)(2,1)}), bf16[16,16,512]{2,1,0:T(8,128)(2,1)S(1)}, u32[]{:S(2)}, u32[]{:S(2)}) async-start(bf16[16,16,512]{2,1,0:T(8,128)(2,1)} %bitcast.72), calls=%async_computation.2 | async-start | bytes 524288 | tf_op jit(solution)/shard_map/all_to_all | solution.py:534
  56.7 0.7 copy-start.2
  68.1 4.2 %collective-permute-start = (bf16[768,512]{1,0:T(8,128)(2,1)}, bf16[768,512]{1,0:T(8,128)(2,1)S(1)}, u32[]{:S(2)}, u32[]{:S(2)}) collective-permute-start(bf16[768,512]{1,0:T(8,128)(2,1)} %get-tuple-element.111.refs_8_), channel_id=1, source_target_pairs={{0,1},{1,0},{2,3},{3,2},{4,5},{5,4},{6,7},{7,6},{8,9},{9,8},{10,11... | collective-permute-start | bytes 2359304 | tf_op jit(solution)/shard_map/ppermute | solution.py:480
  68.7 12.9 %all-to-all-start.3 = ((bf16[16,16,512]{2,1,0:T(8,128)(2,1)}), bf16[16,16,512]{2,1,0:T(8,128)(2,1)S(1)}, u32[]{:S(2)}, u32[]{:S(2)}) async-start(bf16[16,16,512]{2,1,0:T(8,128)(2,1)} %bitcast.12), calls=%async_computation.3 | async-start | bytes 524288 | tf_op jit(solution)/shard_map/all_to_all | solution.py:534
  72.2 87.2 %all-gather.2.cloned.1.call-start = ((), (), s32[]{:S(2)}) async-start(), calls=%async_computation.5 | async-start | bytes 1671168 | tf_op jit(solution)/shard_map/all_gather | solution.py:802
  73.6 16.0 %collective-permute-start.1 = (bf16[384,512]{1,0:T(8,128)(2,1)S(1)}, bf16[384,512]{1,0:T(8,128)(2,1)S(1)}, u32[]{:S(2)}, u32[]{:S(2)}) collective-permute-start(bf16[384,512]{1,0:T(8,128)(2,1)S(1)} %get-tuple-element.164), channel_id=1, source_target_pairs={{0,2},{1,3},{2,0},{3,1},{4,6},{5,7},{6,4},{7,5},{8,10},{9,11},{10,... | collective-permute-start | bytes 1179656 | tf_op jit(solution)/shard_map/ppermute | solution.py:480
  81.6 0.7 copy-start.4
  89.7 5.1 %collective-permute-start.2 = (bf16[1024,512]{1,0:T(8,128)(2,1)}, bf16[1024,512]{1,0:T(8,128)(2,1)S(1)}, u32[]{:S(2)}, u32[]{:S(2)}) collective-permute-start(bf16[1024,512]{1,0:T(8,128)(2,1)} %shard_map.189.refs_12_), channel_id=1, source_target_pairs={{0,1},{1,0},{2,3},{3,2},{4,5},{5,4},{6,7},{7,6},{8,9},{9,8},{10,11... | collective-permute-start | bytes 3145736 | tf_op jit(solution)/shard_map/ppermute | solution.py:480
  96.4 13.6 %collective-permute-start.3 = (bf16[512,512]{1,0:T(8,128)(2,1)S(1)}, bf16[512,512]{1,0:T(8,128)(2,1)S(1)}, u32[]{:S(2)}, u32[]{:S(2)}) collective-permute-start(bf16[512,512]{1,0:T(8,128)(2,1)S(1)} %get-tuple-element.162), channel_id=1, source_target_pairs={{0,2},{1,3},{2,0},{3,1},{4,6},{5,7},{6,4},{7,5},{8,10},{9,11},{10,... | collective-permute-start | bytes 1572872 | tf_op jit(solution)/shard_map/ppermute | solution.py:480
  96.7 7.5 %collective-permute-start.4 = (bf16[96,512]{1,0:T(8,128)(2,1)S(1)}, bf16[96,512]{1,0:T(8,128)(2,1)S(1)}, u32[]{:S(2)}, u32[]{:S(2)}) collective-permute-start(bf16[96,512]{1,0:T(8,128)(2,1)S(1)} %get-tuple-element.172), channel_id=1, source_target_pairs={{0,4},{1,5},{2,6},{3,7},{4,0},{5,1},{6,2},{7,3},{8,12},{9,13},{10,... | collective-permute-start | bytes 294920 | tf_op jit(solution)/shard_map/ppermute | solution.py:480
  97.3 6.8 %collective-permute-start.5 = (bf16[96,512]{1,0:T(8,128)(2,1)S(1)}, bf16[96,512]{1,0:T(8,128)(2,1)S(1)}, u32[]{:S(2)}, u32[]{:S(2)}) collective-permute-start(bf16[96,512]{1,0:T(8,128)(2,1)S(1)} %get-tuple-element.171), channel_id=1, source_target_pairs={{0,8},{1,9},{2,10},{3,11},{4,12},{5,13},{6,14},{7,15},{8,0},{9,1},... | collective-permute-start | bytes 294920 | tf_op jit(solution)/shard_map/ppermute | solution.py:480
  98.5 6.8 %collective-permute-start.6 = (bf16[96,512]{1,0:T(8,128)(2,1)S(1)}, bf16[96,512]{1,0:T(8,128)(2,1)S(1)}, u32[]{:S(2)}, u32[]{:S(2)}) collective-permute-start(bf16[96,512]{1,0:T(8,128)(2,1)S(1)} %get-tuple-element.170), channel_id=1, source_target_pairs={{0,12},{1,13},{2,14},{3,15},{4,8},{5,9},{6,10},{7,11},{8,4},{9,5},... | collective-permute-start | bytes 294920 | tf_op jit(solution)/shard_map/ppermute | solution.py:480
  110.7 14.5 %all-to-all-start.4 = ((bf16[16,16,512]{2,1,0:T(8,128)(2,1)}), bf16[16,16,512]{2,1,0:T(8,128)(2,1)S(1)}, u32[]{:S(2)}, u32[]{:S(2)}) async-start(bf16[16,16,512]{2,1,0:T(8,128)(2,1)} %bitcast.68), calls=%async_computation.4 | async-start | bytes 524288 | tf_op jit(solution)/shard_map/all_to_all | solution.py:534
  115.1 11.8 %collective-permute-start.7 = (bf16[128,512]{1,0:T(8,128)(2,1)S(1)}, bf16[128,512]{1,0:T(8,128)(2,1)S(1)}, u32[]{:S(2)}, u32[]{:S(2)}) collective-permute-start(bf16[128,512]{1,0:T(8,128)(2,1)S(1)} %get-tuple-element.168), channel_id=1, source_target_pairs={{0,4},{1,5},{2,6},{3,7},{4,0},{5,1},{6,2},{7,3},{8,12},{9,13},{10,... | collective-permute-start | bytes 393224 | tf_op jit(solution)/shard_map/ppermute | solution.py:480
  116.5 14.2 %collective-permute-start.8 = (bf16[128,512]{1,0:T(8,128)(2,1)S(1)}, bf16[128,512]{1,0:T(8,128)(2,1)S(1)}, u32[]{:S(2)}, u32[]{:S(2)}) collective-permute-start(bf16[128,512]{1,0:T(8,128)(2,1)S(1)} %get-tuple-element.167), channel_id=1, source_target_pairs={{0,8},{1,9},{2,10},{3,11},{4,12},{5,13},{6,14},{7,15},{8,0},{9,1},... | collective-permute-start | bytes 393224 | tf_op jit(solution)/shard_map/ppermute | solution.py:480
  118.7 16.2 %collective-permute-start.9 = (bf16[128,512]{1,0:T(8,128)(2,1)S(1)}, bf16[128,512]{1,0:T(8,128)(2,1)S(1)}, u32[]{:S(2)}, u32[]{:S(2)}) collective-permute-start(bf16[128,512]{1,0:T(8,128)(2,1)S(1)} %get-tuple-element.166), channel_id=1, source_target_pairs={{0,12},{1,13},{2,14},{3,15},{4,8},{5,9},{6,10},{7,11},{8,4},{9,5},... | collective-permute-start | bytes 393224 | tf_op jit(solution)/shard_map/ppermute | solution.py:480
  125.2 15.6 %copy-start.3 = (bf16[16,16,512]{2,1,0:T(8,128)(2,1)}, bf16[16,16,512]{2,1,0:T(8,128)(2,1)S(1)}, u32[]{:S(2)}) copy-start(bf16[16,16,512]{2,1,0:T(8,128)(2,1)S(1)} %all-to-all-done.4) | copy-start | bytes 786436
  135.0 8.1 %collective-permute-start.10 = (bf16[128,512]{1,0:T(8,128)(2,1)S(1)}, bf16[128,512]{1,0:T(8,128)(2,1)S(1)}, u32[]{:S(2)}, u32[]{:S(2)}) collective-permute-start(bf16[128,512]{1,0:T(8,128)(2,1)S(1)} %add_convert_fusion.4), channel_id=1, source_target_pairs={{0,4},{1,5},{2,6},{3,7},{4,0},{5,1},{6,2},{7,3},{8,12},{9,13},{10,... | collective-permute-start | bytes 393224 | tf_op jit(solution)/shard_map/ppermute | solution.py:480
  138.6 14.4 %collective-permute-start.11 = (bf16[128,512]{1,0:T(8,128)(2,1)S(1)}, bf16[128,512]{1,0:T(8,128)(2,1)S(1)}, u32[]{:S(2)}, u32[]{:S(2)}) collective-permute-start(bf16[128,512]{1,0:T(8,128)(2,1)S(1)} %add_convert_fusion.4), channel_id=1, source_target_pairs={{0,8},{1,9},{2,10},{3,11},{4,12},{5,13},{6,14},{7,15},{8,0},{9,1},... | collective-permute-start | bytes 393224 | tf_op jit(solution)/shard_map/ppermute | solution.py:480
  138.8 14.2 %collective-permute-start.12 = (bf16[128,512]{1,0:T(8,128)(2,1)S(1)}, bf16[128,512]{1,0:T(8,128)(2,1)S(1)}, u32[]{:S(2)}, u32[]{:S(2)}) collective-permute-start(bf16[128,512]{1,0:T(8,128)(2,1)S(1)} %add_convert_fusion.4), channel_id=1, source_target_pairs={{0,12},{1,13},{2,14},{3,15},{4,8},{5,9},{6,10},{7,11},{8,4},{9,5},... | collective-permute-start | bytes 393224 | tf_op jit(solution)/shard_map/ppermute | solution.py:480
  159.3 1.9 %copy-start = (bf16[1536,512]{1,0:T(8,128)(2,1)S(1)}, bf16[1536,512]{1,0:T(8,128)(2,1)}, u32[]{:S(2)}) copy-start(bf16[1536,512]{1,0:T(8,128)(2,1)} %all-gather.2.cloned.1.call-done) | copy-start | bytes 4718596
  159.5 13.3 %collective-permute-start.13 = (bf16[512,512]{1,0:T(8,128)(2,1)S(1)}, bf16[512,512]{1,0:T(8,128)(2,1)S(1)}, u32[]{:S(2)}, u32[]{:S(2)}) collective-permute-start(bf16[512,512]{1,0:T(8,128)(2,1)S(1)} %bitcast.63), channel_id=1, source_target_pairs={{0,2},{1,3},{2,0},{3,1},{4,6},{5,7},{6,4},{7,5},{8,10},{9,11},{10,... | collective-permute-start | bytes 1572872 | tf_op jit(solution)/shard_map/ppermute | solution.py:480
  160.7 12.1 %collective-permute-start.14 = (bf16[512,512]{1,0:T(8,128)(2,1)S(1)}, bf16[512,512]{1,0:T(8,128)(2,1)S(1)}, u32[]{:S(2)}, u32[]{:S(2)}) collective-permute-start(bf16[512,512]{1,0:T(8,128)(2,1)S(1)} %bitcast.64), channel_id=1, source_target_pairs={{0,1},{1,0},{2,3},{3,2},{4,5},{5,4},{6,7},{7,6},{8,9},{9,8},{10,11... | collective-permute-start | bytes 1572872 | tf_op jit(solution)/shard_map/ppermute | solution.py:480
  172.8 2.6 %collective-permute-start.15 = (bf16[512,512]{1,0:T(8,128)(2,1)S(1)}, bf16[512,512]{1,0:T(8,128)(2,1)S(1)}, u32[]{:S(2)}, u32[]{:S(2)}) collective-permute-start(bf16[512,512]{1,0:T(8,128)(2,1)S(1)} %collective-permute-done.13), channel_id=1, source_target_pairs={{0,1},{1,0},{2,3},{3,2},{4,5},{5,4},{6,7},{7,6},{8,9},{9,8},{10,11... | collective-permute-start | bytes 1572872 | tf_op jit(solution)/shard_map/ppermute | solution.py:480
Sparse Core Ops, SparseCore 0:
  110.8 48.4 all-gather.1

commit v5 on v3

--- a/solution.py
+++ b/solution.py
@@ -443,7 +443,6 @@
         single = not isinstance(outs, (list, tuple))
         out_shape = [outs] if single else list(outs)
         specs = [VMEM] * len(ins) if specs is None else list(specs)
-        moved = sum(item.size * item.dtype.itemsize for item in list(ins) + out_shape)
         count, extra = len(ins), {} if grid is None else {"grid": grid}
         ins = list(ins)
         if self.last is not None:
@@ -459,7 +458,7 @@
             in_specs=specs,
             out_specs=[VMEM] * len(out_shape) if out_specs is None else out_specs,
             compiler_params=pltpu.CompilerParams(vmem_limit_bytes=VMEM_LIMIT),
-            cost_estimate=pl.CostEstimate(flops=flops, bytes_accessed=moved, transcendentals=0),
+            cost_estimate=pl.CostEstimate(flops=1, bytes_accessed=1, transcendentals=0),
             **extra,
         )(*ins)
         self.last = result[-1]
@@ -521,10 +520,32 @@
     return whole.reshape(size * parts[0].shape[0], parts[0].shape[1])
 
 
-def last_step(rows, others, lower, split):
-    half = rows.shape[0]
-    low, high = jnp.where(lower, rows, others), jnp.where(lower, others, rows)
-    return jnp.concatenate([low, high[: split - half]], axis=0), high[split - half :]
+def line_groups(devices, low, width):
+    size, mask = 1 << width, ((1 << width) - 1) << low
+    bases = [device for device in range(devices) if device & mask == 0]
+    return [[base + (turn << low) for turn in range(size)] for base in bases]
+
+
+def line_trade(rows, devices, low, width):
+    groups = line_groups(devices, low, width)
+    size = 1 << width
+    pieces = rows.reshape(size, rows.shape[0] // size, rows.shape[1])
+    return lax.all_to_all(
+        pieces, "dom", split_axis=0, concat_axis=0, axis_index_groups=groups, tiled=True
+    )
+
+
+def line_sum(parts):
+    return jnp.sum(parts.astype(F32), axis=0).astype(BF16)
+
+
+def line_share(rows, devices, low, width):
+    copies = jnp.broadcast_to(rows[None], (1 << width,) + rows.shape)
+    return line_trade(copies.reshape(-1, rows.shape[1]), devices, low, width)
+
+
+def merged(parts):
+    return parts.reshape(-1, parts.shape[-1])
 
 
 def exchange(rows, domains):
@@ -720,8 +741,8 @@
     )
     groups = bit_groups(domains)
     bit_one, bits_two = groups[1], groups[2]
+    node_parts = traded(pieces_of(node_sum, *bit_one), domains, bit_one[0])
     far_grad, node_sum, inner_pre = fence(far_grad, node_sum, inner_pre)
-    node_parts = traded(pieces_of(node_sum, *bit_one), domains, bit_one[0])
     cut_out, cut_pre = line.run(
         cut_backward_kernel,
         [shaped(BF16, cut_rows, latent)] * 2,
@@ -774,16 +795,17 @@
 
     edge_send, place, *node_parts = fence(edge_weights(1, me), me, *node_parts)
     edge_parts = [edge_weights(0, place), across(edge_send, domains, 1)]
-    node_parts = traded(pieces_of(added(*node_parts), *bits_two), domains, bits_two[0])
-    fenced = fence(*edge_parts, *node_parts, inner_pre, cut_pre)
-    edge_sum, node_sum = added(*fenced[:2]), added(*fenced[2:6])
-    inner_pre, cut_pre = fenced[6:]
+    node_parts = line_trade(added(*node_parts), domains, *bits_two)
+    *edge_parts, node_parts, inner_pre, cut_pre = fence(
+        *edge_parts, node_parts, inner_pre, cut_pre
+    )
+    node_sum = line_sum(node_parts)
     for low, width in groups[3:]:
-        node_sum = added(*traded(pieces_of(node_sum, low, width), domains, low))
+        node_sum = line_sum(line_trade(node_sum, domains, low, width))
     for low, width in groups[:2:-1]:
-        node_sum = joined(handed(node_sum, domains, low, width), low)
-    edge_parts = traded(pieces_of(edge_sum, *bit_one), domains, bit_one[0])
-    node_parts = handed(node_sum, domains, *bits_two)
+        node_sum = merged(line_share(node_sum, domains, low, width))
+    edge_parts = traded(pieces_of(added(*edge_parts), *bit_one), domains, bit_one[0])
+    node_parts = line_share(node_sum, domains, *bits_two)
     local_grad, outgoing_grad = line.run(
         input_grads_kernel,
         [shaped(F32, node_rows, latent), shaped(BF16, total_slots, latent)],
@@ -798,11 +820,10 @@
         ],
         (node_rows + total_slots) * 2 * square,
     )
-    returned = exchange(outgoing_grad, domains)
-    fenced = fence(*edge_parts, *node_parts, inner_pre, cut_pre, local_grad)
-    edge_sum, node_sum = added(*fenced[:2]), joined(fenced[2:6], bits_two[0])
-    inner_pre, cut_pre, local_grad = fenced[6:]
-    edge_parts = traded(pieces_of(edge_sum, *bits_two), domains, bits_two[0])
+    fenced = fence(*edge_parts, node_parts, inner_pre, cut_pre, local_grad)
+    edge_parts, node_sum, inner_pre, cut_pre, local_grad = (fenced[:2], *fenced[2:])
+    node_sum = merged(node_sum)
+    edge_parts = line_trade(added(*edge_parts), domains, *bits_two)
     node_parts = handed(node_sum, domains, *bit_one)
     grad_edges = line.run(
         functools.partial(edge_grads_kernel, blocks=blocks),
@@ -818,30 +839,46 @@
         [rows_spec(latent)],
         (blocks + 1,),
     )
-    fenced = fence(*edge_parts, *node_parts, returned, grad_edges)
-    edge_sum, node_sum = added(*fenced[:4]), joined(fenced[4:6], bit_one[0])
-    returned, grad_edges = fenced[6:]
+    edge_parts, *node_parts, grad_edges = fence(edge_parts, *node_parts, grad_edges)
+    edge_sum, node_sum = line_sum(edge_parts), joined(node_parts, bit_one[0])
     for low, width in groups[3:]:
-        edge_sum = added(*traded(pieces_of(edge_sum, low, width), domains, low))
+        edge_sum = line_sum(line_trade(edge_sum, domains, low, width))
     for low, width in groups[:2:-1]:
-        edge_sum = joined(handed(edge_sum, domains, low, width), low)
-    edge_parts = handed(edge_sum, domains, *bits_two)
+        edge_sum = merged(line_share(edge_sum, domains, low, width))
+    edge_parts = line_share(edge_sum, domains, *bits_two)
     others = across(node_sum, domains, 1)
+    edge_parts, node_sum, others, outgoing_grad = fence(
+        edge_parts, node_sum, others, outgoing_grad
+    )
+    edge_sum = merged(edge_parts)
+    edge_parts = handed(edge_sum, domains, *bit_one) + [across(edge_sum, domains, 1)]
+    returned = exchange(outgoing_grad, domains)
+    lower, left = place_of(0, 2) == 0, place_of(bit_one[0], 2) == 0
+    low_rows, high_rows = jnp.where(lower, node_sum, others), jnp.where(lower, others, node_sum)
+    split = 2 * latent - low_rows.shape[0]
+    grad_node_in = jnp.concatenate([low_rows, high_rows[:split]])
+    grad_node_out = high_rows[split:]
+    mine, far, near, grad_node_in, grad_node_out, returned = fence(
+        *edge_parts, grad_node_in, grad_node_out, returned
+    )
+    corner = across(far, domains, 1)
     grad_nodes = line.run(
         node_grads_kernel,
         shaped(F32, node_rows, latent),
         [self_grad, local_grad, asked_marks, returned],
         10**8,
     )
-    *edge_parts, node_sum, others, grad_nodes = fence(*edge_parts, node_sum, others, grad_nodes)
-    edge_parts = handed(joined(edge_parts, bits_two[0]), domains, *bit_one)
-    lower = place_of(0, 2) == 0
-    grad_node_in, grad_node_out = last_step(node_sum, others, lower, 2 * latent)
-    *edge_parts, grad_node_in, grad_node_out = fence(*edge_parts, grad_node_in, grad_node_out)
-    edge_sum = joined(edge_parts, bit_one[0])
-    grad_edge_in, grad_edge_out = last_step(
-        edge_sum, across(edge_sum, domains, 1), lower, 3 * latent
-    )
+    own, other = [mine, far], [near, corner]
+    low_half = [jnp.where(lower, one, two) for one, two in zip(own, other)]
+    high_half = [jnp.where(lower, two, one) for one, two in zip(own, other)]
+    grad_edge_in = jnp.concatenate(
+        [
+            jnp.where(left, low_half[0], low_half[1]),
+            jnp.where(left, low_half[1], low_half[0]),
+            jnp.where(left, high_half[0], high_half[1]),
+        ]
+    )
+    grad_edge_out = jnp.where(left, high_half[1], high_half[0])
     return (
         new_nodes,
         new_edges,

time: 164 us -> 174 us (1.061)
  waiting for transfers between devices: 48.5 us -> 63.3 us
  starting transfers between devices: 51.4 us -> 44.4 us
  other arithmetic: 5.36 us -> 7.21 us
    all_to_all x0 -> x4, waiting for transfers between devices: none -> 24.6 us  [line_trade(): lax.all_to_all(pieces, 'dom', split_axis=0, concat_axis=0, axis_index_gro...]
    ppermute x20 -> x9, starting transfers between devices: 27.3 us -> 7.49 us  [across(): lax.ppermute(rows, 'dom', [(device, device ^ mask) for device in range(de...]
    ppermute x20 -> x9, waiting for transfers between devices: 29.2 us -> 13 us  [across(): lax.ppermute(rows, 'dom', [(device, device ^ mask) for device in range(de...]
    all_to_all x0 -> x4, starting transfers between devices: none -> 14.6 us  [line_trade(): lax.all_to_all(pieces, 'dom', split_axis=0, concat_axis=0, axis_index_gro...]
    all_to_all x4, waiting for transfers between devices: 15.7 us -> 22 us  [exchange(): lax.all_to_all(split, 'dom', split_axis=0, concat_axis=0, tiled=True)]
  transfers between devices with their start and end apart: 25 -> 18, of which waited for: 13 -> 10; matrix products, arithmetic and copies ran while one was open for 2% -> 3% of each run, Pallas kernels for 22% -> 21%
where the time goes in v5:
time: 174 us; the launch traced here: 172 us
  waiting for transfers between devices  63.3 us (36%)
  Pallas kernels  51.2 us (29%)
  starting transfers between devices  44.4 us (26%)
  other arithmetic  7.21 us (4%)
  local copies, waits for them, and re-layouts  5.54 us (3%)
    pallas_call x15, Pallas kernels, run(): pl.pallas_call(ordered, out_shape=out_shape, in_specs=specs, out_specs=[V...  51.2 us
    all_to_all x4, waiting for transfers between devices, line_trade(): lax.all_to_all(pieces, 'dom', split_axis=0, concat_axis=0, axis_index_gro...  24.6 us
    all_to_all x4, waiting for transfers between devices, exchange(): lax.all_to_all(split, 'dom', split_axis=0, concat_axis=0, tiled=True)  22 us
    all_to_all x4, starting transfers between devices, exchange(): lax.all_to_all(split, 'dom', split_axis=0, concat_axis=0, tiled=True)  15.1 us
    all_to_all x4, starting transfers between devices, line_trade(): lax.all_to_all(pieces, 'dom', split_axis=0, concat_axis=0, axis_index_gro...  14.6 us
    ppermute x9, waiting for transfers between devices, across(): lax.ppermute(rows, 'dom', [(device, device ^ mask) for device in range(de...  13 us
    ppermute x9, starting transfers between devices, across(): lax.ppermute(rows, 'dom', [(device, device ^ mask) for device in range(de...  7.49 us
    all_to_all x1, starting transfers between devices, shards(): asked = lax.all_to_all(ask, 'dom', split_axis=0, concat_axis=0, tiled=True)  7.32 us
  transfers between devices with their start and end apart: 18, of which 10 were waited for; matrix products, arithmetic and copies ran while one was open for 3% of the time, Pallas kernels for 21%

profile of v5, /device:TPU:1, one launch (start us, length us, event | category | flops | bytes accessed | tf_op | source)
XLA Modules:
  0.0 172.4 jit_solution(6325728288658482582)
XLA Ops:
  0.6 1.7 shard_map.179.refs_2_
  2.3 7.3 %all-to-all-start = ((s32[16,1,16]{2,1,0:T(1,128)}), s32[16,1,16]{2,1,0:T(1,128)S(1)}, u32[]{:S(2)}, u32[]{:S(2)}) async-start(s32[16,1,16]{2,1,0:T(1,128)} %bitcast.45), calls=%async_computation | async-start | bytes 16384 | tf_op jit(solution)/shard_map/all_to_all | solution.py:585
  9.7 2.0 %shard_map.180 = (bf16[256,384]{1,0:T(8,128)(2,1)}, bf16[256,384]{1,0:T(8,128)(2,1)}) custom-call(s32[1,128]{1,0:T(1,128)} %bitcast.48, s32[1,128]{1,0:T(1,128)} %bitcast.51, s32[16,16]{1,0:T(8,128)} %shard_map.179.refs_2_), custom_call_target="tpu_custom_call" | custom-call | flops 1 | bytes 1 | tf_op jit(solution)/shard_map/pallas_call | solution.py:455
  11.7 3.7 %all-to-all-done = s32[16,1,16]{2,1,0:T(1,128)S(1)} async-done(((s32[16,1,16]{2,1,0:T(1,128)}), s32[16,1,16]{2,1,0:T(1,128)S(1)}, u32[]{:S(2)}, u32[]{:S(2)}) %all-to-all-start) | async-done | bytes 1056 | tf_op jit(solution)/shard_map/all_to_all | solution.py:585
  16.0 2.0 %shard_map.181 = (bf16[256,512]{1,0:T(8,128)(2,1)}, bf16[256,128]{1,0:T(8,128)(2,1)}) custom-call(s32[16,16]{1,0:T(8,128)} %bitcast.46, bf16[128,512]{1,0:T(8,128)(2,1)} %refs_1_.7, bf16[256,384]{1,0:T(8,128)(2,1)} %get-tuple-element.77.refs_2_.refs_1_.refs_0_.refs_3_), custom_call_target="tpu_custom_call" | custom-call | flops 1 | bytes 1 | tf_op jit(solution)/shard_map/pallas_call | solution.py:455
  18.0 4.0 %all-to-all-start.1 = ((bf16[16,16,512]{2,1,0:T(8,128)(2,1)}), bf16[16,16,512]{2,1,0:T(8,128)(2,1)S(1)}, u32[]{:S(2)}, u32[]{:S(2)}) async-start(bf16[16,16,512]{2,1,0:T(8,128)(2,1)} %bitcast.44), calls=%async_computation.1 | async-start | bytes 524288 | tf_op jit(solution)/shard_map/all_to_all | solution.py:554
  22.0 6.3 %shard_map.182 = (bf16[512,128]{1,0:T(8,128)(2,1)}, bf16[512,128]{1,0:T(8,128)(2,1)}, bf16[512,512]{1,0:T(8,128)(2,1)}, bf16[512,512]{1,0:T(8,128)(2,1)}, bf16[5...) custom-call(s32[2,256]{1,0:T(2,128)} %bitcast.49, ...), custom_call_target="tpu_custom_call" | custom-call | flops 1 | bytes 1 | tf_op jit(solution)/shard_map/pallas_call | solution.py:455
  28.3 3.3 %all-to-all-done.1 = bf16[16,16,512]{2,1,0:T(8,128)(2,1)S(1)} async-done(((bf16[16,16,512]{2,1,0:T(8,128)(2,1)}), bf16[16,16,512]{2,1,0:T(8,128)(2,1)S(1)}, u32[]{:S(2)}, u32[]{:S(2)}) %all-to-all-start.1) | async-done | bytes 262176 | tf_op jit(solution)/shard_map/all_to_all | solution.py:554
  31.6 0.7 copy-done.2
  32.3 4.3 %shard_map.183 = (bf16[256,512]{1,0:T(8,128)(2,1)}, bf16[256,512]{1,0:T(8,128)(2,1)}, bf16[256,512]{1,0:T(8,128)(2,1)}, f32[256,512]{1,0:T(8,128)}, f32[256,512]...) custom-call(bf16[256,384]{1,0:T(8,128)(2,1)} %get-tuple-element.76.refs_0_.refs_2_, ...), custom_call_target="tpu_custom_call" | custom-call | flops 1 | bytes 1 | tf_op jit(solution)/shard_map/pallas_call | solution.py:455
  36.6 4.0 %all-to-all-start.2 = ((bf16[16,16,512]{2,1,0:T(8,128)(2,1)}), bf16[16,16,512]{2,1,0:T(8,128)(2,1)S(1)}, u32[]{:S(2)}, u32[]{:S(2)}) async-start(bf16[16,16,512]{2,1,0:T(8,128)(2,1)} %bitcast.42), calls=%async_computation.2 | async-start | bytes 524288 | tf_op jit(solution)/shard_map/all_to_all | solution.py:554
  40.6 2.7 %shard_map.184.refs_7_ = bf16[768,512]{1,0:T(8,128)(2,1)} custom-call(bf16[768,512]{1,0:T(8,128)(2,1)} %refs_1_.9, f32[512,512]{1,0:T(8,128)} %get-tuple-element.83.refs_1_.refs_3_, f32[256,512]{1,0:T(8,128)} %get-tuple-element.84.refs_2_.refs_4_, bf16[256,512]{1,0:T(8,128)(2,1)} %get-tuple-element.81.refs_3_), custom_call_target="tpu_custom_call" | custom-call | flops 1 | bytes 1 | tf_op jit(solution)/shard_map/pallas_call | solution.py:455
  43.2 6.9 %all-to-all-done.2 = bf16[16,16,512]{2,1,0:T(8,128)(2,1)S(1)} async-done(((bf16[16,16,512]{2,1,0:T(8,128)(2,1)}), bf16[16,16,512]{2,1,0:T(8,128)(2,1)S(1)}, u32[]{:S(2)}, u32[]{:S(2)}) %all-to-all-start.2) | async-done | bytes 262176 | tf_op jit(solution)/shard_map/all_to_all | solution.py:554
  50.1 0.7 copy-done.3
  50.8 4.2 %shard_map.185 = (bf16[128,512]{1,0:T(8,128)(2,1)}, f32[128,512]{1,0:T(8,128)}, bf16[128,512]{1,0:T(8,128)(2,1)}, bf16[256,512]{1,0:T(8,128)(2,1)}, bf16[128,512...) custom-call(bf16[256,512]{1,0:T(8,128)(2,1)} %bitcast.40, ...), custom_call_target="tpu_custom_call" | custom-call | flops 1 | bytes 1 | tf_op jit(solution)/shard_map/pallas_call | solution.py:455
  55.0 2.9 %shard_map.186 = (bf16[768,512]{1,0:T(8,128)(2,1)}, bf16[768,512]{1,0:T(8,128)(2,1)}) custom-call(s32[1]{0:T(128)} %bitcast.11.refs_0_, bf16[128,512]{1,0:T(8,128)(2,1)} %refs_1_.7, bf16[128,512]{1,0:T(8,128)(2,1)} %get-tuple-element.97.refs_2_, bf16[128,512]{1,0:T(8,128)(2,1)} %get-tuple-element.98.refs_3_, bf16[128,512]{1,0:T(8,128)(2,1)} %get-tuple-element.99.refs_4_, ...), custom_call_target="tpu_custom_call" | custom-call | flops 1 | bytes 1 | tf_op jit(solution)/shard_map/pallas_call | solution.py:455
  58.6 3.4 %all-to-all-start.3 = ((bf16[16,16,512]{2,1,0:T(8,128)(2,1)}), bf16[16,16,512]{2,1,0:T(8,128)(2,1)S(1)}, u32[]{:S(2)}, u32[]{:S(2)}) async-start(bf16[16,16,512]{2,1,0:T(8,128)(2,1)} %bitcast.43), calls=%async_computation.3 | async-start | bytes 524288 | tf_op jit(solution)/shard_map/all_to_all | solution.py:554
  62.0 1.3 add_convert_fusion.1
  63.4 1.3 collective-permute-start.1
  64.8 3.6 %shard_map.187 = (bf16[512,512]{1,0:T(8,128)(2,1)}, bf16[512,512]{1,0:T(8,128)(2,1)}) custom-call(bf16[512,128]{1,0:T(8,128)(2,1)} %get-tuple-element.93.refs_0_.refs_1_, bf16[128,512]{1,0:T(8,128)(2,1)} %get-tuple-element.94.refs_1_, bf16[768,512]{1,0:T(8,128)(2,1)} %refs_0_.3, f32[512,512]{1,0:T(8,128)} %get-tuple-element.83.refs_1_.refs_3_, ...), custom_call_target="tpu_custom_call" | custom-call | flops 1 | bytes 1 | tf_op jit(solution)/shard_map/pallas_call | solution.py:455
  68.4 3.1 %all-to-all-done.3 = bf16[16,16,512]{2,1,0:T(8,128)(2,1)S(1)} async-done(((bf16[16,16,512]{2,1,0:T(8,128)(2,1)}), bf16[16,16,512]{2,1,0:T(8,128)(2,1)S(1)}, u32[]{:S(2)}, u32[]{:S(2)}) %all-to-all-start.3) | async-done | bytes 262176 | tf_op jit(solution)/shard_map/all_to_all | solution.py:554
  72.1 3.1 %shard_map.188 = (bf16[256,512]{1,0:T(8,128)(2,1)}, bf16[256,512]{1,0:T(8,128)(2,1)}) custom-call(bf16[256,384]{1,0:T(8,128)(2,1)} %get-tuple-element.77.refs_2_.refs_1_.refs_0_.refs_3_, bf16[128,512]{1,0:T(8,128)(2,1)} %get-tuple-element.94.refs_1_, bf16[256,512]{1,0:T(8,128)(2,1)} %bitcast.38, bf16[768,512]{1,0:T(8,128)(2,1)} %refs_0_.3, ...), custom_call_target="tpu_custom_call" | custom-call | flops 1 | bytes 1 | tf_op jit(solution)/shard_map/pallas_call | solution.py:455
  75.2 4.3 %shard_map.189.refs_12_ = bf16[1024,512]{1,0:T(8,128)(2,1)} custom-call(s32[1]{0:T(128)} %bitcast.11.refs_0_, bf16[768,512]{1,0:T(8,128)(2,1)} %refs_1_.9, bf16[512,512]{1,0:T(8,128)(2,1)} %get-tuple-element.87.refs_2_, bf16[256,512]{1,0:T(8,128)(2,1)} %get-tuple-element.88.refs_3_, bf16[512,512]{1,0:T(8,128)(2,1)} %get-tuple-element.89.refs_4_, ...), custom_call_target="tpu_custom_call" | custom-call | flops 1 | bytes 1 | tf_op jit(solution)/shard_map/pallas_call | solution.py:455
  80.2 0.8 add_convert_fusion.3
  81.0 3.5 %all-to-all-start.4 = ((bf16[4,96,512]{2,1,0:T(8,128)(2,1)}), bf16[4,96,512]{2,1,0:T(8,128)(2,1)S(1)}, u32[]{:S(2)}, u32[]{:S(2)}) async-start(bf16[4,96,512]{2,1,0:T(8,128)(2,1)} %bitcast.17), calls=%async_computation.4 | async-start | bytes 786432 | tf_op jit(solution)/shard_map/all_to_all | solution.py:533
  84.5 4.3 %shard_map.190.refs_7_ = bf16[1024,512]{1,0:T(8,128)(2,1)} custom-call(s32[1]{0:T(128)} %bitcast.11.refs_0_, bf16[768,512]{1,0:T(8,128)(2,1)} %refs_1_.9, bf16[512,512]{1,0:T(8,128)(2,1)} %get-tuple-element.87.refs_2_, bf16[256,512]{1,0:T(8,128)(2,1)} %get-tuple-element.88.refs_3_, bf16[512,512]{1,0:T(8,128)(2,1)} %get-tuple-element.89.refs_4_, ...), custom_call_target="tpu_custom_call" | custom-call | flops 1 | bytes 1 | tf_op jit(solution)/shard_map/pallas_call | solution.py:455
  88.8 7.5 %all-to-all-done.4 = bf16[4,96,512]{2,1,0:T(8,128)(2,1)S(1)} async-done(((bf16[4,96,512]{2,1,0:T(8,128)(2,1)}), bf16[4,96,512]{2,1,0:T(8,128)(2,1)S(1)}, u32[]{:S(2)}, u32[]{:S(2)}) %all-to-all-start.4) | async-done | bytes 393248 | tf_op jit(solution)/shard_map/all_to_all | solution.py:533
  96.4 0.8 broadcast_in_dim.4
  97.2 3.6 %all-to-all-start.5 = ((bf16[4,96,512]{2,1,0:T(8,128)(2,1)}), bf16[4,96,512]{2,1,0:T(8,128)(2,1)S(1)}, u32[]{:S(2)}, u32[]{:S(2)}) async-start(bf16[4,96,512]{2,1,0:T(8,128)(2,1)} %broadcast_in_dim.4), calls=%async_computation.5 | async-start | bytes 786432 | tf_op jit(solution)/shard_map/all_to_all | solution.py:533
  101.3 3.9 %shard_map.191 = (f32[128,512]{1,0:T(8,128)}, bf16[256,512]{1,0:T(8,128)(2,1)}) custom-call(bf16[512,128]{1,0:T(8,128)(2,1)} %get-tuple-element.121.refs_0_, bf16[512,128]{1,0:T(8,128)(2,1)} %get-tuple-element.93.refs_0_.refs_1_, bf16[256,384]{1,0:T(8,128)(2,1)} %get-tuple-element.76.refs_0_.refs_2_, ...), custom_call_target="tpu_custom_call" | custom-call | flops 1 | bytes 1 | tf_op jit(solution)/shard_map/pallas_call | solution.py:455
  105.2 8.8 %collective-permute-done.3 = bf16[512,512]{1,0:T(8,128)(2,1)S(1)} collective-permute-done((bf16[512,512]{1,0:T(8,128)(2,1)S(1)}, bf16[512,512]{1,0:T(8,128)(2,1)S(1)}, u32[]{:S(2)}, u32[]{:S(2)}) %collective-permute-start.3) | collective-permute-done | bytes 524320 | tf_op jit(solution)/shard_map/ppermute | solution.py:479
  113.9 0.9 add_convert_fusion.2
  114.9 4.0 %all-to-all-start.6 = ((bf16[4,128,512]{2,1,0:T(8,128)(2,1)}), bf16[4,128,512]{2,1,0:T(8,128)(2,1)S(1)}, u32[]{:S(2)}, u32[]{:S(2)}) async-start(bf16[4,128,512]{2,1,0:T(8,128)(2,1)} %bitcast.21), calls=%async_computation.6 | async-start | bytes 1048576 | tf_op jit(solution)/shard_map/all_to_all | solution.py:533
  119.1 3.9 %shard_map.192.refs_4_ = f32[768,512]{1,0:T(8,128)} custom-call(bf16[768,512]{1,0:T(8,128)(2,1)} %refs_0_.3, bf16[512,512]{1,0:T(8,128)(2,1)} %get-tuple-element.127.refs_8_.refs_10_.refs_4_.refs_1_, bf16[256,512]{1,0:T(8,128)(2,1)} %get-tuple-element.128.refs_11_.refs_12_.refs_5_.refs_2_, bf16[1536,512]{1,0:T(8,128)(2,1)} %refs_3_.9, ...), custom_call_target="tpu_custom_call" | custom-call | flops 1 | bytes 1 | tf_op jit(solution)/shard_map/pallas_call | solution.py:455
  123.0 4.2 %collective-permute-done.4 = bf16[384,512]{1,0:T(8,128)(2,1)S(1)} collective-permute-done((bf16[384,512]{1,0:T(8,128)(2,1)S(1)}, bf16[384,512]{1,0:T(8,128)(2,1)S(1)}, u32[]{:S(2)}, u32[]{:S(2)}) %collective-permute-start.4) | collective-permute-done | bytes 393248 | tf_op jit(solution)/shard_map/ppermute | solution.py:479
  127.2 5.3 %all-to-all-done.6 = bf16[4,128,512]{2,1,0:T(8,128)(2,1)S(1)} async-done(((bf16[4,128,512]{2,1,0:T(8,128)(2,1)}), bf16[4,128,512]{2,1,0:T(8,128)(2,1)S(1)}, u32[]{:S(2)}, u32[]{:S(2)}) %all-to-all-start.6) | async-done | bytes 524320 | tf_op jit(solution)/shard_map/all_to_all | solution.py:533
  132.6 0.8 broadcast_in_dim.5
  133.4 3.5 %all-to-all-start.7 = ((bf16[4,128,512]{2,1,0:T(8,128)(2,1)}), bf16[4,128,512]{2,1,0:T(8,128)(2,1)S(1)}, u32[]{:S(2)}, u32[]{:S(2)}) async-start(bf16[4,128,512]{2,1,0:T(8,128)(2,1)} %broadcast_in_dim.5), calls=%async_computation.7 | async-start | bytes 1048576 | tf_op jit(solution)/shard_map/all_to_all | solution.py:533
  137.2 1.9 %collective-permute-start.5 = (bf16[768,512]{1,0:T(8,128)(2,1)S(1)}, bf16[768,512]{1,0:T(8,128)(2,1)S(1)}, u32[]{:S(2)}, u32[]{:S(2)}) collective-permute-start(bf16[768,512]{1,0:T(8,128)(2,1)S(1)} %maximum_select_fusion), channel_id=1, source_target_pairs={{0,1},{1,0},{2,3},{3,2},{4,5},{5,4},{6,7},{7,6},{8,9},{9,8},{10,11... | collective-permute-start | bytes 2359304 | tf_op jit(solution)/shard_map/ppermute | solution.py:479
  139.1 11.8 %all-to-all-done.7 = bf16[4,128,512]{2,1,0:T(8,128)(2,1)S(1)} async-done(((bf16[4,128,512]{2,1,0:T(8,128)(2,1)}), bf16[4,128,512]{2,1,0:T(8,128)(2,1)S(1)}, u32[]{:S(2)}, u32[]{:S(2)}) %all-to-all-start.7) | async-done | bytes 524320 | tf_op jit(solution)/shard_map/all_to_all | solution.py:533
  151.3 1.7 %collective-permute-start.7 = (bf16[512,512]{1,0:T(8,128)(2,1)S(1)}, bf16[512,512]{1,0:T(8,128)(2,1)S(1)}, u32[]{:S(2)}, u32[]{:S(2)}) collective-permute-start(bf16[512,512]{1,0:T(8,128)(2,1)S(1)} %bitcast.34), channel_id=1, source_target_pairs={{0,1},{1,0},{2,3},{3,2},{4,5},{5,4},{6,7},{7,6},{8,9},{9,8},{10,11... | collective-permute-start | bytes 1572872 | tf_op jit(solution)/shard_map/ppermute | solution.py:479
  153.0 3.6 %all-to-all-start.8 = ((bf16[16,16,512]{2,1,0:T(8,128)(2,1)}), bf16[16,16,512]{2,1,0:T(8,128)(2,1)S(1)}, u32[]{:S(2)}, u32[]{:S(2)}) async-start(bf16[16,16,512]{2,1,0:T(8,128)(2,1)} %bitcast.24), calls=%async_computation.8 | async-start | bytes 524288 | tf_op jit(solution)/shard_map/all_to_all | solution.py:554
  156.8 0.8 slice.9
  157.6 1.0 pad_maximum_fusion.1
  158.6 8.8 %all-to-all-done.8 = bf16[16,16,512]{2,1,0:T(8,128)(2,1)S(1)} async-done(((bf16[16,16,512]{2,1,0:T(8,128)(2,1)}), bf16[16,16,512]{2,1,0:T(8,128)(2,1)S(1)}, u32[]{:S(2)}, u32[]{:S(2)}) %all-to-all-start.8) | async-done | bytes 262176 | tf_op jit(solution)/shard_map/all_to_all | solution.py:554
  168.1 2.0 %shard_map.193 = f32[128,512]{1,0:T(8,128)} custom-call(f32[128,512]{1,0:T(8,128)} %get-tuple-element.86.refs_0_, f32[128,512]{1,0:T(8,128)} %get-tuple-element.123.refs_1_, bf16[256,128]{1,0:T(8,128)(2,1)} %get-tuple-element.79.refs_5_.refs_1_.refs_2_, bf16[256,512]{1,0:T(8,128)(2,1)} %bitcast.41, f32[768,512]{1,0:T(8,128)} %shard_map.192.refs_4_), custom_call_target="tpu_custom_call" | custom-call | flops 1 | bytes 1 | tf_op jit(solution)/shard_map/pallas_call | solution.py:455
  170.2 1.0 broadcast_select_fusion.6
  171.1 1.2 pad_maximum_fusion
  (32 shorter events, 5.1 us)
Async XLA Ops:
  2.3 13.0 %all-to-all-start = ((s32[16,1,16]{2,1,0:T(1,128)}), s32[16,1,16]{2,1,0:T(1,128)S(1)}, u32[]{:S(2)}, u32[]{:S(2)}) async-start(s32[16,1,16]{2,1,0:T(1,128)} %bitcast.45), calls=%async_computation | async-start | bytes 16384 | tf_op jit(solution)/shard_map/all_to_all | solution.py:585
  15.4 0.6 copy-start.5
  18.0 13.6 %all-to-all-start.1 = ((bf16[16,16,512]{2,1,0:T(8,128)(2,1)}), bf16[16,16,512]{2,1,0:T(8,128)(2,1)S(1)}, u32[]{:S(2)}, u32[]{:S(2)}) async-start(bf16[16,16,512]{2,1,0:T(8,128)(2,1)} %bitcast.44), calls=%async_computation.1 | async-start | bytes 524288 | tf_op jit(solution)/shard_map/all_to_all | solution.py:554
  31.6 0.7 copy-start.2
  36.6 13.5 %all-to-all-start.2 = ((bf16[16,16,512]{2,1,0:T(8,128)(2,1)}), bf16[16,16,512]{2,1,0:T(8,128)(2,1)S(1)}, u32[]{:S(2)}, u32[]{:S(2)}) async-start(bf16[16,16,512]{2,1,0:T(8,128)(2,1)} %bitcast.42), calls=%async_computation.2 | async-start | bytes 524288 | tf_op jit(solution)/shard_map/all_to_all | solution.py:554
  50.1 0.7 copy-start.3
  57.9 4.1 %collective-permute-start = (bf16[768,512]{1,0:T(8,128)(2,1)}, bf16[768,512]{1,0:T(8,128)(2,1)S(1)}, u32[]{:S(2)}, u32[]{:S(2)}) collective-permute-start(bf16[768,512]{1,0:T(8,128)(2,1)} %get-tuple-element.101.refs_7_), channel_id=1, source_target_pairs={{0,1},{1,0},{2,3},{3,2},{4,5},{5,4},{6,7},{7,6},{8,9},{9,8},{10,11... | collective-permute-start | bytes 2359304 | tf_op jit(solution)/shard_map/ppermute | solution.py:479
  58.6 12.9 %all-to-all-start.3 = ((bf16[16,16,512]{2,1,0:T(8,128)(2,1)}), bf16[16,16,512]{2,1,0:T(8,128)(2,1)S(1)}, u32[]{:S(2)}, u32[]{:S(2)}) async-start(bf16[16,16,512]{2,1,0:T(8,128)(2,1)} %bitcast.43), calls=%async_computation.3 | async-start | bytes 524288 | tf_op jit(solution)/shard_map/all_to_all | solution.py:554
  63.4 16.1 %collective-permute-start.1 = (bf16[384,512]{1,0:T(8,128)(2,1)S(1)}, bf16[384,512]{1,0:T(8,128)(2,1)S(1)}, u32[]{:S(2)}, u32[]{:S(2)}) collective-permute-start(bf16[384,512]{1,0:T(8,128)(2,1)S(1)} %get-tuple-element.152), channel_id=1, source_target_pairs={{0,2},{1,3},{2,0},{3,1},{4,6},{5,7},{6,4},{7,5},{8,10},{9,11},{10,... | collective-permute-start | bytes 1179656 | tf_op jit(solution)/shard_map/ppermute | solution.py:479
  71.4 0.7 copy-start.1
  79.5 16.8 %collective-permute-start.2 = (bf16[1024,512]{1,0:T(8,128)(2,1)}, bf16[1024,512]{1,0:T(8,128)(2,1)S(1)}, u32[]{:S(2)}, u32[]{:S(2)}) collective-permute-start(bf16[1024,512]{1,0:T(8,128)(2,1)} %shard_map.189.refs_12_), channel_id=1, source_target_pairs={{0,1},{1,0},{2,3},{3,2},{4,5},{5,4},{6,7},{7,6},{8,9},{9,8},{10,11... | collective-permute-start | bytes 3145736 | tf_op jit(solution)/shard_map/ppermute | solution.py:479
  81.0 15.3 %all-to-all-start.4 = ((bf16[4,96,512]{2,1,0:T(8,128)(2,1)}), bf16[4,96,512]{2,1,0:T(8,128)(2,1)S(1)}, u32[]{:S(2)}, u32[]{:S(2)}) async-start(bf16[4,96,512]{2,1,0:T(8,128)(2,1)} %bitcast.17), calls=%async_computation.4 | async-start | bytes 786432 | tf_op jit(solution)/shard_map/all_to_all | solution.py:533
  88.8 12.0 %copy-start = (bf16[1024,512]{1,0:T(8,128)(2,1)S(1)}, bf16[1024,512]{1,0:T(8,128)(2,1)}, u32[]{:S(2)}) copy-start(bf16[1024,512]{1,0:T(8,128)(2,1)} %shard_map.190.refs_7_) | copy-start | bytes 3145732
  97.2 16.8 %all-to-all-start.5 = ((bf16[4,96,512]{2,1,0:T(8,128)(2,1)}), bf16[4,96,512]{2,1,0:T(8,128)(2,1)S(1)}, u32[]{:S(2)}, u32[]{:S(2)}) async-start(bf16[4,96,512]{2,1,0:T(8,128)(2,1)} %broadcast_in_dim.4), calls=%async_computation.5 | async-start | bytes 786432 | tf_op jit(solution)/shard_map/all_to_all | solution.py:533
  101.2 12.7 %collective-permute-start.3 = (bf16[512,512]{1,0:T(8,128)(2,1)S(1)}, bf16[512,512]{1,0:T(8,128)(2,1)S(1)}, u32[]{:S(2)}, u32[]{:S(2)}) collective-permute-start(bf16[512,512]{1,0:T(8,128)(2,1)S(1)} %get-tuple-element.150), channel_id=1, source_target_pairs={{0,2},{1,3},{2,0},{3,1},{4,6},{5,7},{6,4},{7,5},{8,10},{9,11},{10,... | collective-permute-start | bytes 1572872 | tf_op jit(solution)/shard_map/ppermute | solution.py:479
  114.9 17.6 %all-to-all-start.6 = ((bf16[4,128,512]{2,1,0:T(8,128)(2,1)}), bf16[4,128,512]{2,1,0:T(8,128)(2,1)S(1)}, u32[]{:S(2)}, u32[]{:S(2)}) async-start(bf16[4,128,512]{2,1,0:T(8,128)(2,1)} %bitcast.21), calls=%async_computation.6 | async-start | bytes 1048576 | tf_op jit(solution)/shard_map/all_to_all | solution.py:533
  118.8 8.3 %collective-permute-start.4 = (bf16[384,512]{1,0:T(8,128)(2,1)S(1)}, bf16[384,512]{1,0:T(8,128)(2,1)S(1)}, u32[]{:S(2)}, u32[]{:S(2)}) collective-permute-start(bf16[384,512]{1,0:T(8,128)(2,1)S(1)} %bitcast.36), channel_id=1, source_target_pairs={{0,2},{1,3},{2,0},{3,1},{4,6},{5,7},{6,4},{7,5},{8,10},{9,11},{10,... | collective-permute-start | bytes 1179656 | tf_op jit(solution)/shard_map/ppermute | solution.py:479
  133.4 17.4 %all-to-all-start.7 = ((bf16[4,128,512]{2,1,0:T(8,128)(2,1)}), bf16[4,128,512]{2,1,0:T(8,128)(2,1)S(1)}, u32[]{:S(2)}, u32[]{:S(2)}) async-start(bf16[4,128,512]{2,1,0:T(8,128)(2,1)} %broadcast_in_dim.5), calls=%async_computation.7 | async-start | bytes 1048576 | tf_op jit(solution)/shard_map/all_to_all | solution.py:533
  137.2 13.6 %collective-permute-start.5 = (bf16[768,512]{1,0:T(8,128)(2,1)S(1)}, bf16[768,512]{1,0:T(8,128)(2,1)S(1)}, u32[]{:S(2)}, u32[]{:S(2)}) collective-permute-start(bf16[768,512]{1,0:T(8,128)(2,1)S(1)} %maximum_select_fusion), channel_id=1, source_target_pairs={{0,1},{1,0},{2,3},{3,2},{4,5},{5,4},{6,7},{7,6},{8,9},{9,8},{10,11... | collective-permute-start | bytes 2359304 | tf_op jit(solution)/shard_map/ppermute | solution.py:479
  150.8 16.6 %collective-permute-start.6 = (bf16[512,512]{1,0:T(8,128)(2,1)S(1)}, bf16[512,512]{1,0:T(8,128)(2,1)S(1)}, u32[]{:S(2)}, u32[]{:S(2)}) collective-permute-start(bf16[512,512]{1,0:T(8,128)(2,1)S(1)} %bitcast.33), channel_id=1, source_target_pairs={{0,2},{1,3},{2,0},{3,1},{4,6},{5,7},{6,4},{7,5},{8,10},{9,11},{10,... | collective-permute-start | bytes 1572872 | tf_op jit(solution)/shard_map/ppermute | solution.py:479
  151.3 16.2 %collective-permute-start.7 = (bf16[512,512]{1,0:T(8,128)(2,1)S(1)}, bf16[512,512]{1,0:T(8,128)(2,1)S(1)}, u32[]{:S(2)}, u32[]{:S(2)}) collective-permute-start(bf16[512,512]{1,0:T(8,128)(2,1)S(1)} %bitcast.34), channel_id=1, source_target_pairs={{0,1},{1,0},{2,3},{3,2},{4,5},{5,4},{6,7},{7,6},{8,9},{9,8},{10,11... | collective-permute-start | bytes 1572872 | tf_op jit(solution)/shard_map/ppermute | solution.py:479
  153.0 14.4 %all-to-all-start.8 = ((bf16[16,16,512]{2,1,0:T(8,128)(2,1)}), bf16[16,16,512]{2,1,0:T(8,128)(2,1)S(1)}, u32[]{:S(2)}, u32[]{:S(2)}) async-start(bf16[16,16,512]{2,1,0:T(8,128)(2,1)} %bitcast.24), calls=%async_computation.8 | async-start | bytes 524288 | tf_op jit(solution)/shard_map/all_to_all | solution.py:554
  167.4 0.7 copy-start.4
  167.4 2.7 %collective-permute-start.8 = (bf16[512,512]{1,0:T(8,128)(2,1)S(1)}, bf16[512,512]{1,0:T(8,128)(2,1)S(1)}, u32[]{:S(2)}, u32[]{:S(2)}) collective-permute-start(bf16[512,512]{1,0:T(8,128)(2,1)S(1)} %collective-permute-done.6), channel_id=1, source_target_pairs={{0,1},{1,0},{2,3},{3,2},{4,5},{5,4},{6,7},{7,6},{8,9},{9,8},{10,11... | collective-permute-start | bytes 1572872 | tf_op jit(solution)/shard_map/ppermute | solution.py:479

commit v6 on v4

--- a/solution.py
+++ b/solution.py
@@ -223,6 +223,7 @@
 
 
 def node_kernel(
+    me_ref,
     incoming_ref,
     asked_marks_ref,
     total_ref,
@@ -234,48 +235,32 @@
     self_grad_ref,
     agg_grad_ref,
     reply_ref,
-    aggregate_ref,
-    hidden_ref,
-    grad_out_ref,
-    grad_pre_ref,
+    keep_ref,
+    send_ref,
 ):
     latent = nodes_ref.shape[1]
+    half = latent // 2
     nodes, asked_marks = nodes_ref[...], asked_marks_ref[...]
     aggregate = (total_ref[...] + dot_rows(asked_marks, incoming_ref[...])).astype(BF16)
-    aggregate_ref[...] = aggregate
     pre_hidden = dot(nodes, w_in_ref[:latent]) + dot(aggregate, w_in_ref[latent:])
     hidden, slope = activate(pre_hidden)
-    hidden_ref[...] = hidden
     normed, inv_scale = normalise(dot(hidden, w_out_ref[...]))
     upstream = ct_ref[...].astype(F32)
     grad_out = norm_backward(upstream, normed, inv_scale)
-    grad_out_ref[...] = grad_out
     grad_pre = (dot_cols(grad_out, w_out_ref[...]) * slope).astype(BF16)
-    grad_pre_ref[...] = grad_pre
     agg_grad = dot_cols(grad_pre, w_in_ref[latent:]).astype(BF16)
     agg_grad_ref[...] = agg_grad
     reply_ref[...] = dot(asked_marks, agg_grad).astype(BF16)
     self_grad_ref[...] = upstream + dot_cols(grad_pre, w_in_ref[:latent])
     new_nodes_ref[...] = (nodes.astype(F32) + normed).astype(BF16)
 
-
-def node_weights_kernel(
-    me_ref, nodes_ref, aggregate_ref, hidden_ref, grad_out_ref, grad_pre_ref, keep_ref, send_ref
-):
-    latent = nodes_ref.shape[1]
-    half = latent // 2
-
     def fill(low_ref, high_ref):
-        grad_pre, grad_out = grad_pre_ref[...], grad_out_ref[...]
-        low_ref[:latent] = dot_rows(nodes_ref[...], grad_pre).astype(BF16)
-        low_ref[latent:] = dot_rows(aggregate_ref[:, :half], grad_pre).astype(BF16)
-        high_ref[:half] = dot_rows(aggregate_ref[:, half:], grad_pre).astype(BF16)
-        high_ref[half:] = dot_rows(hidden_ref[...], grad_out).astype(BF16)
-
-    halves(me_ref, keep_ref, send_ref, fill)
-
-
-def halves(me_ref, keep_ref, send_ref, fill):
+        by_aggregate = dot_rows(aggregate, grad_pre).astype(BF16)
+        low_ref[:latent] = dot_rows(nodes, grad_pre).astype(BF16)
+        low_ref[latent:] = by_aggregate[:half]
+        high_ref[:half] = by_aggregate[half:]
+        high_ref[half:] = dot_rows(hidden, grad_out).astype(BF16)
+
     @pl.when((me_ref[0] & 1) == 0)
     def _():
         fill(keep_ref, send_ref)
@@ -313,7 +298,46 @@
     grad_pre_ref[...] = grad_pre
 
 
+def fetch_factors(half, sources, buffers, sems, wait):
+    edges, inner_sender, cut_sender, inner_receiver, cut_receiver = sources[:5]
+    inner_hidden, cut_hidden, inner_out, inner_pre = sources[5:]
+    inner_rows, cut_rows = inner_pre.shape[0], cut_sender.shape[0]
+    inner_edges = edges.at[pl.ds(0, inner_rows)]
+    cut_edges = edges.at[pl.ds(inner_rows, cut_rows)]
+    low = [inner_edges, cut_edges, inner_sender, cut_sender, inner_pre, inner_pre]
+    high = [inner_receiver, cut_receiver, inner_hidden, cut_hidden, inner_pre, inner_out]
+
+    def each(parts):
+        for index, (source, buffer) in enumerate(zip(parts, buffers)):
+            copy = pltpu.make_async_copy(source, buffer, sems.at[index])
+            if wait:
+                copy.wait()
+            else:
+                copy.start()
+
+    @pl.when(half == 0)
+    def _():
+        each(low)
+
+    @pl.when(half != 0)
+    def _():
+        each(high)
+
+
+def edge_rows(half, buffers, cut_pre, cut_out, out_ref):
+    latent = cut_pre.shape[1]
+    first, first_cut, second, second_cut, first_right, second_right = buffers
+    chosen = jnp.where(half == 0, cut_pre.astype(F32), cut_out.astype(F32)).astype(BF16)
+    out_ref[:latent] = (
+        dot_rows(first[...], first_right[...]) + dot_rows(first_cut[...], cut_pre)
+    ).astype(BF16)
+    out_ref[latent:] = (
+        dot_rows(second[...], second_right[...]) + dot_rows(second_cut[...], chosen)
+    ).astype(BF16)
+
+
 def cut_backward_kernel(
+    me_ref,
     receivers_ref,
     agg_grad_ref,
     far_grad_ref,
@@ -322,9 +346,12 @@
     scale_ref,
     slope_ref,
     w_out_ref,
-    grad_out_ref,
-    grad_pre_ref,
+    *refs,
 ):
+    sources, (grad_out_ref, grad_pre_ref, out_ref), rest = refs[:9], refs[9:12], refs[12:]
+    buffers, sems = rest[:-1], rest[-1]
+    half = 1 - (me_ref[0] & 1)
+    fetch_factors(half, sources, buffers, sems, False)
     base = agg_grad_ref.shape[0]
     target = dot(receivers_ref[:, :base], agg_grad_ref[...]) + dot(
         receivers_ref[:, base:], far_grad_ref[...]
@@ -334,48 +361,17 @@
     )
     grad_out_ref[...] = grad_out
     grad_pre_ref[...] = grad_pre
-
-
-def edge_weights_kernel(
-    me_ref,
-    edges_ref,
-    inner_sender_ref,
-    cut_sender_ref,
-    inner_receiver_ref,
-    cut_receiver_ref,
-    inner_hidden_ref,
-    cut_hidden_ref,
-    inner_out_ref,
-    cut_out_ref,
-    inner_pre_ref,
-    cut_pre_ref,
-    out_ref,
-    *,
-    turned,
-):
-    latent = edges_ref.shape[1]
-    inner_rows = inner_pre_ref.shape[0]
-
-    @pl.when((me_ref[0] & 1) == turned)
-    def _():
-        inner_pre, cut_pre = inner_pre_ref[...], cut_pre_ref[...]
-        out_ref[:latent] = (
-            dot_rows(edges_ref[:inner_rows], inner_pre) + dot_rows(edges_ref[inner_rows:], cut_pre)
-        ).astype(BF16)
-        out_ref[latent:] = (
-            dot_rows(inner_sender_ref[...], inner_pre) + dot_rows(cut_sender_ref[...], cut_pre)
-        ).astype(BF16)
-
-    @pl.when((me_ref[0] & 1) != turned)
-    def _():
-        out_ref[:latent] = (
-            dot_rows(inner_receiver_ref[...], inner_pre_ref[...])
-            + dot_rows(cut_receiver_ref[...], cut_pre_ref[...])
-        ).astype(BF16)
-        out_ref[latent:] = (
-            dot_rows(inner_hidden_ref[...], inner_out_ref[...])
-            + dot_rows(cut_hidden_ref[...], cut_out_ref[...])
-        ).astype(BF16)
+    fetch_factors(half, sources, buffers, sems, True)
+    edge_rows(half, buffers, grad_pre, grad_out, out_ref)
+
+
+def edge_weights_kernel(me_ref, cut_out_ref, cut_pre_ref, *refs):
+    sources, out_ref, rest = refs[:9], refs[9], refs[10:]
+    buffers, sems = rest[:-1], rest[-1]
+    half = me_ref[0] & 1
+    fetch_factors(half, sources, buffers, sems, False)
+    fetch_factors(half, sources, buffers, sems, True)
+    edge_rows(half, buffers, cut_pre_ref[...], cut_out_ref[...], out_ref)
 
 
 def input_grads_kernel(
@@ -439,11 +435,10 @@
     def __init__(self):
         self.last = None
 
-    def run(self, body, outs, ins, flops, specs=None, out_specs=None, grid=None):
+    def run(self, body, outs, ins, specs=None, out_specs=None, grid=None, scratch=()):
         single = not isinstance(outs, (list, tuple))
         out_shape = [outs] if single else list(outs)
         specs = [VMEM] * len(ins) if specs is None else list(specs)
-        moved = sum(item.size * item.dtype.itemsize for item in list(ins) + out_shape)
         count, extra = len(ins), {} if grid is None else {"grid": grid}
         ins = list(ins)
         if self.last is not None:
@@ -458,22 +453,17 @@
             out_shape=out_shape,
             in_specs=specs,
             out_specs=[VMEM] * len(out_shape) if out_specs is None else out_specs,
+            scratch_shapes=scratch,
             compiler_params=pltpu.CompilerParams(vmem_limit_bytes=VMEM_LIMIT),
-            cost_estimate=pl.CostEstimate(flops=flops, bytes_accessed=moved, transcendentals=0),
+            cost_estimate=pl.CostEstimate(flops=1, bytes_accessed=1, transcendentals=0),
             **extra,
         )(*ins)
         self.last = result[-1]
         return result[0] if single else result
 
 
-def bit_groups(devices):
-    bits = devices.bit_length() - 1
-    groups = [(low, 1) for low in range(min(2, bits))]
-    low = 2
-    while low < bits:
-        groups.append((low, min(2, bits - low)))
-        low += 2
-    return groups
+def index_bits(devices):
+    return list(range(devices.bit_length() - 1))
 
 
 def across(rows, devices, mask):
@@ -484,48 +474,29 @@
     return lax.optimization_barrier(values)
 
 
-def place_of(low, size):
-    return (lax.axis_index("dom") >> low) & (size - 1)
-
-
-def pieces_of(rows, low, width):
-    size = 1 << width
-    place = place_of(low, size)
-    pieces = rows.reshape(size, rows.shape[0] // size, rows.shape[1])
-    return [lax.dynamic_index_in_dim(pieces, place ^ turn, 0, False) for turn in range(size)]
-
-
-def traded(pieces, devices, low):
-    return pieces[:1] + [
-        across(piece, devices, turn << low) for turn, piece in enumerate(pieces) if turn
-    ]
-
-
-def handed(rows, devices, low, width):
-    return traded([rows] * (1 << width), devices, low)
-
-
-def added(*parts):
-    return sum(part.astype(F32) for part in parts).astype(BF16)
-
-
-def joined(parts, low):
-    size = len(parts)
-    place = place_of(low, size)
-    if size == 2:
-        orders = [jnp.concatenate(parts), jnp.concatenate(parts[::-1])]
-        return jnp.where(place == 0, *orders)
-    whole = jnp.zeros((size,) + parts[0].shape, parts[0].dtype)
-    for turn, part in enumerate(parts):
-        whole = lax.dynamic_update_index_in_dim(whole, part, place ^ turn, 0)
-    return whole.reshape(size * parts[0].shape[0], parts[0].shape[1])
-
-
-def by_owner(rows, groups):
-    sizes = [1 << width for _, width in groups]
-    split = rows.reshape(sizes[::-1] + [-1, rows.shape[1]])
-    turned = list(range(len(sizes)))[::-1] + [len(sizes), len(sizes) + 1]
-    return split.transpose(turned).reshape(rows.shape)
+def place_of(bit):
+    return (lax.axis_index("dom") >> bit) & 1
+
+
+def traded(rows, devices, bit):
+    place = place_of(bit)
+    halves = rows.reshape(2, rows.shape[0] // 2, rows.shape[1])
+    own = lax.dynamic_index_in_dim(halves, place, 0, False)
+    sent = lax.dynamic_index_in_dim(halves, 1 - place, 0, False)
+    return own, across(sent, devices, 1 << bit)
+
+
+def handed(rows, devices, bit):
+    return [rows, across(rows, devices, 1 << bit)]
+
+
+def added(left, right):
+    return (left.astype(F32) + right.astype(F32)).astype(BF16)
+
+
+def joined(parts, bit):
+    orders = [jnp.concatenate(parts), jnp.concatenate(parts[::-1])]
+    return jnp.where(place_of(bit) == 0, *orders)
 
 
 def exchange(rows, domains):
@@ -555,25 +526,22 @@
     slots = max(2, 2 * cut_count // domains)
     total_slots = domains * slots
     table = node_rows + total_slots
-    square = 2 * latent * latent
     me = lax.axis_index("dom").reshape(1)
     line = Line()
 
     ask = line.run(
-        ask_kernel, shaped(jnp.int32, domains, slots), [cut_dest.reshape(1, -1), cut_remote.reshape(1, -1)], 10**7
+        ask_kernel, shaped(jnp.int32, domains, slots), [cut_dest.reshape(1, -1), cut_remote.reshape(1, -1)]
     )
     asked = lax.all_to_all(ask, "dom", split_axis=0, concat_axis=0, tiled=True)
     cut_senders, cut_receivers = line.run(
         functools.partial(cut_marks_kernel, domains=domains, slots=slots),
         [shaped(BF16, cut_rows, table)] * 2,
         [cut_dest.reshape(1, -1), cut_local.reshape(1, -1)],
-        10**8,
     )
     reply, asked_marks = line.run(
         reply_kernel,
         [shaped(BF16, total_slots, latent), shaped(BF16, total_slots, node_rows)],
         [asked, nodes],
-        10**8,
     )
     far = exchange(reply, domains)
 
@@ -603,7 +571,6 @@
         [shaped(kind, inner_rows, width) for kind, width in zip(saved_types, saved_widths)]
         + [shaped(F32, node_rows, latent)],
         [inner_pairs.T, edges, nodes, w_edge_in, w_edge_out],
-        inner_rows * 4 * square,
         [
             pl.BlockSpec((2, block // 2), lambda step: (0, step)),
             rows_spec(latent),
@@ -642,7 +609,6 @@
             w_edge_out,
             inner_total,
         ],
-        cut_rows * 4 * square,
         [
             all_spec(cut_senders),
             all_spec(cut_receivers),
@@ -662,17 +628,14 @@
         new_edges_kernel,
         shaped(BF16, *edges.shape),
         [edges, inner_normed, cut_normed],
-        10**7,
     )
     (
         new_nodes,
         self_grad,
         agg_grad,
         grad_reply,
-        aggregate,
-        node_hidden,
-        node_out,
-        node_pre,
+        node_keep,
+        node_send,
     ) = line.run(
         node_kernel,
         [
@@ -681,11 +644,12 @@
             shaped(BF16, node_rows, latent),
             shaped(BF16, total_slots, latent),
         ]
-        + [shaped(BF16, node_rows, latent)] * 4,
-        [incoming, asked_marks, total, nodes, ct_nodes, w_node_in, w_node_out],
-        node_rows * 6 * square,
+        + [shaped(BF16, 3 * latent // 2, latent)] * 2,
+        [me, incoming, asked_marks, total, nodes, ct_nodes, w_node_in, w_node_out],
+        [SMEM] + [VMEM] * 7,
     )
     far_grad = exchange(grad_reply, domains)
+    node_sum = added(node_keep, across(node_send, domains, 1))
     inner_out, inner_pre = line.run(
         inner_backward_kernel,
         [shaped(BF16, inner_rows, latent)] * 2,
@@ -698,7 +662,6 @@
             inner_slope,
             w_edge_out,
         ],
-        inner_rows * square,
         [
             rows_spec(node_rows),
             all_spec(agg_grad),
@@ -711,45 +674,9 @@
         [rows_spec(latent)] * 2,
         (blocks,),
     )
-    node_keep, node_send = line.run(
-        node_weights_kernel,
-        [shaped(BF16, 3 * latent // 2, latent)] * 2,
-        [me, nodes, aggregate, node_hidden, node_out, node_pre],
-        node_rows * 3 * square,
-        [SMEM] + [VMEM] * 5,
-    )
-    node_sum = added(node_keep, across(node_send, domains, 1))
-    groups = bit_groups(domains)
-    bit_one, bits_two = groups[1], groups[2]
-    node_parts = traded(pieces_of(node_sum, *bit_one), domains, bit_one[0])
+    bits = index_bits(domains)
+    node_parts = traded(node_sum, domains, 1)
     far_grad, node_sum, inner_pre = fence(far_grad, node_sum, inner_pre)
-    cut_out, cut_pre = line.run(
-        cut_backward_kernel,
-        [shaped(BF16, cut_rows, latent)] * 2,
-        [
-            cut_receivers,
-            agg_grad,
-            far_grad,
-            ct_edges,
-            cut_normed,
-            cut_scale,
-            cut_slope,
-            w_edge_out,
-        ],
-        cut_rows * square,
-        [
-            all_spec(cut_receivers),
-            all_spec(agg_grad),
-            all_spec(far_grad),
-            last_rows(ct_edges),
-            all_spec(cut_normed),
-            all_spec(cut_scale),
-            all_spec(cut_slope),
-            all_spec(w_edge_out),
-        ],
-        [rows_spec(latent)] * 2,
-        (1,),
-    )
     factors = [
         edges,
         inner_sender,
@@ -759,26 +686,56 @@
         inner_hidden,
         cut_hidden,
         inner_out,
-        cut_out,
         inner_pre,
-        cut_pre,
     ]
-
-    def edge_weights(turned, place):
-        return line.run(
-            functools.partial(edge_weights_kernel, turned=turned),
-            shaped(BF16, 2 * latent, latent),
-            [place] + factors,
-            (inner_rows + cut_rows) * 2 * square,
-            [SMEM] + [VMEM] * len(factors),
-        )
-
-    edge_send, place, *node_parts = fence(edge_weights(1, me), me, *node_parts)
-    edge_parts = [edge_weights(0, place), across(edge_send, domains, 1)]
+    buffers = [pltpu.VMEM((rows, latent), BF16) for rows in (inner_rows, cut_rows) * 2]
+    buffers += [pltpu.VMEM((inner_rows, latent), BF16)] * 2
+    buffers.append(pltpu.SemaphoreType.DMA((len(buffers),)))
+    cut_out, cut_pre, edge_send = line.run(
+        cut_backward_kernel,
+        [shaped(BF16, cut_rows, latent)] * 2 + [shaped(BF16, 2 * latent, latent)],
+        [
+            me,
+            cut_receivers,
+            agg_grad,
+            far_grad,
+            ct_edges,
+            cut_normed,
+            cut_scale,
+            cut_slope,
+            w_edge_out,
+        ]
+        + factors,
+        [
+            SMEM,
+            all_spec(cut_receivers),
+            all_spec(agg_grad),
+            all_spec(far_grad),
+            last_rows(ct_edges),
+            all_spec(cut_normed),
+            all_spec(cut_scale),
+            all_spec(cut_slope),
+            all_spec(w_edge_out),
+        ]
+        + [ANY] * len(factors),
+        [rows_spec(latent)] * 2 + [rows_spec(latent, 2 * latent)],
+        (1,),
+        buffers,
+    )
+    edge_send, place, *node_parts = fence(edge_send, me, *node_parts)
+    edge_keep = line.run(
+        edge_weights_kernel,
+        shaped(BF16, 2 * latent, latent),
+        [place, cut_out, cut_pre] + factors,
+        [SMEM, VMEM, VMEM] + [ANY] * len(factors),
+        scratch=buffers,
+    )
+    edge_parts = [edge_keep, across(edge_send, domains, 1)]
+    node_parts = traded(added(*node_parts), domains, 2)
     fenced = fence(*edge_parts, *node_parts, inner_pre, cut_pre)
-    edge_parts, node_parts, (inner_pre, cut_pre) = fenced[:2], fenced[2:4], fenced[4:]
-    edge_parts = traded(pieces_of(added(*edge_parts), *bit_one), domains, bit_one[0])
-    node_parts = traded(pieces_of(added(*node_parts), *bits_two), domains, bits_two[0])
+    edge_sum, node_sum, (inner_pre, cut_pre) = added(*fenced[:2]), added(*fenced[2:4]), fenced[4:]
+    edge_parts = traded(edge_sum, domains, 1)
+    node_parts = traded(node_sum, domains, 3)
     local_grad, outgoing_grad = line.run(
         input_grads_kernel,
         [shaped(F32, node_rows, latent), shaped(BF16, total_slots, latent)],
@@ -791,21 +748,24 @@
             cut_pre,
             w_edge_in,
         ],
-        (node_rows + total_slots) * 2 * square,
-    )
-    returned = exchange(outgoing_grad, domains)
+    )
     fenced = fence(*edge_parts, *node_parts, inner_pre, cut_pre, local_grad)
-    edge_parts, node_sum = fenced[:2], added(*fenced[2:6])
-    inner_pre, cut_pre, local_grad = fenced[6:]
-    for low, width in groups[3:]:
-        node_sum = added(*traded(pieces_of(node_sum, low, width), domains, low))
-    node_total = lax.all_gather(node_sum, "dom", axis=0, tiled=True)
-    edge_parts = traded(pieces_of(added(*edge_parts), *bits_two), domains, bits_two[0])
+    edge_sum, node_sum = added(*fenced[:2]), added(*fenced[2:4])
+    inner_pre, cut_pre, local_grad = fenced[4:]
+    for bit in bits[4:]:
+        node_sum = added(*traded(node_sum, domains, bit))
+    for bit in bits[:3:-1]:
+        node_sum = joined(handed(node_sum, domains, bit), bit)
+    edge_parts = traded(edge_sum, domains, 2)
+    node_parts = handed(node_sum, domains, 3)
+    fenced = fence(*edge_parts, *node_parts, inner_pre)
+    edge_sum, node_sum, inner_pre = added(*fenced[:2]), joined(fenced[2:4], 3), fenced[4]
+    edge_parts = traded(edge_sum, domains, 3)
+    node_parts = handed(node_sum, domains, 2)
     grad_edges = line.run(
         functools.partial(edge_grads_kernel, blocks=blocks),
         shaped(F32, *edges.shape),
         [ct_edges, inner_pre, cut_pre, w_edge_in],
-        (inner_rows + cut_rows) * square,
         [
             rows_spec(latent),
             pl.BlockSpec((block, latent), lambda step: (jnp.minimum(step, blocks - 1), 0)),
@@ -815,27 +775,37 @@
         [rows_spec(latent)],
         (blocks + 1,),
     )
-    *edge_parts, returned, grad_edges = fence(*edge_parts, returned, grad_edges)
-    edge_sum = added(*edge_parts)
-    for low, width in groups[3:]:
-        edge_sum = added(*traded(pieces_of(edge_sum, low, width), domains, low))
-    for low, width in groups[:2:-1]:
-        edge_sum = joined(handed(edge_sum, domains, low, width), low)
-    edge_parts = handed(edge_sum, domains, *bits_two)
+    fenced = fence(*edge_parts, *node_parts, grad_edges)
+    edge_sum, node_sum, grad_edges = added(*fenced[:2]), joined(fenced[2:4], 2), fenced[4]
+    for bit in bits[4:]:
+        edge_sum = added(*traded(edge_sum, domains, bit))
+    for bit in bits[:3:-1]:
+        edge_sum = joined(handed(edge_sum, domains, bit), bit)
+    node_parts = handed(node_sum, domains, 1)
+    edge_parts = fence(*handed(edge_sum, domains, 3))
+    edge_parts = handed(joined(edge_parts, 3), domains, 2)
+    *edge_parts, node_sum, other_sum, outgoing_grad = fence(
+        *edge_parts, *node_parts, outgoing_grad
+    )
+    node_sum = joined([node_sum, other_sum], 1)
+    edge_sum = joined(edge_parts, 2)
+    edge_parts = handed(edge_sum, domains, 1) + [across(edge_sum, domains, 1)]
+    others = across(node_sum, domains, 1)
+    returned = exchange(outgoing_grad, domains)
+    lower, left = place_of(0) == 0, place_of(1) == 0
+    low_rows, high_rows = jnp.where(lower, node_sum, others), jnp.where(lower, others, node_sum)
+    split = 2 * latent - low_rows.shape[0]
+    grad_node_in = jnp.concatenate([low_rows, high_rows[:split]])
+    grad_node_out = high_rows[split:]
+    mine, far, near, grad_node_in, grad_node_out, returned = fence(
+        *edge_parts, grad_node_in, grad_node_out, returned
+    )
+    corner = across(far, domains, 1)
     grad_nodes = line.run(
         node_grads_kernel,
         shaped(F32, node_rows, latent),
         [self_grad, local_grad, asked_marks, returned],
-        10**8,
-    )
-    *edge_parts, grad_nodes, node_total = fence(*edge_parts, grad_nodes, node_total)
-    edge_sum = joined(edge_parts, bits_two[0])
-    edge_parts = handed(edge_sum, domains, *bit_one) + [across(edge_sum, domains, 1)]
-    node_total = by_owner(node_total, groups)
-    grad_node_in, grad_node_out = node_total[: 2 * latent], node_total[2 * latent :]
-    mine, far, near, grad_node_in, grad_node_out = fence(*edge_parts, grad_node_in, grad_node_out)
-    corner = across(far, domains, 1)
-    lower, left = place_of(0, 2) == 0, place_of(bit_one[0], 2) == 0
+    )
     own, other = [mine, far], [near, corner]
     low_half = [jnp.where(lower, one, two) for one, two in zip(own, other)]
     high_half = [jnp.where(lower, two, one) for one, two in zip(own, other)]

time: 186 us -> 155 us (0.83)
  between operations: 14.2 us -> 0.88 us
  waiting for transfers between devices: 66.2 us -> 59 us
  starting transfers between devices: 41.6 us -> 34.5 us
  Pallas kernels: 51.3 us -> 48 us
    ppermute x16 -> x17, starting transfers between devices: 18.6 us -> 12 us  [across(): lax.ppermute(rows, 'dom', [(device, device ^ mask) for device in range(de...]
    all_gather x1 -> x0, waiting for transfers between devices: 6.29 us -> none  [shards(): node_total = lax.all_gather(node_sum, 'dom', axis=0, tiled=True)]
    ppermute x16 -> x17, waiting for transfers between devices: 36.9 us -> 31.6 us  [across(): lax.ppermute(rows, 'dom', [(device, device ^ mask) for device in range(de...]
    all_to_all x4, waiting for transfers between devices: 19.4 us -> 23.7 us  [exchange(): lax.all_to_all(split, 'dom', split_axis=0, concat_axis=0, tiled=True)]
    pallas_call x15 -> x13, Pallas kernels: 51.3 us -> 48 us  [run(): pl.pallas_call(ordered, out_shape=out_shape, in_specs=specs, out_specs=[V...]
    convert_element_type x6 -> x8, other arithmetic: 3.84 us -> 3.26 us  [added(): return (left.astype(F32) + right.astype(F32)).astype(BF16)]
  transfers between devices with their start and end apart: 22 -> 22, of which waited for: 15 -> 15; matrix products, arithmetic and copies ran while one was open for 2% -> 3% of each run, Pallas kernels for 18% -> 22%
where the time goes in v6:
time: 155 us; the launch traced here: 154 us
  waiting for transfers between devices  59 us (38%)
  Pallas kernels  48 us (31%)
  starting transfers between devices  34.5 us (22%)
  other arithmetic  7.35 us (5%)
  local copies, waits for them, and re-layouts  4.06 us (3%)
    pallas_call x13, Pallas kernels, run(): pl.pallas_call(ordered, out_shape=out_shape, in_specs=specs, out_specs=[V...  48 us
    ppermute x17, waiting for transfers between devices, across(): lax.ppermute(rows, 'dom', [(device, device ^ mask) for device in range(de...  31.6 us
    all_to_all x4, waiting for transfers between devices, exchange(): lax.all_to_all(split, 'dom', split_axis=0, concat_axis=0, tiled=True)  23.7 us
    all_to_all x4, starting transfers between devices, exchange(): lax.all_to_all(split, 'dom', split_axis=0, concat_axis=0, tiled=True)  15.2 us
    ppermute x17, starting transfers between devices, across(): lax.ppermute(rows, 'dom', [(device, device ^ mask) for device in range(de...  12 us
    all_to_all x1, starting transfers between devices, shards(): asked = lax.all_to_all(ask, 'dom', split_axis=0, concat_axis=0, tiled=True)  7.32 us
    all_to_all x1, waiting for transfers between devices, shards(): asked = lax.all_to_all(ask, 'dom', split_axis=0, concat_axis=0, tiled=True)  3.68 us
    convert_element_type x8, other arithmetic, added(): return (left.astype(F32) + right.astype(F32)).astype(BF16)  3.26 us
  transfers between devices with their start and end apart: 22, of which 15 were waited for; matrix products, arithmetic and copies ran while one was open for 3% of the time, Pallas kernels for 22%

profile of v6, /device:TPU:1, one launch (start us, length us, event | category | flops | bytes accessed | tf_op | source)
XLA Modules:
  0.0 153.8 jit_solution(12424960079819927843)
XLA Ops:
  0.6 1.7 %shard_map.179.refs_2_ = s32[16,16]{1,0:T(8,128)} custom-call(s32[1,128]{1,0:T(1,128)} %bitcast.62, s32[1,128]{1,0:T(1,128)} %bitcast.65), custom_call_target="tpu_custom_call" | custom-call | flops 1 | bytes 1 | tf_op jit(solution)/shard_map/pallas_call | solution.py:451
  2.3 7.3 %all-to-all-start = ((s32[16,1,16]{2,1,0:T(1,128)}), s32[16,1,16]{2,1,0:T(1,128)S(1)}, u32[]{:S(2)}, u32[]{:S(2)}) async-start(s32[16,1,16]{2,1,0:T(1,128)} %bitcast.60), calls=%async_computation | async-start | bytes 16384 | tf_op jit(solution)/shard_map/all_to_all | solution.py:535
  9.7 2.0 %shard_map.180 = (bf16[256,384]{1,0:T(8,128)(2,1)}, bf16[256,384]{1,0:T(8,128)(2,1)}) custom-call(s32[1,128]{1,0:T(1,128)} %bitcast.63, s32[1,128]{1,0:T(1,128)} %bitcast.66, s32[16,16]{1,0:T(8,128)} %shard_map.179.refs_2_), custom_call_target="tpu_custom_call" | custom-call | flops 1 | bytes 1 | tf_op jit(solution)/shard_map/pallas_call | solution.py:451
  11.7 3.7 %all-to-all-done = s32[16,1,16]{2,1,0:T(1,128)S(1)} async-done(((s32[16,1,16]{2,1,0:T(1,128)}), s32[16,1,16]{2,1,0:T(1,128)S(1)}, u32[]{:S(2)}, u32[]{:S(2)}) %all-to-all-start) | async-done | bytes 1056 | tf_op jit(solution)/shard_map/all_to_all | solution.py:535
  16.0 2.0 %shard_map.181 = (bf16[256,512]{1,0:T(8,128)(2,1)}, bf16[256,128]{1,0:T(8,128)(2,1)}) custom-call(s32[16,16]{1,0:T(8,128)} %bitcast.61, bf16[128,512]{1,0:T(8,128)(2,1)} %refs_4_.4, bf16[256,384]{1,0:T(8,128)(2,1)} %get-tuple-element.85.refs_2_.refs_1_.refs_3_), custom_call_target="tpu_custom_call" | custom-call | flops 1 | bytes 1 | tf_op jit(solution)/shard_map/pallas_call | solution.py:451
  18.0 4.0 %all-to-all-start.1 = ((bf16[16,16,512]{2,1,0:T(8,128)(2,1)}), bf16[16,16,512]{2,1,0:T(8,128)(2,1)S(1)}, u32[]{:S(2)}, u32[]{:S(2)}) async-start(bf16[16,16,512]{2,1,0:T(8,128)(2,1)} %bitcast.59), calls=%async_computation.1 | async-start | bytes 524288 | tf_op jit(solution)/shard_map/all_to_all | solution.py:505
  22.0 6.3 %shard_map.182 = (bf16[512,128]{1,0:T(8,128)(2,1)}, bf16[512,128]{1,0:T(8,128)(2,1)}, bf16[512,512]{1,0:T(8,128)(2,1)}, bf16[512,512]{1,0:T(8,128)(2,1)}, bf16[5...) custom-call(s32[2,256]{1,0:T(2,128)} %bitcast.64, ...), custom_call_target="tpu_custom_call" | custom-call | flops 1 | bytes 1 | tf_op jit(solution)/shard_map/pallas_call | solution.py:451
  28.3 3.3 %all-to-all-done.1 = bf16[16,16,512]{2,1,0:T(8,128)(2,1)S(1)} async-done(((bf16[16,16,512]{2,1,0:T(8,128)(2,1)}), bf16[16,16,512]{2,1,0:T(8,128)(2,1)S(1)}, u32[]{:S(2)}, u32[]{:S(2)}) %all-to-all-start.1) | async-done | bytes 262176 | tf_op jit(solution)/shard_map/all_to_all | solution.py:505
  31.6 0.7 copy-done.1
  32.3 4.3 %shard_map.183 = (bf16[256,512]{1,0:T(8,128)(2,1)}, bf16[256,512]{1,0:T(8,128)(2,1)}, bf16[256,512]{1,0:T(8,128)(2,1)}, f32[256,512]{1,0:T(8,128)}, f32[256,512]...) custom-call(bf16[256,384]{1,0:T(8,128)(2,1)} %get-tuple-element.84.refs_0_.refs_2_, ...), custom_call_target="tpu_custom_call" | custom-call | flops 1 | bytes 1 | tf_op jit(solution)/shard_map/pallas_call | solution.py:451
  36.6 4.0 %all-to-all-start.2 = ((bf16[16,16,512]{2,1,0:T(8,128)(2,1)}), bf16[16,16,512]{2,1,0:T(8,128)(2,1)S(1)}, u32[]{:S(2)}, u32[]{:S(2)}) async-start(bf16[16,16,512]{2,1,0:T(8,128)(2,1)} %bitcast.56), calls=%async_computation.2 | async-start | bytes 524288 | tf_op jit(solution)/shard_map/all_to_all | solution.py:505
  40.6 2.7 %shard_map.184.refs_8_ = bf16[768,512]{1,0:T(8,128)(2,1)} custom-call(bf16[768,512]{1,0:T(8,128)(2,1)} %refs_3_.6, f32[512,512]{1,0:T(8,128)} %get-tuple-element.91.refs_1_.refs_3_, f32[256,512]{1,0:T(8,128)} %get-tuple-element.92.refs_2_.refs_5_, bf16[256,512]{1,0:T(8,128)(2,1)} %get-tuple-element.89.refs_3_), custom_call_target="tpu_custom_call" | custom-call | flops 1 | bytes 1 | tf_op jit(solution)/shard_map/pallas_call | solution.py:451
  43.2 6.9 %all-to-all-done.2 = bf16[16,16,512]{2,1,0:T(8,128)(2,1)S(1)} async-done(((bf16[16,16,512]{2,1,0:T(8,128)(2,1)}), bf16[16,16,512]{2,1,0:T(8,128)(2,1)S(1)}, u32[]{:S(2)}, u32[]{:S(2)}) %all-to-all-start.2) | async-done | bytes 262176 | tf_op jit(solution)/shard_map/all_to_all | solution.py:505
  50.1 0.7 copy-done.3
  50.8 5.4 %shard_map.185 = (bf16[128,512]{1,0:T(8,128)(2,1)}, f32[128,512]{1,0:T(8,128)}, bf16[128,512]{1,0:T(8,128)(2,1)}, bf16[256,512]{1,0:T(8,128)(2,1)}, bf16[768,512]{1,0:T(8,128)(2,1)}, /*index=5*/bf16[768,512]{1,0:T(8,128)(2,1)}) custom-call(s32[1]{0:T(128)} %bitcast.refs_0_, bf16[256,512]{1,0:T(8,128)(2,1)} %bitcast.55, ...), custom_call_target="tpu_custom_call" | custom-call | flops 1 | bytes 1 | tf_op jit(solution)/shard_map/pallas_call | solution.py:451
  56.2 0.7 collective-permute-start
  56.9 3.6 %all-to-all-start.3 = ((bf16[16,16,512]{2,1,0:T(8,128)(2,1)}), bf16[16,16,512]{2,1,0:T(8,128)(2,1)S(1)}, u32[]{:S(2)}, u32[]{:S(2)}) async-start(bf16[16,16,512]{2,1,0:T(8,128)(2,1)} %bitcast.58), calls=%async_computation.3 | async-start | bytes 524288 | tf_op jit(solution)/shard_map/all_to_all | solution.py:505
  60.5 1.3 add_convert_fusion.1
  61.9 1.2 collective-permute-start.1
  63.1 3.6 %shard_map.186 = (bf16[512,512]{1,0:T(8,128)(2,1)}, bf16[512,512]{1,0:T(8,128)(2,1)}) custom-call(bf16[512,128]{1,0:T(8,128)(2,1)} %get-tuple-element.99.refs_0_.refs_1_, bf16[128,512]{1,0:T(8,128)(2,1)} %get-tuple-element.95.refs_1_.refs_2_, bf16[768,512]{1,0:T(8,128)(2,1)} %refs_0_.3, f32[512,512]{1,0:T(8,128)} %get-tuple-element.91.refs_1_.refs_3_, ...), custom_call_target="tpu_custom_call" | custom-call | flops 1 | bytes 1 | tf_op jit(solution)/shard_map/pallas_call | solution.py:451
  66.7 3.1 %all-to-all-done.3 = bf16[16,16,512]{2,1,0:T(8,128)(2,1)S(1)} async-done(((bf16[16,16,512]{2,1,0:T(8,128)(2,1)}), bf16[16,16,512]{2,1,0:T(8,128)(2,1)S(1)}, u32[]{:S(2)}, u32[]{:S(2)}) %all-to-all-start.3) | async-done | bytes 262176 | tf_op jit(solution)/shard_map/all_to_all | solution.py:505
  69.7 0.7 copy-done
  70.4 5.4 %shard_map.187 = (bf16[256,512]{1,0:T(8,128)(2,1)}, bf16[256,512]{1,0:T(8,128)(2,1)}, bf16[1024,512]{1,0:T(8,128)(2,1)}) custom-call(s32[1]{0:T(128)} %bitcast.refs_0_, bf16[256,384]{1,0:T(8,128)(2,1)} %get-tuple-element.85.refs_2_.refs_1_.refs_3_, bf16[128,512]{1,0:T(8,128)(2,1)} %get-tuple-element.95.refs_1_.refs_2_, bf16[256,512]{1,0:T(8,128)(2,1)} %bitcast.51, ...), custom_call_target="tpu_custom_call" | custom-call | flops 1 | bytes 1 | tf_op jit(solution)/shard_map/pallas_call | solution.py:451
  75.9 0.8 collective-permute-start.2
  76.9 4.7 %shard_map.188.refs_7_ = bf16[1024,512]{1,0:T(8,128)(2,1)} custom-call(s32[1]{0:T(128)} %bitcast.refs_0_, bf16[256,512]{1,0:T(8,128)(2,1)} %get-tuple-element.116.refs_1_, bf16[256,512]{1,0:T(8,128)(2,1)} %get-tuple-element.140.refs_2_.refs_5_, bf16[768,512]{1,0:T(8,128)(2,1)} %refs_3_.6, bf16[512,512]{1,0:T(8,128)(2,1)} %get-tuple-element.106.refs_10_.refs_4_, ...), custom_call_target="tpu_custom_call" | custom-call | flops 1 | bytes 1 | tf_op jit(solution)/shard_map/pallas_call | solution.py:451
  81.6 1.8 %collective-permute-done.3 = bf16[192,512]{1,0:T(8,128)(2,1)S(1)} collective-permute-done((bf16[192,512]{1,0:T(8,128)(2,1)S(1)}, bf16[192,512]{1,0:T(8,128)(2,1)S(1)}, u32[]{:S(2)}, u32[]{:S(2)}) %collective-permute-start.3) | collective-permute-done | bytes 196640 | tf_op jit(solution)/shard_map/ppermute | solution.py:470
  83.4 1.5 add_convert_fusion
  85.1 1.4 collective-permute-start.5
  86.6 3.9 %shard_map.189 = (f32[128,512]{1,0:T(8,128)}, bf16[256,512]{1,0:T(8,128)(2,1)}) custom-call(bf16[512,128]{1,0:T(8,128)(2,1)} %get-tuple-element.127.refs_0_, bf16[512,128]{1,0:T(8,128)(2,1)} %get-tuple-element.99.refs_0_.refs_1_, bf16[256,384]{1,0:T(8,128)(2,1)} %get-tuple-element.84.refs_0_.refs_2_, ...), custom_call_target="tpu_custom_call" | custom-call | flops 1 | bytes 1 | tf_op jit(solution)/shard_map/pallas_call | solution.py:451
  90.5 1.9 %collective-permute-done.5 = bf16[96,512]{1,0:T(8,128)(2,1)S(1)} collective-permute-done((bf16[96,512]{1,0:T(8,128)(2,1)S(1)}, bf16[96,512]{1,0:T(8,128)(2,1)S(1)}, u32[]{:S(2)}, u32[]{:S(2)}) %collective-permute-start.5) | collective-permute-done | bytes 98336 | tf_op jit(solution)/shard_map/ppermute | solution.py:470
  92.3 5.3 %collective-permute-done.4 = bf16[512,512]{1,0:T(8,128)(2,1)S(1)} collective-permute-done((bf16[512,512]{1,0:T(8,128)(2,1)S(1)}, bf16[512,512]{1,0:T(8,128)(2,1)S(1)}, u32[]{:S(2)}, u32[]{:S(2)}) %collective-permute-start.4) | collective-permute-done | bytes 524320 | tf_op jit(solution)/shard_map/ppermute | solution.py:470
  98.0 1.4 collective-permute-start.7
  99.4 4.8 %collective-permute-done.7 = bf16[96,512]{1,0:T(8,128)(2,1)S(1)} collective-permute-done((bf16[96,512]{1,0:T(8,128)(2,1)S(1)}, bf16[96,512]{1,0:T(8,128)(2,1)S(1)}, u32[]{:S(2)}, u32[]{:S(2)}) %collective-permute-start.7) | collective-permute-done | bytes 98336 | tf_op jit(solution)/shard_map/ppermute | solution.py:470
  104.2 3.0 %collective-permute-done.6 = bf16[256,512]{1,0:T(8,128)(2,1)S(1)} collective-permute-done((bf16[256,512]{1,0:T(8,128)(2,1)S(1)}, bf16[256,512]{1,0:T(8,128)(2,1)S(1)}, u32[]{:S(2)}, u32[]{:S(2)}) %collective-permute-start.6) | collective-permute-done | bytes 262176 | tf_op jit(solution)/shard_map/ppermute | solution.py:470
  107.6 3.9 %shard_map.190.refs_4_ = f32[768,512]{1,0:T(8,128)} custom-call(bf16[768,512]{1,0:T(8,128)(2,1)} %refs_0_.3, bf16[512,512]{1,0:T(8,128)(2,1)} %get-tuple-element.139.refs_17_.refs_18_.refs_11_.refs_4_.refs_1_, bf16[256,512]{1,0:T(8,128)(2,1)} %get-tuple-element.140.refs_2_.refs_5_, bf16[1536,512]{1,0:T(8,128)(2,1)} %refs_3_.7, ...), custom_call_target="tpu_custom_call" | custom-call | flops 1 | bytes 1 | tf_op jit(solution)/shard_map/pallas_call | solution.py:451
  111.5 1.3 collective-permute-done.8
  112.8 1.8 %collective-permute-done.9 = bf16[192,512]{1,0:T(8,128)(2,1)S(1)} collective-permute-done((bf16[192,512]{1,0:T(8,128)(2,1)S(1)}, bf16[192,512]{1,0:T(8,128)(2,1)S(1)}, u32[]{:S(2)}, u32[]{:S(2)}) %collective-permute-start.9) | collective-permute-done | bytes 196640 | tf_op jit(solution)/shard_map/ppermute | solution.py:470
  115.1 5.6 %collective-permute-done.10 = bf16[128,512]{1,0:T(8,128)(2,1)S(1)} collective-permute-done((bf16[128,512]{1,0:T(8,128)(2,1)S(1)}, bf16[128,512]{1,0:T(8,128)(2,1)S(1)}, u32[]{:S(2)}, u32[]{:S(2)}) %collective-permute-start.10) | collective-permute-done | bytes 131104 | tf_op jit(solution)/shard_map/ppermute | solution.py:470
  120.8 1.2 collective-permute-done.12
  122.0 5.0 %collective-permute-done.11 = bf16[256,512]{1,0:T(8,128)(2,1)S(1)} collective-permute-done((bf16[256,512]{1,0:T(8,128)(2,1)S(1)}, bf16[256,512]{1,0:T(8,128)(2,1)S(1)}, u32[]{:S(2)}, u32[]{:S(2)}) %collective-permute-start.11) | collective-permute-done | bytes 262176 | tf_op jit(solution)/shard_map/ppermute | solution.py:470
  127.4 4.7 %collective-permute-start.15 = (bf16[768,512]{1,0:T(8,128)(2,1)S(1)}, bf16[768,512]{1,0:T(8,128)(2,1)S(1)}, u32[]{:S(2)}, u32[]{:S(2)}) collective-permute-start(bf16[768,512]{1,0:T(8,128)(2,1)S(1)} %maximum_select_fusion), channel_id=1, source_target_pairs={{0,1},{1,0},{2,3},{3,2},{4,5},{5,4},{6,7},{7,6},{8,9},{9,8},{10,11... | collective-permute-start | bytes 2359304 | tf_op jit(solution)/shard_map/ppermute | solution.py:470
  132.8 3.5 %all-to-all-start.4 = ((bf16[16,16,512]{2,1,0:T(8,128)(2,1)}), bf16[16,16,512]{2,1,0:T(8,128)(2,1)S(1)}, u32[]{:S(2)}, u32[]{:S(2)}) async-start(bf16[16,16,512]{2,1,0:T(8,128)(2,1)} %bitcast.32), calls=%async_computation.4 | async-start | bytes 524288 | tf_op jit(solution)/shard_map/all_to_all | solution.py:505
  136.5 0.8 slice.9
  137.3 1.0 pad_maximum_fusion.1
  138.4 10.5 %all-to-all-done.4 = bf16[16,16,512]{2,1,0:T(8,128)(2,1)S(1)} async-done(((bf16[16,16,512]{2,1,0:T(8,128)(2,1)}), bf16[16,16,512]{2,1,0:T(8,128)(2,1)S(1)}, u32[]{:S(2)}, u32[]{:S(2)}) %all-to-all-start.4) | async-done | bytes 262176 | tf_op jit(solution)/shard_map/all_to_all | solution.py:505
  149.6 2.0 %shard_map.191 = f32[128,512]{1,0:T(8,128)} custom-call(f32[128,512]{1,0:T(8,128)} %get-tuple-element.94.refs_0_, f32[128,512]{1,0:T(8,128)} %get-tuple-element.129.refs_1_, bf16[256,128]{1,0:T(8,128)(2,1)} %get-tuple-element.87.refs_5_.refs_2_, bf16[256,512]{1,0:T(8,128)(2,1)} %bitcast.54, f32[768,512]{1,0:T(8,128)} %shard_map.190.refs_4_), custom_call_target="tpu_custom_call" | custom-call | flops 1 | bytes 1 | tf_op jit(solution)/shard_map/pallas_call | solution.py:451
  151.6 1.0 broadcast_select_fusion.6
  152.6 1.2 pad_maximum_fusion
  (44 shorter events, 4.3 us)
Async XLA Ops:
  2.3 13.0 %all-to-all-start = ((s32[16,1,16]{2,1,0:T(1,128)}), s32[16,1,16]{2,1,0:T(1,128)S(1)}, u32[]{:S(2)}, u32[]{:S(2)}) async-start(s32[16,1,16]{2,1,0:T(1,128)} %bitcast.60), calls=%async_computation | async-start | bytes 16384 | tf_op jit(solution)/shard_map/all_to_all | solution.py:535
  15.4 0.6 copy-start.4
  18.0 13.6 %all-to-all-start.1 = ((bf16[16,16,512]{2,1,0:T(8,128)(2,1)}), bf16[16,16,512]{2,1,0:T(8,128)(2,1)S(1)}, u32[]{:S(2)}, u32[]{:S(2)}) async-start(bf16[16,16,512]{2,1,0:T(8,128)(2,1)} %bitcast.59), calls=%async_computation.1 | async-start | bytes 524288 | tf_op jit(solution)/shard_map/all_to_all | solution.py:505
  31.6 0.7 copy-start.1
  36.6 13.5 %all-to-all-start.2 = ((bf16[16,16,512]{2,1,0:T(8,128)(2,1)}), bf16[16,16,512]{2,1,0:T(8,128)(2,1)S(1)}, u32[]{:S(2)}, u32[]{:S(2)}) async-start(bf16[16,16,512]{2,1,0:T(8,128)(2,1)} %bitcast.56), calls=%async_computation.2 | async-start | bytes 524288 | tf_op jit(solution)/shard_map/all_to_all | solution.py:505
  50.1 0.7 copy-start.3
  56.2 4.3 %collective-permute-start = (bf16[768,512]{1,0:T(8,128)(2,1)}, bf16[768,512]{1,0:T(8,128)(2,1)S(1)}, u32[]{:S(2)}, u32[]{:S(2)}) collective-permute-start(bf16[768,512]{1,0:T(8,128)(2,1)} %get-tuple-element.98.refs_7_), channel_id=1, source_target_pairs={{0,1},{1,0},{2,3},{3,2},{4,5},{5,4},{6,7},{7,6},{8,9},{9,8},{10,11... | collective-permute-start | bytes 2359304 | tf_op jit(solution)/shard_map/ppermute | solution.py:470
  56.9 12.9 %all-to-all-start.3 = ((bf16[16,16,512]{2,1,0:T(8,128)(2,1)}), bf16[16,16,512]{2,1,0:T(8,128)(2,1)S(1)}, u32[]{:S(2)}, u32[]{:S(2)}) async-start(bf16[16,16,512]{2,1,0:T(8,128)(2,1)} %bitcast.58), calls=%async_computation.3 | async-start | bytes 524288 | tf_op jit(solution)/shard_map/all_to_all | solution.py:505
  61.9 14.0 %collective-permute-start.1 = (bf16[384,512]{1,0:T(8,128)(2,1)S(1)}, bf16[384,512]{1,0:T(8,128)(2,1)S(1)}, u32[]{:S(2)}, u32[]{:S(2)}) collective-permute-start(bf16[384,512]{1,0:T(8,128)(2,1)S(1)} %get-tuple-element.168), channel_id=1, source_target_pairs={{0,2},{1,3},{2,0},{3,1},{4,6},{5,7},{6,4},{7,5},{8,10},{9,11},{10,... | collective-permute-start | bytes 1179656 | tf_op jit(solution)/shard_map/ppermute | solution.py:470
  69.7 0.7 copy-start
  75.9 7.5 %collective-permute-start.2 = (bf16[1024,512]{1,0:T(8,128)(2,1)}, bf16[1024,512]{1,0:T(8,128)(2,1)S(1)}, u32[]{:S(2)}, u32[]{:S(2)}) collective-permute-start(bf16[1024,512]{1,0:T(8,128)(2,1)} %get-tuple-element.118.refs_12_), channel_id=1, source_target_pairs={{0,1},{1,0},{2,3},{3,2},{4,5},{5,4},{6,7},{7,6},{8,9},{9,8},{10,11... | collective-permute-start | bytes 3145736 | tf_op jit(solution)/shard_map/ppermute | solution.py:470
  76.8 6.6 %collective-permute-start.3 = (bf16[192,512]{1,0:T(8,128)(2,1)S(1)}, bf16[192,512]{1,0:T(8,128)(2,1)S(1)}, u32[]{:S(2)}, u32[]{:S(2)}) collective-permute-start(bf16[192,512]{1,0:T(8,128)(2,1)S(1)} %get-tuple-element.172), channel_id=1, source_target_pairs={{0,4},{1,5},{2,6},{3,7},{4,0},{5,1},{6,2},{7,3},{8,12},{9,13},{10,... | collective-permute-start | bytes 589832 | tf_op jit(solution)/shard_map/ppermute | solution.py:470
  85.0 12.7 %collective-permute-start.4 = (bf16[512,512]{1,0:T(8,128)(2,1)S(1)}, bf16[512,512]{1,0:T(8,128)(2,1)S(1)}, u32[]{:S(2)}, u32[]{:S(2)}) collective-permute-start(bf16[512,512]{1,0:T(8,128)(2,1)S(1)} %get-tuple-element.166), channel_id=1, source_target_pairs={{0,2},{1,3},{2,0},{3,1},{4,6},{5,7},{6,4},{7,5},{8,10},{9,11},{10,... | collective-permute-start | bytes 1572872 | tf_op jit(solution)/shard_map/ppermute | solution.py:470
  85.1 7.2 %collective-permute-start.5 = (bf16[96,512]{1,0:T(8,128)(2,1)S(1)}, bf16[96,512]{1,0:T(8,128)(2,1)S(1)}, u32[]{:S(2)}, u32[]{:S(2)}) collective-permute-start(bf16[96,512]{1,0:T(8,128)(2,1)S(1)} %get-tuple-element.176), channel_id=1, source_target_pairs={{0,8},{1,9},{2,10},{3,11},{4,12},{5,13},{6,14},{7,15},{8,0},{9,1},... | collective-permute-start | bytes 294920 | tf_op jit(solution)/shard_map/ppermute | solution.py:470
  97.9 9.3 %collective-permute-start.6 = (bf16[256,512]{1,0:T(8,128)(2,1)S(1)}, bf16[256,512]{1,0:T(8,128)(2,1)S(1)}, u32[]{:S(2)}, u32[]{:S(2)}) collective-permute-start(bf16[256,512]{1,0:T(8,128)(2,1)S(1)} %get-tuple-element.170), channel_id=1, source_target_pairs={{0,4},{1,5},{2,6},{3,7},{4,0},{5,1},{6,2},{7,3},{8,12},{9,13},{10,... | collective-permute-start | bytes 786440 | tf_op jit(solution)/shard_map/ppermute | solution.py:470
  98.0 6.2 %collective-permute-start.7 = (bf16[96,512]{1,0:T(8,128)(2,1)S(1)}, bf16[96,512]{1,0:T(8,128)(2,1)S(1)}, u32[]{:S(2)}, u32[]{:S(2)}) collective-permute-start(bf16[96,512]{1,0:T(8,128)(2,1)S(1)} %add_convert_fusion.7), channel_id=1, source_target_pairs={{0,8},{1,9},{2,10},{3,11},{4,12},{5,13},{6,14},{7,15},{8,0},{9,1},... | collective-permute-start | bytes 294920 | tf_op jit(solution)/shard_map/ppermute | solution.py:470
  107.2 7.4 %collective-permute-start.9 = (bf16[192,512]{1,0:T(8,128)(2,1)S(1)}, bf16[192,512]{1,0:T(8,128)(2,1)S(1)}, u32[]{:S(2)}, u32[]{:S(2)}) collective-permute-start(bf16[192,512]{1,0:T(8,128)(2,1)S(1)} %maximum_select_fusion.4), channel_id=1, source_target_pairs={{0,4},{1,5},{2,6},{3,7},{4,0},{5,1},{6,2},{7,3},{8,12},{9,13},{10,... | collective-permute-start | bytes 589832 | tf_op jit(solution)/shard_map/ppermute | solution.py:470
  107.4 5.4 %collective-permute-start.8 = (bf16[128,512]{1,0:T(8,128)(2,1)S(1)}, bf16[128,512]{1,0:T(8,128)(2,1)S(1)}, u32[]{:S(2)}, u32[]{:S(2)}) collective-permute-start(bf16[128,512]{1,0:T(8,128)(2,1)S(1)} %get-tuple-element.174), channel_id=1, source_target_pairs={{0,8},{1,9},{2,10},{3,11},{4,12},{5,13},{6,14},{7,15},{8,0},{9,1},... | collective-permute-start | bytes 393224 | tf_op jit(solution)/shard_map/ppermute | solution.py:470
  114.7 6.0 %collective-permute-start.10 = (bf16[128,512]{1,0:T(8,128)(2,1)S(1)}, bf16[128,512]{1,0:T(8,128)(2,1)S(1)}, u32[]{:S(2)}, u32[]{:S(2)}) collective-permute-start(bf16[128,512]{1,0:T(8,128)(2,1)S(1)} %add_convert_fusion.6), channel_id=1, source_target_pairs={{0,8},{1,9},{2,10},{3,11},{4,12},{5,13},{6,14},{7,15},{8,0},{9,1},... | collective-permute-start | bytes 393224 | tf_op jit(solution)/shard_map/ppermute | solution.py:470
  115.0 7.0 %collective-permute-start.12 = (bf16[384,512]{1,0:T(8,128)(2,1)S(1)}, bf16[384,512]{1,0:T(8,128)(2,1)S(1)}, u32[]{:S(2)}, u32[]{:S(2)}) collective-permute-start(bf16[384,512]{1,0:T(8,128)(2,1)S(1)} %maximum_select_fusion.2), channel_id=1, source_target_pairs={{0,2},{1,3},{2,0},{3,1},{4,6},{5,7},{6,4},{7,5},{8,10},{9,11},{10,... | collective-permute-start | bytes 1179656 | tf_op jit(solution)/shard_map/ppermute | solution.py:470
  120.7 6.3 %collective-permute-start.11 = (bf16[256,512]{1,0:T(8,128)(2,1)S(1)}, bf16[256,512]{1,0:T(8,128)(2,1)S(1)}, u32[]{:S(2)}, u32[]{:S(2)}) collective-permute-start(bf16[256,512]{1,0:T(8,128)(2,1)S(1)} %maximum_select_fusion.3), channel_id=1, source_target_pairs={{0,4},{1,5},{2,6},{3,7},{4,0},{5,1},{6,2},{7,3},{8,12},{9,13},{10,... | collective-permute-start | bytes 786440 | tf_op jit(solution)/shard_map/ppermute | solution.py:470
  127.4 9.0 %collective-permute-start.15 = (bf16[768,512]{1,0:T(8,128)(2,1)S(1)}, bf16[768,512]{1,0:T(8,128)(2,1)S(1)}, u32[]{:S(2)}, u32[]{:S(2)}) collective-permute-start(bf16[768,512]{1,0:T(8,128)(2,1)S(1)} %maximum_select_fusion), channel_id=1, source_target_pairs={{0,1},{1,0},{2,3},{3,2},{4,5},{5,4},{6,7},{7,6},{8,9},{9,8},{10,11... | collective-permute-start | bytes 2359304 | tf_op jit(solution)/shard_map/ppermute | solution.py:470
  132.2 16.6 %collective-permute-start.13 = (bf16[512,512]{1,0:T(8,128)(2,1)S(1)}, bf16[512,512]{1,0:T(8,128)(2,1)S(1)}, u32[]{:S(2)}, u32[]{:S(2)}) collective-permute-start(bf16[512,512]{1,0:T(8,128)(2,1)S(1)} %maximum_select_fusion.1), channel_id=1, source_target_pairs={{0,2},{1,3},{2,0},{3,1},{4,6},{5,7},{6,4},{7,5},{8,10},{9,11},{10,... | collective-permute-start | bytes 1572872 | tf_op jit(solution)/shard_map/ppermute | solution.py:470
  132.5 16.4 %collective-permute-start.14 = (bf16[512,512]{1,0:T(8,128)(2,1)S(1)}, bf16[512,512]{1,0:T(8,128)(2,1)S(1)}, u32[]{:S(2)}, u32[]{:S(2)}) collective-permute-start(bf16[512,512]{1,0:T(8,128)(2,1)S(1)} %maximum_select_fusion.1), channel_id=1, source_target_pairs={{0,1},{1,0},{2,3},{3,2},{4,5},{5,4},{6,7},{7,6},{8,9},{9,8},{10,11... | collective-permute-start | bytes 1572872 | tf_op jit(solution)/shard_map/ppermute | solution.py:470
  132.8 16.1 %all-to-all-start.4 = ((bf16[16,16,512]{2,1,0:T(8,128)(2,1)}), bf16[16,16,512]{2,1,0:T(8,128)(2,1)S(1)}, u32[]{:S(2)}, u32[]{:S(2)}) async-start(bf16[16,16,512]{2,1,0:T(8,128)(2,1)} %bitcast.32), calls=%async_computation.4 | async-start | bytes 524288 | tf_op jit(solution)/shard_map/all_to_all | solution.py:505
  148.9 0.7 copy-start.2
  148.9 2.7 %collective-permute-start.16 = (bf16[512,512]{1,0:T(8,128)(2,1)S(1)}, bf16[512,512]{1,0:T(8,128)(2,1)S(1)}, u32[]{:S(2)}, u32[]{:S(2)}) collective-permute-start(bf16[512,512]{1,0:T(8,128)(2,1)S(1)} %collective-permute-done.13), channel_id=1, source_target_pairs={{0,1},{1,0},{2,3},{3,2},{4,5},{5,4},{6,7},{7,6},{8,9},{9,8},{10,11... | collective-permute-start | bytes 1572872 | tf_op jit(solution)/shard_map/ppermute | solution.py:470

commit v7 on v6

--- a/solution.py
+++ b/solution.py
@@ -220,6 +220,21 @@
 
     out_ref[:inner_rows] = added(edges_ref[:inner_rows], inner_ref[...])
     out_ref[inner_rows:] = added(edges_ref[inner_rows:], cut_ref[...])
+
+
+def turn_kernel(*refs):
+    edges_ref, inner_refs, cut_refs, out_ref = refs[0], refs[1:4], refs[4:7], refs[7]
+    latent = edges_ref.shape[1]
+    inner_rows = inner_refs[0].shape[0]
+
+    def put(index, inner, cut):
+        rows = pl.ds(index % 2 * latent, latent)
+        out_ref[index // 2, rows, :inner_rows] = inner.T
+        out_ref[index // 2, rows, inner_rows:] = cut.T
+
+    put(0, edges_ref[:inner_rows], edges_ref[inner_rows:])
+    for index in range(3):
+        put(index + 1, inner_refs[index][...], cut_refs[index][...])
 
 
 def node_kernel(
@@ -298,42 +313,37 @@
     grad_pre_ref[...] = grad_pre
 
 
-def fetch_factors(half, sources, buffers, sems, wait):
-    edges, inner_sender, cut_sender, inner_receiver, cut_receiver = sources[:5]
-    inner_hidden, cut_hidden, inner_out, inner_pre = sources[5:]
-    inner_rows, cut_rows = inner_pre.shape[0], cut_sender.shape[0]
-    inner_edges = edges.at[pl.ds(0, inner_rows)]
-    cut_edges = edges.at[pl.ds(inner_rows, cut_rows)]
-    low = [inner_edges, cut_edges, inner_sender, cut_sender, inner_pre, inner_pre]
-    high = [inner_receiver, cut_receiver, inner_hidden, cut_hidden, inner_pre, inner_out]
-
-    def each(parts):
-        for index, (source, buffer) in enumerate(zip(parts, buffers)):
-            copy = pltpu.make_async_copy(source, buffer, sems.at[index])
-            if wait:
-                copy.wait()
-            else:
-                copy.start()
+def fetch(half, sources, buffers, sems):
+    lefts, inner_pre, inner_out = sources
+    left, pre, out = buffers
+    rows = pl.ds(0, inner_pre.shape[0])
+    copies = [
+        pltpu.make_async_copy(lefts.at[half], left, sems.at[0]),
+        pltpu.make_async_copy(inner_pre, pre.at[rows], sems.at[1]),
+        pltpu.make_async_copy(inner_out, out.at[rows], sems.at[2]),
+    ]
+    for copy in copies:
+        copy.start()
+    return copies
+
+
+def weight_rows(half, copies, buffers, cut_pre, cut_out, put):
+    left, pre, out = buffers
+    latent = pre.shape[1]
+    rows = pl.ds(pre.shape[0] - cut_pre.shape[0], cut_pre.shape[0])
+    pre[rows] = cut_pre
+    out[rows] = cut_out
+    for copy in copies:
+        copy.wait()
+    put(0, dot(left[:latent], pre[...]))
 
     @pl.when(half == 0)
     def _():
-        each(low)
+        put(1, dot(left[latent:], pre[...]))
 
     @pl.when(half != 0)
     def _():
-        each(high)
-
-
-def edge_rows(half, buffers, cut_pre, cut_out, out_ref):
-    latent = cut_pre.shape[1]
-    first, first_cut, second, second_cut, first_right, second_right = buffers
-    chosen = jnp.where(half == 0, cut_pre.astype(F32), cut_out.astype(F32)).astype(BF16)
-    out_ref[:latent] = (
-        dot_rows(first[...], first_right[...]) + dot_rows(first_cut[...], cut_pre)
-    ).astype(BF16)
-    out_ref[latent:] = (
-        dot_rows(second[...], second_right[...]) + dot_rows(second_cut[...], chosen)
-    ).astype(BF16)
+        put(1, dot(left[latent:], out[...]))
 
 
 def cut_backward_kernel(
@@ -346,12 +356,18 @@
     scale_ref,
     slope_ref,
     w_out_ref,
-    *refs,
+    lefts_ref,
+    inner_pre_ref,
+    inner_out_ref,
+    grad_out_ref,
+    grad_pre_ref,
+    out_ref,
+    *rest,
 ):
-    sources, (grad_out_ref, grad_pre_ref, out_ref), rest = refs[:9], refs[9:12], refs[12:]
     buffers, sems = rest[:-1], rest[-1]
+    latent = w_out_ref.shape[1]
     half = 1 - (me_ref[0] & 1)
-    fetch_factors(half, sources, buffers, sems, False)
+    copies = fetch(half, (lefts_ref, inner_pre_ref, inner_out_ref), buffers, sems)
     base = agg_grad_ref.shape[0]
     target = dot(receivers_ref[:, :base], agg_grad_ref[...]) + dot(
         receivers_ref[:, base:], far_grad_ref[...]
@@ -361,17 +377,43 @@
     )
     grad_out_ref[...] = grad_out
     grad_pre_ref[...] = grad_pre
-    fetch_factors(half, sources, buffers, sems, True)
-    edge_rows(half, buffers, grad_pre, grad_out, out_ref)
-
-
-def edge_weights_kernel(me_ref, cut_out_ref, cut_pre_ref, *refs):
-    sources, out_ref, rest = refs[:9], refs[9], refs[10:]
+
+    def put(index, value):
+        out_ref[pl.ds(index * latent, latent)] = value.astype(BF16)
+
+    weight_rows(half, copies, buffers, grad_pre, grad_out, put)
+
+
+def edge_weights_kernel(
+    me_ref,
+    received_ref,
+    cut_pre_ref,
+    cut_out_ref,
+    lefts_ref,
+    inner_pre_ref,
+    inner_out_ref,
+    own_ref,
+    sent_ref,
+    *rest,
+):
     buffers, sems = rest[:-1], rest[-1]
+    latent = own_ref.shape[1]
     half = me_ref[0] & 1
-    fetch_factors(half, sources, buffers, sems, False)
-    fetch_factors(half, sources, buffers, sems, True)
-    edge_rows(half, buffers, cut_pre_ref[...], cut_out_ref[...], out_ref)
+    copies = fetch(half, (lefts_ref, inner_pre_ref, inner_out_ref), buffers, sems)
+    place = (me_ref[0] >> 1) & 1
+
+    def put(index, value):
+        total = (value + received_ref[pl.ds(index * latent, latent)].astype(F32)).astype(BF16)
+
+        @pl.when(place == index)
+        def _():
+            own_ref[...] = total
+
+        @pl.when(place != index)
+        def _():
+            sent_ref[...] = total
+
+    weight_rows(half, copies, buffers, cut_pre_ref[...], cut_out_ref[...], put)
 
 
 def input_grads_kernel(
@@ -629,6 +671,19 @@
         shaped(BF16, *edges.shape),
         [edges, inner_normed, cut_normed],
     )
+    lefts = line.run(
+        turn_kernel,
+        shaped(BF16, 2, 2 * latent, inner_rows + cut_rows),
+        [
+            edges,
+            inner_sender,
+            inner_receiver,
+            inner_hidden,
+            cut_sender,
+            cut_receiver,
+            cut_hidden,
+        ],
+    )
     (
         new_nodes,
         self_grad,
@@ -677,20 +732,13 @@
     bits = index_bits(domains)
     node_parts = traded(node_sum, domains, 1)
     far_grad, node_sum, inner_pre = fence(far_grad, node_sum, inner_pre)
-    factors = [
-        edges,
-        inner_sender,
-        cut_sender,
-        inner_receiver,
-        cut_receiver,
-        inner_hidden,
-        cut_hidden,
-        inner_out,
-        inner_pre,
+    buffers = [
+        pltpu.VMEM((2 * latent, inner_rows + cut_rows), BF16),
+        pltpu.VMEM((inner_rows + cut_rows, latent), BF16),
+        pltpu.VMEM((inner_rows + cut_rows, latent), BF16),
+        pltpu.SemaphoreType.DMA((3,)),
     ]
-    buffers = [pltpu.VMEM((rows, latent), BF16) for rows in (inner_rows, cut_rows) * 2]
-    buffers += [pltpu.VMEM((inner_rows, latent), BF16)] * 2
-    buffers.append(pltpu.SemaphoreType.DMA((len(buffers),)))
+    factors = [lefts, inner_pre, inner_out]
     cut_out, cut_pre, edge_send = line.run(
         cut_backward_kernel,
         [shaped(BF16, cut_rows, latent)] * 2 + [shaped(BF16, 2 * latent, latent)],
@@ -723,19 +771,9 @@
         buffers,
     )
     edge_send, place, *node_parts = fence(edge_send, me, *node_parts)
-    edge_keep = line.run(
-        edge_weights_kernel,
-        shaped(BF16, 2 * latent, latent),
-        [place, cut_out, cut_pre] + factors,
-        [SMEM, VMEM, VMEM] + [ANY] * len(factors),
-        scratch=buffers,
-    )
-    edge_parts = [edge_keep, across(edge_send, domains, 1)]
+    received = across(edge_send, domains, 1)
     node_parts = traded(added(*node_parts), domains, 2)
-    fenced = fence(*edge_parts, *node_parts, inner_pre, cut_pre)
-    edge_sum, node_sum, (inner_pre, cut_pre) = added(*fenced[:2]), added(*fenced[2:4]), fenced[4:]
-    edge_parts = traded(edge_sum, domains, 1)
-    node_parts = traded(node_sum, domains, 3)
+    cut_pre = fence(cut_pre, edge_send)[0]
     local_grad, outgoing_grad = line.run(
         input_grads_kernel,
         [shaped(F32, node_rows, latent), shaped(BF16, total_slots, latent)],
@@ -749,19 +787,22 @@
             w_edge_in,
         ],
     )
-    fenced = fence(*edge_parts, *node_parts, inner_pre, cut_pre, local_grad)
-    edge_sum, node_sum = added(*fenced[:2]), added(*fenced[2:4])
-    inner_pre, cut_pre, local_grad = fenced[4:]
+    edge_own, edge_sent = line.run(
+        edge_weights_kernel,
+        [shaped(BF16, latent, latent)] * 2,
+        [place, received, cut_pre, cut_out] + factors,
+        [SMEM, VMEM, VMEM, VMEM] + [ANY] * len(factors),
+        scratch=buffers,
+    )
+    edge_own, edge_sent, *node_parts, outgoing_grad, inner_pre, cut_pre = fence(
+        edge_own, edge_sent, *node_parts, outgoing_grad, inner_pre, cut_pre
+    )
+    edge_got = across(edge_sent, domains, 2)
+    node_sum = added(*node_parts)
+    node_sum = added(*handed(node_sum, domains, 3))
     for bit in bits[4:]:
-        node_sum = added(*traded(node_sum, domains, bit))
-    for bit in bits[:3:-1]:
-        node_sum = joined(handed(node_sum, domains, bit), bit)
-    edge_parts = traded(edge_sum, domains, 2)
-    node_parts = handed(node_sum, domains, 3)
-    fenced = fence(*edge_parts, *node_parts, inner_pre)
-    edge_sum, node_sum, inner_pre = added(*fenced[:2]), joined(fenced[2:4], 3), fenced[4]
-    edge_parts = traded(edge_sum, domains, 3)
-    node_parts = handed(node_sum, domains, 2)
+        node_sum = added(*handed(node_sum, domains, bit))
+    returned = exchange(outgoing_grad, domains)
     grad_edges = line.run(
         functools.partial(edge_grads_kernel, blocks=blocks),
         shaped(F32, *edges.shape),
@@ -775,37 +816,43 @@
         [rows_spec(latent)],
         (blocks + 1,),
     )
-    fenced = fence(*edge_parts, *node_parts, grad_edges)
-    edge_sum, node_sum, grad_edges = added(*fenced[:2]), joined(fenced[2:4], 2), fenced[4]
+    edge_own, edge_got, node_sum, grad_edges, returned = fence(
+        edge_own, edge_got, node_sum, grad_edges, returned
+    )
+    edge_sum = added(edge_own, edge_got)
+    edge_parts = traded(edge_sum, domains, 2)
+    node_parts = handed(node_sum, domains, 2)
+    fenced = fence(*edge_parts, *node_parts)
+    edge_sum, node_sum = added(*fenced[:2]), joined(fenced[2:4], 2)
+    edge_parts = traded(edge_sum, domains, 3)
+    node_parts = handed(node_sum, domains, 1)
+    grad_nodes = line.run(
+        node_grads_kernel,
+        shaped(F32, node_rows, latent),
+        [self_grad, local_grad, asked_marks, returned],
+    )
+    *edge_parts, grad_nodes = fence(*edge_parts, grad_nodes)
+    edge_sum = added(*edge_parts)
     for bit in bits[4:]:
         edge_sum = added(*traded(edge_sum, domains, bit))
     for bit in bits[:3:-1]:
         edge_sum = joined(handed(edge_sum, domains, bit), bit)
-    node_parts = handed(node_sum, domains, 1)
-    edge_parts = fence(*handed(edge_sum, domains, 3))
+    *edge_parts, node_sum, other_sum = fence(*handed(edge_sum, domains, 3), *node_parts)
+    node_sum = joined([node_sum, other_sum], 1)
+    others = across(node_sum, domains, 1)
     edge_parts = handed(joined(edge_parts, 3), domains, 2)
-    *edge_parts, node_sum, other_sum, outgoing_grad = fence(
-        *edge_parts, *node_parts, outgoing_grad
-    )
-    node_sum = joined([node_sum, other_sum], 1)
+    *edge_parts, node_sum, others = fence(*edge_parts, node_sum, others)
     edge_sum = joined(edge_parts, 2)
     edge_parts = handed(edge_sum, domains, 1) + [across(edge_sum, domains, 1)]
-    others = across(node_sum, domains, 1)
-    returned = exchange(outgoing_grad, domains)
     lower, left = place_of(0) == 0, place_of(1) == 0
     low_rows, high_rows = jnp.where(lower, node_sum, others), jnp.where(lower, others, node_sum)
     split = 2 * latent - low_rows.shape[0]
     grad_node_in = jnp.concatenate([low_rows, high_rows[:split]])
     grad_node_out = high_rows[split:]
-    mine, far, near, grad_node_in, grad_node_out, returned = fence(
-        *edge_parts, grad_node_in, grad_node_out, returned
+    mine, far, near, grad_node_in, grad_node_out = fence(
+        *edge_parts, grad_node_in, grad_node_out
     )
     corner = across(far, domains, 1)
-    grad_nodes = line.run(
-        node_grads_kernel,
-        shaped(F32, node_rows, latent),
-        [self_grad, local_grad, asked_marks, returned],
-    )
     own, other = [mine, far], [near, corner]
     low_half = [jnp.where(lower, one, two) for one, two in zip(own, other)]
     high_half = [jnp.where(lower, two, one) for one, two in zip(own, other)]

time: 155 us -> 167 us (1.077)
  Pallas kernels: 48 us -> 53 us
  waiting for transfers between devices: 59 us -> 63.7 us
  starting transfers between devices: 34.5 us -> 37.8 us
    ppermute x17 -> x16, waiting for transfers between devices: 31.6 us -> 51.2 us  [across(): lax.ppermute(rows, 'dom', [(device, device ^ mask) for device in range(de...]
    all_to_all x4, waiting for transfers between devices: 23.7 us -> 8.9 us  [exchange(): lax.all_to_all(split, 'dom', split_axis=0, concat_axis=0, tiled=True)]
    pallas_call x13 -> x14, Pallas kernels: 48 us -> 53 us  [run(): pl.pallas_call(ordered, out_shape=out_shape, in_specs=specs, out_specs=[V...]
    ppermute x17 -> x16, starting transfers between devices: 12 us -> 14.4 us  [across(): lax.ppermute(rows, 'dom', [(device, device ^ mask) for device in range(de...]
    unnamed x10 -> x14, local copies, waits for them, and re-layouts: 2.94 us -> 3.68 us
  transfers between devices with their start and end apart: 22 -> 21, of which waited for: 15 -> 11; matrix products, arithmetic and copies ran while one was open for 3% -> 2% of each run, Pallas kernels for 22% -> 24%
where the time goes in v7:
time: 167 us; the launch traced here: 166 us
  waiting for transfers between devices  63.7 us (38%)
  Pallas kernels  53 us (32%)
  starting transfers between devices  37.8 us (23%)
  other arithmetic  5.86 us (4%)
  local copies, waits for them, and re-layouts  4.7 us (3%)
    pallas_call x14, Pallas kernels, run(): pl.pallas_call(ordered, out_shape=out_shape, in_specs=specs, out_specs=[V...  53 us
    ppermute x16, waiting for transfers between devices, across(): lax.ppermute(rows, 'dom', [(device, device ^ mask) for device in range(de...  51.2 us
    all_to_all x4, starting transfers between devices, exchange(): lax.all_to_all(split, 'dom', split_axis=0, concat_axis=0, tiled=True)  16.1 us
    ppermute x16, starting transfers between devices, across(): lax.ppermute(rows, 'dom', [(device, device ^ mask) for device in range(de...  14.4 us
    all_to_all x4, waiting for transfers between devices, exchange(): lax.all_to_all(split, 'dom', split_axis=0, concat_axis=0, tiled=True)  8.9 us
    all_to_all x1, starting transfers between devices, shards(): asked = lax.all_to_all(ask, 'dom', split_axis=0, concat_axis=0, tiled=True)  7.32 us
    unnamed x14, local copies, waits for them, and re-layouts  3.68 us
    all_to_all x1, waiting for transfers between devices, shards(): asked = lax.all_to_all(ask, 'dom', split_axis=0, concat_axis=0, tiled=True)  3.68 us
  transfers between devices with their start and end apart: 21, of which 11 were waited for; matrix products, arithmetic and copies ran while one was open for 2% of the time, Pallas kernels for 24%

profile of v7, /device:TPU:1, one launch (start us, length us, event | category | flops | bytes accessed | tf_op | source)
XLA Modules:
  0.0 166.1 jit_solution(694879307300546428)
XLA Ops:
  0.6 1.7 %shard_map.179.refs_2_ = s32[16,16]{1,0:T(8,128)} custom-call(s32[1,128]{1,0:T(1,128)} %bitcast.50, s32[1,128]{1,0:T(1,128)} %bitcast.53), custom_call_target="tpu_custom_call" | custom-call | flops 1 | bytes 1 | tf_op jit(solution)/shard_map/pallas_call | solution.py:493
  2.3 7.3 %all-to-all-start = ((s32[16,1,16]{2,1,0:T(1,128)}), s32[16,1,16]{2,1,0:T(1,128)S(1)}, u32[]{:S(2)}, u32[]{:S(2)}) async-start(s32[16,1,16]{2,1,0:T(1,128)} %bitcast.48), calls=%async_computation | async-start | bytes 16384 | tf_op jit(solution)/shard_map/all_to_all | solution.py:577
  9.7 2.0 %shard_map.180 = (bf16[256,384]{1,0:T(8,128)(2,1)}, bf16[256,384]{1,0:T(8,128)(2,1)}) custom-call(s32[1,128]{1,0:T(1,128)} %bitcast.51, s32[1,128]{1,0:T(1,128)} %bitcast.54, s32[16,16]{1,0:T(8,128)} %shard_map.179.refs_2_), custom_call_target="tpu_custom_call" | custom-call | flops 1 | bytes 1 | tf_op jit(solution)/shard_map/pallas_call | solution.py:493
  11.7 3.7 %all-to-all-done = s32[16,1,16]{2,1,0:T(1,128)S(1)} async-done(((s32[16,1,16]{2,1,0:T(1,128)}), s32[16,1,16]{2,1,0:T(1,128)S(1)}, u32[]{:S(2)}, u32[]{:S(2)}) %all-to-all-start) | async-done | bytes 1056 | tf_op jit(solution)/shard_map/all_to_all | solution.py:577
  16.0 2.0 %shard_map.181 = (bf16[256,512]{1,0:T(8,128)(2,1)}, bf16[256,128]{1,0:T(8,128)(2,1)}) custom-call(s32[16,16]{1,0:T(8,128)} %bitcast.49, bf16[128,512]{1,0:T(8,128)(2,1)} %refs_4_.4, bf16[256,384]{1,0:T(8,128)(2,1)} %get-tuple-element.84.refs_2_.refs_1_.refs_3_), custom_call_target="tpu_custom_call" | custom-call | flops 1 | bytes 1 | tf_op jit(solution)/shard_map/pallas_call | solution.py:493
  18.0 4.0 %all-to-all-start.1 = ((bf16[16,16,512]{2,1,0:T(8,128)(2,1)}), bf16[16,16,512]{2,1,0:T(8,128)(2,1)S(1)}, u32[]{:S(2)}, u32[]{:S(2)}) async-start(bf16[16,16,512]{2,1,0:T(8,128)(2,1)} %bitcast.47), calls=%async_computation.1 | async-start | bytes 524288 | tf_op jit(solution)/shard_map/all_to_all | solution.py:547
  22.0 6.3 %shard_map.182 = (bf16[512,128]{1,0:T(8,128)(2,1)}, bf16[512,128]{1,0:T(8,128)(2,1)}, bf16[512,512]{1,0:T(8,128)(2,1)}, bf16[512,512]{1,0:T(8,128)(2,1)}, bf16[5...) custom-call(s32[2,256]{1,0:T(2,128)} %bitcast.52, ...), custom_call_target="tpu_custom_call" | custom-call | flops 1 | bytes 1 | tf_op jit(solution)/shard_map/pallas_call | solution.py:493
  28.3 3.3 %all-to-all-done.1 = bf16[16,16,512]{2,1,0:T(8,128)(2,1)S(1)} async-done(((bf16[16,16,512]{2,1,0:T(8,128)(2,1)}), bf16[16,16,512]{2,1,0:T(8,128)(2,1)S(1)}, u32[]{:S(2)}, u32[]{:S(2)}) %all-to-all-start.1) | async-done | bytes 262176 | tf_op jit(solution)/shard_map/all_to_all | solution.py:547
  31.6 0.7 copy-done.2
  32.3 4.3 %shard_map.183 = (bf16[256,512]{1,0:T(8,128)(2,1)}, bf16[256,512]{1,0:T(8,128)(2,1)}, bf16[256,512]{1,0:T(8,128)(2,1)}, f32[256,512]{1,0:T(8,128)}, f32[256,512]...) custom-call(bf16[256,384]{1,0:T(8,128)(2,1)} %get-tuple-element.83.refs_0_.refs_2_, ...), custom_call_target="tpu_custom_call" | custom-call | flops 1 | bytes 1 | tf_op jit(solution)/shard_map/pallas_call | solution.py:493
  36.6 4.0 %all-to-all-start.2 = ((bf16[16,16,512]{2,1,0:T(8,128)(2,1)}), bf16[16,16,512]{2,1,0:T(8,128)(2,1)S(1)}, u32[]{:S(2)}, u32[]{:S(2)}) async-start(bf16[16,16,512]{2,1,0:T(8,128)(2,1)} %bitcast.45), calls=%async_computation.2 | async-start | bytes 524288 | tf_op jit(solution)/shard_map/all_to_all | solution.py:547
  40.6 2.7 %shard_map.184.refs_7_ = bf16[768,512]{1,0:T(8,128)(2,1)} custom-call(bf16[768,512]{1,0:T(8,128)(2,1)} %refs_0_.4, f32[512,512]{1,0:T(8,128)} %get-tuple-element.96.refs_1_.refs_3_, f32[256,512]{1,0:T(8,128)} %get-tuple-element.97.refs_2_.refs_5_, bf16[256,512]{1,0:T(8,128)(2,1)} %get-tuple-element.88.refs_3_), custom_call_target="tpu_custom_call" | custom-call | flops 1 | bytes 1 | tf_op jit(solution)/shard_map/pallas_call | solution.py:493
  43.2 4.3 %shard_map.185.refs_8_.refs_9_.refs_4_ = bf16[2,1024,768]{2,1,0:T(8,128)(2,1)} custom-call(bf16[768,512]{1,0:T(8,128)(2,1)} %refs_0_.4, bf16[512,512]{1,0:T(8,128)(2,1)} %get-tuple-element.90.refs_1_, bf16[512,512]{1,0:T(8,128)(2,1)} %get-tuple-element.91.refs_2_, bf16[512,512]{1,0:T(8,128)(2,1)} %get-tuple-element.92.refs_3_, ...), custom_call_target="tpu_custom_call" | custom-call | flops 1 | bytes 1 | tf_op jit(solution)/shard_map/pallas_call | solution.py:493
  47.6 2.5 %all-to-all-done.2 = bf16[16,16,512]{2,1,0:T(8,128)(2,1)S(1)} async-done(((bf16[16,16,512]{2,1,0:T(8,128)(2,1)}), bf16[16,16,512]{2,1,0:T(8,128)(2,1)S(1)}, u32[]{:S(2)}, u32[]{:S(2)}) %all-to-all-start.2) | async-done | bytes 262176 | tf_op jit(solution)/shard_map/all_to_all | solution.py:547
  50.1 0.7 copy-done.1
  50.8 5.4 %shard_map.186 = (bf16[128,512]{1,0:T(8,128)(2,1)}, f32[128,512]{1,0:T(8,128)}, bf16[128,512]{1,0:T(8,128)(2,1)}, bf16[256,512]{1,0:T(8,128)(2,1)}, bf16[768,512]{1,0:T(8,128)(2,1)}, /*index=5*/bf16[768,512]{1,0:T(8,128)(2,1)}) custom-call(s32[1]{0:T(128)} %bitcast.refs_0_, bf16[256,512]{1,0:T(8,128)(2,1)} %bitcast.41, ...), custom_call_target="tpu_custom_call" | custom-call | flops 1 | bytes 1 | tf_op jit(solution)/shard_map/pallas_call | solution.py:493
  56.8 3.4 %all-to-all-start.3 = ((bf16[16,16,512]{2,1,0:T(8,128)(2,1)}), bf16[16,16,512]{2,1,0:T(8,128)(2,1)S(1)}, u32[]{:S(2)}, u32[]{:S(2)}) async-start(bf16[16,16,512]{2,1,0:T(8,128)(2,1)} %bitcast.46), calls=%async_computation.3 | async-start | bytes 524288 | tf_op jit(solution)/shard_map/all_to_all | solution.py:547
  60.3 1.3 add_convert_fusion
  61.7 1.3 collective-permute-start.1
  63.0 3.6 %shard_map.187 = (bf16[512,512]{1,0:T(8,128)(2,1)}, bf16[512,512]{1,0:T(8,128)(2,1)}) custom-call(bf16[512,128]{1,0:T(8,128)(2,1)} %get-tuple-element.103.refs_0_.refs_1_, bf16[128,512]{1,0:T(8,128)(2,1)} %get-tuple-element.99.refs_1_.refs_2_, bf16[768,512]{1,0:T(8,128)(2,1)} %refs_0_.5, f32[512,512]{1,0:T(8,128)} %get-tuple-element.96.refs_1_.refs_3_, ...), custom_call_target="tpu_custom_call" | custom-call | flops 1 | bytes 1 | tf_op jit(solution)/shard_map/pallas_call | solution.py:493
  66.6 3.1 %all-to-all-done.3 = bf16[16,16,512]{2,1,0:T(8,128)(2,1)S(1)} async-done(((bf16[16,16,512]{2,1,0:T(8,128)(2,1)}), bf16[16,16,512]{2,1,0:T(8,128)(2,1)S(1)}, u32[]{:S(2)}, u32[]{:S(2)}) %all-to-all-start.3) | async-done | bytes 262176 | tf_op jit(solution)/shard_map/all_to_all | solution.py:547
  69.7 0.7 copy-done
  70.4 5.7 %shard_map.188 = (bf16[256,512]{1,0:T(8,128)(2,1)}, bf16[256,512]{1,0:T(8,128)(2,1)}, bf16[1024,512]{1,0:T(8,128)(2,1)}) custom-call(s32[1]{0:T(128)} %bitcast.refs_0_, bf16[256,384]{1,0:T(8,128)(2,1)} %get-tuple-element.84.refs_2_.refs_1_.refs_3_, bf16[128,512]{1,0:T(8,128)(2,1)} %get-tuple-element.99.refs_1_.refs_2_, bf16[256,512]{1,0:T(8,128)(2,1)} %bitcast.40, ...), custom_call_target="tpu_custom_call" | custom-call | flops 1 | bytes 1 | tf_op jit(solution)/shard_map/pallas_call | solution.py:493
  76.1 0.8 collective-permute-start.2
  77.1 3.9 %shard_map.189 = (f32[128,512]{1,0:T(8,128)}, bf16[256,512]{1,0:T(8,128)(2,1)}) custom-call(bf16[512,128]{1,0:T(8,128)(2,1)} %get-tuple-element.118.refs_0_, bf16[512,128]{1,0:T(8,128)(2,1)} %get-tuple-element.103.refs_0_.refs_1_, bf16[256,384]{1,0:T(8,128)(2,1)} %get-tuple-element.83.refs_0_.refs_2_, ...), custom_call_target="tpu_custom_call" | custom-call | flops 1 | bytes 1 | tf_op jit(solution)/shard_map/pallas_call | solution.py:493
  81.0 1.0 copy-done.3
  82.0 5.3 %shard_map.190 = (bf16[512,512]{1,0:T(8,128)(2,1)}, bf16[512,512]{1,0:T(8,128)(2,1)}) custom-call(s32[1]{0:T(128)} %bitcast.refs_0_, bf16[1024,512]{1,0:T(8,128)(2,1)} %copy-done.3, bf16[256,512]{1,0:T(8,128)(2,1)} %get-tuple-element.129.refs_5_.refs_2_, bf16[256,512]{1,0:T(8,128)(2,1)} %get-tuple-element.117.refs_3_, ...), custom_call_target="tpu_custom_call" | custom-call | flops 1 | bytes 1 | tf_op jit(solution)/shard_map/pallas_call | solution.py:493
  87.9 4.6 %all-to-all-start.4 = ((bf16[16,16,512]{2,1,0:T(8,128)(2,1)}), bf16[16,16,512]{2,1,0:T(8,128)(2,1)S(1)}, u32[]{:S(2)}, u32[]{:S(2)}) async-start(bf16[16,16,512]{2,1,0:T(8,128)(2,1)} %bitcast.20), calls=%async_computation.4 | async-start | bytes 524288 | tf_op jit(solution)/shard_map/all_to_all | solution.py:547
  92.6 2.4 %collective-permute-start.5 = (bf16[192,512]{1,0:T(8,128)(2,1)S(1)}, bf16[192,512]{1,0:T(8,128)(2,1)S(1)}, u32[]{:S(2)}, u32[]{:S(2)}) collective-permute-start(bf16[192,512]{1,0:T(8,128)(2,1)S(1)} %add_convert_fusion.5), channel_id=1, source_target_pairs={{0,8},{1,9},{2,10},{3,11},{4,12},{5,13},{6,14},{7,15},{8,0},{9,1},... | collective-permute-start | bytes 589832 | tf_op jit(solution)/shard_map/ppermute | solution.py:512
  95.0 3.9 %shard_map.191.refs_4_ = f32[768,512]{1,0:T(8,128)} custom-call(bf16[768,512]{1,0:T(8,128)(2,1)} %refs_0_.5, bf16[512,512]{1,0:T(8,128)(2,1)} %get-tuple-element.128.refs_10_.refs_12_.refs_4_.refs_5_.refs_1_, bf16[256,512]{1,0:T(8,128)(2,1)} %get-tuple-element.129.refs_5_.refs_2_, bf16[1536,512]{1,0:T(8,128)(2,1)} %refs_3_.5, ...), custom_call_target="tpu_custom_call" | custom-call | flops 1 | bytes 1 | tf_op jit(solution)/shard_map/pallas_call | solution.py:493
  98.9 11.0 %collective-permute-done.5 = bf16[192,512]{1,0:T(8,128)(2,1)S(1)} collective-permute-done((bf16[192,512]{1,0:T(8,128)(2,1)S(1)}, bf16[192,512]{1,0:T(8,128)(2,1)S(1)}, u32[]{:S(2)}, u32[]{:S(2)}) %collective-permute-start.5) | collective-permute-done | bytes 196640 | tf_op jit(solution)/shard_map/ppermute | solution.py:512
  110.2 1.5 collective-permute-start.7
  111.7 9.7 %collective-permute-done.7 = bf16[192,512]{1,0:T(8,128)(2,1)S(1)} collective-permute-done((bf16[192,512]{1,0:T(8,128)(2,1)S(1)}, bf16[192,512]{1,0:T(8,128)(2,1)S(1)}, u32[]{:S(2)}, u32[]{:S(2)}) %collective-permute-start.7) | collective-permute-done | bytes 196640 | tf_op jit(solution)/shard_map/ppermute | solution.py:512
  121.5 0.7 collective-permute-start.8
  122.3 1.4 collective-permute-start.10
  123.7 2.0 %shard_map.192 = f32[128,512]{1,0:T(8,128)} custom-call(f32[128,512]{1,0:T(8,128)} %get-tuple-element.136.refs_0_, f32[128,512]{1,0:T(8,128)} %get-tuple-element.137.refs_1_, bf16[256,128]{1,0:T(8,128)(2,1)} %get-tuple-element.86.refs_5_.refs_2_, bf16[256,512]{1,0:T(8,128)(2,1)} %bitcast.44, f32[768,512]{1,0:T(8,128)} %shard_map.191.refs_4_), custom_call_target="tpu_custom_call" | custom-call | flops 1 | bytes 1 | tf_op jit(solution)/shard_map/pallas_call | solution.py:493
  125.7 4.4 %collective-permute-done.8 = bf16[128,512]{1,0:T(8,128)(2,1)S(1)} collective-permute-done((bf16[128,512]{1,0:T(8,128)(2,1)S(1)}, bf16[128,512]{1,0:T(8,128)(2,1)S(1)}, u32[]{:S(2)}, u32[]{:S(2)}) %collective-permute-start.8) | collective-permute-done | bytes 131104 | tf_op jit(solution)/shard_map/ppermute | solution.py:512
  130.3 8.4 %collective-permute-done.9 = bf16[128,512]{1,0:T(8,128)(2,1)S(1)} collective-permute-done((bf16[128,512]{1,0:T(8,128)(2,1)S(1)}, bf16[128,512]{1,0:T(8,128)(2,1)S(1)}, u32[]{:S(2)}, u32[]{:S(2)}) %collective-permute-start.9) | collective-permute-done | bytes 131104 | tf_op jit(solution)/shard_map/ppermute | solution.py:512
  139.7 7.9 %collective-permute-done.11 = bf16[256,512]{1,0:T(8,128)(2,1)S(1)} collective-permute-done((bf16[256,512]{1,0:T(8,128)(2,1)S(1)}, bf16[256,512]{1,0:T(8,128)(2,1)S(1)}, u32[]{:S(2)}, u32[]{:S(2)}) %collective-permute-start.11) | collective-permute-done | bytes 262176 | tf_op jit(solution)/shard_map/ppermute | solution.py:512
  147.9 1.5 collective-permute-start.13
  149.3 1.1 collective-permute-start.14
  150.6 0.8 slice.9
  151.4 1.0 pad_maximum_fusion.1
  152.4 8.2 %collective-permute-done.13 = bf16[512,512]{1,0:T(8,128)(2,1)S(1)} collective-permute-done((bf16[512,512]{1,0:T(8,128)(2,1)S(1)}, bf16[512,512]{1,0:T(8,128)(2,1)S(1)}, u32[]{:S(2)}, u32[]{:S(2)}) %collective-permute-start.13) | collective-permute-done | bytes 524320 | tf_op jit(solution)/shard_map/ppermute | solution.py:512
  160.6 1.7 %collective-permute-start.15 = (bf16[512,512]{1,0:T(8,128)(2,1)S(1)}, bf16[512,512]{1,0:T(8,128)(2,1)S(1)}, u32[]{:S(2)}, u32[]{:S(2)}) collective-permute-start(bf16[512,512]{1,0:T(8,128)(2,1)S(1)} %collective-permute-done.13), channel_id=1, source_target_pairs={{0,1},{1,0},{2,3},{3,2},{4,5},{5,4},{6,7},{7,6},{8,9},{9,8},{10,11... | collective-permute-start | bytes 1572872 | tf_op jit(solution)/shard_map/ppermute | solution.py:512
  162.3 1.5 collective-permute-done.15
  163.8 1.0 broadcast_select_fusion.6
  164.8 1.2 pad_maximum_fusion
  (43 shorter events, 4.3 us)
Async XLA Ops:
  2.3 13.0 %all-to-all-start = ((s32[16,1,16]{2,1,0:T(1,128)}), s32[16,1,16]{2,1,0:T(1,128)S(1)}, u32[]{:S(2)}, u32[]{:S(2)}) async-start(s32[16,1,16]{2,1,0:T(1,128)} %bitcast.48), calls=%async_computation | async-start | bytes 16384 | tf_op jit(solution)/shard_map/all_to_all | solution.py:577
  15.4 0.6 copy-start.6
  18.0 13.6 %all-to-all-start.1 = ((bf16[16,16,512]{2,1,0:T(8,128)(2,1)}), bf16[16,16,512]{2,1,0:T(8,128)(2,1)S(1)}, u32[]{:S(2)}, u32[]{:S(2)}) async-start(bf16[16,16,512]{2,1,0:T(8,128)(2,1)} %bitcast.47), calls=%async_computation.1 | async-start | bytes 524288 | tf_op jit(solution)/shard_map/all_to_all | solution.py:547
  31.6 0.7 copy-start.2
  36.6 13.5 %all-to-all-start.2 = ((bf16[16,16,512]{2,1,0:T(8,128)(2,1)}), bf16[16,16,512]{2,1,0:T(8,128)(2,1)S(1)}, u32[]{:S(2)}, u32[]{:S(2)}) async-start(bf16[16,16,512]{2,1,0:T(8,128)(2,1)} %bitcast.45), calls=%async_computation.2 | async-start | bytes 524288 | tf_op jit(solution)/shard_map/all_to_all | solution.py:547
  50.1 0.7 copy-start.1
  56.2 4.1 %collective-permute-start = (bf16[768,512]{1,0:T(8,128)(2,1)}, bf16[768,512]{1,0:T(8,128)(2,1)S(1)}, u32[]{:S(2)}, u32[]{:S(2)}) collective-permute-start(bf16[768,512]{1,0:T(8,128)(2,1)} %get-tuple-element.102.refs_7_), channel_id=1, source_target_pairs={{0,1},{1,0},{2,3},{3,2},{4,5},{5,4},{6,7},{7,6},{8,9},{9,8},{10,11... | collective-permute-start | bytes 2359304 | tf_op jit(solution)/shard_map/ppermute | solution.py:512
  56.8 12.9 %all-to-all-start.3 = ((bf16[16,16,512]{2,1,0:T(8,128)(2,1)}), bf16[16,16,512]{2,1,0:T(8,128)(2,1)S(1)}, u32[]{:S(2)}, u32[]{:S(2)}) async-start(bf16[16,16,512]{2,1,0:T(8,128)(2,1)} %bitcast.46), calls=%async_computation.3 | async-start | bytes 524288 | tf_op jit(solution)/shard_map/all_to_all | solution.py:547
  61.7 14.4 %collective-permute-start.1 = (bf16[384,512]{1,0:T(8,128)(2,1)S(1)}, bf16[384,512]{1,0:T(8,128)(2,1)S(1)}, u32[]{:S(2)}, u32[]{:S(2)}) collective-permute-start(bf16[384,512]{1,0:T(8,128)(2,1)S(1)} %get-tuple-element.164), channel_id=1, source_target_pairs={{0,2},{1,3},{2,0},{3,1},{4,6},{5,7},{6,4},{7,5},{8,10},{9,11},{10,... | collective-permute-start | bytes 1179656 | tf_op jit(solution)/shard_map/ppermute | solution.py:512
  69.7 0.7 copy-start
  76.1 4.9 %collective-permute-start.2 = (bf16[1024,512]{1,0:T(8,128)(2,1)}, bf16[1024,512]{1,0:T(8,128)(2,1)S(1)}, u32[]{:S(2)}, u32[]{:S(2)}) collective-permute-start(bf16[1024,512]{1,0:T(8,128)(2,1)} %get-tuple-element.114.refs_7_), channel_id=1, source_target_pairs={{0,1},{1,0},{2,3},{3,2},{4,5},{5,4},{6,7},{7,6},{8,9},{9,8},{10,11... | collective-permute-start | bytes 3145736 | tf_op jit(solution)/shard_map/ppermute | solution.py:512
  77.0 10.2 %collective-permute-start.3 = (bf16[192,512]{1,0:T(8,128)(2,1)S(1)}, bf16[192,512]{1,0:T(8,128)(2,1)S(1)}, u32[]{:S(2)}, u32[]{:S(2)}) collective-permute-start(bf16[192,512]{1,0:T(8,128)(2,1)S(1)} %get-tuple-element.168), channel_id=1, source_target_pairs={{0,4},{1,5},{2,6},{3,7},{4,0},{5,1},{6,2},{7,3},{8,12},{9,13},{10,... | collective-permute-start | bytes 589832 | tf_op jit(solution)/shard_map/ppermute | solution.py:512
  81.0 1.0 copy-start.3
  87.3 22.7 %collective-permute-start.4 = (bf16[512,512]{1,0:T(8,128)(2,1)}, bf16[512,512]{1,0:T(8,128)(2,1)S(1)}, u32[]{:S(2)}, u32[]{:S(2)}) collective-permute-start(bf16[512,512]{1,0:T(8,128)(2,1)} %get-tuple-element.125.refs_4_), channel_id=1, source_target_pairs={{0,2},{1,3},{2,0},{3,1},{4,6},{5,7},{6,4},{7,5},{8,10},{9,11},{10,... | collective-permute-start | bytes 1572872 | tf_op jit(solution)/shard_map/ppermute | solution.py:512
  87.9 22.0 %all-to-all-start.4 = ((bf16[16,16,512]{2,1,0:T(8,128)(2,1)}), bf16[16,16,512]{2,1,0:T(8,128)(2,1)S(1)}, u32[]{:S(2)}, u32[]{:S(2)}) async-start(bf16[16,16,512]{2,1,0:T(8,128)(2,1)} %bitcast.20), calls=%async_computation.4 | async-start | bytes 524288 | tf_op jit(solution)/shard_map/all_to_all | solution.py:547
  92.6 17.3 %copy-start.5 = (bf16[512,512]{1,0:T(8,128)(2,1)S(1)}, bf16[512,512]{1,0:T(8,128)(2,1)}, u32[]{:S(2)}) copy-start(bf16[512,512]{1,0:T(8,128)(2,1)} %get-tuple-element.131) | copy-start | bytes 1572868
  92.6 17.2 %collective-permute-start.5 = (bf16[192,512]{1,0:T(8,128)(2,1)S(1)}, bf16[192,512]{1,0:T(8,128)(2,1)S(1)}, u32[]{:S(2)}, u32[]{:S(2)}) collective-permute-start(bf16[192,512]{1,0:T(8,128)(2,1)S(1)} %add_convert_fusion.5), channel_id=1, source_target_pairs={{0,8},{1,9},{2,10},{3,11},{4,12},{5,13},{6,14},{7,15},{8,0},{9,1},... | collective-permute-start | bytes 589832 | tf_op jit(solution)/shard_map/ppermute | solution.py:512
  109.9 11.5 %copy-start.4 = (bf16[16,16,512]{2,1,0:T(8,128)(2,1)}, bf16[16,16,512]{2,1,0:T(8,128)(2,1)S(1)}, u32[]{:S(2)}) copy-start(bf16[16,16,512]{2,1,0:T(8,128)(2,1)S(1)} %all-to-all-done.4) | copy-start | bytes 786436
  110.1 11.2 %collective-permute-start.6 = (bf16[256,512]{1,0:T(8,128)(2,1)S(1)}, bf16[256,512]{1,0:T(8,128)(2,1)S(1)}, u32[]{:S(2)}, u32[]{:S(2)}) collective-permute-start(bf16[256,512]{1,0:T(8,128)(2,1)S(1)} %get-tuple-element.166), channel_id=1, source_target_pairs={{0,4},{1,5},{2,6},{3,7},{4,0},{5,1},{6,2},{7,3},{8,12},{9,13},{10,... | collective-permute-start | bytes 786440 | tf_op jit(solution)/shard_map/ppermute | solution.py:512
  110.2 11.1 %collective-permute-start.7 = (bf16[192,512]{1,0:T(8,128)(2,1)S(1)}, bf16[192,512]{1,0:T(8,128)(2,1)S(1)}, u32[]{:S(2)}, u32[]{:S(2)}) collective-permute-start(bf16[192,512]{1,0:T(8,128)(2,1)S(1)} %add_convert_fusion.4), channel_id=1, source_target_pairs={{0,4},{1,5},{2,6},{3,7},{4,0},{5,1},{6,2},{7,3},{8,12},{9,13},{10,... | collective-permute-start | bytes 589832 | tf_op jit(solution)/shard_map/ppermute | solution.py:512
  121.5 8.7 %collective-permute-start.8 = (bf16[128,512]{1,0:T(8,128)(2,1)S(1)}, bf16[128,512]{1,0:T(8,128)(2,1)S(1)}, u32[]{:S(2)}, u32[]{:S(2)}) collective-permute-start(bf16[128,512]{1,0:T(8,128)(2,1)S(1)} %get-tuple-element.170), channel_id=1, source_target_pairs={{0,8},{1,9},{2,10},{3,11},{4,12},{5,13},{6,14},{7,15},{8,0},{9,1},... | collective-permute-start | bytes 393224 | tf_op jit(solution)/shard_map/ppermute | solution.py:512
  122.3 16.4 %collective-permute-start.10 = (bf16[384,512]{1,0:T(8,128)(2,1)S(1)}, bf16[384,512]{1,0:T(8,128)(2,1)S(1)}, u32[]{:S(2)}, u32[]{:S(2)}) collective-permute-start(bf16[384,512]{1,0:T(8,128)(2,1)S(1)} %maximum_select_fusion.2), channel_id=1, source_target_pairs={{0,2},{1,3},{2,0},{3,1},{4,6},{5,7},{6,4},{7,5},{8,10},{9,11},{10,... | collective-permute-start | bytes 1179656 | tf_op jit(solution)/shard_map/ppermute | solution.py:512
  130.2 8.5 %collective-permute-start.9 = (bf16[128,512]{1,0:T(8,128)(2,1)S(1)}, bf16[128,512]{1,0:T(8,128)(2,1)S(1)}, u32[]{:S(2)}, u32[]{:S(2)}) collective-permute-start(bf16[128,512]{1,0:T(8,128)(2,1)S(1)} %add_convert_fusion.6), channel_id=1, source_target_pairs={{0,8},{1,9},{2,10},{3,11},{4,12},{5,13},{6,14},{7,15},{8,0},{9,1},... | collective-permute-start | bytes 393224 | tf_op jit(solution)/shard_map/ppermute | solution.py:512
  139.0 8.6 %collective-permute-start.12 = (bf16[768,512]{1,0:T(8,128)(2,1)S(1)}, bf16[768,512]{1,0:T(8,128)(2,1)S(1)}, u32[]{:S(2)}, u32[]{:S(2)}) collective-permute-start(bf16[768,512]{1,0:T(8,128)(2,1)S(1)} %maximum_select_fusion), channel_id=1, source_target_pairs={{0,1},{1,0},{2,3},{3,2},{4,5},{5,4},{6,7},{7,6},{8,9},{9,8},{10,11... | collective-permute-start | bytes 2359304 | tf_op jit(solution)/shard_map/ppermute | solution.py:512
  139.7 8.0 %collective-permute-start.11 = (bf16[256,512]{1,0:T(8,128)(2,1)S(1)}, bf16[256,512]{1,0:T(8,128)(2,1)S(1)}, u32[]{:S(2)}, u32[]{:S(2)}) collective-permute-start(bf16[256,512]{1,0:T(8,128)(2,1)S(1)} %maximum_select_fusion.3), channel_id=1, source_target_pairs={{0,4},{1,5},{2,6},{3,7},{4,0},{5,1},{6,2},{7,3},{8,12},{9,13},{10,... | collective-permute-start | bytes 786440 | tf_op jit(solution)/shard_map/ppermute | solution.py:512
  147.9 12.7 %collective-permute-start.13 = (bf16[512,512]{1,0:T(8,128)(2,1)S(1)}, bf16[512,512]{1,0:T(8,128)(2,1)S(1)}, u32[]{:S(2)}, u32[]{:S(2)}) collective-permute-start(bf16[512,512]{1,0:T(8,128)(2,1)S(1)} %maximum_select_fusion.1), channel_id=1, source_target_pairs={{0,2},{1,3},{2,0},{3,1},{4,6},{5,7},{6,4},{7,5},{8,10},{9,11},{10,... | collective-permute-start | bytes 1572872 | tf_op jit(solution)/shard_map/ppermute | solution.py:512
  149.3 11.2 %collective-permute-start.14 = (bf16[512,512]{1,0:T(8,128)(2,1)S(1)}, bf16[512,512]{1,0:T(8,128)(2,1)S(1)}, u32[]{:S(2)}, u32[]{:S(2)}) collective-permute-start(bf16[512,512]{1,0:T(8,128)(2,1)S(1)} %maximum_select_fusion.1), channel_id=1, source_target_pairs={{0,1},{1,0},{2,3},{3,2},{4,5},{5,4},{6,7},{7,6},{8,9},{9,8},{10,11... | collective-permute-start | bytes 1572872 | tf_op jit(solution)/shard_map/ppermute | solution.py:512
  160.6 3.2 %collective-permute-start.15 = (bf16[512,512]{1,0:T(8,128)(2,1)S(1)}, bf16[512,512]{1,0:T(8,128)(2,1)S(1)}, u32[]{:S(2)}, u32[]{:S(2)}) collective-permute-start(bf16[512,512]{1,0:T(8,128)(2,1)S(1)} %collective-permute-done.13), channel_id=1, source_target_pairs={{0,1},{1,0},{2,3},{3,2},{4,5},{5,4},{6,7},{7,6},{8,9},{9,8},{10,11... | collective-permute-start | bytes 1572872 | tf_op jit(solution)/shard_map/ppermute | solution.py:512

commit v8 on v6

--- a/solution.py
+++ b/solution.py
@@ -478,20 +478,20 @@
     return (lax.axis_index("dom") >> bit) & 1
 
 
-def traded(rows, devices, bit):
+def split(parts, bit):
     place = place_of(bit)
-    halves = rows.reshape(2, rows.shape[0] // 2, rows.shape[1])
-    own = lax.dynamic_index_in_dim(halves, place, 0, False)
-    sent = lax.dynamic_index_in_dim(halves, 1 - place, 0, False)
-    return own, across(sent, devices, 1 << bit)
+    halves = [part.reshape(2, part.shape[0] // 2, part.shape[1]) for part in parts]
+    own = [lax.dynamic_index_in_dim(half, place, 0, False) for half in halves]
+    sent = [lax.dynamic_index_in_dim(half, 1 - place, 0, False) for half in halves]
+    return own, added(*sent)
 
 
 def handed(rows, devices, bit):
     return [rows, across(rows, devices, 1 << bit)]
 
 
-def added(left, right):
-    return (left.astype(F32) + right.astype(F32)).astype(BF16)
+def added(*parts):
+    return sum(part.astype(F32) for part in parts).astype(BF16)
 
 
 def joined(parts, bit):
@@ -675,7 +675,8 @@
         (blocks,),
     )
     bits = index_bits(domains)
-    node_parts = traded(node_sum, domains, 1)
+    node_own, node_sent = split([node_sum], 1)
+    node_parts = [*node_own, across(node_sent, domains, 2)]
     far_grad, node_sum, inner_pre = fence(far_grad, node_sum, inner_pre)
     factors = [
         edges,
@@ -723,6 +724,9 @@
         buffers,
     )
     edge_send, place, *node_parts = fence(edge_send, me, *node_parts)
+    received = across(edge_send, domains, 1)
+    node_own, node_sent = split(node_parts, 2)
+    node_got = across(node_sent, domains, 4)
     edge_keep = line.run(
         edge_weights_kernel,
         shaped(BF16, 2 * latent, latent),
@@ -730,12 +734,13 @@
         [SMEM, VMEM, VMEM] + [ANY] * len(factors),
         scratch=buffers,
     )
-    edge_parts = [edge_keep, across(edge_send, domains, 1)]
-    node_parts = traded(added(*node_parts), domains, 2)
-    fenced = fence(*edge_parts, *node_parts, inner_pre, cut_pre)
-    edge_sum, node_sum, (inner_pre, cut_pre) = added(*fenced[:2]), added(*fenced[2:4]), fenced[4:]
-    edge_parts = traded(edge_sum, domains, 1)
-    node_parts = traded(node_sum, domains, 3)
+    edge_own, edge_sent = split(fence(edge_keep, received), 1)
+    edge_sent, inner_pre, cut_pre = fence(edge_sent, inner_pre, cut_pre)
+    node_got = fence(node_got, edge_sent)[0]
+    edge_got = across(edge_sent, domains, 2)
+    node_sum = added(*node_own, node_got)
+    for bit in bits[3:]:
+        node_sum = added(*handed(node_sum, domains, bit))
     local_grad, outgoing_grad = line.run(
         input_grads_kernel,
         [shaped(F32, node_rows, latent), shaped(BF16, total_slots, latent)],
@@ -749,19 +754,14 @@
             w_edge_in,
         ],
     )
-    fenced = fence(*edge_parts, *node_parts, inner_pre, cut_pre, local_grad)
-    edge_sum, node_sum = added(*fenced[:2]), added(*fenced[2:4])
-    inner_pre, cut_pre, local_grad = fenced[4:]
-    for bit in bits[4:]:
-        node_sum = added(*traded(node_sum, domains, bit))
-    for bit in bits[:3:-1]:
-        node_sum = joined(handed(node_sum, domains, bit), bit)
-    edge_parts = traded(edge_sum, domains, 2)
-    node_parts = handed(node_sum, domains, 3)
-    fenced = fence(*edge_parts, *node_parts, inner_pre)
-    edge_sum, node_sum, inner_pre = added(*fenced[:2]), joined(fenced[2:4], 3), fenced[4]
-    edge_parts = traded(edge_sum, domains, 3)
-    node_parts = handed(node_sum, domains, 2)
+    edge_got, node_sum, inner_pre, cut_pre, local_grad = fence(
+        edge_got, node_sum, inner_pre, cut_pre, local_grad
+    )
+    edge_own, edge_sent = split([*edge_own, edge_got], 2)
+    edge_got, *node_parts = fence(across(edge_sent, domains, 4), *handed(node_sum, domains, 2))
+    edge_own, edge_sent = split([*edge_own, edge_got], 3)
+    edge_got = across(edge_sent, domains, 8)
+    node_parts = handed(joined(node_parts, 2), domains, 1)
     grad_edges = line.run(
         functools.partial(edge_grads_kernel, blocks=blocks),
         shaped(F32, *edges.shape),
@@ -775,28 +775,26 @@
         [rows_spec(latent)],
         (blocks + 1,),
     )
-    fenced = fence(*edge_parts, *node_parts, grad_edges)
-    edge_sum, node_sum, grad_edges = added(*fenced[:2]), joined(fenced[2:4], 2), fenced[4]
+    edge_got, grad_edges, outgoing_grad = fence(edge_got, grad_edges, outgoing_grad)
+    edge_sum = added(*edge_own, edge_got)
     for bit in bits[4:]:
-        edge_sum = added(*traded(edge_sum, domains, bit))
+        own, sent = split([edge_sum], bit)
+        edge_sum = added(*own, across(sent, domains, 1 << bit))
     for bit in bits[:3:-1]:
         edge_sum = joined(handed(edge_sum, domains, bit), bit)
-    node_parts = handed(node_sum, domains, 1)
-    edge_parts = fence(*handed(edge_sum, domains, 3))
+    returned = exchange(outgoing_grad, domains)
+    *edge_parts, node_sum, other_sum = fence(*handed(edge_sum, domains, 3), *node_parts)
     edge_parts = handed(joined(edge_parts, 3), domains, 2)
-    *edge_parts, node_sum, other_sum, outgoing_grad = fence(
-        *edge_parts, *node_parts, outgoing_grad
-    )
     node_sum = joined([node_sum, other_sum], 1)
+    others = across(node_sum, domains, 1)
+    *edge_parts, node_sum, others = fence(*edge_parts, node_sum, others)
     edge_sum = joined(edge_parts, 2)
     edge_parts = handed(edge_sum, domains, 1) + [across(edge_sum, domains, 1)]
-    others = across(node_sum, domains, 1)
-    returned = exchange(outgoing_grad, domains)
     lower, left = place_of(0) == 0, place_of(1) == 0
     low_rows, high_rows = jnp.where(lower, node_sum, others), jnp.where(lower, others, node_sum)
-    split = 2 * latent - low_rows.shape[0]
-    grad_node_in = jnp.concatenate([low_rows, high_rows[:split]])
-    grad_node_out = high_rows[split:]
+    cut_at = 2 * latent - low_rows.shape[0]
+    grad_node_in = jnp.concatenate([low_rows, high_rows[:cut_at]])
+    grad_node_out = high_rows[cut_at:]
     mine, far, near, grad_node_in, grad_node_out, returned = fence(
         *edge_parts, grad_node_in, grad_node_out, returned
     )

time: 155 us -> 156 us (level)
  starting transfers between devices: 34.5 us -> 38.7 us
  waiting for transfers between devices: 59 us -> 55.8 us
    ppermute x17 -> x16, starting transfers between devices: 12 us -> 15.5 us  [across(): lax.ppermute(rows, 'dom', [(device, device ^ mask) for device in range(de...]
    ppermute x17 -> x16, waiting for transfers between devices: 31.6 us -> 29.9 us  [across(): lax.ppermute(rows, 'dom', [(device, device ^ mask) for device in range(de...]
    convert_element_type x8 -> x7, other arithmetic: 3.26 us -> 3.69 us  [added(): return sum((part.astype(F32) for part in parts)).astype(BF16)]
  transfers between devices with their start and end apart: 22 -> 21, of which waited for: 15 -> 11; matrix products, arithmetic and copies ran while one was open for 3% -> 4% of each run, Pallas kernels for 22% -> 22%
where the time goes in v8:
time: 156 us; the launch traced here: 155 us
  waiting for transfers between devices  55.8 us (36%)
  Pallas kernels  48 us (31%)
  starting transfers between devices  38.7 us (25%)
  other arithmetic  7.81 us (5%)
  local copies, waits for them, and re-layouts  3.98 us (3%)
    pallas_call x13, Pallas kernels, run(): pl.pallas_call(ordered, out_shape=out_shape, in_specs=specs, out_specs=[V...  48 us
    ppermute x16, waiting for transfers between devices, across(): lax.ppermute(rows, 'dom', [(device, device ^ mask) for device in range(de...  29.9 us
    all_to_all x4, waiting for transfers between devices, exchange(): lax.all_to_all(split, 'dom', split_axis=0, concat_axis=0, tiled=True)  22.2 us
    all_to_all x4, starting transfers between devices, exchange(): lax.all_to_all(split, 'dom', split_axis=0, concat_axis=0, tiled=True)  15.9 us
    ppermute x16, starting transfers between devices, across(): lax.ppermute(rows, 'dom', [(device, device ^ mask) for device in range(de...  15.5 us
    all_to_all x1, starting transfers between devices, shards(): asked = lax.all_to_all(ask, 'dom', split_axis=0, concat_axis=0, tiled=True)  7.32 us
    convert_element_type x7, other arithmetic, added(): return sum((part.astype(F32) for part in parts)).astype(BF16)  3.69 us
    all_to_all x1, waiting for transfers between devices, shards(): asked = lax.all_to_all(ask, 'dom', split_axis=0, concat_axis=0, tiled=True)  3.68 us
  transfers between devices with their start and end apart: 21, of which 11 were waited for; matrix products, arithmetic and copies ran while one was open for 4% of the time, Pallas kernels for 22%

profile of v8, /device:TPU:1, one launch (start us, length us, event | category | flops | bytes accessed | tf_op | source)
XLA Modules:
  0.0 155.1 jit_solution(944229657406284122)
XLA Ops:
  0.6 1.7 %shard_map.179.refs_2_ = s32[16,16]{1,0:T(8,128)} custom-call(s32[1,128]{1,0:T(1,128)} %bitcast.81, s32[1,128]{1,0:T(1,128)} %bitcast.84), custom_call_target="tpu_custom_call" | custom-call | flops 1 | bytes 1 | tf_op jit(solution)/shard_map/pallas_call | solution.py:451
  2.3 7.3 %all-to-all-start = ((s32[16,1,16]{2,1,0:T(1,128)}), s32[16,1,16]{2,1,0:T(1,128)S(1)}, u32[]{:S(2)}, u32[]{:S(2)}) async-start(s32[16,1,16]{2,1,0:T(1,128)} %bitcast.79), calls=%async_computation | async-start | bytes 16384 | tf_op jit(solution)/shard_map/all_to_all | solution.py:535
  9.7 2.0 %shard_map.180 = (bf16[256,384]{1,0:T(8,128)(2,1)}, bf16[256,384]{1,0:T(8,128)(2,1)}) custom-call(s32[1,128]{1,0:T(1,128)} %bitcast.82, s32[1,128]{1,0:T(1,128)} %bitcast.85, s32[16,16]{1,0:T(8,128)} %shard_map.179.refs_2_), custom_call_target="tpu_custom_call" | custom-call | flops 1 | bytes 1 | tf_op jit(solution)/shard_map/pallas_call | solution.py:451
  11.7 3.7 %all-to-all-done = s32[16,1,16]{2,1,0:T(1,128)S(1)} async-done(((s32[16,1,16]{2,1,0:T(1,128)}), s32[16,1,16]{2,1,0:T(1,128)S(1)}, u32[]{:S(2)}, u32[]{:S(2)}) %all-to-all-start) | async-done | bytes 1056 | tf_op jit(solution)/shard_map/all_to_all | solution.py:535
  15.4 0.6 copy-done.5
  16.0 2.0 %shard_map.181 = (bf16[256,512]{1,0:T(8,128)(2,1)}, bf16[256,128]{1,0:T(8,128)(2,1)}) custom-call(s32[16,16]{1,0:T(8,128)} %bitcast.80, bf16[128,512]{1,0:T(8,128)(2,1)} %refs_4_.4, bf16[256,384]{1,0:T(8,128)(2,1)} %get-tuple-element.80.refs_2_.refs_1_.refs_3_), custom_call_target="tpu_custom_call" | custom-call | flops 1 | bytes 1 | tf_op jit(solution)/shard_map/pallas_call | solution.py:451
  18.0 4.0 %all-to-all-start.1 = ((bf16[16,16,512]{2,1,0:T(8,128)(2,1)}), bf16[16,16,512]{2,1,0:T(8,128)(2,1)S(1)}, u32[]{:S(2)}, u32[]{:S(2)}) async-start(bf16[16,16,512]{2,1,0:T(8,128)(2,1)} %bitcast.76), calls=%async_computation.1 | async-start | bytes 524288 | tf_op jit(solution)/shard_map/all_to_all | solution.py:505
  22.0 6.2 %shard_map.182 = (bf16[512,128]{1,0:T(8,128)(2,1)}, bf16[512,128]{1,0:T(8,128)(2,1)}, bf16[512,512]{1,0:T(8,128)(2,1)}, bf16[512,512]{1,0:T(8,128)(2,1)}, bf16[5...) custom-call(s32[2,256]{1,0:T(2,128)} %bitcast.83, ...), custom_call_target="tpu_custom_call" | custom-call | flops 1 | bytes 1 | tf_op jit(solution)/shard_map/pallas_call | solution.py:451
  28.3 3.3 %all-to-all-done.1 = bf16[16,16,512]{2,1,0:T(8,128)(2,1)S(1)} async-done(((bf16[16,16,512]{2,1,0:T(8,128)(2,1)}), bf16[16,16,512]{2,1,0:T(8,128)(2,1)S(1)}, u32[]{:S(2)}, u32[]{:S(2)}) %all-to-all-start.1) | async-done | bytes 262176 | tf_op jit(solution)/shard_map/all_to_all | solution.py:505
  31.6 0.7 copy-done.2
  32.3 4.3 %shard_map.183 = (bf16[256,512]{1,0:T(8,128)(2,1)}, bf16[256,512]{1,0:T(8,128)(2,1)}, bf16[256,512]{1,0:T(8,128)(2,1)}, f32[256,512]{1,0:T(8,128)}, f32[256,512]...) custom-call(bf16[256,384]{1,0:T(8,128)(2,1)} %get-tuple-element.79.refs_0_.refs_2_, ...), custom_call_target="tpu_custom_call" | custom-call | flops 1 | bytes 1 | tf_op jit(solution)/shard_map/pallas_call | solution.py:451
  36.6 4.0 %all-to-all-start.2 = ((bf16[16,16,512]{2,1,0:T(8,128)(2,1)}), bf16[16,16,512]{2,1,0:T(8,128)(2,1)S(1)}, u32[]{:S(2)}, u32[]{:S(2)}) async-start(bf16[16,16,512]{2,1,0:T(8,128)(2,1)} %bitcast.70), calls=%async_computation.2 | async-start | bytes 524288 | tf_op jit(solution)/shard_map/all_to_all | solution.py:505
  40.6 2.7 %shard_map.184.refs_8_ = bf16[768,512]{1,0:T(8,128)(2,1)} custom-call(bf16[768,512]{1,0:T(8,128)(2,1)} %refs_3_.6, f32[512,512]{1,0:T(8,128)} %get-tuple-element.86.refs_1_.refs_3_, f32[256,512]{1,0:T(8,128)} %get-tuple-element.87.refs_2_.refs_5_, bf16[256,512]{1,0:T(8,128)(2,1)} %get-tuple-element.84.refs_3_), custom_call_target="tpu_custom_call" | custom-call | flops 1 | bytes 1 | tf_op jit(solution)/shard_map/pallas_call | solution.py:451
  43.2 6.9 %all-to-all-done.2 = bf16[16,16,512]{2,1,0:T(8,128)(2,1)S(1)} async-done(((bf16[16,16,512]{2,1,0:T(8,128)(2,1)}), bf16[16,16,512]{2,1,0:T(8,128)(2,1)S(1)}, u32[]{:S(2)}, u32[]{:S(2)}) %all-to-all-start.2) | async-done | bytes 262176 | tf_op jit(solution)/shard_map/all_to_all | solution.py:505
  50.1 0.7 copy-done.4
  50.8 5.4 %shard_map.185 = (bf16[128,512]{1,0:T(8,128)(2,1)}, f32[128,512]{1,0:T(8,128)}, bf16[128,512]{1,0:T(8,128)(2,1)}, bf16[256,512]{1,0:T(8,128)(2,1)}, bf16[768,512]{1,0:T(8,128)(2,1)}, /*index=5*/bf16[768,512]{1,0:T(8,128)(2,1)}) custom-call(s32[1]{0:T(128)} %bitcast.refs_0_, bf16[256,512]{1,0:T(8,128)(2,1)} %bitcast.69, ...), custom_call_target="tpu_custom_call" | custom-call | flops 1 | bytes 1 | tf_op jit(solution)/shard_map/pallas_call | solution.py:451
  56.2 0.7 collective-permute-start
  56.9 3.6 %all-to-all-start.3 = ((bf16[16,16,512]{2,1,0:T(8,128)(2,1)}), bf16[16,16,512]{2,1,0:T(8,128)(2,1)S(1)}, u32[]{:S(2)}, u32[]{:S(2)}) async-start(bf16[16,16,512]{2,1,0:T(8,128)(2,1)} %bitcast.75), calls=%async_computation.3 | async-start | bytes 524288 | tf_op jit(solution)/shard_map/all_to_all | solution.py:505
  60.5 1.3 add_convert_fusion
  61.9 1.2 collective-permute-start.1
  63.1 3.6 %shard_map.186 = (bf16[512,512]{1,0:T(8,128)(2,1)}, bf16[512,512]{1,0:T(8,128)(2,1)}) custom-call(bf16[512,128]{1,0:T(8,128)(2,1)} %get-tuple-element.94.refs_0_.refs_1_, bf16[128,512]{1,0:T(8,128)(2,1)} %get-tuple-element.90.refs_1_.refs_2_, bf16[768,512]{1,0:T(8,128)(2,1)} %refs_0_.3, f32[512,512]{1,0:T(8,128)} %get-tuple-element.86.refs_1_.refs_3_, ...), custom_call_target="tpu_custom_call" | custom-call | flops 1 | bytes 1 | tf_op jit(solution)/shard_map/pallas_call | solution.py:451
  66.7 3.1 %all-to-all-done.3 = bf16[16,16,512]{2,1,0:T(8,128)(2,1)S(1)} async-done(((bf16[16,16,512]{2,1,0:T(8,128)(2,1)}), bf16[16,16,512]{2,1,0:T(8,128)(2,1)S(1)}, u32[]{:S(2)}, u32[]{:S(2)}) %all-to-all-start.3) | async-done | bytes 262176 | tf_op jit(solution)/shard_map/all_to_all | solution.py:505
  69.7 0.7 copy-done.1
  70.4 5.4 %shard_map.187 = (bf16[256,512]{1,0:T(8,128)(2,1)}, bf16[256,512]{1,0:T(8,128)(2,1)}, bf16[1024,512]{1,0:T(8,128)(2,1)}) custom-call(s32[1]{0:T(128)} %bitcast.refs_0_, bf16[256,384]{1,0:T(8,128)(2,1)} %get-tuple-element.80.refs_2_.refs_1_.refs_3_, bf16[128,512]{1,0:T(8,128)(2,1)} %get-tuple-element.90.refs_1_.refs_2_, bf16[256,512]{1,0:T(8,128)(2,1)} %bitcast.60, ...), custom_call_target="tpu_custom_call" | custom-call | flops 1 | bytes 1 | tf_op jit(solution)/shard_map/pallas_call | solution.py:451
  75.9 0.8 collective-permute-start.2
  76.8 4.7 %shard_map.188.refs_7_ = bf16[1024,512]{1,0:T(8,128)(2,1)} custom-call(s32[1]{0:T(128)} %bitcast.refs_0_, bf16[256,512]{1,0:T(8,128)(2,1)} %get-tuple-element.111.refs_1_, bf16[256,512]{1,0:T(8,128)(2,1)} %get-tuple-element.129.refs_2_.refs_5_, bf16[768,512]{1,0:T(8,128)(2,1)} %refs_3_.6, bf16[512,512]{1,0:T(8,128)(2,1)} %get-tuple-element.101.refs_10_.refs_4_, ...), custom_call_target="tpu_custom_call" | custom-call | flops 1 | bytes 1 | tf_op jit(solution)/shard_map/pallas_call | solution.py:451
  81.5 2.0 %fusion = bf16[512,512]{1,0:T(8,128)(2,1)} fusion(bf16[2,512,512]{2,1,0:T(8,128)(2,1)S(1)} %bitcast.58, s32[]{:T(128)S(6)} %select_n.120, bf16[2,512,512]{2,1,0:T(8,128)(2,1)} %bitcast.49), kind=kLoop, calls=%fused_computation.7 | loop fusion | flops 1048576 | bytes 1572868 | tf_op jit(solution)/shard_map/convert_element_type | solution.py:494
  83.5 0.6 collective-permute-start.3
  84.2 1.6 %collective-permute-start.5 = (bf16[192,512]{1,0:T(8,128)(2,1)S(1)}, bf16[192,512]{1,0:T(8,128)(2,1)S(1)}, u32[]{:S(2)}, u32[]{:S(2)}) collective-permute-start(bf16[192,512]{1,0:T(8,128)(2,1)S(1)} %fusion.1), channel_id=1, source_target_pairs={{0,8},{1,9},{2,10},{3,11},{4,12},{5,13},{6,14},{7,15},{8,0},{9,1},... | collective-permute-start | bytes 589832 | tf_op jit(solution)/shard_map/ppermute | solution.py:470
  85.8 4.0 %shard_map.189 = (f32[128,512]{1,0:T(8,128)}, bf16[256,512]{1,0:T(8,128)(2,1)}) custom-call(bf16[512,128]{1,0:T(8,128)(2,1)} %get-tuple-element.122.refs_0_, bf16[512,128]{1,0:T(8,128)(2,1)} %get-tuple-element.94.refs_0_.refs_1_, bf16[256,384]{1,0:T(8,128)(2,1)} %get-tuple-element.79.refs_0_.refs_2_, ...), custom_call_target="tpu_custom_call" | custom-call | flops 1 | bytes 1 | tf_op jit(solution)/shard_map/pallas_call | solution.py:451
  89.8 5.8 %collective-permute-done.5 = bf16[192,512]{1,0:T(8,128)(2,1)S(1)} collective-permute-done((bf16[192,512]{1,0:T(8,128)(2,1)S(1)}, bf16[192,512]{1,0:T(8,128)(2,1)S(1)}, u32[]{:S(2)}, u32[]{:S(2)}) %collective-permute-start.5) | collective-permute-done | bytes 196640 | tf_op jit(solution)/shard_map/ppermute | solution.py:470
  95.7 0.7 collective-permute-done.3
  96.5 2.0 %collective-permute-start.6 = (bf16[256,512]{1,0:T(8,128)(2,1)S(1)}, bf16[256,512]{1,0:T(8,128)(2,1)S(1)}, u32[]{:S(2)}, u32[]{:S(2)}) collective-permute-start(bf16[256,512]{1,0:T(8,128)(2,1)S(1)} %fusion.2), channel_id=1, source_target_pairs={{0,4},{1,5},{2,6},{3,7},{4,0},{5,1},{6,2},{7,3},{8,12},{9,13},{10,... | collective-permute-start | bytes 786440 | tf_op jit(solution)/shard_map/ppermute | solution.py:470
  98.7 9.2 %collective-permute-done.7 = bf16[192,512]{1,0:T(8,128)(2,1)S(1)} collective-permute-done((bf16[192,512]{1,0:T(8,128)(2,1)S(1)}, bf16[192,512]{1,0:T(8,128)(2,1)S(1)}, u32[]{:S(2)}, u32[]{:S(2)}) %collective-permute-start.7) | collective-permute-done | bytes 196640 | tf_op jit(solution)/shard_map/ppermute | solution.py:470
  108.0 1.5 collective-permute-start.8
  109.6 0.9 collective-permute-start.10
  110.5 3.9 %shard_map.190.refs_4_ = f32[768,512]{1,0:T(8,128)} custom-call(bf16[768,512]{1,0:T(8,128)(2,1)} %refs_0_.3, bf16[512,512]{1,0:T(8,128)(2,1)} %get-tuple-element.128.refs_17_.refs_18_.refs_11_.refs_4_.refs_1_, bf16[256,512]{1,0:T(8,128)(2,1)} %get-tuple-element.129.refs_2_.refs_5_, bf16[1536,512]{1,0:T(8,128)(2,1)} %refs_3_.7, ...), custom_call_target="tpu_custom_call" | custom-call | flops 1 | bytes 1 | tf_op jit(solution)/shard_map/pallas_call | solution.py:451
  114.8 6.1 %collective-permute-done.9 = bf16[128,512]{1,0:T(8,128)(2,1)S(1)} collective-permute-done((bf16[128,512]{1,0:T(8,128)(2,1)S(1)}, bf16[128,512]{1,0:T(8,128)(2,1)S(1)}, u32[]{:S(2)}, u32[]{:S(2)}) %collective-permute-start.9) | collective-permute-done | bytes 131104 | tf_op jit(solution)/shard_map/ppermute | solution.py:470
  121.2 4.0 %collective-permute-start.12 = (bf16[768,512]{1,0:T(8,128)(2,1)S(1)}, bf16[768,512]{1,0:T(8,128)(2,1)S(1)}, u32[]{:S(2)}, u32[]{:S(2)}) collective-permute-start(bf16[768,512]{1,0:T(8,128)(2,1)S(1)} %maximum_select_fusion), channel_id=1, source_target_pairs={{0,1},{1,0},{2,3},{3,2},{4,5},{5,4},{6,7},{7,6},{8,9},{9,8},{10,11... | collective-permute-start | bytes 2359304 | tf_op jit(solution)/shard_map/ppermute | solution.py:470
  125.3 7.9 %collective-permute-done.11 = bf16[256,512]{1,0:T(8,128)(2,1)S(1)} collective-permute-done((bf16[256,512]{1,0:T(8,128)(2,1)S(1)}, bf16[256,512]{1,0:T(8,128)(2,1)S(1)}, u32[]{:S(2)}, u32[]{:S(2)}) %collective-permute-start.11) | collective-permute-done | bytes 262176 | tf_op jit(solution)/shard_map/ppermute | solution.py:470
  133.8 1.1 collective-permute-start.14
  134.9 4.2 %all-to-all-start.4 = ((bf16[16,16,512]{2,1,0:T(8,128)(2,1)}), bf16[16,16,512]{2,1,0:T(8,128)(2,1)S(1)}, u32[]{:S(2)}, u32[]{:S(2)}) async-start(bf16[16,16,512]{2,1,0:T(8,128)(2,1)} %bitcast.34), calls=%async_computation.4 | async-start | bytes 524288 | tf_op jit(solution)/shard_map/all_to_all | solution.py:505
  139.3 0.8 slice.9
  140.1 1.0 pad_maximum_fusion.1
  141.1 9.0 %all-to-all-done.4 = bf16[16,16,512]{2,1,0:T(8,128)(2,1)S(1)} async-done(((bf16[16,16,512]{2,1,0:T(8,128)(2,1)}), bf16[16,16,512]{2,1,0:T(8,128)(2,1)S(1)}, u32[]{:S(2)}, u32[]{:S(2)}) %all-to-all-start.4) | async-done | bytes 262176 | tf_op jit(solution)/shard_map/all_to_all | solution.py:505
  150.8 2.0 %shard_map.191 = f32[128,512]{1,0:T(8,128)} custom-call(f32[128,512]{1,0:T(8,128)} %get-tuple-element.89.refs_0_, f32[128,512]{1,0:T(8,128)} %get-tuple-element.124.refs_1_, bf16[256,128]{1,0:T(8,128)(2,1)} %get-tuple-element.82.refs_5_.refs_2_, bf16[256,512]{1,0:T(8,128)(2,1)} %bitcast.68, f32[768,512]{1,0:T(8,128)} %shard_map.190.refs_4_), custom_call_target="tpu_custom_call" | custom-call | flops 1 | bytes 1 | tf_op jit(solution)/shard_map/pallas_call | solution.py:451
  152.9 1.0 broadcast_select_fusion.6
  153.8 1.2 pad_maximum_fusion
  (42 shorter events, 3.0 us)
Async XLA Ops:
  2.3 13.0 %all-to-all-start = ((s32[16,1,16]{2,1,0:T(1,128)}), s32[16,1,16]{2,1,0:T(1,128)S(1)}, u32[]{:S(2)}, u32[]{:S(2)}) async-start(s32[16,1,16]{2,1,0:T(1,128)} %bitcast.79), calls=%async_computation | async-start | bytes 16384 | tf_op jit(solution)/shard_map/all_to_all | solution.py:535
  15.4 0.6 copy-start.5
  18.0 13.6 %all-to-all-start.1 = ((bf16[16,16,512]{2,1,0:T(8,128)(2,1)}), bf16[16,16,512]{2,1,0:T(8,128)(2,1)S(1)}, u32[]{:S(2)}, u32[]{:S(2)}) async-start(bf16[16,16,512]{2,1,0:T(8,128)(2,1)} %bitcast.76), calls=%async_computation.1 | async-start | bytes 524288 | tf_op jit(solution)/shard_map/all_to_all | solution.py:505
  31.6 0.7 copy-start.2
  36.6 13.5 %all-to-all-start.2 = ((bf16[16,16,512]{2,1,0:T(8,128)(2,1)}), bf16[16,16,512]{2,1,0:T(8,128)(2,1)S(1)}, u32[]{:S(2)}, u32[]{:S(2)}) async-start(bf16[16,16,512]{2,1,0:T(8,128)(2,1)} %bitcast.70), calls=%async_computation.2 | async-start | bytes 524288 | tf_op jit(solution)/shard_map/all_to_all | solution.py:505
  50.1 0.7 copy-start.4
  56.2 4.3 %collective-permute-start = (bf16[768,512]{1,0:T(8,128)(2,1)}, bf16[768,512]{1,0:T(8,128)(2,1)S(1)}, u32[]{:S(2)}, u32[]{:S(2)}) collective-permute-start(bf16[768,512]{1,0:T(8,128)(2,1)} %get-tuple-element.93.refs_7_), channel_id=1, source_target_pairs={{0,1},{1,0},{2,3},{3,2},{4,5},{5,4},{6,7},{7,6},{8,9},{9,8},{10,11... | collective-permute-start | bytes 2359304 | tf_op jit(solution)/shard_map/ppermute | solution.py:470
  56.9 12.9 %all-to-all-start.3 = ((bf16[16,16,512]{2,1,0:T(8,128)(2,1)}), bf16[16,16,512]{2,1,0:T(8,128)(2,1)S(1)}, u32[]{:S(2)}, u32[]{:S(2)}) async-start(bf16[16,16,512]{2,1,0:T(8,128)(2,1)} %bitcast.75), calls=%async_computation.3 | async-start | bytes 524288 | tf_op jit(solution)/shard_map/all_to_all | solution.py:505
  61.9 14.0 %collective-permute-start.1 = (bf16[384,512]{1,0:T(8,128)(2,1)S(1)}, bf16[384,512]{1,0:T(8,128)(2,1)S(1)}, u32[]{:S(2)}, u32[]{:S(2)}) collective-permute-start(bf16[384,512]{1,0:T(8,128)(2,1)S(1)} %get-tuple-element.156), channel_id=1, source_target_pairs={{0,2},{1,3},{2,0},{3,1},{4,6},{5,7},{6,4},{7,5},{8,10},{9,11},{10,... | collective-permute-start | bytes 1179656 | tf_op jit(solution)/shard_map/ppermute | solution.py:470
  69.7 0.7 copy-start.1
  75.9 5.6 %collective-permute-start.2 = (bf16[1024,512]{1,0:T(8,128)(2,1)}, bf16[1024,512]{1,0:T(8,128)(2,1)S(1)}, u32[]{:S(2)}, u32[]{:S(2)}) collective-permute-start(bf16[1024,512]{1,0:T(8,128)(2,1)} %get-tuple-element.113.refs_12_), channel_id=1, source_target_pairs={{0,1},{1,0},{2,3},{3,2},{4,5},{5,4},{6,7},{7,6},{8,9},{9,8},{10,11... | collective-permute-start | bytes 3145736 | tf_op jit(solution)/shard_map/ppermute | solution.py:470
  76.7 7.5 %collective-permute-start.4 = (bf16[192,512]{1,0:T(8,128)(2,1)S(1)}, bf16[192,512]{1,0:T(8,128)(2,1)S(1)}, u32[]{:S(2)}, u32[]{:S(2)}) collective-permute-start(bf16[192,512]{1,0:T(8,128)(2,1)S(1)} %fusion.4), channel_id=1, source_target_pairs={{0,4},{1,5},{2,6},{3,7},{4,0},{5,1},{6,2},{7,3},{8,12},{9,13},{10,... | collective-permute-start | bytes 589832 | tf_op jit(solution)/shard_map/ppermute | solution.py:470
  83.5 12.9 %collective-permute-start.3 = (bf16[512,512]{1,0:T(8,128)(2,1)}, bf16[512,512]{1,0:T(8,128)(2,1)S(1)}, u32[]{:S(2)}, u32[]{:S(2)}) collective-permute-start(bf16[512,512]{1,0:T(8,128)(2,1)} %fusion), channel_id=1, source_target_pairs={{0,2},{1,3},{2,0},{3,1},{4,6},{5,7},{6,4},{7,5},{8,10},{9,11},{10,... | collective-permute-start | bytes 1572872 | tf_op jit(solution)/shard_map/ppermute | solution.py:470
  84.2 11.4 %collective-permute-start.5 = (bf16[192,512]{1,0:T(8,128)(2,1)S(1)}, bf16[192,512]{1,0:T(8,128)(2,1)S(1)}, u32[]{:S(2)}, u32[]{:S(2)}) collective-permute-start(bf16[192,512]{1,0:T(8,128)(2,1)S(1)} %fusion.1), channel_id=1, source_target_pairs={{0,8},{1,9},{2,10},{3,11},{4,12},{5,13},{6,14},{7,15},{8,0},{9,1},... | collective-permute-start | bytes 589832 | tf_op jit(solution)/shard_map/ppermute | solution.py:470
  85.8 4.0 %copy-start = (bf16[1024,512]{1,0:T(8,128)(2,1)S(1)}, bf16[1024,512]{1,0:T(8,128)(2,1)}, u32[]{:S(2)}) copy-start(bf16[1024,512]{1,0:T(8,128)(2,1)} %shard_map.188.refs_7_) | copy-start | bytes 3145732
  96.5 11.4 %collective-permute-start.6 = (bf16[256,512]{1,0:T(8,128)(2,1)S(1)}, bf16[256,512]{1,0:T(8,128)(2,1)S(1)}, u32[]{:S(2)}, u32[]{:S(2)}) collective-permute-start(bf16[256,512]{1,0:T(8,128)(2,1)S(1)} %fusion.2), channel_id=1, source_target_pairs={{0,4},{1,5},{2,6},{3,7},{4,0},{5,1},{6,2},{7,3},{8,12},{9,13},{10,... | collective-permute-start | bytes 786440 | tf_op jit(solution)/shard_map/ppermute | solution.py:470
  98.6 9.4 %collective-permute-start.7 = (bf16[192,512]{1,0:T(8,128)(2,1)S(1)}, bf16[192,512]{1,0:T(8,128)(2,1)S(1)}, u32[]{:S(2)}, u32[]{:S(2)}) collective-permute-start(bf16[192,512]{1,0:T(8,128)(2,1)S(1)} %add_convert_fusion.3), channel_id=1, source_target_pairs={{0,4},{1,5},{2,6},{3,7},{4,0},{5,1},{6,2},{7,3},{8,12},{9,13},{10,... | collective-permute-start | bytes 589832 | tf_op jit(solution)/shard_map/ppermute | solution.py:470
  108.0 6.5 %collective-permute-start.8 = (bf16[128,512]{1,0:T(8,128)(2,1)S(1)}, bf16[128,512]{1,0:T(8,128)(2,1)S(1)}, u32[]{:S(2)}, u32[]{:S(2)}) collective-permute-start(bf16[128,512]{1,0:T(8,128)(2,1)S(1)} %fusion.5), channel_id=1, source_target_pairs={{0,8},{1,9},{2,10},{3,11},{4,12},{5,13},{6,14},{7,15},{8,0},{9,1},... | collective-permute-start | bytes 393224 | tf_op jit(solution)/shard_map/ppermute | solution.py:470
  109.6 11.2 %collective-permute-start.10 = (bf16[384,512]{1,0:T(8,128)(2,1)S(1)}, bf16[384,512]{1,0:T(8,128)(2,1)S(1)}, u32[]{:S(2)}, u32[]{:S(2)}) collective-permute-start(bf16[384,512]{1,0:T(8,128)(2,1)S(1)} %maximum_select_fusion.2), channel_id=1, source_target_pairs={{0,2},{1,3},{2,0},{3,1},{4,6},{5,7},{6,4},{7,5},{8,10},{9,11},{10,... | collective-permute-start | bytes 1179656 | tf_op jit(solution)/shard_map/ppermute | solution.py:470
  114.7 6.2 %collective-permute-start.9 = (bf16[128,512]{1,0:T(8,128)(2,1)S(1)}, bf16[128,512]{1,0:T(8,128)(2,1)S(1)}, u32[]{:S(2)}, u32[]{:S(2)}) collective-permute-start(bf16[128,512]{1,0:T(8,128)(2,1)S(1)} %fusion.3), channel_id=1, source_target_pairs={{0,8},{1,9},{2,10},{3,11},{4,12},{5,13},{6,14},{7,15},{8,0},{9,1},... | collective-permute-start | bytes 393224 | tf_op jit(solution)/shard_map/ppermute | solution.py:470
  121.2 12.1 %collective-permute-start.12 = (bf16[768,512]{1,0:T(8,128)(2,1)S(1)}, bf16[768,512]{1,0:T(8,128)(2,1)S(1)}, u32[]{:S(2)}, u32[]{:S(2)}) collective-permute-start(bf16[768,512]{1,0:T(8,128)(2,1)S(1)} %maximum_select_fusion), channel_id=1, source_target_pairs={{0,1},{1,0},{2,3},{3,2},{4,5},{5,4},{6,7},{7,6},{8,9},{9,8},{10,11... | collective-permute-start | bytes 2359304 | tf_op jit(solution)/shard_map/ppermute | solution.py:470
  125.3 8.0 %collective-permute-start.11 = (bf16[256,512]{1,0:T(8,128)(2,1)S(1)}, bf16[256,512]{1,0:T(8,128)(2,1)S(1)}, u32[]{:S(2)}, u32[]{:S(2)}) collective-permute-start(bf16[256,512]{1,0:T(8,128)(2,1)S(1)} %maximum_select_fusion.3), channel_id=1, source_target_pairs={{0,4},{1,5},{2,6},{3,7},{4,0},{5,1},{6,2},{7,3},{8,12},{9,13},{10,... | collective-permute-start | bytes 786440 | tf_op jit(solution)/shard_map/ppermute | solution.py:470
  133.5 16.6 %collective-permute-start.13 = (bf16[512,512]{1,0:T(8,128)(2,1)S(1)}, bf16[512,512]{1,0:T(8,128)(2,1)S(1)}, u32[]{:S(2)}, u32[]{:S(2)}) collective-permute-start(bf16[512,512]{1,0:T(8,128)(2,1)S(1)} %maximum_select_fusion.1), channel_id=1, source_target_pairs={{0,2},{1,3},{2,0},{3,1},{4,6},{5,7},{6,4},{7,5},{8,10},{9,11},{10,... | collective-permute-start | bytes 1572872 | tf_op jit(solution)/shard_map/ppermute | solution.py:470
  133.8 16.3 %collective-permute-start.14 = (bf16[512,512]{1,0:T(8,128)(2,1)S(1)}, bf16[512,512]{1,0:T(8,128)(2,1)S(1)}, u32[]{:S(2)}, u32[]{:S(2)}) collective-permute-start(bf16[512,512]{1,0:T(8,128)(2,1)S(1)} %maximum_select_fusion.1), channel_id=1, source_target_pairs={{0,1},{1,0},{2,3},{3,2},{4,5},{5,4},{6,7},{7,6},{8,9},{9,8},{10,11... | collective-permute-start | bytes 1572872 | tf_op jit(solution)/shard_map/ppermute | solution.py:470
  134.9 15.2 %all-to-all-start.4 = ((bf16[16,16,512]{2,1,0:T(8,128)(2,1)}), bf16[16,16,512]{2,1,0:T(8,128)(2,1)S(1)}, u32[]{:S(2)}, u32[]{:S(2)}) async-start(bf16[16,16,512]{2,1,0:T(8,128)(2,1)} %bitcast.34), calls=%async_computation.4 | async-start | bytes 524288 | tf_op jit(solution)/shard_map/all_to_all | solution.py:505
  150.1 0.7 copy-start.3
  150.1 2.7 %collective-permute-start.15 = (bf16[512,512]{1,0:T(8,128)(2,1)S(1)}, bf16[512,512]{1,0:T(8,128)(2,1)S(1)}, u32[]{:S(2)}, u32[]{:S(2)}) collective-permute-start(bf16[512,512]{1,0:T(8,128)(2,1)S(1)} %collective-permute-done.13), channel_id=1, source_target_pairs={{0,1},{1,0},{2,3},{3,2},{4,5},{5,4},{6,7},{7,6},{8,9},{9,8},{10,11... | collective-permute-start | bytes 1572872 | tf_op jit(solution)/shard_map/ppermute | solution.py:470

commit v9 on v8

--- a/solution.py
+++ b/solution.py
@@ -84,6 +84,12 @@
     return (inv_scale * centered).astype(BF16)
 
 
+def loading(source, buffer, sem):
+    copy = pltpu.make_async_copy(source, buffer, sem)
+    copy.start()
+    return copy
+
+
 def ask_kernel(dest_ref, remote_ref, ask_ref):
     domains, slots = ask_ref.shape
     dest_marks, rank = slot_ranks(to_column(dest_ref[...]).astype(jnp.int32), domains)
@@ -92,7 +98,8 @@
     ask_ref[...] = dot_rows(dest_marks, wanted).astype(jnp.int32)
 
 
-def reply_kernel(asked_ref, nodes_ref, reply_ref, asked_marks_ref):
+def reply_kernel(asked_hbm, nodes_ref, reply_ref, asked_marks_ref, asked_ref, sem):
+    loading(asked_hbm, asked_ref, sem).wait()
     domains, slots = asked_ref.shape
     total = domains * slots
     shift = slots.bit_length() - 1
@@ -178,7 +185,7 @@
     receivers_ref,
     edges_ref,
     nodes_ref,
-    far_ref,
+    far_hbm,
     w_in_ref,
     w_out_ref,
     inner_total_ref,
@@ -190,7 +197,10 @@
     scale_ref,
     total_ref,
     outgoing_ref,
+    far_ref,
+    sem,
 ):
+    loading(far_hbm, far_ref, sem).wait()
     base = nodes_ref.shape[0]
     nodes, far = nodes_ref[...], far_ref[...]
 
@@ -224,7 +234,7 @@
 
 def node_kernel(
     me_ref,
-    incoming_ref,
+    incoming_hbm,
     asked_marks_ref,
     total_ref,
     nodes_ref,
@@ -237,7 +247,10 @@
     reply_ref,
     keep_ref,
     send_ref,
+    incoming_ref,
+    sem,
 ):
+    loading(incoming_hbm, incoming_ref, sem).wait()
     latent = nodes_ref.shape[1]
     half = latent // 2
     nodes, asked_marks = nodes_ref[...], asked_marks_ref[...]
@@ -276,6 +289,7 @@
 
 
 def inner_backward_kernel(
+    me_ref,
     receivers_ref,
     agg_grad_ref,
     ct_ref,
@@ -283,9 +297,15 @@
     scale_ref,
     slope_ref,
     w_out_ref,
+    edges_ref,
+    sender_ref,
+    receiver_ref,
+    hidden_ref,
     grad_out_ref,
     grad_pre_ref,
+    part_ref,
 ):
+    latent = w_out_ref.shape[1]
     grad_out, grad_pre = edge_backward(
         ct_ref[...],
         dot(receivers_ref[...], agg_grad_ref[...]),
@@ -296,6 +316,20 @@
     )
     grad_out_ref[...] = grad_out
     grad_pre_ref[...] = grad_pre
+
+    @pl.when(pl.program_id(0) == 0)
+    def _():
+        part_ref[...] = jnp.zeros_like(part_ref)
+
+    @pl.when((me_ref[0] & 1) != 0)
+    def _():
+        part_ref[:latent] += dot_rows(edges_ref[...], grad_pre)
+        part_ref[latent:] += dot_rows(sender_ref[...], grad_pre)
+
+    @pl.when((me_ref[0] & 1) == 0)
+    def _():
+        part_ref[:latent] += dot_rows(receiver_ref[...], grad_pre)
+        part_ref[latent:] += dot_rows(hidden_ref[...], grad_out)
 
 
 def fetch_factors(half, sources, buffers, sems, wait):
@@ -324,45 +358,59 @@
         each(high)
 
 
-def edge_rows(half, buffers, cut_pre, cut_out, out_ref):
-    latent = cut_pre.shape[1]
-    first, first_cut, second, second_cut, first_right, second_right = buffers
-    chosen = jnp.where(half == 0, cut_pre.astype(F32), cut_out.astype(F32)).astype(BF16)
-    out_ref[:latent] = (
-        dot_rows(first[...], first_right[...]) + dot_rows(first_cut[...], cut_pre)
-    ).astype(BF16)
-    out_ref[latent:] = (
-        dot_rows(second[...], second_right[...]) + dot_rows(second_cut[...], chosen)
-    ).astype(BF16)
+def place_rows(me_ref, index, latent):
+    return pl.ds(pl.multiple_of((index ^ ((me_ref[0] >> 1) & 1)) * latent, latent), latent)
 
 
 def cut_backward_kernel(
     me_ref,
     receivers_ref,
     agg_grad_ref,
-    far_grad_ref,
+    far_grad_hbm,
     ct_ref,
     normed_ref,
     scale_ref,
     slope_ref,
     w_out_ref,
-    *refs,
+    part_hbm,
+    edges_ref,
+    sender_ref,
+    receiver_ref,
+    hidden_ref,
+    grad_out_ref,
+    grad_pre_ref,
+    out_ref,
+    far_grad_ref,
+    part_ref,
+    sems,
 ):
-    sources, (grad_out_ref, grad_pre_ref, out_ref), rest = refs[:9], refs[9:12], refs[12:]
-    buffers, sems = rest[:-1], rest[-1]
-    half = 1 - (me_ref[0] & 1)
-    fetch_factors(half, sources, buffers, sems, False)
+    latent = w_out_ref.shape[1]
+    far_copy = loading(far_grad_hbm, far_grad_ref, sems.at[0])
+    part_copy = loading(part_hbm, part_ref, sems.at[1])
     base = agg_grad_ref.shape[0]
-    target = dot(receivers_ref[:, :base], agg_grad_ref[...]) + dot(
-        receivers_ref[:, base:], far_grad_ref[...]
-    )
+    near_grads = dot(receivers_ref[:, :base], agg_grad_ref[...])
+    far_copy.wait()
+    target = near_grads + dot(receivers_ref[:, base:], far_grad_ref[...])
     grad_out, grad_pre = edge_backward(
         ct_ref[...], target, normed_ref[...], scale_ref[...], slope_ref[...], w_out_ref[...]
     )
     grad_out_ref[...] = grad_out
     grad_pre_ref[...] = grad_pre
-    fetch_factors(half, sources, buffers, sems, True)
-    edge_rows(half, buffers, grad_pre, grad_out, out_ref)
+    part_copy.wait()
+
+    def put(index, value):
+        rows = pl.ds(index * latent, latent)
+        out_ref[place_rows(me_ref, index, latent)] = (part_ref[rows] + value).astype(BF16)
+
+    @pl.when((me_ref[0] & 1) != 0)
+    def _():
+        put(0, dot_rows(edges_ref[...], grad_pre))
+        put(1, dot_rows(sender_ref[...], grad_pre))
+
+    @pl.when((me_ref[0] & 1) == 0)
+    def _():
+        put(0, dot_rows(receiver_ref[...], grad_pre))
+        put(1, dot_rows(hidden_ref[...], grad_out))
 
 
 def edge_weights_kernel(me_ref, cut_out_ref, cut_pre_ref, *refs):
@@ -371,7 +419,16 @@
     half = me_ref[0] & 1
     fetch_factors(half, sources, buffers, sems, False)
     fetch_factors(half, sources, buffers, sems, True)
-    edge_rows(half, buffers, cut_pre_ref[...], cut_out_ref[...], out_ref)
+    cut_pre, cut_out = cut_pre_ref[...], cut_out_ref[...]
+    latent = cut_pre.shape[1]
+    first, first_cut, second, second_cut, first_right, second_right = buffers
+    chosen = jnp.where(half == 0, cut_pre.astype(F32), cut_out.astype(F32)).astype(BF16)
+    out_ref[place_rows(me_ref, 0, latent)] = (
+        dot_rows(first[...], first_right[...]) + dot_rows(first_cut[...], cut_pre)
+    ).astype(BF16)
+    out_ref[place_rows(me_ref, 1, latent)] = (
+        dot_rows(second[...], second_right[...]) + dot_rows(second_cut[...], chosen)
+    ).astype(BF16)
 
 
 def input_grads_kernel(
@@ -416,13 +473,17 @@
         out_ref[...] = ct_ref[...].astype(F32) + dot_cols(cut_pre_ref[...], w_edge_ref[...])
 
 
-def node_grads_kernel(self_ref, local_ref, asked_marks_ref, returned_ref, out_ref):
+def node_grads_kernel(
+    self_ref, local_ref, asked_marks_ref, returned_hbm, out_ref, returned_ref, sem
+):
+    loading(returned_hbm, returned_ref, sem).wait()
     out_ref[...] = (
         self_ref[...] + local_ref[...] + dot_rows(asked_marks_ref[...], returned_ref[...])
     )
 
 
 VMEM = pl.BlockSpec(memory_space=pltpu.VMEM)
+HBM = pl.BlockSpec(memory_space=pltpu.HBM)
 SMEM = pl.BlockSpec(memory_space=pltpu.SMEM)
 ANY = pl.BlockSpec(memory_space=pl.ANY)
 
@@ -497,6 +558,12 @@
 def joined(parts, bit):
     orders = [jnp.concatenate(parts), jnp.concatenate(parts[::-1])]
     return jnp.where(place_of(bit) == 0, *orders)
+
+
+def put_quarter(rows, piece, quarter):
+    start = (jnp.minimum(quarter, 2) * piece.shape[0], 0)
+    kept = lax.dynamic_slice(rows, start, piece.shape)
+    return lax.dynamic_update_slice(rows, jnp.where(quarter < 3, piece, kept), start)
 
 
 def exchange(rows, domains):
@@ -542,6 +609,8 @@
         reply_kernel,
         [shaped(BF16, total_slots, latent), shaped(BF16, total_slots, node_rows)],
         [asked, nodes],
+        [HBM, VMEM],
+        scratch=[pltpu.VMEM(asked.shape, jnp.int32), pltpu.SemaphoreType.DMA],
     )
     far = exchange(reply, domains)
 
@@ -614,7 +683,7 @@
             all_spec(cut_receivers),
             last_rows(edges),
             all_spec(nodes),
-            all_spec(far),
+            HBM,
             all_spec(w_edge_in),
             all_spec(w_edge_out),
             all_spec(inner_total),
@@ -622,6 +691,7 @@
         [rows_spec(width) for width in saved_widths[2:]]
         + [all_spec(nodes), rows_spec(latent, total_slots)],
         (1,),
+        [pltpu.VMEM(far.shape, BF16), pltpu.SemaphoreType.DMA],
     )
     incoming = exchange(outgoing, domains)
     new_edges = line.run(
@@ -646,14 +716,16 @@
         ]
         + [shaped(BF16, 3 * latent // 2, latent)] * 2,
         [me, incoming, asked_marks, total, nodes, ct_nodes, w_node_in, w_node_out],
-        [SMEM] + [VMEM] * 7,
+        [SMEM, HBM] + [VMEM] * 6,
+        scratch=[pltpu.VMEM(incoming.shape, BF16), pltpu.SemaphoreType.DMA],
     )
     far_grad = exchange(grad_reply, domains)
     node_sum = added(node_keep, across(node_send, domains, 1))
-    inner_out, inner_pre = line.run(
+    inner_out, inner_pre, inner_part = line.run(
         inner_backward_kernel,
-        [shaped(BF16, inner_rows, latent)] * 2,
-        [
+        [shaped(BF16, inner_rows, latent)] * 2 + [shaped(F32, 2 * latent, latent)],
+        [
+            me,
             inner_receivers,
             agg_grad,
             ct_edges,
@@ -661,8 +733,13 @@
             inner_scale,
             inner_slope,
             w_edge_out,
+            edges,
+            inner_sender,
+            inner_receiver,
+            inner_hidden,
         ],
         [
+            SMEM,
             rows_spec(node_rows),
             all_spec(agg_grad),
             rows_spec(latent),
@@ -670,14 +747,16 @@
             rows_spec(1),
             rows_spec(latent),
             all_spec(w_edge_out),
-        ],
-        [rows_spec(latent)] * 2,
+        ]
+        + [rows_spec(latent)] * 4,
+        [rows_spec(latent)] * 2
+        + [pl.BlockSpec((2 * latent, latent), lambda step: (0, 0))],
         (blocks,),
     )
     bits = index_bits(domains)
     node_own, node_sent = split([node_sum], 1)
     node_parts = [*node_own, across(node_sent, domains, 2)]
-    far_grad, node_sum, inner_pre = fence(far_grad, node_sum, inner_pre)
+    far_grad, node_sum, inner_part = fence(far_grad, node_sum, inner_part)
     factors = [
         edges,
         inner_sender,
@@ -705,23 +784,33 @@
             cut_scale,
             cut_slope,
             w_edge_out,
-        ]
-        + factors,
+            inner_part,
+            edges,
+            cut_sender,
+            cut_receiver,
+            cut_hidden,
+        ],
         [
             SMEM,
             all_spec(cut_receivers),
             all_spec(agg_grad),
-            all_spec(far_grad),
+            HBM,
             last_rows(ct_edges),
             all_spec(cut_normed),
             all_spec(cut_scale),
             all_spec(cut_slope),
             all_spec(w_edge_out),
+            HBM,
+            last_rows(edges),
         ]
-        + [ANY] * len(factors),
+        + [all_spec(cut_sender)] * 3,
         [rows_spec(latent)] * 2 + [rows_spec(latent, 2 * latent)],
         (1,),
-        buffers,
+        [
+            pltpu.VMEM(far_grad.shape, BF16),
+            pltpu.VMEM(inner_part.shape, F32),
+            pltpu.SemaphoreType.DMA((2,)),
+        ],
     )
     edge_send, place, *node_parts = fence(edge_send, me, *node_parts)
     received = across(edge_send, domains, 1)
@@ -734,7 +823,9 @@
         [SMEM, VMEM, VMEM] + [ANY] * len(factors),
         scratch=buffers,
     )
-    edge_own, edge_sent = split(fence(edge_keep, received), 1)
+    edge_keep, received = fence(edge_keep, received)
+    edge_own = [edge_keep[:latent], received[:latent]]
+    edge_sent = added(edge_keep[latent:], received[latent:])
     edge_sent, inner_pre, cut_pre = fence(edge_sent, inner_pre, cut_pre)
     node_got = fence(node_got, edge_sent)[0]
     edge_got = across(edge_sent, domains, 2)
@@ -758,10 +849,7 @@
         edge_got, node_sum, inner_pre, cut_pre, local_grad
     )
     edge_own, edge_sent = split([*edge_own, edge_got], 2)
-    edge_got, *node_parts = fence(across(edge_sent, domains, 4), *handed(node_sum, domains, 2))
-    edge_own, edge_sent = split([*edge_own, edge_got], 3)
-    edge_got = across(edge_sent, domains, 8)
-    node_parts = handed(joined(node_parts, 2), domains, 1)
+    edge_got = across(edge_sent, domains, 4)
     grad_edges = line.run(
         functools.partial(edge_grads_kernel, blocks=blocks),
         shaped(F32, *edges.shape),
@@ -775,46 +863,50 @@
         [rows_spec(latent)],
         (blocks + 1,),
     )
-    edge_got, grad_edges, outgoing_grad = fence(edge_got, grad_edges, outgoing_grad)
+    edge_got, node_sum, grad_edges = fence(edge_got, node_sum, grad_edges)
+    edge_own, edge_sent = split([*edge_own, edge_got], 3)
+    edge_got, *node_parts = fence(across(edge_sent, domains, 8), *handed(node_sum, domains, 2))
     edge_sum = added(*edge_own, edge_got)
     for bit in bits[4:]:
         own, sent = split([edge_sum], bit)
         edge_sum = added(*own, across(sent, domains, 1 << bit))
     for bit in bits[:3:-1]:
         edge_sum = joined(handed(edge_sum, domains, bit), bit)
+    node_parts = handed(joined(node_parts, 2), domains, 1)
+    edge_parts = fence(*handed(edge_sum, domains, 3))
+    edge_parts = handed(joined(edge_parts, 3), domains, 2)
+    *edge_parts, node_sum, other_sum, outgoing_grad = fence(
+        *edge_parts, *node_parts, outgoing_grad
+    )
+    edge_sum = joined(edge_parts, 2)
+    node_sum = joined([node_sum, other_sum], 1)
+    far, near = across(edge_sum, domains, 2), across(edge_sum, domains, 1)
+    others = across(node_sum, domains, 1)
     returned = exchange(outgoing_grad, domains)
-    *edge_parts, node_sum, other_sum = fence(*handed(edge_sum, domains, 3), *node_parts)
-    edge_parts = handed(joined(edge_parts, 3), domains, 2)
-    node_sum = joined([node_sum, other_sum], 1)
-    others = across(node_sum, domains, 1)
-    *edge_parts, node_sum, others = fence(*edge_parts, node_sum, others)
-    edge_sum = joined(edge_parts, 2)
-    edge_parts = handed(edge_sum, domains, 1) + [across(edge_sum, domains, 1)]
-    lower, left = place_of(0) == 0, place_of(1) == 0
+    lower = place_of(0) == 0
     low_rows, high_rows = jnp.where(lower, node_sum, others), jnp.where(lower, others, node_sum)
     cut_at = 2 * latent - low_rows.shape[0]
     grad_node_in = jnp.concatenate([low_rows, high_rows[:cut_at]])
     grad_node_out = high_rows[cut_at:]
-    mine, far, near, grad_node_in, grad_node_out, returned = fence(
-        *edge_parts, grad_node_in, grad_node_out, returned
+    mine = place_of(0) * 2 + place_of(1)
+    rows = put_quarter(jnp.zeros((3 * latent, latent), BF16), edge_sum, mine)
+    rows = put_quarter(rows, near, mine ^ 2)
+    far, near, edge_sum, rows, grad_node_in, grad_node_out, returned = fence(
+        far, near, edge_sum, rows, grad_node_in, grad_node_out, returned
     )
     corner = across(far, domains, 1)
+    rows = put_quarter(rows, far, mine ^ 1)
+    last = jnp.where(mine == 3, edge_sum, jnp.where(mine == 1, near, far))
     grad_nodes = line.run(
         node_grads_kernel,
         shaped(F32, node_rows, latent),
         [self_grad, local_grad, asked_marks, returned],
-    )
-    own, other = [mine, far], [near, corner]
-    low_half = [jnp.where(lower, one, two) for one, two in zip(own, other)]
-    high_half = [jnp.where(lower, two, one) for one, two in zip(own, other)]
-    grad_edge_in = jnp.concatenate(
-        [
-            jnp.where(left, low_half[0], low_half[1]),
-            jnp.where(left, low_half[1], low_half[0]),
-            jnp.where(left, high_half[0], high_half[1]),
-        ]
-    )
-    grad_edge_out = jnp.where(left, high_half[1], high_half[0])
+        [VMEM, VMEM, VMEM, HBM],
+        scratch=[pltpu.VMEM(returned.shape, BF16), pltpu.SemaphoreType.DMA],
+    )
+    corner, rows, last, grad_nodes = fence(corner, rows, last, grad_nodes)
+    grad_edge_in = put_quarter(rows, corner, mine ^ 3)
+    grad_edge_out = jnp.where(mine == 0, corner, last)
     return (
         new_nodes,
         new_edges,

time: 156 us -> 156 us (level)
  waiting for transfers between devices: 55.8 us -> 42.4 us
  Pallas kernels: 48 us -> 53.8 us
  starting transfers between devices: 38.7 us -> 42.6 us
  local copies, waits for them, and re-layouts: 3.98 us -> 5.93 us
  other arithmetic: 7.81 us -> 9.62 us
    ppermute x16, waiting for transfers between devices: 29.9 us -> 21.3 us  [across(): lax.ppermute(rows, 'dom', [(device, device ^ mask) for device in range(de...]
    pallas_call x13, Pallas kernels: 48 us -> 53.8 us  [run(): pl.pallas_call(ordered, out_shape=out_shape, in_specs=specs, out_specs=[V...]
    all_to_all x4, waiting for transfers between devices: 22.2 us -> 17.3 us  [exchange(): lax.all_to_all(split, 'dom', split_axis=0, concat_axis=0, tiled=True)]
    ppermute x16, starting transfers between devices: 15.5 us -> 17.6 us  [across(): lax.ppermute(rows, 'dom', [(device, device ^ mask) for device in range(de...]
    all_to_all x4, starting transfers between devices: 15.9 us -> 17.6 us  [exchange(): lax.all_to_all(split, 'dom', split_axis=0, concat_axis=0, tiled=True)]
  transfers between devices with their start and end apart: 21 -> 21, of which waited for: 11 -> 13; matrix products, arithmetic and copies ran while one was open for 4% -> 6% of each run, Pallas kernels for 22% -> 24%
where the time goes in v9:
time: 156 us; the launch traced here: 155 us
  Pallas kernels  53.8 us (34%)
  starting transfers between devices  42.6 us (27%)
  waiting for transfers between devices  42.4 us (27%)
  other arithmetic  9.62 us (6%)
  local copies, waits for them, and re-layouts  5.93 us (4%)
    pallas_call x13, Pallas kernels, run(): pl.pallas_call(ordered, out_shape=out_shape, in_specs=specs, out_specs=[V...  53.8 us
    ppermute x16, waiting for transfers between devices, across(): lax.ppermute(rows, 'dom', [(device, device ^ mask) for device in range(de...  21.3 us
    all_to_all x4, starting transfers between devices, exchange(): lax.all_to_all(split, 'dom', split_axis=0, concat_axis=0, tiled=True)  17.6 us
    ppermute x16, starting transfers between devices, across(): lax.ppermute(rows, 'dom', [(device, device ^ mask) for device in range(de...  17.6 us
    all_to_all x4, waiting for transfers between devices, exchange(): lax.all_to_all(split, 'dom', split_axis=0, concat_axis=0, tiled=True)  17.3 us
    all_to_all x1, starting transfers between devices, shards(): asked = lax.all_to_all(ask, 'dom', split_axis=0, concat_axis=0, tiled=True)  7.32 us
    unnamed x12, local copies, waits for them, and re-layouts  3.85 us
    convert_element_type x7, other arithmetic, added(): return sum((part.astype(F32) for part in parts)).astype(BF16)  3.84 us
  transfers between devices with their start and end apart: 21, of which 13 were waited for; matrix products, arithmetic and copies ran while one was open for 6% of the time, Pallas kernels for 24%

profile of v9, /device:TPU:1, one launch (start us, length us, event | category | flops | bytes accessed | tf_op | source)
XLA Modules:
  0.0 155.2 jit_solution(9863804828767872748)
XLA Ops:
  0.6 1.7 %shard_map.179.refs_2_ = s32[16,16]{1,0:T(8,128)} custom-call(s32[1,128]{1,0:T(1,128)} %bitcast.71, s32[1,128]{1,0:T(1,128)} %bitcast.74), custom_call_target="tpu_custom_call" | custom-call | flops 1 | bytes 1 | tf_op jit(solution)/shard_map/pallas_call | solution.py:512
  2.3 7.3 %all-to-all-start = ((s32[16,1,16]{2,1,0:T(1,128)}), s32[16,1,16]{2,1,0:T(1,128)S(1)}, u32[]{:S(2)}, u32[]{:S(2)}) async-start(s32[16,1,16]{2,1,0:T(1,128)} %bitcast.69), calls=%async_computation | async-start | bytes 16384 | tf_op jit(solution)/shard_map/all_to_all | solution.py:602
  9.7 2.0 %shard_map.180 = (bf16[256,384]{1,0:T(8,128)(2,1)}, bf16[256,384]{1,0:T(8,128)(2,1)}) custom-call(s32[1,128]{1,0:T(1,128)} %bitcast.72, s32[1,128]{1,0:T(1,128)} %bitcast.75, s32[16,16]{1,0:T(8,128)} %shard_map.179.refs_2_), custom_call_target="tpu_custom_call" | custom-call | flops 1 | bytes 1 | tf_op jit(solution)/shard_map/pallas_call | solution.py:512
  11.7 3.7 %all-to-all-done = s32[16,1,16]{2,1,0:T(1,128)S(1)} async-done(((s32[16,1,16]{2,1,0:T(1,128)}), s32[16,1,16]{2,1,0:T(1,128)S(1)}, u32[]{:S(2)}, u32[]{:S(2)}) %all-to-all-start) | async-done | bytes 1056 | tf_op jit(solution)/shard_map/all_to_all | solution.py:602
  16.0 2.7 %shard_map.181 = (bf16[256,512]{1,0:T(8,128)(2,1)}, bf16[256,128]{1,0:T(8,128)(2,1)}) custom-call(s32[16,16]{1,0:T(8,128)} %bitcast.70, bf16[128,512]{1,0:T(8,128)(2,1)} %refs_4_.4, bf16[256,384]{1,0:T(8,128)(2,1)} %get-tuple-element.85.refs_2_.refs_1_.refs_3_), custom_call_target="tpu_custom_call" | custom-call | flops 1 | bytes 1 | tf_op jit(solution)/shard_map/pallas_call | solution.py:512
  18.7 4.1 %all-to-all-start.1 = ((bf16[16,16,512]{2,1,0:T(8,128)(2,1)}), bf16[16,16,512]{2,1,0:T(8,128)(2,1)S(1)}, u32[]{:S(2)}, u32[]{:S(2)}) async-start(bf16[16,16,512]{2,1,0:T(8,128)(2,1)} %bitcast.66), calls=%async_computation.1 | async-start | bytes 524288 | tf_op jit(solution)/shard_map/all_to_all | solution.py:572
  22.7 6.3 %shard_map.182 = (bf16[512,128]{1,0:T(8,128)(2,1)}, bf16[512,128]{1,0:T(8,128)(2,1)}, bf16[512,512]{1,0:T(8,128)(2,1)}, bf16[512,512]{1,0:T(8,128)(2,1)}, bf16[5...) custom-call(s32[2,256]{1,0:T(2,128)} %bitcast.73, ...), custom_call_target="tpu_custom_call" | custom-call | flops 1 | bytes 1 | tf_op jit(solution)/shard_map/pallas_call | solution.py:512
  29.0 3.3 %all-to-all-done.1 = bf16[16,16,512]{2,1,0:T(8,128)(2,1)S(1)} async-done(((bf16[16,16,512]{2,1,0:T(8,128)(2,1)}), bf16[16,16,512]{2,1,0:T(8,128)(2,1)S(1)}, u32[]{:S(2)}, u32[]{:S(2)}) %all-to-all-start.1) | async-done | bytes 262176 | tf_op jit(solution)/shard_map/all_to_all | solution.py:572
  33.0 5.1 %shard_map.183 = (bf16[256,512]{1,0:T(8,128)(2,1)}, bf16[256,512]{1,0:T(8,128)(2,1)}, bf16[256,512]{1,0:T(8,128)(2,1)}, f32[256,512]{1,0:T(8,128)}, f32[256,512]...) custom-call(bf16[256,384]{1,0:T(8,128)(2,1)} %get-tuple-element.84.refs_0_.refs_2_, ...), custom_call_target="tpu_custom_call" | custom-call | flops 1 | bytes 1 | tf_op jit(solution)/shard_map/pallas_call | solution.py:512
  38.1 4.0 %all-to-all-start.2 = ((bf16[16,16,512]{2,1,0:T(8,128)(2,1)}), bf16[16,16,512]{2,1,0:T(8,128)(2,1)S(1)}, u32[]{:S(2)}, u32[]{:S(2)}) async-start(bf16[16,16,512]{2,1,0:T(8,128)(2,1)} %bitcast.62), calls=%async_computation.2 | async-start | bytes 524288 | tf_op jit(solution)/shard_map/all_to_all | solution.py:572
  42.2 2.7 %shard_map.184.refs_8_ = bf16[768,512]{1,0:T(8,128)(2,1)} custom-call(bf16[768,512]{1,0:T(8,128)(2,1)} %refs_3_.8, f32[512,512]{1,0:T(8,128)} %get-tuple-element.91.refs_1_.refs_4_, f32[256,512]{1,0:T(8,128)} %get-tuple-element.92.refs_2_.refs_5_, bf16[256,512]{1,0:T(8,128)(2,1)} %get-tuple-element.89.refs_3_), custom_call_target="tpu_custom_call" | custom-call | flops 1 | bytes 1 | tf_op jit(solution)/shard_map/pallas_call | solution.py:512
  44.8 6.9 %all-to-all-done.2 = bf16[16,16,512]{2,1,0:T(8,128)(2,1)S(1)} async-done(((bf16[16,16,512]{2,1,0:T(8,128)(2,1)}), bf16[16,16,512]{2,1,0:T(8,128)(2,1)S(1)}, u32[]{:S(2)}, u32[]{:S(2)}) %all-to-all-start.2) | async-done | bytes 262176 | tf_op jit(solution)/shard_map/all_to_all | solution.py:572
  52.4 6.3 %shard_map.185 = (bf16[128,512]{1,0:T(8,128)(2,1)}, f32[128,512]{1,0:T(8,128)}, bf16[128,512]{1,0:T(8,128)(2,1)}, bf16[256,512]{1,0:T(8,128)(2,1)}, bf16[768,512]{1,0:T(8,128)(2,1)}, /*index=5*/bf16[768,512]{1,0:T(8,128)(2,1)}) custom-call(s32[1]{0:T(128)} %bitcast.refs_0_, bf16[256,512]{1,0:T(8,128)(2,1)} %bitcast.61, ...), custom_call_target="tpu_custom_call" | custom-call | flops 1 | bytes 1 | tf_op jit(solution)/shard_map/pallas_call | solution.py:512
  58.7 0.7 collective-permute-start
  59.4 3.4 %all-to-all-start.3 = ((bf16[16,16,512]{2,1,0:T(8,128)(2,1)}), bf16[16,16,512]{2,1,0:T(8,128)(2,1)S(1)}, u32[]{:S(2)}, u32[]{:S(2)}) async-start(bf16[16,16,512]{2,1,0:T(8,128)(2,1)} %bitcast.65), calls=%async_computation.3 | async-start | bytes 524288 | tf_op jit(solution)/shard_map/all_to_all | solution.py:572
  62.9 1.3 add_convert_fusion
  64.3 1.4 collective-permute-start.1
  65.6 6.0 %shard_map.186 = (bf16[512,512]{1,0:T(8,128)(2,1)}, bf16[512,512]{1,0:T(8,128)(2,1)}, f32[1024,512]{1,0:T(8,128)}) custom-call(s32[1]{0:T(128)} %bitcast.refs_0_, bf16[512,128]{1,0:T(8,128)(2,1)} %get-tuple-element.98.refs_1_, bf16[128,512]{1,0:T(8,128)(2,1)} %get-tuple-element.94.refs_2_, bf16[768,512]{1,0:T(8,128)(2,1)} %refs_0_.3, ...), custom_call_target="tpu_custom_call" | custom-call | flops 1 | bytes 1 | tf_op jit(solution)/shard_map/pallas_call | solution.py:512
  73.0 5.4 %shard_map.187 = (bf16[256,512]{1,0:T(8,128)(2,1)}, bf16[256,512]{1,0:T(8,128)(2,1)}, bf16[1024,512]{1,0:T(8,128)(2,1)}) custom-call(s32[1]{0:T(128)} %bitcast.refs_0_, bf16[256,384]{1,0:T(8,128)(2,1)} %get-tuple-element.85.refs_2_.refs_1_.refs_3_, bf16[128,512]{1,0:T(8,128)(2,1)} %get-tuple-element.94.refs_2_, bf16[256,512]{1,0:T(8,128)(2,1)} %bitcast.53, ...), custom_call_target="tpu_custom_call" | custom-call | flops 1 | bytes 1 | tf_op jit(solution)/shard_map/pallas_call | solution.py:512
  78.4 0.7 collective-permute-start.2
  79.9 4.7 %shard_map.188.refs_7_ = bf16[1024,512]{1,0:T(8,128)(2,1)} custom-call(s32[1]{0:T(128)} %bitcast.refs_0_, bf16[256,512]{1,0:T(8,128)(2,1)} %get-tuple-element.114.refs_1_, bf16[256,512]{1,0:T(8,128)(2,1)} %get-tuple-element.132.refs_2_.refs_5_, bf16[768,512]{1,0:T(8,128)(2,1)} %refs_3_.8, bf16[512,512]{1,0:T(8,128)(2,1)} %get-tuple-element.101.refs_9_.refs_4_, ...), custom_call_target="tpu_custom_call" | custom-call | flops 1 | bytes 1 | tf_op jit(solution)/shard_map/pallas_call | solution.py:512
  84.6 1.2 add_convert_fusion.1
  86.2 2.2 %collective-permute-start.5 = (bf16[192,512]{1,0:T(8,128)(2,1)S(1)}, bf16[192,512]{1,0:T(8,128)(2,1)S(1)}, u32[]{:S(2)}, u32[]{:S(2)}) collective-permute-start(bf16[192,512]{1,0:T(8,128)(2,1)S(1)} %fusion), channel_id=1, source_target_pairs={{0,8},{1,9},{2,10},{3,11},{4,12},{5,13},{6,14},{7,15},{8,0},{9,1},... | collective-permute-start | bytes 589832 | tf_op jit(solution)/shard_map/ppermute | solution.py:531
  88.4 4.0 %shard_map.189 = (f32[128,512]{1,0:T(8,128)}, bf16[256,512]{1,0:T(8,128)(2,1)}) custom-call(bf16[512,128]{1,0:T(8,128)(2,1)} %get-tuple-element.127.refs_0_, bf16[512,128]{1,0:T(8,128)(2,1)} %get-tuple-element.98.refs_1_, bf16[256,384]{1,0:T(8,128)(2,1)} %get-tuple-element.84.refs_0_.refs_2_, bf16[256,384]{1,0:T(8,128)(2,1)} %get-tuple-element.85.refs_2_.refs_1_.refs_3_, ...), custom_call_target="tpu_custom_call" | custom-call | flops 1 | bytes 1 | tf_op jit(solution)/shard_map/pallas_call | solution.py:512
  92.5 5.3 %collective-permute-done.5 = bf16[192,512]{1,0:T(8,128)(2,1)S(1)} collective-permute-done((bf16[192,512]{1,0:T(8,128)(2,1)S(1)}, bf16[192,512]{1,0:T(8,128)(2,1)S(1)}, u32[]{:S(2)}, u32[]{:S(2)}) %collective-permute-start.5) | collective-permute-done | bytes 196640 | tf_op jit(solution)/shard_map/ppermute | solution.py:531
  97.8 1.4 collective-permute-done.3
  99.2 1.1 fusion.1
  100.2 1.0 collective-permute-start.6
  101.2 3.9 %shard_map.190.refs_4_ = f32[768,512]{1,0:T(8,128)} custom-call(bf16[768,512]{1,0:T(8,128)(2,1)} %refs_0_.3, bf16[512,512]{1,0:T(8,128)(2,1)} %get-tuple-element.131.refs_11_.refs_4_.refs_1_, bf16[256,512]{1,0:T(8,128)(2,1)} %get-tuple-element.132.refs_2_.refs_5_, bf16[1536,512]{1,0:T(8,128)(2,1)} %refs_3_.9, bf16[256,512]{1,0:T(8,128)(2,1)} %get-tuple-element.145.refs_4_), custom_call_target="tpu_custom_call" | custom-call | flops 1 | bytes 1 | tf_op jit(solution)/shard_map/pallas_call | solution.py:512
  105.2 1.0 constant_dynamic-slice_fusion
  106.1 0.8 collective-permute-done.6
  107.0 0.9 collective-permute-start.8
  107.9 1.5 collective-permute-start.7
  109.5 3.3 %collective-permute-done.7 = bf16[128,512]{1,0:T(8,128)(2,1)S(1)} collective-permute-done((bf16[128,512]{1,0:T(8,128)(2,1)S(1)}, bf16[128,512]{1,0:T(8,128)(2,1)S(1)}, u32[]{:S(2)}, u32[]{:S(2)}) %collective-permute-start.7) | collective-permute-done | bytes 131104 | tf_op jit(solution)/shard_map/ppermute | solution.py:531
  113.0 2.8 %collective-permute-start.9 = (bf16[128,512]{1,0:T(8,128)(2,1)S(1)}, bf16[128,512]{1,0:T(8,128)(2,1)S(1)}, u32[]{:S(2)}, u32[]{:S(2)}) collective-permute-start(bf16[128,512]{1,0:T(8,128)(2,1)S(1)} %fusion.2), channel_id=1, source_target_pairs={{0,8},{1,9},{2,10},{3,11},{4,12},{5,13},{6,14},{7,15},{8,0},{9,1},... | collective-permute-start | bytes 393224 | tf_op jit(solution)/shard_map/ppermute | solution.py:531
  116.0 5.0 %collective-permute-done.9 = bf16[128,512]{1,0:T(8,128)(2,1)S(1)} collective-permute-done((bf16[128,512]{1,0:T(8,128)(2,1)S(1)}, bf16[128,512]{1,0:T(8,128)(2,1)S(1)}, u32[]{:S(2)}, u32[]{:S(2)}) %collective-permute-start.9) | collective-permute-done | bytes 131104 | tf_op jit(solution)/shard_map/ppermute | solution.py:531
  121.1 1.8 %collective-permute-done.11 = bf16[384,512]{1,0:T(8,128)(2,1)S(1)} collective-permute-done((bf16[384,512]{1,0:T(8,128)(2,1)S(1)}, bf16[384,512]{1,0:T(8,128)(2,1)S(1)}, u32[]{:S(2)}, u32[]{:S(2)}) %collective-permute-start.11) | collective-permute-done | bytes 393248 | tf_op jit(solution)/shard_map/ppermute | solution.py:531
  122.9 3.7 %collective-permute-done.10 = bf16[256,512]{1,0:T(8,128)(2,1)S(1)} collective-permute-done((bf16[256,512]{1,0:T(8,128)(2,1)S(1)}, bf16[256,512]{1,0:T(8,128)(2,1)S(1)}, u32[]{:S(2)}, u32[]{:S(2)}) %collective-permute-start.10) | collective-permute-done | bytes 262176 | tf_op jit(solution)/shard_map/ppermute | solution.py:531
  126.9 4.1 %collective-permute-start.14 = (bf16[768,512]{1,0:T(8,128)(2,1)S(1)}, bf16[768,512]{1,0:T(8,128)(2,1)}, u32[]{:S(2)}, u32[]{:S(2)}) collective-permute-start(bf16[768,512]{1,0:T(8,128)(2,1)S(1)} %maximum_select_fusion), channel_id=1, source_target_pairs={{0,1},{1,0},{2,3},{3,2},{4,5},{5,4},{6,7},{7,6},{8,9},{9,8},{10,11... | collective-permute-start | bytes 2359304 | tf_op jit(solution)/shard_map/ppermute | solution.py:531
  132.2 6.1 %all-to-all-start.4 = ((bf16[16,16,512]{2,1,0:T(8,128)(2,1)}), bf16[16,16,512]{2,1,0:T(8,128)(2,1)}, u32[]{:S(2)}, u32[]{:S(2)}) async-start(bf16[16,16,512]{2,1,0:T(8,128)(2,1)} %bitcast.52), calls=%async_computation.4 | async-start | bytes 524288 | tf_op jit(solution)/shard_map/all_to_all | solution.py:572
  138.5 1.2 broadcast_select_fusion.1
  139.8 0.8 slice.25
  140.6 1.0 pad_maximum_fusion
  141.7 6.6 %all-to-all-done.4 = bf16[16,16,512]{2,1,0:T(8,128)(2,1)} async-done(((bf16[16,16,512]{2,1,0:T(8,128)(2,1)}), bf16[16,16,512]{2,1,0:T(8,128)(2,1)}, u32[]{:S(2)}, u32[]{:S(2)}) %all-to-all-start.4) | async-done | bytes 262176 | tf_op jit(solution)/shard_map/all_to_all | solution.py:572
  148.7 2.9 %shard_map.191 = f32[128,512]{1,0:T(8,128)} custom-call(f32[128,512]{1,0:T(8,128)} %get-tuple-element.150.refs_0_, f32[128,512]{1,0:T(8,128)} %get-tuple-element.151.refs_1_, bf16[256,128]{1,0:T(8,128)(2,1)} %get-tuple-element.87.refs_5_.refs_2_, bf16[256,512]{1,0:T(8,128)(2,1)} %bitcast.32.refs_3_, f32[768,512]{1,0:T(8,128)} %shard_map.190.refs_4_), custom_call_target="tpu_custom_call" | custom-call | flops 1 | bytes 1 | tf_op jit(solution)/shard_map/pallas_call | solution.py:512
  151.6 1.4 select_select_fusion
  152.9 1.1 broadcast_select_fusion.2
  154.0 1.1 copy-done.1
  (44 shorter events, 7.3 us)
Async XLA Ops:
  2.3 13.0 %all-to-all-start = ((s32[16,1,16]{2,1,0:T(1,128)}), s32[16,1,16]{2,1,0:T(1,128)S(1)}, u32[]{:S(2)}, u32[]{:S(2)}) async-start(s32[16,1,16]{2,1,0:T(1,128)} %bitcast.69), calls=%async_computation | async-start | bytes 16384 | tf_op jit(solution)/shard_map/all_to_all | solution.py:602
  15.4 0.6 copy-start.5
  18.7 13.6 %all-to-all-start.1 = ((bf16[16,16,512]{2,1,0:T(8,128)(2,1)}), bf16[16,16,512]{2,1,0:T(8,128)(2,1)S(1)}, u32[]{:S(2)}, u32[]{:S(2)}) async-start(bf16[16,16,512]{2,1,0:T(8,128)(2,1)} %bitcast.66), calls=%async_computation.1 | async-start | bytes 524288 | tf_op jit(solution)/shard_map/all_to_all | solution.py:572
  32.3 0.7 copy-start.3
  38.1 13.6 %all-to-all-start.2 = ((bf16[16,16,512]{2,1,0:T(8,128)(2,1)}), bf16[16,16,512]{2,1,0:T(8,128)(2,1)S(1)}, u32[]{:S(2)}, u32[]{:S(2)}) async-start(bf16[16,16,512]{2,1,0:T(8,128)(2,1)} %bitcast.62), calls=%async_computation.2 | async-start | bytes 524288 | tf_op jit(solution)/shard_map/all_to_all | solution.py:572
  51.7 0.7 copy-start.4
  58.7 4.2 %collective-permute-start = (bf16[768,512]{1,0:T(8,128)(2,1)}, bf16[768,512]{1,0:T(8,128)(2,1)S(1)}, u32[]{:S(2)}, u32[]{:S(2)}) collective-permute-start(bf16[768,512]{1,0:T(8,128)(2,1)} %get-tuple-element.97.refs_12_), channel_id=1, source_target_pairs={{0,1},{1,0},{2,3},{3,2},{4,5},{5,4},{6,7},{7,6},{8,9},{9,8},{10,11... | collective-permute-start | bytes 2359304 | tf_op jit(solution)/shard_map/ppermute | solution.py:531
  59.4 12.9 %all-to-all-start.3 = ((bf16[16,16,512]{2,1,0:T(8,128)(2,1)}), bf16[16,16,512]{2,1,0:T(8,128)(2,1)S(1)}, u32[]{:S(2)}, u32[]{:S(2)}) async-start(bf16[16,16,512]{2,1,0:T(8,128)(2,1)} %bitcast.65), calls=%async_computation.3 | async-start | bytes 524288 | tf_op jit(solution)/shard_map/all_to_all | solution.py:572
  64.3 14.2 %collective-permute-start.1 = (bf16[384,512]{1,0:T(8,128)(2,1)S(1)}, bf16[384,512]{1,0:T(8,128)(2,1)S(1)}, u32[]{:S(2)}, u32[]{:S(2)}) collective-permute-start(bf16[384,512]{1,0:T(8,128)(2,1)S(1)} %get-tuple-element.164), channel_id=1, source_target_pairs={{0,2},{1,3},{2,0},{3,1},{4,6},{5,7},{6,4},{7,5},{8,10},{9,11},{10,... | collective-permute-start | bytes 1179656 | tf_op jit(solution)/shard_map/ppermute | solution.py:531
  72.3 0.7 copy-start.2
  78.4 6.2 %collective-permute-start.2 = (bf16[1024,512]{1,0:T(8,128)(2,1)}, bf16[1024,512]{1,0:T(8,128)(2,1)S(1)}, u32[]{:S(2)}, u32[]{:S(2)}) collective-permute-start(bf16[1024,512]{1,0:T(8,128)(2,1)} %get-tuple-element.118.refs_12_), channel_id=1, source_target_pairs={{0,1},{1,0},{2,3},{3,2},{4,5},{5,4},{6,7},{7,6},{8,9},{9,8},{10,11... | collective-permute-start | bytes 3145736 | tf_op jit(solution)/shard_map/ppermute | solution.py:531
  79.2 6.9 %collective-permute-start.4 = (bf16[192,512]{1,0:T(8,128)(2,1)S(1)}, bf16[192,512]{1,0:T(8,128)(2,1)S(1)}, u32[]{:S(2)}, u32[]{:S(2)}) collective-permute-start(bf16[192,512]{1,0:T(8,128)(2,1)S(1)} %fusion.3), channel_id=1, source_target_pairs={{0,4},{1,5},{2,6},{3,7},{4,0},{5,1},{6,2},{7,3},{8,12},{9,13},{10,... | collective-permute-start | bytes 589832 | tf_op jit(solution)/shard_map/ppermute | solution.py:531
  85.8 13.4 %collective-permute-start.3 = (bf16[512,512]{1,0:T(8,128)(2,1)S(1)}, bf16[512,512]{1,0:T(8,128)(2,1)}, u32[]{:S(2)}, u32[]{:S(2)}) collective-permute-start(bf16[512,512]{1,0:T(8,128)(2,1)S(1)} %add_convert_fusion.1), channel_id=1, source_target_pairs={{0,2},{1,3},{2,0},{3,1},{4,6},{5,7},{6,4},{7,5},{8,10},{9,11},{10,... | collective-permute-start | bytes 1572872 | tf_op jit(solution)/shard_map/ppermute | solution.py:531
  86.2 11.6 %collective-permute-start.5 = (bf16[192,512]{1,0:T(8,128)(2,1)S(1)}, bf16[192,512]{1,0:T(8,128)(2,1)S(1)}, u32[]{:S(2)}, u32[]{:S(2)}) collective-permute-start(bf16[192,512]{1,0:T(8,128)(2,1)S(1)} %fusion), channel_id=1, source_target_pairs={{0,8},{1,9},{2,10},{3,11},{4,12},{5,13},{6,14},{7,15},{8,0},{9,1},... | collective-permute-start | bytes 589832 | tf_op jit(solution)/shard_map/ppermute | solution.py:531
  88.4 4.0 %copy-start = (bf16[1024,512]{1,0:T(8,128)(2,1)S(1)}, bf16[1024,512]{1,0:T(8,128)(2,1)}, u32[]{:S(2)}) copy-start(bf16[1024,512]{1,0:T(8,128)(2,1)} %shard_map.188.refs_7_) | copy-start | bytes 3145732
  100.2 6.7 %collective-permute-start.6 = (bf16[256,512]{1,0:T(8,128)(2,1)S(1)}, bf16[256,512]{1,0:T(8,128)(2,1)S(1)}, u32[]{:S(2)}, u32[]{:S(2)}) collective-permute-start(bf16[256,512]{1,0:T(8,128)(2,1)S(1)} %fusion.1), channel_id=1, source_target_pairs={{0,4},{1,5},{2,6},{3,7},{4,0},{5,1},{6,2},{7,3},{8,12},{9,13},{10,... | collective-permute-start | bytes 786440 | tf_op jit(solution)/shard_map/ppermute | solution.py:531
  107.0 5.9 %collective-permute-start.8 = (bf16[192,512]{1,0:T(8,128)(2,1)S(1)}, bf16[192,512]{1,0:T(8,128)(2,1)S(1)}, u32[]{:S(2)}, u32[]{:S(2)}) collective-permute-start(bf16[192,512]{1,0:T(8,128)(2,1)S(1)} %add_convert_fusion.3), channel_id=1, source_target_pairs={{0,4},{1,5},{2,6},{3,7},{4,0},{5,1},{6,2},{7,3},{8,12},{9,13},{10,... | collective-permute-start | bytes 589832 | tf_op jit(solution)/shard_map/ppermute | solution.py:531
  107.9 4.9 %collective-permute-start.7 = (bf16[128,512]{1,0:T(8,128)(2,1)S(1)}, bf16[128,512]{1,0:T(8,128)(2,1)S(1)}, u32[]{:S(2)}, u32[]{:S(2)}) collective-permute-start(bf16[128,512]{1,0:T(8,128)(2,1)S(1)} %fusion.4), channel_id=1, source_target_pairs={{0,8},{1,9},{2,10},{3,11},{4,12},{5,13},{6,14},{7,15},{8,0},{9,1},... | collective-permute-start | bytes 393224 | tf_op jit(solution)/shard_map/ppermute | solution.py:531
  113.0 8.0 %collective-permute-start.9 = (bf16[128,512]{1,0:T(8,128)(2,1)S(1)}, bf16[128,512]{1,0:T(8,128)(2,1)S(1)}, u32[]{:S(2)}, u32[]{:S(2)}) collective-permute-start(bf16[128,512]{1,0:T(8,128)(2,1)S(1)} %fusion.2), channel_id=1, source_target_pairs={{0,8},{1,9},{2,10},{3,11},{4,12},{5,13},{6,14},{7,15},{8,0},{9,1},... | collective-permute-start | bytes 393224 | tf_op jit(solution)/shard_map/ppermute | solution.py:531
  115.9 7.0 %collective-permute-start.11 = (bf16[384,512]{1,0:T(8,128)(2,1)S(1)}, bf16[384,512]{1,0:T(8,128)(2,1)S(1)}, u32[]{:S(2)}, u32[]{:S(2)}) collective-permute-start(bf16[384,512]{1,0:T(8,128)(2,1)S(1)} %maximum_select_fusion.2), channel_id=1, source_target_pairs={{0,2},{1,3},{2,0},{3,1},{4,6},{5,7},{6,4},{7,5},{8,10},{9,11},{10,... | collective-permute-start | bytes 1179656 | tf_op jit(solution)/shard_map/ppermute | solution.py:531
  121.0 5.6 %collective-permute-start.10 = (bf16[256,512]{1,0:T(8,128)(2,1)S(1)}, bf16[256,512]{1,0:T(8,128)(2,1)S(1)}, u32[]{:S(2)}, u32[]{:S(2)}) collective-permute-start(bf16[256,512]{1,0:T(8,128)(2,1)S(1)} %maximum_select_fusion.3), channel_id=1, source_target_pairs={{0,4},{1,5},{2,6},{3,7},{4,0},{5,1},{6,2},{7,3},{8,12},{9,13},{10,... | collective-permute-start | bytes 786440 | tf_op jit(solution)/shard_map/ppermute | solution.py:531
  126.9 11.6 %collective-permute-start.14 = (bf16[768,512]{1,0:T(8,128)(2,1)S(1)}, bf16[768,512]{1,0:T(8,128)(2,1)}, u32[]{:S(2)}, u32[]{:S(2)}) collective-permute-start(bf16[768,512]{1,0:T(8,128)(2,1)S(1)} %maximum_select_fusion), channel_id=1, source_target_pairs={{0,1},{1,0},{2,3},{3,2},{4,5},{5,4},{6,7},{7,6},{8,9},{9,8},{10,11... | collective-permute-start | bytes 2359304 | tf_op jit(solution)/shard_map/ppermute | solution.py:531
  131.4 6.9 %collective-permute-start.13 = (bf16[512,512]{1,0:T(8,128)(2,1)S(1)}, bf16[512,512]{1,0:T(8,128)(2,1)S(1)}, u32[]{:S(2)}, u32[]{:S(2)}) collective-permute-start(bf16[512,512]{1,0:T(8,128)(2,1)S(1)} %get-tuple-element.148), channel_id=1, source_target_pairs={{0,1},{1,0},{2,3},{3,2},{4,5},{5,4},{6,7},{7,6},{8,9},{9,8},{10,11... | collective-permute-start | bytes 1572872 | tf_op jit(solution)/shard_map/ppermute | solution.py:531
  131.5 16.8 %collective-permute-start.12 = (bf16[512,512]{1,0:T(8,128)(2,1)S(1)}, bf16[512,512]{1,0:T(8,128)(2,1)}, u32[]{:S(2)}, u32[]{:S(2)}) collective-permute-start(bf16[512,512]{1,0:T(8,128)(2,1)S(1)} %get-tuple-element.148), channel_id=1, source_target_pairs={{0,2},{1,3},{2,0},{3,1},{4,6},{5,7},{6,4},{7,5},{8,10},{9,11},{10,... | collective-permute-start | bytes 1572872 | tf_op jit(solution)/shard_map/ppermute | solution.py:531
  132.2 16.1 %all-to-all-start.4 = ((bf16[16,16,512]{2,1,0:T(8,128)(2,1)}), bf16[16,16,512]{2,1,0:T(8,128)(2,1)}, u32[]{:S(2)}, u32[]{:S(2)}) async-start(bf16[16,16,512]{2,1,0:T(8,128)(2,1)} %bitcast.52), calls=%async_computation.4 | async-start | bytes 524288 | tf_op jit(solution)/shard_map/all_to_all | solution.py:572
  148.3 4.7 %collective-permute-start.15 = (bf16[512,512]{1,0:T(8,128)(2,1)}, bf16[512,512]{1,0:T(8,128)(2,1)S(1)}, u32[]{:S(2)}, u32[]{:S(2)}) collective-permute-start(bf16[512,512]{1,0:T(8,128)(2,1)} %collective-permute-done.12), channel_id=1, source_target_pairs={{0,1},{1,0},{2,3},{3,2},{4,5},{5,4},{6,7},{7,6},{8,9},{9,8},{10,11... | collective-permute-start | bytes 1572872 | tf_op jit(solution)/shard_map/ppermute | solution.py:531
  154.0 1.1 copy-start.1

commit v10 on v8

--- a/solution.py
+++ b/solution.py
@@ -324,14 +324,18 @@
         each(high)
 
 
-def edge_rows(half, buffers, cut_pre, cut_out, out_ref):
+def place_rows(me_ref, index, latent):
+    return pl.ds(pl.multiple_of((index ^ ((me_ref[0] >> 1) & 1)) * latent, latent), latent)
+
+
+def edge_rows(me_ref, half, buffers, cut_pre, cut_out, out_ref):
     latent = cut_pre.shape[1]
     first, first_cut, second, second_cut, first_right, second_right = buffers
     chosen = jnp.where(half == 0, cut_pre.astype(F32), cut_out.astype(F32)).astype(BF16)
-    out_ref[:latent] = (
+    out_ref[place_rows(me_ref, 0, latent)] = (
         dot_rows(first[...], first_right[...]) + dot_rows(first_cut[...], cut_pre)
     ).astype(BF16)
-    out_ref[latent:] = (
+    out_ref[place_rows(me_ref, 1, latent)] = (
         dot_rows(second[...], second_right[...]) + dot_rows(second_cut[...], chosen)
     ).astype(BF16)
 
@@ -362,7 +366,7 @@
     grad_out_ref[...] = grad_out
     grad_pre_ref[...] = grad_pre
     fetch_factors(half, sources, buffers, sems, True)
-    edge_rows(half, buffers, grad_pre, grad_out, out_ref)
+    edge_rows(me_ref, half, buffers, grad_pre, grad_out, out_ref)
 
 
 def edge_weights_kernel(me_ref, cut_out_ref, cut_pre_ref, *refs):
@@ -371,7 +375,7 @@
     half = me_ref[0] & 1
     fetch_factors(half, sources, buffers, sems, False)
     fetch_factors(half, sources, buffers, sems, True)
-    edge_rows(half, buffers, cut_pre_ref[...], cut_out_ref[...], out_ref)
+    edge_rows(me_ref, half, buffers, cut_pre_ref[...], cut_out_ref[...], out_ref)
 
 
 def input_grads_kernel(
@@ -734,7 +738,9 @@
         [SMEM, VMEM, VMEM] + [ANY] * len(factors),
         scratch=buffers,
     )
-    edge_own, edge_sent = split(fence(edge_keep, received), 1)
+    edge_keep, received = fence(edge_keep, received)
+    edge_own = [edge_keep[:latent], received[:latent]]
+    edge_sent = added(edge_keep[latent:], received[latent:])
     edge_sent, inner_pre, cut_pre = fence(edge_sent, inner_pre, cut_pre)
     node_got = fence(node_got, edge_sent)[0]
     edge_got = across(edge_sent, domains, 2)
@@ -757,11 +763,8 @@
     edge_got, node_sum, inner_pre, cut_pre, local_grad = fence(
         edge_got, node_sum, inner_pre, cut_pre, local_grad
     )
-    edge_own, edge_sent = split([*edge_own, edge_got], 2)
-    edge_got, *node_parts = fence(across(edge_sent, domains, 4), *handed(node_sum, domains, 2))
-    edge_own, edge_sent = split([*edge_own, edge_got], 3)
-    edge_got = across(edge_sent, domains, 8)
-    node_parts = handed(joined(node_parts, 2), domains, 1)
+    edge_own, edge_sent = split([added(*edge_own, edge_got)], 2)
+    edge_got = across(edge_sent, domains, 4)
     grad_edges = line.run(
         functools.partial(edge_grads_kernel, blocks=blocks),
         shaped(F32, *edges.shape),
@@ -775,28 +778,34 @@
         [rows_spec(latent)],
         (blocks + 1,),
     )
-    edge_got, grad_edges, outgoing_grad = fence(edge_got, grad_edges, outgoing_grad)
+    edge_got, node_sum, grad_edges = fence(edge_got, node_sum, grad_edges)
+    edge_own, edge_sent = split([added(*edge_own, edge_got)], 3)
+    edge_sent, node_sum = fence(edge_sent, node_sum)
+    edge_got, *node_parts = fence(across(edge_sent, domains, 8), *handed(node_sum, domains, 2))
     edge_sum = added(*edge_own, edge_got)
     for bit in bits[4:]:
         own, sent = split([edge_sum], bit)
         edge_sum = added(*own, across(sent, domains, 1 << bit))
     for bit in bits[:3:-1]:
         edge_sum = joined(handed(edge_sum, domains, bit), bit)
+    node_parts = handed(joined(node_parts, 2), domains, 1)
+    edge_parts = fence(*handed(edge_sum, domains, 3))
+    edge_parts = handed(joined(edge_parts, 3), domains, 2)
+    *edge_parts, node_sum, other_sum, outgoing_grad = fence(
+        *edge_parts, *node_parts, outgoing_grad
+    )
+    edge_sum = joined(edge_parts, 2)
+    node_sum = joined([node_sum, other_sum], 1)
+    far, near = across(edge_sum, domains, 2), across(edge_sum, domains, 1)
+    others = across(node_sum, domains, 1)
     returned = exchange(outgoing_grad, domains)
-    *edge_parts, node_sum, other_sum = fence(*handed(edge_sum, domains, 3), *node_parts)
-    edge_parts = handed(joined(edge_parts, 3), domains, 2)
-    node_sum = joined([node_sum, other_sum], 1)
-    others = across(node_sum, domains, 1)
-    *edge_parts, node_sum, others = fence(*edge_parts, node_sum, others)
-    edge_sum = joined(edge_parts, 2)
-    edge_parts = handed(edge_sum, domains, 1) + [across(edge_sum, domains, 1)]
     lower, left = place_of(0) == 0, place_of(1) == 0
     low_rows, high_rows = jnp.where(lower, node_sum, others), jnp.where(lower, others, node_sum)
     cut_at = 2 * latent - low_rows.shape[0]
     grad_node_in = jnp.concatenate([low_rows, high_rows[:cut_at]])
     grad_node_out = high_rows[cut_at:]
-    mine, far, near, grad_node_in, grad_node_out, returned = fence(
-        *edge_parts, grad_node_in, grad_node_out, returned
+    far, near, grad_node_in, grad_node_out, returned = fence(
+        far, near, grad_node_in, grad_node_out, returned
     )
     corner = across(far, domains, 1)
     grad_nodes = line.run(
@@ -804,7 +813,7 @@
         shaped(F32, node_rows, latent),
         [self_grad, local_grad, asked_marks, returned],
     )
-    own, other = [mine, far], [near, corner]
+    own, other = [edge_sum, far], [near, corner]
     low_half = [jnp.where(lower, one, two) for one, two in zip(own, other)]
     high_half = [jnp.where(lower, two, one) for one, two in zip(own, other)]
     grad_edge_in = jnp.concatenate(

time: 156 us -> 152 us (0.974)
  waiting for transfers between devices: 55.8 us -> 49 us
  starting transfers between devices: 38.7 us -> 40.9 us
    ppermute x16, waiting for transfers between devices: 29.9 us -> 22.5 us  [across(): lax.ppermute(rows, 'dom', [(device, device ^ mask) for device in range(de...]
    ppermute x16, starting transfers between devices: 15.5 us -> 17.1 us  [across(): lax.ppermute(rows, 'dom', [(device, device ^ mask) for device in range(de...]
    convert_element_type x7 -> x8, other arithmetic: 3.69 us -> 4.06 us  [added(): return sum((part.astype(F32) for part in parts)).astype(BF16)]
  transfers between devices with their start and end apart: 21 -> 21, of which waited for: 11 -> 12; matrix products, arithmetic and copies ran while one was open for 4% -> 3% of each run, Pallas kernels for 22% -> 23%
where the time goes in v10:
time: 152 us; the launch traced here: 151 us
  waiting for transfers between devices  49 us (32%)
  Pallas kernels  48 us (32%)
  starting transfers between devices  40.9 us (27%)
  other arithmetic  8.12 us (5%)
  local copies, waits for them, and re-layouts  3.9 us (3%)
    pallas_call x13, Pallas kernels, run(): pl.pallas_call(ordered, out_shape=out_shape, in_specs=specs, out_specs=[V...  48 us
    all_to_all x4, waiting for transfers between devices, exchange(): lax.all_to_all(split, 'dom', split_axis=0, concat_axis=0, tiled=True)  22.8 us
    ppermute x16, waiting for transfers between devices, across(): lax.ppermute(rows, 'dom', [(device, device ^ mask) for device in range(de...  22.5 us
    ppermute x16, starting transfers between devices, across(): lax.ppermute(rows, 'dom', [(device, device ^ mask) for device in range(de...  17.1 us
    all_to_all x4, starting transfers between devices, exchange(): lax.all_to_all(split, 'dom', split_axis=0, concat_axis=0, tiled=True)  16.5 us
    all_to_all x1, starting transfers between devices, shards(): asked = lax.all_to_all(ask, 'dom', split_axis=0, concat_axis=0, tiled=True)  7.32 us
    convert_element_type x8, other arithmetic, added(): return sum((part.astype(F32) for part in parts)).astype(BF16)  4.06 us
    all_to_all x1, waiting for transfers between devices, shards(): asked = lax.all_to_all(ask, 'dom', split_axis=0, concat_axis=0, tiled=True)  3.67 us
  transfers between devices with their start and end apart: 21, of which 12 were waited for; matrix products, arithmetic and copies ran while one was open for 3% of the time, Pallas kernels for 23%

profile of v10, /device:TPU:1, one launch (start us, length us, event | category | flops | bytes accessed | tf_op | source)
XLA Modules:
  0.0 150.8 jit_solution(16716971304827301048)
XLA Ops:
  0.6 1.7 %shard_map.179.refs_2_ = s32[16,16]{1,0:T(8,128)} custom-call(s32[1,128]{1,0:T(1,128)} %bitcast.60, s32[1,128]{1,0:T(1,128)} %bitcast.63), custom_call_target="tpu_custom_call" | custom-call | flops 1 | bytes 1 | tf_op jit(solution)/shard_map/pallas_call | solution.py:455
  2.3 7.3 %all-to-all-start = ((s32[16,1,16]{2,1,0:T(1,128)}), s32[16,1,16]{2,1,0:T(1,128)S(1)}, u32[]{:S(2)}, u32[]{:S(2)}) async-start(s32[16,1,16]{2,1,0:T(1,128)} %bitcast.58), calls=%async_computation | async-start | bytes 16384 | tf_op jit(solution)/shard_map/all_to_all | solution.py:539
  9.7 2.0 %shard_map.180 = (bf16[256,384]{1,0:T(8,128)(2,1)}, bf16[256,384]{1,0:T(8,128)(2,1)}) custom-call(s32[1,128]{1,0:T(1,128)} %bitcast.61, s32[1,128]{1,0:T(1,128)} %bitcast.64, s32[16,16]{1,0:T(8,128)} %shard_map.179.refs_2_), custom_call_target="tpu_custom_call" | custom-call | flops 1 | bytes 1 | tf_op jit(solution)/shard_map/pallas_call | solution.py:455
  11.7 3.7 %all-to-all-done = s32[16,1,16]{2,1,0:T(1,128)S(1)} async-done(((s32[16,1,16]{2,1,0:T(1,128)}), s32[16,1,16]{2,1,0:T(1,128)S(1)}, u32[]{:S(2)}, u32[]{:S(2)}) %all-to-all-start) | async-done | bytes 1056 | tf_op jit(solution)/shard_map/all_to_all | solution.py:539
  16.0 2.0 %shard_map.181 = (bf16[256,512]{1,0:T(8,128)(2,1)}, bf16[256,128]{1,0:T(8,128)(2,1)}) custom-call(s32[16,16]{1,0:T(8,128)} %bitcast.59, bf16[128,512]{1,0:T(8,128)(2,1)} %refs_4_.4, bf16[256,384]{1,0:T(8,128)(2,1)} %get-tuple-element.80.refs_2_.refs_1_.refs_3_), custom_call_target="tpu_custom_call" | custom-call | flops 1 | bytes 1 | tf_op jit(solution)/shard_map/pallas_call | solution.py:455
  18.0 4.0 %all-to-all-start.1 = ((bf16[16,16,512]{2,1,0:T(8,128)(2,1)}), bf16[16,16,512]{2,1,0:T(8,128)(2,1)S(1)}, u32[]{:S(2)}, u32[]{:S(2)}) async-start(bf16[16,16,512]{2,1,0:T(8,128)(2,1)} %bitcast.57), calls=%async_computation.1 | async-start | bytes 524288 | tf_op jit(solution)/shard_map/all_to_all | solution.py:509
  22.0 6.3 %shard_map.182 = (bf16[512,128]{1,0:T(8,128)(2,1)}, bf16[512,128]{1,0:T(8,128)(2,1)}, bf16[512,512]{1,0:T(8,128)(2,1)}, bf16[512,512]{1,0:T(8,128)(2,1)}, bf16[5...) custom-call(s32[2,256]{1,0:T(2,128)} %bitcast.62, ...), custom_call_target="tpu_custom_call" | custom-call | flops 1 | bytes 1 | tf_op jit(solution)/shard_map/pallas_call | solution.py:455
  28.3 3.3 %all-to-all-done.1 = bf16[16,16,512]{2,1,0:T(8,128)(2,1)S(1)} async-done(((bf16[16,16,512]{2,1,0:T(8,128)(2,1)}), bf16[16,16,512]{2,1,0:T(8,128)(2,1)S(1)}, u32[]{:S(2)}, u32[]{:S(2)}) %all-to-all-start.1) | async-done | bytes 262176 | tf_op jit(solution)/shard_map/all_to_all | solution.py:509
  31.6 0.7 copy-done.2
  32.3 4.3 %shard_map.183 = (bf16[256,512]{1,0:T(8,128)(2,1)}, bf16[256,512]{1,0:T(8,128)(2,1)}, bf16[256,512]{1,0:T(8,128)(2,1)}, f32[256,512]{1,0:T(8,128)}, f32[256,512]...) custom-call(bf16[256,384]{1,0:T(8,128)(2,1)} %get-tuple-element.79.refs_0_.refs_2_, ...), custom_call_target="tpu_custom_call" | custom-call | flops 1 | bytes 1 | tf_op jit(solution)/shard_map/pallas_call | solution.py:455
  36.6 4.0 %all-to-all-start.2 = ((bf16[16,16,512]{2,1,0:T(8,128)(2,1)}), bf16[16,16,512]{2,1,0:T(8,128)(2,1)S(1)}, u32[]{:S(2)}, u32[]{:S(2)}) async-start(bf16[16,16,512]{2,1,0:T(8,128)(2,1)} %bitcast.53), calls=%async_computation.2 | async-start | bytes 524288 | tf_op jit(solution)/shard_map/all_to_all | solution.py:509
  40.6 2.7 %shard_map.184.refs_8_ = bf16[768,512]{1,0:T(8,128)(2,1)} custom-call(bf16[768,512]{1,0:T(8,128)(2,1)} %refs_3_.6, f32[512,512]{1,0:T(8,128)} %get-tuple-element.86.refs_1_.refs_3_, f32[256,512]{1,0:T(8,128)} %get-tuple-element.87.refs_2_.refs_5_, bf16[256,512]{1,0:T(8,128)(2,1)} %get-tuple-element.84.refs_3_), custom_call_target="tpu_custom_call" | custom-call | flops 1 | bytes 1 | tf_op jit(solution)/shard_map/pallas_call | solution.py:455
  43.2 6.9 %all-to-all-done.2 = bf16[16,16,512]{2,1,0:T(8,128)(2,1)S(1)} async-done(((bf16[16,16,512]{2,1,0:T(8,128)(2,1)}), bf16[16,16,512]{2,1,0:T(8,128)(2,1)S(1)}, u32[]{:S(2)}, u32[]{:S(2)}) %all-to-all-start.2) | async-done | bytes 262176 | tf_op jit(solution)/shard_map/all_to_all | solution.py:509
  50.1 0.7 copy-done.4
  50.8 5.4 %shard_map.185 = (bf16[128,512]{1,0:T(8,128)(2,1)}, f32[128,512]{1,0:T(8,128)}, bf16[128,512]{1,0:T(8,128)(2,1)}, bf16[256,512]{1,0:T(8,128)(2,1)}, bf16[768,512]{1,0:T(8,128)(2,1)}, /*index=5*/bf16[768,512]{1,0:T(8,128)(2,1)}) custom-call(s32[1]{0:T(128)} %bitcast.refs_0_, bf16[256,512]{1,0:T(8,128)(2,1)} %bitcast.52, ...), custom_call_target="tpu_custom_call" | custom-call | flops 1 | bytes 1 | tf_op jit(solution)/shard_map/pallas_call | solution.py:455
  56.9 3.6 %all-to-all-start.3 = ((bf16[16,16,512]{2,1,0:T(8,128)(2,1)}), bf16[16,16,512]{2,1,0:T(8,128)(2,1)S(1)}, u32[]{:S(2)}, u32[]{:S(2)}) async-start(bf16[16,16,512]{2,1,0:T(8,128)(2,1)} %bitcast.56), calls=%async_computation.3 | async-start | bytes 524288 | tf_op jit(solution)/shard_map/all_to_all | solution.py:509
  60.5 1.3 add_convert_fusion
  61.9 1.2 collective-permute-start.1
  63.1 3.6 %shard_map.186 = (bf16[512,512]{1,0:T(8,128)(2,1)}, bf16[512,512]{1,0:T(8,128)(2,1)}) custom-call(bf16[512,128]{1,0:T(8,128)(2,1)} %get-tuple-element.94.refs_0_.refs_1_, bf16[128,512]{1,0:T(8,128)(2,1)} %get-tuple-element.90.refs_1_.refs_2_, bf16[768,512]{1,0:T(8,128)(2,1)} %refs_0_.3, f32[512,512]{1,0:T(8,128)} %get-tuple-element.86.refs_1_.refs_3_, ...), custom_call_target="tpu_custom_call" | custom-call | flops 1 | bytes 1 | tf_op jit(solution)/shard_map/pallas_call | solution.py:455
  66.7 3.1 %all-to-all-done.3 = bf16[16,16,512]{2,1,0:T(8,128)(2,1)S(1)} async-done(((bf16[16,16,512]{2,1,0:T(8,128)(2,1)}), bf16[16,16,512]{2,1,0:T(8,128)(2,1)S(1)}, u32[]{:S(2)}, u32[]{:S(2)}) %all-to-all-start.3) | async-done | bytes 262176 | tf_op jit(solution)/shard_map/all_to_all | solution.py:509
  69.7 0.7 copy-done.1
  70.4 5.4 %shard_map.187 = (bf16[256,512]{1,0:T(8,128)(2,1)}, bf16[256,512]{1,0:T(8,128)(2,1)}, bf16[1024,512]{1,0:T(8,128)(2,1)}) custom-call(s32[1]{0:T(128)} %bitcast.refs_0_, bf16[256,384]{1,0:T(8,128)(2,1)} %get-tuple-element.80.refs_2_.refs_1_.refs_3_, bf16[128,512]{1,0:T(8,128)(2,1)} %get-tuple-element.90.refs_1_.refs_2_, bf16[256,512]{1,0:T(8,128)(2,1)} %bitcast.47, ...), custom_call_target="tpu_custom_call" | custom-call | flops 1 | bytes 1 | tf_op jit(solution)/shard_map/pallas_call | solution.py:455
  75.9 0.8 collective-permute-start.2
  76.8 4.7 %shard_map.188.refs_7_ = bf16[1024,512]{1,0:T(8,128)(2,1)} custom-call(s32[1]{0:T(128)} %bitcast.refs_0_, bf16[256,512]{1,0:T(8,128)(2,1)} %get-tuple-element.111.refs_1_, bf16[256,512]{1,0:T(8,128)(2,1)} %get-tuple-element.128.refs_2_.refs_5_, bf16[768,512]{1,0:T(8,128)(2,1)} %refs_3_.6, bf16[512,512]{1,0:T(8,128)(2,1)} %get-tuple-element.101.refs_10_.refs_4_, ...), custom_call_target="tpu_custom_call" | custom-call | flops 1 | bytes 1 | tf_op jit(solution)/shard_map/pallas_call | solution.py:455
  81.5 1.2 add_convert_fusion.2
  82.7 0.7 collective-permute-start.3
  83.5 1.6 %collective-permute-start.5 = (bf16[192,512]{1,0:T(8,128)(2,1)S(1)}, bf16[192,512]{1,0:T(8,128)(2,1)S(1)}, u32[]{:S(2)}, u32[]{:S(2)}) collective-permute-start(bf16[192,512]{1,0:T(8,128)(2,1)S(1)} %fusion.1), channel_id=1, source_target_pairs={{0,8},{1,9},{2,10},{3,11},{4,12},{5,13},{6,14},{7,15},{8,0},{9,1},... | collective-permute-start | bytes 589832 | tf_op jit(solution)/shard_map/ppermute | solution.py:474
  85.1 4.0 %shard_map.189 = (f32[128,512]{1,0:T(8,128)}, bf16[256,512]{1,0:T(8,128)(2,1)}) custom-call(bf16[512,128]{1,0:T(8,128)(2,1)} %get-tuple-element.122.refs_0_, bf16[512,128]{1,0:T(8,128)(2,1)} %get-tuple-element.94.refs_0_.refs_1_, bf16[256,384]{1,0:T(8,128)(2,1)} %get-tuple-element.79.refs_0_.refs_2_, ...), custom_call_target="tpu_custom_call" | custom-call | flops 1 | bytes 1 | tf_op jit(solution)/shard_map/pallas_call | solution.py:455
  89.1 5.8 %collective-permute-done.5 = bf16[192,512]{1,0:T(8,128)(2,1)S(1)} collective-permute-done((bf16[192,512]{1,0:T(8,128)(2,1)S(1)}, bf16[192,512]{1,0:T(8,128)(2,1)S(1)}, u32[]{:S(2)}, u32[]{:S(2)}) %collective-permute-start.5) | collective-permute-done | bytes 196640 | tf_op jit(solution)/shard_map/ppermute | solution.py:474
  95.6 1.2 add_convert_fusion.1
  96.9 2.0 %collective-permute-start.6 = (bf16[256,512]{1,0:T(8,128)(2,1)S(1)}, bf16[256,512]{1,0:T(8,128)(2,1)S(1)}, u32[]{:S(2)}, u32[]{:S(2)}) collective-permute-start(bf16[256,512]{1,0:T(8,128)(2,1)S(1)} %dynamic-slice_bitcast_fusion.2), channel_id=1, source_target_pairs={{0,4},{1,5},{2,6},{3,7},{4,0},{5,1},{6,2},{7,3},{8,12},{9,13},{10,... | collective-permute-start | bytes 786440 | tf_op jit(solution)/shard_map/ppermute | solution.py:474
  98.9 3.9 %shard_map.190.refs_4_ = f32[768,512]{1,0:T(8,128)} custom-call(bf16[768,512]{1,0:T(8,128)(2,1)} %refs_0_.3, bf16[512,512]{1,0:T(8,128)(2,1)} %get-tuple-element.127.refs_17_.refs_18_.refs_11_.refs_4_.refs_1_, bf16[256,512]{1,0:T(8,128)(2,1)} %get-tuple-element.128.refs_2_.refs_5_, bf16[1536,512]{1,0:T(8,128)(2,1)} %refs_3_.7, ...), custom_call_target="tpu_custom_call" | custom-call | flops 1 | bytes 1 | tf_op jit(solution)/shard_map/pallas_call | solution.py:455
  102.8 1.3 collective-permute-done.6
  104.2 1.5 %collective-permute-start.8 = (bf16[192,512]{1,0:T(8,128)(2,1)S(1)}, bf16[192,512]{1,0:T(8,128)(2,1)S(1)}, u32[]{:S(2)}, u32[]{:S(2)}) collective-permute-start(bf16[192,512]{1,0:T(8,128)(2,1)S(1)} %add_convert_fusion.3), channel_id=1, source_target_pairs={{0,4},{1,5},{2,6},{3,7},{4,0},{5,1},{6,2},{7,3},{8,12},{9,13},{10,... | collective-permute-start | bytes 589832 | tf_op jit(solution)/shard_map/ppermute | solution.py:474
  105.8 0.7 collective-permute-start.7
  106.5 5.0 %collective-permute-done.7 = bf16[128,512]{1,0:T(8,128)(2,1)S(1)} collective-permute-done((bf16[128,512]{1,0:T(8,128)(2,1)S(1)}, bf16[128,512]{1,0:T(8,128)(2,1)S(1)}, u32[]{:S(2)}, u32[]{:S(2)}) %collective-permute-start.7) | collective-permute-done | bytes 131104 | tf_op jit(solution)/shard_map/ppermute | solution.py:474
  111.5 2.1 %collective-permute-start.9 = (bf16[128,512]{1,0:T(8,128)(2,1)S(1)}, bf16[128,512]{1,0:T(8,128)(2,1)S(1)}, u32[]{:S(2)}, u32[]{:S(2)}) collective-permute-start(bf16[128,512]{1,0:T(8,128)(2,1)S(1)} %fusion.2), channel_id=1, source_target_pairs={{0,8},{1,9},{2,10},{3,11},{4,12},{5,13},{6,14},{7,15},{8,0},{9,1},... | collective-permute-start | bytes 393224 | tf_op jit(solution)/shard_map/ppermute | solution.py:474
  113.8 3.9 %collective-permute-done.9 = bf16[128,512]{1,0:T(8,128)(2,1)S(1)} collective-permute-done((bf16[128,512]{1,0:T(8,128)(2,1)S(1)}, bf16[128,512]{1,0:T(8,128)(2,1)S(1)}, u32[]{:S(2)}, u32[]{:S(2)}) %collective-permute-start.9) | collective-permute-done | bytes 131104 | tf_op jit(solution)/shard_map/ppermute | solution.py:474
  117.9 2.9 %collective-permute-done.11 = bf16[384,512]{1,0:T(8,128)(2,1)S(1)} collective-permute-done((bf16[384,512]{1,0:T(8,128)(2,1)S(1)}, bf16[384,512]{1,0:T(8,128)(2,1)S(1)}, u32[]{:S(2)}, u32[]{:S(2)}) %collective-permute-start.11) | collective-permute-done | bytes 393248 | tf_op jit(solution)/shard_map/ppermute | solution.py:474
  120.8 2.9 %collective-permute-done.10 = bf16[256,512]{1,0:T(8,128)(2,1)S(1)} collective-permute-done((bf16[256,512]{1,0:T(8,128)(2,1)S(1)}, bf16[256,512]{1,0:T(8,128)(2,1)S(1)}, u32[]{:S(2)}, u32[]{:S(2)}) %collective-permute-start.10) | collective-permute-done | bytes 262176 | tf_op jit(solution)/shard_map/ppermute | solution.py:474
  124.0 5.0 %collective-permute-start.14 = (bf16[768,512]{1,0:T(8,128)(2,1)S(1)}, bf16[768,512]{1,0:T(8,128)(2,1)S(1)}, u32[]{:S(2)}, u32[]{:S(2)}) collective-permute-start(bf16[768,512]{1,0:T(8,128)(2,1)S(1)} %maximum_select_fusion), channel_id=1, source_target_pairs={{0,1},{1,0},{2,3},{3,2},{4,5},{5,4},{6,7},{7,6},{8,9},{9,8},{10,11... | collective-permute-start | bytes 2359304 | tf_op jit(solution)/shard_map/ppermute | solution.py:474
  129.4 4.9 %all-to-all-start.4 = ((bf16[16,16,512]{2,1,0:T(8,128)(2,1)}), bf16[16,16,512]{2,1,0:T(8,128)(2,1)S(1)}, u32[]{:S(2)}, u32[]{:S(2)}) async-start(bf16[16,16,512]{2,1,0:T(8,128)(2,1)} %bitcast.27), calls=%async_computation.4 | async-start | bytes 524288 | tf_op jit(solution)/shard_map/all_to_all | solution.py:509
  134.5 0.8 slice.25
  135.3 1.0 pad_maximum_fusion.1
  136.3 9.6 %all-to-all-done.4 = bf16[16,16,512]{2,1,0:T(8,128)(2,1)S(1)} async-done(((bf16[16,16,512]{2,1,0:T(8,128)(2,1)}), bf16[16,16,512]{2,1,0:T(8,128)(2,1)S(1)}, u32[]{:S(2)}, u32[]{:S(2)}) %all-to-all-start.4) | async-done | bytes 262176 | tf_op jit(solution)/shard_map/all_to_all | solution.py:509
  146.6 2.0 %shard_map.191 = f32[128,512]{1,0:T(8,128)} custom-call(f32[128,512]{1,0:T(8,128)} %get-tuple-element.89.refs_0_, f32[128,512]{1,0:T(8,128)} %get-tuple-element.124.refs_1_, bf16[256,128]{1,0:T(8,128)(2,1)} %get-tuple-element.82.refs_5_.refs_2_, bf16[256,512]{1,0:T(8,128)(2,1)} %bitcast.51, f32[768,512]{1,0:T(8,128)} %shard_map.190.refs_4_), custom_call_target="tpu_custom_call" | custom-call | flops 1 | bytes 1 | tf_op jit(solution)/shard_map/pallas_call | solution.py:455
  148.6 1.0 broadcast_select_fusion.6
  149.6 1.2 pad_maximum_fusion
  (40 shorter events, 4.2 us)
Async XLA Ops:
  2.3 13.0 %all-to-all-start = ((s32[16,1,16]{2,1,0:T(1,128)}), s32[16,1,16]{2,1,0:T(1,128)S(1)}, u32[]{:S(2)}, u32[]{:S(2)}) async-start(s32[16,1,16]{2,1,0:T(1,128)} %bitcast.58), calls=%async_computation | async-start | bytes 16384 | tf_op jit(solution)/shard_map/all_to_all | solution.py:539
  15.4 0.6 copy-start.5
  18.0 13.6 %all-to-all-start.1 = ((bf16[16,16,512]{2,1,0:T(8,128)(2,1)}), bf16[16,16,512]{2,1,0:T(8,128)(2,1)S(1)}, u32[]{:S(2)}, u32[]{:S(2)}) async-start(bf16[16,16,512]{2,1,0:T(8,128)(2,1)} %bitcast.57), calls=%async_computation.1 | async-start | bytes 524288 | tf_op jit(solution)/shard_map/all_to_all | solution.py:509
  31.6 0.7 copy-start.2
  36.6 13.5 %all-to-all-start.2 = ((bf16[16,16,512]{2,1,0:T(8,128)(2,1)}), bf16[16,16,512]{2,1,0:T(8,128)(2,1)S(1)}, u32[]{:S(2)}, u32[]{:S(2)}) async-start(bf16[16,16,512]{2,1,0:T(8,128)(2,1)} %bitcast.53), calls=%async_computation.2 | async-start | bytes 524288 | tf_op jit(solution)/shard_map/all_to_all | solution.py:509
  50.1 0.7 copy-start.4
  56.2 4.3 %collective-permute-start = (bf16[768,512]{1,0:T(8,128)(2,1)}, bf16[768,512]{1,0:T(8,128)(2,1)S(1)}, u32[]{:S(2)}, u32[]{:S(2)}) collective-permute-start(bf16[768,512]{1,0:T(8,128)(2,1)} %get-tuple-element.93.refs_7_), channel_id=1, source_target_pairs={{0,1},{1,0},{2,3},{3,2},{4,5},{5,4},{6,7},{7,6},{8,9},{9,8},{10,11... | collective-permute-start | bytes 2359304 | tf_op jit(solution)/shard_map/ppermute | solution.py:474
  56.9 12.9 %all-to-all-start.3 = ((bf16[16,16,512]{2,1,0:T(8,128)(2,1)}), bf16[16,16,512]{2,1,0:T(8,128)(2,1)S(1)}, u32[]{:S(2)}, u32[]{:S(2)}) async-start(bf16[16,16,512]{2,1,0:T(8,128)(2,1)} %bitcast.56), calls=%async_computation.3 | async-start | bytes 524288 | tf_op jit(solution)/shard_map/all_to_all | solution.py:509
  61.9 14.0 %collective-permute-start.1 = (bf16[384,512]{1,0:T(8,128)(2,1)S(1)}, bf16[384,512]{1,0:T(8,128)(2,1)S(1)}, u32[]{:S(2)}, u32[]{:S(2)}) collective-permute-start(bf16[384,512]{1,0:T(8,128)(2,1)S(1)} %get-tuple-element.156), channel_id=1, source_target_pairs={{0,2},{1,3},{2,0},{3,1},{4,6},{5,7},{6,4},{7,5},{8,10},{9,11},{10,... | collective-permute-start | bytes 1179656 | tf_op jit(solution)/shard_map/ppermute | solution.py:474
  69.7 0.7 copy-start.1
  75.9 5.6 %collective-permute-start.2 = (bf16[1024,512]{1,0:T(8,128)(2,1)}, bf16[1024,512]{1,0:T(8,128)(2,1)S(1)}, u32[]{:S(2)}, u32[]{:S(2)}) collective-permute-start(bf16[1024,512]{1,0:T(8,128)(2,1)} %get-tuple-element.113.refs_12_), channel_id=1, source_target_pairs={{0,1},{1,0},{2,3},{3,2},{4,5},{5,4},{6,7},{7,6},{8,9},{9,8},{10,11... | collective-permute-start | bytes 3145736 | tf_op jit(solution)/shard_map/ppermute | solution.py:474
  76.7 6.7 %collective-permute-start.4 = (bf16[192,512]{1,0:T(8,128)(2,1)S(1)}, bf16[192,512]{1,0:T(8,128)(2,1)S(1)}, u32[]{:S(2)}, u32[]{:S(2)}) collective-permute-start(bf16[192,512]{1,0:T(8,128)(2,1)S(1)} %fusion.3), channel_id=1, source_target_pairs={{0,4},{1,5},{2,6},{3,7},{4,0},{5,1},{6,2},{7,3},{8,12},{9,13},{10,... | collective-permute-start | bytes 589832 | tf_op jit(solution)/shard_map/ppermute | solution.py:474
  82.7 12.9 %collective-permute-start.3 = (bf16[512,512]{1,0:T(8,128)(2,1)S(1)}, bf16[512,512]{1,0:T(8,128)(2,1)}, u32[]{:S(2)}, u32[]{:S(2)}) collective-permute-start(bf16[512,512]{1,0:T(8,128)(2,1)S(1)} %add_convert_fusion.2), channel_id=1, source_target_pairs={{0,2},{1,3},{2,0},{3,1},{4,6},{5,7},{6,4},{7,5},{8,10},{9,11},{10,... | collective-permute-start | bytes 1572872 | tf_op jit(solution)/shard_map/ppermute | solution.py:474
  83.5 11.4 %collective-permute-start.5 = (bf16[192,512]{1,0:T(8,128)(2,1)S(1)}, bf16[192,512]{1,0:T(8,128)(2,1)S(1)}, u32[]{:S(2)}, u32[]{:S(2)}) collective-permute-start(bf16[192,512]{1,0:T(8,128)(2,1)S(1)} %fusion.1), channel_id=1, source_target_pairs={{0,8},{1,9},{2,10},{3,11},{4,12},{5,13},{6,14},{7,15},{8,0},{9,1},... | collective-permute-start | bytes 589832 | tf_op jit(solution)/shard_map/ppermute | solution.py:474
  85.1 10.5 %copy-start = (bf16[1024,512]{1,0:T(8,128)(2,1)S(1)}, bf16[1024,512]{1,0:T(8,128)(2,1)}, u32[]{:S(2)}) copy-start(bf16[1024,512]{1,0:T(8,128)(2,1)} %shard_map.188.refs_7_) | copy-start | bytes 3145732
  96.9 7.2 %collective-permute-start.6 = (bf16[256,512]{1,0:T(8,128)(2,1)S(1)}, bf16[256,512]{1,0:T(8,128)(2,1)S(1)}, u32[]{:S(2)}, u32[]{:S(2)}) collective-permute-start(bf16[256,512]{1,0:T(8,128)(2,1)S(1)} %dynamic-slice_bitcast_fusion.2), channel_id=1, source_target_pairs={{0,4},{1,5},{2,6},{3,7},{4,0},{5,1},{6,2},{7,3},{8,12},{9,13},{10,... | collective-permute-start | bytes 786440 | tf_op jit(solution)/shard_map/ppermute | solution.py:474
  104.2 7.2 %collective-permute-start.8 = (bf16[192,512]{1,0:T(8,128)(2,1)S(1)}, bf16[192,512]{1,0:T(8,128)(2,1)S(1)}, u32[]{:S(2)}, u32[]{:S(2)}) collective-permute-start(bf16[192,512]{1,0:T(8,128)(2,1)S(1)} %add_convert_fusion.3), channel_id=1, source_target_pairs={{0,4},{1,5},{2,6},{3,7},{4,0},{5,1},{6,2},{7,3},{8,12},{9,13},{10,... | collective-permute-start | bytes 589832 | tf_op jit(solution)/shard_map/ppermute | solution.py:474
  105.8 5.7 %collective-permute-start.7 = (bf16[128,512]{1,0:T(8,128)(2,1)S(1)}, bf16[128,512]{1,0:T(8,128)(2,1)S(1)}, u32[]{:S(2)}, u32[]{:S(2)}) collective-permute-start(bf16[128,512]{1,0:T(8,128)(2,1)S(1)} %dynamic-slice_bitcast_fusion.3), channel_id=1, source_target_pairs={{0,8},{1,9},{2,10},{3,11},{4,12},{5,13},{6,14},{7,15},{8,0},{9,1},... | collective-permute-start | bytes 393224 | tf_op jit(solution)/shard_map/ppermute | solution.py:474
  111.5 6.2 %collective-permute-start.9 = (bf16[128,512]{1,0:T(8,128)(2,1)S(1)}, bf16[128,512]{1,0:T(8,128)(2,1)S(1)}, u32[]{:S(2)}, u32[]{:S(2)}) collective-permute-start(bf16[128,512]{1,0:T(8,128)(2,1)S(1)} %fusion.2), channel_id=1, source_target_pairs={{0,8},{1,9},{2,10},{3,11},{4,12},{5,13},{6,14},{7,15},{8,0},{9,1},... | collective-permute-start | bytes 393224 | tf_op jit(solution)/shard_map/ppermute | solution.py:474
  113.7 7.0 %collective-permute-start.11 = (bf16[384,512]{1,0:T(8,128)(2,1)S(1)}, bf16[384,512]{1,0:T(8,128)(2,1)S(1)}, u32[]{:S(2)}, u32[]{:S(2)}) collective-permute-start(bf16[384,512]{1,0:T(8,128)(2,1)S(1)} %maximum_select_fusion.2), channel_id=1, source_target_pairs={{0,2},{1,3},{2,0},{3,1},{4,6},{5,7},{6,4},{7,5},{8,10},{9,11},{10,... | collective-permute-start | bytes 1179656 | tf_op jit(solution)/shard_map/ppermute | solution.py:474
  117.8 5.9 %collective-permute-start.10 = (bf16[256,512]{1,0:T(8,128)(2,1)S(1)}, bf16[256,512]{1,0:T(8,128)(2,1)S(1)}, u32[]{:S(2)}, u32[]{:S(2)}) collective-permute-start(bf16[256,512]{1,0:T(8,128)(2,1)S(1)} %maximum_select_fusion.3), channel_id=1, source_target_pairs={{0,4},{1,5},{2,6},{3,7},{4,0},{5,1},{6,2},{7,3},{8,12},{9,13},{10,... | collective-permute-start | bytes 786440 | tf_op jit(solution)/shard_map/ppermute | solution.py:474
  124.0 10.3 %collective-permute-start.14 = (bf16[768,512]{1,0:T(8,128)(2,1)S(1)}, bf16[768,512]{1,0:T(8,128)(2,1)S(1)}, u32[]{:S(2)}, u32[]{:S(2)}) collective-permute-start(bf16[768,512]{1,0:T(8,128)(2,1)S(1)} %maximum_select_fusion), channel_id=1, source_target_pairs={{0,1},{1,0},{2,3},{3,2},{4,5},{5,4},{6,7},{7,6},{8,9},{9,8},{10,11... | collective-permute-start | bytes 2359304 | tf_op jit(solution)/shard_map/ppermute | solution.py:474
  129.2 16.6 %collective-permute-start.12 = (bf16[512,512]{1,0:T(8,128)(2,1)S(1)}, bf16[512,512]{1,0:T(8,128)(2,1)S(1)}, u32[]{:S(2)}, u32[]{:S(2)}) collective-permute-start(bf16[512,512]{1,0:T(8,128)(2,1)S(1)} %maximum_select_fusion.1), channel_id=1, source_target_pairs={{0,2},{1,3},{2,0},{3,1},{4,6},{5,7},{6,4},{7,5},{8,10},{9,11},{10,... | collective-permute-start | bytes 1572872 | tf_op jit(solution)/shard_map/ppermute | solution.py:474
  129.3 16.6 %collective-permute-start.13 = (bf16[512,512]{1,0:T(8,128)(2,1)S(1)}, bf16[512,512]{1,0:T(8,128)(2,1)S(1)}, u32[]{:S(2)}, u32[]{:S(2)}) collective-permute-start(bf16[512,512]{1,0:T(8,128)(2,1)S(1)} %maximum_select_fusion.1), channel_id=1, source_target_pairs={{0,1},{1,0},{2,3},{3,2},{4,5},{5,4},{6,7},{7,6},{8,9},{9,8},{10,11... | collective-permute-start | bytes 1572872 | tf_op jit(solution)/shard_map/ppermute | solution.py:474
  129.4 16.5 %all-to-all-start.4 = ((bf16[16,16,512]{2,1,0:T(8,128)(2,1)}), bf16[16,16,512]{2,1,0:T(8,128)(2,1)S(1)}, u32[]{:S(2)}, u32[]{:S(2)}) async-start(bf16[16,16,512]{2,1,0:T(8,128)(2,1)} %bitcast.27), calls=%async_computation.4 | async-start | bytes 524288 | tf_op jit(solution)/shard_map/all_to_all | solution.py:509
  145.9 0.7 copy-start.3
  145.9 2.7 %collective-permute-start.15 = (bf16[512,512]{1,0:T(8,128)(2,1)S(1)}, bf16[512,512]{1,0:T(8,128)(2,1)S(1)}, u32[]{:S(2)}, u32[]{:S(2)}) collective-permute-start(bf16[512,512]{1,0:T(8,128)(2,1)S(1)} %collective-permute-done.12), channel_id=1, source_target_pairs={{0,1},{1,0},{2,3},{3,2},{4,5},{5,4},{6,7},{7,6},{8,9},{9,8},{10,11... | collective-permute-start | bytes 1572872 | tf_op jit(solution)/shard_map/ppermute | solution.py:474

commit v11 on v10

--- a/solution.py
+++ b/solution.py
@@ -298,22 +298,22 @@
     grad_pre_ref[...] = grad_pre
 
 
-def fetch_factors(half, sources, buffers, sems, wait):
+def fetch_factors(half, sources, buffers, sems, wait=None):
     edges, inner_sender, cut_sender, inner_receiver, cut_receiver = sources[:5]
     inner_hidden, cut_hidden, inner_out, inner_pre = sources[5:]
     inner_rows, cut_rows = inner_pre.shape[0], cut_sender.shape[0]
     inner_edges = edges.at[pl.ds(0, inner_rows)]
     cut_edges = edges.at[pl.ds(inner_rows, cut_rows)]
-    low = [inner_edges, cut_edges, inner_sender, cut_sender, inner_pre, inner_pre]
-    high = [inner_receiver, cut_receiver, inner_hidden, cut_hidden, inner_pre, inner_out]
+    low = [inner_edges, cut_edges, inner_pre, inner_sender, cut_sender, inner_pre]
+    high = [inner_receiver, cut_receiver, inner_pre, inner_hidden, cut_hidden, inner_out]
 
     def each(parts):
         for index, (source, buffer) in enumerate(zip(parts, buffers)):
             copy = pltpu.make_async_copy(source, buffer, sems.at[index])
-            if wait:
+            if wait is None:
+                copy.start()
+            elif index in wait:
                 copy.wait()
-            else:
-                copy.start()
 
     @pl.when(half == 0)
     def _():
@@ -328,13 +328,15 @@
     return pl.ds(pl.multiple_of((index ^ ((me_ref[0] >> 1) & 1)) * latent, latent), latent)
 
 
-def edge_rows(me_ref, half, buffers, cut_pre, cut_out, out_ref):
+def edge_rows(me_ref, half, sources, buffers, sems, cut_pre, cut_out, out_ref):
     latent = cut_pre.shape[1]
-    first, first_cut, second, second_cut, first_right, second_right = buffers
+    first, first_cut, first_right, second, second_cut, second_right = buffers
     chosen = jnp.where(half == 0, cut_pre.astype(F32), cut_out.astype(F32)).astype(BF16)
+    fetch_factors(half, sources, buffers, sems, (0, 1, 2))
     out_ref[place_rows(me_ref, 0, latent)] = (
         dot_rows(first[...], first_right[...]) + dot_rows(first_cut[...], cut_pre)
     ).astype(BF16)
+    fetch_factors(half, sources, buffers, sems, (3, 4, 5))
     out_ref[place_rows(me_ref, 1, latent)] = (
         dot_rows(second[...], second_right[...]) + dot_rows(second_cut[...], chosen)
     ).astype(BF16)
@@ -355,7 +357,7 @@
     sources, (grad_out_ref, grad_pre_ref, out_ref), rest = refs[:9], refs[9:12], refs[12:]
     buffers, sems = rest[:-1], rest[-1]
     half = 1 - (me_ref[0] & 1)
-    fetch_factors(half, sources, buffers, sems, False)
+    fetch_factors(half, sources, buffers, sems)
     base = agg_grad_ref.shape[0]
     target = dot(receivers_ref[:, :base], agg_grad_ref[...]) + dot(
         receivers_ref[:, base:], far_grad_ref[...]
@@ -365,17 +367,17 @@
     )
     grad_out_ref[...] = grad_out
     grad_pre_ref[...] = grad_pre
-    fetch_factors(half, sources, buffers, sems, True)
-    edge_rows(me_ref, half, buffers, grad_pre, grad_out, out_ref)
+    edge_rows(me_ref, half, sources, buffers, sems, grad_pre, grad_out, out_ref)
 
 
 def edge_weights_kernel(me_ref, cut_out_ref, cut_pre_ref, *refs):
     sources, out_ref, rest = refs[:9], refs[9], refs[10:]
     buffers, sems = rest[:-1], rest[-1]
     half = me_ref[0] & 1
-    fetch_factors(half, sources, buffers, sems, False)
-    fetch_factors(half, sources, buffers, sems, True)
-    edge_rows(me_ref, half, buffers, cut_pre_ref[...], cut_out_ref[...], out_ref)
+    fetch_factors(half, sources, buffers, sems)
+    edge_rows(
+        me_ref, half, sources, buffers, sems, cut_pre_ref[...], cut_out_ref[...], out_ref
+    )
 
 
 def input_grads_kernel(
@@ -693,8 +695,9 @@
         inner_out,
         inner_pre,
     ]
-    buffers = [pltpu.VMEM((rows, latent), BF16) for rows in (inner_rows, cut_rows) * 2]
-    buffers += [pltpu.VMEM((inner_rows, latent), BF16)] * 2
+    buffers = [
+        pltpu.VMEM((rows, latent), BF16) for rows in (inner_rows, cut_rows, inner_rows) * 2
+    ]
     buffers.append(pltpu.SemaphoreType.DMA((len(buffers),)))
     cut_out, cut_pre, edge_send = line.run(
         cut_backward_kernel,
@@ -739,7 +742,6 @@
         scratch=buffers,
     )
     edge_keep, received = fence(edge_keep, received)
-    edge_own = [edge_keep[:latent], received[:latent]]
     edge_sent = added(edge_keep[latent:], received[latent:])
     edge_sent, inner_pre, cut_pre = fence(edge_sent, inner_pre, cut_pre)
     node_got = fence(node_got, edge_sent)[0]
@@ -747,6 +749,8 @@
     node_sum = added(*node_own, node_got)
     for bit in bits[3:]:
         node_sum = added(*handed(node_sum, domains, bit))
+    edge_keep, received = fence(edge_keep, received, edge_sent)[:2]
+    edge_own = added(edge_keep[:latent], received[:latent])
     local_grad, outgoing_grad = line.run(
         input_grads_kernel,
         [shaped(F32, node_rows, latent), shaped(BF16, total_slots, latent)],
@@ -760,10 +764,10 @@
             w_edge_in,
         ],
     )
-    edge_got, node_sum, inner_pre, cut_pre, local_grad = fence(
-        edge_got, node_sum, inner_pre, cut_pre, local_grad
-    )
-    edge_own, edge_sent = split([added(*edge_own, edge_got)], 2)
+    edge_own, edge_got, node_sum, inner_pre, cut_pre, local_grad = fence(
+        edge_own, edge_got, node_sum, inner_pre, cut_pre, local_grad
+    )
+    edge_own, edge_sent = split([added(edge_own, edge_got)], 2)
     edge_got = across(edge_sent, domains, 4)
     grad_edges = line.run(
         functools.partial(edge_grads_kernel, blocks=blocks),
@@ -779,20 +783,15 @@
         (blocks + 1,),
     )
     edge_got, node_sum, grad_edges = fence(edge_got, node_sum, grad_edges)
-    edge_own, edge_sent = split([added(*edge_own, edge_got)], 3)
-    edge_sent, node_sum = fence(edge_sent, node_sum)
-    edge_got, *node_parts = fence(across(edge_sent, domains, 8), *handed(node_sum, domains, 2))
     edge_sum = added(*edge_own, edge_got)
+    edge_sum, node_sum = fence(edge_sum, node_sum)
+    edge_got = across(edge_sum, domains, 8)
+    node_parts = handed(joined(handed(node_sum, domains, 2), 2), domains, 1)
+    edge_sum = added(*fence(edge_sum, edge_got))
     for bit in bits[4:]:
-        own, sent = split([edge_sum], bit)
-        edge_sum = added(*own, across(sent, domains, 1 << bit))
-    for bit in bits[:3:-1]:
-        edge_sum = joined(handed(edge_sum, domains, bit), bit)
-    node_parts = handed(joined(node_parts, 2), domains, 1)
-    edge_parts = fence(*handed(edge_sum, domains, 3))
-    edge_parts = handed(joined(edge_parts, 3), domains, 2)
+        edge_sum = added(*handed(edge_sum, domains, bit))
     *edge_parts, node_sum, other_sum, outgoing_grad = fence(
-        *edge_parts, *node_parts, outgoing_grad
+        *handed(edge_sum, domains, 2), *node_parts, outgoing_grad
     )
     edge_sum = joined(edge_parts, 2)
     node_sum = joined([node_sum, other_sum], 1)
@@ -813,9 +812,11 @@
         shaped(F32, node_rows, latent),
         [self_grad, local_grad, asked_marks, returned],
     )
-    own, other = [edge_sum, far], [near, corner]
-    low_half = [jnp.where(lower, one, two) for one, two in zip(own, other)]
-    high_half = [jnp.where(lower, two, one) for one, two in zip(own, other)]
+    high_half = [jnp.where(lower, near, edge_sum), jnp.where(lower, corner, far)]
+    grad_edge_out = jnp.where(left, high_half[1], high_half[0])
+    edge_sum, far, near, corner = fence(edge_sum, far, near, corner)
+    low_half = [jnp.where(lower, edge_sum, near), jnp.where(lower, far, corner)]
+    high_half = [jnp.where(lower, near, edge_sum), jnp.where(lower, corner, far)]
     grad_edge_in = jnp.concatenate(
         [
             jnp.where(left, low_half[0], low_half[1]),
@@ -823,7 +824,6 @@
             jnp.where(left, high_half[0], high_half[1]),
         ]
     )
-    grad_edge_out = jnp.where(left, high_half[1], high_half[0])
     return (
         new_nodes,
         new_edges,

time: 152 us -> 151 us (level)
  starting transfers between devices: 40.9 us -> 35.8 us
  waiting for transfers between devices: 49 us -> 53.8 us
    ppermute x16 -> x15, waiting for transfers between devices: 22.5 us -> 26.8 us  [across(): lax.ppermute(rows, 'dom', [(device, device ^ mask) for device in range(de...]
    ppermute x16 -> x15, starting transfers between devices: 17.1 us -> 13.3 us  [across(): lax.ppermute(rows, 'dom', [(device, device ^ mask) for device in range(de...]
    convert_element_type x8 -> x9, other arithmetic: 4.06 us -> 3.11 us  [added(): return sum((part.astype(F32) for part in parts)).astype(BF16)]
  transfers between devices with their start and end apart: 21 -> 20, of which waited for: 12 -> 12; matrix products, arithmetic and copies ran while one was open for 3% -> 4% of each run, Pallas kernels for 23% -> 23%
where the time goes in v11:
time: 151 us; the launch traced here: 150 us
  waiting for transfers between devices  53.8 us (36%)
  Pallas kernels  47.7 us (32%)
  starting transfers between devices  35.8 us (24%)
  other arithmetic  8.15 us (5%)
  local copies, waits for them, and re-layouts  3.88 us (3%)
    pallas_call x13, Pallas kernels, run(): pl.pallas_call(ordered, out_shape=out_shape, in_specs=specs, out_specs=[V...  47.7 us
    ppermute x15, waiting for transfers between devices, across(): lax.ppermute(rows, 'dom', [(device, device ^ mask) for device in range(de...  26.8 us
    all_to_all x4, waiting for transfers between devices, exchange(): lax.all_to_all(split, 'dom', split_axis=0, concat_axis=0, tiled=True)  23.3 us
    all_to_all x4, starting transfers between devices, exchange(): lax.all_to_all(split, 'dom', split_axis=0, concat_axis=0, tiled=True)  15.2 us
    ppermute x15, starting transfers between devices, across(): lax.ppermute(rows, 'dom', [(device, device ^ mask) for device in range(de...  13.3 us
    all_to_all x1, starting transfers between devices, shards(): asked = lax.all_to_all(ask, 'dom', split_axis=0, concat_axis=0, tiled=True)  7.32 us
    all_to_all x1, waiting for transfers between devices, shards(): asked = lax.all_to_all(ask, 'dom', split_axis=0, concat_axis=0, tiled=True)  3.67 us
    convert_element_type x9, other arithmetic, added(): return sum((part.astype(F32) for part in parts)).astype(BF16)  3.11 us
  transfers between devices with their start and end apart: 20, of which 12 were waited for; matrix products, arithmetic and copies ran while one was open for 4% of the time, Pallas kernels for 23%

profile of v11, /device:TPU:1, one launch (start us, length us, event | category | flops | bytes accessed | tf_op | source)
XLA Modules:
  0.0 150.1 jit_solution(9775367860608787994)
XLA Ops:
  0.6 1.7 %shard_map.179.refs_2_ = s32[16,16]{1,0:T(8,128)} custom-call(s32[1,128]{1,0:T(1,128)} %bitcast.52, s32[1,128]{1,0:T(1,128)} %bitcast.55), custom_call_target="tpu_custom_call" | custom-call | flops 1 | bytes 1 | tf_op jit(solution)/shard_map/pallas_call | solution.py:457
  2.3 7.3 %all-to-all-start = ((s32[16,1,16]{2,1,0:T(1,128)}), s32[16,1,16]{2,1,0:T(1,128)S(1)}, u32[]{:S(2)}, u32[]{:S(2)}) async-start(s32[16,1,16]{2,1,0:T(1,128)} %bitcast.50), calls=%async_computation | async-start | bytes 16384 | tf_op jit(solution)/shard_map/all_to_all | solution.py:541
  9.7 2.0 %shard_map.180 = (bf16[256,384]{1,0:T(8,128)(2,1)}, bf16[256,384]{1,0:T(8,128)(2,1)}) custom-call(s32[1,128]{1,0:T(1,128)} %bitcast.53, s32[1,128]{1,0:T(1,128)} %bitcast.56, s32[16,16]{1,0:T(8,128)} %shard_map.179.refs_2_), custom_call_target="tpu_custom_call" | custom-call | flops 1 | bytes 1 | tf_op jit(solution)/shard_map/pallas_call | solution.py:457
  11.7 3.7 %all-to-all-done = s32[16,1,16]{2,1,0:T(1,128)S(1)} async-done(((s32[16,1,16]{2,1,0:T(1,128)}), s32[16,1,16]{2,1,0:T(1,128)S(1)}, u32[]{:S(2)}, u32[]{:S(2)}) %all-to-all-start) | async-done | bytes 1056 | tf_op jit(solution)/shard_map/all_to_all | solution.py:541
  15.4 0.6 copy-done.5
  16.0 2.0 %shard_map.181 = (bf16[256,512]{1,0:T(8,128)(2,1)}, bf16[256,128]{1,0:T(8,128)(2,1)}) custom-call(s32[16,16]{1,0:T(8,128)} %bitcast.51, bf16[128,512]{1,0:T(8,128)(2,1)} %refs_4_.4, bf16[256,384]{1,0:T(8,128)(2,1)} %get-tuple-element.84.refs_2_.refs_1_.refs_3_), custom_call_target="tpu_custom_call" | custom-call | flops 1 | bytes 1 | tf_op jit(solution)/shard_map/pallas_call | solution.py:457
  18.0 4.0 %all-to-all-start.1 = ((bf16[16,16,512]{2,1,0:T(8,128)(2,1)}), bf16[16,16,512]{2,1,0:T(8,128)(2,1)S(1)}, u32[]{:S(2)}, u32[]{:S(2)}) async-start(bf16[16,16,512]{2,1,0:T(8,128)(2,1)} %bitcast.49), calls=%async_computation.1 | async-start | bytes 524288 | tf_op jit(solution)/shard_map/all_to_all | solution.py:511
  22.0 6.3 %shard_map.182 = (bf16[512,128]{1,0:T(8,128)(2,1)}, bf16[512,128]{1,0:T(8,128)(2,1)}, bf16[512,512]{1,0:T(8,128)(2,1)}, bf16[512,512]{1,0:T(8,128)(2,1)}, bf16[5...) custom-call(s32[2,256]{1,0:T(2,128)} %bitcast.54, ...), custom_call_target="tpu_custom_call" | custom-call | flops 1 | bytes 1 | tf_op jit(solution)/shard_map/pallas_call | solution.py:457
  28.3 3.3 %all-to-all-done.1 = bf16[16,16,512]{2,1,0:T(8,128)(2,1)S(1)} async-done(((bf16[16,16,512]{2,1,0:T(8,128)(2,1)}), bf16[16,16,512]{2,1,0:T(8,128)(2,1)S(1)}, u32[]{:S(2)}, u32[]{:S(2)}) %all-to-all-start.1) | async-done | bytes 262176 | tf_op jit(solution)/shard_map/all_to_all | solution.py:511
  31.6 0.7 copy-done.2
  32.3 4.3 %shard_map.183 = (bf16[256,512]{1,0:T(8,128)(2,1)}, bf16[256,512]{1,0:T(8,128)(2,1)}, bf16[256,512]{1,0:T(8,128)(2,1)}, f32[256,512]{1,0:T(8,128)}, f32[256,512]...) custom-call(bf16[256,384]{1,0:T(8,128)(2,1)} %get-tuple-element.83.refs_0_.refs_2_, ...), custom_call_target="tpu_custom_call" | custom-call | flops 1 | bytes 1 | tf_op jit(solution)/shard_map/pallas_call | solution.py:457
  36.6 4.0 %all-to-all-start.2 = ((bf16[16,16,512]{2,1,0:T(8,128)(2,1)}), bf16[16,16,512]{2,1,0:T(8,128)(2,1)S(1)}, u32[]{:S(2)}, u32[]{:S(2)}) async-start(bf16[16,16,512]{2,1,0:T(8,128)(2,1)} %bitcast.45), calls=%async_computation.2 | async-start | bytes 524288 | tf_op jit(solution)/shard_map/all_to_all | solution.py:511
  40.6 2.7 %shard_map.184.refs_8_ = bf16[768,512]{1,0:T(8,128)(2,1)} custom-call(bf16[768,512]{1,0:T(8,128)(2,1)} %refs_3_.6, f32[512,512]{1,0:T(8,128)} %get-tuple-element.90.refs_1_.refs_3_, f32[256,512]{1,0:T(8,128)} %get-tuple-element.91.refs_2_.refs_5_, bf16[256,512]{1,0:T(8,128)(2,1)} %get-tuple-element.88.refs_3_), custom_call_target="tpu_custom_call" | custom-call | flops 1 | bytes 1 | tf_op jit(solution)/shard_map/pallas_call | solution.py:457
  43.2 6.9 %all-to-all-done.2 = bf16[16,16,512]{2,1,0:T(8,128)(2,1)S(1)} async-done(((bf16[16,16,512]{2,1,0:T(8,128)(2,1)}), bf16[16,16,512]{2,1,0:T(8,128)(2,1)S(1)}, u32[]{:S(2)}, u32[]{:S(2)}) %all-to-all-start.2) | async-done | bytes 262176 | tf_op jit(solution)/shard_map/all_to_all | solution.py:511
  50.1 0.7 copy-done.4
  50.8 5.4 %shard_map.185 = (bf16[128,512]{1,0:T(8,128)(2,1)}, f32[128,512]{1,0:T(8,128)}, bf16[128,512]{1,0:T(8,128)(2,1)}, bf16[256,512]{1,0:T(8,128)(2,1)}, bf16[768,512]{1,0:T(8,128)(2,1)}, /*index=5*/bf16[768,512]{1,0:T(8,128)(2,1)}) custom-call(s32[1]{0:T(128)} %bitcast.refs_0_, bf16[256,512]{1,0:T(8,128)(2,1)} %bitcast.44, ...), custom_call_target="tpu_custom_call" | custom-call | flops 1 | bytes 1 | tf_op jit(solution)/shard_map/pallas_call | solution.py:457
  56.2 0.7 collective-permute-start
  56.8 3.6 %all-to-all-start.3 = ((bf16[16,16,512]{2,1,0:T(8,128)(2,1)}), bf16[16,16,512]{2,1,0:T(8,128)(2,1)S(1)}, u32[]{:S(2)}, u32[]{:S(2)}) async-start(bf16[16,16,512]{2,1,0:T(8,128)(2,1)} %bitcast.48), calls=%async_computation.3 | async-start | bytes 524288 | tf_op jit(solution)/shard_map/all_to_all | solution.py:511
  60.5 1.3 add_convert_fusion
  61.9 1.2 collective-permute-start.1
  63.1 3.6 %shard_map.186 = (bf16[512,512]{1,0:T(8,128)(2,1)}, bf16[512,512]{1,0:T(8,128)(2,1)}) custom-call(bf16[512,128]{1,0:T(8,128)(2,1)} %get-tuple-element.98.refs_0_.refs_1_, bf16[128,512]{1,0:T(8,128)(2,1)} %get-tuple-element.94.refs_1_.refs_2_, bf16[768,512]{1,0:T(8,128)(2,1)} %refs_0_.3, f32[512,512]{1,0:T(8,128)} %get-tuple-element.90.refs_1_.refs_3_, ...), custom_call_target="tpu_custom_call" | custom-call | flops 1 | bytes 1 | tf_op jit(solution)/shard_map/pallas_call | solution.py:457
  66.7 3.1 %all-to-all-done.3 = bf16[16,16,512]{2,1,0:T(8,128)(2,1)S(1)} async-done(((bf16[16,16,512]{2,1,0:T(8,128)(2,1)}), bf16[16,16,512]{2,1,0:T(8,128)(2,1)S(1)}, u32[]{:S(2)}, u32[]{:S(2)}) %all-to-all-start.3) | async-done | bytes 262176 | tf_op jit(solution)/shard_map/all_to_all | solution.py:511
  69.7 0.7 copy-done.1
  70.4 5.2 %shard_map.187 = (bf16[256,512]{1,0:T(8,128)(2,1)}, bf16[256,512]{1,0:T(8,128)(2,1)}, bf16[1024,512]{1,0:T(8,128)(2,1)}) custom-call(s32[1]{0:T(128)} %bitcast.refs_0_, bf16[256,384]{1,0:T(8,128)(2,1)} %get-tuple-element.84.refs_2_.refs_1_.refs_3_, bf16[128,512]{1,0:T(8,128)(2,1)} %get-tuple-element.94.refs_1_.refs_2_, bf16[256,512]{1,0:T(8,128)(2,1)} %bitcast.41, ...), custom_call_target="tpu_custom_call" | custom-call | flops 1 | bytes 1 | tf_op jit(solution)/shard_map/pallas_call | solution.py:457
  75.7 1.3 collective-permute-start.2
  77.1 4.6 %shard_map.188.refs_7_ = bf16[1024,512]{1,0:T(8,128)(2,1)} custom-call(s32[1]{0:T(128)} %bitcast.refs_0_, bf16[256,512]{1,0:T(8,128)(2,1)} %get-tuple-element.115.refs_1_, bf16[256,512]{1,0:T(8,128)(2,1)} %get-tuple-element.135.refs_2_.refs_5_, bf16[768,512]{1,0:T(8,128)(2,1)} %refs_3_.6, bf16[512,512]{1,0:T(8,128)(2,1)} %get-tuple-element.105.refs_10_.refs_4_, ...), custom_call_target="tpu_custom_call" | custom-call | flops 1 | bytes 1 | tf_op jit(solution)/shard_map/pallas_call | solution.py:457
  81.7 1.2 add_convert_fusion.3
  83.7 1.2 collective-permute-start.5
  84.9 4.0 %shard_map.189 = (f32[128,512]{1,0:T(8,128)}, bf16[256,512]{1,0:T(8,128)(2,1)}) custom-call(bf16[512,128]{1,0:T(8,128)(2,1)} %get-tuple-element.128.refs_0_, bf16[512,128]{1,0:T(8,128)(2,1)} %get-tuple-element.98.refs_0_.refs_1_, bf16[256,384]{1,0:T(8,128)(2,1)} %get-tuple-element.83.refs_0_.refs_2_, ...), custom_call_target="tpu_custom_call" | custom-call | flops 1 | bytes 1 | tf_op jit(solution)/shard_map/pallas_call | solution.py:457
  89.0 6.1 %collective-permute-done.5 = bf16[192,512]{1,0:T(8,128)(2,1)S(1)} collective-permute-done((bf16[192,512]{1,0:T(8,128)(2,1)S(1)}, bf16[192,512]{1,0:T(8,128)(2,1)S(1)}, u32[]{:S(2)}, u32[]{:S(2)}) %collective-permute-start.5) | collective-permute-done | bytes 196640 | tf_op jit(solution)/shard_map/ppermute | solution.py:476
  95.2 1.1 collective-permute-done.3
  96.4 1.4 collective-permute-start.6
  97.8 3.9 %shard_map.190.refs_4_ = f32[768,512]{1,0:T(8,128)} custom-call(bf16[768,512]{1,0:T(8,128)(2,1)} %refs_0_.3, bf16[512,512]{1,0:T(8,128)(2,1)} %get-tuple-element.134.refs_17_.refs_18_.refs_11_.refs_4_.refs_1_, bf16[256,512]{1,0:T(8,128)(2,1)} %get-tuple-element.135.refs_2_.refs_5_, bf16[1536,512]{1,0:T(8,128)(2,1)} %refs_3_.7, ...), custom_call_target="tpu_custom_call" | custom-call | flops 1 | bytes 1 | tf_op jit(solution)/shard_map/pallas_call | solution.py:457
  101.7 1.5 %collective-permute-done.6 = bf16[256,512]{1,0:T(8,128)(2,1)S(1)} collective-permute-done((bf16[256,512]{1,0:T(8,128)(2,1)S(1)}, bf16[256,512]{1,0:T(8,128)(2,1)S(1)}, u32[]{:S(2)}, u32[]{:S(2)}) %collective-permute-start.6) | collective-permute-done | bytes 262176 | tf_op jit(solution)/shard_map/ppermute | solution.py:476
  103.3 1.3 collective-permute-start.9
  104.7 0.7 collective-permute-start.7
  105.4 2.5 %collective-permute-done.9 = bf16[192,512]{1,0:T(8,128)(2,1)S(1)} collective-permute-done((bf16[192,512]{1,0:T(8,128)(2,1)S(1)}, bf16[192,512]{1,0:T(8,128)(2,1)S(1)}, u32[]{:S(2)}, u32[]{:S(2)}) %collective-permute-start.9) | collective-permute-done | bytes 196640 | tf_op jit(solution)/shard_map/ppermute | solution.py:476
  108.5 9.5 %collective-permute-done.7 = bf16[256,512]{1,0:T(8,128)(2,1)S(1)} collective-permute-done((bf16[256,512]{1,0:T(8,128)(2,1)S(1)}, bf16[256,512]{1,0:T(8,128)(2,1)S(1)}, u32[]{:S(2)}, u32[]{:S(2)}) %collective-permute-start.7) | collective-permute-done | bytes 262176 | tf_op jit(solution)/shard_map/ppermute | solution.py:476
  118.2 5.9 %collective-permute-done.8 = bf16[256,512]{1,0:T(8,128)(2,1)S(1)} collective-permute-done((bf16[256,512]{1,0:T(8,128)(2,1)S(1)}, bf16[256,512]{1,0:T(8,128)(2,1)S(1)}, u32[]{:S(2)}, u32[]{:S(2)}) %collective-permute-start.8) | collective-permute-done | bytes 262176 | tf_op jit(solution)/shard_map/ppermute | solution.py:476
  124.4 2.9 %collective-permute-start.13 = (bf16[768,512]{1,0:T(8,128)(2,1)S(1)}, bf16[768,512]{1,0:T(8,128)(2,1)S(1)}, u32[]{:S(2)}, u32[]{:S(2)}) collective-permute-start(bf16[768,512]{1,0:T(8,128)(2,1)S(1)} %maximum_select_fusion), channel_id=1, source_target_pairs={{0,1},{1,0},{2,3},{3,2},{4,5},{5,4},{6,7},{7,6},{8,9},{9,8},{10,11... | collective-permute-start | bytes 2359304 | tf_op jit(solution)/shard_map/ppermute | solution.py:476
  127.5 0.7 collective-permute-start.11
  128.5 3.5 %all-to-all-start.4 = ((bf16[16,16,512]{2,1,0:T(8,128)(2,1)}), bf16[16,16,512]{2,1,0:T(8,128)(2,1)S(1)}, u32[]{:S(2)}, u32[]{:S(2)}) async-start(bf16[16,16,512]{2,1,0:T(8,128)(2,1)} %bitcast.24), calls=%async_computation.4 | async-start | bytes 524288 | tf_op jit(solution)/shard_map/all_to_all | solution.py:511
  132.1 0.8 slice.25
  133.0 1.0 pad_maximum_fusion.1
  134.0 10.1 %all-to-all-done.4 = bf16[16,16,512]{2,1,0:T(8,128)(2,1)S(1)} async-done(((bf16[16,16,512]{2,1,0:T(8,128)(2,1)}), bf16[16,16,512]{2,1,0:T(8,128)(2,1)S(1)}, u32[]{:S(2)}, u32[]{:S(2)}) %all-to-all-start.4) | async-done | bytes 262176 | tf_op jit(solution)/shard_map/all_to_all | solution.py:511
  144.8 2.0 %shard_map.191 = f32[128,512]{1,0:T(8,128)} custom-call(f32[128,512]{1,0:T(8,128)} %get-tuple-element.93.refs_0_, f32[128,512]{1,0:T(8,128)} %get-tuple-element.130.refs_1_, bf16[256,128]{1,0:T(8,128)(2,1)} %get-tuple-element.86.refs_5_.refs_2_, bf16[256,512]{1,0:T(8,128)(2,1)} %bitcast.43, f32[768,512]{1,0:T(8,128)} %shard_map.190.refs_4_), custom_call_target="tpu_custom_call" | custom-call | flops 1 | bytes 1 | tf_op jit(solution)/shard_map/pallas_call | solution.py:457
  146.9 2.0 %broadcast_select_fusion.5 = (bf16[512,512]{1,0:T(8,128)(2,1)S(1)}, bf16[512,512]{1,0:T(8,128)(2,1)S(1)}, bf16[512,512]{1,0:T(8,128)(2,1)S(1)}, bf16[512,512]{1,0:T(8,128)(2,1)}) fusion(pred[]{:T(512)S(6)} %eq.13, bf16[512,512]{1,0:T(8,128)(2,1)S(1)} %maximum_select_fusion.1, bf16[512,512]{1,0:T(8,128)(2,1)} %collective-permute-done.12, pred[]{:T(512)S(6)} %eq.12, ...), kind=kLoop, calls=%fused_computation.18 | loop fusion | flops 2621440 | bytes 4194306 | tf_op jit(solution)/shard_map/jit(_where)/select_n | solution.py:822
  148.9 1.2 pad_maximum_fusion
  (37 shorter events, 3.8 us)
Async XLA Ops:
  2.3 13.0 %all-to-all-start = ((s32[16,1,16]{2,1,0:T(1,128)}), s32[16,1,16]{2,1,0:T(1,128)S(1)}, u32[]{:S(2)}, u32[]{:S(2)}) async-start(s32[16,1,16]{2,1,0:T(1,128)} %bitcast.50), calls=%async_computation | async-start | bytes 16384 | tf_op jit(solution)/shard_map/all_to_all | solution.py:541
  15.4 0.6 copy-start.5
  18.0 13.6 %all-to-all-start.1 = ((bf16[16,16,512]{2,1,0:T(8,128)(2,1)}), bf16[16,16,512]{2,1,0:T(8,128)(2,1)S(1)}, u32[]{:S(2)}, u32[]{:S(2)}) async-start(bf16[16,16,512]{2,1,0:T(8,128)(2,1)} %bitcast.49), calls=%async_computation.1 | async-start | bytes 524288 | tf_op jit(solution)/shard_map/all_to_all | solution.py:511
  31.6 0.7 copy-start.2
  36.6 13.5 %all-to-all-start.2 = ((bf16[16,16,512]{2,1,0:T(8,128)(2,1)}), bf16[16,16,512]{2,1,0:T(8,128)(2,1)S(1)}, u32[]{:S(2)}, u32[]{:S(2)}) async-start(bf16[16,16,512]{2,1,0:T(8,128)(2,1)} %bitcast.45), calls=%async_computation.2 | async-start | bytes 524288 | tf_op jit(solution)/shard_map/all_to_all | solution.py:511
  50.1 0.7 copy-start.4
  56.2 4.3 %collective-permute-start = (bf16[768,512]{1,0:T(8,128)(2,1)}, bf16[768,512]{1,0:T(8,128)(2,1)S(1)}, u32[]{:S(2)}, u32[]{:S(2)}) collective-permute-start(bf16[768,512]{1,0:T(8,128)(2,1)} %get-tuple-element.97.refs_7_), channel_id=1, source_target_pairs={{0,1},{1,0},{2,3},{3,2},{4,5},{5,4},{6,7},{7,6},{8,9},{9,8},{10,11... | collective-permute-start | bytes 2359304 | tf_op jit(solution)/shard_map/ppermute | solution.py:476
  56.8 12.9 %all-to-all-start.3 = ((bf16[16,16,512]{2,1,0:T(8,128)(2,1)}), bf16[16,16,512]{2,1,0:T(8,128)(2,1)S(1)}, u32[]{:S(2)}, u32[]{:S(2)}) async-start(bf16[16,16,512]{2,1,0:T(8,128)(2,1)} %bitcast.48), calls=%async_computation.3 | async-start | bytes 524288 | tf_op jit(solution)/shard_map/all_to_all | solution.py:511
  61.9 13.8 %collective-permute-start.1 = (bf16[384,512]{1,0:T(8,128)(2,1)S(1)}, bf16[384,512]{1,0:T(8,128)(2,1)S(1)}, u32[]{:S(2)}, u32[]{:S(2)}) collective-permute-start(bf16[384,512]{1,0:T(8,128)(2,1)S(1)} %get-tuple-element.163), channel_id=1, source_target_pairs={{0,2},{1,3},{2,0},{3,1},{4,6},{5,7},{6,4},{7,5},{8,10},{9,11},{10,... | collective-permute-start | bytes 1179656 | tf_op jit(solution)/shard_map/ppermute | solution.py:476
  69.7 0.7 copy-start.1
  75.7 6.0 %collective-permute-start.2 = (bf16[1024,512]{1,0:T(8,128)(2,1)}, bf16[1024,512]{1,0:T(8,128)(2,1)S(1)}, u32[]{:S(2)}, u32[]{:S(2)}) collective-permute-start(bf16[1024,512]{1,0:T(8,128)(2,1)} %get-tuple-element.117.refs_12_), channel_id=1, source_target_pairs={{0,1},{1,0},{2,3},{3,2},{4,5},{5,4},{6,7},{7,6},{8,9},{9,8},{10,11... | collective-permute-start | bytes 3145736 | tf_op jit(solution)/shard_map/ppermute | solution.py:476
  77.0 6.6 %collective-permute-start.4 = (bf16[192,512]{1,0:T(8,128)(2,1)S(1)}, bf16[192,512]{1,0:T(8,128)(2,1)S(1)}, u32[]{:S(2)}, u32[]{:S(2)}) collective-permute-start(bf16[192,512]{1,0:T(8,128)(2,1)S(1)} %fusion.2), channel_id=1, source_target_pairs={{0,4},{1,5},{2,6},{3,7},{4,0},{5,1},{6,2},{7,3},{8,12},{9,13},{10,... | collective-permute-start | bytes 589832 | tf_op jit(solution)/shard_map/ppermute | solution.py:476
  82.9 13.4 %collective-permute-start.3 = (bf16[512,512]{1,0:T(8,128)(2,1)S(1)}, bf16[512,512]{1,0:T(8,128)(2,1)S(1)}, u32[]{:S(2)}, u32[]{:S(2)}) collective-permute-start(bf16[512,512]{1,0:T(8,128)(2,1)S(1)} %add_convert_fusion.3), channel_id=1, source_target_pairs={{0,2},{1,3},{2,0},{3,1},{4,6},{5,7},{6,4},{7,5},{8,10},{9,11},{10,... | collective-permute-start | bytes 1572872 | tf_op jit(solution)/shard_map/ppermute | solution.py:476
  83.7 11.4 %collective-permute-start.5 = (bf16[192,512]{1,0:T(8,128)(2,1)S(1)}, bf16[192,512]{1,0:T(8,128)(2,1)S(1)}, u32[]{:S(2)}, u32[]{:S(2)}) collective-permute-start(bf16[192,512]{1,0:T(8,128)(2,1)S(1)} %fusion.1), channel_id=1, source_target_pairs={{0,8},{1,9},{2,10},{3,11},{4,12},{5,13},{6,14},{7,15},{8,0},{9,1},... | collective-permute-start | bytes 589832 | tf_op jit(solution)/shard_map/ppermute | solution.py:476
  84.9 4.0 %copy-start = (bf16[1024,512]{1,0:T(8,128)(2,1)S(1)}, bf16[1024,512]{1,0:T(8,128)(2,1)}, u32[]{:S(2)}) copy-start(bf16[1024,512]{1,0:T(8,128)(2,1)} %shard_map.188.refs_7_) | copy-start | bytes 3145732
  96.4 6.8 %collective-permute-start.6 = (bf16[256,512]{1,0:T(8,128)(2,1)S(1)}, bf16[256,512]{1,0:T(8,128)(2,1)S(1)}, u32[]{:S(2)}, u32[]{:S(2)}) collective-permute-start(bf16[256,512]{1,0:T(8,128)(2,1)S(1)} %dynamic-slice_bitcast_fusion.2), channel_id=1, source_target_pairs={{0,4},{1,5},{2,6},{3,7},{4,0},{5,1},{6,2},{7,3},{8,12},{9,13},{10,... | collective-permute-start | bytes 786440 | tf_op jit(solution)/shard_map/ppermute | solution.py:476
  103.3 4.6 %collective-permute-start.9 = (bf16[192,512]{1,0:T(8,128)(2,1)S(1)}, bf16[192,512]{1,0:T(8,128)(2,1)S(1)}, u32[]{:S(2)}, u32[]{:S(2)}) collective-permute-start(bf16[192,512]{1,0:T(8,128)(2,1)S(1)} %add_convert_fusion.5), channel_id=1, source_target_pairs={{0,4},{1,5},{2,6},{3,7},{4,0},{5,1},{6,2},{7,3},{8,12},{9,13},{10,... | collective-permute-start | bytes 589832 | tf_op jit(solution)/shard_map/ppermute | solution.py:476
  104.7 13.4 %collective-permute-start.7 = (bf16[256,512]{1,0:T(8,128)(2,1)S(1)}, bf16[256,512]{1,0:T(8,128)(2,1)S(1)}, u32[]{:S(2)}, u32[]{:S(2)}) collective-permute-start(bf16[256,512]{1,0:T(8,128)(2,1)S(1)} %fusion), channel_id=1, source_target_pairs={{0,8},{1,9},{2,10},{3,11},{4,12},{5,13},{6,14},{7,15},{8,0},{9,1},... | collective-permute-start | bytes 786440 | tf_op jit(solution)/shard_map/ppermute | solution.py:476
  108.0 16.0 %collective-permute-start.10 = (bf16[384,512]{1,0:T(8,128)(2,1)S(1)}, bf16[384,512]{1,0:T(8,128)(2,1)S(1)}, u32[]{:S(2)}, u32[]{:S(2)}) collective-permute-start(bf16[384,512]{1,0:T(8,128)(2,1)S(1)} %maximum_select_fusion.2), channel_id=1, source_target_pairs={{0,2},{1,3},{2,0},{3,1},{4,6},{5,7},{6,4},{7,5},{8,10},{9,11},{10,... | collective-permute-start | bytes 1179656 | tf_op jit(solution)/shard_map/ppermute | solution.py:476
  118.1 6.0 %collective-permute-start.8 = (bf16[256,512]{1,0:T(8,128)(2,1)S(1)}, bf16[256,512]{1,0:T(8,128)(2,1)S(1)}, u32[]{:S(2)}, u32[]{:S(2)}) collective-permute-start(bf16[256,512]{1,0:T(8,128)(2,1)S(1)} %add_convert_fusion.4), channel_id=1, source_target_pairs={{0,4},{1,5},{2,6},{3,7},{4,0},{5,1},{6,2},{7,3},{8,12},{9,13},{10,... | collective-permute-start | bytes 786440 | tf_op jit(solution)/shard_map/ppermute | solution.py:476
  124.4 7.6 %collective-permute-start.13 = (bf16[768,512]{1,0:T(8,128)(2,1)S(1)}, bf16[768,512]{1,0:T(8,128)(2,1)S(1)}, u32[]{:S(2)}, u32[]{:S(2)}) collective-permute-start(bf16[768,512]{1,0:T(8,128)(2,1)S(1)} %maximum_select_fusion), channel_id=1, source_target_pairs={{0,1},{1,0},{2,3},{3,2},{4,5},{5,4},{6,7},{7,6},{8,9},{9,8},{10,11... | collective-permute-start | bytes 2359304 | tf_op jit(solution)/shard_map/ppermute | solution.py:476
  127.5 16.6 %collective-permute-start.11 = (bf16[512,512]{1,0:T(8,128)(2,1)S(1)}, bf16[512,512]{1,0:T(8,128)(2,1)S(1)}, u32[]{:S(2)}, u32[]{:S(2)}) collective-permute-start(bf16[512,512]{1,0:T(8,128)(2,1)S(1)} %maximum_select_fusion.1), channel_id=1, source_target_pairs={{0,2},{1,3},{2,0},{3,1},{4,6},{5,7},{6,4},{7,5},{8,10},{9,11},{10,... | collective-permute-start | bytes 1572872 | tf_op jit(solution)/shard_map/ppermute | solution.py:476
  128.2 15.9 %collective-permute-start.12 = (bf16[512,512]{1,0:T(8,128)(2,1)S(1)}, bf16[512,512]{1,0:T(8,128)(2,1)}, u32[]{:S(2)}, u32[]{:S(2)}) collective-permute-start(bf16[512,512]{1,0:T(8,128)(2,1)S(1)} %maximum_select_fusion.1), channel_id=1, source_target_pairs={{0,1},{1,0},{2,3},{3,2},{4,5},{5,4},{6,7},{7,6},{8,9},{9,8},{10,11... | collective-permute-start | bytes 1572872 | tf_op jit(solution)/shard_map/ppermute | solution.py:476
  128.5 15.6 %all-to-all-start.4 = ((bf16[16,16,512]{2,1,0:T(8,128)(2,1)}), bf16[16,16,512]{2,1,0:T(8,128)(2,1)S(1)}, u32[]{:S(2)}, u32[]{:S(2)}) async-start(bf16[16,16,512]{2,1,0:T(8,128)(2,1)} %bitcast.24), calls=%async_computation.4 | async-start | bytes 524288 | tf_op jit(solution)/shard_map/all_to_all | solution.py:511
  144.1 0.7 copy-start.3
  144.1 2.7 %collective-permute-start.14 = (bf16[512,512]{1,0:T(8,128)(2,1)S(1)}, bf16[512,512]{1,0:T(8,128)(2,1)S(1)}, u32[]{:S(2)}, u32[]{:S(2)}) collective-permute-start(bf16[512,512]{1,0:T(8,128)(2,1)S(1)} %collective-permute-done.11), channel_id=1, source_target_pairs={{0,1},{1,0},{2,3},{3,2},{4,5},{5,4},{6,7},{7,6},{8,9},{9,8},{10,11... | collective-permute-start | bytes 1572872 | tf_op jit(solution)/shard_map/ppermute | solution.py:476

commit v12 on v11

--- a/solution.py
+++ b/solution.py
@@ -159,8 +159,8 @@
         edges_ref[...], sender, receiver, w_in_ref, w_out_ref
     )
     hidden_ref[...] = hidden
-    slope_ref[...] = slope
-    normed_ref[...] = normed
+    slope_ref[...] = slope.astype(BF16)
+    normed_ref[...] = normed.astype(BF16)
     scale_ref[...] = inv_scale
     part = dot_rows(receivers, normed.astype(BF16))
 
@@ -204,8 +204,8 @@
         edges_ref[...], sender, receiver, w_in_ref, w_out_ref
     )
     hidden_ref[...] = hidden
-    slope_ref[...] = slope
-    normed_ref[...] = normed
+    slope_ref[...] = slope.astype(BF16)
+    normed_ref[...] = normed.astype(BF16)
     scale_ref[...] = inv_scale
     message = normed.astype(BF16)
     total_ref[...] = inner_total_ref[...] + dot_rows(receivers_ref[:, :base], message)
@@ -216,7 +216,7 @@
     inner_rows = inner_ref.shape[0]
 
     def added(edge, normed):
-        return (edge.astype(F32) + normed.astype(BF16).astype(F32)).astype(BF16)
+        return (edge.astype(F32) + normed.astype(F32)).astype(BF16)
 
     out_ref[:inner_rows] = added(edges_ref[:inner_rows], inner_ref[...])
     out_ref[inner_rows:] = added(edges_ref[inner_rows:], cut_ref[...])
@@ -271,8 +271,9 @@
 
 
 def edge_backward(ct, target_grads, normed, inv_scale, slope, w_out):
-    grad_out = norm_backward(ct.astype(F32) + target_grads, normed, inv_scale)
-    return grad_out, (dot_cols(grad_out, w_out) * slope).astype(BF16)
+    upstream = ct.astype(F32) + target_grads
+    grad_out = norm_backward(upstream, normed.astype(F32), inv_scale)
+    return grad_out, (dot_cols(grad_out, w_out) * slope.astype(F32)).astype(BF16)
 
 
 def inner_backward_kernel(
@@ -332,11 +333,10 @@
     latent = cut_pre.shape[1]
     first, first_cut, first_right, second, second_cut, second_right = buffers
     chosen = jnp.where(half == 0, cut_pre.astype(F32), cut_out.astype(F32)).astype(BF16)
-    fetch_factors(half, sources, buffers, sems, (0, 1, 2))
+    fetch_factors(half, sources, buffers, sems, range(6))
     out_ref[place_rows(me_ref, 0, latent)] = (
         dot_rows(first[...], first_right[...]) + dot_rows(first_cut[...], cut_pre)
     ).astype(BF16)
-    fetch_factors(half, sources, buffers, sems, (3, 4, 5))
     out_ref[place_rows(me_ref, 1, latent)] = (
         dot_rows(second[...], second_right[...]) + dot_rows(second_cut[...], chosen)
     ).astype(BF16)
@@ -561,7 +561,7 @@
         return pl.BlockSpec(array.shape, lambda step: (0, 0))
 
     saved_widths = [node_rows, node_rows, latent, latent, latent, latent, latent, 1]
-    saved_types = [BF16, BF16, BF16, BF16, BF16, F32, F32, F32]
+    saved_types = [BF16] * 7 + [F32]
     (
         inner_senders,
         inner_receivers,
@@ -784,39 +784,36 @@
     )
     edge_got, node_sum, grad_edges = fence(edge_got, node_sum, grad_edges)
     edge_sum = added(*edge_own, edge_got)
-    edge_sum, node_sum = fence(edge_sum, node_sum)
+    edge_sum, node_sum, outgoing_grad = fence(edge_sum, node_sum, outgoing_grad)
     edge_got = across(edge_sum, domains, 8)
     node_parts = handed(joined(handed(node_sum, domains, 2), 2), domains, 1)
-    edge_sum = added(*fence(edge_sum, edge_got))
+    returned = exchange(outgoing_grad, domains)
+    edge_sum, edge_got, returned = fence(edge_sum, edge_got, returned)
+    edge_sum = added(edge_sum, edge_got)
     for bit in bits[4:]:
         edge_sum = added(*handed(edge_sum, domains, bit))
-    *edge_parts, node_sum, other_sum, outgoing_grad = fence(
-        *handed(edge_sum, domains, 2), *node_parts, outgoing_grad
+    grad_nodes = line.run(
+        node_grads_kernel,
+        shaped(F32, node_rows, latent),
+        [self_grad, local_grad, asked_marks, returned],
+    )
+    *edge_parts, node_sum, other_sum, grad_nodes = fence(
+        *handed(edge_sum, domains, 2), *node_parts, grad_nodes
     )
     edge_sum = joined(edge_parts, 2)
     node_sum = joined([node_sum, other_sum], 1)
     far, near = across(edge_sum, domains, 2), across(edge_sum, domains, 1)
     others = across(node_sum, domains, 1)
-    returned = exchange(outgoing_grad, domains)
     lower, left = place_of(0) == 0, place_of(1) == 0
     low_rows, high_rows = jnp.where(lower, node_sum, others), jnp.where(lower, others, node_sum)
     cut_at = 2 * latent - low_rows.shape[0]
     grad_node_in = jnp.concatenate([low_rows, high_rows[:cut_at]])
     grad_node_out = high_rows[cut_at:]
-    far, near, grad_node_in, grad_node_out, returned = fence(
-        far, near, grad_node_in, grad_node_out, returned
-    )
+    far, near, grad_node_in, grad_node_out = fence(far, near, grad_node_in, grad_node_out)
     corner = across(far, domains, 1)
-    grad_nodes = line.run(
-        node_grads_kernel,
-        shaped(F32, node_rows, latent),
-        [self_grad, local_grad, asked_marks, returned],
-    )
+    low_half = [jnp.where(lower, edge_sum, near), jnp.where(lower, far, corner)]
     high_half = [jnp.where(lower, near, edge_sum), jnp.where(lower, corner, far)]
     grad_edge_out = jnp.where(left, high_half[1], high_half[0])
-    edge_sum, far, near, corner = fence(edge_sum, far, near, corner)
-    low_half = [jnp.where(lower, edge_sum, near), jnp.where(lower, far, corner)]
-    high_half = [jnp.where(lower, near, edge_sum), jnp.where(lower, corner, far)]
     grad_edge_in = jnp.concatenate(
         [
             jnp.where(left, low_half[0], low_half[1]),

time: 151 us -> 158 us (1.046)
  starting transfers between devices: 35.8 us -> 41.4 us
  waiting for transfers between devices: 53.8 us -> 55.8 us
    ppermute x15, waiting for transfers between devices: 26.8 us -> 38.4 us  [across(): lax.ppermute(rows, 'dom', [(device, device ^ mask) for device in range(de...]
    all_to_all x4, waiting for transfers between devices: 23.3 us -> 13.8 us  [exchange(): lax.all_to_all(split, 'dom', split_axis=0, concat_axis=0, tiled=True)]
    ppermute x15, starting transfers between devices: 13.3 us -> 16.6 us  [across(): lax.ppermute(rows, 'dom', [(device, device ^ mask) for device in range(de...]
    all_to_all x4, starting transfers between devices: 15.2 us -> 17.6 us  [exchange(): lax.all_to_all(split, 'dom', split_axis=0, concat_axis=0, tiled=True)]
  transfers between devices with their start and end apart: 20 -> 20, of which waited for: 12 -> 14; matrix products, arithmetic and copies ran while one was open for 4% -> 3% of each run, Pallas kernels for 23% -> 22%
where the time goes in v12:
time: 158 us; the launch traced here: 157 us
  waiting for transfers between devices  55.8 us (35%)
  Pallas kernels  47.3 us (30%)
  starting transfers between devices  41.4 us (26%)
  other arithmetic  7.11 us (4%)
  local copies, waits for them, and re-layouts  4.19 us (3%)
    pallas_call x13, Pallas kernels, run(): pl.pallas_call(ordered, out_shape=out_shape, in_specs=specs, out_specs=[V...  47.3 us
    ppermute x15, waiting for transfers between devices, across(): lax.ppermute(rows, 'dom', [(device, device ^ mask) for device in range(de...  38.4 us
    all_to_all x4, starting transfers between devices, exchange(): lax.all_to_all(split, 'dom', split_axis=0, concat_axis=0, tiled=True)  17.6 us
    ppermute x15, starting transfers between devices, across(): lax.ppermute(rows, 'dom', [(device, device ^ mask) for device in range(de...  16.6 us
    all_to_all x4, waiting for transfers between devices, exchange(): lax.all_to_all(split, 'dom', split_axis=0, concat_axis=0, tiled=True)  13.8 us
    all_to_all x1, starting transfers between devices, shards(): asked = lax.all_to_all(ask, 'dom', split_axis=0, concat_axis=0, tiled=True)  7.32 us
    all_to_all x1, waiting for transfers between devices, shards(): asked = lax.all_to_all(ask, 'dom', split_axis=0, concat_axis=0, tiled=True)  3.67 us
    unnamed x12, local copies, waits for them, and re-layouts  3.26 us
  transfers between devices with their start and end apart: 20, of which 14 were waited for; matrix products, arithmetic and copies ran while one was open for 3% of the time, Pallas kernels for 22%

profile of v12, /device:TPU:1, one launch (start us, length us, event | category | flops | bytes accessed | tf_op | source)
XLA Modules:
  0.0 156.6 jit_solution(7669296072773996631)
XLA Ops:
  0.6 1.7 %shard_map.179.refs_2_ = s32[16,16]{1,0:T(8,128)} custom-call(s32[1,128]{1,0:T(1,128)} %bitcast.52, s32[1,128]{1,0:T(1,128)} %bitcast.55), custom_call_target="tpu_custom_call" | custom-call | flops 1 | bytes 1 | tf_op jit(solution)/shard_map/pallas_call | solution.py:457
  2.3 7.3 %all-to-all-start = ((s32[16,1,16]{2,1,0:T(1,128)}), s32[16,1,16]{2,1,0:T(1,128)S(1)}, u32[]{:S(2)}, u32[]{:S(2)}) async-start(s32[16,1,16]{2,1,0:T(1,128)} %bitcast.50), calls=%async_computation | async-start | bytes 16384 | tf_op jit(solution)/shard_map/all_to_all | solution.py:541
  9.7 2.0 %shard_map.180 = (bf16[256,384]{1,0:T(8,128)(2,1)}, bf16[256,384]{1,0:T(8,128)(2,1)}) custom-call(s32[1,128]{1,0:T(1,128)} %bitcast.53, s32[1,128]{1,0:T(1,128)} %bitcast.56, s32[16,16]{1,0:T(8,128)} %shard_map.179.refs_2_), custom_call_target="tpu_custom_call" | custom-call | flops 1 | bytes 1 | tf_op jit(solution)/shard_map/pallas_call | solution.py:457
  11.7 3.7 %all-to-all-done = s32[16,1,16]{2,1,0:T(1,128)S(1)} async-done(((s32[16,1,16]{2,1,0:T(1,128)}), s32[16,1,16]{2,1,0:T(1,128)S(1)}, u32[]{:S(2)}, u32[]{:S(2)}) %all-to-all-start) | async-done | bytes 1056 | tf_op jit(solution)/shard_map/all_to_all | solution.py:541
  16.0 2.0 %shard_map.181 = (bf16[256,512]{1,0:T(8,128)(2,1)}, bf16[256,128]{1,0:T(8,128)(2,1)}) custom-call(s32[16,16]{1,0:T(8,128)} %bitcast.51, bf16[128,512]{1,0:T(8,128)(2,1)} %refs_4_.4, bf16[256,384]{1,0:T(8,128)(2,1)} %get-tuple-element.81.refs_2_.refs_1_.refs_3_), custom_call_target="tpu_custom_call" | custom-call | flops 1 | bytes 1 | tf_op jit(solution)/shard_map/pallas_call | solution.py:457
  18.0 4.0 %all-to-all-start.1 = ((bf16[16,16,512]{2,1,0:T(8,128)(2,1)}), bf16[16,16,512]{2,1,0:T(8,128)(2,1)S(1)}, u32[]{:S(2)}, u32[]{:S(2)}) async-start(bf16[16,16,512]{2,1,0:T(8,128)(2,1)} %bitcast.49), calls=%async_computation.1 | async-start | bytes 524288 | tf_op jit(solution)/shard_map/all_to_all | solution.py:511
  22.0 6.1 %shard_map.182 = (bf16[512,128]{1,0:T(8,128)(2,1)}, bf16[512,128]{1,0:T(8,128)(2,1)}, bf16[512,512]{1,0:T(8,128)(2,1)}, bf16[512,512]{1,0:T(8,128)(2,1)}, bf16[5...) custom-call(s32[2,256]{1,0:T(2,128)} %bitcast.54, ...), custom_call_target="tpu_custom_call" | custom-call | flops 1 | bytes 1 | tf_op jit(solution)/shard_map/pallas_call | solution.py:457
  28.2 3.4 %all-to-all-done.1 = bf16[16,16,512]{2,1,0:T(8,128)(2,1)S(1)} async-done(((bf16[16,16,512]{2,1,0:T(8,128)(2,1)}), bf16[16,16,512]{2,1,0:T(8,128)(2,1)S(1)}, u32[]{:S(2)}, u32[]{:S(2)}) %all-to-all-start.1) | async-done | bytes 262176 | tf_op jit(solution)/shard_map/all_to_all | solution.py:511
  31.6 0.7 copy-done.2
  32.3 4.2 %shard_map.183 = (bf16[256,512]{1,0:T(8,128)(2,1)}, bf16[256,512]{1,0:T(8,128)(2,1)}, bf16[256,512]{1,0:T(8,128)(2,1)}, bf16[256,512]{1,0:T(8,128)(2,1)}, bf16[2...) custom-call(bf16[256,384]{1,0:T(8,128)(2,1)} %get-tuple-element.80.refs_0_.refs_2_, ...), custom_call_target="tpu_custom_call" | custom-call | flops 1 | bytes 1 | tf_op jit(solution)/shard_map/pallas_call | solution.py:457
  36.5 4.0 %all-to-all-start.2 = ((bf16[16,16,512]{2,1,0:T(8,128)(2,1)}), bf16[16,16,512]{2,1,0:T(8,128)(2,1)S(1)}, u32[]{:S(2)}, u32[]{:S(2)}) async-start(bf16[16,16,512]{2,1,0:T(8,128)(2,1)} %bitcast.43), calls=%async_computation.2 | async-start | bytes 524288 | tf_op jit(solution)/shard_map/all_to_all | solution.py:511
  40.5 2.4 %shard_map.184.refs_8_ = bf16[768,512]{1,0:T(8,128)(2,1)} custom-call(bf16[768,512]{1,0:T(8,128)(2,1)} %refs_3_.6, bf16[512,512]{1,0:T(8,128)(2,1)} %get-tuple-element.87.refs_1_.refs_3_, bf16[256,512]{1,0:T(8,128)(2,1)} %get-tuple-element.88.refs_2_.refs_5_, bf16[256,512]{1,0:T(8,128)(2,1)} %get-tuple-element.85.refs_3_), custom_call_target="tpu_custom_call" | custom-call | flops 1 | bytes 1 | tf_op jit(solution)/shard_map/pallas_call | solution.py:457
  42.9 7.1 %all-to-all-done.2 = bf16[16,16,512]{2,1,0:T(8,128)(2,1)S(1)} async-done(((bf16[16,16,512]{2,1,0:T(8,128)(2,1)}), bf16[16,16,512]{2,1,0:T(8,128)(2,1)S(1)}, u32[]{:S(2)}, u32[]{:S(2)}) %all-to-all-start.2) | async-done | bytes 262176 | tf_op jit(solution)/shard_map/all_to_all | solution.py:511
  50.8 5.4 %shard_map.185 = (bf16[128,512]{1,0:T(8,128)(2,1)}, f32[128,512]{1,0:T(8,128)}, bf16[128,512]{1,0:T(8,128)(2,1)}, bf16[256,512]{1,0:T(8,128)(2,1)}, bf16[768,512]{1,0:T(8,128)(2,1)}, /*index=5*/bf16[768,512]{1,0:T(8,128)(2,1)}) custom-call(s32[1]{0:T(128)} %bitcast.refs_0_, bf16[256,512]{1,0:T(8,128)(2,1)} %bitcast.45, ...), custom_call_target="tpu_custom_call" | custom-call | flops 1 | bytes 1 | tf_op jit(solution)/shard_map/pallas_call | solution.py:457
  56.8 3.4 %all-to-all-start.3 = ((bf16[16,16,512]{2,1,0:T(8,128)(2,1)}), bf16[16,16,512]{2,1,0:T(8,128)(2,1)S(1)}, u32[]{:S(2)}, u32[]{:S(2)}) async-start(bf16[16,16,512]{2,1,0:T(8,128)(2,1)} %bitcast.48), calls=%async_computation.3 | async-start | bytes 524288 | tf_op jit(solution)/shard_map/all_to_all | solution.py:511
  60.2 1.3 add_convert_fusion
  61.7 1.3 collective-permute-start.1
  63.0 3.5 %shard_map.186 = (bf16[512,512]{1,0:T(8,128)(2,1)}, bf16[512,512]{1,0:T(8,128)(2,1)}) custom-call(bf16[512,128]{1,0:T(8,128)(2,1)} %get-tuple-element.94.refs_0_.refs_1_, bf16[128,512]{1,0:T(8,128)(2,1)} %get-tuple-element.90.refs_1_.refs_2_, bf16[768,512]{1,0:T(8,128)(2,1)} %refs_0_.3, bf16[512,512]{1,0:T(8,128)(2,1)} %get-tuple-element.87.refs_1_.refs_3_, ...), custom_call_target="tpu_custom_call" | custom-call | flops 1 | bytes 1 | tf_op jit(solution)/shard_map/pallas_call | solution.py:457
  66.5 3.2 %all-to-all-done.3 = bf16[16,16,512]{2,1,0:T(8,128)(2,1)S(1)} async-done(((bf16[16,16,512]{2,1,0:T(8,128)(2,1)}), bf16[16,16,512]{2,1,0:T(8,128)(2,1)S(1)}, u32[]{:S(2)}, u32[]{:S(2)}) %all-to-all-start.3) | async-done | bytes 262176 | tf_op jit(solution)/shard_map/all_to_all | solution.py:511
  70.4 5.3 %shard_map.187 = (bf16[256,512]{1,0:T(8,128)(2,1)}, bf16[256,512]{1,0:T(8,128)(2,1)}, bf16[1024,512]{1,0:T(8,128)(2,1)}) custom-call(s32[1]{0:T(128)} %bitcast.refs_0_, bf16[256,384]{1,0:T(8,128)(2,1)} %get-tuple-element.81.refs_2_.refs_1_.refs_3_, bf16[128,512]{1,0:T(8,128)(2,1)} %get-tuple-element.90.refs_1_.refs_2_, bf16[256,512]{1,0:T(8,128)(2,1)} %bitcast.41, ...), custom_call_target="tpu_custom_call" | custom-call | flops 1 | bytes 1 | tf_op jit(solution)/shard_map/pallas_call | solution.py:457
  75.7 0.8 collective-permute-start.2
  76.6 4.8 %shard_map.188.refs_7_ = bf16[1024,512]{1,0:T(8,128)(2,1)} custom-call(s32[1]{0:T(128)} %bitcast.refs_0_, bf16[256,512]{1,0:T(8,128)(2,1)} %get-tuple-element.111.refs_1_, bf16[256,512]{1,0:T(8,128)(2,1)} %get-tuple-element.130.refs_2_.refs_5_, bf16[768,512]{1,0:T(8,128)(2,1)} %refs_3_.6, bf16[512,512]{1,0:T(8,128)(2,1)} %get-tuple-element.101.refs_10_.refs_4_, ...), custom_call_target="tpu_custom_call" | custom-call | flops 1 | bytes 1 | tf_op jit(solution)/shard_map/pallas_call | solution.py:457
  81.3 1.2 add_convert_fusion.3
  82.5 0.8 collective-permute-start.3
  83.4 1.7 %collective-permute-start.5 = (bf16[192,512]{1,0:T(8,128)(2,1)S(1)}, bf16[192,512]{1,0:T(8,128)(2,1)S(1)}, u32[]{:S(2)}, u32[]{:S(2)}) collective-permute-start(bf16[192,512]{1,0:T(8,128)(2,1)S(1)} %fusion.1), channel_id=1, source_target_pairs={{0,8},{1,9},{2,10},{3,11},{4,12},{5,13},{6,14},{7,15},{8,0},{9,1},... | collective-permute-start | bytes 589832 | tf_op jit(solution)/shard_map/ppermute | solution.py:476
  85.1 3.9 %shard_map.189 = (f32[128,512]{1,0:T(8,128)}, bf16[256,512]{1,0:T(8,128)(2,1)}) custom-call(bf16[512,128]{1,0:T(8,128)(2,1)} %get-tuple-element.124.refs_0_, bf16[512,128]{1,0:T(8,128)(2,1)} %get-tuple-element.94.refs_0_.refs_1_, bf16[256,384]{1,0:T(8,128)(2,1)} %get-tuple-element.80.refs_0_.refs_2_, ...), custom_call_target="tpu_custom_call" | custom-call | flops 1 | bytes 1 | tf_op jit(solution)/shard_map/pallas_call | solution.py:457
  89.2 5.7 %collective-permute-done.5 = bf16[192,512]{1,0:T(8,128)(2,1)S(1)} collective-permute-done((bf16[192,512]{1,0:T(8,128)(2,1)S(1)}, bf16[192,512]{1,0:T(8,128)(2,1)S(1)}, u32[]{:S(2)}, u32[]{:S(2)}) %collective-permute-start.5) | collective-permute-done | bytes 196640 | tf_op jit(solution)/shard_map/ppermute | solution.py:476
  95.5 2.0 %collective-permute-start.6 = (bf16[256,512]{1,0:T(8,128)(2,1)S(1)}, bf16[256,512]{1,0:T(8,128)(2,1)S(1)}, u32[]{:S(2)}, u32[]{:S(2)}) collective-permute-start(bf16[256,512]{1,0:T(8,128)(2,1)S(1)} %dynamic-slice_bitcast_fusion.2), channel_id=1, source_target_pairs={{0,4},{1,5},{2,6},{3,7},{4,0},{5,1},{6,2},{7,3},{8,12},{9,13},{10,... | collective-permute-start | bytes 786440 | tf_op jit(solution)/shard_map/ppermute | solution.py:476
  97.5 3.9 %shard_map.190.refs_4_ = f32[768,512]{1,0:T(8,128)} custom-call(bf16[768,512]{1,0:T(8,128)(2,1)} %refs_0_.3, bf16[512,512]{1,0:T(8,128)(2,1)} %get-tuple-element.129.refs_17_.refs_18_.refs_11_.refs_4_.refs_1_, bf16[256,512]{1,0:T(8,128)(2,1)} %get-tuple-element.130.refs_2_.refs_5_, bf16[1536,512]{1,0:T(8,128)(2,1)} %refs_3_.7, ...), custom_call_target="tpu_custom_call" | custom-call | flops 1 | bytes 1 | tf_op jit(solution)/shard_map/pallas_call | solution.py:457
  101.4 1.3 collective-permute-done.6
  102.7 6.1 %all-to-all-start.4 = ((bf16[16,16,512]{2,1,0:T(8,128)(2,1)}), bf16[16,16,512]{2,1,0:T(8,128)(2,1)S(1)}, u32[]{:S(2)}, u32[]{:S(2)}) async-start(bf16[16,16,512]{2,1,0:T(8,128)(2,1)} %bitcast.24), calls=%async_computation.4 | async-start | bytes 524288 | tf_op jit(solution)/shard_map/all_to_all | solution.py:511
  108.8 1.4 collective-permute-start.9
  110.2 2.1 %collective-permute-start.7 = (bf16[256,512]{1,0:T(8,128)(2,1)S(1)}, bf16[256,512]{1,0:T(8,128)(2,1)S(1)}, u32[]{:S(2)}, u32[]{:S(2)}) collective-permute-start(bf16[256,512]{1,0:T(8,128)(2,1)S(1)} %fusion), channel_id=1, source_target_pairs={{0,8},{1,9},{2,10},{3,11},{4,12},{5,13},{6,14},{7,15},{8,0},{9,1},... | collective-permute-start | bytes 786440 | tf_op jit(solution)/shard_map/ppermute | solution.py:476
  112.3 11.1 %collective-permute-done.9 = bf16[192,512]{1,0:T(8,128)(2,1)S(1)} collective-permute-done((bf16[192,512]{1,0:T(8,128)(2,1)S(1)}, bf16[192,512]{1,0:T(8,128)(2,1)S(1)}, u32[]{:S(2)}, u32[]{:S(2)}) %collective-permute-start.9) | collective-permute-done | bytes 196640 | tf_op jit(solution)/shard_map/ppermute | solution.py:476
  123.6 1.2 collective-permute-start.10
  124.8 4.1 %collective-permute-done.7 = bf16[256,512]{1,0:T(8,128)(2,1)S(1)} collective-permute-done((bf16[256,512]{1,0:T(8,128)(2,1)S(1)}, bf16[256,512]{1,0:T(8,128)(2,1)S(1)}, u32[]{:S(2)}, u32[]{:S(2)}) %collective-permute-start.7) | collective-permute-done | bytes 262176 | tf_op jit(solution)/shard_map/ppermute | solution.py:476
  129.7 2.0 %shard_map.191 = f32[128,512]{1,0:T(8,128)} custom-call(f32[128,512]{1,0:T(8,128)} %get-tuple-element.139.refs_0_, f32[128,512]{1,0:T(8,128)} %get-tuple-element.140.refs_1_, bf16[256,128]{1,0:T(8,128)(2,1)} %get-tuple-element.83.refs_5_.refs_2_, bf16[256,512]{1,0:T(8,128)(2,1)} %bitcast.44, f32[768,512]{1,0:T(8,128)} %shard_map.190.refs_4_), custom_call_target="tpu_custom_call" | custom-call | flops 1 | bytes 1 | tf_op jit(solution)/shard_map/pallas_call | solution.py:457
  131.7 1.7 %collective-permute-done.10 = bf16[384,512]{1,0:T(8,128)(2,1)S(1)} collective-permute-done((bf16[384,512]{1,0:T(8,128)(2,1)S(1)}, bf16[384,512]{1,0:T(8,128)(2,1)S(1)}, u32[]{:S(2)}, u32[]{:S(2)}) %collective-permute-start.10) | collective-permute-done | bytes 393248 | tf_op jit(solution)/shard_map/ppermute | solution.py:476
  133.4 2.6 %collective-permute-done.8 = bf16[256,512]{1,0:T(8,128)(2,1)S(1)} collective-permute-done((bf16[256,512]{1,0:T(8,128)(2,1)S(1)}, bf16[256,512]{1,0:T(8,128)(2,1)S(1)}, u32[]{:S(2)}, u32[]{:S(2)}) %collective-permute-start.8) | collective-permute-done | bytes 262176 | tf_op jit(solution)/shard_map/ppermute | solution.py:476
  136.3 1.8 %collective-permute-start.13 = (bf16[768,512]{1,0:T(8,128)(2,1)S(1)}, bf16[768,512]{1,0:T(8,128)(2,1)S(1)}, u32[]{:S(2)}, u32[]{:S(2)}) collective-permute-start(bf16[768,512]{1,0:T(8,128)(2,1)S(1)} %maximum_select_fusion), channel_id=1, source_target_pairs={{0,1},{1,0},{2,3},{3,2},{4,5},{5,4},{6,7},{7,6},{8,9},{9,8},{10,11... | collective-permute-start | bytes 2359304 | tf_op jit(solution)/shard_map/ppermute | solution.py:476
  138.5 1.2 collective-permute-start.11
  140.2 0.8 slice.25
  141.1 1.0 pad_maximum_fusion.1
  142.1 9.5 %collective-permute-done.11 = bf16[512,512]{1,0:T(8,128)(2,1)S(1)} collective-permute-done((bf16[512,512]{1,0:T(8,128)(2,1)S(1)}, bf16[512,512]{1,0:T(8,128)(2,1)S(1)}, u32[]{:S(2)}, u32[]{:S(2)}) %collective-permute-start.11) | collective-permute-done | bytes 524320 | tf_op jit(solution)/shard_map/ppermute | solution.py:476
  151.6 1.3 collective-permute-start.14
  152.9 1.5 collective-permute-done.14
  154.4 1.0 broadcast_select_fusion.6
  155.4 1.2 pad_maximum_fusion
  (37 shorter events, 5.7 us)
Async XLA Ops:
  2.3 13.0 %all-to-all-start = ((s32[16,1,16]{2,1,0:T(1,128)}), s32[16,1,16]{2,1,0:T(1,128)S(1)}, u32[]{:S(2)}, u32[]{:S(2)}) async-start(s32[16,1,16]{2,1,0:T(1,128)} %bitcast.50), calls=%async_computation | async-start | bytes 16384 | tf_op jit(solution)/shard_map/all_to_all | solution.py:541
  15.4 0.6 copy-start.5
  18.0 13.6 %all-to-all-start.1 = ((bf16[16,16,512]{2,1,0:T(8,128)(2,1)}), bf16[16,16,512]{2,1,0:T(8,128)(2,1)S(1)}, u32[]{:S(2)}, u32[]{:S(2)}) async-start(bf16[16,16,512]{2,1,0:T(8,128)(2,1)} %bitcast.49), calls=%async_computation.1 | async-start | bytes 524288 | tf_op jit(solution)/shard_map/all_to_all | solution.py:511
  31.6 0.7 copy-start.2
  36.5 13.6 %all-to-all-start.2 = ((bf16[16,16,512]{2,1,0:T(8,128)(2,1)}), bf16[16,16,512]{2,1,0:T(8,128)(2,1)S(1)}, u32[]{:S(2)}, u32[]{:S(2)}) async-start(bf16[16,16,512]{2,1,0:T(8,128)(2,1)} %bitcast.43), calls=%async_computation.2 | async-start | bytes 524288 | tf_op jit(solution)/shard_map/all_to_all | solution.py:511
  50.1 0.7 copy-start.4
  56.1 4.1 %collective-permute-start = (bf16[768,512]{1,0:T(8,128)(2,1)}, bf16[768,512]{1,0:T(8,128)(2,1)S(1)}, u32[]{:S(2)}, u32[]{:S(2)}) collective-permute-start(bf16[768,512]{1,0:T(8,128)(2,1)} %get-tuple-element.93.refs_7_), channel_id=1, source_target_pairs={{0,1},{1,0},{2,3},{3,2},{4,5},{5,4},{6,7},{7,6},{8,9},{9,8},{10,11... | collective-permute-start | bytes 2359304 | tf_op jit(solution)/shard_map/ppermute | solution.py:476
  56.8 12.9 %all-to-all-start.3 = ((bf16[16,16,512]{2,1,0:T(8,128)(2,1)}), bf16[16,16,512]{2,1,0:T(8,128)(2,1)S(1)}, u32[]{:S(2)}, u32[]{:S(2)}) async-start(bf16[16,16,512]{2,1,0:T(8,128)(2,1)} %bitcast.48), calls=%async_computation.3 | async-start | bytes 524288 | tf_op jit(solution)/shard_map/all_to_all | solution.py:511
  61.7 14.0 %collective-permute-start.1 = (bf16[384,512]{1,0:T(8,128)(2,1)S(1)}, bf16[384,512]{1,0:T(8,128)(2,1)S(1)}, u32[]{:S(2)}, u32[]{:S(2)}) collective-permute-start(bf16[384,512]{1,0:T(8,128)(2,1)S(1)} %get-tuple-element.158), channel_id=1, source_target_pairs={{0,2},{1,3},{2,0},{3,1},{4,6},{5,7},{6,4},{7,5},{8,10},{9,11},{10,... | collective-permute-start | bytes 1179656 | tf_op jit(solution)/shard_map/ppermute | solution.py:476
  69.7 0.7 copy-start.1
  75.7 5.7 %collective-permute-start.2 = (bf16[1024,512]{1,0:T(8,128)(2,1)}, bf16[1024,512]{1,0:T(8,128)(2,1)S(1)}, u32[]{:S(2)}, u32[]{:S(2)}) collective-permute-start(bf16[1024,512]{1,0:T(8,128)(2,1)} %get-tuple-element.113.refs_12_), channel_id=1, source_target_pairs={{0,1},{1,0},{2,3},{3,2},{4,5},{5,4},{6,7},{7,6},{8,9},{9,8},{10,11... | collective-permute-start | bytes 3145736 | tf_op jit(solution)/shard_map/ppermute | solution.py:476
  76.5 6.8 %collective-permute-start.4 = (bf16[192,512]{1,0:T(8,128)(2,1)S(1)}, bf16[192,512]{1,0:T(8,128)(2,1)S(1)}, u32[]{:S(2)}, u32[]{:S(2)}) collective-permute-start(bf16[192,512]{1,0:T(8,128)(2,1)S(1)} %fusion.2), channel_id=1, source_target_pairs={{0,4},{1,5},{2,6},{3,7},{4,0},{5,1},{6,2},{7,3},{8,12},{9,13},{10,... | collective-permute-start | bytes 589832 | tf_op jit(solution)/shard_map/ppermute | solution.py:476
  82.5 12.8 %collective-permute-start.3 = (bf16[512,512]{1,0:T(8,128)(2,1)S(1)}, bf16[512,512]{1,0:T(8,128)(2,1)S(1)}, u32[]{:S(2)}, u32[]{:S(2)}) collective-permute-start(bf16[512,512]{1,0:T(8,128)(2,1)S(1)} %add_convert_fusion.3), channel_id=1, source_target_pairs={{0,2},{1,3},{2,0},{3,1},{4,6},{5,7},{6,4},{7,5},{8,10},{9,11},{10,... | collective-permute-start | bytes 1572872 | tf_op jit(solution)/shard_map/ppermute | solution.py:476
  83.4 11.5 %collective-permute-start.5 = (bf16[192,512]{1,0:T(8,128)(2,1)S(1)}, bf16[192,512]{1,0:T(8,128)(2,1)S(1)}, u32[]{:S(2)}, u32[]{:S(2)}) collective-permute-start(bf16[192,512]{1,0:T(8,128)(2,1)S(1)} %fusion.1), channel_id=1, source_target_pairs={{0,8},{1,9},{2,10},{3,11},{4,12},{5,13},{6,14},{7,15},{8,0},{9,1},... | collective-permute-start | bytes 589832 | tf_op jit(solution)/shard_map/ppermute | solution.py:476
  85.1 3.9 %copy-start = (bf16[1024,512]{1,0:T(8,128)(2,1)S(1)}, bf16[1024,512]{1,0:T(8,128)(2,1)}, u32[]{:S(2)}) copy-start(bf16[1024,512]{1,0:T(8,128)(2,1)} %shard_map.188.refs_7_) | copy-start | bytes 3145732
  95.5 7.2 %collective-permute-start.6 = (bf16[256,512]{1,0:T(8,128)(2,1)S(1)}, bf16[256,512]{1,0:T(8,128)(2,1)S(1)}, u32[]{:S(2)}, u32[]{:S(2)}) collective-permute-start(bf16[256,512]{1,0:T(8,128)(2,1)S(1)} %dynamic-slice_bitcast_fusion.2), channel_id=1, source_target_pairs={{0,4},{1,5},{2,6},{3,7},{4,0},{5,1},{6,2},{7,3},{8,12},{9,13},{10,... | collective-permute-start | bytes 786440 | tf_op jit(solution)/shard_map/ppermute | solution.py:476
  102.7 26.2 %all-to-all-start.4 = ((bf16[16,16,512]{2,1,0:T(8,128)(2,1)}), bf16[16,16,512]{2,1,0:T(8,128)(2,1)S(1)}, u32[]{:S(2)}, u32[]{:S(2)}) async-start(bf16[16,16,512]{2,1,0:T(8,128)(2,1)} %bitcast.24), calls=%async_computation.4 | async-start | bytes 524288 | tf_op jit(solution)/shard_map/all_to_all | solution.py:511
  108.8 14.6 %collective-permute-start.9 = (bf16[192,512]{1,0:T(8,128)(2,1)S(1)}, bf16[192,512]{1,0:T(8,128)(2,1)S(1)}, u32[]{:S(2)}, u32[]{:S(2)}) collective-permute-start(bf16[192,512]{1,0:T(8,128)(2,1)S(1)} %add_convert_fusion.5), channel_id=1, source_target_pairs={{0,4},{1,5},{2,6},{3,7},{4,0},{5,1},{6,2},{7,3},{8,12},{9,13},{10,... | collective-permute-start | bytes 589832 | tf_op jit(solution)/shard_map/ppermute | solution.py:476
  110.2 18.7 %collective-permute-start.7 = (bf16[256,512]{1,0:T(8,128)(2,1)S(1)}, bf16[256,512]{1,0:T(8,128)(2,1)S(1)}, u32[]{:S(2)}, u32[]{:S(2)}) collective-permute-start(bf16[256,512]{1,0:T(8,128)(2,1)S(1)} %fusion), channel_id=1, source_target_pairs={{0,8},{1,9},{2,10},{3,11},{4,12},{5,13},{6,14},{7,15},{8,0},{9,1},... | collective-permute-start | bytes 786440 | tf_op jit(solution)/shard_map/ppermute | solution.py:476
  123.6 9.8 %collective-permute-start.10 = (bf16[384,512]{1,0:T(8,128)(2,1)S(1)}, bf16[384,512]{1,0:T(8,128)(2,1)S(1)}, u32[]{:S(2)}, u32[]{:S(2)}) collective-permute-start(bf16[384,512]{1,0:T(8,128)(2,1)S(1)} %maximum_select_fusion.2), channel_id=1, source_target_pairs={{0,2},{1,3},{2,0},{3,1},{4,6},{5,7},{6,4},{7,5},{8,10},{9,11},{10,... | collective-permute-start | bytes 1179656 | tf_op jit(solution)/shard_map/ppermute | solution.py:476
  128.9 0.7 copy-start.3
  129.0 7.0 %collective-permute-start.8 = (bf16[256,512]{1,0:T(8,128)(2,1)S(1)}, bf16[256,512]{1,0:T(8,128)(2,1)S(1)}, u32[]{:S(2)}, u32[]{:S(2)}) collective-permute-start(bf16[256,512]{1,0:T(8,128)(2,1)S(1)} %add_convert_fusion.4), channel_id=1, source_target_pairs={{0,4},{1,5},{2,6},{3,7},{4,0},{5,1},{6,2},{7,3},{8,12},{9,13},{10,... | collective-permute-start | bytes 786440 | tf_op jit(solution)/shard_map/ppermute | solution.py:476
  136.3 3.7 %collective-permute-start.13 = (bf16[768,512]{1,0:T(8,128)(2,1)S(1)}, bf16[768,512]{1,0:T(8,128)(2,1)S(1)}, u32[]{:S(2)}, u32[]{:S(2)}) collective-permute-start(bf16[768,512]{1,0:T(8,128)(2,1)S(1)} %maximum_select_fusion), channel_id=1, source_target_pairs={{0,1},{1,0},{2,3},{3,2},{4,5},{5,4},{6,7},{7,6},{8,9},{9,8},{10,11... | collective-permute-start | bytes 2359304 | tf_op jit(solution)/shard_map/ppermute | solution.py:476
  138.4 3.7 %collective-permute-start.12 = (bf16[512,512]{1,0:T(8,128)(2,1)S(1)}, bf16[512,512]{1,0:T(8,128)(2,1)S(1)}, u32[]{:S(2)}, u32[]{:S(2)}) collective-permute-start(bf16[512,512]{1,0:T(8,128)(2,1)S(1)} %maximum_select_fusion.1), channel_id=1, source_target_pairs={{0,1},{1,0},{2,3},{3,2},{4,5},{5,4},{6,7},{7,6},{8,9},{9,8},{10,11... | collective-permute-start | bytes 1572872 | tf_op jit(solution)/shard_map/ppermute | solution.py:476
  138.5 13.1 %collective-permute-start.11 = (bf16[512,512]{1,0:T(8,128)(2,1)S(1)}, bf16[512,512]{1,0:T(8,128)(2,1)S(1)}, u32[]{:S(2)}, u32[]{:S(2)}) collective-permute-start(bf16[512,512]{1,0:T(8,128)(2,1)S(1)} %maximum_select_fusion.1), channel_id=1, source_target_pairs={{0,2},{1,3},{2,0},{3,1},{4,6},{5,7},{6,4},{7,5},{8,10},{9,11},{10,... | collective-permute-start | bytes 1572872 | tf_op jit(solution)/shard_map/ppermute | solution.py:476
  151.6 2.8 %collective-permute-start.14 = (bf16[512,512]{1,0:T(8,128)(2,1)S(1)}, bf16[512,512]{1,0:T(8,128)(2,1)S(1)}, u32[]{:S(2)}, u32[]{:S(2)}) collective-permute-start(bf16[512,512]{1,0:T(8,128)(2,1)S(1)} %collective-permute-done.11), channel_id=1, source_target_pairs={{0,1},{1,0},{2,3},{3,2},{4,5},{5,4},{6,7},{7,6},{8,9},{9,8},{10,11... | collective-permute-start | bytes 1572872 | tf_op jit(solution)/shard_map/ppermute | solution.py:476

commit v13 on v11

--- a/solution.py
+++ b/solution.py
@@ -90,20 +90,6 @@
     rank_marks = jnp.where(rank == iota((rank.shape[0], slots), 1).astype(F32), 1.0, 0.0)
     wanted = (rank_marks * to_column(remote_ref[...])).astype(BF16)
     ask_ref[...] = dot_rows(dest_marks, wanted).astype(jnp.int32)
-
-
-def reply_kernel(asked_ref, nodes_ref, reply_ref, asked_marks_ref):
-    domains, slots = asked_ref.shape
-    total = domains * slots
-    shift = slots.bit_length() - 1
-    spread = marks((iota((total, domains), 0) >> shift) == iota((total, domains), 1))
-    listed = dot(spread, asked_ref[...].astype(F32).astype(BF16))
-    at_slot = (iota((total, slots), 0) & (slots - 1)) == iota((total, slots), 1)
-    column = jnp.sum(jnp.where(at_slot, listed, 0.0), axis=1, keepdims=True)
-    node_rows = nodes_ref.shape[0]
-    asked_marks = marks(column == iota((total, node_rows), 1).astype(F32))
-    asked_marks_ref[...] = asked_marks
-    reply_ref[...] = dot(asked_marks, nodes_ref[...]).astype(BF16)
 
 
 def cut_marks_kernel(dest_ref, local_ref, senders_ref, receivers_ref, *, domains, slots):
@@ -298,7 +284,7 @@
     grad_pre_ref[...] = grad_pre
 
 
-def fetch_factors(half, sources, buffers, sems, wait=None):
+def fetch_factors(half, sources, buffers, sems, wait=False):
     edges, inner_sender, cut_sender, inner_receiver, cut_receiver = sources[:5]
     inner_hidden, cut_hidden, inner_out, inner_pre = sources[5:]
     inner_rows, cut_rows = inner_pre.shape[0], cut_sender.shape[0]
@@ -310,10 +296,10 @@
     def each(parts):
         for index, (source, buffer) in enumerate(zip(parts, buffers)):
             copy = pltpu.make_async_copy(source, buffer, sems.at[index])
-            if wait is None:
+            if wait:
+                copy.wait()
+            else:
                 copy.start()
-            elif index in wait:
-                copy.wait()
 
     @pl.when(half == 0)
     def _():
@@ -332,11 +318,10 @@
     latent = cut_pre.shape[1]
     first, first_cut, first_right, second, second_cut, second_right = buffers
     chosen = jnp.where(half == 0, cut_pre.astype(F32), cut_out.astype(F32)).astype(BF16)
-    fetch_factors(half, sources, buffers, sems, (0, 1, 2))
+    fetch_factors(half, sources, buffers, sems, True)
     out_ref[place_rows(me_ref, 0, latent)] = (
         dot_rows(first[...], first_right[...]) + dot_rows(first_cut[...], cut_pre)
     ).astype(BF16)
-    fetch_factors(half, sources, buffers, sems, (3, 4, 5))
     out_ref[place_rows(me_ref, 1, latent)] = (
         dot_rows(second[...], second_right[...]) + dot_rows(second_cut[...], chosen)
     ).astype(BF16)
@@ -420,12 +405,6 @@
     @pl.when(jnp.logical_not(inside))
     def _():
         out_ref[...] = ct_ref[...].astype(F32) + dot_cols(cut_pre_ref[...], w_edge_ref[...])
-
-
-def node_grads_kernel(self_ref, local_ref, asked_marks_ref, returned_ref, out_ref):
-    out_ref[...] = (
-        self_ref[...] + local_ref[...] + dot_rows(asked_marks_ref[...], returned_ref[...])
-    )
 
 
 VMEM = pl.BlockSpec(memory_space=pltpu.VMEM)
@@ -544,11 +523,12 @@
         [shaped(BF16, cut_rows, table)] * 2,
         [cut_dest.reshape(1, -1), cut_local.reshape(1, -1)],
     )
-    reply, asked_marks = line.run(
-        reply_kernel,
-        [shaped(BF16, total_slots, latent), shaped(BF16, total_slots, node_rows)],
-        [asked, nodes],
-    )
+    asked_marks = jnp.where(
+        asked[:, :, None] == jnp.arange(node_rows, dtype=jnp.int32)[None, None], 1.0, 0.0
+    ).astype(BF16)
+    reply = lax.dot_general(asked_marks, nodes, (((2,), (0,)), ((), ())), preferred_element_type=F32)
+    reply = reply.astype(BF16).reshape(total_slots, latent)
+    asked_marks = asked_marks.reshape(total_slots, node_rows)
     far = exchange(reply, domains)
 
     block = cut_rows
@@ -807,16 +787,10 @@
         far, near, grad_node_in, grad_node_out, returned
     )
     corner = across(far, domains, 1)
-    grad_nodes = line.run(
-        node_grads_kernel,
-        shaped(F32, node_rows, latent),
-        [self_grad, local_grad, asked_marks, returned],
-    )
+    grad_nodes = self_grad + local_grad + dot_rows(asked_marks, returned)
+    low_half = [jnp.where(lower, edge_sum, near), jnp.where(lower, far, corner)]
     high_half = [jnp.where(lower, near, edge_sum), jnp.where(lower, corner, far)]
     grad_edge_out = jnp.where(left, high_half[1], high_half[0])
-    edge_sum, far, near, corner = fence(edge_sum, far, near, corner)
-    low_half = [jnp.where(lower, edge_sum, near), jnp.where(lower, far, corner)]
-    high_half = [jnp.where(lower, near, edge_sum), jnp.where(lower, corner, far)]
     grad_edge_in = jnp.concatenate(
         [
             jnp.where(left, low_half[0], low_half[1]),

time: 151 us -> 151 us (level)
  blocking collectives: 0 us -> 13 us
  starting transfers between devices: 35.8 us -> 28.8 us
  waiting for transfers between devices: 53.8 us -> 46.9 us
  Pallas kernels: 47.7 us -> 44.1 us
  matrix products: 0 us -> 2.87 us
    all_to_all x0 -> x1, blocking collectives: none -> 13 us  [shards(): asked = lax.all_to_all(ask, 'dom', split_axis=0, concat_axis=0, tiled=True)]
    all_to_all x1 -> x0, starting transfers between devices: 7.32 us -> none  [shards(): asked = lax.all_to_all(ask, 'dom', split_axis=0, concat_axis=0, tiled=True)]
    all_to_all x1 -> x0, waiting for transfers between devices: 3.67 us -> none  [shards(): asked = lax.all_to_all(ask, 'dom', split_axis=0, concat_axis=0, tiled=True)]
    pallas_call x13 -> x11, Pallas kernels: 47.7 us -> 44.1 us  [run(): pl.pallas_call(ordered, out_shape=out_shape, in_specs=specs, out_specs=[V...]
    all_to_all x4, waiting for transfers between devices: 23.3 us -> 19.8 us  [exchange(): lax.all_to_all(split, 'dom', split_axis=0, concat_axis=0, tiled=True)]
    dot_general x0 -> x2, matrix products: none -> 2.87 us  [the longest x1 1.87 us: shards(): lax.dot_general(asked_marks, nodes, (((2,), (0,)), ((), ())), preferred_e...]
  transfers between devices with their start and end apart: 20 -> 19, of which waited for: 12 -> 11; matrix products, arithmetic and copies ran while one was open for 4% -> 6% of each run, Pallas kernels for 23% -> 22%
where the time goes in v13:
time: 151 us; the launch traced here: 150 us
  waiting for transfers between devices  46.9 us (31%)
  Pallas kernels  44.1 us (29%)
  starting transfers between devices  28.8 us (19%)
  blocking collectives  13 us (9%)
  other arithmetic  9.56 us (6%)
  local copies, waits for them, and re-layouts  3.65 us (2%)
  matrix products  2.87 us (2%)
    pallas_call x11, Pallas kernels, run(): pl.pallas_call(ordered, out_shape=out_shape, in_specs=specs, out_specs=[V...  44.1 us
    ppermute x15, waiting for transfers between devices, across(): lax.ppermute(rows, 'dom', [(device, device ^ mask) for device in range(de...  27.1 us
    all_to_all x4, waiting for transfers between devices, exchange(): lax.all_to_all(split, 'dom', split_axis=0, concat_axis=0, tiled=True)  19.8 us
    all_to_all x4, starting transfers between devices, exchange(): lax.all_to_all(split, 'dom', split_axis=0, concat_axis=0, tiled=True)  16.1 us
    all_to_all x1, blocking collectives, shards(): asked = lax.all_to_all(ask, 'dom', split_axis=0, concat_axis=0, tiled=True)  13 us
    ppermute x15, starting transfers between devices, across(): lax.ppermute(rows, 'dom', [(device, device ^ mask) for device in range(de...  12.7 us
    convert_element_type x9, other arithmetic, added(): return sum((part.astype(F32) for part in parts)).astype(BF16)  3.11 us
  transfers between devices with their start and end apart: 19, of which 11 were waited for; matrix products, arithmetic and copies ran while one was open for 6% of the time, Pallas kernels for 22%

profile of v13, /device:TPU:1, one launch (start us, length us, event | category | flops | bytes accessed | tf_op | source)
XLA Modules:
  0.0 149.7 jit_solution(14224401082526225112)
XLA Ops:
  0.6 1.7 %shard_map.179.refs_2_ = s32[16,16]{1,0:T(8,128)} custom-call(s32[1,128]{1,0:T(1,128)} %bitcast.54, s32[1,128]{1,0:T(1,128)} %bitcast.57), custom_call_target="tpu_custom_call" | custom-call | flops 1 | bytes 1 | tf_op jit(solution)/shard_map/pallas_call | solution.py:436
  2.3 13.0 %all_to_all.29 = s32[16,1,16]{2,1,0:T(1,128)S(1)} all-to-all(s32[16,1,16]{2,1,0:T(1,128)} %bitcast.53), channel_id=1, replica_groups=mesh['groups'=2,'dom'=16] {'dom'}, dimensions={0} | all-to-all | bytes 2048 | tf_op jit(solution)/shard_map/all_to_all | solution.py:520
  15.4 1.9 %convolution_convert_fusion = bf16[16,16,512]{2,1,0:T(8,128)(2,1)} fusion(bf16[128,512]{1,0:T(8,128)(2,1)} %refs_4_.4, s32[16,16]{1,0:T(8,128)S(1)} %bitcast.52), kind=kOutput, calls=%fused_computation.2 | convolution fusion | flops 33783808 | bytes 394240 | tf_op jit(solution)/shard_map/dot_general | solution.py:529
  17.2 4.0 %all-to-all-start.1 = ((bf16[16,16,512]{2,1,0:T(8,128)(2,1)}), bf16[16,16,512]{2,1,0:T(8,128)(2,1)S(1)}, u32[]{:S(2)}, u32[]{:S(2)}) async-start(bf16[16,16,512]{2,1,0:T(8,128)(2,1)} %convolution_convert_fusion), calls=%async_computation.1 | async-start | bytes 524288 | tf_op jit(solution)/shard_map/all_to_all | solution.py:490
  21.3 2.0 %shard_map.180 = (bf16[256,384]{1,0:T(8,128)(2,1)}, bf16[256,384]{1,0:T(8,128)(2,1)}) custom-call(s32[1,128]{1,0:T(1,128)} %bitcast.55, s32[1,128]{1,0:T(1,128)} %bitcast.58, s32[16,16]{1,0:T(8,128)} %shard_map.179.refs_2_), custom_call_target="tpu_custom_call" | custom-call | flops 1 | bytes 1 | tf_op jit(solution)/shard_map/pallas_call | solution.py:436
  23.3 6.3 %shard_map.181 = (bf16[512,128]{1,0:T(8,128)(2,1)}, bf16[512,128]{1,0:T(8,128)(2,1)}, bf16[512,512]{1,0:T(8,128)(2,1)}, bf16[512,512]{1,0:T(8,128)(2,1)}, bf16[5...) custom-call(s32[2,256]{1,0:T(2,128)} %bitcast.56, ...), custom_call_target="tpu_custom_call" | custom-call | flops 1 | bytes 1 | tf_op jit(solution)/shard_map/pallas_call | solution.py:436
  29.6 1.3 all-to-all-done.1
  30.8 0.7 copy-done.2
  31.5 4.3 %shard_map.182 = (bf16[256,512]{1,0:T(8,128)(2,1)}, bf16[256,512]{1,0:T(8,128)(2,1)}, bf16[256,512]{1,0:T(8,128)(2,1)}, f32[256,512]{1,0:T(8,128)}, f32[256,512]...) custom-call(bf16[256,384]{1,0:T(8,128)(2,1)} %get-tuple-element.77.refs_0_.refs_2_, ...), custom_call_target="tpu_custom_call" | custom-call | flops 1 | bytes 1 | tf_op jit(solution)/shard_map/pallas_call | solution.py:436
  35.8 4.8 %all-to-all-start.2 = ((bf16[16,16,512]{2,1,0:T(8,128)(2,1)}), bf16[16,16,512]{2,1,0:T(8,128)(2,1)S(1)}, u32[]{:S(2)}, u32[]{:S(2)}) async-start(bf16[16,16,512]{2,1,0:T(8,128)(2,1)} %bitcast.48), calls=%async_computation.2 | async-start | bytes 524288 | tf_op jit(solution)/shard_map/all_to_all | solution.py:490
  41.2 0.7 reduce.3
  41.9 0.7 select_convert_fusion.refs_2_
  42.6 2.7 %shard_map.183.refs_8_ = bf16[768,512]{1,0:T(8,128)(2,1)} custom-call(bf16[768,512]{1,0:T(8,128)(2,1)} %refs_3_.6, f32[512,512]{1,0:T(8,128)} %get-tuple-element.82.refs_1_.refs_3_, f32[256,512]{1,0:T(8,128)} %get-tuple-element.83.refs_2_.refs_5_, bf16[256,512]{1,0:T(8,128)(2,1)} %get-tuple-element.80.refs_3_), custom_call_target="tpu_custom_call" | custom-call | flops 1 | bytes 1 | tf_op jit(solution)/shard_map/pallas_call | solution.py:436
  45.3 4.8 %all-to-all-done.2 = bf16[16,16,512]{2,1,0:T(8,128)(2,1)S(1)} async-done(((bf16[16,16,512]{2,1,0:T(8,128)(2,1)}), bf16[16,16,512]{2,1,0:T(8,128)(2,1)S(1)}, u32[]{:S(2)}, u32[]{:S(2)}) %all-to-all-start.2) | async-done | bytes 262176 | tf_op jit(solution)/shard_map/all_to_all | solution.py:490
  50.1 0.7 copy-done.3
  50.8 5.4 %shard_map.184 = (bf16[128,512]{1,0:T(8,128)(2,1)}, f32[128,512]{1,0:T(8,128)}, bf16[128,512]{1,0:T(8,128)(2,1)}, bf16[256,512]{1,0:T(8,128)(2,1)}, bf16[768,512]{1,0:T(8,128)(2,1)}, /*index=5*/bf16[768,512]{1,0:T(8,128)(2,1)}) custom-call(s32[1]{0:T(128)} %bitcast.refs_0_, bf16[256,512]{1,0:T(8,128)(2,1)} %bitcast.47, ...), custom_call_target="tpu_custom_call" | custom-call | flops 1 | bytes 1 | tf_op jit(solution)/shard_map/pallas_call | solution.py:436
  56.2 0.6 collective-permute-start
  56.9 3.6 %all-to-all-start.3 = ((bf16[16,16,512]{2,1,0:T(8,128)(2,1)}), bf16[16,16,512]{2,1,0:T(8,128)(2,1)S(1)}, u32[]{:S(2)}, u32[]{:S(2)}) async-start(bf16[16,16,512]{2,1,0:T(8,128)(2,1)} %bitcast.51), calls=%async_computation.3 | async-start | bytes 524288 | tf_op jit(solution)/shard_map/all_to_all | solution.py:490
  60.5 1.3 add_convert_fusion
  61.9 1.2 collective-permute-start.1
  63.1 3.6 %shard_map.185 = (bf16[512,512]{1,0:T(8,128)(2,1)}, bf16[512,512]{1,0:T(8,128)(2,1)}) custom-call(bf16[512,128]{1,0:T(8,128)(2,1)} %get-tuple-element.90.refs_0_.refs_1_, bf16[128,512]{1,0:T(8,128)(2,1)} %get-tuple-element.86.refs_1_.refs_2_, bf16[768,512]{1,0:T(8,128)(2,1)} %refs_0_.3, f32[512,512]{1,0:T(8,128)} %get-tuple-element.82.refs_1_.refs_3_, ...), custom_call_target="tpu_custom_call" | custom-call | flops 1 | bytes 1 | tf_op jit(solution)/shard_map/pallas_call | solution.py:436
  66.7 3.1 %all-to-all-done.3 = bf16[16,16,512]{2,1,0:T(8,128)(2,1)S(1)} async-done(((bf16[16,16,512]{2,1,0:T(8,128)(2,1)}), bf16[16,16,512]{2,1,0:T(8,128)(2,1)S(1)}, u32[]{:S(2)}, u32[]{:S(2)}) %all-to-all-start.3) | async-done | bytes 262176 | tf_op jit(solution)/shard_map/all_to_all | solution.py:490
  69.7 0.7 copy-done.1
  70.4 5.6 %shard_map.186 = (bf16[256,512]{1,0:T(8,128)(2,1)}, bf16[256,512]{1,0:T(8,128)(2,1)}, bf16[1024,512]{1,0:T(8,128)(2,1)}) custom-call(s32[1]{0:T(128)} %bitcast.refs_0_, bf16[256,384]{1,0:T(8,128)(2,1)} %get-tuple-element.78.refs_5_.refs_1_.refs_3_, bf16[128,512]{1,0:T(8,128)(2,1)} %get-tuple-element.86.refs_1_.refs_2_, bf16[256,512]{1,0:T(8,128)(2,1)} %bitcast.45, ...), custom_call_target="tpu_custom_call" | custom-call | flops 1 | bytes 1 | tf_op jit(solution)/shard_map/pallas_call | solution.py:436
  76.0 1.2 collective-permute-start.2
  77.3 4.8 %shard_map.187.refs_7_ = bf16[1024,512]{1,0:T(8,128)(2,1)} custom-call(s32[1]{0:T(128)} %bitcast.refs_0_, bf16[256,512]{1,0:T(8,128)(2,1)} %get-tuple-element.107.refs_1_, bf16[256,512]{1,0:T(8,128)(2,1)} %get-tuple-element.127.refs_2_.refs_5_, bf16[768,512]{1,0:T(8,128)(2,1)} %refs_3_.6, bf16[512,512]{1,0:T(8,128)(2,1)} %get-tuple-element.97.refs_10_.refs_4_, ...), custom_call_target="tpu_custom_call" | custom-call | flops 1 | bytes 1 | tf_op jit(solution)/shard_map/pallas_call | solution.py:436
  82.1 1.2 add_convert_fusion.3
  83.2 0.6 collective-permute-start.3
  83.9 1.3 collective-permute-start.5
  85.2 3.9 %shard_map.188 = (f32[128,512]{1,0:T(8,128)}, bf16[256,512]{1,0:T(8,128)(2,1)}) custom-call(bf16[512,128]{1,0:T(8,128)(2,1)} %get-tuple-element.120.refs_0_, bf16[512,128]{1,0:T(8,128)(2,1)} %get-tuple-element.90.refs_0_.refs_1_, bf16[256,384]{1,0:T(8,128)(2,1)} %get-tuple-element.77.refs_0_.refs_2_, ...), custom_call_target="tpu_custom_call" | custom-call | flops 1 | bytes 1 | tf_op jit(solution)/shard_map/pallas_call | solution.py:436
  89.3 5.9 %collective-permute-done.5 = bf16[192,512]{1,0:T(8,128)(2,1)S(1)} collective-permute-done((bf16[192,512]{1,0:T(8,128)(2,1)S(1)}, bf16[192,512]{1,0:T(8,128)(2,1)S(1)}, u32[]{:S(2)}, u32[]{:S(2)}) %collective-permute-start.5) | collective-permute-done | bytes 196640 | tf_op jit(solution)/shard_map/ppermute | solution.py:455
  95.3 1.2 collective-permute-done.3
  96.6 1.6 %collective-permute-start.6 = (bf16[256,512]{1,0:T(8,128)(2,1)S(1)}, bf16[256,512]{1,0:T(8,128)(2,1)S(1)}, u32[]{:S(2)}, u32[]{:S(2)}) collective-permute-start(bf16[256,512]{1,0:T(8,128)(2,1)S(1)} %dynamic-slice_bitcast_fusion.2), channel_id=1, source_target_pairs={{0,4},{1,5},{2,6},{3,7},{4,0},{5,1},{6,2},{7,3},{8,12},{9,13},{10,... | collective-permute-start | bytes 786440 | tf_op jit(solution)/shard_map/ppermute | solution.py:455
  98.2 3.9 %shard_map.189 = f32[768,512]{1,0:T(8,128)} custom-call(bf16[768,512]{1,0:T(8,128)(2,1)} %refs_0_.3, bf16[512,512]{1,0:T(8,128)(2,1)} %get-tuple-element.126.refs_17_.refs_18_.refs_11_.refs_4_.refs_1_, bf16[256,512]{1,0:T(8,128)(2,1)} %get-tuple-element.127.refs_2_.refs_5_, bf16[1536,512]{1,0:T(8,128)(2,1)} %refs_3_.7, ...), custom_call_target="tpu_custom_call" | custom-call | flops 1 | bytes 1 | tf_op jit(solution)/shard_map/pallas_call | solution.py:436
  102.1 1.3 collective-permute-done.6
  103.5 1.5 %collective-permute-start.9 = (bf16[192,512]{1,0:T(8,128)(2,1)S(1)}, bf16[192,512]{1,0:T(8,128)(2,1)S(1)}, u32[]{:S(2)}, u32[]{:S(2)}) collective-permute-start(bf16[192,512]{1,0:T(8,128)(2,1)S(1)} %add_convert_fusion.5), channel_id=1, source_target_pairs={{0,4},{1,5},{2,6},{3,7},{4,0},{5,1},{6,2},{7,3},{8,12},{9,13},{10,... | collective-permute-start | bytes 589832 | tf_op jit(solution)/shard_map/ppermute | solution.py:455
  105.0 0.7 collective-permute-start.7
  105.7 2.3 %collective-permute-done.9 = bf16[192,512]{1,0:T(8,128)(2,1)S(1)} collective-permute-done((bf16[192,512]{1,0:T(8,128)(2,1)S(1)}, bf16[192,512]{1,0:T(8,128)(2,1)S(1)}, u32[]{:S(2)}, u32[]{:S(2)}) %collective-permute-start.9) | collective-permute-done | bytes 196640 | tf_op jit(solution)/shard_map/ppermute | solution.py:455
  108.5 9.9 %collective-permute-done.7 = bf16[256,512]{1,0:T(8,128)(2,1)S(1)} collective-permute-done((bf16[256,512]{1,0:T(8,128)(2,1)S(1)}, bf16[256,512]{1,0:T(8,128)(2,1)S(1)}, u32[]{:S(2)}, u32[]{:S(2)}) %collective-permute-start.7) | collective-permute-done | bytes 262176 | tf_op jit(solution)/shard_map/ppermute | solution.py:455
  118.6 6.0 %collective-permute-done.8 = bf16[256,512]{1,0:T(8,128)(2,1)S(1)} collective-permute-done((bf16[256,512]{1,0:T(8,128)(2,1)S(1)}, bf16[256,512]{1,0:T(8,128)(2,1)S(1)}, u32[]{:S(2)}, u32[]{:S(2)}) %collective-permute-start.8) | collective-permute-done | bytes 262176 | tf_op jit(solution)/shard_map/ppermute | solution.py:455
  124.9 2.8 %collective-permute-start.13 = (bf16[768,512]{1,0:T(8,128)(2,1)S(1)}, bf16[768,512]{1,0:T(8,128)(2,1)S(1)}, u32[]{:S(2)}, u32[]{:S(2)}) collective-permute-start(bf16[768,512]{1,0:T(8,128)(2,1)S(1)} %maximum_select_fusion), channel_id=1, source_target_pairs={{0,1},{1,0},{2,3},{3,2},{4,5},{5,4},{6,7},{7,6},{8,9},{9,8},{10,11... | collective-permute-start | bytes 2359304 | tf_op jit(solution)/shard_map/ppermute | solution.py:455
  128.3 3.6 %all-to-all-start.4 = ((bf16[16,16,512]{2,1,0:T(8,128)(2,1)}), bf16[16,16,512]{2,1,0:T(8,128)(2,1)S(1)}, u32[]{:S(2)}, u32[]{:S(2)}) async-start(bf16[16,16,512]{2,1,0:T(8,128)(2,1)} %bitcast.24), calls=%async_computation.4 | async-start | bytes 524288 | tf_op jit(solution)/shard_map/all_to_all | solution.py:490
  132.0 0.8 slice.25
  132.8 1.0 pad_maximum_fusion.1
  133.9 10.6 %all-to-all-done.4 = bf16[16,16,512]{2,1,0:T(8,128)(2,1)S(1)} async-done(((bf16[16,16,512]{2,1,0:T(8,128)(2,1)}), bf16[16,16,512]{2,1,0:T(8,128)(2,1)S(1)}, u32[]{:S(2)}, u32[]{:S(2)}) %all-to-all-start.4) | async-done | bytes 262176 | tf_op jit(solution)/shard_map/all_to_all | solution.py:490
  144.9 1.0 add_add_fusion
  146.5 2.0 %broadcast_select_fusion.6 = (bf16[512,512]{1,0:T(8,128)(2,1)}, bf16[512,512]{1,0:T(8,128)(2,1)S(1)}, bf16[512,512]{1,0:T(8,128)(2,1)S(1)}, bf16[512,512]{1,0:T(8,128)(2,1)S(1)}) fusion(pred[]{:T(512)S(6)} %eq.45, bf16[512,512]{1,0:T(8,128)(2,1)} %collective-permute-done.12, bf16[512,512]{1,0:T(8,128)(2,1)S(1)} %maximum_select_fusion.1, pred[]{:T(512)S(6)} %eq.44, ...), kind=kLoop, calls=%fused_computation.18 | loop fusion | flops 2097152 | bytes 4194306 | tf_op jit(solution)/shard_map/jit(_where)/select_n | solution.py:793
  148.5 1.2 pad_maximum_fusion
  (40 shorter events, 3.9 us)
Async XLA Ops:
  17.2 13.6 %all-to-all-start.1 = ((bf16[16,16,512]{2,1,0:T(8,128)(2,1)}), bf16[16,16,512]{2,1,0:T(8,128)(2,1)S(1)}, u32[]{:S(2)}, u32[]{:S(2)}) async-start(bf16[16,16,512]{2,1,0:T(8,128)(2,1)} %convolution_convert_fusion), calls=%async_computation.1 | async-start | bytes 524288 | tf_op jit(solution)/shard_map/all_to_all | solution.py:490
  30.8 0.7 copy-start.2
  35.8 14.3 %all-to-all-start.2 = ((bf16[16,16,512]{2,1,0:T(8,128)(2,1)}), bf16[16,16,512]{2,1,0:T(8,128)(2,1)S(1)}, u32[]{:S(2)}, u32[]{:S(2)}) async-start(bf16[16,16,512]{2,1,0:T(8,128)(2,1)} %bitcast.48), calls=%async_computation.2 | async-start | bytes 524288 | tf_op jit(solution)/shard_map/all_to_all | solution.py:490
  50.1 0.7 copy-start.3
  56.2 4.3 %collective-permute-start = (bf16[768,512]{1,0:T(8,128)(2,1)}, bf16[768,512]{1,0:T(8,128)(2,1)S(1)}, u32[]{:S(2)}, u32[]{:S(2)}) collective-permute-start(bf16[768,512]{1,0:T(8,128)(2,1)} %get-tuple-element.89.refs_7_), channel_id=1, source_target_pairs={{0,1},{1,0},{2,3},{3,2},{4,5},{5,4},{6,7},{7,6},{8,9},{9,8},{10,11... | collective-permute-start | bytes 2359304 | tf_op jit(solution)/shard_map/ppermute | solution.py:455
  56.9 12.9 %all-to-all-start.3 = ((bf16[16,16,512]{2,1,0:T(8,128)(2,1)}), bf16[16,16,512]{2,1,0:T(8,128)(2,1)S(1)}, u32[]{:S(2)}, u32[]{:S(2)}) async-start(bf16[16,16,512]{2,1,0:T(8,128)(2,1)} %bitcast.51), calls=%async_computation.3 | async-start | bytes 524288 | tf_op jit(solution)/shard_map/all_to_all | solution.py:490
  61.9 14.1 %collective-permute-start.1 = (bf16[384,512]{1,0:T(8,128)(2,1)S(1)}, bf16[384,512]{1,0:T(8,128)(2,1)S(1)}, u32[]{:S(2)}, u32[]{:S(2)}) collective-permute-start(bf16[384,512]{1,0:T(8,128)(2,1)S(1)} %get-tuple-element.152), channel_id=1, source_target_pairs={{0,2},{1,3},{2,0},{3,1},{4,6},{5,7},{6,4},{7,5},{8,10},{9,11},{10,... | collective-permute-start | bytes 1179656 | tf_op jit(solution)/shard_map/ppermute | solution.py:455
  69.7 0.7 copy-start.1
  76.0 6.1 %collective-permute-start.2 = (bf16[1024,512]{1,0:T(8,128)(2,1)}, bf16[1024,512]{1,0:T(8,128)(2,1)S(1)}, u32[]{:S(2)}, u32[]{:S(2)}) collective-permute-start(bf16[1024,512]{1,0:T(8,128)(2,1)} %get-tuple-element.109.refs_12_), channel_id=1, source_target_pairs={{0,1},{1,0},{2,3},{3,2},{4,5},{5,4},{6,7},{7,6},{8,9},{9,8},{10,11... | collective-permute-start | bytes 3145736 | tf_op jit(solution)/shard_map/ppermute | solution.py:455
  77.2 6.6 %collective-permute-start.4 = (bf16[192,512]{1,0:T(8,128)(2,1)S(1)}, bf16[192,512]{1,0:T(8,128)(2,1)S(1)}, u32[]{:S(2)}, u32[]{:S(2)}) collective-permute-start(bf16[192,512]{1,0:T(8,128)(2,1)S(1)} %fusion.2), channel_id=1, source_target_pairs={{0,4},{1,5},{2,6},{3,7},{4,0},{5,1},{6,2},{7,3},{8,12},{9,13},{10,... | collective-permute-start | bytes 589832 | tf_op jit(solution)/shard_map/ppermute | solution.py:455
  83.2 13.2 %collective-permute-start.3 = (bf16[512,512]{1,0:T(8,128)(2,1)S(1)}, bf16[512,512]{1,0:T(8,128)(2,1)S(1)}, u32[]{:S(2)}, u32[]{:S(2)}) collective-permute-start(bf16[512,512]{1,0:T(8,128)(2,1)S(1)} %add_convert_fusion.3), channel_id=1, source_target_pairs={{0,2},{1,3},{2,0},{3,1},{4,6},{5,7},{6,4},{7,5},{8,10},{9,11},{10,... | collective-permute-start | bytes 1572872 | tf_op jit(solution)/shard_map/ppermute | solution.py:455
  83.9 11.3 %collective-permute-start.5 = (bf16[192,512]{1,0:T(8,128)(2,1)S(1)}, bf16[192,512]{1,0:T(8,128)(2,1)S(1)}, u32[]{:S(2)}, u32[]{:S(2)}) collective-permute-start(bf16[192,512]{1,0:T(8,128)(2,1)S(1)} %fusion.1), channel_id=1, source_target_pairs={{0,8},{1,9},{2,10},{3,11},{4,12},{5,13},{6,14},{7,15},{8,0},{9,1},... | collective-permute-start | bytes 589832 | tf_op jit(solution)/shard_map/ppermute | solution.py:455
  85.2 3.9 %copy-start = (bf16[1024,512]{1,0:T(8,128)(2,1)S(1)}, bf16[1024,512]{1,0:T(8,128)(2,1)}, u32[]{:S(2)}) copy-start(bf16[1024,512]{1,0:T(8,128)(2,1)} %shard_map.187.refs_7_) | copy-start | bytes 3145732
  96.6 6.7 %collective-permute-start.6 = (bf16[256,512]{1,0:T(8,128)(2,1)S(1)}, bf16[256,512]{1,0:T(8,128)(2,1)S(1)}, u32[]{:S(2)}, u32[]{:S(2)}) collective-permute-start(bf16[256,512]{1,0:T(8,128)(2,1)S(1)} %dynamic-slice_bitcast_fusion.2), channel_id=1, source_target_pairs={{0,4},{1,5},{2,6},{3,7},{4,0},{5,1},{6,2},{7,3},{8,12},{9,13},{10,... | collective-permute-start | bytes 786440 | tf_op jit(solution)/shard_map/ppermute | solution.py:455
  103.5 4.6 %collective-permute-start.9 = (bf16[192,512]{1,0:T(8,128)(2,1)S(1)}, bf16[192,512]{1,0:T(8,128)(2,1)S(1)}, u32[]{:S(2)}, u32[]{:S(2)}) collective-permute-start(bf16[192,512]{1,0:T(8,128)(2,1)S(1)} %add_convert_fusion.5), channel_id=1, source_target_pairs={{0,4},{1,5},{2,6},{3,7},{4,0},{5,1},{6,2},{7,3},{8,12},{9,13},{10,... | collective-permute-start | bytes 589832 | tf_op jit(solution)/shard_map/ppermute | solution.py:455
  105.0 13.4 %collective-permute-start.7 = (bf16[256,512]{1,0:T(8,128)(2,1)S(1)}, bf16[256,512]{1,0:T(8,128)(2,1)S(1)}, u32[]{:S(2)}, u32[]{:S(2)}) collective-permute-start(bf16[256,512]{1,0:T(8,128)(2,1)S(1)} %fusion), channel_id=1, source_target_pairs={{0,8},{1,9},{2,10},{3,11},{4,12},{5,13},{6,14},{7,15},{8,0},{9,1},... | collective-permute-start | bytes 786440 | tf_op jit(solution)/shard_map/ppermute | solution.py:455
  108.2 16.4 %collective-permute-start.10 = (bf16[384,512]{1,0:T(8,128)(2,1)S(1)}, bf16[384,512]{1,0:T(8,128)(2,1)S(1)}, u32[]{:S(2)}, u32[]{:S(2)}) collective-permute-start(bf16[384,512]{1,0:T(8,128)(2,1)S(1)} %maximum_select_fusion.2), channel_id=1, source_target_pairs={{0,2},{1,3},{2,0},{3,1},{4,6},{5,7},{6,4},{7,5},{8,10},{9,11},{10,... | collective-permute-start | bytes 1179656 | tf_op jit(solution)/shard_map/ppermute | solution.py:455
  118.5 6.0 %collective-permute-start.8 = (bf16[256,512]{1,0:T(8,128)(2,1)S(1)}, bf16[256,512]{1,0:T(8,128)(2,1)S(1)}, u32[]{:S(2)}, u32[]{:S(2)}) collective-permute-start(bf16[256,512]{1,0:T(8,128)(2,1)S(1)} %add_convert_fusion.4), channel_id=1, source_target_pairs={{0,4},{1,5},{2,6},{3,7},{4,0},{5,1},{6,2},{7,3},{8,12},{9,13},{10,... | collective-permute-start | bytes 786440 | tf_op jit(solution)/shard_map/ppermute | solution.py:455
  124.9 7.0 %collective-permute-start.13 = (bf16[768,512]{1,0:T(8,128)(2,1)S(1)}, bf16[768,512]{1,0:T(8,128)(2,1)S(1)}, u32[]{:S(2)}, u32[]{:S(2)}) collective-permute-start(bf16[768,512]{1,0:T(8,128)(2,1)S(1)} %maximum_select_fusion), channel_id=1, source_target_pairs={{0,1},{1,0},{2,3},{3,2},{4,5},{5,4},{6,7},{7,6},{8,9},{9,8},{10,11... | collective-permute-start | bytes 2359304 | tf_op jit(solution)/shard_map/ppermute | solution.py:455
  127.9 16.6 %collective-permute-start.11 = (bf16[512,512]{1,0:T(8,128)(2,1)S(1)}, bf16[512,512]{1,0:T(8,128)(2,1)S(1)}, u32[]{:S(2)}, u32[]{:S(2)}) collective-permute-start(bf16[512,512]{1,0:T(8,128)(2,1)S(1)} %maximum_select_fusion.1), channel_id=1, source_target_pairs={{0,2},{1,3},{2,0},{3,1},{4,6},{5,7},{6,4},{7,5},{8,10},{9,11},{10,... | collective-permute-start | bytes 1572872 | tf_op jit(solution)/shard_map/ppermute | solution.py:455
  128.0 16.5 %collective-permute-start.12 = (bf16[512,512]{1,0:T(8,128)(2,1)S(1)}, bf16[512,512]{1,0:T(8,128)(2,1)}, u32[]{:S(2)}, u32[]{:S(2)}) collective-permute-start(bf16[512,512]{1,0:T(8,128)(2,1)S(1)} %maximum_select_fusion.1), channel_id=1, source_target_pairs={{0,1},{1,0},{2,3},{3,2},{4,5},{5,4},{6,7},{7,6},{8,9},{9,8},{10,11... | collective-permute-start | bytes 1572872 | tf_op jit(solution)/shard_map/ppermute | solution.py:455
  128.3 16.2 %all-to-all-start.4 = ((bf16[16,16,512]{2,1,0:T(8,128)(2,1)}), bf16[16,16,512]{2,1,0:T(8,128)(2,1)S(1)}, u32[]{:S(2)}, u32[]{:S(2)}) async-start(bf16[16,16,512]{2,1,0:T(8,128)(2,1)} %bitcast.24), calls=%async_computation.4 | async-start | bytes 524288 | tf_op jit(solution)/shard_map/all_to_all | solution.py:490
  132.0 12.9 %copy-start.4 = (f32[128,512]{1,0:T(8,128)S(1)}, f32[128,512]{1,0:T(8,128)}, u32[]{:S(2)}) copy-start(f32[128,512]{1,0:T(8,128)} %get-tuple-element.85) | copy-start | bytes 786436
  132.0 12.9 %copy-start.5 = (f32[128,512]{1,0:T(8,128)S(1)}, f32[128,512]{1,0:T(8,128)}, u32[]{:S(2)}) copy-start(f32[128,512]{1,0:T(8,128)} %get-tuple-element.122) | copy-start | bytes 786436
  144.5 1.9 %collective-permute-start.14 = (bf16[512,512]{1,0:T(8,128)(2,1)S(1)}, bf16[512,512]{1,0:T(8,128)(2,1)S(1)}, u32[]{:S(2)}, u32[]{:S(2)}) collective-permute-start(bf16[512,512]{1,0:T(8,128)(2,1)S(1)} %collective-permute-done.11), channel_id=1, source_target_pairs={{0,1},{1,0},{2,3},{3,2},{4,5},{5,4},{6,7},{7,6},{8,9},{9,8},{10,11... | collective-permute-start | bytes 1572872 | tf_op jit(solution)/shard_map/ppermute | solution.py:455

commit v14 on v13

--- a/solution.py
+++ b/solution.py
@@ -284,14 +284,14 @@
     grad_pre_ref[...] = grad_pre
 
 
-def fetch_factors(half, sources, buffers, sems, wait=False):
+def fetch_factors(half, sources, buffers, sems, wait):
     edges, inner_sender, cut_sender, inner_receiver, cut_receiver = sources[:5]
     inner_hidden, cut_hidden, inner_out, inner_pre = sources[5:]
     inner_rows, cut_rows = inner_pre.shape[0], cut_sender.shape[0]
     inner_edges = edges.at[pl.ds(0, inner_rows)]
     cut_edges = edges.at[pl.ds(inner_rows, cut_rows)]
-    low = [inner_edges, cut_edges, inner_pre, inner_sender, cut_sender, inner_pre]
-    high = [inner_receiver, cut_receiver, inner_pre, inner_hidden, cut_hidden, inner_out]
+    low = [inner_edges, cut_edges, inner_sender, cut_sender, inner_pre, inner_pre]
+    high = [inner_receiver, cut_receiver, inner_hidden, cut_hidden, inner_pre, inner_out]
 
     def each(parts):
         for index, (source, buffer) in enumerate(zip(parts, buffers)):
@@ -314,11 +314,10 @@
     return pl.ds(pl.multiple_of((index ^ ((me_ref[0] >> 1) & 1)) * latent, latent), latent)
 
 
-def edge_rows(me_ref, half, sources, buffers, sems, cut_pre, cut_out, out_ref):
+def edge_rows(me_ref, half, buffers, cut_pre, cut_out, out_ref):
     latent = cut_pre.shape[1]
-    first, first_cut, first_right, second, second_cut, second_right = buffers
+    first, first_cut, second, second_cut, first_right, second_right = buffers
     chosen = jnp.where(half == 0, cut_pre.astype(F32), cut_out.astype(F32)).astype(BF16)
-    fetch_factors(half, sources, buffers, sems, True)
     out_ref[place_rows(me_ref, 0, latent)] = (
         dot_rows(first[...], first_right[...]) + dot_rows(first_cut[...], cut_pre)
     ).astype(BF16)
@@ -342,7 +341,7 @@
     sources, (grad_out_ref, grad_pre_ref, out_ref), rest = refs[:9], refs[9:12], refs[12:]
     buffers, sems = rest[:-1], rest[-1]
     half = 1 - (me_ref[0] & 1)
-    fetch_factors(half, sources, buffers, sems)
+    fetch_factors(half, sources, buffers, sems, False)
     base = agg_grad_ref.shape[0]
     target = dot(receivers_ref[:, :base], agg_grad_ref[...]) + dot(
         receivers_ref[:, base:], far_grad_ref[...]
@@ -352,17 +351,47 @@
     )
     grad_out_ref[...] = grad_out
     grad_pre_ref[...] = grad_pre
-    edge_rows(me_ref, half, sources, buffers, sems, grad_pre, grad_out, out_ref)
+    fetch_factors(half, sources, buffers, sems, True)
+    edge_rows(me_ref, half, buffers, grad_pre, grad_out, out_ref)
 
 
 def edge_weights_kernel(me_ref, cut_out_ref, cut_pre_ref, *refs):
     sources, out_ref, rest = refs[:9], refs[9], refs[10:]
     buffers, sems = rest[:-1], rest[-1]
     half = me_ref[0] & 1
-    fetch_factors(half, sources, buffers, sems)
-    edge_rows(
-        me_ref, half, sources, buffers, sems, cut_pre_ref[...], cut_out_ref[...], out_ref
-    )
+    fetch_factors(half, sources, buffers, sems, False)
+    fetch_factors(half, sources, buffers, sems, True)
+    edge_rows(me_ref, half, buffers, cut_pre_ref[...], cut_out_ref[...], out_ref)
+
+
+def place_quarters(me_ref, pieces, outs, sems):
+    mine = (me_ref[0] & 1) * 2 + ((me_ref[0] >> 1) & 1)
+
+    def each(wait):
+        for index, (piece, distance) in enumerate(pieces):
+            rows = piece.shape[0]
+            for quarter in range(4):
+                inside = (quarter + 1) * rows <= outs[0].shape[0]
+                goal = outs[0].at[pl.ds(quarter * rows, rows)] if inside else outs[1]
+                copy = pltpu.make_async_copy(piece, goal, sems.at[index])
+
+                @pl.when((mine ^ distance) == quarter)
+                def _():
+                    if wait:
+                        copy.wait()
+                    else:
+                        copy.start()
+
+    each(False)
+    each(True)
+
+
+def first_quarters_kernel(me_ref, mine_ref, near_ref, in_ref, out_ref, sems):
+    place_quarters(me_ref, [(mine_ref, 0), (near_ref, 2)], (in_ref, out_ref), sems)
+
+
+def last_quarters_kernel(me_ref, far_ref, corner_ref, _, __, in_ref, out_ref, sems):
+    place_quarters(me_ref, [(far_ref, 1), (corner_ref, 3)], (in_ref, out_ref), sems)
 
 
 def input_grads_kernel(
@@ -410,6 +439,7 @@
 VMEM = pl.BlockSpec(memory_space=pltpu.VMEM)
 SMEM = pl.BlockSpec(memory_space=pltpu.SMEM)
 ANY = pl.BlockSpec(memory_space=pl.ANY)
+HBM = pl.BlockSpec(memory_space=pltpu.HBM)
 
 
 def shaped(dtype, *shape):
@@ -420,7 +450,9 @@
     def __init__(self):
         self.last = None
 
-    def run(self, body, outs, ins, specs=None, out_specs=None, grid=None, scratch=()):
+    def run(
+        self, body, outs, ins, specs=None, out_specs=None, grid=None, scratch=(), limit=VMEM_LIMIT, aliases=None
+    ):
         single = not isinstance(outs, (list, tuple))
         out_shape = [outs] if single else list(outs)
         specs = [VMEM] * len(ins) if specs is None else list(specs)
@@ -439,7 +471,8 @@
             in_specs=specs,
             out_specs=[VMEM] * len(out_shape) if out_specs is None else out_specs,
             scratch_shapes=scratch,
-            compiler_params=pltpu.CompilerParams(vmem_limit_bytes=VMEM_LIMIT),
+            input_output_aliases=aliases or {},
+            compiler_params=pltpu.CompilerParams(vmem_limit_bytes=limit),
             cost_estimate=pl.CostEstimate(flops=1, bytes_accessed=1, transcendentals=0),
             **extra,
         )(*ins)
@@ -675,9 +708,8 @@
         inner_out,
         inner_pre,
     ]
-    buffers = [
-        pltpu.VMEM((rows, latent), BF16) for rows in (inner_rows, cut_rows, inner_rows) * 2
-    ]
+    buffers = [pltpu.VMEM((rows, latent), BF16) for rows in (inner_rows, cut_rows) * 2]
+    buffers += [pltpu.VMEM((inner_rows, latent), BF16)] * 2
     buffers.append(pltpu.SemaphoreType.DMA((len(buffers),)))
     cut_out, cut_pre, edge_send = line.run(
         cut_backward_kernel,
@@ -778,25 +810,29 @@
     far, near = across(edge_sum, domains, 2), across(edge_sum, domains, 1)
     others = across(node_sum, domains, 1)
     returned = exchange(outgoing_grad, domains)
-    lower, left = place_of(0) == 0, place_of(1) == 0
+    lower = place_of(0) == 0
     low_rows, high_rows = jnp.where(lower, node_sum, others), jnp.where(lower, others, node_sum)
     cut_at = 2 * latent - low_rows.shape[0]
     grad_node_in = jnp.concatenate([low_rows, high_rows[:cut_at]])
     grad_node_out = high_rows[cut_at:]
-    far, near, grad_node_in, grad_node_out, returned = fence(
-        far, near, grad_node_in, grad_node_out, returned
+    quarters = [shaped(BF16, 3 * latent, latent), shaped(BF16, latent, latent)]
+    copies = dict(out_specs=[HBM] * 2, scratch=[pltpu.SemaphoreType.DMA((2,))], limit=2**20)
+    grad_edge_in, grad_edge_out = line.run(
+        first_quarters_kernel, quarters, [me, edge_sum, near], [SMEM, ANY, ANY], **copies
+    )
+    far, grad_edge_in, grad_edge_out, grad_node_in, grad_node_out, returned = fence(
+        far, grad_edge_in, grad_edge_out, grad_node_in, grad_node_out, returned
     )
     corner = across(far, domains, 1)
     grad_nodes = self_grad + local_grad + dot_rows(asked_marks, returned)
-    low_half = [jnp.where(lower, edge_sum, near), jnp.where(lower, far, corner)]
-    high_half = [jnp.where(lower, near, edge_sum), jnp.where(lower, corner, far)]
-    grad_edge_out = jnp.where(left, high_half[1], high_half[0])
-    grad_edge_in = jnp.concatenate(
-        [
-            jnp.where(left, low_half[0], low_half[1]),
-            jnp.where(left, low_half[1], low_half[0]),
-            jnp.where(left, high_half[0], high_half[1]),
-        ]
+    corner, grad_nodes = fence(corner, grad_nodes)
+    grad_edge_in, grad_edge_out = Line().run(
+        last_quarters_kernel,
+        quarters,
+        [me, far, corner, grad_edge_in, grad_edge_out],
+        [SMEM, ANY, ANY, HBM, HBM],
+        aliases={3: 0, 4: 1},
+        **copies,
     )
     return (
         new_nodes,

time: 151 us -> 149 us (0.987)
  waiting for transfers between devices: 46.9 us -> 42.7 us
  Pallas kernels: 44.1 us -> 45.9 us
    all_to_all x4, waiting for transfers between devices: 19.8 us -> 16.6 us  [exchange(): lax.all_to_all(split, 'dom', split_axis=0, concat_axis=0, tiled=True)]
    select_n x1 -> x0, other arithmetic: 2.01 us -> none  [shards(): grad_edge_out = jnp.where(left, high_half[1], high_half[0])]
    pallas_call x11 -> x13, Pallas kernels: 44.1 us -> 45.9 us  [run(): pl.pallas_call(ordered, out_shape=out_shape, in_specs=specs, out_specs=[V...]
  transfers between devices with their start and end apart: 19 -> 19, of which waited for: 11 -> 11; matrix products, arithmetic and copies ran while one was open for 6% -> 7% of each run, Pallas kernels for 22% -> 23%
where the time goes in v14:
time: 149 us; the launch traced here: 148 us
  Pallas kernels  45.9 us (31%)
  waiting for transfers between devices  42.7 us (29%)
  starting transfers between devices  30 us (20%)
  blocking collectives  13 us (9%)
  other arithmetic  8.55 us (6%)
  local copies, waits for them, and re-layouts  3.65 us (2%)
  matrix products  2.87 us (2%)
    pallas_call x13, Pallas kernels, run(): pl.pallas_call(ordered, out_shape=out_shape, in_specs=specs, out_specs=[V...  45.9 us
    ppermute x15, waiting for transfers between devices, across(): lax.ppermute(rows, 'dom', [(device, device ^ mask) for device in range(de...  26 us
    all_to_all x4, starting transfers between devices, exchange(): lax.all_to_all(split, 'dom', split_axis=0, concat_axis=0, tiled=True)  17.1 us
    all_to_all x4, waiting for transfers between devices, exchange(): lax.all_to_all(split, 'dom', split_axis=0, concat_axis=0, tiled=True)  16.6 us
    all_to_all x1, blocking collectives, shards(): asked = lax.all_to_all(ask, 'dom', split_axis=0, concat_axis=0, tiled=True)  13 us
    ppermute x15, starting transfers between devices, across(): lax.ppermute(rows, 'dom', [(device, device ^ mask) for device in range(de...  12.9 us
    convert_element_type x9, other arithmetic, added(): return sum((part.astype(F32) for part in parts)).astype(BF16)  3.11 us
  transfers between devices with their start and end apart: 19, of which 11 were waited for; matrix products, arithmetic and copies ran while one was open for 7% of the time, Pallas kernels for 23%

profile of v14, /device:TPU:1, one launch (start us, length us, event | category | flops | bytes accessed | tf_op | source)
XLA Modules:
  0.0 147.7 jit_solution(7248312407701601943)
XLA Ops:
  0.6 1.7 %shard_map.179.refs_2_ = s32[16,16]{1,0:T(8,128)} custom-call(s32[1,128]{1,0:T(1,128)} %bitcast.54, s32[1,128]{1,0:T(1,128)} %bitcast.57), custom_call_target="tpu_custom_call" | custom-call | flops 1 | bytes 1 | tf_op jit(solution)/shard_map/pallas_call | solution.py:468
  2.3 13.0 %all_to_all.29 = s32[16,1,16]{2,1,0:T(1,128)S(1)} all-to-all(s32[16,1,16]{2,1,0:T(1,128)} %bitcast.53), channel_id=1, replica_groups=mesh['groups'=2,'dom'=16] {'dom'}, dimensions={0} | all-to-all | bytes 2048 | tf_op jit(solution)/shard_map/all_to_all | solution.py:553
  15.4 1.9 %convolution_convert_fusion = bf16[16,16,512]{2,1,0:T(8,128)(2,1)} fusion(bf16[128,512]{1,0:T(8,128)(2,1)} %refs_4_.4, s32[16,16]{1,0:T(8,128)S(1)} %bitcast.52), kind=kOutput, calls=%fused_computation.1 | convolution fusion | flops 33783808 | bytes 394240 | tf_op jit(solution)/shard_map/dot_general | solution.py:562
  17.2 4.0 %all-to-all-start.1 = ((bf16[16,16,512]{2,1,0:T(8,128)(2,1)}), bf16[16,16,512]{2,1,0:T(8,128)(2,1)S(1)}, u32[]{:S(2)}, u32[]{:S(2)}) async-start(bf16[16,16,512]{2,1,0:T(8,128)(2,1)} %convolution_convert_fusion), calls=%async_computation.1 | async-start | bytes 524288 | tf_op jit(solution)/shard_map/all_to_all | solution.py:523
  21.3 2.0 %shard_map.180 = (bf16[256,384]{1,0:T(8,128)(2,1)}, bf16[256,384]{1,0:T(8,128)(2,1)}) custom-call(s32[1,128]{1,0:T(1,128)} %bitcast.55, s32[1,128]{1,0:T(1,128)} %bitcast.58, s32[16,16]{1,0:T(8,128)} %shard_map.179.refs_2_), custom_call_target="tpu_custom_call" | custom-call | flops 1 | bytes 1 | tf_op jit(solution)/shard_map/pallas_call | solution.py:468
  23.3 6.3 %shard_map.181 = (bf16[512,128]{1,0:T(8,128)(2,1)}, bf16[512,128]{1,0:T(8,128)(2,1)}, bf16[512,512]{1,0:T(8,128)(2,1)}, bf16[512,512]{1,0:T(8,128)(2,1)}, bf16[5...) custom-call(s32[2,256]{1,0:T(2,128)} %bitcast.56, ...), custom_call_target="tpu_custom_call" | custom-call | flops 1 | bytes 1 | tf_op jit(solution)/shard_map/pallas_call | solution.py:468
  29.6 1.2 all-to-all-done.1
  30.8 0.7 copy-done.3
  31.5 4.3 %shard_map.182 = (bf16[256,512]{1,0:T(8,128)(2,1)}, bf16[256,512]{1,0:T(8,128)(2,1)}, bf16[256,512]{1,0:T(8,128)(2,1)}, f32[256,512]{1,0:T(8,128)}, f32[256,512]...) custom-call(bf16[256,384]{1,0:T(8,128)(2,1)} %get-tuple-element.84.refs_0_.refs_2_, ...), custom_call_target="tpu_custom_call" | custom-call | flops 1 | bytes 1 | tf_op jit(solution)/shard_map/pallas_call | solution.py:468
  35.8 4.9 %all-to-all-start.2 = ((bf16[16,16,512]{2,1,0:T(8,128)(2,1)}), bf16[16,16,512]{2,1,0:T(8,128)(2,1)S(1)}, u32[]{:S(2)}, u32[]{:S(2)}) async-start(bf16[16,16,512]{2,1,0:T(8,128)(2,1)} %bitcast.48), calls=%async_computation.2 | async-start | bytes 524288 | tf_op jit(solution)/shard_map/all_to_all | solution.py:523
  41.2 0.7 reduce.3
  41.9 0.7 select_convert_fusion.refs_2_
  42.7 2.7 %shard_map.183.refs_8_ = bf16[768,512]{1,0:T(8,128)(2,1)} custom-call(bf16[768,512]{1,0:T(8,128)(2,1)} %refs_3_.6, f32[512,512]{1,0:T(8,128)} %get-tuple-element.89.refs_1_.refs_3_, f32[256,512]{1,0:T(8,128)} %get-tuple-element.90.refs_2_.refs_5_, bf16[256,512]{1,0:T(8,128)(2,1)} %get-tuple-element.87.refs_3_), custom_call_target="tpu_custom_call" | custom-call | flops 1 | bytes 1 | tf_op jit(solution)/shard_map/pallas_call | solution.py:468
  45.3 4.8 %all-to-all-done.2 = bf16[16,16,512]{2,1,0:T(8,128)(2,1)S(1)} async-done(((bf16[16,16,512]{2,1,0:T(8,128)(2,1)}), bf16[16,16,512]{2,1,0:T(8,128)(2,1)S(1)}, u32[]{:S(2)}, u32[]{:S(2)}) %all-to-all-start.2) | async-done | bytes 262176 | tf_op jit(solution)/shard_map/all_to_all | solution.py:523
  50.2 0.7 copy-done.4
  50.9 5.4 %shard_map.184 = (bf16[128,512]{1,0:T(8,128)(2,1)}, f32[128,512]{1,0:T(8,128)}, bf16[128,512]{1,0:T(8,128)(2,1)}, bf16[256,512]{1,0:T(8,128)(2,1)}, bf16[768,512]{1,0:T(8,128)(2,1)}, /*index=5*/bf16[768,512]{1,0:T(8,128)(2,1)}) custom-call(s32[1]{0:T(128)} %bitcast.refs_0_, bf16[256,512]{1,0:T(8,128)(2,1)} %bitcast.47, ...), custom_call_target="tpu_custom_call" | custom-call | flops 1 | bytes 1 | tf_op jit(solution)/shard_map/pallas_call | solution.py:468
  56.9 3.6 %all-to-all-start.3 = ((bf16[16,16,512]{2,1,0:T(8,128)(2,1)}), bf16[16,16,512]{2,1,0:T(8,128)(2,1)S(1)}, u32[]{:S(2)}, u32[]{:S(2)}) async-start(bf16[16,16,512]{2,1,0:T(8,128)(2,1)} %bitcast.51), calls=%async_computation.3 | async-start | bytes 524288 | tf_op jit(solution)/shard_map/all_to_all | solution.py:523
  60.5 1.3 add_convert_fusion
  61.9 1.2 collective-permute-start.1
  63.1 3.6 %shard_map.185 = (bf16[512,512]{1,0:T(8,128)(2,1)}, bf16[512,512]{1,0:T(8,128)(2,1)}) custom-call(bf16[512,128]{1,0:T(8,128)(2,1)} %get-tuple-element.96.refs_0_.refs_1_, bf16[128,512]{1,0:T(8,128)(2,1)} %get-tuple-element.92.refs_1_.refs_2_, bf16[768,512]{1,0:T(8,128)(2,1)} %refs_0_.3, f32[512,512]{1,0:T(8,128)} %get-tuple-element.89.refs_1_.refs_3_, ...), custom_call_target="tpu_custom_call" | custom-call | flops 1 | bytes 1 | tf_op jit(solution)/shard_map/pallas_call | solution.py:468
  66.7 3.1 %all-to-all-done.3 = bf16[16,16,512]{2,1,0:T(8,128)(2,1)S(1)} async-done(((bf16[16,16,512]{2,1,0:T(8,128)(2,1)}), bf16[16,16,512]{2,1,0:T(8,128)(2,1)S(1)}, u32[]{:S(2)}, u32[]{:S(2)}) %all-to-all-start.3) | async-done | bytes 262176 | tf_op jit(solution)/shard_map/all_to_all | solution.py:523
  69.7 0.7 copy-done.2
  70.4 5.4 %shard_map.186 = (bf16[256,512]{1,0:T(8,128)(2,1)}, bf16[256,512]{1,0:T(8,128)(2,1)}, bf16[1024,512]{1,0:T(8,128)(2,1)}) custom-call(s32[1]{0:T(128)} %bitcast.refs_0_, bf16[256,384]{1,0:T(8,128)(2,1)} %get-tuple-element.85.refs_5_.refs_1_.refs_3_, bf16[128,512]{1,0:T(8,128)(2,1)} %get-tuple-element.92.refs_1_.refs_2_, bf16[256,512]{1,0:T(8,128)(2,1)} %bitcast.45, ...), custom_call_target="tpu_custom_call" | custom-call | flops 1 | bytes 1 | tf_op jit(solution)/shard_map/pallas_call | solution.py:468
  75.9 0.8 collective-permute-start.2
  76.8 4.7 %shard_map.187.refs_7_ = bf16[1024,512]{1,0:T(8,128)(2,1)} custom-call(s32[1]{0:T(128)} %bitcast.refs_0_, bf16[256,512]{1,0:T(8,128)(2,1)} %get-tuple-element.113.refs_1_, bf16[256,512]{1,0:T(8,128)(2,1)} %get-tuple-element.132.refs_2_.refs_5_, bf16[768,512]{1,0:T(8,128)(2,1)} %refs_3_.6, bf16[512,512]{1,0:T(8,128)(2,1)} %get-tuple-element.103.refs_10_.refs_4_, ...), custom_call_target="tpu_custom_call" | custom-call | flops 1 | bytes 1 | tf_op jit(solution)/shard_map/pallas_call | solution.py:468
  81.6 1.2 add_convert_fusion.3
  82.7 0.7 collective-permute-start.3
  83.5 1.6 %collective-permute-start.5 = (bf16[192,512]{1,0:T(8,128)(2,1)S(1)}, bf16[192,512]{1,0:T(8,128)(2,1)S(1)}, u32[]{:S(2)}, u32[]{:S(2)}) collective-permute-start(bf16[192,512]{1,0:T(8,128)(2,1)S(1)} %fusion.1), channel_id=1, source_target_pairs={{0,8},{1,9},{2,10},{3,11},{4,12},{5,13},{6,14},{7,15},{8,0},{9,1},... | collective-permute-start | bytes 589832 | tf_op jit(solution)/shard_map/ppermute | solution.py:488
  85.1 4.0 %shard_map.188 = (f32[128,512]{1,0:T(8,128)}, bf16[256,512]{1,0:T(8,128)(2,1)}) custom-call(bf16[512,128]{1,0:T(8,128)(2,1)} %get-tuple-element.126.refs_0_, bf16[512,128]{1,0:T(8,128)(2,1)} %get-tuple-element.96.refs_0_.refs_1_, bf16[256,384]{1,0:T(8,128)(2,1)} %get-tuple-element.84.refs_0_.refs_2_, ...), custom_call_target="tpu_custom_call" | custom-call | flops 1 | bytes 1 | tf_op jit(solution)/shard_map/pallas_call | solution.py:468
  89.2 5.7 %collective-permute-done.5 = bf16[192,512]{1,0:T(8,128)(2,1)S(1)} collective-permute-done((bf16[192,512]{1,0:T(8,128)(2,1)S(1)}, bf16[192,512]{1,0:T(8,128)(2,1)S(1)}, u32[]{:S(2)}, u32[]{:S(2)}) %collective-permute-start.5) | collective-permute-done | bytes 196640 | tf_op jit(solution)/shard_map/ppermute | solution.py:488
  95.7 2.0 %collective-permute-start.6 = (bf16[256,512]{1,0:T(8,128)(2,1)S(1)}, bf16[256,512]{1,0:T(8,128)(2,1)S(1)}, u32[]{:S(2)}, u32[]{:S(2)}) collective-permute-start(bf16[256,512]{1,0:T(8,128)(2,1)S(1)} %dynamic-slice_bitcast_fusion.2), channel_id=1, source_target_pairs={{0,4},{1,5},{2,6},{3,7},{4,0},{5,1},{6,2},{7,3},{8,12},{9,13},{10,... | collective-permute-start | bytes 786440 | tf_op jit(solution)/shard_map/ppermute | solution.py:488
  97.7 3.9 %shard_map.189.refs_3_ = f32[768,512]{1,0:T(8,128)} custom-call(bf16[768,512]{1,0:T(8,128)(2,1)} %refs_0_.3, bf16[512,512]{1,0:T(8,128)(2,1)} %get-tuple-element.131.refs_17_.refs_18_.refs_11_.refs_4_.refs_1_, bf16[256,512]{1,0:T(8,128)(2,1)} %get-tuple-element.132.refs_2_.refs_5_, bf16[1536,512]{1,0:T(8,128)(2,1)} %refs_3_.7, ...), custom_call_target="tpu_custom_call" | custom-call | flops 1 | bytes 1 | tf_op jit(solution)/shard_map/pallas_call | solution.py:468
  101.6 1.3 collective-permute-done.6
  102.9 1.5 %collective-permute-start.9 = (bf16[192,512]{1,0:T(8,128)(2,1)S(1)}, bf16[192,512]{1,0:T(8,128)(2,1)S(1)}, u32[]{:S(2)}, u32[]{:S(2)}) collective-permute-start(bf16[192,512]{1,0:T(8,128)(2,1)S(1)} %add_convert_fusion.5), channel_id=1, source_target_pairs={{0,4},{1,5},{2,6},{3,7},{4,0},{5,1},{6,2},{7,3},{8,12},{9,13},{10,... | collective-permute-start | bytes 589832 | tf_op jit(solution)/shard_map/ppermute | solution.py:488
  104.5 0.7 collective-permute-start.7
  105.2 2.3 %collective-permute-done.9 = bf16[192,512]{1,0:T(8,128)(2,1)S(1)} collective-permute-done((bf16[192,512]{1,0:T(8,128)(2,1)S(1)}, bf16[192,512]{1,0:T(8,128)(2,1)S(1)}, u32[]{:S(2)}, u32[]{:S(2)}) %collective-permute-start.9) | collective-permute-done | bytes 196640 | tf_op jit(solution)/shard_map/ppermute | solution.py:488
  107.8 9.9 %collective-permute-done.7 = bf16[256,512]{1,0:T(8,128)(2,1)S(1)} collective-permute-done((bf16[256,512]{1,0:T(8,128)(2,1)S(1)}, bf16[256,512]{1,0:T(8,128)(2,1)S(1)}, u32[]{:S(2)}, u32[]{:S(2)}) %collective-permute-start.7) | collective-permute-done | bytes 262176 | tf_op jit(solution)/shard_map/ppermute | solution.py:488
  117.8 5.7 %collective-permute-done.8 = bf16[256,512]{1,0:T(8,128)(2,1)S(1)} collective-permute-done((bf16[256,512]{1,0:T(8,128)(2,1)S(1)}, bf16[256,512]{1,0:T(8,128)(2,1)S(1)}, u32[]{:S(2)}, u32[]{:S(2)}) %collective-permute-start.8) | collective-permute-done | bytes 262176 | tf_op jit(solution)/shard_map/ppermute | solution.py:488
  123.5 1.2 maximum_select_fusion
  124.7 3.0 %collective-permute-start.13 = (bf16[768,512]{1,0:T(8,128)(2,1)}, bf16[768,512]{1,0:T(8,128)(2,1)}, u32[]{:S(2)}, u32[]{:S(2)}) collective-permute-start(bf16[768,512]{1,0:T(8,128)(2,1)} %maximum_select_fusion), channel_id=1, source_target_pairs={{0,1},{1,0},{2,3},{3,2},{4,5},{5,4},{6,7},{7,6},{8,9},{9,8},{10,11... | collective-permute-start | bytes 2359304 | tf_op jit(solution)/shard_map/ppermute | solution.py:488
  128.1 4.6 %all-to-all-start.4 = ((bf16[16,16,512]{2,1,0:T(8,128)(2,1)}), bf16[16,16,512]{2,1,0:T(8,128)(2,1)S(1)}, u32[]{:S(2)}, u32[]{:S(2)}) async-start(bf16[16,16,512]{2,1,0:T(8,128)(2,1)} %bitcast.24), calls=%async_computation.4 | async-start | bytes 524288 | tf_op jit(solution)/shard_map/all_to_all | solution.py:523
  132.7 1.0 shard_map.190
  133.7 1.5 %broadcast_select_fusion.1 = (bf16[768,512]{1,0:T(8,128)(2,1)S(1)}, bf16[768,512]{1,0:T(8,128)(2,1)S(1)}) fusion(bf16[768,512]{1,0:T(8,128)(2,1)} %maximum_select_fusion, bf16[768,512]{1,0:T(8,128)(2,1)} %collective-permute-done.13, pred[]{:T(512)S(6)} %eq.43), kind=kLoop, calls=%fused_computation.8 | loop fusion | flops 786432 | bytes 3145729 | tf_op jit(solution)/shard_map/jit(_where)/select_n | solution.py:814
  135.2 0.8 slice.25
  136.1 1.0 pad_maximum_fusion
  137.1 7.5 %all-to-all-done.4 = bf16[16,16,512]{2,1,0:T(8,128)(2,1)S(1)} async-done(((bf16[16,16,512]{2,1,0:T(8,128)(2,1)}), bf16[16,16,512]{2,1,0:T(8,128)(2,1)S(1)}, u32[]{:S(2)}, u32[]{:S(2)}) %all-to-all-start.4) | async-done | bytes 262176 | tf_op jit(solution)/shard_map/all_to_all | solution.py:523
  145.1 1.0 add_add_fusion
  146.6 1.0 shard_map.191
  (42 shorter events, 4.1 us)
Async XLA Ops:
  17.2 13.6 %all-to-all-start.1 = ((bf16[16,16,512]{2,1,0:T(8,128)(2,1)}), bf16[16,16,512]{2,1,0:T(8,128)(2,1)S(1)}, u32[]{:S(2)}, u32[]{:S(2)}) async-start(bf16[16,16,512]{2,1,0:T(8,128)(2,1)} %convolution_convert_fusion), calls=%async_computation.1 | async-start | bytes 524288 | tf_op jit(solution)/shard_map/all_to_all | solution.py:523
  30.8 0.7 copy-start.3
  35.8 14.4 %all-to-all-start.2 = ((bf16[16,16,512]{2,1,0:T(8,128)(2,1)}), bf16[16,16,512]{2,1,0:T(8,128)(2,1)S(1)}, u32[]{:S(2)}, u32[]{:S(2)}) async-start(bf16[16,16,512]{2,1,0:T(8,128)(2,1)} %bitcast.48), calls=%async_computation.2 | async-start | bytes 524288 | tf_op jit(solution)/shard_map/all_to_all | solution.py:523
  50.2 0.7 copy-start.4
  56.2 4.3 %collective-permute-start = (bf16[768,512]{1,0:T(8,128)(2,1)}, bf16[768,512]{1,0:T(8,128)(2,1)S(1)}, u32[]{:S(2)}, u32[]{:S(2)}) collective-permute-start(bf16[768,512]{1,0:T(8,128)(2,1)} %get-tuple-element.95.refs_7_), channel_id=1, source_target_pairs={{0,1},{1,0},{2,3},{3,2},{4,5},{5,4},{6,7},{7,6},{8,9},{9,8},{10,11... | collective-permute-start | bytes 2359304 | tf_op jit(solution)/shard_map/ppermute | solution.py:488
  56.9 12.9 %all-to-all-start.3 = ((bf16[16,16,512]{2,1,0:T(8,128)(2,1)}), bf16[16,16,512]{2,1,0:T(8,128)(2,1)S(1)}, u32[]{:S(2)}, u32[]{:S(2)}) async-start(bf16[16,16,512]{2,1,0:T(8,128)(2,1)} %bitcast.51), calls=%async_computation.3 | async-start | bytes 524288 | tf_op jit(solution)/shard_map/all_to_all | solution.py:523
  61.9 14.0 %collective-permute-start.1 = (bf16[384,512]{1,0:T(8,128)(2,1)S(1)}, bf16[384,512]{1,0:T(8,128)(2,1)S(1)}, u32[]{:S(2)}, u32[]{:S(2)}) collective-permute-start(bf16[384,512]{1,0:T(8,128)(2,1)S(1)} %get-tuple-element.162), channel_id=1, source_target_pairs={{0,2},{1,3},{2,0},{3,1},{4,6},{5,7},{6,4},{7,5},{8,10},{9,11},{10,... | collective-permute-start | bytes 1179656 | tf_op jit(solution)/shard_map/ppermute | solution.py:488
  69.7 0.7 copy-start.2
  75.9 5.6 %collective-permute-start.2 = (bf16[1024,512]{1,0:T(8,128)(2,1)}, bf16[1024,512]{1,0:T(8,128)(2,1)S(1)}, u32[]{:S(2)}, u32[]{:S(2)}) collective-permute-start(bf16[1024,512]{1,0:T(8,128)(2,1)} %get-tuple-element.115.refs_12_), channel_id=1, source_target_pairs={{0,1},{1,0},{2,3},{3,2},{4,5},{5,4},{6,7},{7,6},{8,9},{9,8},{10,11... | collective-permute-start | bytes 3145736 | tf_op jit(solution)/shard_map/ppermute | solution.py:488
  76.7 6.7 %collective-permute-start.4 = (bf16[192,512]{1,0:T(8,128)(2,1)S(1)}, bf16[192,512]{1,0:T(8,128)(2,1)S(1)}, u32[]{:S(2)}, u32[]{:S(2)}) collective-permute-start(bf16[192,512]{1,0:T(8,128)(2,1)S(1)} %fusion.2), channel_id=1, source_target_pairs={{0,4},{1,5},{2,6},{3,7},{4,0},{5,1},{6,2},{7,3},{8,12},{9,13},{10,... | collective-permute-start | bytes 589832 | tf_op jit(solution)/shard_map/ppermute | solution.py:488
  82.7 12.8 %collective-permute-start.3 = (bf16[512,512]{1,0:T(8,128)(2,1)S(1)}, bf16[512,512]{1,0:T(8,128)(2,1)S(1)}, u32[]{:S(2)}, u32[]{:S(2)}) collective-permute-start(bf16[512,512]{1,0:T(8,128)(2,1)S(1)} %add_convert_fusion.3), channel_id=1, source_target_pairs={{0,2},{1,3},{2,0},{3,1},{4,6},{5,7},{6,4},{7,5},{8,10},{9,11},{10,... | collective-permute-start | bytes 1572872 | tf_op jit(solution)/shard_map/ppermute | solution.py:488
  83.5 11.4 %collective-permute-start.5 = (bf16[192,512]{1,0:T(8,128)(2,1)S(1)}, bf16[192,512]{1,0:T(8,128)(2,1)S(1)}, u32[]{:S(2)}, u32[]{:S(2)}) collective-permute-start(bf16[192,512]{1,0:T(8,128)(2,1)S(1)} %fusion.1), channel_id=1, source_target_pairs={{0,8},{1,9},{2,10},{3,11},{4,12},{5,13},{6,14},{7,15},{8,0},{9,1},... | collective-permute-start | bytes 589832 | tf_op jit(solution)/shard_map/ppermute | solution.py:488
  85.1 4.0 %copy-start.1 = (bf16[1024,512]{1,0:T(8,128)(2,1)S(1)}, bf16[1024,512]{1,0:T(8,128)(2,1)}, u32[]{:S(2)}) copy-start(bf16[1024,512]{1,0:T(8,128)(2,1)} %shard_map.187.refs_7_) | copy-start | bytes 3145732
  95.7 7.2 %collective-permute-start.6 = (bf16[256,512]{1,0:T(8,128)(2,1)S(1)}, bf16[256,512]{1,0:T(8,128)(2,1)S(1)}, u32[]{:S(2)}, u32[]{:S(2)}) collective-permute-start(bf16[256,512]{1,0:T(8,128)(2,1)S(1)} %dynamic-slice_bitcast_fusion.2), channel_id=1, source_target_pairs={{0,4},{1,5},{2,6},{3,7},{4,0},{5,1},{6,2},{7,3},{8,12},{9,13},{10,... | collective-permute-start | bytes 786440 | tf_op jit(solution)/shard_map/ppermute | solution.py:488
  102.9 4.6 %collective-permute-start.9 = (bf16[192,512]{1,0:T(8,128)(2,1)S(1)}, bf16[192,512]{1,0:T(8,128)(2,1)S(1)}, u32[]{:S(2)}, u32[]{:S(2)}) collective-permute-start(bf16[192,512]{1,0:T(8,128)(2,1)S(1)} %add_convert_fusion.5), channel_id=1, source_target_pairs={{0,4},{1,5},{2,6},{3,7},{4,0},{5,1},{6,2},{7,3},{8,12},{9,13},{10,... | collective-permute-start | bytes 589832 | tf_op jit(solution)/shard_map/ppermute | solution.py:488
  104.5 13.2 %collective-permute-start.7 = (bf16[256,512]{1,0:T(8,128)(2,1)S(1)}, bf16[256,512]{1,0:T(8,128)(2,1)S(1)}, u32[]{:S(2)}, u32[]{:S(2)}) collective-permute-start(bf16[256,512]{1,0:T(8,128)(2,1)S(1)} %fusion), channel_id=1, source_target_pairs={{0,8},{1,9},{2,10},{3,11},{4,12},{5,13},{6,14},{7,15},{8,0},{9,1},... | collective-permute-start | bytes 786440 | tf_op jit(solution)/shard_map/ppermute | solution.py:488
  107.7 15.9 %collective-permute-start.10 = (bf16[384,512]{1,0:T(8,128)(2,1)S(1)}, bf16[384,512]{1,0:T(8,128)(2,1)S(1)}, u32[]{:S(2)}, u32[]{:S(2)}) collective-permute-start(bf16[384,512]{1,0:T(8,128)(2,1)S(1)} %maximum_select_fusion.2), channel_id=1, source_target_pairs={{0,2},{1,3},{2,0},{3,1},{4,6},{5,7},{6,4},{7,5},{8,10},{9,11},{10,... | collective-permute-start | bytes 1179656 | tf_op jit(solution)/shard_map/ppermute | solution.py:488
  117.7 5.8 %collective-permute-start.8 = (bf16[256,512]{1,0:T(8,128)(2,1)S(1)}, bf16[256,512]{1,0:T(8,128)(2,1)S(1)}, u32[]{:S(2)}, u32[]{:S(2)}) collective-permute-start(bf16[256,512]{1,0:T(8,128)(2,1)S(1)} %add_convert_fusion.4), channel_id=1, source_target_pairs={{0,4},{1,5},{2,6},{3,7},{4,0},{5,1},{6,2},{7,3},{8,12},{9,13},{10,... | collective-permute-start | bytes 786440 | tf_op jit(solution)/shard_map/ppermute | solution.py:488
  117.8 14.9 %copy-start = (f32[768,512]{1,0:T(8,128)S(1)}, f32[768,512]{1,0:T(8,128)}, u32[]{:S(2)}) copy-start(f32[768,512]{1,0:T(8,128)} %shard_map.189.refs_3_) | copy-start | bytes 4718596
  124.7 9.0 %collective-permute-start.13 = (bf16[768,512]{1,0:T(8,128)(2,1)}, bf16[768,512]{1,0:T(8,128)(2,1)}, u32[]{:S(2)}, u32[]{:S(2)}) collective-permute-start(bf16[768,512]{1,0:T(8,128)(2,1)} %maximum_select_fusion), channel_id=1, source_target_pairs={{0,1},{1,0},{2,3},{3,2},{4,5},{5,4},{6,7},{7,6},{8,9},{9,8},{10,11... | collective-permute-start | bytes 2359304 | tf_op jit(solution)/shard_map/ppermute | solution.py:488
  127.9 4.8 %collective-permute-start.12 = (bf16[512,512]{1,0:T(8,128)(2,1)S(1)}, bf16[512,512]{1,0:T(8,128)(2,1)S(1)}, u32[]{:S(2)}, u32[]{:S(2)}) collective-permute-start(bf16[512,512]{1,0:T(8,128)(2,1)S(1)} %maximum_select_fusion.1.refs_1_), channel_id=1, source_target_pairs={{0,1},{1,0},{2,3},{3,2},{4,5},{5,4},{6,7},{7,6},{8,9},{9,8},{10,11... | collective-permute-start | bytes 1572872 | tf_op jit(solution)/shard_map/ppermute | solution.py:488
  128.0 16.6 %collective-permute-start.11 = (bf16[512,512]{1,0:T(8,128)(2,1)S(1)}, bf16[512,512]{1,0:T(8,128)(2,1)S(1)}, u32[]{:S(2)}, u32[]{:S(2)}) collective-permute-start(bf16[512,512]{1,0:T(8,128)(2,1)S(1)} %maximum_select_fusion.1.refs_1_), channel_id=1, source_target_pairs={{0,2},{1,3},{2,0},{3,1},{4,6},{5,7},{6,4},{7,5},{8,10},{9,11},{10,... | collective-permute-start | bytes 1572872 | tf_op jit(solution)/shard_map/ppermute | solution.py:488
  128.1 16.6 %all-to-all-start.4 = ((bf16[16,16,512]{2,1,0:T(8,128)(2,1)}), bf16[16,16,512]{2,1,0:T(8,128)(2,1)S(1)}, u32[]{:S(2)}, u32[]{:S(2)}) async-start(bf16[16,16,512]{2,1,0:T(8,128)(2,1)} %bitcast.24), calls=%async_computation.4 | async-start | bytes 524288 | tf_op jit(solution)/shard_map/all_to_all | solution.py:523
  135.2 9.8 %copy-start.5 = (f32[128,512]{1,0:T(8,128)S(1)}, f32[128,512]{1,0:T(8,128)}, u32[]{:S(2)}) copy-start(f32[128,512]{1,0:T(8,128)} %get-tuple-element.148) | copy-start | bytes 786436
  135.2 9.8 %copy-start.6 = (f32[128,512]{1,0:T(8,128)S(1)}, f32[128,512]{1,0:T(8,128)}, u32[]{:S(2)}) copy-start(f32[128,512]{1,0:T(8,128)} %get-tuple-element.149) | copy-start | bytes 786436
  144.7 1.9 %collective-permute-start.14 = (bf16[512,512]{1,0:T(8,128)(2,1)S(1)}, bf16[512,512]{1,0:T(8,128)(2,1)S(1)}, u32[]{:S(2)}, u32[]{:S(2)}) collective-permute-start(bf16[512,512]{1,0:T(8,128)(2,1)S(1)} %collective-permute-done.11.refs_1_), channel_id=1, source_target_pairs={{0,1},{1,0},{2,3},{3,2},{4,5},{5,4},{6,7},{7,6},{8,9},{9,8},{10,11... | collective-permute-start | bytes 1572872 | tf_op jit(solution)/shard_map/ppermute | solution.py:488

commit v15 on v14

--- a/solution.py
+++ b/solution.py
@@ -366,21 +366,28 @@
 
 def place_quarters(me_ref, pieces, outs, sems):
     mine = (me_ref[0] & 1) * 2 + ((me_ref[0] >> 1) & 1)
+    tops = (0, outs[0].shape[0])
 
     def each(wait):
         for index, (piece, distance) in enumerate(pieces):
             rows = piece.shape[0]
             for quarter in range(4):
-                inside = (quarter + 1) * rows <= outs[0].shape[0]
-                goal = outs[0].at[pl.ds(quarter * rows, rows)] if inside else outs[1]
-                copy = pltpu.make_async_copy(piece, goal, sems.at[index])
 
                 @pl.when((mine ^ distance) == quarter)
                 def _():
-                    if wait:
-                        copy.wait()
-                    else:
-                        copy.start()
+                    for side, (out, top) in enumerate(zip(outs, tops)):
+                        first = max(quarter * rows, top)
+                        count = min((quarter + 1) * rows, top + out.shape[0]) - first
+                        if count > 0:
+                            copy = pltpu.make_async_copy(
+                                piece.at[pl.ds(first - quarter * rows, count)],
+                                out.at[pl.ds(first - top, count)],
+                                sems.at[2 * index + side],
+                            )
+                            if wait:
+                                copy.wait()
+                            else:
+                                copy.start()
 
     each(False)
     each(True)
@@ -392,6 +399,11 @@
 
 def last_quarters_kernel(me_ref, far_ref, corner_ref, _, __, in_ref, out_ref, sems):
     place_quarters(me_ref, [(far_ref, 1), (corner_ref, 3)], (in_ref, out_ref), sems)
+
+
+def all_quarters_kernel(me_ref, mine_ref, far_ref, near_ref, corner_ref, in_ref, out_ref, sems):
+    pieces = [(mine_ref, 0), (far_ref, 1), (near_ref, 2), (corner_ref, 3)]
+    place_quarters(me_ref, pieces, (in_ref, out_ref), sems)
 
 
 def input_grads_kernel(
@@ -802,23 +814,25 @@
     edge_sum = added(*fence(edge_sum, edge_got))
     for bit in bits[4:]:
         edge_sum = added(*handed(edge_sum, domains, bit))
-    *edge_parts, node_sum, other_sum, outgoing_grad = fence(
+    *edge_parts, node_near, node_far, outgoing_grad = fence(
         *handed(edge_sum, domains, 2), *node_parts, outgoing_grad
     )
     edge_sum = joined(edge_parts, 2)
-    node_sum = joined([node_sum, other_sum], 1)
     far, near = across(edge_sum, domains, 2), across(edge_sum, domains, 1)
-    others = across(node_sum, domains, 1)
+    node_parts = [node_near, node_far]
+    node_parts += [across(part, domains, 1) for part in node_parts]
     returned = exchange(outgoing_grad, domains)
-    lower = place_of(0) == 0
-    low_rows, high_rows = jnp.where(lower, node_sum, others), jnp.where(lower, others, node_sum)
-    cut_at = 2 * latent - low_rows.shape[0]
-    grad_node_in = jnp.concatenate([low_rows, high_rows[:cut_at]])
-    grad_node_out = high_rows[cut_at:]
     quarters = [shaped(BF16, 3 * latent, latent), shaped(BF16, latent, latent)]
-    copies = dict(out_specs=[HBM] * 2, scratch=[pltpu.SemaphoreType.DMA((2,))], limit=2**20)
+    copies = dict(out_specs=[HBM] * 2, scratch=[pltpu.SemaphoreType.DMA((8,))], limit=2**20)
     grad_edge_in, grad_edge_out = line.run(
         first_quarters_kernel, quarters, [me, edge_sum, near], [SMEM, ANY, ANY], **copies
+    )
+    grad_node_in, grad_node_out = line.run(
+        all_quarters_kernel,
+        [shaped(BF16, 2 * latent, latent), shaped(BF16, latent, latent)],
+        [me] + node_parts,
+        [SMEM] + [ANY] * 4,
+        **copies,
     )
     far, grad_edge_in, grad_edge_out, grad_node_in, grad_node_out, returned = fence(
         far, grad_edge_in, grad_edge_out, grad_node_in, grad_node_out, returned

time: 149 us -> 153 us (1.027)
  Pallas kernels: 45.9 us -> 59.1 us
  waiting for transfers between devices: 42.7 us -> 35.5 us
  other arithmetic: 8.55 us -> 4.85 us
    pallas_call x13 -> x14, Pallas kernels: 45.9 us -> 59.1 us  [run(): pl.pallas_call(ordered, out_shape=out_shape, in_specs=specs, out_specs=[V...]
    all_to_all x4, waiting for transfers between devices: 16.6 us -> 9.1 us  [exchange(): lax.all_to_all(split, 'dom', split_axis=0, concat_axis=0, tiled=True)]
    unnamed x14 -> x12, local copies, waits for them, and re-layouts: 2.13 us -> 3.16 us
    ppermute x15 -> x16, waiting for transfers between devices: 26 us -> 26.4 us  [across(): lax.ppermute(rows, 'dom', [(device, device ^ mask) for device in range(de...]
    ppermute x15 -> x16, starting transfers between devices: 12.9 us -> 13.2 us  [across(): lax.ppermute(rows, 'dom', [(device, device ^ mask) for device in range(de...]
  transfers between devices with their start and end apart: 19 -> 20, of which waited for: 11 -> 11; matrix products, arithmetic and copies ran while one was open for 7% -> 5% of each run, Pallas kernels for 23% -> 31%
where the time goes in v15:
time: 153 us; the launch traced here: 151 us
  Pallas kernels  59.1 us (39%)
  waiting for transfers between devices  35.5 us (23%)
  starting transfers between devices  30 us (20%)
  blocking collectives  13 us (8%)
  other arithmetic  4.85 us (3%)
  matrix products  3.98 us (3%)
  local copies, waits for them, and re-layouts  3.83 us (3%)
    pallas_call x14, Pallas kernels, run(): pl.pallas_call(ordered, out_shape=out_shape, in_specs=specs, out_specs=[V...  59.1 us
    ppermute x16, waiting for transfers between devices, across(): lax.ppermute(rows, 'dom', [(device, device ^ mask) for device in range(de...  26.4 us
    all_to_all x4, starting transfers between devices, exchange(): lax.all_to_all(split, 'dom', split_axis=0, concat_axis=0, tiled=True)  16.8 us
    ppermute x16, starting transfers between devices, across(): lax.ppermute(rows, 'dom', [(device, device ^ mask) for device in range(de...  13.2 us
    all_to_all x1, blocking collectives, shards(): asked = lax.all_to_all(ask, 'dom', split_axis=0, concat_axis=0, tiled=True)  13 us
    all_to_all x4, waiting for transfers between devices, exchange(): lax.all_to_all(split, 'dom', split_axis=0, concat_axis=0, tiled=True)  9.1 us
    unnamed x12, local copies, waits for them, and re-layouts  3.16 us
    convert_element_type x9, other arithmetic, added(): return sum((part.astype(F32) for part in parts)).astype(BF16)  3.11 us
  transfers between devices with their start and end apart: 20, of which 11 were waited for; matrix products, arithmetic and copies ran while one was open for 5% of the time, Pallas kernels for 31%

profile of v15, /device:TPU:1, one launch (start us, length us, event | category | flops | bytes accessed | tf_op | source)
XLA Modules:
  0.0 151.3 jit_solution(6593320403176031174)
XLA Ops:
  0.6 1.7 %shard_map.179.refs_2_ = s32[16,16]{1,0:T(8,128)} custom-call(s32[1,128]{1,0:T(1,128)} %bitcast.54, s32[1,128]{1,0:T(1,128)} %bitcast.57), custom_call_target="tpu_custom_call" | custom-call | flops 1 | bytes 1 | tf_op jit(solution)/shard_map/pallas_call | solution.py:480
  2.3 13.0 %all_to_all.29 = s32[16,1,16]{2,1,0:T(1,128)S(1)} all-to-all(s32[16,1,16]{2,1,0:T(1,128)} %bitcast.53), channel_id=1, replica_groups=mesh['groups'=2,'dom'=16] {'dom'}, dimensions={0} | all-to-all | bytes 2048 | tf_op jit(solution)/shard_map/all_to_all | solution.py:565
  15.4 1.9 %convolution_convert_fusion = bf16[16,16,512]{2,1,0:T(8,128)(2,1)} fusion(bf16[128,512]{1,0:T(8,128)(2,1)} %refs_4_.4, s32[16,16]{1,0:T(8,128)S(1)} %bitcast.52), kind=kOutput, calls=%fused_computation.1 | convolution fusion | flops 33783808 | bytes 394240 | tf_op jit(solution)/shard_map/dot_general | solution.py:574
  17.2 4.0 %all-to-all-start.1 = ((bf16[16,16,512]{2,1,0:T(8,128)(2,1)}), bf16[16,16,512]{2,1,0:T(8,128)(2,1)S(1)}, u32[]{:S(2)}, u32[]{:S(2)}) async-start(bf16[16,16,512]{2,1,0:T(8,128)(2,1)} %convolution_convert_fusion), calls=%async_computation.1 | async-start | bytes 524288 | tf_op jit(solution)/shard_map/all_to_all | solution.py:535
  21.3 2.0 %shard_map.180 = (bf16[256,384]{1,0:T(8,128)(2,1)}, bf16[256,384]{1,0:T(8,128)(2,1)}) custom-call(s32[1,128]{1,0:T(1,128)} %bitcast.55, s32[1,128]{1,0:T(1,128)} %bitcast.58, s32[16,16]{1,0:T(8,128)} %shard_map.179.refs_2_), custom_call_target="tpu_custom_call" | custom-call | flops 1 | bytes 1 | tf_op jit(solution)/shard_map/pallas_call | solution.py:480
  23.3 6.3 %shard_map.181 = (bf16[512,128]{1,0:T(8,128)(2,1)}, bf16[512,128]{1,0:T(8,128)(2,1)}, bf16[512,512]{1,0:T(8,128)(2,1)}, bf16[512,512]{1,0:T(8,128)(2,1)}, bf16[5...) custom-call(s32[2,256]{1,0:T(2,128)} %bitcast.56, ...), custom_call_target="tpu_custom_call" | custom-call | flops 1 | bytes 1 | tf_op jit(solution)/shard_map/pallas_call | solution.py:480
  29.6 1.2 all-to-all-done.1
  30.8 0.7 copy-done.4
  31.5 4.3 %shard_map.182 = (bf16[256,512]{1,0:T(8,128)(2,1)}, bf16[256,512]{1,0:T(8,128)(2,1)}, bf16[256,512]{1,0:T(8,128)(2,1)}, f32[256,512]{1,0:T(8,128)}, f32[256,512]...) custom-call(bf16[256,384]{1,0:T(8,128)(2,1)} %get-tuple-element.86.refs_0_.refs_2_, ...), custom_call_target="tpu_custom_call" | custom-call | flops 1 | bytes 1 | tf_op jit(solution)/shard_map/pallas_call | solution.py:480
  35.8 4.9 %all-to-all-start.2 = ((bf16[16,16,512]{2,1,0:T(8,128)(2,1)}), bf16[16,16,512]{2,1,0:T(8,128)(2,1)S(1)}, u32[]{:S(2)}, u32[]{:S(2)}) async-start(bf16[16,16,512]{2,1,0:T(8,128)(2,1)} %bitcast.48), calls=%async_computation.2 | async-start | bytes 524288 | tf_op jit(solution)/shard_map/all_to_all | solution.py:535
  41.2 0.7 reduce.3
  41.9 0.7 select_convert_fusion.refs_2_
  42.7 2.7 %shard_map.183.refs_8_ = bf16[768,512]{1,0:T(8,128)(2,1)} custom-call(bf16[768,512]{1,0:T(8,128)(2,1)} %refs_3_.6, f32[512,512]{1,0:T(8,128)} %get-tuple-element.91.refs_1_.refs_3_, f32[256,512]{1,0:T(8,128)} %get-tuple-element.92.refs_2_.refs_5_, bf16[256,512]{1,0:T(8,128)(2,1)} %get-tuple-element.89.refs_3_), custom_call_target="tpu_custom_call" | custom-call | flops 1 | bytes 1 | tf_op jit(solution)/shard_map/pallas_call | solution.py:480
  45.3 4.8 %all-to-all-done.2 = bf16[16,16,512]{2,1,0:T(8,128)(2,1)S(1)} async-done(((bf16[16,16,512]{2,1,0:T(8,128)(2,1)}), bf16[16,16,512]{2,1,0:T(8,128)(2,1)S(1)}, u32[]{:S(2)}, u32[]{:S(2)}) %all-to-all-start.2) | async-done | bytes 262176 | tf_op jit(solution)/shard_map/all_to_all | solution.py:535
  50.2 0.7 copy-done.5
  50.9 5.4 %shard_map.184 = (bf16[128,512]{1,0:T(8,128)(2,1)}, f32[128,512]{1,0:T(8,128)}, bf16[128,512]{1,0:T(8,128)(2,1)}, bf16[256,512]{1,0:T(8,128)(2,1)}, bf16[768,512]{1,0:T(8,128)(2,1)}, /*index=5*/bf16[768,512]{1,0:T(8,128)(2,1)}) custom-call(s32[1]{0:T(128)} %bitcast.refs_0_, bf16[256,512]{1,0:T(8,128)(2,1)} %bitcast.47, ...), custom_call_target="tpu_custom_call" | custom-call | flops 1 | bytes 1 | tf_op jit(solution)/shard_map/pallas_call | solution.py:480
  56.2 0.6 collective-permute-start
  56.9 3.6 %all-to-all-start.3 = ((bf16[16,16,512]{2,1,0:T(8,128)(2,1)}), bf16[16,16,512]{2,1,0:T(8,128)(2,1)S(1)}, u32[]{:S(2)}, u32[]{:S(2)}) async-start(bf16[16,16,512]{2,1,0:T(8,128)(2,1)} %bitcast.51), calls=%async_computation.3 | async-start | bytes 524288 | tf_op jit(solution)/shard_map/all_to_all | solution.py:535
  60.5 1.3 add_convert_fusion
  61.9 1.2 collective-permute-start.1
  63.1 3.6 %shard_map.185 = (bf16[512,512]{1,0:T(8,128)(2,1)}, bf16[512,512]{1,0:T(8,128)(2,1)}) custom-call(bf16[512,128]{1,0:T(8,128)(2,1)} %get-tuple-element.98.refs_0_.refs_1_, bf16[128,512]{1,0:T(8,128)(2,1)} %get-tuple-element.94.refs_1_.refs_2_, bf16[768,512]{1,0:T(8,128)(2,1)} %refs_0_.3, f32[512,512]{1,0:T(8,128)} %get-tuple-element.91.refs_1_.refs_3_, ...), custom_call_target="tpu_custom_call" | custom-call | flops 1 | bytes 1 | tf_op jit(solution)/shard_map/pallas_call | solution.py:480
  66.7 3.1 %all-to-all-done.3 = bf16[16,16,512]{2,1,0:T(8,128)(2,1)S(1)} async-done(((bf16[16,16,512]{2,1,0:T(8,128)(2,1)}), bf16[16,16,512]{2,1,0:T(8,128)(2,1)S(1)}, u32[]{:S(2)}, u32[]{:S(2)}) %all-to-all-start.3) | async-done | bytes 262176 | tf_op jit(solution)/shard_map/all_to_all | solution.py:535
  69.7 0.7 copy-done.3
  70.4 5.4 %shard_map.186 = (bf16[256,512]{1,0:T(8,128)(2,1)}, bf16[256,512]{1,0:T(8,128)(2,1)}, bf16[1024,512]{1,0:T(8,128)(2,1)}) custom-call(s32[1]{0:T(128)} %bitcast.refs_0_, bf16[256,384]{1,0:T(8,128)(2,1)} %get-tuple-element.87.refs_5_.refs_1_.refs_3_, bf16[128,512]{1,0:T(8,128)(2,1)} %get-tuple-element.94.refs_1_.refs_2_, bf16[256,512]{1,0:T(8,128)(2,1)} %bitcast.45, ...), custom_call_target="tpu_custom_call" | custom-call | flops 1 | bytes 1 | tf_op jit(solution)/shard_map/pallas_call | solution.py:480
  75.9 0.8 collective-permute-start.2
  76.8 4.7 %shard_map.187.refs_7_ = bf16[1024,512]{1,0:T(8,128)(2,1)} custom-call(s32[1]{0:T(128)} %bitcast.refs_0_, bf16[256,512]{1,0:T(8,128)(2,1)} %get-tuple-element.115.refs_1_, bf16[256,512]{1,0:T(8,128)(2,1)} %get-tuple-element.134.refs_2_.refs_5_, bf16[768,512]{1,0:T(8,128)(2,1)} %refs_3_.6, bf16[512,512]{1,0:T(8,128)(2,1)} %get-tuple-element.105.refs_10_.refs_4_, ...), custom_call_target="tpu_custom_call" | custom-call | flops 1 | bytes 1 | tf_op jit(solution)/shard_map/pallas_call | solution.py:480
  81.6 1.2 add_convert_fusion.3
  82.7 0.7 collective-permute-start.3
  83.5 1.6 %collective-permute-start.5 = (bf16[192,512]{1,0:T(8,128)(2,1)S(1)}, bf16[192,512]{1,0:T(8,128)(2,1)S(1)}, u32[]{:S(2)}, u32[]{:S(2)}) collective-permute-start(bf16[192,512]{1,0:T(8,128)(2,1)S(1)} %fusion.1), channel_id=1, source_target_pairs={{0,8},{1,9},{2,10},{3,11},{4,12},{5,13},{6,14},{7,15},{8,0},{9,1},... | collective-permute-start | bytes 589832 | tf_op jit(solution)/shard_map/ppermute | solution.py:500
  85.1 4.0 %shard_map.188 = (f32[128,512]{1,0:T(8,128)}, bf16[256,512]{1,0:T(8,128)(2,1)}) custom-call(bf16[512,128]{1,0:T(8,128)(2,1)} %get-tuple-element.128.refs_0_, bf16[512,128]{1,0:T(8,128)(2,1)} %get-tuple-element.98.refs_0_.refs_1_, bf16[256,384]{1,0:T(8,128)(2,1)} %get-tuple-element.86.refs_0_.refs_2_, ...), custom_call_target="tpu_custom_call" | custom-call | flops 1 | bytes 1 | tf_op jit(solution)/shard_map/pallas_call | solution.py:480
  89.2 5.7 %collective-permute-done.5 = bf16[192,512]{1,0:T(8,128)(2,1)S(1)} collective-permute-done((bf16[192,512]{1,0:T(8,128)(2,1)S(1)}, bf16[192,512]{1,0:T(8,128)(2,1)S(1)}, u32[]{:S(2)}, u32[]{:S(2)}) %collective-permute-start.5) | collective-permute-done | bytes 196640 | tf_op jit(solution)/shard_map/ppermute | solution.py:500
  95.0 0.5 collective-permute-done.3
  95.7 2.0 %collective-permute-start.6 = (bf16[256,512]{1,0:T(8,128)(2,1)S(1)}, bf16[256,512]{1,0:T(8,128)(2,1)S(1)}, u32[]{:S(2)}, u32[]{:S(2)}) collective-permute-start(bf16[256,512]{1,0:T(8,128)(2,1)S(1)} %dynamic-slice_bitcast_fusion.2), channel_id=1, source_target_pairs={{0,4},{1,5},{2,6},{3,7},{4,0},{5,1},{6,2},{7,3},{8,12},{9,13},{10,... | collective-permute-start | bytes 786440 | tf_op jit(solution)/shard_map/ppermute | solution.py:500
  97.7 3.9 %shard_map.189.refs_3_ = f32[768,512]{1,0:T(8,128)} custom-call(bf16[768,512]{1,0:T(8,128)(2,1)} %refs_0_.3, bf16[512,512]{1,0:T(8,128)(2,1)} %get-tuple-element.133.refs_17_.refs_18_.refs_11_.refs_4_.refs_1_, bf16[256,512]{1,0:T(8,128)(2,1)} %get-tuple-element.134.refs_2_.refs_5_, bf16[1536,512]{1,0:T(8,128)(2,1)} %refs_3_.7, ...), custom_call_target="tpu_custom_call" | custom-call | flops 1 | bytes 1 | tf_op jit(solution)/shard_map/pallas_call | solution.py:480
  101.6 1.3 collective-permute-done.6
  102.9 1.5 %collective-permute-start.9 = (bf16[192,512]{1,0:T(8,128)(2,1)S(1)}, bf16[192,512]{1,0:T(8,128)(2,1)S(1)}, u32[]{:S(2)}, u32[]{:S(2)}) collective-permute-start(bf16[192,512]{1,0:T(8,128)(2,1)S(1)} %add_convert_fusion.5), channel_id=1, source_target_pairs={{0,4},{1,5},{2,6},{3,7},{4,0},{5,1},{6,2},{7,3},{8,12},{9,13},{10,... | collective-permute-start | bytes 589832 | tf_op jit(solution)/shard_map/ppermute | solution.py:500
  104.5 0.7 collective-permute-start.7
  105.2 2.3 %collective-permute-done.9 = bf16[192,512]{1,0:T(8,128)(2,1)S(1)} collective-permute-done((bf16[192,512]{1,0:T(8,128)(2,1)S(1)}, bf16[192,512]{1,0:T(8,128)(2,1)S(1)}, u32[]{:S(2)}, u32[]{:S(2)}) %collective-permute-start.9) | collective-permute-done | bytes 196640 | tf_op jit(solution)/shard_map/ppermute | solution.py:500
  107.8 9.9 %collective-permute-done.7 = bf16[256,512]{1,0:T(8,128)(2,1)S(1)} collective-permute-done((bf16[256,512]{1,0:T(8,128)(2,1)S(1)}, bf16[256,512]{1,0:T(8,128)(2,1)S(1)}, u32[]{:S(2)}, u32[]{:S(2)}) %collective-permute-start.7) | collective-permute-done | bytes 262176 | tf_op jit(solution)/shard_map/ppermute | solution.py:500
  117.8 5.7 %collective-permute-done.8 = bf16[256,512]{1,0:T(8,128)(2,1)S(1)} collective-permute-done((bf16[256,512]{1,0:T(8,128)(2,1)S(1)}, bf16[256,512]{1,0:T(8,128)(2,1)S(1)}, u32[]{:S(2)}, u32[]{:S(2)}) %collective-permute-start.8) | collective-permute-done | bytes 262176 | tf_op jit(solution)/shard_map/ppermute | solution.py:500
  123.8 3.0 %collective-permute-start.12 = (bf16[512,512]{1,0:T(8,128)(2,1)S(1)}, bf16[512,512]{1,0:T(8,128)(2,1)S(1)}, u32[]{:S(2)}, u32[]{:S(2)}) collective-permute-start(bf16[512,512]{1,0:T(8,128)(2,1)S(1)} %maximum_select_fusion.refs_1_), channel_id=1, source_target_pairs={{0,1},{1,0},{2,3},{3,2},{4,5},{5,4},{6,7},{7,6},{8,9},{9,8},{10,11... | collective-permute-start | bytes 1572872 | tf_op jit(solution)/shard_map/ppermute | solution.py:500
  126.8 4.3 %all-to-all-start.4 = ((bf16[16,16,512]{2,1,0:T(8,128)(2,1)}), bf16[16,16,512]{2,1,0:T(8,128)(2,1)}, u32[]{:S(2)}, u32[]{:S(2)}) async-start(bf16[16,16,512]{2,1,0:T(8,128)(2,1)} %bitcast.44), calls=%async_computation.4 | async-start | bytes 524288 | tf_op jit(solution)/shard_map/all_to_all | solution.py:535
  131.6 1.0 shard_map.190
  132.8 0.8 collective-permute-done.14.refs_4_
  133.6 1.0 copy-done.1
  134.6 13.1 %shard_map.191 = (bf16[1024,512]{1,0:T(8,128)(2,1)}, bf16[512,512]{1,0:T(8,128)(2,1)}) custom-call(s32[1]{0:T(128)} %bitcast.refs_0_, bf16[384,512]{1,0:T(8,128)(2,1)S(1)} %maximum_select_fusion.1.refs_1_, bf16[384,512]{1,0:T(8,128)(2,1)} %collective-permute-done.10.refs_2_, bf16[384,512]{1,0:T(8,128)(2,1)S(1)} %collective-permute-done.13.refs_3_, ...), custom_call_target="tpu_custom_call" | custom-call | flops 1 | bytes 1 | tf_op jit(solution)/shard_map/pallas_call | solution.py:480
  148.0 2.1 %add_add_fusion = f32[128,512]{1,0:T(8,128)} fusion(f32[128,512]{1,0:T(8,128)} %get-tuple-element.152, f32[128,512]{1,0:T(8,128)} %get-tuple-element.153, bf16[256,512]{1,0:T(8,128)(2,1)} %bitcast.25, s32[256]{0:T(256)S(1)} %eq.32), kind=kOutput, calls=%fused_computation.16 | convolution fusion | flops 33783808 | bytes 1049600 | tf_op jit(solution)/shard_map/dot_general | solution.py:20
  150.1 1.0 shard_map.192
  (38 shorter events, 2.8 us)
Async XLA Ops:
  17.2 13.6 %all-to-all-start.1 = ((bf16[16,16,512]{2,1,0:T(8,128)(2,1)}), bf16[16,16,512]{2,1,0:T(8,128)(2,1)S(1)}, u32[]{:S(2)}, u32[]{:S(2)}) async-start(bf16[16,16,512]{2,1,0:T(8,128)(2,1)} %convolution_convert_fusion), calls=%async_computation.1 | async-start | bytes 524288 | tf_op jit(solution)/shard_map/all_to_all | solution.py:535
  30.8 0.7 copy-start.4
  35.8 14.4 %all-to-all-start.2 = ((bf16[16,16,512]{2,1,0:T(8,128)(2,1)}), bf16[16,16,512]{2,1,0:T(8,128)(2,1)S(1)}, u32[]{:S(2)}, u32[]{:S(2)}) async-start(bf16[16,16,512]{2,1,0:T(8,128)(2,1)} %bitcast.48), calls=%async_computation.2 | async-start | bytes 524288 | tf_op jit(solution)/shard_map/all_to_all | solution.py:535
  50.2 0.7 copy-start.5
  56.2 4.3 %collective-permute-start = (bf16[768,512]{1,0:T(8,128)(2,1)}, bf16[768,512]{1,0:T(8,128)(2,1)S(1)}, u32[]{:S(2)}, u32[]{:S(2)}) collective-permute-start(bf16[768,512]{1,0:T(8,128)(2,1)} %get-tuple-element.97.refs_7_), channel_id=1, source_target_pairs={{0,1},{1,0},{2,3},{3,2},{4,5},{5,4},{6,7},{7,6},{8,9},{9,8},{10,11... | collective-permute-start | bytes 2359304 | tf_op jit(solution)/shard_map/ppermute | solution.py:500
  56.9 12.9 %all-to-all-start.3 = ((bf16[16,16,512]{2,1,0:T(8,128)(2,1)}), bf16[16,16,512]{2,1,0:T(8,128)(2,1)S(1)}, u32[]{:S(2)}, u32[]{:S(2)}) async-start(bf16[16,16,512]{2,1,0:T(8,128)(2,1)} %bitcast.51), calls=%async_computation.3 | async-start | bytes 524288 | tf_op jit(solution)/shard_map/all_to_all | solution.py:535
  61.9 14.0 %collective-permute-start.1 = (bf16[384,512]{1,0:T(8,128)(2,1)S(1)}, bf16[384,512]{1,0:T(8,128)(2,1)S(1)}, u32[]{:S(2)}, u32[]{:S(2)}) collective-permute-start(bf16[384,512]{1,0:T(8,128)(2,1)S(1)} %get-tuple-element.164), channel_id=1, source_target_pairs={{0,2},{1,3},{2,0},{3,1},{4,6},{5,7},{6,4},{7,5},{8,10},{9,11},{10,... | collective-permute-start | bytes 1179656 | tf_op jit(solution)/shard_map/ppermute | solution.py:500
  69.7 0.7 copy-start.3
  75.9 5.6 %collective-permute-start.2 = (bf16[1024,512]{1,0:T(8,128)(2,1)}, bf16[1024,512]{1,0:T(8,128)(2,1)S(1)}, u32[]{:S(2)}, u32[]{:S(2)}) collective-permute-start(bf16[1024,512]{1,0:T(8,128)(2,1)} %get-tuple-element.117.refs_12_), channel_id=1, source_target_pairs={{0,1},{1,0},{2,3},{3,2},{4,5},{5,4},{6,7},{7,6},{8,9},{9,8},{10,11... | collective-permute-start | bytes 3145736 | tf_op jit(solution)/shard_map/ppermute | solution.py:500
  76.7 6.7 %collective-permute-start.4 = (bf16[192,512]{1,0:T(8,128)(2,1)S(1)}, bf16[192,512]{1,0:T(8,128)(2,1)S(1)}, u32[]{:S(2)}, u32[]{:S(2)}) collective-permute-start(bf16[192,512]{1,0:T(8,128)(2,1)S(1)} %fusion.2), channel_id=1, source_target_pairs={{0,4},{1,5},{2,6},{3,7},{4,0},{5,1},{6,2},{7,3},{8,12},{9,13},{10,... | collective-permute-start | bytes 589832 | tf_op jit(solution)/shard_map/ppermute | solution.py:500
  82.7 12.8 %collective-permute-start.3 = (bf16[512,512]{1,0:T(8,128)(2,1)S(1)}, bf16[512,512]{1,0:T(8,128)(2,1)S(1)}, u32[]{:S(2)}, u32[]{:S(2)}) collective-permute-start(bf16[512,512]{1,0:T(8,128)(2,1)S(1)} %add_convert_fusion.3), channel_id=1, source_target_pairs={{0,2},{1,3},{2,0},{3,1},{4,6},{5,7},{6,4},{7,5},{8,10},{9,11},{10,... | collective-permute-start | bytes 1572872 | tf_op jit(solution)/shard_map/ppermute | solution.py:500
  83.5 11.4 %collective-permute-start.5 = (bf16[192,512]{1,0:T(8,128)(2,1)S(1)}, bf16[192,512]{1,0:T(8,128)(2,1)S(1)}, u32[]{:S(2)}, u32[]{:S(2)}) collective-permute-start(bf16[192,512]{1,0:T(8,128)(2,1)S(1)} %fusion.1), channel_id=1, source_target_pairs={{0,8},{1,9},{2,10},{3,11},{4,12},{5,13},{6,14},{7,15},{8,0},{9,1},... | collective-permute-start | bytes 589832 | tf_op jit(solution)/shard_map/ppermute | solution.py:500
  85.1 4.0 %copy-start.2 = (bf16[1024,512]{1,0:T(8,128)(2,1)S(1)}, bf16[1024,512]{1,0:T(8,128)(2,1)}, u32[]{:S(2)}) copy-start(bf16[1024,512]{1,0:T(8,128)(2,1)} %shard_map.187.refs_7_) | copy-start | bytes 3145732
  95.7 7.2 %collective-permute-start.6 = (bf16[256,512]{1,0:T(8,128)(2,1)S(1)}, bf16[256,512]{1,0:T(8,128)(2,1)S(1)}, u32[]{:S(2)}, u32[]{:S(2)}) collective-permute-start(bf16[256,512]{1,0:T(8,128)(2,1)S(1)} %dynamic-slice_bitcast_fusion.2), channel_id=1, source_target_pairs={{0,4},{1,5},{2,6},{3,7},{4,0},{5,1},{6,2},{7,3},{8,12},{9,13},{10,... | collective-permute-start | bytes 786440 | tf_op jit(solution)/shard_map/ppermute | solution.py:500
  102.9 4.6 %collective-permute-start.9 = (bf16[192,512]{1,0:T(8,128)(2,1)S(1)}, bf16[192,512]{1,0:T(8,128)(2,1)S(1)}, u32[]{:S(2)}, u32[]{:S(2)}) collective-permute-start(bf16[192,512]{1,0:T(8,128)(2,1)S(1)} %add_convert_fusion.5), channel_id=1, source_target_pairs={{0,4},{1,5},{2,6},{3,7},{4,0},{5,1},{6,2},{7,3},{8,12},{9,13},{10,... | collective-permute-start | bytes 589832 | tf_op jit(solution)/shard_map/ppermute | solution.py:500
  104.5 13.2 %collective-permute-start.7 = (bf16[256,512]{1,0:T(8,128)(2,1)S(1)}, bf16[256,512]{1,0:T(8,128)(2,1)S(1)}, u32[]{:S(2)}, u32[]{:S(2)}) collective-permute-start(bf16[256,512]{1,0:T(8,128)(2,1)S(1)} %fusion), channel_id=1, source_target_pairs={{0,8},{1,9},{2,10},{3,11},{4,12},{5,13},{6,14},{7,15},{8,0},{9,1},... | collective-permute-start | bytes 786440 | tf_op jit(solution)/shard_map/ppermute | solution.py:500
  105.2 26.4 %copy-start = (f32[768,512]{1,0:T(8,128)S(1)}, f32[768,512]{1,0:T(8,128)}, u32[]{:S(2)}) copy-start(f32[768,512]{1,0:T(8,128)} %shard_map.189.refs_3_) | copy-start | bytes 4718596
  107.7 15.9 %collective-permute-start.10 = (bf16[384,512]{1,0:T(8,128)(2,1)S(1)}, bf16[384,512]{1,0:T(8,128)(2,1)}, u32[]{:S(2)}, u32[]{:S(2)}) collective-permute-start(bf16[384,512]{1,0:T(8,128)(2,1)S(1)} %maximum_select_fusion.1.refs_1_), channel_id=1, source_target_pairs={{0,2},{1,3},{2,0},{3,1},{4,6},{5,7},{6,4},{7,5},{8,10},{9,11},{10,... | collective-permute-start | bytes 1179656 | tf_op jit(solution)/shard_map/ppermute | solution.py:500
  117.7 5.8 %collective-permute-start.8 = (bf16[256,512]{1,0:T(8,128)(2,1)S(1)}, bf16[256,512]{1,0:T(8,128)(2,1)S(1)}, u32[]{:S(2)}, u32[]{:S(2)}) collective-permute-start(bf16[256,512]{1,0:T(8,128)(2,1)S(1)} %add_convert_fusion.4), channel_id=1, source_target_pairs={{0,4},{1,5},{2,6},{3,7},{4,0},{5,1},{6,2},{7,3},{8,12},{9,13},{10,... | collective-permute-start | bytes 786440 | tf_op jit(solution)/shard_map/ppermute | solution.py:500
  123.8 7.8 %collective-permute-start.12 = (bf16[512,512]{1,0:T(8,128)(2,1)S(1)}, bf16[512,512]{1,0:T(8,128)(2,1)S(1)}, u32[]{:S(2)}, u32[]{:S(2)}) collective-permute-start(bf16[512,512]{1,0:T(8,128)(2,1)S(1)} %maximum_select_fusion.refs_1_), channel_id=1, source_target_pairs={{0,1},{1,0},{2,3},{3,2},{4,5},{5,4},{6,7},{7,6},{8,9},{9,8},{10,11... | collective-permute-start | bytes 1572872 | tf_op jit(solution)/shard_map/ppermute | solution.py:500
  126.8 20.9 %collective-permute-start.11 = (bf16[512,512]{1,0:T(8,128)(2,1)S(1)}, bf16[512,512]{1,0:T(8,128)(2,1)S(1)}, u32[]{:S(2)}, u32[]{:S(2)}) collective-permute-start(bf16[512,512]{1,0:T(8,128)(2,1)S(1)} %maximum_select_fusion.refs_1_), channel_id=1, source_target_pairs={{0,2},{1,3},{2,0},{3,1},{4,6},{5,7},{6,4},{7,5},{8,10},{9,11},{10,... | collective-permute-start | bytes 1572872 | tf_op jit(solution)/shard_map/ppermute | solution.py:500
  126.8 20.9 %all-to-all-start.4 = ((bf16[16,16,512]{2,1,0:T(8,128)(2,1)}), bf16[16,16,512]{2,1,0:T(8,128)(2,1)}, u32[]{:S(2)}, u32[]{:S(2)}) async-start(bf16[16,16,512]{2,1,0:T(8,128)(2,1)} %bitcast.44), calls=%async_computation.4 | async-start | bytes 524288 | tf_op jit(solution)/shard_map/all_to_all | solution.py:535
  131.1 1.7 %collective-permute-start.13 = (bf16[384,512]{1,0:T(8,128)(2,1)S(1)}, bf16[384,512]{1,0:T(8,128)(2,1)S(1)}, u32[]{:S(2)}, u32[]{:S(2)}) collective-permute-start(bf16[384,512]{1,0:T(8,128)(2,1)S(1)} %maximum_select_fusion.1.refs_1_), channel_id=1, source_target_pairs={{0,1},{1,0},{2,3},{3,2},{4,5},{5,4},{6,7},{7,6},{8,9},{9,8},{10,11... | collective-permute-start | bytes 1179656 | tf_op jit(solution)/shard_map/ppermute | solution.py:500
  131.3 2.3 %collective-permute-start.14 = (bf16[384,512]{1,0:T(8,128)(2,1)}, bf16[384,512]{1,0:T(8,128)(2,1)S(1)}, u32[]{:S(2)}, u32[]{:S(2)}) collective-permute-start(bf16[384,512]{1,0:T(8,128)(2,1)} %collective-permute-done.10.refs_2_), channel_id=1, source_target_pairs={{0,1},{1,0},{2,3},{3,2},{4,5},{5,4},{6,7},{7,6},{8,9},{9,8},{10,11... | collective-permute-start | bytes 1179656 | tf_op jit(solution)/shard_map/ppermute | solution.py:500
  133.6 1.0 copy-start.1
  147.7 2.4 %collective-permute-start.15 = (bf16[512,512]{1,0:T(8,128)(2,1)S(1)}, bf16[512,512]{1,0:T(8,128)(2,1)S(1)}, u32[]{:S(2)}, u32[]{:S(2)}) collective-permute-start(bf16[512,512]{1,0:T(8,128)(2,1)S(1)} %collective-permute-done.11.refs_1_), channel_id=1, source_target_pairs={{0,1},{1,0},{2,3},{3,2},{4,5},{5,4},{6,7},{7,6},{8,9},{9,8},{10,11... | collective-permute-start | bytes 1572872 | tf_op jit(solution)/shard_map/ppermute | solution.py:500

commit v16 on v15

--- a/solution.py
+++ b/solution.py
@@ -831,8 +831,8 @@
         all_quarters_kernel,
         [shaped(BF16, 2 * latent, latent), shaped(BF16, latent, latent)],
         [me] + node_parts,
-        [SMEM] + [ANY] * 4,
-        **copies,
+        [SMEM] + [VMEM] * 4,
+        **(copies | {"limit": VMEM_LIMIT}),
     )
     far, grad_edge_in, grad_edge_out, grad_node_in, grad_node_out, returned = fence(
         far, grad_edge_in, grad_edge_out, grad_node_in, grad_node_out, returned

time: 153 us -> 148 us (0.967)
  Pallas kernels: 59.1 us -> 48.6 us
  waiting for transfers between devices: 35.5 us -> 42.9 us
    pallas_call x14, Pallas kernels: 59.1 us -> 48.6 us  [run(): pl.pallas_call(ordered, out_shape=out_shape, in_specs=specs, out_specs=[V...]
    all_to_all x4, waiting for transfers between devices: 9.1 us -> 16.4 us  [exchange(): lax.all_to_all(split, 'dom', split_axis=0, concat_axis=0, tiled=True)]
    unnamed x12 -> x18, local copies, waits for them, and re-layouts: 3.16 us -> 2.13 us
  transfers between devices with their start and end apart: 20 -> 20, of which waited for: 11 -> 12; matrix products, arithmetic and copies ran while one was open for 5% -> 5% of each run, Pallas kernels for 31% -> 25%
where the time goes in v16:
time: 148 us; the launch traced here: 147 us
  Pallas kernels  48.6 us (33%)
  waiting for transfers between devices  42.9 us (29%)
  starting transfers between devices  30 us (20%)
  blocking collectives  13 us (9%)
  other arithmetic  4.84 us (3%)
  matrix products  3.82 us (3%)
  local copies, waits for them, and re-layouts  2.81 us (2%)
    pallas_call x14, Pallas kernels, run(): pl.pallas_call(ordered, out_shape=out_shape, in_specs=specs, out_specs=[V...  48.6 us
    ppermute x16, waiting for transfers between devices, across(): lax.ppermute(rows, 'dom', [(device, device ^ mask) for device in range(de...  26.6 us
    all_to_all x4, starting transfers between devices, exchange(): lax.all_to_all(split, 'dom', split_axis=0, concat_axis=0, tiled=True)  16.7 us
    all_to_all x4, waiting for transfers between devices, exchange(): lax.all_to_all(split, 'dom', split_axis=0, concat_axis=0, tiled=True)  16.4 us
    ppermute x16, starting transfers between devices, across(): lax.ppermute(rows, 'dom', [(device, device ^ mask) for device in range(de...  13.3 us
    all_to_all x1, blocking collectives, shards(): asked = lax.all_to_all(ask, 'dom', split_axis=0, concat_axis=0, tiled=True)  13 us
    convert_element_type x9, other arithmetic, added(): return sum((part.astype(F32) for part in parts)).astype(BF16)  3.11 us
  transfers between devices with their start and end apart: 20, of which 12 were waited for; matrix products, arithmetic and copies ran while one was open for 5% of the time, Pallas kernels for 25%

profile of v16, /device:TPU:1, one launch (start us, length us, event | category | flops | bytes accessed | tf_op | source)
XLA Modules:
  0.0 147.1 jit_solution(9233817009873986867)
XLA Ops:
  0.6 1.7 %shard_map.179.refs_2_ = s32[16,16]{1,0:T(8,128)} custom-call(s32[1,128]{1,0:T(1,128)} %bitcast.54, s32[1,128]{1,0:T(1,128)} %bitcast.57), custom_call_target="tpu_custom_call" | custom-call | flops 1 | bytes 1 | tf_op jit(solution)/shard_map/pallas_call | solution.py:480
  2.3 13.0 %all_to_all.29 = s32[16,1,16]{2,1,0:T(1,128)S(1)} all-to-all(s32[16,1,16]{2,1,0:T(1,128)} %bitcast.53), channel_id=1, replica_groups=mesh['groups'=2,'dom'=16] {'dom'}, dimensions={0} | all-to-all | bytes 2048 | tf_op jit(solution)/shard_map/all_to_all | solution.py:565
  15.4 1.9 %convolution_convert_fusion = bf16[16,16,512]{2,1,0:T(8,128)(2,1)} fusion(bf16[128,512]{1,0:T(8,128)(2,1)} %refs_4_.4, s32[16,16]{1,0:T(8,128)S(1)} %bitcast.52), kind=kOutput, calls=%fused_computation.1 | convolution fusion | flops 33783808 | bytes 394240 | tf_op jit(solution)/shard_map/dot_general | solution.py:574
  17.2 4.0 %all-to-all-start.1 = ((bf16[16,16,512]{2,1,0:T(8,128)(2,1)}), bf16[16,16,512]{2,1,0:T(8,128)(2,1)S(1)}, u32[]{:S(2)}, u32[]{:S(2)}) async-start(bf16[16,16,512]{2,1,0:T(8,128)(2,1)} %convolution_convert_fusion), calls=%async_computation.1 | async-start | bytes 524288 | tf_op jit(solution)/shard_map/all_to_all | solution.py:535
  21.3 2.0 %shard_map.180 = (bf16[256,384]{1,0:T(8,128)(2,1)}, bf16[256,384]{1,0:T(8,128)(2,1)}) custom-call(s32[1,128]{1,0:T(1,128)} %bitcast.55, s32[1,128]{1,0:T(1,128)} %bitcast.58, s32[16,16]{1,0:T(8,128)} %shard_map.179.refs_2_), custom_call_target="tpu_custom_call" | custom-call | flops 1 | bytes 1 | tf_op jit(solution)/shard_map/pallas_call | solution.py:480
  23.3 6.3 %shard_map.181 = (bf16[512,128]{1,0:T(8,128)(2,1)}, bf16[512,128]{1,0:T(8,128)(2,1)}, bf16[512,512]{1,0:T(8,128)(2,1)}, bf16[512,512]{1,0:T(8,128)(2,1)}, bf16[5...) custom-call(s32[2,256]{1,0:T(2,128)} %bitcast.56, ...), custom_call_target="tpu_custom_call" | custom-call | flops 1 | bytes 1 | tf_op jit(solution)/shard_map/pallas_call | solution.py:480
  29.6 1.2 all-to-all-done.1
  30.8 0.7 copy-done.4
  31.5 4.3 %shard_map.182 = (bf16[256,512]{1,0:T(8,128)(2,1)}, bf16[256,512]{1,0:T(8,128)(2,1)}, bf16[256,512]{1,0:T(8,128)(2,1)}, f32[256,512]{1,0:T(8,128)}, f32[256,512]...) custom-call(bf16[256,384]{1,0:T(8,128)(2,1)} %get-tuple-element.86.refs_0_.refs_2_, ...), custom_call_target="tpu_custom_call" | custom-call | flops 1 | bytes 1 | tf_op jit(solution)/shard_map/pallas_call | solution.py:480
  35.8 4.9 %all-to-all-start.2 = ((bf16[16,16,512]{2,1,0:T(8,128)(2,1)}), bf16[16,16,512]{2,1,0:T(8,128)(2,1)S(1)}, u32[]{:S(2)}, u32[]{:S(2)}) async-start(bf16[16,16,512]{2,1,0:T(8,128)(2,1)} %bitcast.48), calls=%async_computation.2 | async-start | bytes 524288 | tf_op jit(solution)/shard_map/all_to_all | solution.py:535
  41.2 0.7 reduce.3
  41.9 0.7 select_convert_fusion.refs_2_
  42.6 2.7 %shard_map.183.refs_8_ = bf16[768,512]{1,0:T(8,128)(2,1)} custom-call(bf16[768,512]{1,0:T(8,128)(2,1)} %refs_3_.6, f32[512,512]{1,0:T(8,128)} %get-tuple-element.91.refs_1_.refs_3_, f32[256,512]{1,0:T(8,128)} %get-tuple-element.92.refs_2_.refs_5_, bf16[256,512]{1,0:T(8,128)(2,1)} %get-tuple-element.89.refs_3_), custom_call_target="tpu_custom_call" | custom-call | flops 1 | bytes 1 | tf_op jit(solution)/shard_map/pallas_call | solution.py:480
  45.3 4.8 %all-to-all-done.2 = bf16[16,16,512]{2,1,0:T(8,128)(2,1)S(1)} async-done(((bf16[16,16,512]{2,1,0:T(8,128)(2,1)}), bf16[16,16,512]{2,1,0:T(8,128)(2,1)S(1)}, u32[]{:S(2)}, u32[]{:S(2)}) %all-to-all-start.2) | async-done | bytes 262176 | tf_op jit(solution)/shard_map/all_to_all | solution.py:535
  50.2 0.7 copy-done.5
  50.9 5.4 %shard_map.184 = (bf16[128,512]{1,0:T(8,128)(2,1)}, f32[128,512]{1,0:T(8,128)}, bf16[128,512]{1,0:T(8,128)(2,1)}, bf16[256,512]{1,0:T(8,128)(2,1)}, bf16[768,512]{1,0:T(8,128)(2,1)}, /*index=5*/bf16[768,512]{1,0:T(8,128)(2,1)}) custom-call(s32[1]{0:T(128)} %bitcast.refs_0_, bf16[256,512]{1,0:T(8,128)(2,1)} %bitcast.47, ...), custom_call_target="tpu_custom_call" | custom-call | flops 1 | bytes 1 | tf_op jit(solution)/shard_map/pallas_call | solution.py:480
  56.2 0.6 collective-permute-start
  56.9 3.6 %all-to-all-start.3 = ((bf16[16,16,512]{2,1,0:T(8,128)(2,1)}), bf16[16,16,512]{2,1,0:T(8,128)(2,1)S(1)}, u32[]{:S(2)}, u32[]{:S(2)}) async-start(bf16[16,16,512]{2,1,0:T(8,128)(2,1)} %bitcast.51), calls=%async_computation.3 | async-start | bytes 524288 | tf_op jit(solution)/shard_map/all_to_all | solution.py:535
  60.5 1.3 add_convert_fusion
  61.9 1.2 collective-permute-start.1
  63.1 3.6 %shard_map.185 = (bf16[512,512]{1,0:T(8,128)(2,1)}, bf16[512,512]{1,0:T(8,128)(2,1)}) custom-call(bf16[512,128]{1,0:T(8,128)(2,1)} %get-tuple-element.98.refs_0_.refs_1_, bf16[128,512]{1,0:T(8,128)(2,1)} %get-tuple-element.94.refs_1_.refs_2_, bf16[768,512]{1,0:T(8,128)(2,1)} %refs_0_.3, f32[512,512]{1,0:T(8,128)} %get-tuple-element.91.refs_1_.refs_3_, ...), custom_call_target="tpu_custom_call" | custom-call | flops 1 | bytes 1 | tf_op jit(solution)/shard_map/pallas_call | solution.py:480
  66.7 3.1 %all-to-all-done.3 = bf16[16,16,512]{2,1,0:T(8,128)(2,1)S(1)} async-done(((bf16[16,16,512]{2,1,0:T(8,128)(2,1)}), bf16[16,16,512]{2,1,0:T(8,128)(2,1)S(1)}, u32[]{:S(2)}, u32[]{:S(2)}) %all-to-all-start.3) | async-done | bytes 262176 | tf_op jit(solution)/shard_map/all_to_all | solution.py:535
  69.8 0.7 copy-done.3
  70.5 5.4 %shard_map.186 = (bf16[256,512]{1,0:T(8,128)(2,1)}, bf16[256,512]{1,0:T(8,128)(2,1)}, bf16[1024,512]{1,0:T(8,128)(2,1)}) custom-call(s32[1]{0:T(128)} %bitcast.refs_0_, bf16[256,384]{1,0:T(8,128)(2,1)} %get-tuple-element.87.refs_5_.refs_1_.refs_3_, bf16[128,512]{1,0:T(8,128)(2,1)} %get-tuple-element.94.refs_1_.refs_2_, bf16[256,512]{1,0:T(8,128)(2,1)} %bitcast.45, ...), custom_call_target="tpu_custom_call" | custom-call | flops 1 | bytes 1 | tf_op jit(solution)/shard_map/pallas_call | solution.py:480
  75.9 0.8 collective-permute-start.2
  76.8 4.7 %shard_map.187.refs_7_ = bf16[1024,512]{1,0:T(8,128)(2,1)} custom-call(s32[1]{0:T(128)} %bitcast.refs_0_, bf16[256,512]{1,0:T(8,128)(2,1)} %get-tuple-element.115.refs_1_, bf16[256,512]{1,0:T(8,128)(2,1)} %get-tuple-element.134.refs_2_.refs_5_, bf16[768,512]{1,0:T(8,128)(2,1)} %refs_3_.6, bf16[512,512]{1,0:T(8,128)(2,1)} %get-tuple-element.105.refs_10_.refs_4_, ...), custom_call_target="tpu_custom_call" | custom-call | flops 1 | bytes 1 | tf_op jit(solution)/shard_map/pallas_call | solution.py:480
  81.6 1.2 add_convert_fusion.3
  82.7 0.7 collective-permute-start.3
  83.5 1.6 %collective-permute-start.5 = (bf16[192,512]{1,0:T(8,128)(2,1)S(1)}, bf16[192,512]{1,0:T(8,128)(2,1)S(1)}, u32[]{:S(2)}, u32[]{:S(2)}) collective-permute-start(bf16[192,512]{1,0:T(8,128)(2,1)S(1)} %fusion.1), channel_id=1, source_target_pairs={{0,8},{1,9},{2,10},{3,11},{4,12},{5,13},{6,14},{7,15},{8,0},{9,1},... | collective-permute-start | bytes 589832 | tf_op jit(solution)/shard_map/ppermute | solution.py:500
  85.1 4.0 %shard_map.188 = (f32[128,512]{1,0:T(8,128)}, bf16[256,512]{1,0:T(8,128)(2,1)}) custom-call(bf16[512,128]{1,0:T(8,128)(2,1)} %get-tuple-element.128.refs_0_, bf16[512,128]{1,0:T(8,128)(2,1)} %get-tuple-element.98.refs_0_.refs_1_, bf16[256,384]{1,0:T(8,128)(2,1)} %get-tuple-element.86.refs_0_.refs_2_, ...), custom_call_target="tpu_custom_call" | custom-call | flops 1 | bytes 1 | tf_op jit(solution)/shard_map/pallas_call | solution.py:480
  89.2 5.7 %collective-permute-done.5 = bf16[192,512]{1,0:T(8,128)(2,1)S(1)} collective-permute-done((bf16[192,512]{1,0:T(8,128)(2,1)S(1)}, bf16[192,512]{1,0:T(8,128)(2,1)S(1)}, u32[]{:S(2)}, u32[]{:S(2)}) %collective-permute-start.5) | collective-permute-done | bytes 196640 | tf_op jit(solution)/shard_map/ppermute | solution.py:500
  95.0 0.6 collective-permute-done.3
  95.7 2.0 %collective-permute-start.6 = (bf16[256,512]{1,0:T(8,128)(2,1)S(1)}, bf16[256,512]{1,0:T(8,128)(2,1)S(1)}, u32[]{:S(2)}, u32[]{:S(2)}) collective-permute-start(bf16[256,512]{1,0:T(8,128)(2,1)S(1)} %dynamic-slice_bitcast_fusion.2), channel_id=1, source_target_pairs={{0,4},{1,5},{2,6},{3,7},{4,0},{5,1},{6,2},{7,3},{8,12},{9,13},{10,... | collective-permute-start | bytes 786440 | tf_op jit(solution)/shard_map/ppermute | solution.py:500
  97.7 3.9 %shard_map.189.refs_3_ = f32[768,512]{1,0:T(8,128)} custom-call(bf16[768,512]{1,0:T(8,128)(2,1)} %refs_0_.3, bf16[512,512]{1,0:T(8,128)(2,1)} %get-tuple-element.133.refs_17_.refs_18_.refs_11_.refs_4_.refs_1_, bf16[256,512]{1,0:T(8,128)(2,1)} %get-tuple-element.134.refs_2_.refs_5_, bf16[1536,512]{1,0:T(8,128)(2,1)} %refs_3_.7, ...), custom_call_target="tpu_custom_call" | custom-call | flops 1 | bytes 1 | tf_op jit(solution)/shard_map/pallas_call | solution.py:480
  101.6 1.3 collective-permute-done.6
  103.0 1.5 %collective-permute-start.9 = (bf16[192,512]{1,0:T(8,128)(2,1)S(1)}, bf16[192,512]{1,0:T(8,128)(2,1)S(1)}, u32[]{:S(2)}, u32[]{:S(2)}) collective-permute-start(bf16[192,512]{1,0:T(8,128)(2,1)S(1)} %add_convert_fusion.5), channel_id=1, source_target_pairs={{0,4},{1,5},{2,6},{3,7},{4,0},{5,1},{6,2},{7,3},{8,12},{9,13},{10,... | collective-permute-start | bytes 589832 | tf_op jit(solution)/shard_map/ppermute | solution.py:500
  104.5 0.7 collective-permute-start.7
  105.2 2.3 %collective-permute-done.9 = bf16[192,512]{1,0:T(8,128)(2,1)S(1)} collective-permute-done((bf16[192,512]{1,0:T(8,128)(2,1)S(1)}, bf16[192,512]{1,0:T(8,128)(2,1)S(1)}, u32[]{:S(2)}, u32[]{:S(2)}) %collective-permute-start.9) | collective-permute-done | bytes 196640 | tf_op jit(solution)/shard_map/ppermute | solution.py:500
  107.8 9.9 %collective-permute-done.7 = bf16[256,512]{1,0:T(8,128)(2,1)S(1)} collective-permute-done((bf16[256,512]{1,0:T(8,128)(2,1)S(1)}, bf16[256,512]{1,0:T(8,128)(2,1)S(1)}, u32[]{:S(2)}, u32[]{:S(2)}) %collective-permute-start.7) | collective-permute-done | bytes 262176 | tf_op jit(solution)/shard_map/ppermute | solution.py:500
  117.8 5.7 %collective-permute-done.8 = bf16[256,512]{1,0:T(8,128)(2,1)S(1)} collective-permute-done((bf16[256,512]{1,0:T(8,128)(2,1)S(1)}, bf16[256,512]{1,0:T(8,128)(2,1)S(1)}, u32[]{:S(2)}, u32[]{:S(2)}) %collective-permute-start.8) | collective-permute-done | bytes 262176 | tf_op jit(solution)/shard_map/ppermute | solution.py:500
  123.8 3.1 %collective-permute-start.12 = (bf16[512,512]{1,0:T(8,128)(2,1)S(1)}, bf16[512,512]{1,0:T(8,128)(2,1)S(1)}, u32[]{:S(2)}, u32[]{:S(2)}) collective-permute-start(bf16[512,512]{1,0:T(8,128)(2,1)S(1)} %maximum_select_fusion.refs_1_), channel_id=1, source_target_pairs={{0,1},{1,0},{2,3},{3,2},{4,5},{5,4},{6,7},{7,6},{8,9},{9,8},{10,11... | collective-permute-start | bytes 1572872 | tf_op jit(solution)/shard_map/ppermute | solution.py:500
  126.8 4.2 %all-to-all-start.4 = ((bf16[16,16,512]{2,1,0:T(8,128)(2,1)}), bf16[16,16,512]{2,1,0:T(8,128)(2,1)}, u32[]{:S(2)}, u32[]{:S(2)}) async-start(bf16[16,16,512]{2,1,0:T(8,128)(2,1)} %bitcast.44), calls=%async_computation.4 | async-start | bytes 524288 | tf_op jit(solution)/shard_map/all_to_all | solution.py:535
  131.6 1.0 shard_map.190
  132.8 0.9 collective-permute-done.14.refs_4_
  133.7 2.6 %shard_map.191 = (bf16[1024,512]{1,0:T(8,128)(2,1)}, bf16[512,512]{1,0:T(8,128)(2,1)}) custom-call(s32[1]{0:T(128)} %bitcast.refs_0_, bf16[384,512]{1,0:T(8,128)(2,1)} %copy-done.2, bf16[384,512]{1,0:T(8,128)(2,1)} %collective-permute-done.10.refs_2_, bf16[384,512]{1,0:T(8,128)(2,1)} %copy-done.6, bf16[384,512]{1,0:T(8,128)(2,1)} %collective-permute-done.14.refs_4_, ...), custom_call_target="tpu_custom_call" | custom-call | flops 1 | bytes 1 | tf_op jit(solution)/shard_map/pallas_call | solution.py:480
  136.3 7.3 %all-to-all-done.4 = bf16[16,16,512]{2,1,0:T(8,128)(2,1)} async-done(((bf16[16,16,512]{2,1,0:T(8,128)(2,1)}), bf16[16,16,512]{2,1,0:T(8,128)(2,1)}, u32[]{:S(2)}, u32[]{:S(2)}) %all-to-all-start.4) | async-done | bytes 262176 | tf_op jit(solution)/shard_map/all_to_all | solution.py:535
  143.9 1.9 %add_add_fusion = f32[128,512]{1,0:T(8,128)} fusion(f32[128,512]{1,0:T(8,128)S(1)} %copy-done.7, f32[128,512]{1,0:T(8,128)S(1)} %copy-done.8, bf16[256,512]{1,0:T(8,128)(2,1)} %bitcast.25, s32[256]{0:T(256)S(1)} %eq.32), kind=kOutput, calls=%fused_computation.16 | convolution fusion | flops 33783808 | bytes 1049600 | tf_op jit(solution)/shard_map/dot_general | solution.py:20
  145.9 1.0 shard_map.192
  (44 shorter events, 2.9 us)
Async XLA Ops:
  17.2 13.6 %all-to-all-start.1 = ((bf16[16,16,512]{2,1,0:T(8,128)(2,1)}), bf16[16,16,512]{2,1,0:T(8,128)(2,1)S(1)}, u32[]{:S(2)}, u32[]{:S(2)}) async-start(bf16[16,16,512]{2,1,0:T(8,128)(2,1)} %convolution_convert_fusion), calls=%async_computation.1 | async-start | bytes 524288 | tf_op jit(solution)/shard_map/all_to_all | solution.py:535
  30.8 0.7 copy-start.4
  35.8 14.4 %all-to-all-start.2 = ((bf16[16,16,512]{2,1,0:T(8,128)(2,1)}), bf16[16,16,512]{2,1,0:T(8,128)(2,1)S(1)}, u32[]{:S(2)}, u32[]{:S(2)}) async-start(bf16[16,16,512]{2,1,0:T(8,128)(2,1)} %bitcast.48), calls=%async_computation.2 | async-start | bytes 524288 | tf_op jit(solution)/shard_map/all_to_all | solution.py:535
  50.2 0.7 copy-start.5
  56.2 4.3 %collective-permute-start = (bf16[768,512]{1,0:T(8,128)(2,1)}, bf16[768,512]{1,0:T(8,128)(2,1)S(1)}, u32[]{:S(2)}, u32[]{:S(2)}) collective-permute-start(bf16[768,512]{1,0:T(8,128)(2,1)} %get-tuple-element.97.refs_7_), channel_id=1, source_target_pairs={{0,1},{1,0},{2,3},{3,2},{4,5},{5,4},{6,7},{7,6},{8,9},{9,8},{10,11... | collective-permute-start | bytes 2359304 | tf_op jit(solution)/shard_map/ppermute | solution.py:500
  56.9 12.9 %all-to-all-start.3 = ((bf16[16,16,512]{2,1,0:T(8,128)(2,1)}), bf16[16,16,512]{2,1,0:T(8,128)(2,1)S(1)}, u32[]{:S(2)}, u32[]{:S(2)}) async-start(bf16[16,16,512]{2,1,0:T(8,128)(2,1)} %bitcast.51), calls=%async_computation.3 | async-start | bytes 524288 | tf_op jit(solution)/shard_map/all_to_all | solution.py:535
  61.9 14.0 %collective-permute-start.1 = (bf16[384,512]{1,0:T(8,128)(2,1)S(1)}, bf16[384,512]{1,0:T(8,128)(2,1)S(1)}, u32[]{:S(2)}, u32[]{:S(2)}) collective-permute-start(bf16[384,512]{1,0:T(8,128)(2,1)S(1)} %get-tuple-element.164), channel_id=1, source_target_pairs={{0,2},{1,3},{2,0},{3,1},{4,6},{5,7},{6,4},{7,5},{8,10},{9,11},{10,... | collective-permute-start | bytes 1179656 | tf_op jit(solution)/shard_map/ppermute | solution.py:500
  69.7 0.7 copy-start.3
  75.9 5.7 %collective-permute-start.2 = (bf16[1024,512]{1,0:T(8,128)(2,1)}, bf16[1024,512]{1,0:T(8,128)(2,1)S(1)}, u32[]{:S(2)}, u32[]{:S(2)}) collective-permute-start(bf16[1024,512]{1,0:T(8,128)(2,1)} %get-tuple-element.117.refs_12_), channel_id=1, source_target_pairs={{0,1},{1,0},{2,3},{3,2},{4,5},{5,4},{6,7},{7,6},{8,9},{9,8},{10,11... | collective-permute-start | bytes 3145736 | tf_op jit(solution)/shard_map/ppermute | solution.py:500
  76.7 6.7 %collective-permute-start.4 = (bf16[192,512]{1,0:T(8,128)(2,1)S(1)}, bf16[192,512]{1,0:T(8,128)(2,1)S(1)}, u32[]{:S(2)}, u32[]{:S(2)}) collective-permute-start(bf16[192,512]{1,0:T(8,128)(2,1)S(1)} %fusion.2), channel_id=1, source_target_pairs={{0,4},{1,5},{2,6},{3,7},{4,0},{5,1},{6,2},{7,3},{8,12},{9,13},{10,... | collective-permute-start | bytes 589832 | tf_op jit(solution)/shard_map/ppermute | solution.py:500
  82.7 12.8 %collective-permute-start.3 = (bf16[512,512]{1,0:T(8,128)(2,1)S(1)}, bf16[512,512]{1,0:T(8,128)(2,1)S(1)}, u32[]{:S(2)}, u32[]{:S(2)}) collective-permute-start(bf16[512,512]{1,0:T(8,128)(2,1)S(1)} %add_convert_fusion.3), channel_id=1, source_target_pairs={{0,2},{1,3},{2,0},{3,1},{4,6},{5,7},{6,4},{7,5},{8,10},{9,11},{10,... | collective-permute-start | bytes 1572872 | tf_op jit(solution)/shard_map/ppermute | solution.py:500
  83.5 11.4 %collective-permute-start.5 = (bf16[192,512]{1,0:T(8,128)(2,1)S(1)}, bf16[192,512]{1,0:T(8,128)(2,1)S(1)}, u32[]{:S(2)}, u32[]{:S(2)}) collective-permute-start(bf16[192,512]{1,0:T(8,128)(2,1)S(1)} %fusion.1), channel_id=1, source_target_pairs={{0,8},{1,9},{2,10},{3,11},{4,12},{5,13},{6,14},{7,15},{8,0},{9,1},... | collective-permute-start | bytes 589832 | tf_op jit(solution)/shard_map/ppermute | solution.py:500
  85.1 4.0 %copy-start.1 = (bf16[1024,512]{1,0:T(8,128)(2,1)S(1)}, bf16[1024,512]{1,0:T(8,128)(2,1)}, u32[]{:S(2)}) copy-start(bf16[1024,512]{1,0:T(8,128)(2,1)} %shard_map.187.refs_7_) | copy-start | bytes 3145732
  95.7 7.2 %collective-permute-start.6 = (bf16[256,512]{1,0:T(8,128)(2,1)S(1)}, bf16[256,512]{1,0:T(8,128)(2,1)S(1)}, u32[]{:S(2)}, u32[]{:S(2)}) collective-permute-start(bf16[256,512]{1,0:T(8,128)(2,1)S(1)} %dynamic-slice_bitcast_fusion.2), channel_id=1, source_target_pairs={{0,4},{1,5},{2,6},{3,7},{4,0},{5,1},{6,2},{7,3},{8,12},{9,13},{10,... | collective-permute-start | bytes 786440 | tf_op jit(solution)/shard_map/ppermute | solution.py:500
  103.0 4.6 %collective-permute-start.9 = (bf16[192,512]{1,0:T(8,128)(2,1)S(1)}, bf16[192,512]{1,0:T(8,128)(2,1)S(1)}, u32[]{:S(2)}, u32[]{:S(2)}) collective-permute-start(bf16[192,512]{1,0:T(8,128)(2,1)S(1)} %add_convert_fusion.5), channel_id=1, source_target_pairs={{0,4},{1,5},{2,6},{3,7},{4,0},{5,1},{6,2},{7,3},{8,12},{9,13},{10,... | collective-permute-start | bytes 589832 | tf_op jit(solution)/shard_map/ppermute | solution.py:500
  104.5 13.2 %collective-permute-start.7 = (bf16[256,512]{1,0:T(8,128)(2,1)S(1)}, bf16[256,512]{1,0:T(8,128)(2,1)S(1)}, u32[]{:S(2)}, u32[]{:S(2)}) collective-permute-start(bf16[256,512]{1,0:T(8,128)(2,1)S(1)} %fusion), channel_id=1, source_target_pairs={{0,8},{1,9},{2,10},{3,11},{4,12},{5,13},{6,14},{7,15},{8,0},{9,1},... | collective-permute-start | bytes 786440 | tf_op jit(solution)/shard_map/ppermute | solution.py:500
  105.2 26.3 %copy-start = (f32[768,512]{1,0:T(8,128)S(1)}, f32[768,512]{1,0:T(8,128)}, u32[]{:S(2)}) copy-start(f32[768,512]{1,0:T(8,128)} %shard_map.189.refs_3_) | copy-start | bytes 4718596
  107.7 24.9 %copy-start.2 = (bf16[384,512]{1,0:T(8,128)(2,1)}, bf16[384,512]{1,0:T(8,128)(2,1)S(1)}, u32[]{:S(2)}) copy-start(bf16[384,512]{1,0:T(8,128)(2,1)S(1)} %maximum_select_fusion.1.refs_1_) | copy-start | bytes 1179652
  107.7 15.8 %collective-permute-start.10 = (bf16[384,512]{1,0:T(8,128)(2,1)S(1)}, bf16[384,512]{1,0:T(8,128)(2,1)}, u32[]{:S(2)}, u32[]{:S(2)}) collective-permute-start(bf16[384,512]{1,0:T(8,128)(2,1)S(1)} %maximum_select_fusion.1.refs_1_), channel_id=1, source_target_pairs={{0,2},{1,3},{2,0},{3,1},{4,6},{5,7},{6,4},{7,5},{8,10},{9,11},{10,... | collective-permute-start | bytes 1179656 | tf_op jit(solution)/shard_map/ppermute | solution.py:500
  117.8 5.8 %collective-permute-start.8 = (bf16[256,512]{1,0:T(8,128)(2,1)S(1)}, bf16[256,512]{1,0:T(8,128)(2,1)S(1)}, u32[]{:S(2)}, u32[]{:S(2)}) collective-permute-start(bf16[256,512]{1,0:T(8,128)(2,1)S(1)} %add_convert_fusion.4), channel_id=1, source_target_pairs={{0,4},{1,5},{2,6},{3,7},{4,0},{5,1},{6,2},{7,3},{8,12},{9,13},{10,... | collective-permute-start | bytes 786440 | tf_op jit(solution)/shard_map/ppermute | solution.py:500
  123.8 7.8 %collective-permute-start.12 = (bf16[512,512]{1,0:T(8,128)(2,1)S(1)}, bf16[512,512]{1,0:T(8,128)(2,1)S(1)}, u32[]{:S(2)}, u32[]{:S(2)}) collective-permute-start(bf16[512,512]{1,0:T(8,128)(2,1)S(1)} %maximum_select_fusion.refs_1_), channel_id=1, source_target_pairs={{0,1},{1,0},{2,3},{3,2},{4,5},{5,4},{6,7},{7,6},{8,9},{9,8},{10,11... | collective-permute-start | bytes 1572872 | tf_op jit(solution)/shard_map/ppermute | solution.py:500
  126.8 16.7 %collective-permute-start.11 = (bf16[512,512]{1,0:T(8,128)(2,1)S(1)}, bf16[512,512]{1,0:T(8,128)(2,1)S(1)}, u32[]{:S(2)}, u32[]{:S(2)}) collective-permute-start(bf16[512,512]{1,0:T(8,128)(2,1)S(1)} %maximum_select_fusion.refs_1_), channel_id=1, source_target_pairs={{0,2},{1,3},{2,0},{3,1},{4,6},{5,7},{6,4},{7,5},{8,10},{9,11},{10,... | collective-permute-start | bytes 1572872 | tf_op jit(solution)/shard_map/ppermute | solution.py:500
  126.8 16.7 %all-to-all-start.4 = ((bf16[16,16,512]{2,1,0:T(8,128)(2,1)}), bf16[16,16,512]{2,1,0:T(8,128)(2,1)}, u32[]{:S(2)}, u32[]{:S(2)}) async-start(bf16[16,16,512]{2,1,0:T(8,128)(2,1)} %bitcast.44), calls=%async_computation.4 | async-start | bytes 524288 | tf_op jit(solution)/shard_map/all_to_all | solution.py:535
  131.0 1.8 %collective-permute-start.13 = (bf16[384,512]{1,0:T(8,128)(2,1)S(1)}, bf16[384,512]{1,0:T(8,128)(2,1)S(1)}, u32[]{:S(2)}, u32[]{:S(2)}) collective-permute-start(bf16[384,512]{1,0:T(8,128)(2,1)S(1)} %maximum_select_fusion.1.refs_1_), channel_id=1, source_target_pairs={{0,1},{1,0},{2,3},{3,2},{4,5},{5,4},{6,7},{7,6},{8,9},{9,8},{10,11... | collective-permute-start | bytes 1179656 | tf_op jit(solution)/shard_map/ppermute | solution.py:500
  131.2 2.4 %collective-permute-start.14 = (bf16[384,512]{1,0:T(8,128)(2,1)}, bf16[384,512]{1,0:T(8,128)(2,1)}, u32[]{:S(2)}, u32[]{:S(2)}) collective-permute-start(bf16[384,512]{1,0:T(8,128)(2,1)} %collective-permute-done.10.refs_2_), channel_id=1, source_target_pairs={{0,1},{1,0},{2,3},{3,2},{4,5},{5,4},{6,7},{7,6},{8,9},{9,8},{10,11... | collective-permute-start | bytes 1179656 | tf_op jit(solution)/shard_map/ppermute | solution.py:500
  132.6 11.3 %copy-start.7 = (f32[128,512]{1,0:T(8,128)S(1)}, f32[128,512]{1,0:T(8,128)}, u32[]{:S(2)}) copy-start(f32[128,512]{1,0:T(8,128)} %get-tuple-element.152) | copy-start | bytes 786436
  132.6 11.3 %copy-start.8 = (f32[128,512]{1,0:T(8,128)S(1)}, f32[128,512]{1,0:T(8,128)}, u32[]{:S(2)}) copy-start(f32[128,512]{1,0:T(8,128)} %get-tuple-element.153) | copy-start | bytes 786436
  132.8 0.9 copy-start.6
  143.5 2.4 %collective-permute-start.15 = (bf16[512,512]{1,0:T(8,128)(2,1)S(1)}, bf16[512,512]{1,0:T(8,128)(2,1)S(1)}, u32[]{:S(2)}, u32[]{:S(2)}) collective-permute-start(bf16[512,512]{1,0:T(8,128)(2,1)S(1)} %collective-permute-done.11.refs_1_), channel_id=1, source_target_pairs={{0,1},{1,0},{2,3},{3,2},{4,5},{5,4},{6,7},{7,6},{8,9},{9,8},{10,11... | collective-permute-start | bytes 1572872 | tf_op jit(solution)/shard_map/ppermute | solution.py:500

commit v17 on v16

--- a/solution.py
+++ b/solution.py
@@ -90,6 +90,20 @@
     rank_marks = jnp.where(rank == iota((rank.shape[0], slots), 1).astype(F32), 1.0, 0.0)
     wanted = (rank_marks * to_column(remote_ref[...])).astype(BF16)
     ask_ref[...] = dot_rows(dest_marks, wanted).astype(jnp.int32)
+
+
+def reply_kernel(asked_ref, nodes_ref, reply_ref, asked_marks_ref):
+    domains, slots = asked_ref.shape
+    total = domains * slots
+    shift = slots.bit_length() - 1
+    spread = marks((iota((total, domains), 0) >> shift) == iota((total, domains), 1))
+    listed = dot(spread, asked_ref[...].astype(F32).astype(BF16))
+    at_slot = (iota((total, slots), 0) & (slots - 1)) == iota((total, slots), 1)
+    column = jnp.sum(jnp.where(at_slot, listed, 0.0), axis=1, keepdims=True)
+    node_rows = nodes_ref.shape[0]
+    asked_marks = marks(column == iota((total, node_rows), 1).astype(F32))
+    asked_marks_ref[...] = asked_marks
+    reply_ref[...] = dot(asked_marks, nodes_ref[...]).astype(BF16)
 
 
 def cut_marks_kernel(dest_ref, local_ref, senders_ref, receivers_ref, *, domains, slots):
@@ -568,12 +582,12 @@
         [shaped(BF16, cut_rows, table)] * 2,
         [cut_dest.reshape(1, -1), cut_local.reshape(1, -1)],
     )
-    asked_marks = jnp.where(
-        asked[:, :, None] == jnp.arange(node_rows, dtype=jnp.int32)[None, None], 1.0, 0.0
-    ).astype(BF16)
-    reply = lax.dot_general(asked_marks, nodes, (((2,), (0,)), ((), ())), preferred_element_type=F32)
-    reply = reply.astype(BF16).reshape(total_slots, latent)
-    asked_marks = asked_marks.reshape(total_slots, node_rows)
+    reply, asked_marks = line.run(
+        reply_kernel,
+        [shaped(BF16, total_slots, latent), shaped(BF16, total_slots, node_rows)],
+        [asked, nodes],
+        limit=2**22,
+    )
     far = exchange(reply, domains)
 
     block = cut_rows

time: 148 us -> 149 us (level)
  blocking collectives: 13 us -> 0 us
  waiting for transfers between devices: 42.9 us -> 50.6 us
  starting transfers between devices: 30 us -> 36.6 us
  matrix products: 3.82 us -> 1.86 us
  local copies, waits for them, and re-layouts: 2.81 us -> 4.69 us
    all_to_all x1 -> x0, blocking collectives: 13 us -> none  [shards(): asked = lax.all_to_all(ask, 'dom', split_axis=0, concat_axis=0, tiled=True)]
    all_to_all x0 -> x1, starting transfers between devices: none -> 7.32 us  [shards(): asked = lax.all_to_all(ask, 'dom', split_axis=0, concat_axis=0, tiled=True)]
    all_to_all x4, waiting for transfers between devices: 16.4 us -> 20.4 us  [exchange(): lax.all_to_all(split, 'dom', split_axis=0, concat_axis=0, tiled=True)]
    all_to_all x0 -> x1, waiting for transfers between devices: none -> 3.67 us  [shards(): asked = lax.all_to_all(ask, 'dom', split_axis=0, concat_axis=0, tiled=True)]
    unnamed x18 -> x26, local copies, waits for them, and re-layouts: 2.13 us -> 4.6 us
    dot_general x1 -> x0, matrix products: 1.87 us -> none  [shards(): lax.dot_general(asked_marks, nodes, (((2,), (0,)), ((), ())), preferred_e...]
    pallas_call x14 -> x15, Pallas kernels: 48.6 us -> 49.7 us  [run(): pl.pallas_call(ordered, out_shape=out_shape, in_specs=specs, out_specs=[V...]
  transfers between devices with their start and end apart: 20 -> 21, of which waited for: 12 -> 13; matrix products, arithmetic and copies ran while one was open for 5% -> 3% of each run, Pallas kernels for 25% -> 24%
where the time goes in v17:
time: 149 us; the launch traced here: 148 us
  waiting for transfers between devices  50.6 us (34%)
  Pallas kernels  49.7 us (33%)
  starting transfers between devices  36.6 us (25%)
  local copies, waits for them, and re-layouts  4.69 us (3%)
  other arithmetic  3.45 us (2%)
  matrix products  1.86 us (1%)
    pallas_call x15, Pallas kernels, run(): pl.pallas_call(ordered, out_shape=out_shape, in_specs=specs, out_specs=[V...  49.7 us
    ppermute x16, waiting for transfers between devices, across(): lax.ppermute(rows, 'dom', [(device, device ^ mask) for device in range(de...  26.5 us
    all_to_all x4, waiting for transfers between devices, exchange(): lax.all_to_all(split, 'dom', split_axis=0, concat_axis=0, tiled=True)  20.4 us
    all_to_all x4, starting transfers between devices, exchange(): lax.all_to_all(split, 'dom', split_axis=0, concat_axis=0, tiled=True)  15.9 us
    ppermute x16, starting transfers between devices, across(): lax.ppermute(rows, 'dom', [(device, device ^ mask) for device in range(de...  13.4 us
    all_to_all x1, starting transfers between devices, shards(): asked = lax.all_to_all(ask, 'dom', split_axis=0, concat_axis=0, tiled=True)  7.32 us
    unnamed x26, local copies, waits for them, and re-layouts  4.6 us
    all_to_all x1, waiting for transfers between devices, shards(): asked = lax.all_to_all(ask, 'dom', split_axis=0, concat_axis=0, tiled=True)  3.67 us
  transfers between devices with their start and end apart: 21, of which 13 were waited for; matrix products, arithmetic and copies ran while one was open for 3% of the time, Pallas kernels for 24%

profile of v17, /device:TPU:1, one launch (start us, length us, event | category | flops | bytes accessed | tf_op | source)
XLA Modules:
  0.0 147.9 jit_solution(7510461653171221828)
XLA Ops:
  0.6 1.7 %shard_map.179.refs_2_ = s32[16,16]{1,0:T(8,128)} custom-call(s32[1,128]{1,0:T(1,128)} %bitcast.53, s32[1,128]{1,0:T(1,128)} %bitcast.56), custom_call_target="tpu_custom_call" | custom-call | flops 1 | bytes 1 | tf_op jit(solution)/shard_map/pallas_call | solution.py:494
  2.3 7.3 %all-to-all-start = ((s32[16,1,16]{2,1,0:T(1,128)}), s32[16,1,16]{2,1,0:T(1,128)S(1)}, u32[]{:S(2)}, u32[]{:S(2)}) async-start(s32[16,1,16]{2,1,0:T(1,128)} %bitcast.52), calls=%async_computation | async-start | bytes 16384 | tf_op jit(solution)/shard_map/all_to_all | solution.py:579
  9.7 2.0 %shard_map.180 = (bf16[256,384]{1,0:T(8,128)(2,1)}, bf16[256,384]{1,0:T(8,128)(2,1)}) custom-call(s32[1,128]{1,0:T(1,128)} %bitcast.54, s32[1,128]{1,0:T(1,128)} %bitcast.57, s32[16,16]{1,0:T(8,128)} %shard_map.179.refs_2_), custom_call_target="tpu_custom_call" | custom-call | flops 1 | bytes 1 | tf_op jit(solution)/shard_map/pallas_call | solution.py:494
  11.7 3.7 %all-to-all-done = s32[16,1,16]{2,1,0:T(1,128)S(1)} async-done(((s32[16,1,16]{2,1,0:T(1,128)}), s32[16,1,16]{2,1,0:T(1,128)S(1)}, u32[]{:S(2)}, u32[]{:S(2)}) %all-to-all-start) | async-done | bytes 1056 | tf_op jit(solution)/shard_map/all_to_all | solution.py:579
  15.4 0.9 copy-done.1
  16.3 0.9 copy-done.2
  17.2 1.1 shard_map.181
  18.9 4.0 %all-to-all-start.1 = ((bf16[16,16,512]{2,1,0:T(8,128)(2,1)}), bf16[16,16,512]{2,1,0:T(8,128)(2,1)S(1)}, u32[]{:S(2)}, u32[]{:S(2)}) async-start(bf16[16,16,512]{2,1,0:T(8,128)(2,1)} %bitcast.7), calls=%async_computation.1 | async-start | bytes 524288 | tf_op jit(solution)/shard_map/all_to_all | solution.py:549
  23.0 6.3 %shard_map.182 = (bf16[512,128]{1,0:T(8,128)(2,1)}, bf16[512,128]{1,0:T(8,128)(2,1)}, bf16[512,512]{1,0:T(8,128)(2,1)}, bf16[512,512]{1,0:T(8,128)(2,1)}, bf16[5...) custom-call(s32[2,256]{1,0:T(2,128)} %bitcast.55, ...), custom_call_target="tpu_custom_call" | custom-call | flops 1 | bytes 1 | tf_op jit(solution)/shard_map/pallas_call | solution.py:494
  29.2 3.3 %all-to-all-done.1 = bf16[16,16,512]{2,1,0:T(8,128)(2,1)S(1)} async-done(((bf16[16,16,512]{2,1,0:T(8,128)(2,1)}), bf16[16,16,512]{2,1,0:T(8,128)(2,1)S(1)}, u32[]{:S(2)}, u32[]{:S(2)}) %all-to-all-start.1) | async-done | bytes 262176 | tf_op jit(solution)/shard_map/all_to_all | solution.py:549
  32.5 0.7 copy-done.8
  33.2 4.3 %shard_map.183 = (bf16[256,512]{1,0:T(8,128)(2,1)}, bf16[256,512]{1,0:T(8,128)(2,1)}, bf16[256,512]{1,0:T(8,128)(2,1)}, f32[256,512]{1,0:T(8,128)}, f32[256,512]...) custom-call(bf16[256,384]{1,0:T(8,128)(2,1)} %get-tuple-element.88.refs_0_.refs_2_, ...), custom_call_target="tpu_custom_call" | custom-call | flops 1 | bytes 1 | tf_op jit(solution)/shard_map/pallas_call | solution.py:494
  37.5 4.0 %all-to-all-start.2 = ((bf16[16,16,512]{2,1,0:T(8,128)(2,1)}), bf16[16,16,512]{2,1,0:T(8,128)(2,1)S(1)}, u32[]{:S(2)}, u32[]{:S(2)}) async-start(bf16[16,16,512]{2,1,0:T(8,128)(2,1)} %bitcast.48), calls=%async_computation.2 | async-start | bytes 524288 | tf_op jit(solution)/shard_map/all_to_all | solution.py:549
  41.5 2.7 %shard_map.184.refs_8_ = bf16[768,512]{1,0:T(8,128)(2,1)} custom-call(bf16[768,512]{1,0:T(8,128)(2,1)} %refs_3_.6, f32[512,512]{1,0:T(8,128)} %get-tuple-element.95.refs_1_.refs_3_, f32[256,512]{1,0:T(8,128)} %get-tuple-element.96.refs_2_.refs_5_, bf16[256,512]{1,0:T(8,128)(2,1)} %get-tuple-element.93.refs_3_), custom_call_target="tpu_custom_call" | custom-call | flops 1 | bytes 1 | tf_op jit(solution)/shard_map/pallas_call | solution.py:494
  44.2 6.9 %all-to-all-done.2 = bf16[16,16,512]{2,1,0:T(8,128)(2,1)S(1)} async-done(((bf16[16,16,512]{2,1,0:T(8,128)(2,1)}), bf16[16,16,512]{2,1,0:T(8,128)(2,1)S(1)}, u32[]{:S(2)}, u32[]{:S(2)}) %all-to-all-start.2) | async-done | bytes 262176 | tf_op jit(solution)/shard_map/all_to_all | solution.py:549
  51.1 0.7 copy-done.9
  51.8 5.4 %shard_map.185 = (bf16[128,512]{1,0:T(8,128)(2,1)}, f32[128,512]{1,0:T(8,128)}, bf16[128,512]{1,0:T(8,128)(2,1)}, bf16[256,512]{1,0:T(8,128)(2,1)}, bf16[768,512]{1,0:T(8,128)(2,1)}, /*index=5*/bf16[768,512]{1,0:T(8,128)(2,1)}) custom-call(s32[1]{0:T(128)} %bitcast.refs_0_, bf16[256,512]{1,0:T(8,128)(2,1)} %bitcast.47, bf16[256,128]{1,0:T(8,128)(2,1)} %copy-done.3, ...), custom_call_target="tpu_custom_call" | custom-call | flops 1 | bytes 1 | tf_op jit(solution)/shard_map/pallas_call | solution.py:494
  57.1 0.7 collective-permute-start
  57.8 3.6 %all-to-all-start.3 = ((bf16[16,16,512]{2,1,0:T(8,128)(2,1)}), bf16[16,16,512]{2,1,0:T(8,128)(2,1)S(1)}, u32[]{:S(2)}, u32[]{:S(2)}) async-start(bf16[16,16,512]{2,1,0:T(8,128)(2,1)} %bitcast.51), calls=%async_computation.3 | async-start | bytes 524288 | tf_op jit(solution)/shard_map/all_to_all | solution.py:549
  61.4 1.3 add_convert_fusion
  62.9 1.2 collective-permute-start.1
  64.0 3.6 %shard_map.186 = (bf16[512,512]{1,0:T(8,128)(2,1)}, bf16[512,512]{1,0:T(8,128)(2,1)}) custom-call(bf16[512,128]{1,0:T(8,128)(2,1)} %get-tuple-element.102.refs_0_.refs_1_, bf16[128,512]{1,0:T(8,128)(2,1)} %get-tuple-element.98.refs_1_.refs_2_, bf16[768,512]{1,0:T(8,128)(2,1)} %refs_0_.3, f32[512,512]{1,0:T(8,128)} %get-tuple-element.95.refs_1_.refs_3_, ...), custom_call_target="tpu_custom_call" | custom-call | flops 1 | bytes 1 | tf_op jit(solution)/shard_map/pallas_call | solution.py:494
  67.6 3.0 %all-to-all-done.3 = bf16[16,16,512]{2,1,0:T(8,128)(2,1)S(1)} async-done(((bf16[16,16,512]{2,1,0:T(8,128)(2,1)}), bf16[16,16,512]{2,1,0:T(8,128)(2,1)S(1)}, u32[]{:S(2)}, u32[]{:S(2)}) %all-to-all-start.3) | async-done | bytes 262176 | tf_op jit(solution)/shard_map/all_to_all | solution.py:549
  70.7 0.7 copy-done.7
  71.4 5.4 %shard_map.187 = (bf16[256,512]{1,0:T(8,128)(2,1)}, bf16[256,512]{1,0:T(8,128)(2,1)}, bf16[1024,512]{1,0:T(8,128)(2,1)}) custom-call(s32[1]{0:T(128)} %bitcast.refs_0_, bf16[256,384]{1,0:T(8,128)(2,1)} %get-tuple-element.89.refs_2_.refs_1_.refs_3_, bf16[128,512]{1,0:T(8,128)(2,1)} %get-tuple-element.98.refs_1_.refs_2_, bf16[256,512]{1,0:T(8,128)(2,1)} %bitcast.45, ...), custom_call_target="tpu_custom_call" | custom-call | flops 1 | bytes 1 | tf_op jit(solution)/shard_map/pallas_call | solution.py:494
  76.8 0.8 collective-permute-start.2
  77.7 4.7 %shard_map.188.refs_7_ = bf16[1024,512]{1,0:T(8,128)(2,1)} custom-call(s32[1]{0:T(128)} %bitcast.refs_0_, bf16[256,512]{1,0:T(8,128)(2,1)} %get-tuple-element.119.refs_1_, bf16[256,512]{1,0:T(8,128)(2,1)} %get-tuple-element.138.refs_2_.refs_5_, bf16[768,512]{1,0:T(8,128)(2,1)} %refs_3_.6, bf16[512,512]{1,0:T(8,128)(2,1)} %get-tuple-element.109.refs_10_.refs_4_, ...), custom_call_target="tpu_custom_call" | custom-call | flops 1 | bytes 1 | tf_op jit(solution)/shard_map/pallas_call | solution.py:494
  82.5 1.2 add_convert_fusion.3
  83.7 0.7 collective-permute-start.3
  84.5 1.6 %collective-permute-start.5 = (bf16[192,512]{1,0:T(8,128)(2,1)S(1)}, bf16[192,512]{1,0:T(8,128)(2,1)S(1)}, u32[]{:S(2)}, u32[]{:S(2)}) collective-permute-start(bf16[192,512]{1,0:T(8,128)(2,1)S(1)} %fusion.1), channel_id=1, source_target_pairs={{0,8},{1,9},{2,10},{3,11},{4,12},{5,13},{6,14},{7,15},{8,0},{9,1},... | collective-permute-start | bytes 589832 | tf_op jit(solution)/shard_map/ppermute | solution.py:514
  86.0 3.9 %shard_map.189 = (f32[128,512]{1,0:T(8,128)}, bf16[256,512]{1,0:T(8,128)(2,1)}) custom-call(bf16[512,128]{1,0:T(8,128)(2,1)} %get-tuple-element.132.refs_0_, bf16[512,128]{1,0:T(8,128)(2,1)} %get-tuple-element.102.refs_0_.refs_1_, bf16[256,384]{1,0:T(8,128)(2,1)} %get-tuple-element.88.refs_0_.refs_2_, ...), custom_call_target="tpu_custom_call" | custom-call | flops 1 | bytes 1 | tf_op jit(solution)/shard_map/pallas_call | solution.py:494
  90.1 5.7 %collective-permute-done.5 = bf16[192,512]{1,0:T(8,128)(2,1)S(1)} collective-permute-done((bf16[192,512]{1,0:T(8,128)(2,1)S(1)}, bf16[192,512]{1,0:T(8,128)(2,1)S(1)}, u32[]{:S(2)}, u32[]{:S(2)}) %collective-permute-start.5) | collective-permute-done | bytes 196640 | tf_op jit(solution)/shard_map/ppermute | solution.py:514
  96.6 2.0 %collective-permute-start.6 = (bf16[256,512]{1,0:T(8,128)(2,1)S(1)}, bf16[256,512]{1,0:T(8,128)(2,1)S(1)}, u32[]{:S(2)}, u32[]{:S(2)}) collective-permute-start(bf16[256,512]{1,0:T(8,128)(2,1)S(1)} %dynamic-slice_bitcast_fusion.2), channel_id=1, source_target_pairs={{0,4},{1,5},{2,6},{3,7},{4,0},{5,1},{6,2},{7,3},{8,12},{9,13},{10,... | collective-permute-start | bytes 786440 | tf_op jit(solution)/shard_map/ppermute | solution.py:514
  98.6 3.9 %shard_map.190.refs_3_ = f32[768,512]{1,0:T(8,128)} custom-call(bf16[768,512]{1,0:T(8,128)(2,1)} %refs_0_.3, bf16[512,512]{1,0:T(8,128)(2,1)} %get-tuple-element.137.refs_17_.refs_18_.refs_11_.refs_4_.refs_1_, bf16[256,512]{1,0:T(8,128)(2,1)} %get-tuple-element.138.refs_2_.refs_5_, bf16[1536,512]{1,0:T(8,128)(2,1)} %refs_3_.7, ...), custom_call_target="tpu_custom_call" | custom-call | flops 1 | bytes 1 | tf_op jit(solution)/shard_map/pallas_call | solution.py:494
  102.5 1.3 collective-permute-done.6
  103.9 1.5 %collective-permute-start.9 = (bf16[192,512]{1,0:T(8,128)(2,1)S(1)}, bf16[192,512]{1,0:T(8,128)(2,1)S(1)}, u32[]{:S(2)}, u32[]{:S(2)}) collective-permute-start(bf16[192,512]{1,0:T(8,128)(2,1)S(1)} %add_convert_fusion.5), channel_id=1, source_target_pairs={{0,4},{1,5},{2,6},{3,7},{4,0},{5,1},{6,2},{7,3},{8,12},{9,13},{10,... | collective-permute-start | bytes 589832 | tf_op jit(solution)/shard_map/ppermute | solution.py:514
  105.4 0.8 collective-permute-start.7
  106.2 2.3 %collective-permute-done.9 = bf16[192,512]{1,0:T(8,128)(2,1)S(1)} collective-permute-done((bf16[192,512]{1,0:T(8,128)(2,1)S(1)}, bf16[192,512]{1,0:T(8,128)(2,1)S(1)}, u32[]{:S(2)}, u32[]{:S(2)}) %collective-permute-start.9) | collective-permute-done | bytes 196640 | tf_op jit(solution)/shard_map/ppermute | solution.py:514
  108.7 9.9 %collective-permute-done.7 = bf16[256,512]{1,0:T(8,128)(2,1)S(1)} collective-permute-done((bf16[256,512]{1,0:T(8,128)(2,1)S(1)}, bf16[256,512]{1,0:T(8,128)(2,1)S(1)}, u32[]{:S(2)}, u32[]{:S(2)}) %collective-permute-start.7) | collective-permute-done | bytes 262176 | tf_op jit(solution)/shard_map/ppermute | solution.py:514
  118.7 5.7 %collective-permute-done.8 = bf16[256,512]{1,0:T(8,128)(2,1)S(1)} collective-permute-done((bf16[256,512]{1,0:T(8,128)(2,1)S(1)}, bf16[256,512]{1,0:T(8,128)(2,1)S(1)}, u32[]{:S(2)}, u32[]{:S(2)}) %collective-permute-start.8) | collective-permute-done | bytes 262176 | tf_op jit(solution)/shard_map/ppermute | solution.py:514
  124.7 3.1 %collective-permute-start.12 = (bf16[512,512]{1,0:T(8,128)(2,1)S(1)}, bf16[512,512]{1,0:T(8,128)(2,1)S(1)}, u32[]{:S(2)}, u32[]{:S(2)}) collective-permute-start(bf16[512,512]{1,0:T(8,128)(2,1)S(1)} %maximum_select_fusion.refs_1_), channel_id=1, source_target_pairs={{0,1},{1,0},{2,3},{3,2},{4,5},{5,4},{6,7},{7,6},{8,9},{9,8},{10,11... | collective-permute-start | bytes 1572872 | tf_op jit(solution)/shard_map/ppermute | solution.py:514
  127.7 4.3 %all-to-all-start.4 = ((bf16[16,16,512]{2,1,0:T(8,128)(2,1)}), bf16[16,16,512]{2,1,0:T(8,128)(2,1)}, u32[]{:S(2)}, u32[]{:S(2)}) async-start(bf16[16,16,512]{2,1,0:T(8,128)(2,1)} %bitcast.44), calls=%async_computation.4 | async-start | bytes 524288 | tf_op jit(solution)/shard_map/all_to_all | solution.py:549
  132.5 1.0 shard_map.191
  133.8 0.9 collective-permute-done.14.refs_4_
  134.7 2.6 %shard_map.192 = (bf16[1024,512]{1,0:T(8,128)(2,1)}, bf16[512,512]{1,0:T(8,128)(2,1)}) custom-call(s32[1]{0:T(128)} %bitcast.refs_0_, bf16[384,512]{1,0:T(8,128)(2,1)} %copy-done.6, bf16[384,512]{1,0:T(8,128)(2,1)} %collective-permute-done.10.refs_2_, bf16[384,512]{1,0:T(8,128)(2,1)} %copy-done.10, bf16[384,512]{1,0:T(8,128)(2,1)} %collective-permute-done.14.refs_4_, ...), custom_call_target="tpu_custom_call" | custom-call | flops 1 | bytes 1 | tf_op jit(solution)/shard_map/pallas_call | solution.py:494
  137.2 7.2 %all-to-all-done.4 = bf16[16,16,512]{2,1,0:T(8,128)(2,1)} async-done(((bf16[16,16,512]{2,1,0:T(8,128)(2,1)}), bf16[16,16,512]{2,1,0:T(8,128)(2,1)}, u32[]{:S(2)}, u32[]{:S(2)}) %all-to-all-start.4) | async-done | bytes 262176 | tf_op jit(solution)/shard_map/all_to_all | solution.py:549
  144.8 1.9 %add_add_fusion = f32[128,512]{1,0:T(8,128)} fusion(f32[128,512]{1,0:T(8,128)S(1)} %copy-done.11, f32[128,512]{1,0:T(8,128)S(1)} %copy-done.12, bf16[256,128]{1,0:T(8,128)(2,1)S(1)} %copy-done.4, bf16[256,512]{1,0:T(8,128)(2,1)} %bitcast.25), kind=kOutput, calls=%fused_computation.15 | convolution fusion | flops 33685504 | bytes 1114112 | tf_op jit(solution)/shard_map/dot_general | solution.py:20
  146.7 1.0 shard_map.193
  (49 shorter events, 3.5 us)
Async XLA Ops:
  2.3 13.0 %all-to-all-start = ((s32[16,1,16]{2,1,0:T(1,128)}), s32[16,1,16]{2,1,0:T(1,128)S(1)}, u32[]{:S(2)}, u32[]{:S(2)}) async-start(s32[16,1,16]{2,1,0:T(1,128)} %bitcast.52), calls=%async_computation | async-start | bytes 16384 | tf_op jit(solution)/shard_map/all_to_all | solution.py:579
  15.4 0.9 copy-start.1
  16.3 0.9 copy-start.2
  18.3 0.6 copy-start.3
  18.9 13.6 %all-to-all-start.1 = ((bf16[16,16,512]{2,1,0:T(8,128)(2,1)}), bf16[16,16,512]{2,1,0:T(8,128)(2,1)S(1)}, u32[]{:S(2)}, u32[]{:S(2)}) async-start(bf16[16,16,512]{2,1,0:T(8,128)(2,1)} %bitcast.7), calls=%async_computation.1 | async-start | bytes 524288 | tf_op jit(solution)/shard_map/all_to_all | solution.py:549
  32.5 0.7 copy-start.8
  37.5 13.5 %all-to-all-start.2 = ((bf16[16,16,512]{2,1,0:T(8,128)(2,1)}), bf16[16,16,512]{2,1,0:T(8,128)(2,1)S(1)}, u32[]{:S(2)}, u32[]{:S(2)}) async-start(bf16[16,16,512]{2,1,0:T(8,128)(2,1)} %bitcast.48), calls=%async_computation.2 | async-start | bytes 524288 | tf_op jit(solution)/shard_map/all_to_all | solution.py:549
  51.1 0.7 copy-start.9
  57.1 4.3 %collective-permute-start = (bf16[768,512]{1,0:T(8,128)(2,1)}, bf16[768,512]{1,0:T(8,128)(2,1)S(1)}, u32[]{:S(2)}, u32[]{:S(2)}) collective-permute-start(bf16[768,512]{1,0:T(8,128)(2,1)} %get-tuple-element.101.refs_7_), channel_id=1, source_target_pairs={{0,1},{1,0},{2,3},{3,2},{4,5},{5,4},{6,7},{7,6},{8,9},{9,8},{10,11... | collective-permute-start | bytes 2359304 | tf_op jit(solution)/shard_map/ppermute | solution.py:514
  57.8 12.9 %all-to-all-start.3 = ((bf16[16,16,512]{2,1,0:T(8,128)(2,1)}), bf16[16,16,512]{2,1,0:T(8,128)(2,1)S(1)}, u32[]{:S(2)}, u32[]{:S(2)}) async-start(bf16[16,16,512]{2,1,0:T(8,128)(2,1)} %bitcast.51), calls=%async_computation.3 | async-start | bytes 524288 | tf_op jit(solution)/shard_map/all_to_all | solution.py:549
  62.9 14.0 %collective-permute-start.1 = (bf16[384,512]{1,0:T(8,128)(2,1)S(1)}, bf16[384,512]{1,0:T(8,128)(2,1)S(1)}, u32[]{:S(2)}, u32[]{:S(2)}) collective-permute-start(bf16[384,512]{1,0:T(8,128)(2,1)S(1)} %get-tuple-element.168), channel_id=1, source_target_pairs={{0,2},{1,3},{2,0},{3,1},{4,6},{5,7},{6,4},{7,5},{8,10},{9,11},{10,... | collective-permute-start | bytes 1179656 | tf_op jit(solution)/shard_map/ppermute | solution.py:514
  70.7 0.7 copy-start.7
  76.8 5.6 %collective-permute-start.2 = (bf16[1024,512]{1,0:T(8,128)(2,1)}, bf16[1024,512]{1,0:T(8,128)(2,1)S(1)}, u32[]{:S(2)}, u32[]{:S(2)}) collective-permute-start(bf16[1024,512]{1,0:T(8,128)(2,1)} %get-tuple-element.121.refs_12_), channel_id=1, source_target_pairs={{0,1},{1,0},{2,3},{3,2},{4,5},{5,4},{6,7},{7,6},{8,9},{9,8},{10,11... | collective-permute-start | bytes 3145736 | tf_op jit(solution)/shard_map/ppermute | solution.py:514
  77.6 6.7 %collective-permute-start.4 = (bf16[192,512]{1,0:T(8,128)(2,1)S(1)}, bf16[192,512]{1,0:T(8,128)(2,1)S(1)}, u32[]{:S(2)}, u32[]{:S(2)}) collective-permute-start(bf16[192,512]{1,0:T(8,128)(2,1)S(1)} %fusion.2), channel_id=1, source_target_pairs={{0,4},{1,5},{2,6},{3,7},{4,0},{5,1},{6,2},{7,3},{8,12},{9,13},{10,... | collective-permute-start | bytes 589832 | tf_op jit(solution)/shard_map/ppermute | solution.py:514
  83.7 12.8 %collective-permute-start.3 = (bf16[512,512]{1,0:T(8,128)(2,1)S(1)}, bf16[512,512]{1,0:T(8,128)(2,1)S(1)}, u32[]{:S(2)}, u32[]{:S(2)}) collective-permute-start(bf16[512,512]{1,0:T(8,128)(2,1)S(1)} %add_convert_fusion.3), channel_id=1, source_target_pairs={{0,2},{1,3},{2,0},{3,1},{4,6},{5,7},{6,4},{7,5},{8,10},{9,11},{10,... | collective-permute-start | bytes 1572872 | tf_op jit(solution)/shard_map/ppermute | solution.py:514
  84.5 11.4 %collective-permute-start.5 = (bf16[192,512]{1,0:T(8,128)(2,1)S(1)}, bf16[192,512]{1,0:T(8,128)(2,1)S(1)}, u32[]{:S(2)}, u32[]{:S(2)}) collective-permute-start(bf16[192,512]{1,0:T(8,128)(2,1)S(1)} %fusion.1), channel_id=1, source_target_pairs={{0,8},{1,9},{2,10},{3,11},{4,12},{5,13},{6,14},{7,15},{8,0},{9,1},... | collective-permute-start | bytes 589832 | tf_op jit(solution)/shard_map/ppermute | solution.py:514
  86.0 3.9 %copy-start.5 = (bf16[1024,512]{1,0:T(8,128)(2,1)S(1)}, bf16[1024,512]{1,0:T(8,128)(2,1)}, u32[]{:S(2)}) copy-start(bf16[1024,512]{1,0:T(8,128)(2,1)} %shard_map.188.refs_7_) | copy-start | bytes 3145732
  96.6 7.2 %collective-permute-start.6 = (bf16[256,512]{1,0:T(8,128)(2,1)S(1)}, bf16[256,512]{1,0:T(8,128)(2,1)S(1)}, u32[]{:S(2)}, u32[]{:S(2)}) collective-permute-start(bf16[256,512]{1,0:T(8,128)(2,1)S(1)} %dynamic-slice_bitcast_fusion.2), channel_id=1, source_target_pairs={{0,4},{1,5},{2,6},{3,7},{4,0},{5,1},{6,2},{7,3},{8,12},{9,13},{10,... | collective-permute-start | bytes 786440 | tf_op jit(solution)/shard_map/ppermute | solution.py:514
  103.9 4.6 %collective-permute-start.9 = (bf16[192,512]{1,0:T(8,128)(2,1)S(1)}, bf16[192,512]{1,0:T(8,128)(2,1)S(1)}, u32[]{:S(2)}, u32[]{:S(2)}) collective-permute-start(bf16[192,512]{1,0:T(8,128)(2,1)S(1)} %add_convert_fusion.5), channel_id=1, source_target_pairs={{0,4},{1,5},{2,6},{3,7},{4,0},{5,1},{6,2},{7,3},{8,12},{9,13},{10,... | collective-permute-start | bytes 589832 | tf_op jit(solution)/shard_map/ppermute | solution.py:514
  105.4 13.2 %collective-permute-start.7 = (bf16[256,512]{1,0:T(8,128)(2,1)S(1)}, bf16[256,512]{1,0:T(8,128)(2,1)S(1)}, u32[]{:S(2)}, u32[]{:S(2)}) collective-permute-start(bf16[256,512]{1,0:T(8,128)(2,1)S(1)} %fusion), channel_id=1, source_target_pairs={{0,8},{1,9},{2,10},{3,11},{4,12},{5,13},{6,14},{7,15},{8,0},{9,1},... | collective-permute-start | bytes 786440 | tf_op jit(solution)/shard_map/ppermute | solution.py:514
  106.2 26.4 %copy-start = (f32[768,512]{1,0:T(8,128)S(1)}, f32[768,512]{1,0:T(8,128)}, u32[]{:S(2)}) copy-start(f32[768,512]{1,0:T(8,128)} %shard_map.190.refs_3_) | copy-start | bytes 4718596
  108.6 25.0 %copy-start.6 = (bf16[384,512]{1,0:T(8,128)(2,1)}, bf16[384,512]{1,0:T(8,128)(2,1)S(1)}, u32[]{:S(2)}) copy-start(bf16[384,512]{1,0:T(8,128)(2,1)S(1)} %maximum_select_fusion.1.refs_1_) | copy-start | bytes 1179652
  108.6 15.8 %collective-permute-start.10 = (bf16[384,512]{1,0:T(8,128)(2,1)S(1)}, bf16[384,512]{1,0:T(8,128)(2,1)}, u32[]{:S(2)}, u32[]{:S(2)}) collective-permute-start(bf16[384,512]{1,0:T(8,128)(2,1)S(1)} %maximum_select_fusion.1.refs_1_), channel_id=1, source_target_pairs={{0,2},{1,3},{2,0},{3,1},{4,6},{5,7},{6,4},{7,5},{8,10},{9,11},{10,... | collective-permute-start | bytes 1179656 | tf_op jit(solution)/shard_map/ppermute | solution.py:514
  118.7 5.8 %collective-permute-start.8 = (bf16[256,512]{1,0:T(8,128)(2,1)S(1)}, bf16[256,512]{1,0:T(8,128)(2,1)S(1)}, u32[]{:S(2)}, u32[]{:S(2)}) collective-permute-start(bf16[256,512]{1,0:T(8,128)(2,1)S(1)} %add_convert_fusion.4), channel_id=1, source_target_pairs={{0,4},{1,5},{2,6},{3,7},{4,0},{5,1},{6,2},{7,3},{8,12},{9,13},{10,... | collective-permute-start | bytes 786440 | tf_op jit(solution)/shard_map/ppermute | solution.py:514
  124.7 7.9 %collective-permute-start.12 = (bf16[512,512]{1,0:T(8,128)(2,1)S(1)}, bf16[512,512]{1,0:T(8,128)(2,1)S(1)}, u32[]{:S(2)}, u32[]{:S(2)}) collective-permute-start(bf16[512,512]{1,0:T(8,128)(2,1)S(1)} %maximum_select_fusion.refs_1_), channel_id=1, source_target_pairs={{0,1},{1,0},{2,3},{3,2},{4,5},{5,4},{6,7},{7,6},{8,9},{9,8},{10,11... | collective-permute-start | bytes 1572872 | tf_op jit(solution)/shard_map/ppermute | solution.py:514
  127.7 16.7 %collective-permute-start.11 = (bf16[512,512]{1,0:T(8,128)(2,1)S(1)}, bf16[512,512]{1,0:T(8,128)(2,1)S(1)}, u32[]{:S(2)}, u32[]{:S(2)}) collective-permute-start(bf16[512,512]{1,0:T(8,128)(2,1)S(1)} %maximum_select_fusion.refs_1_), channel_id=1, source_target_pairs={{0,2},{1,3},{2,0},{3,1},{4,6},{5,7},{6,4},{7,5},{8,10},{9,11},{10,... | collective-permute-start | bytes 1572872 | tf_op jit(solution)/shard_map/ppermute | solution.py:514
  127.7 16.7 %all-to-all-start.4 = ((bf16[16,16,512]{2,1,0:T(8,128)(2,1)}), bf16[16,16,512]{2,1,0:T(8,128)(2,1)}, u32[]{:S(2)}, u32[]{:S(2)}) async-start(bf16[16,16,512]{2,1,0:T(8,128)(2,1)} %bitcast.44), calls=%async_computation.4 | async-start | bytes 524288 | tf_op jit(solution)/shard_map/all_to_all | solution.py:549
  132.0 1.7 %collective-permute-start.13 = (bf16[384,512]{1,0:T(8,128)(2,1)S(1)}, bf16[384,512]{1,0:T(8,128)(2,1)S(1)}, u32[]{:S(2)}, u32[]{:S(2)}) collective-permute-start(bf16[384,512]{1,0:T(8,128)(2,1)S(1)} %maximum_select_fusion.1.refs_1_), channel_id=1, source_target_pairs={{0,1},{1,0},{2,3},{3,2},{4,5},{5,4},{6,7},{7,6},{8,9},{9,8},{10,11... | collective-permute-start | bytes 1179656 | tf_op jit(solution)/shard_map/ppermute | solution.py:514
  132.2 2.4 %collective-permute-start.14 = (bf16[384,512]{1,0:T(8,128)(2,1)}, bf16[384,512]{1,0:T(8,128)(2,1)}, u32[]{:S(2)}, u32[]{:S(2)}) collective-permute-start(bf16[384,512]{1,0:T(8,128)(2,1)} %collective-permute-done.10.refs_2_), channel_id=1, source_target_pairs={{0,1},{1,0},{2,3},{3,2},{4,5},{5,4},{6,7},{7,6},{8,9},{9,8},{10,11... | collective-permute-start | bytes 1179656 | tf_op jit(solution)/shard_map/ppermute | solution.py:514
  133.6 11.2 %copy-start.4 = (bf16[256,128]{1,0:T(8,128)(2,1)S(1)}, bf16[256,128]{1,0:T(8,128)(2,1)}, u32[]{:S(2)}) copy-start(bf16[256,128]{1,0:T(8,128)(2,1)} %copy-done.3) | copy-start | bytes 196612
  133.6 11.2 %copy-start.11 = (f32[128,512]{1,0:T(8,128)S(1)}, f32[128,512]{1,0:T(8,128)}, u32[]{:S(2)}) copy-start(f32[128,512]{1,0:T(8,128)} %get-tuple-element.156) | copy-start | bytes 786436
  133.6 11.2 %copy-start.12 = (f32[128,512]{1,0:T(8,128)S(1)}, f32[128,512]{1,0:T(8,128)}, u32[]{:S(2)}) copy-start(f32[128,512]{1,0:T(8,128)} %get-tuple-element.157) | copy-start | bytes 786436
  133.8 0.9 copy-start.10
  144.4 2.3 %collective-permute-start.15 = (bf16[512,512]{1,0:T(8,128)(2,1)S(1)}, bf16[512,512]{1,0:T(8,128)(2,1)S(1)}, u32[]{:S(2)}, u32[]{:S(2)}) collective-permute-start(bf16[512,512]{1,0:T(8,128)(2,1)S(1)} %collective-permute-done.11.refs_1_), channel_id=1, source_target_pairs={{0,1},{1,0},{2,3},{3,2},{4,5},{5,4},{6,7},{7,6},{8,9},{9,8},{10,11... | collective-permute-start | bytes 1572872 | tf_op jit(solution)/shard_map/ppermute | solution.py:514

commit v18 on v16

--- a/solution.py
+++ b/solution.py
@@ -314,16 +314,12 @@
     return pl.ds(pl.multiple_of((index ^ ((me_ref[0] >> 1) & 1)) * latent, latent), latent)
 
 
-def edge_rows(me_ref, half, buffers, cut_pre, cut_out, out_ref):
+def edge_rows(half, buffers, cut_pre, cut_out, put):
     latent = cut_pre.shape[1]
     first, first_cut, second, second_cut, first_right, second_right = buffers
     chosen = jnp.where(half == 0, cut_pre.astype(F32), cut_out.astype(F32)).astype(BF16)
-    out_ref[place_rows(me_ref, 0, latent)] = (
-        dot_rows(first[...], first_right[...]) + dot_rows(first_cut[...], cut_pre)
-    ).astype(BF16)
-    out_ref[place_rows(me_ref, 1, latent)] = (
-        dot_rows(second[...], second_right[...]) + dot_rows(second_cut[...], chosen)
-    ).astype(BF16)
+    put(0, dot_rows(first[...], first_right[...]) + dot_rows(first_cut[...], cut_pre))
+    put(1, dot_rows(second[...], second_right[...]) + dot_rows(second_cut[...], chosen))
 
 
 def cut_backward_kernel(
@@ -352,16 +348,31 @@
     grad_out_ref[...] = grad_out
     grad_pre_ref[...] = grad_pre
     fetch_factors(half, sources, buffers, sems, True)
-    edge_rows(me_ref, half, buffers, grad_pre, grad_out, out_ref)
+
+    def put(index, value):
+        out_ref[place_rows(me_ref, index, value.shape[1])] = value.astype(BF16)
+
+    edge_rows(half, buffers, grad_pre, grad_out, put)
 
 
 def edge_weights_kernel(me_ref, cut_out_ref, cut_pre_ref, *refs):
-    sources, out_ref, rest = refs[:9], refs[9], refs[10:]
+    sources, (own_ref, sent_ref), rest = refs[:9], refs[9:11], refs[11:]
     buffers, sems = rest[:-1], rest[-1]
     half = me_ref[0] & 1
     fetch_factors(half, sources, buffers, sems, False)
     fetch_factors(half, sources, buffers, sems, True)
-    edge_rows(me_ref, half, buffers, cut_pre_ref[...], cut_out_ref[...], out_ref)
+    place = (me_ref[0] >> 1) & 1
+
+    def put(index, value):
+        @pl.when(place == index)
+        def _():
+            own_ref[...] = value.astype(BF16)
+
+        @pl.when(place != index)
+        def _():
+            sent_ref[...] = value.astype(BF16)
+
+    edge_rows(half, buffers, cut_pre_ref[...], cut_out_ref[...], put)
 
 
 def place_quarters(me_ref, pieces, outs, sems):
@@ -758,23 +769,23 @@
     received = across(edge_send, domains, 1)
     node_own, node_sent = split(node_parts, 2)
     node_got = across(node_sent, domains, 4)
-    edge_keep = line.run(
+    own_keep, sent_keep = line.run(
         edge_weights_kernel,
-        shaped(BF16, 2 * latent, latent),
+        [shaped(BF16, latent, latent)] * 2,
         [place, cut_out, cut_pre] + factors,
         [SMEM, VMEM, VMEM] + [ANY] * len(factors),
         scratch=buffers,
     )
-    edge_keep, received = fence(edge_keep, received)
-    edge_sent = added(edge_keep[latent:], received[latent:])
+    own_keep, sent_keep, received = fence(own_keep, sent_keep, received)
+    edge_sent = added(sent_keep, received[latent:])
     edge_sent, inner_pre, cut_pre = fence(edge_sent, inner_pre, cut_pre)
     node_got = fence(node_got, edge_sent)[0]
     edge_got = across(edge_sent, domains, 2)
     node_sum = added(*node_own, node_got)
     for bit in bits[3:]:
         node_sum = added(*handed(node_sum, domains, bit))
-    edge_keep, received = fence(edge_keep, received, edge_sent)[:2]
-    edge_own = added(edge_keep[:latent], received[:latent])
+    own_keep, received = fence(own_keep, received, edge_sent)[:2]
+    edge_own = added(own_keep, received[:latent])
     local_grad, outgoing_grad = line.run(
         input_grads_kernel,
         [shaped(F32, node_rows, latent), shaped(BF16, total_slots, latent)],

time: 148 us -> 149 us (level)
  no operation moved by 1% of the time
where the time goes in v18:
time: 149 us; the launch traced here: 148 us
  Pallas kernels  49 us (33%)
  waiting for transfers between devices  42.7 us (29%)
  starting transfers between devices  30.2 us (20%)
  blocking collectives  13 us (9%)
  other arithmetic  4.85 us (3%)
  matrix products  3.82 us (3%)
  local copies, waits for them, and re-layouts  2.81 us (2%)
    pallas_call x14, Pallas kernels, run(): pl.pallas_call(ordered, out_shape=out_shape, in_specs=specs, out_specs=[V...  49 us
    ppermute x16, waiting for transfers between devices, across(): lax.ppermute(rows, 'dom', [(device, device ^ mask) for device in range(de...  26.5 us
    all_to_all x4, starting transfers between devices, exchange(): lax.all_to_all(split, 'dom', split_axis=0, concat_axis=0, tiled=True)  16.7 us
    all_to_all x4, waiting for transfers between devices, exchange(): lax.all_to_all(split, 'dom', split_axis=0, concat_axis=0, tiled=True)  16.3 us
    ppermute x16, starting transfers between devices, across(): lax.ppermute(rows, 'dom', [(device, device ^ mask) for device in range(de...  13.6 us
    all_to_all x1, blocking collectives, shards(): asked = lax.all_to_all(ask, 'dom', split_axis=0, concat_axis=0, tiled=True)  13 us
    convert_element_type x9, other arithmetic, added(): return sum((part.astype(F32) for part in parts)).astype(BF16)  3.11 us
  transfers between devices with their start and end apart: 20, of which 12 were waited for; matrix products, arithmetic and copies ran while one was open for 5% of the time, Pallas kernels for 25%

profile of v18, /device:TPU:1, one launch (start us, length us, event | category | flops | bytes accessed | tf_op | source)
XLA Modules:
  0.0 147.5 jit_solution(1510275473812639973)
XLA Ops:
  0.6 1.7 %shard_map.179.refs_2_ = s32[16,16]{1,0:T(8,128)} custom-call(s32[1,128]{1,0:T(1,128)} %bitcast.54, s32[1,128]{1,0:T(1,128)} %bitcast.57), custom_call_target="tpu_custom_call" | custom-call | flops 1 | bytes 1 | tf_op jit(solution)/shard_map/pallas_call | solution.py:491
  2.3 13.0 %all_to_all.29 = s32[16,1,16]{2,1,0:T(1,128)S(1)} all-to-all(s32[16,1,16]{2,1,0:T(1,128)} %bitcast.53), channel_id=1, replica_groups=mesh['groups'=2,'dom'=16] {'dom'}, dimensions={0} | all-to-all | bytes 2048 | tf_op jit(solution)/shard_map/all_to_all | solution.py:576
  15.4 1.9 %convolution_convert_fusion = bf16[16,16,512]{2,1,0:T(8,128)(2,1)} fusion(bf16[128,512]{1,0:T(8,128)(2,1)} %refs_4_.4, s32[16,16]{1,0:T(8,128)S(1)} %bitcast.52), kind=kOutput, calls=%fused_computation.1 | convolution fusion | flops 33783808 | bytes 394240 | tf_op jit(solution)/shard_map/dot_general | solution.py:585
  17.2 4.0 %all-to-all-start.1 = ((bf16[16,16,512]{2,1,0:T(8,128)(2,1)}), bf16[16,16,512]{2,1,0:T(8,128)(2,1)S(1)}, u32[]{:S(2)}, u32[]{:S(2)}) async-start(bf16[16,16,512]{2,1,0:T(8,128)(2,1)} %convolution_convert_fusion), calls=%async_computation.1 | async-start | bytes 524288 | tf_op jit(solution)/shard_map/all_to_all | solution.py:546
  21.3 2.0 %shard_map.180 = (bf16[256,384]{1,0:T(8,128)(2,1)}, bf16[256,384]{1,0:T(8,128)(2,1)}) custom-call(s32[1,128]{1,0:T(1,128)} %bitcast.55, s32[1,128]{1,0:T(1,128)} %bitcast.58, s32[16,16]{1,0:T(8,128)} %shard_map.179.refs_2_), custom_call_target="tpu_custom_call" | custom-call | flops 1 | bytes 1 | tf_op jit(solution)/shard_map/pallas_call | solution.py:491
  23.3 6.3 %shard_map.181 = (bf16[512,128]{1,0:T(8,128)(2,1)}, bf16[512,128]{1,0:T(8,128)(2,1)}, bf16[512,512]{1,0:T(8,128)(2,1)}, bf16[512,512]{1,0:T(8,128)(2,1)}, bf16[5...) custom-call(s32[2,256]{1,0:T(2,128)} %bitcast.56, ...), custom_call_target="tpu_custom_call" | custom-call | flops 1 | bytes 1 | tf_op jit(solution)/shard_map/pallas_call | solution.py:491
  29.6 1.3 all-to-all-done.1
  30.8 0.7 copy-done.3
  31.5 4.3 %shard_map.182 = (bf16[256,512]{1,0:T(8,128)(2,1)}, bf16[256,512]{1,0:T(8,128)(2,1)}, bf16[256,512]{1,0:T(8,128)(2,1)}, f32[256,512]{1,0:T(8,128)}, f32[256,512]...) custom-call(bf16[256,384]{1,0:T(8,128)(2,1)} %get-tuple-element.89.refs_0_.refs_2_, ...), custom_call_target="tpu_custom_call" | custom-call | flops 1 | bytes 1 | tf_op jit(solution)/shard_map/pallas_call | solution.py:491
  35.8 4.9 %all-to-all-start.2 = ((bf16[16,16,512]{2,1,0:T(8,128)(2,1)}), bf16[16,16,512]{2,1,0:T(8,128)(2,1)S(1)}, u32[]{:S(2)}, u32[]{:S(2)}) async-start(bf16[16,16,512]{2,1,0:T(8,128)(2,1)} %bitcast.48), calls=%async_computation.2 | async-start | bytes 524288 | tf_op jit(solution)/shard_map/all_to_all | solution.py:546
  41.2 0.7 reduce.3
  41.9 0.7 select_convert_fusion.refs_2_
  42.7 2.7 %shard_map.183.refs_8_ = bf16[768,512]{1,0:T(8,128)(2,1)} custom-call(bf16[768,512]{1,0:T(8,128)(2,1)} %refs_3_.6, f32[512,512]{1,0:T(8,128)} %get-tuple-element.94.refs_1_.refs_3_, f32[256,512]{1,0:T(8,128)} %get-tuple-element.95.refs_2_.refs_5_, bf16[256,512]{1,0:T(8,128)(2,1)} %get-tuple-element.92.refs_3_), custom_call_target="tpu_custom_call" | custom-call | flops 1 | bytes 1 | tf_op jit(solution)/shard_map/pallas_call | solution.py:491
  45.3 4.8 %all-to-all-done.2 = bf16[16,16,512]{2,1,0:T(8,128)(2,1)S(1)} async-done(((bf16[16,16,512]{2,1,0:T(8,128)(2,1)}), bf16[16,16,512]{2,1,0:T(8,128)(2,1)S(1)}, u32[]{:S(2)}, u32[]{:S(2)}) %all-to-all-start.2) | async-done | bytes 262176 | tf_op jit(solution)/shard_map/all_to_all | solution.py:546
  50.2 0.7 copy-done.4
  50.9 5.4 %shard_map.184 = (bf16[128,512]{1,0:T(8,128)(2,1)}, f32[128,512]{1,0:T(8,128)}, bf16[128,512]{1,0:T(8,128)(2,1)}, bf16[256,512]{1,0:T(8,128)(2,1)}, bf16[768,512]{1,0:T(8,128)(2,1)}, /*index=5*/bf16[768,512]{1,0:T(8,128)(2,1)}) custom-call(s32[1]{0:T(128)} %bitcast.refs_0_, bf16[256,512]{1,0:T(8,128)(2,1)} %bitcast.47, ...), custom_call_target="tpu_custom_call" | custom-call | flops 1 | bytes 1 | tf_op jit(solution)/shard_map/pallas_call | solution.py:491
  56.2 0.6 collective-permute-start
  56.9 3.4 %all-to-all-start.3 = ((bf16[16,16,512]{2,1,0:T(8,128)(2,1)}), bf16[16,16,512]{2,1,0:T(8,128)(2,1)S(1)}, u32[]{:S(2)}, u32[]{:S(2)}) async-start(bf16[16,16,512]{2,1,0:T(8,128)(2,1)} %bitcast.51), calls=%async_computation.3 | async-start | bytes 524288 | tf_op jit(solution)/shard_map/all_to_all | solution.py:546
  60.3 1.3 add_convert_fusion
  61.8 1.3 collective-permute-start.1
  63.1 3.6 %shard_map.185 = (bf16[512,512]{1,0:T(8,128)(2,1)}, bf16[512,512]{1,0:T(8,128)(2,1)}) custom-call(bf16[512,128]{1,0:T(8,128)(2,1)} %get-tuple-element.101.refs_0_.refs_1_, bf16[128,512]{1,0:T(8,128)(2,1)} %get-tuple-element.97.refs_1_.refs_2_, bf16[768,512]{1,0:T(8,128)(2,1)} %refs_0_.3, f32[512,512]{1,0:T(8,128)} %get-tuple-element.94.refs_1_.refs_3_, ...), custom_call_target="tpu_custom_call" | custom-call | flops 1 | bytes 1 | tf_op jit(solution)/shard_map/pallas_call | solution.py:491
  66.7 3.1 %all-to-all-done.3 = bf16[16,16,512]{2,1,0:T(8,128)(2,1)S(1)} async-done(((bf16[16,16,512]{2,1,0:T(8,128)(2,1)}), bf16[16,16,512]{2,1,0:T(8,128)(2,1)S(1)}, u32[]{:S(2)}, u32[]{:S(2)}) %all-to-all-start.3) | async-done | bytes 262176 | tf_op jit(solution)/shard_map/all_to_all | solution.py:546
  69.8 0.7 copy-done.2
  70.5 5.4 %shard_map.186 = (bf16[256,512]{1,0:T(8,128)(2,1)}, bf16[256,512]{1,0:T(8,128)(2,1)}, bf16[1024,512]{1,0:T(8,128)(2,1)}) custom-call(s32[1]{0:T(128)} %bitcast.refs_0_, bf16[256,384]{1,0:T(8,128)(2,1)} %get-tuple-element.90.refs_5_.refs_1_.refs_3_, bf16[128,512]{1,0:T(8,128)(2,1)} %get-tuple-element.97.refs_1_.refs_2_, bf16[256,512]{1,0:T(8,128)(2,1)} %bitcast.45, ...), custom_call_target="tpu_custom_call" | custom-call | flops 1 | bytes 1 | tf_op jit(solution)/shard_map/pallas_call | solution.py:491
  75.9 0.8 collective-permute-start.2
  76.8 5.2 %shard_map.187 = (bf16[512,512]{1,0:T(8,128)(2,1)}, bf16[512,512]{1,0:T(8,128)(2,1)}) custom-call(s32[1]{0:T(128)} %bitcast.refs_0_, bf16[256,512]{1,0:T(8,128)(2,1)} %get-tuple-element.118.refs_1_, bf16[256,512]{1,0:T(8,128)(2,1)} %get-tuple-element.140.refs_2_.refs_5_, bf16[768,512]{1,0:T(8,128)(2,1)} %refs_3_.6, ...), custom_call_target="tpu_custom_call" | custom-call | flops 1 | bytes 1 | tf_op jit(solution)/shard_map/pallas_call | solution.py:491
  82.0 1.2 add_convert_fusion.3
  83.2 0.7 collective-permute-start.3
  84.0 1.6 %collective-permute-start.5 = (bf16[192,512]{1,0:T(8,128)(2,1)S(1)}, bf16[192,512]{1,0:T(8,128)(2,1)S(1)}, u32[]{:S(2)}, u32[]{:S(2)}) collective-permute-start(bf16[192,512]{1,0:T(8,128)(2,1)S(1)} %fusion.1), channel_id=1, source_target_pairs={{0,8},{1,9},{2,10},{3,11},{4,12},{5,13},{6,14},{7,15},{8,0},{9,1},... | collective-permute-start | bytes 589832 | tf_op jit(solution)/shard_map/ppermute | solution.py:511
  85.6 3.9 %shard_map.188 = (f32[128,512]{1,0:T(8,128)}, bf16[256,512]{1,0:T(8,128)(2,1)}) custom-call(bf16[512,128]{1,0:T(8,128)(2,1)} %get-tuple-element.134.refs_0_, bf16[512,128]{1,0:T(8,128)(2,1)} %get-tuple-element.101.refs_0_.refs_1_, bf16[256,384]{1,0:T(8,128)(2,1)} %get-tuple-element.89.refs_0_.refs_2_, ...), custom_call_target="tpu_custom_call" | custom-call | flops 1 | bytes 1 | tf_op jit(solution)/shard_map/pallas_call | solution.py:491
  89.7 5.7 %collective-permute-done.5 = bf16[192,512]{1,0:T(8,128)(2,1)S(1)} collective-permute-done((bf16[192,512]{1,0:T(8,128)(2,1)S(1)}, bf16[192,512]{1,0:T(8,128)(2,1)S(1)}, u32[]{:S(2)}, u32[]{:S(2)}) %collective-permute-start.5) | collective-permute-done | bytes 196640 | tf_op jit(solution)/shard_map/ppermute | solution.py:511
  95.4 0.5 collective-permute-done.3
  96.2 2.0 %collective-permute-start.6 = (bf16[256,512]{1,0:T(8,128)(2,1)S(1)}, bf16[256,512]{1,0:T(8,128)(2,1)S(1)}, u32[]{:S(2)}, u32[]{:S(2)}) collective-permute-start(bf16[256,512]{1,0:T(8,128)(2,1)S(1)} %dynamic-slice_bitcast_fusion.2), channel_id=1, source_target_pairs={{0,4},{1,5},{2,6},{3,7},{4,0},{5,1},{6,2},{7,3},{8,12},{9,13},{10,... | collective-permute-start | bytes 786440 | tf_op jit(solution)/shard_map/ppermute | solution.py:511
  98.2 3.9 %shard_map.189.refs_3_ = f32[768,512]{1,0:T(8,128)} custom-call(bf16[768,512]{1,0:T(8,128)(2,1)} %refs_0_.3, bf16[512,512]{1,0:T(8,128)(2,1)} %get-tuple-element.139.refs_17_.refs_18_.refs_11_.refs_4_.refs_1_, bf16[256,512]{1,0:T(8,128)(2,1)} %get-tuple-element.140.refs_2_.refs_5_, bf16[1536,512]{1,0:T(8,128)(2,1)} %refs_3_.7, ...), custom_call_target="tpu_custom_call" | custom-call | flops 1 | bytes 1 | tf_op jit(solution)/shard_map/pallas_call | solution.py:491
  102.1 1.3 collective-permute-done.6
  103.4 1.5 %collective-permute-start.9 = (bf16[192,512]{1,0:T(8,128)(2,1)S(1)}, bf16[192,512]{1,0:T(8,128)(2,1)S(1)}, u32[]{:S(2)}, u32[]{:S(2)}) collective-permute-start(bf16[192,512]{1,0:T(8,128)(2,1)S(1)} %add_convert_fusion.5), channel_id=1, source_target_pairs={{0,4},{1,5},{2,6},{3,7},{4,0},{5,1},{6,2},{7,3},{8,12},{9,13},{10,... | collective-permute-start | bytes 589832 | tf_op jit(solution)/shard_map/ppermute | solution.py:511
  105.0 0.7 collective-permute-start.7
  105.7 2.3 %collective-permute-done.9 = bf16[192,512]{1,0:T(8,128)(2,1)S(1)} collective-permute-done((bf16[192,512]{1,0:T(8,128)(2,1)S(1)}, bf16[192,512]{1,0:T(8,128)(2,1)S(1)}, u32[]{:S(2)}, u32[]{:S(2)}) %collective-permute-start.9) | collective-permute-done | bytes 196640 | tf_op jit(solution)/shard_map/ppermute | solution.py:511
  108.3 9.9 %collective-permute-done.7 = bf16[256,512]{1,0:T(8,128)(2,1)S(1)} collective-permute-done((bf16[256,512]{1,0:T(8,128)(2,1)S(1)}, bf16[256,512]{1,0:T(8,128)(2,1)S(1)}, u32[]{:S(2)}, u32[]{:S(2)}) %collective-permute-start.7) | collective-permute-done | bytes 262176 | tf_op jit(solution)/shard_map/ppermute | solution.py:511
  118.3 5.7 %collective-permute-done.8 = bf16[256,512]{1,0:T(8,128)(2,1)S(1)} collective-permute-done((bf16[256,512]{1,0:T(8,128)(2,1)S(1)}, bf16[256,512]{1,0:T(8,128)(2,1)S(1)}, u32[]{:S(2)}, u32[]{:S(2)}) %collective-permute-start.8) | collective-permute-done | bytes 262176 | tf_op jit(solution)/shard_map/ppermute | solution.py:511
  124.2 3.1 %collective-permute-start.12 = (bf16[512,512]{1,0:T(8,128)(2,1)S(1)}, bf16[512,512]{1,0:T(8,128)(2,1)S(1)}, u32[]{:S(2)}, u32[]{:S(2)}) collective-permute-start(bf16[512,512]{1,0:T(8,128)(2,1)S(1)} %maximum_select_fusion.refs_1_), channel_id=1, source_target_pairs={{0,1},{1,0},{2,3},{3,2},{4,5},{5,4},{6,7},{7,6},{8,9},{9,8},{10,11... | collective-permute-start | bytes 1572872 | tf_op jit(solution)/shard_map/ppermute | solution.py:511
  127.3 4.4 %all-to-all-start.4 = ((bf16[16,16,512]{2,1,0:T(8,128)(2,1)}), bf16[16,16,512]{2,1,0:T(8,128)(2,1)}, u32[]{:S(2)}, u32[]{:S(2)}) async-start(bf16[16,16,512]{2,1,0:T(8,128)(2,1)} %bitcast.44), calls=%async_computation.4 | async-start | bytes 524288 | tf_op jit(solution)/shard_map/all_to_all | solution.py:546
  132.1 1.0 shard_map.190
  133.3 0.9 collective-permute-done.14.refs_4_
  134.3 2.6 %shard_map.191 = (bf16[1024,512]{1,0:T(8,128)(2,1)}, bf16[512,512]{1,0:T(8,128)(2,1)}) custom-call(s32[1]{0:T(128)} %bitcast.refs_0_, bf16[384,512]{1,0:T(8,128)(2,1)} %copy-done.1, bf16[384,512]{1,0:T(8,128)(2,1)} %collective-permute-done.10.refs_2_, bf16[384,512]{1,0:T(8,128)(2,1)} %copy-done.6, bf16[384,512]{1,0:T(8,128)(2,1)} %collective-permute-done.14.refs_4_, ...), custom_call_target="tpu_custom_call" | custom-call | flops 1 | bytes 1 | tf_op jit(solution)/shard_map/pallas_call | solution.py:491
  136.8 7.1 %all-to-all-done.4 = bf16[16,16,512]{2,1,0:T(8,128)(2,1)} async-done(((bf16[16,16,512]{2,1,0:T(8,128)(2,1)}), bf16[16,16,512]{2,1,0:T(8,128)(2,1)}, u32[]{:S(2)}, u32[]{:S(2)}) %all-to-all-start.4) | async-done | bytes 262176 | tf_op jit(solution)/shard_map/all_to_all | solution.py:546
  144.4 1.9 %add_add_fusion = f32[128,512]{1,0:T(8,128)} fusion(f32[128,512]{1,0:T(8,128)S(1)} %copy-done.7, f32[128,512]{1,0:T(8,128)S(1)} %copy-done.8, bf16[256,512]{1,0:T(8,128)(2,1)} %bitcast.25, s32[256]{0:T(256)S(1)} %eq.32), kind=kOutput, calls=%fused_computation.16 | convolution fusion | flops 33783808 | bytes 1049600 | tf_op jit(solution)/shard_map/dot_general | solution.py:20
  146.3 1.0 shard_map.192
  (44 shorter events, 2.9 us)
Async XLA Ops:
  17.2 13.6 %all-to-all-start.1 = ((bf16[16,16,512]{2,1,0:T(8,128)(2,1)}), bf16[16,16,512]{2,1,0:T(8,128)(2,1)S(1)}, u32[]{:S(2)}, u32[]{:S(2)}) async-start(bf16[16,16,512]{2,1,0:T(8,128)(2,1)} %convolution_convert_fusion), calls=%async_computation.1 | async-start | bytes 524288 | tf_op jit(solution)/shard_map/all_to_all | solution.py:546
  30.8 0.7 copy-start.3
  35.8 14.4 %all-to-all-start.2 = ((bf16[16,16,512]{2,1,0:T(8,128)(2,1)}), bf16[16,16,512]{2,1,0:T(8,128)(2,1)S(1)}, u32[]{:S(2)}, u32[]{:S(2)}) async-start(bf16[16,16,512]{2,1,0:T(8,128)(2,1)} %bitcast.48), calls=%async_computation.2 | async-start | bytes 524288 | tf_op jit(solution)/shard_map/all_to_all | solution.py:546
  50.2 0.7 copy-start.4
  56.2 4.1 %collective-permute-start = (bf16[768,512]{1,0:T(8,128)(2,1)}, bf16[768,512]{1,0:T(8,128)(2,1)S(1)}, u32[]{:S(2)}, u32[]{:S(2)}) collective-permute-start(bf16[768,512]{1,0:T(8,128)(2,1)} %get-tuple-element.100.refs_7_), channel_id=1, source_target_pairs={{0,1},{1,0},{2,3},{3,2},{4,5},{5,4},{6,7},{7,6},{8,9},{9,8},{10,11... | collective-permute-start | bytes 2359304 | tf_op jit(solution)/shard_map/ppermute | solution.py:511
  56.9 12.9 %all-to-all-start.3 = ((bf16[16,16,512]{2,1,0:T(8,128)(2,1)}), bf16[16,16,512]{2,1,0:T(8,128)(2,1)S(1)}, u32[]{:S(2)}, u32[]{:S(2)}) async-start(bf16[16,16,512]{2,1,0:T(8,128)(2,1)} %bitcast.51), calls=%async_computation.3 | async-start | bytes 524288 | tf_op jit(solution)/shard_map/all_to_all | solution.py:546
  61.8 14.2 %collective-permute-start.1 = (bf16[384,512]{1,0:T(8,128)(2,1)S(1)}, bf16[384,512]{1,0:T(8,128)(2,1)S(1)}, u32[]{:S(2)}, u32[]{:S(2)}) collective-permute-start(bf16[384,512]{1,0:T(8,128)(2,1)S(1)} %get-tuple-element.170), channel_id=1, source_target_pairs={{0,2},{1,3},{2,0},{3,1},{4,6},{5,7},{6,4},{7,5},{8,10},{9,11},{10,... | collective-permute-start | bytes 1179656 | tf_op jit(solution)/shard_map/ppermute | solution.py:511
  69.8 0.7 copy-start.2
  75.9 6.1 %collective-permute-start.2 = (bf16[1024,512]{1,0:T(8,128)(2,1)}, bf16[1024,512]{1,0:T(8,128)(2,1)S(1)}, u32[]{:S(2)}, u32[]{:S(2)}) collective-permute-start(bf16[1024,512]{1,0:T(8,128)(2,1)} %get-tuple-element.122.refs_12_), channel_id=1, source_target_pairs={{0,1},{1,0},{2,3},{3,2},{4,5},{5,4},{6,7},{7,6},{8,9},{9,8},{10,11... | collective-permute-start | bytes 3145736 | tf_op jit(solution)/shard_map/ppermute | solution.py:511
  76.7 7.2 %collective-permute-start.4 = (bf16[192,512]{1,0:T(8,128)(2,1)S(1)}, bf16[192,512]{1,0:T(8,128)(2,1)S(1)}, u32[]{:S(2)}, u32[]{:S(2)}) collective-permute-start(bf16[192,512]{1,0:T(8,128)(2,1)S(1)} %fusion.2), channel_id=1, source_target_pairs={{0,4},{1,5},{2,6},{3,7},{4,0},{5,1},{6,2},{7,3},{8,12},{9,13},{10,... | collective-permute-start | bytes 589832 | tf_op jit(solution)/shard_map/ppermute | solution.py:511
  83.2 12.8 %collective-permute-start.3 = (bf16[512,512]{1,0:T(8,128)(2,1)S(1)}, bf16[512,512]{1,0:T(8,128)(2,1)S(1)}, u32[]{:S(2)}, u32[]{:S(2)}) collective-permute-start(bf16[512,512]{1,0:T(8,128)(2,1)S(1)} %add_convert_fusion.3), channel_id=1, source_target_pairs={{0,2},{1,3},{2,0},{3,1},{4,6},{5,7},{6,4},{7,5},{8,10},{9,11},{10,... | collective-permute-start | bytes 1572872 | tf_op jit(solution)/shard_map/ppermute | solution.py:511
  84.0 11.4 %collective-permute-start.5 = (bf16[192,512]{1,0:T(8,128)(2,1)S(1)}, bf16[192,512]{1,0:T(8,128)(2,1)S(1)}, u32[]{:S(2)}, u32[]{:S(2)}) collective-permute-start(bf16[192,512]{1,0:T(8,128)(2,1)S(1)} %fusion.1), channel_id=1, source_target_pairs={{0,8},{1,9},{2,10},{3,11},{4,12},{5,13},{6,14},{7,15},{8,0},{9,1},... | collective-permute-start | bytes 589832 | tf_op jit(solution)/shard_map/ppermute | solution.py:511
  85.6 3.9 %copy-start.5 = (bf16[512,512]{1,0:T(8,128)(2,1)S(1)}, bf16[512,512]{1,0:T(8,128)(2,1)}, u32[]{:S(2)}) copy-start(bf16[512,512]{1,0:T(8,128)(2,1)} %get-tuple-element.127) | copy-start | bytes 1572868
  96.2 7.2 %collective-permute-start.6 = (bf16[256,512]{1,0:T(8,128)(2,1)S(1)}, bf16[256,512]{1,0:T(8,128)(2,1)S(1)}, u32[]{:S(2)}, u32[]{:S(2)}) collective-permute-start(bf16[256,512]{1,0:T(8,128)(2,1)S(1)} %dynamic-slice_bitcast_fusion.2), channel_id=1, source_target_pairs={{0,4},{1,5},{2,6},{3,7},{4,0},{5,1},{6,2},{7,3},{8,12},{9,13},{10,... | collective-permute-start | bytes 786440 | tf_op jit(solution)/shard_map/ppermute | solution.py:511
  103.4 4.6 %collective-permute-start.9 = (bf16[192,512]{1,0:T(8,128)(2,1)S(1)}, bf16[192,512]{1,0:T(8,128)(2,1)S(1)}, u32[]{:S(2)}, u32[]{:S(2)}) collective-permute-start(bf16[192,512]{1,0:T(8,128)(2,1)S(1)} %add_convert_fusion.5), channel_id=1, source_target_pairs={{0,4},{1,5},{2,6},{3,7},{4,0},{5,1},{6,2},{7,3},{8,12},{9,13},{10,... | collective-permute-start | bytes 589832 | tf_op jit(solution)/shard_map/ppermute | solution.py:511
  105.0 13.1 %collective-permute-start.7 = (bf16[256,512]{1,0:T(8,128)(2,1)S(1)}, bf16[256,512]{1,0:T(8,128)(2,1)S(1)}, u32[]{:S(2)}, u32[]{:S(2)}) collective-permute-start(bf16[256,512]{1,0:T(8,128)(2,1)S(1)} %fusion), channel_id=1, source_target_pairs={{0,8},{1,9},{2,10},{3,11},{4,12},{5,13},{6,14},{7,15},{8,0},{9,1},... | collective-permute-start | bytes 786440 | tf_op jit(solution)/shard_map/ppermute | solution.py:511
  105.7 26.4 %copy-start = (f32[768,512]{1,0:T(8,128)S(1)}, f32[768,512]{1,0:T(8,128)}, u32[]{:S(2)}) copy-start(f32[768,512]{1,0:T(8,128)} %shard_map.189.refs_3_) | copy-start | bytes 4718596
  108.2 25.0 %copy-start.1 = (bf16[384,512]{1,0:T(8,128)(2,1)}, bf16[384,512]{1,0:T(8,128)(2,1)S(1)}, u32[]{:S(2)}) copy-start(bf16[384,512]{1,0:T(8,128)(2,1)S(1)} %maximum_select_fusion.1.refs_1_) | copy-start | bytes 1179652
  108.2 15.8 %collective-permute-start.10 = (bf16[384,512]{1,0:T(8,128)(2,1)S(1)}, bf16[384,512]{1,0:T(8,128)(2,1)}, u32[]{:S(2)}, u32[]{:S(2)}) collective-permute-start(bf16[384,512]{1,0:T(8,128)(2,1)S(1)} %maximum_select_fusion.1.refs_1_), channel_id=1, source_target_pairs={{0,2},{1,3},{2,0},{3,1},{4,6},{5,7},{6,4},{7,5},{8,10},{9,11},{10,... | collective-permute-start | bytes 1179656 | tf_op jit(solution)/shard_map/ppermute | solution.py:511
  118.2 5.8 %collective-permute-start.8 = (bf16[256,512]{1,0:T(8,128)(2,1)S(1)}, bf16[256,512]{1,0:T(8,128)(2,1)S(1)}, u32[]{:S(2)}, u32[]{:S(2)}) collective-permute-start(bf16[256,512]{1,0:T(8,128)(2,1)S(1)} %add_convert_fusion.4), channel_id=1, source_target_pairs={{0,4},{1,5},{2,6},{3,7},{4,0},{5,1},{6,2},{7,3},{8,12},{9,13},{10,... | collective-permute-start | bytes 786440 | tf_op jit(solution)/shard_map/ppermute | solution.py:511
  124.2 7.9 %collective-permute-start.12 = (bf16[512,512]{1,0:T(8,128)(2,1)S(1)}, bf16[512,512]{1,0:T(8,128)(2,1)S(1)}, u32[]{:S(2)}, u32[]{:S(2)}) collective-permute-start(bf16[512,512]{1,0:T(8,128)(2,1)S(1)} %maximum_select_fusion.refs_1_), channel_id=1, source_target_pairs={{0,1},{1,0},{2,3},{3,2},{4,5},{5,4},{6,7},{7,6},{8,9},{9,8},{10,11... | collective-permute-start | bytes 1572872 | tf_op jit(solution)/shard_map/ppermute | solution.py:511
  127.3 16.7 %collective-permute-start.11 = (bf16[512,512]{1,0:T(8,128)(2,1)S(1)}, bf16[512,512]{1,0:T(8,128)(2,1)S(1)}, u32[]{:S(2)}, u32[]{:S(2)}) collective-permute-start(bf16[512,512]{1,0:T(8,128)(2,1)S(1)} %maximum_select_fusion.refs_1_), channel_id=1, source_target_pairs={{0,2},{1,3},{2,0},{3,1},{4,6},{5,7},{6,4},{7,5},{8,10},{9,11},{10,... | collective-permute-start | bytes 1572872 | tf_op jit(solution)/shard_map/ppermute | solution.py:511
  127.3 16.7 %all-to-all-start.4 = ((bf16[16,16,512]{2,1,0:T(8,128)(2,1)}), bf16[16,16,512]{2,1,0:T(8,128)(2,1)}, u32[]{:S(2)}, u32[]{:S(2)}) async-start(bf16[16,16,512]{2,1,0:T(8,128)(2,1)} %bitcast.44), calls=%async_computation.4 | async-start | bytes 524288 | tf_op jit(solution)/shard_map/all_to_all | solution.py:546
  131.6 1.7 %collective-permute-start.13 = (bf16[384,512]{1,0:T(8,128)(2,1)S(1)}, bf16[384,512]{1,0:T(8,128)(2,1)S(1)}, u32[]{:S(2)}, u32[]{:S(2)}) collective-permute-start(bf16[384,512]{1,0:T(8,128)(2,1)S(1)} %maximum_select_fusion.1.refs_1_), channel_id=1, source_target_pairs={{0,1},{1,0},{2,3},{3,2},{4,5},{5,4},{6,7},{7,6},{8,9},{9,8},{10,11... | collective-permute-start | bytes 1179656 | tf_op jit(solution)/shard_map/ppermute | solution.py:511
  131.8 2.4 %collective-permute-start.14 = (bf16[384,512]{1,0:T(8,128)(2,1)}, bf16[384,512]{1,0:T(8,128)(2,1)}, u32[]{:S(2)}, u32[]{:S(2)}) collective-permute-start(bf16[384,512]{1,0:T(8,128)(2,1)} %collective-permute-done.10.refs_2_), channel_id=1, source_target_pairs={{0,1},{1,0},{2,3},{3,2},{4,5},{5,4},{6,7},{7,6},{8,9},{9,8},{10,11... | collective-permute-start | bytes 1179656 | tf_op jit(solution)/shard_map/ppermute | solution.py:511
  133.2 11.2 %copy-start.7 = (f32[128,512]{1,0:T(8,128)S(1)}, f32[128,512]{1,0:T(8,128)}, u32[]{:S(2)}) copy-start(f32[128,512]{1,0:T(8,128)} %get-tuple-element.158) | copy-start | bytes 786436
  133.2 11.2 %copy-start.8 = (f32[128,512]{1,0:T(8,128)S(1)}, f32[128,512]{1,0:T(8,128)}, u32[]{:S(2)}) copy-start(f32[128,512]{1,0:T(8,128)} %get-tuple-element.159) | copy-start | bytes 786436
  133.3 0.9 copy-start.6
  144.0 2.4 %collective-permute-start.15 = (bf16[512,512]{1,0:T(8,128)(2,1)S(1)}, bf16[512,512]{1,0:T(8,128)(2,1)S(1)}, u32[]{:S(2)}, u32[]{:S(2)}) collective-permute-start(bf16[512,512]{1,0:T(8,128)(2,1)S(1)} %collective-permute-done.11.refs_1_), channel_id=1, source_target_pairs={{0,1},{1,0},{2,3},{3,2},{4,5},{5,4},{6,7},{7,6},{8,9},{9,8},{10,11... | collective-permute-start | bytes 1572872 | tf_op jit(solution)/shard_map/ppermute | solution.py:511
